TPU v7x, 128 devices: a whole 4x4x4 slice. The times are simulated.
128 devices in a mesh: shard: 16 (over x, y_hi, core), ctx: 4 (over z), tp: 2 (over y_lo).
Axes of the slice: x: 4, y: 4 (y_hi: 2, y_lo: 2; y = y_hi * 2 + y_lo), z: 4, core: 2. Of those that a mesh axis runs over, the one named last changes fastest.
Arguments:
- tokens: bfloat16 [8192, 2048], P(('shard', 'ctx')), may hold values from -6 to 6
- seg_lengths: int32 [16, 13], P('shard'), may hold values from 16 to 128, as said below
- seg_parents: int32 [16, 13], P('shard'), may hold values from 0 to 4, as said below
- gain_in: bfloat16 [2048], P('shard'), may hold values from 0.5 to 1.5
- w_query: bfloat16 [2048, 2048], P('shard', 'tp'), may hold values from -0.125 to 0.125
- w_key: bfloat16 [2048, 1024], P('shard', 'tp'), may hold values from -0.125 to 0.125
- w_value: bfloat16 [2048, 1024], P('shard', 'tp'), may hold values from -0.125 to 0.125
- w_gate_attn: bfloat16 [2048, 2048], P('shard', 'tp'), may hold values from -0.125 to 0.125
- w_out: bfloat16 [2048, 2048], P('tp', 'shard'), may hold values from -2 to 2
- gain_query: bfloat16 [128], P('shard'), may hold values from 0.5 to 1.5
- gain_key: bfloat16 [128], P('shard'), may hold values from 0.5 to 1.5
- gain_mid: bfloat16 [2048], P('shard'), may hold values from 0.5 to 1.5
- w_gate: bfloat16 [2048, 6144], P('shard', 'tp'), may hold values from -0.125 to 0.125
- w_up: bfloat16 [2048, 6144], P('shard', 'tp'), may hold values from -0.125 to 0.125
- w_down: bfloat16 [6144, 2048], P('tp', 'shard'), may hold values from -0.078125 to 0.078125
- cotangent: bfloat16 [8192, 2048], P(('shard', 'ctx')), may hold values from -6 to 6
Outputs:
- layer_out: float32 [8192, 2048], P(('shard', 'ctx'))
- input_grad: float32 [8192, 2048], P(('shard', 'ctx'))
- grad_gain_in: float32 [2048], P('shard')
- grad_query: float32 [2048, 2048], P('shard', 'tp')
- grad_key: float32 [2048, 1024], P('shard', 'tp')
- grad_value: float32 [2048, 1024], P('shard', 'tp')
- grad_gate_attn: float32 [2048, 2048], P('shard', 'tp')
- grad_out: float32 [2048, 2048], P('tp', 'shard')
- grad_gain_query: float32 [128], P('shard')
- grad_gain_key: float32 [128], P('shard')
- grad_gain_mid: float32 [2048], P('shard')
- grad_gate: float32 [2048, 6144], P('shard', 'tp')
- grad_up: float32 [2048, 6144], P('shard', 'tp')
- grad_down: float32 [6144, 2048], P('tp', 'shard')
Inputs may be any that keep to these rules, and one draw needn't show every extreme that they name: `seg_lengths`: each row describes one tree of 512 tokens; segment 0 (the trunk) has 128 tokens, segments 1 to 4 are branches, 5 to 12 leaves; a row sums to 512, and some segment has exactly 16. `seg_parents`: segment 0 and every branch have parent 0; every leaf has a branch as parent, each branch exactly two leaves.
All inputs are finite; a program needn't handle non-finite values.
Results may differ from a plain program's by a relative error of at most 0.025.
Values may be sent and summed in bfloat16 or wider, within the bound.
No kernel may reach another device: no remote copies, remote signals or barrier semaphores. Data moves between devices by JAX's collectives and lax.ppermute only.
A program may use at most 256 MiB of HBM per device.

v0:
```python
import math

import jax
import jax.numpy as jnp
from jax import lax
from jax.sharding import PartitionSpec as P

HQ = 16
HK = 8
HD = 128


EPS = 1e-06
BASE = 1000000.0
NEG = -1e30


def rms_scale(inputs):
    return lax.rsqrt(jnp.mean(inputs * inputs, axis=-1, keepdims=True) + EPS)


def lookup(onehot, table):
    return jnp.sum(onehot * table[None, :], axis=1)


def tree_layout(lengths, parents, places):
    labels = jnp.arange(lengths.shape[0], dtype=jnp.int32)
    ends = jnp.cumsum(lengths)
    starts = ends - lengths
    parent_hot = (parents[:, None] == labels[None, :]).astype(jnp.int32)
    grand = lookup(parent_hot, parents)
    parent_len = lookup(parent_hot, lengths)
    grand_hot = (grand[:, None] == labels[None, :]).astype(jnp.int32)
    grand_len = lookup(grand_hot, lengths)
    before = jnp.where(labels == 0, 0, parent_len + jnp.where(parents == 0, 0, grand_len))
    segment = jnp.sum((places[:, None] >= ends[None, :]).astype(jnp.int32), axis=1)
    token_hot = (segment[:, None] == labels[None, :]).astype(jnp.int32)
    position = places - lookup(token_hot, starts) + lookup(token_hot, before)
    return (segment, lookup(token_hot, parents), lookup(token_hot, grand), position)


def rope_tables(position, columns):
    halfway = columns // 2
    frequency = jnp.exp(jnp.arange(halfway, dtype=jnp.float32) * (-2.0 * math.log(BASE) / columns))
    angles = position.astype(jnp.float32)[:, None] * frequency[None, :]
    angles = jnp.concatenate([angles, angles], axis=1)
    return (jnp.cos(angles)[:, None, :], jnp.sin(angles)[:, None, :])


def rotate(inputs, cosine_table, sine_table):
    halfway = inputs.shape[-1] // 2
    turned = jnp.concatenate([-inputs[..., halfway:], inputs[..., :halfway]], axis=-1)
    return inputs * cosine_table + turned * sine_table


def turn_back(grads, cosine_table, sine_table):
    scaled = grads * sine_table
    halfway = grads.shape[-1] // 2
    return grads * cosine_table + jnp.concatenate(
        [scaled[..., halfway:], -scaled[..., :halfway]], axis=-1
    )


def norm_back(grads, inputs, factor, gain_full):
    scaled = gain_full * grads
    return factor * scaled - inputs * factor**3 * jnp.mean(scaled * inputs, axis=-1, keepdims=True)


def contract_rows(left, right):
    return lax.dot_general(
        left, right, (((0,), (0,)), ((), ())), preferred_element_type=jnp.float32
    )


def times_back(left, right):
    return lax.dot_general(
        left, right, (((1,), (1,)), ((), ())), preferred_element_type=jnp.float32
    )


def shards(
    tokens,
    seg_lengths,
    seg_parents,
    gain_in,
    w_query,
    w_key,
    w_value,
    w_gate_attn,
    w_out,
    gain_query,
    gain_key,
    gain_mid,
    w_gate,
    w_up,
    w_down,
    cotangent,
):
    length = tokens.shape[0]
    total_len = length * lax.axis_size("ctx")
    local_heads = HQ // lax.axis_size("tp")
    local_kv = HK // lax.axis_size("tp")
    group = HQ // HK
    scale = 1.0 / math.sqrt(HD)
    hidden_cols = w_gate.shape[1]
    attn_full = (
        lax.all_gather(gain_in, "shard", axis=0, tiled=True),
        lax.all_gather(w_query, "shard", axis=0, tiled=True),
        lax.all_gather(w_key, "shard", axis=0, tiled=True),
        lax.all_gather(w_value, "shard", axis=0, tiled=True),
        lax.all_gather(w_gate_attn, "shard", axis=0, tiled=True),
        lax.all_gather(w_out, "shard", axis=1, tiled=True),
        lax.all_gather(gain_query, "shard", axis=0, tiled=True),
        lax.all_gather(gain_key, "shard", axis=0, tiled=True),
    )
    ffn_full = (
        lax.all_gather(gain_mid, "shard", axis=0, tiled=True),
        lax.all_gather(w_gate, "shard", axis=0, tiled=True),
        lax.all_gather(w_up, "shard", axis=0, tiled=True),
        lax.all_gather(w_down, "shard", axis=1, tiled=True),
    )
    gain_one = attn_full[0].astype(jnp.float32)
    gain_qnorm = attn_full[6].astype(jnp.float32)
    gain_knorm = attn_full[7].astype(jnp.float32)
    gain_two = ffn_full[0].astype(jnp.float32)
    places = lax.axis_index("ctx") * length + jnp.arange(length, dtype=jnp.int32)
    key_places = jnp.arange(total_len, dtype=jnp.int32)
    segment, parent_seg, grand_seg, position = tree_layout(seg_lengths[0], seg_parents[0], places)
    key_segment = tree_layout(seg_lengths[0], seg_parents[0], key_places)[0]
    allowed = (
        (key_segment[None, :] == segment[:, None])
        | (key_segment[None, :] == parent_seg[:, None])
        | (key_segment[None, :] == grand_seg[:, None])
    ) & (key_places[None, :] <= places[:, None])
    allowed = allowed[:, None, None, :]
    cosine_table, sine_table = rope_tables(position, HD)
    inputs = tokens.astype(jnp.float32)
    factor_one = rms_scale(inputs)
    normed = (inputs * factor_one * gain_one).astype(jnp.bfloat16)
    q_pre = jnp.dot(normed, attn_full[1], preferred_element_type=jnp.float32).reshape(
        length, local_heads, HD
    )
    k_pre = jnp.dot(normed, attn_full[2], preferred_element_type=jnp.float32).reshape(
        length, local_kv, HD
    )
    value_low = jnp.dot(normed, attn_full[3], preferred_element_type=jnp.float32).astype(
        jnp.bfloat16
    )
    gate_pre = jnp.dot(normed, attn_full[4], preferred_element_type=jnp.float32).reshape(
        length, local_heads, HD
    )
    factor_q = rms_scale(q_pre)
    factor_k = rms_scale(k_pre)
    query_low = rotate(q_pre * factor_q * gain_qnorm, cosine_table, sine_table).astype(jnp.bfloat16)
    key_low = rotate(k_pre * factor_k * gain_knorm, cosine_table, sine_table).astype(jnp.bfloat16)
    key_rows, value_rows = (
        lax.all_gather(key_low.reshape(length, local_kv * HD), "ctx", axis=0, tiled=True),
        lax.all_gather(value_low, "ctx", axis=0, tiled=True),
    )
    key_all = key_rows.reshape(total_len, local_kv, HD)
    value_all = value_rows.reshape(total_len, local_kv, HD)
    query_group = query_low.reshape(length, local_kv, group, HD)
    scores = (
        jnp.einsum("tgrd,jgd->tgrj", query_group, key_all, preferred_element_type=jnp.float32)
        * scale
    )
    scores = jnp.where(allowed, scores, NEG)
    probs = jnp.exp(scores - jnp.max(scores, axis=-1, keepdims=True))
    probs = probs / jnp.sum(probs, axis=-1, keepdims=True)
    probs_low = probs.astype(jnp.bfloat16)
    attended = jnp.einsum(
        "tgrj,jgd->tgrd", probs_low, value_all, preferred_element_type=jnp.float32
    ).reshape(length, local_heads, HD)
    sigmoid_gate = jax.nn.sigmoid(gate_pre)
    gated = (attended * sigmoid_gate).astype(jnp.bfloat16).reshape(length, local_heads * HD)
    attn_part = jnp.dot(gated, attn_full[5], preferred_element_type=jnp.float32)
    middle = inputs + lax.psum(attn_part, "tp")
    factor_two = rms_scale(middle)
    normed_mid = (middle * factor_two * gain_two).astype(jnp.bfloat16)
    gate_val = jnp.dot(normed_mid, ffn_full[1], preferred_element_type=jnp.float32)
    up_val = jnp.dot(normed_mid, ffn_full[2], preferred_element_type=jnp.float32)
    sigmoid_ffn = jax.nn.sigmoid(gate_val)
    hidden = (gate_val * sigmoid_ffn * up_val).astype(jnp.bfloat16)
    ffn_part = jnp.dot(hidden, ffn_full[3], preferred_element_type=jnp.float32)
    layer_out = middle + lax.psum(ffn_part.astype(jnp.bfloat16), "tp").astype(jnp.float32)
    weights_all = (
        lax.all_gather(gain_in, "shard", axis=0, tiled=True),
        lax.all_gather(w_query, "shard", axis=0, tiled=True),
        lax.all_gather(w_key, "shard", axis=0, tiled=True),
        lax.all_gather(w_value, "shard", axis=0, tiled=True),
        lax.all_gather(w_gate_attn, "shard", axis=0, tiled=True),
        lax.all_gather(w_out, "shard", axis=1, tiled=True),
        lax.all_gather(gain_query, "shard", axis=0, tiled=True),
        lax.all_gather(gain_key, "shard", axis=0, tiled=True),
        lax.all_gather(gain_mid, "shard", axis=0, tiled=True),
        lax.all_gather(w_gate, "shard", axis=0, tiled=True),
        lax.all_gather(w_up, "shard", axis=0, tiled=True),
        lax.all_gather(w_down, "shard", axis=1, tiled=True),
    )
    attn_back = weights_all[:8]
    ffn_back = weights_all[8:]
    grad_top = cotangent.astype(jnp.float32)
    d_hidden = times_back(cotangent, ffn_back[3])
    d_gate = (d_hidden * up_val * sigmoid_ffn * (1.0 + gate_val * (1.0 - sigmoid_ffn))).astype(
        jnp.bfloat16
    )
    d_up = (d_hidden * gate_val * sigmoid_ffn).astype(jnp.bfloat16)
    ffn_rows = lax.psum_scatter(
        jnp.concatenate(
            [
                contract_rows(normed_mid, d_gate),
                contract_rows(normed_mid, d_up),
                contract_rows(cotangent, hidden),
            ],
            axis=1,
        ).astype(jnp.bfloat16),
        "shard",
        scatter_dimension=0,
        tiled=True,
    )
    d_normed_mid = lax.psum(times_back(d_gate, ffn_back[1]) + times_back(d_up, ffn_back[2]), "tp")
    mid_terms = d_normed_mid * middle * factor_two
    d_middle = grad_top + norm_back(
        d_normed_mid, middle, factor_two, ffn_back[0].astype(jnp.float32)
    )
    d_middle_low = d_middle.astype(jnp.bfloat16)
    d_gated = times_back(d_middle_low, attn_back[5]).reshape(length, local_heads, HD)
    d_attended = (d_gated * sigmoid_gate).astype(jnp.bfloat16).reshape(length, local_kv, group, HD)
    d_gate_pre = (
        (d_gated * attended * sigmoid_gate * (1.0 - sigmoid_gate))
        .astype(jnp.bfloat16)
        .reshape(length, local_heads * HD)
    )
    d_probs = jnp.einsum(
        "tgrd,jgd->tgrj", d_attended, value_all, preferred_element_type=jnp.float32
    )
    d_scores = (probs * (d_probs - jnp.sum(probs * d_probs, axis=-1, keepdims=True))).astype(
        jnp.bfloat16
    )
    d_query = (
        jnp.einsum("tgrj,jgd->tgrd", d_scores, key_all, preferred_element_type=jnp.float32).reshape(
            length, local_heads, HD
        )
        * scale
    )
    d_key_rows = (
        jnp.einsum("tgrj,tgrd->jgd", d_scores, query_group, preferred_element_type=jnp.float32)
        * scale
    )
    d_value_rows = jnp.einsum(
        "tgrj,tgrd->jgd", probs_low, d_attended, preferred_element_type=jnp.float32
    )
    kv_grad_rows = lax.psum_scatter(
        jnp.concatenate(
            [
                d_key_rows.reshape(lax.axis_size("ctx") * length, local_kv * HD),
                d_value_rows.reshape(lax.axis_size("ctx") * length, local_kv * HD),
            ],
            axis=1,
        ).astype(jnp.bfloat16),
        "ctx",
        scatter_dimension=0,
        tiled=True,
    ).astype(jnp.float32)
    d_key = kv_grad_rows[:, : local_kv * HD].reshape(length, local_kv, HD)
    d_value_low = kv_grad_rows[:, local_kv * HD :].astype(jnp.bfloat16)
    d_qhead = turn_back(d_query, cosine_table, sine_table)
    d_khead = turn_back(d_key, cosine_table, sine_table)
    q_terms_part = jnp.sum(d_qhead * q_pre * factor_q, axis=1)
    k_terms_part = jnp.sum(d_khead * k_pre * factor_k, axis=1)
    d_q_pre = (
        norm_back(d_qhead, q_pre, factor_q, gain_qnorm)
        .astype(jnp.bfloat16)
        .reshape(length, local_heads * HD)
    )
    d_k_pre = (
        norm_back(d_khead, k_pre, factor_k, gain_knorm)
        .astype(jnp.bfloat16)
        .reshape(length, local_kv * HD)
    )
    normed_part = (
        times_back(d_q_pre, attn_back[1])
        + times_back(d_k_pre, attn_back[2])
        + times_back(d_value_low, attn_back[3])
        + times_back(d_gate_pre, attn_back[4])
    )
    d_normed, q_terms, k_terms = (
        lax.psum(normed_part.astype(jnp.bfloat16), "tp").astype(jnp.float32),
        lax.psum(q_terms_part.astype(jnp.bfloat16), "tp").astype(jnp.float32),
        lax.psum(k_terms_part.astype(jnp.bfloat16), "tp").astype(jnp.float32),
    )
    in_terms = d_normed * inputs * factor_one
    input_grad = d_middle + norm_back(
        d_normed, inputs, factor_one, attn_back[0].astype(jnp.float32)
    )
    attn_sums = (
        lax.psum_scatter(
            jnp.sum(in_terms, axis=0).astype(jnp.bfloat16), "shard", scatter_dimension=0, tiled=True
        ).astype(jnp.float32),
        lax.psum_scatter(
            contract_rows(normed, d_q_pre).astype(jnp.bfloat16),
            "shard",
            scatter_dimension=0,
            tiled=True,
        ).astype(jnp.float32),
        lax.psum_scatter(
            contract_rows(normed, d_k_pre).astype(jnp.bfloat16),
            "shard",
            scatter_dimension=0,
            tiled=True,
        ).astype(jnp.float32),
        lax.psum_scatter(
            contract_rows(normed, d_value_low).astype(jnp.bfloat16),
            "shard",
            scatter_dimension=0,
            tiled=True,
        ).astype(jnp.float32),
        lax.psum_scatter(
            contract_rows(normed, d_gate_pre).astype(jnp.bfloat16),
            "shard",
            scatter_dimension=0,
            tiled=True,
        ).astype(jnp.float32),
        lax.psum_scatter(
            contract_rows(gated, d_middle_low).astype(jnp.bfloat16),
            "shard",
            scatter_dimension=1,
            tiled=True,
        ).astype(jnp.float32),
        lax.psum_scatter(
            jnp.sum(q_terms, axis=0).astype(jnp.bfloat16), "shard", scatter_dimension=0, tiled=True
        ).astype(jnp.float32),
        lax.psum_scatter(
            jnp.sum(k_terms, axis=0).astype(jnp.bfloat16), "shard", scatter_dimension=0, tiled=True
        ).astype(jnp.float32),
        lax.psum_scatter(
            jnp.sum(mid_terms, axis=0).astype(jnp.bfloat16),
            "shard",
            scatter_dimension=0,
            tiled=True,
        ).astype(jnp.float32),
    )
    summed = (
        lax.psum(attn_sums[0].astype(jnp.bfloat16), "ctx").astype(jnp.float32),
        lax.psum(attn_sums[1].astype(jnp.bfloat16), "ctx").astype(jnp.float32),
        lax.psum(attn_sums[2].astype(jnp.bfloat16), "ctx").astype(jnp.float32),
        lax.psum(attn_sums[3].astype(jnp.bfloat16), "ctx").astype(jnp.float32),
        lax.psum(attn_sums[4].astype(jnp.bfloat16), "ctx").astype(jnp.float32),
        lax.psum(attn_sums[5].astype(jnp.bfloat16), "ctx").astype(jnp.float32),
        lax.psum(attn_sums[6].astype(jnp.bfloat16), "ctx").astype(jnp.float32),
        lax.psum(attn_sums[7].astype(jnp.bfloat16), "ctx").astype(jnp.float32),
        lax.psum(attn_sums[8].astype(jnp.bfloat16), "ctx").astype(jnp.float32),
        lax.psum(ffn_rows, "ctx").astype(jnp.float32),
    )
    ffn_summed = summed[9]
    grad_gate = ffn_summed[:, :hidden_cols]
    grad_up = ffn_summed[:, hidden_cols : 2 * hidden_cols]
    grad_down = ffn_summed[:, 2 * hidden_cols :].T
    return (
        layer_out,
        input_grad,
        summed[0],
        summed[1],
        summed[2],
        summed[3],
        summed[4],
        summed[5],
        summed[6],
        summed[7],
        summed[8],
        grad_gate,
        grad_up,
        grad_down,
    )


def solution(mesh):
    return jax.shard_map(
        shards,
        mesh=mesh,
        in_specs=(
            P(("shard", "ctx"), None),
            P("shard", None),
            P("shard", None),
            P("shard"),
            P("shard", "tp"),
            P("shard", "tp"),
            P("shard", "tp"),
            P("shard", "tp"),
            P("tp", "shard"),
            P("shard"),
            P("shard"),
            P("shard"),
            P("shard", "tp"),
            P("shard", "tp"),
            P("tp", "shard"),
            P(("shard", "ctx"), None),
        ),
        out_specs=(
            P(("shard", "ctx"), None),
            P(("shard", "ctx"), None),
            P("shard"),
            P("shard", "tp"),
            P("shard", "tp"),
            P("shard", "tp"),
            P("shard", "tp"),
            P("tp", "shard"),
            P("shard"),
            P("shard"),
            P("shard"),
            P("shard", "tp"),
            P("shard", "tp"),
            P("tp", "shard"),
        ),
        check_vma=False,
    )
```

profile of v0, /device:TPU:1, one launch (start us, length us, event | category | flops | bytes accessed | tf_op | source)
XLA Modules:
  0.0 1598.5 jit_solution(4900241033887237965)
XLA Ops:
  14.3 34.2 %all-reduce.7 = (bf16[128]{0:T(256)(128)(2,1)S(1)}, bf16[128]{0:T(256)(128)(2,1)S(1)}) all-reduce(bf16[128]{0:T(256)(128)(2,1)S(1)} %dynamic-update-slice, bf16[128]{0:T(256)(128)(2,1)S(1)} %dynamic-update-slice.1), channel_id=1, replica_groups=mesh['shard'=16,'ctx'=4,'tp'=2] {'shard'}, use_global_device_ids=true, to_apply=%add | all-reduce | flops 256 | bytes 1024
  49.0 24.4 %all-gather = bf16[16,1,128]{2,1,0:T(2,128)(2,1)S(1)} all-gather(bf16[1,1,128]{2,1,0:T(2,128)(2,1)} %bitcast.259), channel_id=1, replica_groups=mesh['shard'=16,'ctx'=4,'tp'=2] {'shard'}, dimensions={0}, use_global_device_ids=true | all-gather | bytes 4352 | tf_op jit(solution)/shard_map/all_gather | solution.py:107
  80.3 2.1 fusion.64
  84.5 12.3 all_gather.57
  98.1 14.2 all-gather.11.cloned.1.call-done
  112.3 2.1 convolution_convert_fusion.8
  114.4 11.3 all_gather.54
  126.6 43.0 %all-gather.15.cloned.1.call-done = bf16[2048,1024]{1,0:T(8,128)(2,1)} async-done(((bf16[128,1024]{1,0:T(8,128)(2,1)}), bf16[2048,1024]{1,0:T(8,128)(2,1)}) %all-gather.15.cloned.1.call-update) | async-done | bytes 4194320 | tf_op jit(solution)/shard_map/all_gather | solution.py:108
  169.5 2.9 fusion.62
  173.8 3.1 fusion.71
  176.9 2.9 fusion.31
  181.0 45.6 %all-gather.17.cloned.1.call-done = bf16[2048,1024]{1,0:T(8,128)(2,1)} async-done(((bf16[128,1024]{1,0:T(8,128)(2,1)}), bf16[2048,1024]{1,0:T(8,128)(2,1)}) %all-gather.17.cloned.1.call-update) | async-done | bytes 4194320 | tf_op jit(solution)/shard_map/all_gather | solution.py:111
  226.6 3.8 multiply_convert_fusion.6
  230.4 56.2 %all-gather.19.cloned.1.call-done = bf16[1024,2048]{1,0:T(8,128)(2,1)} async-done(((bf16[1024,128]{1,0:T(8,128)(2,1)}), bf16[1024,2048]{1,0:T(8,128)(2,1)}) %all-gather.19.cloned.1.call-update) | async-done | bytes 4194320 | tf_op jit(solution)/shard_map/all_gather | solution.py:112
  286.6 3.9 fusion.72
  292.8 21.6 %all-gather.1 = bf16[16,1,128]{2,1,0:T(2,128)(2,1)S(1)} all-gather(bf16[1,1,128]{2,1,0:T(2,128)(2,1)S(1)} %bitcast.260), channel_id=1, replica_groups=mesh['shard'=16,'ctx'=4,'tp'=2] {'shard'}, dimensions={0}, use_global_device_ids=true | all-gather | bytes 4352 | tf_op jit(solution)/shard_map/all_gather | solution.py:117
  314.4 21.3 %all-reduce.18.cloned.1.call-done = f32[128,2048]{1,0:T(8,128)} async-done(((f32[128,2048]{1,0:T(8,128)}), f32[128,2048]{1,0:T(8,128)}) %all-reduce.18.cloned.1.call-update) | async-done | bytes 1048592 | tf_op jit(solution)/shard_map/psum | solution.py:177
  338.3 92.3 %all-gather.23.cloned.1.call-done = bf16[2048,3072]{1,0:T(8,128)(2,1)} async-done(((bf16[128,3072]{1,0:T(8,128)(2,1)}), bf16[2048,3072]{1,0:T(8,128)(2,1)}) %all-gather.23.cloned.1.call-update) | async-done | bytes 12582928 | tf_op jit(solution)/shard_map/all_gather | solution.py:119
  430.6 7.6 fusion.74
  438.2 83.8 %all-gather.21.cloned.1.call-done = bf16[2048,3072]{1,0:T(8,128)(2,1)} async-done(((bf16[128,3072]{1,0:T(8,128)(2,1)}), bf16[2048,3072]{1,0:T(8,128)(2,1)}) %all-gather.21.cloned.1.call-update) | async-done | bytes 12582928 | tf_op jit(solution)/shard_map/all_gather | solution.py:118
  522.0 7.6 fusion.73
  529.6 94.4 %all-gather.25.cloned.1.call-done = bf16[3072,2048]{1,0:T(8,128)(2,1)} async-done(((bf16[3072,128]{1,0:T(8,128)(2,1)}), bf16[3072,2048]{1,0:T(8,128)(2,1)}) %all-gather.25.cloned.1.call-update) | async-done | bytes 12582928 | tf_op jit(solution)/shard_map/all_gather | solution.py:120
  624.0 11.7 multiply_convert_fusion
  635.7 10.2 fusion.75
  645.9 6.9 convolution_add_fusion.3
  652.9 44.6 %all-reduce.20.cloned.1.call-done = f32[128,2048]{1,0:T(8,128)} async-done(((f32[128,2048]{1,0:T(8,128)}), f32[128,2048]{1,0:T(8,128)}) %all-reduce.20.cloned.1.call-update) | async-done | bytes 1048592 | tf_op jit(solution)/shard_map/psum | solution.py:221
  701.2 2.3 multiply_convert_fusion.5
  705.3 3.1 fusion.7
  708.4 2.0 copy.200
  710.5 2.4 fusion.2
  715.4 2.1 copy.199
  717.5 2.3 pad_maximum_fusion.1
  719.9 4.5 convolution_convert_fusion.2
  724.4 6.3 copy.201
  730.8 12.6 reduce-scatter.10.cloned.1.call-done
  743.4 3.1 convolution_convert_fusion.5
  751.3 2.1 multiply_reduce_fusion.6
  754.2 2.1 convolution_convert_fusion.6
  756.4 3.3 convolution_convert_fusion.3
  760.8 2.1 copy.160
  763.9 2.1 copy.162
  769.5 2.1 copy.161
  771.6 2.0 copy.198
  774.1 2.0 fusion.26
  776.8 3.4 convolution_convert_fusion.4
  781.3 7.6 convert_bitcast_fusion
  788.9 6.4 convolution_convert_fusion
  795.3 6.6 convolution_convert_fusion.1
  801.9 25.9 %pad_maximum_fusion = bf16[2048,9216]{1,0:T(8,128)(2,1)} fusion(bf16[2048,3072]{1,0:T(8,128)(2,1)} %convert_bitcast_fusion, bf16[2048,3072]{1,0:T(8,128)(2,1)} %convolution_convert_fusion, bf16[2048,3072]{1,0:T(8,128)(2,1)} %convolution_convert_fusion.1), kind=kLoop, calls=%fused_computation.1 | loop fusion | flops 113246208 | bytes 75497472 | tf_op jit(solution)/shard_map/concatenate | solution.py:209
  827.9 7.4 convolution_convert_fusion.7
  837.2 2.6 convolution_add_fusion.2
  842.0 2.3 fusion.1
  846.2 54.8 %reduce-scatter.16.cloned.1.call-done = bf16[128,512]{1,0:T(8,128)(2,1)} async-done(((bf16[2048,512]{1,0:T(8,128)(2,1)}), bf16[128,512]{1,0:T(8,128)(2,1)}) %reduce-scatter.16.cloned.1.call-update) | async-done | bytes 131088 | tf_op jit(solution)/shard_map/reduce_scatter | solution.py:312
  901.0 73.8 %reduce-scatter.14.cloned.1.call-done = bf16[128,512]{1,0:T(8,128)(2,1)} async-done(((bf16[2048,512]{1,0:T(8,128)(2,1)}), bf16[128,512]{1,0:T(8,128)(2,1)}) %reduce-scatter.14.cloned.1.call-update) | async-done | bytes 131088 | tf_op jit(solution)/shard_map/reduce_scatter | solution.py:306
  974.8 83.9 %reduce-scatter.18.cloned.1.call-done = bf16[128,1024]{1,0:T(8,128)(2,1)} async-done(((bf16[2048,1024]{1,0:T(8,128)(2,1)}), bf16[128,1024]{1,0:T(8,128)(2,1)}) %reduce-scatter.18.cloned.1.call-update) | async-done | bytes 262160 | tf_op jit(solution)/shard_map/reduce_scatter | solution.py:318
  1058.6 83.7 %reduce-scatter.12.cloned.1.call-done = bf16[128,1024]{1,0:T(8,128)(2,1)} async-done(((bf16[2048,1024]{1,0:T(8,128)(2,1)}), bf16[128,1024]{1,0:T(8,128)(2,1)}) %reduce-scatter.12.cloned.1.call-update) | async-done | bytes 262160 | tf_op jit(solution)/shard_map/reduce_scatter | solution.py:300
  1142.3 269.7 %reduce-scatter.20.cloned.1.call-done = bf16[128,9216]{1,0:T(8,128)(2,1)} async-done(((bf16[2048,9216]{1,0:T(8,128)(2,1)}), bf16[128,9216]{1,0:T(8,128)(2,1)}) %reduce-scatter.20.cloned.1.call-update) | async-done | bytes 2359312 | tf_op jit(solution)/shard_map/reduce_scatter | solution.py:208
  1413.4 30.5 %all-reduce.24.cloned.1.call-done = (bf16[128,128]{0,1:T(8,128)(2,1)}, bf16[128,128]{1,0:T(8,128)(2,1)}) async-done(((bf16[128,128]{0,1:T(8,128)(2,1)}, bf16[128,128]{1,0:T(8,128)(2,1)}), (bf16[128,128]{0,1:T(8,128)(2,1)}, bf16[128,128]{1,0:T(8,128)(2,1)})) %all-reduce.24.cloned.1.call-update) | async-done | bytes 65552 | tf_op jit(solution)/shard_map/psum | solution.py:289
  1445.6 49.9 %all-reduce.26.cloned.1.call-done = (bf16[128,2048]{1,0:T(8,128)(2,1)}, bf16[128,2048]{1,0:T(8,128)(2,1)}) async-done(((bf16[128,2048]{1,0:T(8,128)(2,1)}, bf16[128,2048]{1,0:T(8,128)(2,1)}), (bf16[128,2048]{1,0:T(8,128)(2,1)}, bf16[128,2048]{1,0:T(8,128)(2,1)})) %all-reduce.26.cloned.1.call-update) | async-done | bytes 1048592 | tf_op jit(solution)/shard_map/psum | solution.py:185
  1496.8 34.1 %all-reduce.6 = (bf16[2048]{0:T(1024)(128)(2,1)S(1)}, bf16[128]{0:T(256)(128)(2,1)S(1)}, bf16[128]{0:T(256)(128)(2,1)S(1)}, bf16[2048]{0:T(1024)(128)(2,1)S(1)}) all-reduce(bf16[2048]{0:T(1024)(128)(2,1)S(1)} %get-tuple-element.88, bf16[128]{0:T(256)(128)(2,1)S(1)} %reduce_sum.258, ...), channel_id=3, replica_groups=mesh['shard'=16,'ctx'=4,'tp'=2] {'shard'}, use_global_device_ids=true, to_apply=%region_27.28.clone | all-reduce | flops 4352 | bytes 17408
  1531.2 8.6 all-reduce.8
  1541.9 2.1 convert_add_fusion.1
  1545.5 35.5 %all-reduce.22.cloned.1.call-done = (bf16[128,1024]{1,0:T(8,128)(2,1)}, bf16[128,512]{1,0:T(8,128)(2,1)}, bf16[128,512]{1,0:T(8,128)(2,1)}, bf16[128,1024]{1,0:T...) async-done(((bf16[128,1024]{1,0:T(8,128)(2,1)}, bf16[128,512]{1,0:T(8,128)(2,1)}, bf16[128,512]{1,0:T(8,128)(2,1)}, bf16[128,1024]{1,0:T(8,128)(2,1)}, ...) | async-done | bytes 3407888 | tf_op jit(solution)/shard_map/psum | solution.py:345
  1581.0 3.5 fusion.67
  (275 shorter events, 66.2 us)
Async XLA Ops:
  7.2 71.6 %copy-start = (bf16[128,2048]{1,0:T(8,128)(2,1)S(1)}, bf16[128,2048]{1,0:T(8,128)(2,1)}, u32[]{:S(2)}) copy-start(bf16[128,2048]{1,0:T(8,128)(2,1)} %param.16) | copy-start | bytes 1572868
  7.2 73.1 %all-gather.13.cloned.1.call-start = ((), (), s32[]{:S(2)}) async-start(), calls=%async_computation.8 | async-start | bytes 2228224 | tf_op jit(solution)/shard_map/all_gather | solution.py:109
  7.9 104.3 %all-gather.11.cloned.1.call-start = ((), (), s32[]{:S(2)}) async-start(), calls=%async_computation.7 | async-start | bytes 2228224 | tf_op jit(solution)/shard_map/all_gather | solution.py:110
  8.7 160.9 %all-gather.15.cloned.1.call-start = ((), (), s32[]{:S(2)}) async-start(), calls=%async_computation.9 | async-start | bytes 4456448 | tf_op jit(solution)/shard_map/all_gather | solution.py:108
  9.4 217.2 %all-gather.17.cloned.1.call-start = ((), (), s32[]{:S(2)}) async-start(), calls=%async_computation.10 | async-start | bytes 4456448 | tf_op jit(solution)/shard_map/all_gather | solution.py:111
  10.0 276.7 %all-gather.19.cloned.1.call-start = ((), (), s32[]{:S(2)}) async-start(), calls=%async_computation.11 | async-start | bytes 4456448 | tf_op jit(solution)/shard_map/all_gather | solution.py:112
  10.6 325.1 %all-reduce.18.cloned.1.call-start = ((), (), s32[]{:S(2)}) async-start(), calls=%async_computation.12 | async-start | bytes 2097152 | tf_op jit(solution)/shard_map/psum | solution.py:177
  48.5 35.0 %copy-start.53 = (f32[128]{0:T(128)}, f32[128]{0:T(128)S(1)}, u32[]{:S(2)}) copy-start(f32[128]{0:T(128)S(1)} %convert_element_type.192) | copy-start | bytes 1540
  78.6 5.3 copy-start.35
  79.5 147.1 %copy-start.45 = (f32[128]{0:T(128)}, f32[128]{0:T(128)S(1)}, u32[]{:S(2)}) copy-start(f32[128]{0:T(128)S(1)} %get-tuple-element.148) | copy-start | bytes 1540
  79.5 4.9 copy-start.47
  84.3 13.8 copy-start.16
  84.4 30.0 %copy-start.18 = (f32[128,4,128]{2,1,0:T(4,128)}, f32[128,4,128]{2,1,0:T(4,128)S(1)}, u32[]{:S(2)}) copy-start(f32[128,4,128]{2,1,0:T(4,128)S(1)} %mul.570) | copy-start | bytes 786436
  126.6 46.8 %copy-start.50 = (f32[128]{0:T(128)S(1)}, f32[128]{0:T(128)}, u32[]{:S(2)}) copy-start(f32[128]{0:T(128)} %convert_element_type.195) | copy-start | bytes 1540
  173.8 6.0 copy-start.31
  173.8 3.1 copy-start.37
  181.0 49.4 %copy-start.27 = (f32[128,1024]{1,0:T(8,128)}, f32[128,1024]{1,0:T(8,128)S(1)}, u32[]{:S(2)}) copy-start(f32[128,1024]{1,0:T(8,128)S(1)} %copy.154) | copy-start | bytes 1572868
  230.4 60.1 %copy-start.33 = (bf16[128,1024]{1,0:T(8,128)(2,1)}, bf16[128,1024]{1,0:T(8,128)(2,1)S(1)}, u32[]{:S(2)}) copy-start(bf16[128,1024]{1,0:T(8,128)(2,1)S(1)} %get-tuple-element.153) | copy-start | bytes 786436
  290.5 140.1 %all-gather.23.cloned.1.call-start = ((), (), s32[]{:S(2)}) async-start(), calls=%async_computation.14 | async-start | bytes 13369344 | tf_op jit(solution)/shard_map/all_gather | solution.py:119
  291.3 230.7 %all-gather.21.cloned.1.call-start = ((), (), s32[]{:S(2)}) async-start(), calls=%async_computation.13 | async-start | bytes 13369344 | tf_op jit(solution)/shard_map/all_gather | solution.py:118
  292.0 332.0 %all-gather.25.cloned.1.call-start = ((), (), s32[]{:S(2)}) async-start(), calls=%async_computation.15 | async-start | bytes 13369344 | tf_op jit(solution)/shard_map/all_gather | solution.py:120
  292.8 404.8 %all-reduce.20.cloned.1.call-start = ((), (), s32[]{:S(2)}) async-start(), calls=%async_computation.16 | async-start | bytes 2097152 | tf_op jit(solution)/shard_map/psum | solution.py:221
  624.0 21.9 %slice-start = ((s8[12582912]{0:T(1024)(128)(4,1)}), s8[4194304]{0:T(1024)(128)(4,1)S(1)}, s32[]{:S(2)}) async-start(s8[12582912]{0:T(1024)(128)(4,1)} %bitcast.208), calls=%async_computation.27 | async-start | bytes 8388608
  624.0 21.9 %slice-start.1 = ((s8[12582912]{0:T(1024)(128)(4,1)}), s8[4194304]{0:T(1024)(128)(4,1)S(1)}, s32[]{:S(2)}) async-start(s8[12582912]{0:T(1024)(128)(4,1)} %bitcast.208), calls=%async_computation.28 | async-start | bytes 8388608
  635.7 10.2 slice-start.2
  652.9 46.4 %copy-start.56 = (f32[128]{0:T(128)S(1)}, f32[128]{0:T(128)}, u32[]{:S(2)}) copy-start(f32[128]{0:T(128)} %copy-done.55) | copy-start | bytes 1540
  652.9 46.4 %copy-start.60 = (f32[128]{0:T(128)S(1)}, f32[128]{0:T(128)}, u32[]{:S(2)}) copy-start(f32[128]{0:T(128)} %get-tuple-element.149) | copy-start | bytes 1540
  652.9 90.5 %reduce-scatter.10.cloned.1.call-start = ((), (), s32[]{:S(2)}) async-start(), calls=%async_computation.17 | async-start | bytes 1310720 | tf_op jit(solution)/shard_map/reduce_scatter | solution.py:253
  697.6 3.6 copy-start.2
  701.2 4.2 copy-start.32
  701.2 4.2 copy-start.58
  715.4 4.4 copy-start.34
  719.8 124.5 %reduce-scatter.22.cloned.1.call-start = ((), (), s32[]{:S(2)}) async-start(), calls=%async_computation.23 | async-start | bytes 4456448
  730.7 12.7 copy-start.46
  730.7 15.8 copy-start.52
  730.7 170.3 %reduce-scatter.16.cloned.1.call-start = ((), (), s32[]{:S(2)}) async-start(), calls=%async_computation.20 | async-start | bytes 2228224 | tf_op jit(solution)/shard_map/reduce_scatter | solution.py:312
  746.4 3.6 copy-start.36
  746.4 4.9 copy-start.13
  746.4 4.9 copy-start.54
  746.5 228.3 %reduce-scatter.14.cloned.1.call-start = ((), (), s32[]{:S(2)}) async-start(), calls=%async_computation.19 | async-start | bytes 2228224 | tf_op jit(solution)/shard_map/reduce_scatter | solution.py:306
  750.0 3.9 copy-start.17
  750.0 3.9 copy-start.19
  750.0 3.9 copy-start.29
  750.0 3.9 copy-start.48
  756.3 302.3 %reduce-scatter.18.cloned.1.call-start = ((), (), s32[]{:S(2)}) async-start(), calls=%async_computation.21 | async-start | bytes 4456448 | tf_op jit(solution)/shard_map/reduce_scatter | solution.py:318
  759.7 3.2 copy-start.51
  759.7 3.2 copy-start.49
  759.7 382.6 %reduce-scatter.12.cloned.1.call-start = ((), (), s32[]{:S(2)}) async-start(), calls=%async_computation.18 | async-start | bytes 4456448 | tf_op jit(solution)/shard_map/reduce_scatter | solution.py:300
  762.9 4.8 copy-start.42
  769.4 4.7 copy-start.10
  780.2 631.8 %reduce-scatter.20.cloned.1.call-start = ((), (), s32[]{:S(2)}) async-start(), calls=%async_computation.22 | async-start | bytes 40108032 | tf_op jit(solution)/shard_map/reduce_scatter | solution.py:208
  781.3 7.6 copy-start.15
  788.9 6.4 copy-start.14
  827.8 616.1 %all-reduce.24.cloned.1.call-start = ((), (), s32[]{:S(2)}) async-start(), calls=%async_computation.25 | async-start | bytes 131072 | tf_op jit(solution)/shard_map/psum | solution.py:289
  827.9 7.4 copy-start.1
  827.9 7.4 copy-start.22
  836.9 658.6 %all-reduce.26.cloned.1.call-start = ((), (), s32[]{:S(2)}) async-start(), calls=%async_computation.26 | async-start | bytes 2097152 | tf_op jit(solution)/shard_map/psum | solution.py:185
  844.3 736.7 %all-reduce.22.cloned.1.call-start = ((), (), s32[]{:S(2)}) async-start(), calls=%async_computation.24 | async-start | bytes 6815744 | tf_op jit(solution)/shard_map/psum | solution.py:345
  1412.0 132.0 %copy-start.4 = (f32[128,2048]{1,0:T(8,128)S(1)}, f32[128,2048]{1,0:T(8,128)}, u32[]{:S(2)}) copy-start(f32[128,2048]{1,0:T(8,128)} %copy-done.3) | copy-start | bytes 3145732
  1412.1 132.0 %copy-start.59 = (f32[128]{0:T(128)S(1)}, f32[128]{0:T(128)}, u32[]{:S(2)}) copy-start(f32[128]{0:T(128)} %get-tuple-element.147) | copy-start | bytes 1540
  1539.9 4.2 copy-start.24
  1581.0 3.5 copy-start.5
  1584.6 3.2 copy-start.40
  1585.1 3.6 copy-start.39
  (21 other events, 38.4 us)
Sparse Core Ops, SparseCore 0:
  10.4 51.9 all-gather.12
  64.9 47.3 all-gather.10
  114.7 54.8 all-gather.14
  171.8 54.7 all-gather.16
  228.7 57.8 all-gather.18
  290.7 44.9 all-reduce.17
  338.3 92.2 all-gather.22
  433.3 88.6 all-gather.20
  524.5 99.4 all-gather.24
  653.0 44.5 all-reduce.19
  720.0 23.3 reduce-scatter.9
  747.8 79.8 reduce-scatter.21
  831.6 69.3 reduce-scatter.15
  904.8 69.9 reduce-scatter.13
  978.7 79.9 reduce-scatter.17
  1063.1 79.1 reduce-scatter.11
  1146.7 265.2 reduce-scatter.19
  1415.6 28.2 all-reduce.23
  1447.1 48.2 all-reduce.25
  1498.7 82.2 all-reduce.21
where the time goes:
time: 1610 us; the launch traced here: 1600 us
  waiting for transfers between devices  1190 us (74%)
  blocking collectives  146 us (9%)
  matrix products  127 us (8%)
  other arithmetic  65.8 us (4%)
  local copies, waits for them, and re-layouts  45.2 us (3%)
  between operations  17.7 us (1%)
    reduce_scatter x1, waiting for transfers between devices, shards(): lax.psum_scatter(jnp.concatenate([contract_rows(normed_mid, d_gate), cont...  270 us
    all_gather x1, waiting for transfers between devices, shards(): lax.all_gather(w_down, 'shard', axis=1, tiled=True)  94.4 us
    all_gather x1, waiting for transfers between devices, shards(): lax.all_gather(w_up, 'shard', axis=0, tiled=True)  92.3 us
    reduce_scatter x1, waiting for transfers between devices, shards(): lax.psum_scatter(contract_rows(normed, d_gate_pre).astype(jnp.bfloat16),...  83.9 us
    all_gather x1, waiting for transfers between devices, shards(): lax.all_gather(w_gate, 'shard', axis=0, tiled=True)  83.8 us
    reduce_scatter x1, waiting for transfers between devices, shards(): lax.psum_scatter(contract_rows(normed, d_q_pre).astype(jnp.bfloat16), 'sh...  83.7 us
    reduce_scatter x1, waiting for transfers between devices, shards(): lax.psum_scatter(contract_rows(normed, d_k_pre).astype(jnp.bfloat16), 'sh...  73.8 us
    unnamed x2, blocking collectives  68.3 us
  transfers between devices with their start and end apart: 20, of which 18 were waited for; matrix products, arithmetic and copies ran while one was open for 11% of the time, Pallas kernels for 0%

commit v1 on v0

v1 whole, which is shorter than its diff:
```python
import math

import jax
import jax.numpy as jnp
from jax import lax
from jax.sharding import PartitionSpec as P

HD = 128
EPS = 1e-06
BASE = 1000000.0
NEG = -1e30
F32 = jnp.float32
BF16 = jnp.bfloat16
PLANE = ("shard", "tp")


def lookup(onehot, table):
    return jnp.sum(onehot * table[None, :], axis=1)


def tree_layout(lengths, parents, places):
    labels = jnp.arange(lengths.shape[0], dtype=jnp.int32)
    ends = jnp.cumsum(lengths)
    starts = ends - lengths
    parent_hot = (parents[:, None] == labels[None, :]).astype(jnp.int32)
    grand = lookup(parent_hot, parents)
    parent_len = lookup(parent_hot, lengths)
    grand_hot = (grand[:, None] == labels[None, :]).astype(jnp.int32)
    grand_len = lookup(grand_hot, lengths)
    before = jnp.where(labels == 0, 0, parent_len + jnp.where(parents == 0, 0, grand_len))
    segment = jnp.sum((places[:, None] >= ends[None, :]).astype(jnp.int32), axis=1)
    token_hot = (segment[:, None] == labels[None, :]).astype(jnp.int32)
    position = places - lookup(token_hot, starts) + lookup(token_hot, before)
    return (segment, lookup(token_hot, parents), lookup(token_hot, grand), position)


def rope_tables(position, columns):
    halfway = columns // 2
    frequency = jnp.exp(jnp.arange(halfway, dtype=F32) * (-2.0 * math.log(BASE) / columns))
    angles = position.astype(F32)[:, None] * frequency[None, :]
    angles = jnp.concatenate([angles, angles], axis=1)
    return (jnp.cos(angles)[:, None, :], jnp.sin(angles)[:, None, :])


def rotate(inputs, cosine_table, sine_table):
    halfway = inputs.shape[-1] // 2
    turned = jnp.concatenate([-inputs[..., halfway:], inputs[..., :halfway]], axis=-1)
    return inputs * cosine_table + turned * sine_table


def turn_back(grads, cosine_table, sine_table):
    scaled = grads * sine_table
    halfway = grads.shape[-1] // 2
    return grads * cosine_table + jnp.concatenate(
        [scaled[..., halfway:], -scaled[..., :halfway]], axis=-1
    )


def rms_scale(inputs):
    return lax.rsqrt(jnp.mean(inputs * inputs, axis=-1, keepdims=True) + EPS)


def dot(left, right):
    return jnp.dot(left, right, preferred_element_type=F32)


def dot_rows(left, right):
    return lax.dot_general(left, right, (((0,), (0,)), ((), ())), preferred_element_type=F32)


def dot_back(left, right):
    return lax.dot_general(left, right, (((1,), (1,)), ((), ())), preferred_element_type=F32)


def make_shards(mesh):
    n_shard, n_ctx, n_tp = mesh.shape["shard"], mesh.shape["ctx"], mesh.shape["tp"]
    pairs = n_shard // 2

    def joint(pair, core, tp):
        return (pair * 2 + core) * n_tp + tp

    core_perm = [(i, i ^ 1) for i in range(n_shard)]
    planes = [
        [joint(pair, core, tp) for pair in range(pairs) for tp in range(n_tp)] for core in range(2)
    ]
    swap_perm = [
        edge
        for pair in range(pairs)
        for edge in (
            (joint(pair, 1, 0), joint(pair, 0, 1)),
            (joint(pair, 0, 1), joint(pair, 1, 0)),
        )
    ]
    across_perm = [(joint(pair, t, t), joint(pair, t, 1 - t)) for pair in range(pairs) for t in range(2)]

    def core_swap(value):
        return lax.ppermute(value, "shard", core_perm)

    def ctx_gather(value):
        wide = jnp.broadcast_to(value[None], (n_ctx,) + value.shape)
        return lax.all_to_all(wide, "ctx", 0, 0).reshape((-1,) + value.shape[1:])

    def ctx_scatter(value):
        split = value.reshape((n_ctx, value.shape[0] // n_ctx) + value.shape[1:])
        return jnp.sum(lax.all_to_all(split, "ctx", 0, 0).astype(F32), axis=0)

    def gather_tree(own):
        mine = ctx_gather(own)
        return jnp.concatenate([mine, core_swap(mine)], axis=0)

    def scatter_tree(part):
        half = part.shape[0] // 2
        received = core_swap(part[half:].astype(BF16))
        return ctx_scatter((part[:half] + received.astype(F32)).astype(BF16))

    def plane_gather(value):
        return lax.all_gather(value, PLANE, axis=0, tiled=True, axis_index_groups=planes)

    def plane_scatter(value):
        return lax.psum_scatter(
            value.astype(BF16), PLANE, scatter_dimension=0, tiled=True, axis_index_groups=planes
        )

    def shards(
        tokens,
        seg_lengths,
        seg_parents,
        gain_in,
        w_query,
        w_key,
        w_value,
        w_gate_attn,
        w_out,
        gain_query,
        gain_key,
        gain_mid,
        w_gate,
        w_up,
        w_down,
        cotangent,
    ):
        core = lax.axis_index("shard") % 2
        tp = lax.axis_index("tp")
        ctx = lax.axis_index("ctx")
        native = core == tp
        rows = tokens.shape[0] // 2
        scale = 1.0 / math.sqrt(HD)

        def swapped(value):
            return jnp.where(native, value, lax.ppermute(value, PLANE, swap_perm))

        def quarter(weight, axis):
            size = weight.shape[axis] // n_ctx
            return lax.dynamic_slice_in_dim(weight, ctx * size, size, axis)

        gain_one = gain_in.astype(F32)[:, None]
        gain_two = gain_mid.astype(F32)[:, None]
        first = jnp.concatenate(
            [quarter(w, 1) for w in (w_query, w_key, w_value, w_gate_attn)], axis=1
        )
        first = (first.astype(F32) * gain_one).astype(BF16)
        second = jnp.concatenate([quarter(w_gate, 1), quarter(w_up, 1)], axis=1)
        second = (second.astype(F32) * gain_two).astype(BF16)
        w1 = plane_gather(swapped(first))
        w_out_t = plane_gather(swapped(quarter(w_out, 0).T))
        w2 = plane_gather(swapped(second))
        w_down_t = plane_gather(swapped(quarter(w_down, 0).T))
        head_gains = lax.all_gather(
            jnp.concatenate([gain_query[None], gain_key[None]], axis=0), "shard", axis=1, tiled=True
        ).astype(F32)
        gain_q, gain_k = head_gains[0], head_gains[1]

        both = jnp.stack([tokens, cotangent])
        keep = lax.dynamic_slice_in_dim(both, core * rows, rows, 1)
        give = lax.dynamic_slice_in_dim(both, (1 - core) * rows, rows, 1)
        own = jnp.where(native, keep, core_swap(give))
        tree = jnp.concatenate([seg_lengths, seg_parents], axis=0)
        tree = jnp.where(native, tree, core_swap(tree))
        own_x, own_cot = own[0], own[1]
        x_all = gather_tree(own_x)
        cot_all = gather_tree(own_cot)

        length = x_all.shape[0]
        half_at = jnp.where(jnp.arange(2) == 0, core, 1 - core) * rows
        places = (
            half_at[:, None, None]
            + jnp.arange(n_ctx, dtype=jnp.int32)[None, :, None] * (2 * rows)
            + jnp.arange(rows, dtype=jnp.int32)[None, None, :]
        ).reshape(-1)
        segment, parent_seg, grand_seg, position = tree_layout(tree[0], tree[1], places)
        allowed = (
            (segment[None, :] == segment[:, None])
            | (segment[None, :] == parent_seg[:, None])
            | (segment[None, :] == grand_seg[:, None])
        ) & (places[None, :] <= places[:, None])
        cosine_table, sine_table = rope_tables(position, HD)

        x_f = x_all.astype(F32)
        xn = (x_f * rms_scale(x_f)).astype(BF16)
        qkvg = dot(xn, w1)
        q_pre = qkvg[:, : 2 * HD].reshape(length, 2, HD)
        k_pre = qkvg[:, 2 * HD : 3 * HD].reshape(length, 1, HD)
        value = qkvg[:, 3 * HD : 4 * HD].astype(BF16)
        gate_pre = qkvg[:, 4 * HD :].reshape(length, 2, HD)
        factor_q, factor_k = rms_scale(q_pre), rms_scale(k_pre)
        query = rotate(q_pre * factor_q * gain_q, cosine_table, sine_table).astype(BF16)
        key = rotate(k_pre * factor_k * gain_k, cosine_table, sine_table).astype(BF16)[:, 0]
        scores = jnp.einsum("trd,jd->rtj", query, key, preferred_element_type=F32) * scale
        scores = jnp.where(allowed[None], scores, NEG)
        probs = jnp.exp(scores - jnp.max(scores, axis=-1, keepdims=True))
        probs = probs / jnp.sum(probs, axis=-1, keepdims=True)
        probs_low = probs.astype(BF16)
        attended = jnp.einsum("rtj,jd->trd", probs_low, value, preferred_element_type=F32)
        sigmoid_gate = jax.nn.sigmoid(gate_pre)
        gated = (attended * sigmoid_gate).astype(BF16).reshape(length, 2 * HD)
        own_x_f = own_x.astype(F32)
        middle = own_x_f + scatter_tree(dot_back(gated, w_out_t))
        factor_two = rms_scale(middle)
        un = gather_tree((middle * factor_two).astype(BF16))

        gate_up = dot(un, w2)
        units = w_down_t.shape[1]
        gate_val, up_val = gate_up[:, :units], gate_up[:, units:]
        sig = jax.nn.sigmoid(gate_val)
        hidden = (gate_val * sig * up_val).astype(BF16)
        d_hidden = dot(cot_all, w_down_t)
        d_gate = (d_hidden * up_val * sig * (1.0 + gate_val * (1.0 - sig))).astype(BF16)
        d_up = (d_hidden * gate_val * sig).astype(BF16)
        d_gate_up = jnp.concatenate([d_gate, d_up], axis=1)
        layer_own = middle + scatter_tree(dot_back(hidden, w_down_t))
        d_un = scatter_tree(dot_back(d_gate_up, w2))
        d_middle = (
            own_cot.astype(F32)
            + factor_two * d_un
            - middle * factor_two**3 * jnp.mean(d_un * middle, axis=-1, keepdims=True)
        )
        mid_terms = jnp.sum(d_un * middle * factor_two, axis=0)
        d_middle_low = gather_tree(d_middle.astype(BF16))
        grad_ffn = plane_scatter(
            jnp.concatenate([dot_rows(un, d_gate_up), dot_rows(cot_all, hidden)], axis=1)
        )

        d_gated = dot(d_middle_low, w_out_t).reshape(length, 2, HD)
        d_attended = (d_gated * sigmoid_gate).astype(BF16)
        d_gate_pre = (d_gated * attended * sigmoid_gate * (1.0 - sigmoid_gate)).astype(BF16)
        d_probs = jnp.einsum("trd,jd->rtj", d_attended, value, preferred_element_type=F32)
        d_scores = (probs * (d_probs - jnp.sum(probs * d_probs, axis=-1, keepdims=True))).astype(BF16)
        d_query = jnp.einsum("rtj,jd->trd", d_scores, key, preferred_element_type=F32) * scale
        d_key = jnp.einsum("rtj,trd->jd", d_scores, query, preferred_element_type=F32) * scale
        d_value = jnp.einsum("rtj,trd->jd", probs_low, d_attended, preferred_element_type=F32)
        d_qhead = turn_back(d_query, cosine_table, sine_table)
        d_khead = turn_back(d_key[:, None], cosine_table, sine_table)
        q_terms = jnp.sum(d_qhead * q_pre * factor_q, axis=(0, 1))
        k_terms = jnp.sum(d_khead * k_pre * factor_k, axis=(0, 1))

        def head_back(grads, inputs, factor, gain):
            scaled = gain * grads
            return factor * scaled - inputs * factor**3 * jnp.mean(
                scaled * inputs, axis=-1, keepdims=True
            )

        d_q_pre = head_back(d_qhead, q_pre, factor_q, gain_q).astype(BF16).reshape(length, -1)
        d_k_pre = head_back(d_khead, k_pre, factor_k, gain_k).astype(BF16).reshape(length, -1)
        d_qkvg = jnp.concatenate(
            [d_q_pre, d_k_pre, d_value.astype(BF16), d_gate_pre.reshape(length, -1)], axis=1
        )
        d_xn = scatter_tree(dot_back(d_qkvg, w1))
        factor_one = rms_scale(own_x_f)
        input_own = (
            d_middle
            + factor_one * d_xn
            - own_x_f * factor_one**3 * jnp.mean(d_xn * own_x_f, axis=-1, keepdims=True)
        )
        in_terms = jnp.sum(d_xn * own_x_f * factor_one, axis=0)

        def spread(terms):
            per = terms.shape[0] // n_shard
            wide = jnp.pad(terms.reshape(n_shard, per), ((0, 0), (0, HD - per)))
            return wide.reshape(-1)

        columns = jnp.stack([in_terms, mid_terms, spread(q_terms), spread(k_terms)], axis=1)
        columns = jnp.pad(columns, ((0, 0), (0, HD - 4)))
        grad_attn = plane_scatter(
            jnp.concatenate(
                [dot_rows(xn, d_qkvg), dot_rows(d_middle_low, gated), columns], axis=1
            )
        )
        gains_part = grad_attn[:, -HD:]
        gains_part = (gains_part.astype(F32) + core_swap(gains_part).astype(F32)).astype(BF16)
        grad_attn = jnp.concatenate([grad_attn[:, :-HD], gains_part], axis=1)

        def owners(block):
            block = swapped(block)
            wide = jnp.broadcast_to(block[None], (n_ctx,) + block.shape)
            return lax.all_to_all(wide, "ctx", 0, 0).astype(F32)

        def side(parts):
            return parts.transpose(1, 0, 2).reshape(parts.shape[1], -1)

        def down(parts):
            return parts.transpose(0, 2, 1).reshape(-1, parts.shape[1])

        ffn = owners(grad_ffn)
        grad_gate = side(ffn[:, :, :units]) * gain_two
        grad_up = side(ffn[:, :, units : 2 * units]) * gain_two
        grad_down = down(ffn[:, :, 2 * units :])
        attn = owners(grad_attn)
        grad_query = side(attn[:, :, : 2 * HD]) * gain_one
        grad_key = side(attn[:, :, 2 * HD : 3 * HD]) * gain_one
        grad_value = side(attn[:, :, 3 * HD : 4 * HD]) * gain_one
        grad_gate_attn = side(attn[:, :, 4 * HD : 6 * HD]) * gain_one
        grad_out = down(attn[:, :, 6 * HD : 8 * HD])
        gains = jnp.sum(attn[:, :, 8 * HD :], axis=0)
        head_rows = gain_query.shape[0]

        def finish(part):
            low = part.astype(BF16)
            sibling = core_swap(low)
            full = jnp.where(
                core == 0,
                jnp.concatenate([low, sibling], axis=0),
                jnp.concatenate([sibling, low], axis=0),
            )
            return jnp.where(native, full, lax.ppermute(full, PLANE, across_perm)).astype(F32)

        return (
            finish(layer_own),
            finish(input_own),
            gains[:, 0] / gain_one[:, 0],
            grad_query,
            grad_key,
            grad_value,
            grad_gate_attn,
            grad_out,
            gains[:head_rows, 2],
            gains[:head_rows, 3],
            gains[:, 1] / gain_two[:, 0],
            grad_gate,
            grad_up,
            grad_down,
        )

    return shards


def solution(mesh):
    return jax.shard_map(
        make_shards(mesh),
        mesh=mesh,
        in_specs=(
            P(("shard", "ctx"), None),
            P("shard", None),
            P("shard", None),
            P("shard"),
            P("shard", "tp"),
            P("shard", "tp"),
            P("shard", "tp"),
            P("shard", "tp"),
            P("tp", "shard"),
            P("shard"),
            P("shard"),
            P("shard"),
            P("shard", "tp"),
            P("shard", "tp"),
            P("tp", "shard"),
            P(("shard", "ctx"), None),
        ),
        out_specs=(
            P(("shard", "ctx"), None),
            P(("shard", "ctx"), None),
            P("shard"),
            P("shard", "tp"),
            P("shard", "tp"),
            P("shard", "tp"),
            P("shard", "tp"),
            P("tp", "shard"),
            P("shard"),
            P("shard"),
            P("shard"),
            P("shard", "tp"),
            P("shard", "tp"),
            P("tp", "shard"),
        ),
        check_vma=False,
    )
```

time: 1610 us -> 612 us (0.38)
  waiting for transfers between devices: 1190 us -> 218 us
  matrix products: 127 us -> 62.5 us
  starting transfers between devices: 1.27 us -> 60.6 us
  blocking collectives: 146 us -> 111 us
  local copies, waits for them, and re-layouts: 45.2 us -> 70.4 us
    reduce_scatter x6 -> x0, waiting for transfers between devices: 578 us -> none  [the longest x1 270 us: shards(): lax.psum_scatter(jnp.concatenate([contract_rows(normed_mid, d_gate), cont...]
    all_gather x8 -> x4, waiting for transfers between devices: 429 us -> 38.7 us  [plane_gather(): lax.all_gather(value, PLANE, axis=0, tiled=True, axis_index_groups=planes)]
    psum x5 -> x0, waiting for transfers between devices: 182 us -> none  [the longest x1 49.9 us: shards(): lax.psum(ffn_part.astype(jnp.bfloat16), 'tp').astype(jnp.float32)]
    unnamed x21 -> x8, waiting for transfers between devices: 5.4 us -> 93.1 us
    all_to_all x0 -> x5, blocking collectives: none -> 85.8 us  [the longest x3 50.3 us: ctx_gather(): return lax.all_to_all(wide, 'ctx', 0, 0).reshape((-1,) + value.shape[1:])]
    unnamed x2 -> x0, blocking collectives: 68.3 us -> none
    dot_general x29 -> x17, matrix products: 124 us -> 59.1 us  [the longest x4 20.2 us: dot(): return jnp.dot(left, right, preferred_element_type=F32)]
    all_to_all x0 -> x5, waiting for transfers between devices: none -> 63.4 us  [the longest x2 27.4 us: owners(): return lax.all_to_all(wide, 'ctx', 0, 0).astype(F32)]
  transfers between devices with their start and end apart: 20 -> 32, of which waited for: 18 -> 18; matrix products, arithmetic and copies ran while one was open for 11% -> 20% of each run, Pallas kernels for 0% -> 0%
where the time goes in v1:
time: 612 us; the launch traced here: 601 us
  waiting for transfers between devices  218 us (36%)
  blocking collectives  111 us (18%)
  local copies, waits for them, and re-layouts  70.4 us (12%)
  other arithmetic  63 us (10%)
  matrix products  62.5 us (10%)
  starting transfers between devices  60.6 us (10%)
  between operations  15.7 us (3%)
    unnamed x8, waiting for transfers between devices  93.1 us
    all_to_all x3, blocking collectives, ctx_gather(): return lax.all_to_all(wide, 'ctx', 0, 0).reshape((-1,) + value.shape[1:])  50.3 us
    all_gather x4, waiting for transfers between devices, plane_gather(): lax.all_gather(value, PLANE, axis=0, tiled=True, axis_index_groups=planes)  38.7 us
    all_to_all x2, blocking collectives, ctx_scatter(): return jnp.sum(lax.all_to_all(split, 'ctx', 0, 0).astype(F32), axis=0)  35.4 us
    unnamed x179, local copies, waits for them, and re-layouts  32.1 us
    all_to_all x2, waiting for transfers between devices, owners(): return lax.all_to_all(wide, 'ctx', 0, 0).astype(F32)  27.4 us
    all_gather x1, blocking collectives, shards(): lax.all_gather(jnp.concatenate([gain_query[None], gain_key[None]], axis=0...  25.5 us
    ppermute x6, starting transfers between devices, swapped(): return jnp.where(native, value, lax.ppermute(value, PLANE, swap_perm))  22 us
  transfers between devices with their start and end apart: 32, of which 18 were waited for; matrix products, arithmetic and copies ran while one was open for 20% of the time, Pallas kernels for 0%

profile of v1, /device:TPU:1, one launch (start us, length us, event | category | flops | bytes accessed | tf_op | source)
XLA Modules:
  0.0 601.4 jit_solution(16203547630800446451)
XLA Ops:
  10.1 4.6 collective-permute-start.2
  14.8 3.3 collective-permute-done.2
  19.8 3.6 collective-permute-start.4
  28.2 3.6 collective-permute-start.7
  31.8 6.9 %collective-permute-done.7 = bf16[128,1536]{1,0:T(8,128)(2,1)S(1)} collective-permute-done((bf16[128,1536]{1,0:T(8,128)(2,1)S(1)}, bf16[128,1536]{1,0:T(8,128)(2,1)S(1)}, u32[]{:S(2)}, u32[]{:S(2)}) %collective-permute-start.7) | collective-permute-done | bytes 393248 | tf_op jit(solution)/shard_map/ppermute | solution.py:150
  41.3 2.8 collective-permute-start.8
  44.3 25.5 %all-gather = bf16[16,8,2]{1,2,0:T(2,128)(2,1)S(1)} all-gather(bf16[1,8,2]{1,2,0:T(2,128)(2,1)S(1)} %maximum_bitcast_fusion), channel_id=1, replica_groups=mesh['shard'=16,'ctx'=4,'tp'=2] {'shard'}, dimensions={0}, use_global_device_ids=true | all-gather | bytes 544 | tf_op jit(solution)/shard_map/all_gather | solution.py:168
  72.8 4.2 all-to-all-start
  77.5 14.1 %all-to-all-done = bf16[4,64,2048]{2,1,0:T(8,128)(2,1)S(1)} async-done(((bf16[4,64,2048]{2,1,0:T(8,128)(2,1)}), bf16[4,64,2048]{2,1,0:T(8,128)(2,1)S(1)}, u32[]{:S(2)}, u32[]{:S(2)}) %all-to-all-start) | async-done | bytes 1048608 | tf_op jit(solution)/shard_map/all_to_all | solution.py:101
  96.3 4.4 fusion.72
  111.2 2.4 fusion.36
  114.8 3.5 fusion.115
  118.3 3.1 multiply_convert_fusion.7
  121.4 2.0 fusion.124
  123.5 2.1 copy-done
  128.8 2.3 fusion.6
  131.1 17.3 %all_to_all.50 = bf16[4,64,2048]{2,1,0:T(8,128)(2,1)S(1)} all-to-all(bf16[4,64,2048]{2,1,0:T(8,128)(2,1)S(1)} %bitcast.289), channel_id=1, replica_groups=mesh['shard'=16,'ctx'=4,'tp'=2] {'ctx'}, dimensions={0} | all-to-all | bytes 2097152 | tf_op jit(solution)/shard_map/all_to_all | solution.py:105
  150.0 16.4 %all_to_all.51 = bf16[4,64,2048]{2,1,0:T(8,128)(2,1)S(1)} all-to-all(bf16[4,64,2048]{2,1,0:T(8,128)(2,1)S(1)} %broadcast_in_dim.51), channel_id=1, replica_groups=mesh['shard'=16,'ctx'=4,'tp'=2] {'ctx'}, dimensions={0} | all-to-all | bytes 2097152 | tf_op jit(solution)/shard_map/all_to_all | solution.py:101
  166.3 2.1 collective-permute-start.6
  168.6 18.1 %all_to_all.52 = bf16[4,64,2048]{2,1,0:T(8,128)(2,1)} all-to-all(bf16[4,64,2048]{2,1,0:T(8,128)(2,1)S(1)} %broadcast_in_dim.52), channel_id=1, replica_groups=mesh['shard'=16,'ctx'=4,'tp'=2] {'ctx'}, dimensions={0} | all-to-all | bytes 2097152 | tf_op jit(solution)/shard_map/all_to_all | solution.py:101
  187.8 8.6 %fusion.13 = f32[512,1536]{1,0:T(8,128)} fusion(bf16[2048,1536]{1,0:T(8,128)(2,1)} %all-gather.10.cloned.1.call-done, bf16[256,2048]{1,0:T(8,128)(2,1)} %collective-permute-done.6, bf16[256,2048]{1,0:T(8,128)(2,1)} %bitcast.303), kind=kOutput, calls=%fused_computation.46 | convolution fusion | flops 3225419776 | bytes 11534336 | tf_op jit(solution)/shard_map/dot_general | solution.py:64
  196.3 38.7 %all-gather.12.cloned.1.call-done = bf16[2048,768]{0,1:T(8,128)(2,1)} async-done(((bf16[128,768]{0,1:T(8,128)(2,1)}), bf16[2048,768]{0,1:T(8,128)(2,1)}) %all-gather.12.cloned.1.call-update) | async-done | bytes 3145744 | tf_op jit(solution)/shard_map/all_gather | solution.py:117
  235.0 6.6 %multiply_convert_fusion.1 = (bf16[512,768]{1,0:T(8,128)(2,1)S(1)}, bf16[512,768]{1,0:T(8,128)(2,1)S(1)}, bf16[512,768]{1,0:T(8,128)(2,1)}) fusion(f32[512,1536]{1,0:T(8,128)} %fusion.13, bf16[2048,768]{0,1:T(8,128)(2,1)} %all-gather.12.cloned.1.call-done, bf16[256,2048]{1,0:T(8,128)(2,1)S(1)} %collective-permute-done.12, bf16[256,2048]{1,0:T(8,128)(2,1)} %bitcast.40), kind=kOutput, calls=%fused_computation.41 | convolution fusion | flops 1621098496 | bytes 10747904 | tf_op jit(solution)/shard_map/dot_general | solution.py:64
  241.6 3.4 fusion.23
  246.8 2.3 collective-permute-done.13
  249.5 18.2 %all_to_all.53 = bf16[4,64,2048]{2,1,0:T(8,128)(2,1)S(1)} all-to-all(bf16[4,64,2048]{2,1,0:T(8,128)(2,1)S(1)} %bitcast.290), channel_id=1, replica_groups=mesh['shard'=16,'ctx'=4,'tp'=2] {'ctx'}, dimensions={0} | all-to-all | bytes 2097152 | tf_op jit(solution)/shard_map/all_to_all | solution.py:105
  269.5 15.9 %all_to_all.54 = bf16[4,64,2048]{2,1,0:T(8,128)(2,1)S(1)} all-to-all(bf16[4,64,2048]{2,1,0:T(8,128)(2,1)S(1)} %broadcast_in_dim.54), channel_id=1, replica_groups=mesh['shard'=16,'ctx'=4,'tp'=2] {'ctx'}, dimensions={0} | all-to-all | bytes 2097152 | tf_op jit(solution)/shard_map/all_to_all | solution.py:101
  285.3 3.2 collective-permute-start.14
  288.5 2.3 collective-permute-done.14
  292.8 3.0 fusion.15
  295.9 2.3 fusion.7
  312.4 3.9 fusion.61
  316.3 2.0 copy-done.16
  321.3 3.1 fusion.3
  324.4 4.4 all-to-all-start.7
  329.7 3.4 convolution_convert_fusion.3
  333.1 3.6 convolution_convert_fusion.1
  336.7 7.0 %all-to-all-done.7 = bf16[4,64,2048]{2,1,0:T(8,128)(2,1)} async-done(((bf16[4,64,2048]{2,1,0:T(8,128)(2,1)}), bf16[4,64,2048]{2,1,0:T(8,128)(2,1)}, u32[]{:S(2)}, u32[]{:S(2)}) %all-to-all-start.7) | async-done | bytes 1048608 | tf_op jit(solution)/shard_map/all_to_all | solution.py:105
  345.5 3.9 pad_maximum_fusion.1
  349.4 6.7 %copy.276 = bf16[2048,1152]{1,0:T(8,128)(2,1)} copy(bf16[2048,1152]{0,1:T(8,128)(2,1)} %pad_maximum_fusion.1) | data formatting | bytes 9437184
  357.3 3.5 convolution_convert_fusion.2
  360.8 5.0 convolution_convert_fusion
  365.8 11.2 %pad_maximum_fusion = bf16[2048,2304]{0,1:T(8,128)(2,1)} fusion(bf16[2048,768]{0,1:T(8,128)(2,1)S(1)} %convolution_convert_fusion.2, bf16[2048,1536]{0,1:T(8,128)(2,1)S(1)} %convolution_convert_fusion), kind=kLoop, calls=%fused_computation.1 | loop fusion | flops 18874368 | bytes 18874368 | tf_op jit(solution)/shard_map/concatenate | solution.py:240
  377.0 12.7 %copy.278 = bf16[2048,2304]{1,0:T(8,128)(2,1)} copy(bf16[2048,2304]{0,1:T(8,128)(2,1)} %pad_maximum_fusion) | data formatting | bytes 18874368
  389.7 3.7 fusion.125
  394.8 2.3 collective-permute-done.9
  398.3 4.4 all-to-all-start.3
  402.8 14.9 %all-to-all-done.3 = bf16[4,64,2048]{2,1,0:T(8,128)(2,1)} async-done(((bf16[4,64,2048]{2,1,0:T(8,128)(2,1)}), bf16[4,64,2048]{2,1,0:T(8,128)(2,1)}, u32[]{:S(2)}, u32[]{:S(2)}) %all-to-all-start.3) | async-done | bytes 1048608 | tf_op jit(solution)/shard_map/all_to_all | solution.py:105
  419.1 11.9 %reduce-scatter.7.cloned.1.call-done = bf16[128,1152]{1,0:T(8,128)(2,1)} async-done(((bf16[2048,1152]{1,0:T(8,128)(2,1)}), bf16[128,1152]{1,0:T(8,128)(2,1)}) %reduce-scatter.7.cloned.1.call-update) | async-done | bytes 294928
  431.9 2.4 collective-permute-start.18
  435.6 2.8 collective-permute-start.19
  442.1 81.1 %reduce-scatter.9.cloned.1.call-done = bf16[128,2304]{1,0:T(8,128)(2,1)} async-done(((bf16[2048,2304]{1,0:T(8,128)(2,1)}), bf16[128,2304]{1,0:T(8,128)(2,1)}) %reduce-scatter.9.cloned.1.call-update) | async-done | bytes 589840
  524.5 4.5 collective-permute-start.20
  530.3 4.1 all-to-all-start.8
  534.4 2.1 select_convert_fusion.1
  536.9 13.0 %all-to-all-done.8 = bf16[4,128,1152]{1,2,0:T(8,128)(2,1)S(1)} async-done(((bf16[4,128,1152]{1,2,0:T(8,128)(2,1)}), bf16[4,128,1152]{1,2,0:T(8,128)(2,1)S(1)}, u32[]{:S(2)}, u32[]{:S(2)}) %all-to-all-start.8) | async-done | bytes 1179680 | tf_op jit(solution)/shard_map/all_to_all | solution.py:295
  551.7 3.8 all-to-all-start.9
  555.5 2.1 select_convert_fusion
  563.2 2.0 copy.273
  565.2 2.0 copy.270
  570.5 14.4 %all-to-all-done.9 = bf16[4,128,2304]{1,2,0:T(8,128)(2,1)S(1)} async-done(((bf16[4,128,2304]{1,2,0:T(8,128)(2,1)}), bf16[4,128,2304]{1,2,0:T(8,128)(2,1)S(1)}, u32[]{:S(2)}, u32[]{:S(2)}) %all-to-all-start.9) | async-done | bytes 2359328 | tf_op jit(solution)/shard_map/all_to_all | solution.py:295
  584.9 2.3 fusion.111
  587.2 2.0 copy.275
  590.9 3.5 broadcast_multiply_fusion
  (351 shorter events, 89.3 us)
Async XLA Ops:
  7.2 19.7 %copy-start.70 = (bf16[128]{0:T(256)(128)(2,1)S(1)}, bf16[128]{0:T(256)(128)(2,1)}, u32[]{:S(2)}) copy-start(bf16[128]{0:T(256)(128)(2,1)} %param.27) | copy-start | bytes 772
  7.2 89.1 %all-gather.6.cloned.1.call-start = ((), (), s32[]{:S(2)}) async-start(), calls=%async_computation.12 | async-start | bytes 3342336 | tf_op jit(solution)/shard_map/all_gather | solution.py:117
  7.9 10.2 %copy-start.47 = (f32[128]{0:T(128)}, f32[128]{0:T(128)S(1)}, u32[]{:S(2)}) copy-start(f32[128]{0:T(128)S(1)} %convert_element_type.186) | copy-start | bytes 1540
  10.1 7.9 %collective-permute-start.2 = (bf16[128,768]{0,1:T(8,128)(2,1)S(1)}, bf16[128,768]{0,1:T(8,128)(2,1)S(1)}, u32[]{:S(2)}, u32[]{:S(2)}) collective-permute-start(bf16[128,768]{0,1:T(8,128)(2,1)S(1)} %multiply_convert_fusion.8), channel_id=1, source_target_pairs={{8,1},{1,8},{24,17},{17,24},{40,33},{33,40},{56,49},{49,56},{72,65... | collective-permute-start | bytes 589832 | tf_op jit(solution)/shard_map/ppermute | solution.py:150
  14.7 24.8 %copy-start.58 = (s32[1,13]{1,0:T(1,128)S(1)}, s32[1,13]{1,0:T(1,128)}, u32[]{:S(2)}) copy-start(s32[1,13]{1,0:T(1,128)} %param.18) | copy-start | bytes 160
  14.7 24.8 %copy-start.59 = (s32[1,13]{1,0:T(1,128)S(1)}, s32[1,13]{1,0:T(1,128)}, u32[]{:S(2)}) copy-start(s32[1,13]{1,0:T(1,128)} %param.17) | copy-start | bytes 160
  18.8 25.3 %copy-start.20 = (bf16[128,2048]{1,0:T(8,128)(2,1)S(1)}, bf16[128,2048]{1,0:T(8,128)(2,1)}, u32[]{:S(2)}) copy-start(bf16[128,2048]{1,0:T(8,128)(2,1)} %param.16) | copy-start | bytes 1572868
  18.8 25.4 %copy-start.21 = (bf16[128,2048]{1,0:T(8,128)(2,1)S(1)}, bf16[128,2048]{1,0:T(8,128)(2,1)}, u32[]{:S(2)}) copy-start(bf16[128,2048]{1,0:T(8,128)(2,1)} %param.31) | copy-start | bytes 1572868
  18.8 102.6 %all-gather.8.cloned.1.call-start = ((), (), s32[]{:S(2)}) async-start(), calls=%async_computation.13 | async-start | bytes 1114112 | tf_op jit(solution)/shard_map/all_gather | solution.py:117
  19.8 5.6 collective-permute-start.4
  26.8 160.9 %all-gather.10.cloned.1.call-start = ((), (), s32[]{:S(2)}) async-start(), calls=%async_computation.14 | async-start | bytes 6684672 | tf_op jit(solution)/shard_map/all_gather | solution.py:117
  26.9 17.2 %copy-start.60 = (f32[128]{0:T(128)}, f32[128]{0:T(128)S(1)}, u32[]{:S(2)}) copy-start(f32[128]{0:T(128)S(1)} %convert_element_type.202) | copy-start | bytes 1540
  28.0 16.3 %copy-start.75 = (bf16[8]{0:T(256)(128)(2,1)S(1)}, bf16[8]{0:T(256)(128)(2,1)}, u32[]{:S(2)}) copy-start(bf16[8]{0:T(256)(128)(2,1)} %param.26) | copy-start | bytes 52
  28.0 16.3 %copy-start.76 = (bf16[8]{0:T(256)(128)(2,1)S(1)}, bf16[8]{0:T(256)(128)(2,1)}, u32[]{:S(2)}) copy-start(bf16[8]{0:T(256)(128)(2,1)} %param.25) | copy-start | bytes 52
  28.2 10.6 %collective-permute-start.7 = (bf16[128,1536]{1,0:T(8,128)(2,1)S(1)}, bf16[128,1536]{1,0:T(8,128)(2,1)S(1)}, u32[]{:S(2)}, u32[]{:S(2)}) collective-permute-start(bf16[128,1536]{1,0:T(8,128)(2,1)S(1)} %multiply_convert_fusion.3), channel_id=1, source_target_pairs={{8,1},{1,8},{24,17},{17,24},{40,33},{33,40},{56,49},{49,56},{72,65... | collective-permute-start | bytes 1179656 | tf_op jit(solution)/shard_map/ppermute | solution.py:150
  39.6 37.5 %collective-permute-start.3 = (s32[2,13]{1,0:T(2,128)S(1)}, s32[2,13]{1,0:T(2,128)S(1)}, u32[]{:S(2)}, u32[]{:S(2)}) collective-permute-start(s32[2,13]{1,0:T(2,128)S(1)} %pad_add_fusion), channel_id=1, source_target_pairs={{0,8},{8,0},{16,24},{24,16},{32,40},{40,32},{48,56},{56,48},{64,72... | collective-permute-start | bytes 320 | tf_op jit(solution)/shard_map/ppermute | solution.py:97
  41.3 85.1 %collective-permute-start.8 = (bf16[128,768]{0,1:T(8,128)(2,1)}, bf16[128,768]{0,1:T(8,128)(2,1)}, u32[]{:S(2)}, u32[]{:S(2)}) collective-permute-start(bf16[128,768]{0,1:T(8,128)(2,1)} %dynamic-slice_bitcast_fusion), channel_id=1, source_target_pairs={{8,1},{1,8},{24,17},{17,24},{40,33},{33,40},{56,49},{49,56},{72,65... | collective-permute-start | bytes 589832 | tf_op jit(solution)/shard_map/ppermute | solution.py:150
  44.2 26.6 %collective-permute-start = (bf16[2,64,2048]{2,1,0:T(8,128)(2,1)S(1)}, bf16[2,64,2048]{2,1,0:T(8,128)(2,1)S(1)}, u32[]{:S(2)}, u32[]{:S(2)}) collective-permute-start(bf16[2,64,2048]{2,1,0:T(8,128)(2,1)S(1)} %fusion.31), channel_id=1, source_target_pairs={{0,8},{8,0},{16,24},{24,16},{32,40},{40,32},{48,56},{56,48},{64,72... | collective-permute-start | bytes 1572872 | tf_op jit(solution)/shard_map/ppermute | solution.py:97
  70.1 31.7 %copy-start.40 = (f32[128]{0:T(128)}, f32[128]{0:T(128)S(1)}, u32[]{:S(2)}) copy-start(f32[128]{0:T(128)S(1)} %get-tuple-element.72) | copy-start | bytes 1540
  70.1 38.1 %copy-start.42 = (f32[128]{0:T(128)}, f32[128]{0:T(128)S(1)}, u32[]{:S(2)}) copy-start(f32[128]{0:T(128)S(1)} %get-tuple-element.73) | copy-start | bytes 1540
  72.8 18.9 %all-to-all-start = ((bf16[4,64,2048]{2,1,0:T(8,128)(2,1)}), bf16[4,64,2048]{2,1,0:T(8,128)(2,1)S(1)}, u32[]{:S(2)}, u32[]{:S(2)}) async-start(bf16[4,64,2048]{2,1,0:T(8,128)(2,1)} %broadcast_in_dim.39), calls=%async_computation | async-start | bytes 2097152 | tf_op jit(solution)/shard_map/all_to_all | solution.py:101
  77.0 158.1 %all-gather.12.cloned.1.call-start = ((), (), s32[]{:S(2)}) async-start(), calls=%async_computation.15 | async-start | bytes 3342336 | tf_op jit(solution)/shard_map/all_gather | solution.py:117
  91.7 3.6 collective-permute-start.1
  96.3 4.4 copy-start.56
  125.7 3.1 collective-permute-start.5
  149.7 18.7 %copy-start.31 = (bf16[64,2048]{1,0:T(8,128)(2,1)S(1)}, bf16[64,2048]{1,0:T(8,128)(2,1)}, u32[]{:S(2)}) copy-start(bf16[64,2048]{1,0:T(8,128)(2,1)} %get-tuple-element.50) | copy-start | bytes 786436
  166.3 20.3 %copy-start.28 = (bf16[4,64,2048]{2,1,0:T(8,128)(2,1)}, bf16[4,64,2048]{2,1,0:T(8,128)(2,1)S(1)}, u32[]{:S(2)}) copy-start(bf16[4,64,2048]{2,1,0:T(8,128)(2,1)S(1)} %all_to_all.51) | copy-start | bytes 3145732
  166.3 21.4 %collective-permute-start.6 = (bf16[256,2048]{1,0:T(8,128)(2,1)S(1)}, bf16[256,2048]{1,0:T(8,128)(2,1)}, u32[]{:S(2)}, u32[]{:S(2)}) collective-permute-start(bf16[256,2048]{1,0:T(8,128)(2,1)S(1)} %bitcast.302), channel_id=1, source_target_pairs={{0,8},{8,0},{16,24},{24,16},{32,40},{40,32},{48,56},{56,48},{64,72... | collective-permute-start | bytes 3145736 | tf_op jit(solution)/shard_map/ppermute | solution.py:97
  186.7 9.7 %collective-permute-start.12 = (bf16[256,2048]{1,0:T(8,128)(2,1)}, bf16[256,2048]{1,0:T(8,128)(2,1)S(1)}, u32[]{:S(2)}, u32[]{:S(2)}) collective-permute-start(bf16[256,2048]{1,0:T(8,128)(2,1)} %bitcast.40), channel_id=1, source_target_pairs={{0,8},{8,0},{16,24},{24,16},{32,40},{40,32},{48,56},{56,48},{64,72... | collective-permute-start | bytes 3145736 | tf_op jit(solution)/shard_map/ppermute | solution.py:97
  196.3 45.3 %copy-start.73 = (bf16[256,2048]{1,0:T(8,128)(2,1)}, bf16[256,2048]{1,0:T(8,128)(2,1)S(1)}, u32[]{:S(2)}) copy-start(bf16[256,2048]{1,0:T(8,128)(2,1)S(1)} %collective-permute-done.12) | copy-start | bytes 3145732
  235.0 6.6 %copy-start.72 = (bf16[2048,1536]{1,0:T(8,128)(2,1)S(1)}, bf16[2048,1536]{1,0:T(8,128)(2,1)}, u32[]{:S(2)}) copy-start(bf16[2048,1536]{1,0:T(8,128)(2,1)} %all-gather.10.cloned.1.call-done) | copy-start | bytes 18874372
  245.2 3.9 collective-permute-start.13
  249.4 18.3 %copy-start.45 = (f32[64]{0:T(128)S(1)}, f32[64]{0:T(128)}, u32[]{:S(2)}) copy-start(f32[64]{0:T(128)} %copy-done.44) | copy-start | bytes 772
  249.5 19.6 %copy-start.62 = (f32[64]{0:T(128)S(1)}, f32[64]{0:T(128)}, u32[]{:S(2)}) copy-start(f32[64]{0:T(128)} %get-tuple-element.87) | copy-start | bytes 772
  269.3 21.5 %copy-start.34 = (bf16[2048,256]{0,1:T(8,128)(2,1)S(1)}, bf16[2048,256]{0,1:T(8,128)(2,1)}, u32[]{:S(2)}) copy-start(bf16[2048,256]{0,1:T(8,128)(2,1)} %all-gather.8.cloned.1.call-done) | copy-start | bytes 3145732
  285.3 6.2 %copy-start.30 = (bf16[4,64,2048]{2,1,0:T(8,128)(2,1)}, bf16[4,64,2048]{2,1,0:T(8,128)(2,1)S(1)}, u32[]{:S(2)}) copy-start(bf16[4,64,2048]{2,1,0:T(8,128)(2,1)S(1)} %all_to_all.54) | copy-start | bytes 3145732
  285.3 6.5 %copy-start.23 = (f32[512,256]{0,1:T(8,128)S(1)}, f32[512,256]{0,1:T(8,128)}, u32[]{:S(2)}) copy-start(f32[512,256]{0,1:T(8,128)} %copy-done.22) | copy-start | bytes 1572868
  285.3 6.5 %copy-start.36 = (f32[512,2,128]{0,2,1:T(8,128)S(1)}, f32[512,2,128]{0,2,1:T(8,128)}, u32[]{:S(2)}) copy-start(f32[512,2,128]{0,2,1:T(8,128)} %get-tuple-element.92) | copy-start | bytes 1572868
  285.3 5.5 collective-permute-start.14
  318.4 2.9 collective-permute-start.15
  324.4 4.5 copy-start.54
  324.4 5.2 copy-start.35
  324.4 19.3 %all-to-all-start.7 = ((bf16[4,64,2048]{2,1,0:T(8,128)(2,1)}), bf16[4,64,2048]{2,1,0:T(8,128)(2,1)}, u32[]{:S(2)}, u32[]{:S(2)}) async-start(bf16[4,64,2048]{2,1,0:T(8,128)(2,1)} %bitcast.57), calls=%async_computation.7 | async-start | bytes 2097152 | tf_op jit(solution)/shard_map/all_to_all | solution.py:105
  328.8 102.2 %reduce-scatter.7.cloned.1.call-start = ((), (), s32[]{:S(2)}) async-start(), calls=%async_computation.16 | async-start | bytes 5013504
  333.1 12.2 %copy-start.52 = (f32[64]{0:T(128)S(1)}, f32[64]{0:T(128)}, u32[]{:S(2)}) copy-start(f32[64]{0:T(128)} %get-tuple-element.86) | copy-start | bytes 772
  336.7 8.7 %copy-start.39 = (bf16[1,1,16,128]{3,1,2,0:T(2,128)(2,1)S(1)}, bf16[1,1,16,128]{3,1,2,0:T(2,128)(2,1)}, u32[]{:S(2)}) copy-start(bf16[1,1,16,128]{3,1,2,0:T(2,128)(2,1)} %copy.314) | copy-start | bytes 12292
  356.2 167.0 %reduce-scatter.9.cloned.1.call-start = ((), (), s32[]{:S(2)}) async-start(), calls=%async_computation.17 | async-start | bytes 10027008
  393.6 3.4 collective-permute-start.9
  398.3 36.0 %copy-start.46 = (f32[64]{0:T(128)S(1)}, f32[64]{0:T(128)}, u32[]{:S(2)}) copy-start(f32[64]{0:T(128)} %copy-done.44) | copy-start | bytes 772
  398.3 36.0 %copy-start.53 = (f32[64]{0:T(128)S(1)}, f32[64]{0:T(128)}, u32[]{:S(2)}) copy-start(f32[64]{0:T(128)} %get-tuple-element.86) | copy-start | bytes 772
  398.3 36.0 %copy-start.63 = (f32[64]{0:T(128)S(1)}, f32[64]{0:T(128)}, u32[]{:S(2)}) copy-start(f32[64]{0:T(128)} %get-tuple-element.87) | copy-start | bytes 772
  398.3 36.0 %copy-start.65 = (f32[64]{0:T(128)S(1)}, f32[64]{0:T(128)}, u32[]{:S(2)}) copy-start(f32[64]{0:T(128)} %copy-done.64) | copy-start | bytes 772
  398.3 36.0 %copy-start.67 = (f32[64]{0:T(128)S(1)}, f32[64]{0:T(128)}, u32[]{:S(2)}) copy-start(f32[64]{0:T(128)} %get-tuple-element.85) | copy-start | bytes 772
  398.3 19.3 %all-to-all-start.3 = ((bf16[4,64,2048]{2,1,0:T(8,128)(2,1)}), bf16[4,64,2048]{2,1,0:T(8,128)(2,1)}, u32[]{:S(2)}, u32[]{:S(2)}) async-start(bf16[4,64,2048]{2,1,0:T(8,128)(2,1)} %bitcast.288), calls=%async_computation.3 | async-start | bytes 2097152 | tf_op jit(solution)/shard_map/all_to_all | solution.py:105
  431.0 4.4 slice-start.1
  431.9 3.6 collective-permute-start.18
  434.8 5.1 collective-permute-start.16
  434.9 3.6 collective-permute-start.10
  435.6 93.4 %collective-permute-start.19 = (bf16[128,1152]{0,1:T(8,128)(2,1)S(1)}, bf16[128,1152]{0,1:T(8,128)(2,1)S(1)}, u32[]{:S(2)}, u32[]{:S(2)}) collective-permute-start(bf16[128,1152]{0,1:T(8,128)(2,1)S(1)} %pad_maximum_fusion.16), channel_id=1, source_target_pairs={{8,1},{1,8},{24,17},{17,24},{40,33},{33,40},{56,49},{49,56},{72,65... | collective-permute-start | bytes 884744 | tf_op jit(solution)/shard_map/ppermute | solution.py:150
  438.6 95.8 %collective-permute-start.11 = (bf16[128,2048]{1,0:T(8,128)(2,1)S(1)}, bf16[128,2048]{1,0:T(8,128)(2,1)}, u32[]{:S(2)}, u32[]{:S(2)}) collective-permute-start(bf16[128,2048]{1,0:T(8,128)(2,1)S(1)} %maximum_select_fusion), channel_id=1, source_target_pairs={{0,1},{9,8},{16,17},{25,24},{32,33},{41,40},{48,49},{57,56},{64,65... | collective-permute-start | bytes 1572872 | tf_op jit(solution)/shard_map/ppermute | solution.py:324
  440.8 114.7 %collective-permute-start.17 = (bf16[128,2048]{1,0:T(8,128)(2,1)}, bf16[128,2048]{1,0:T(8,128)(2,1)}, u32[]{:S(2)}, u32[]{:S(2)}) collective-permute-start(bf16[128,2048]{1,0:T(8,128)(2,1)} %maximum_select_fusion.1), channel_id=1, source_target_pairs={{0,1},{9,8},{16,17},{25,24},{32,33},{41,40},{48,49},{57,56},{64,65... | collective-permute-start | bytes 1572872 | tf_op jit(solution)/shard_map/ppermute | solution.py:324
  524.5 12.3 %collective-permute-start.20 = (bf16[128,2304]{0,1:T(8,128)(2,1)S(1)}, bf16[128,2304]{0,1:T(8,128)(2,1)S(1)}, u32[]{:S(2)}, u32[]{:S(2)}) collective-permute-start(bf16[128,2304]{0,1:T(8,128)(2,1)S(1)} %copy.279), channel_id=1, source_target_pairs={{8,1},{1,8},{24,17},{17,24},{40,33},{33,40},{56,49},{49,56},{72,65... | collective-permute-start | bytes 1769480 | tf_op jit(solution)/shard_map/ppermute | solution.py:150
  530.3 19.7 %all-to-all-start.8 = ((bf16[4,128,1152]{1,2,0:T(8,128)(2,1)}), bf16[4,128,1152]{1,2,0:T(8,128)(2,1)S(1)}, u32[]{:S(2)}, u32[]{:S(2)}) async-start(bf16[4,128,1152]{1,2,0:T(8,128)(2,1)} %broadcast_in_dim.55), calls=%async_computation.8 | async-start | bytes 2359296 | tf_op jit(solution)/shard_map/all_to_all | solution.py:295
  551.7 33.3 %all-to-all-start.9 = ((bf16[4,128,2304]{1,2,0:T(8,128)(2,1)}), bf16[4,128,2304]{1,2,0:T(8,128)(2,1)S(1)}, u32[]{:S(2)}, u32[]{:S(2)}) async-start(bf16[4,128,2304]{1,2,0:T(8,128)(2,1)} %broadcast_in_dim.56), calls=%async_computation.9 | async-start | bytes 4718592 | tf_op jit(solution)/shard_map/all_to_all | solution.py:295
  (53 other events, 114.6 us)
Sparse Core Ops, SparseCore 0:
  18.9 53.6 all-gather.5
  74.7 42.1 all-gather.7
  119.7 61.9 all-gather.9
  183.7 51.2 all-gather.11
  356.3 74.6 reduce-scatter.6
  434.3 88.7 reduce-scatter.8

commit v2 on v1

v2 whole, which is shorter than its diff:
```python
import math

import jax
import jax.numpy as jnp
from jax import lax
from jax.experimental import pallas as pl
from jax.experimental.pallas import tpu as pltpu
from jax.sharding import PartitionSpec as P

HD = 128
EPS = 1e-06
BASE = 1000000.0
NEG = -1e30
F32 = jnp.float32
BF16 = jnp.bfloat16
PLANE = ("shard", "tp")
SCALE = 1.0 / math.sqrt(HD)
VMEM = 48 << 20


def lookup(onehot, table):
    return jnp.sum(onehot * table[None, :], axis=1)


def tree_layout(lengths, parents, places):
    labels = jnp.arange(lengths.shape[0], dtype=jnp.int32)
    ends = jnp.cumsum(lengths)
    starts = ends - lengths
    parent_hot = (parents[:, None] == labels[None, :]).astype(jnp.int32)
    grand = lookup(parent_hot, parents)
    parent_len = lookup(parent_hot, lengths)
    grand_hot = (grand[:, None] == labels[None, :]).astype(jnp.int32)
    grand_len = lookup(grand_hot, lengths)
    before = jnp.where(labels == 0, 0, parent_len + jnp.where(parents == 0, 0, grand_len))
    segment = jnp.sum((places[:, None] >= ends[None, :]).astype(jnp.int32), axis=1)
    token_hot = (segment[:, None] == labels[None, :]).astype(jnp.int32)
    position = places - lookup(token_hot, starts) + lookup(token_hot, before)
    return (segment, lookup(token_hot, parents), lookup(token_hot, grand), position)


def rope_tables(position, columns):
    halfway = columns // 2
    frequency = jnp.exp(jnp.arange(halfway, dtype=F32) * (-2.0 * math.log(BASE) / columns))
    angles = position.astype(F32)[:, None] * frequency[None, :]
    angles = jnp.concatenate([angles, angles], axis=1)
    return (jnp.cos(angles), jnp.sin(angles))


def rms_scale(inputs):
    return lax.rsqrt(jnp.mean(inputs * inputs, axis=-1, keepdims=True) + EPS)


def dot(left, right):
    return jnp.dot(left, right, preferred_element_type=F32)


def dot_rows(left, right):
    return lax.dot_general(left, right, (((0,), (0,)), ((), ())), preferred_element_type=F32)


def dot_back(left, right):
    return lax.dot_general(left, right, (((1,), (1,)), ((), ())), preferred_element_type=F32)


def turn(inputs):
    halfway = inputs.shape[-1] // 2
    return jnp.concatenate([-inputs[:, halfway:], inputs[:, :halfway]], axis=-1)


def unturn(inputs):
    halfway = inputs.shape[-1] // 2
    return jnp.concatenate([inputs[:, halfway:], -inputs[:, :halfway]], axis=-1)


def head(number):
    return slice(number * HD, (number + 1) * HD)


def call(kernel, grid, in_specs, out_specs, out_shape, flops, scratch=(), moved=8 << 20):
    return pl.pallas_call(
        kernel,
        grid=grid,
        in_specs=in_specs,
        out_specs=out_specs,
        out_shape=out_shape,
        scratch_shapes=scratch,
        compiler_params=pltpu.CompilerParams(
            dimension_semantics=("arbitrary",) * len(grid), vmem_limit_bytes=VMEM
        ),
        cost_estimate=pl.CostEstimate(flops=flops, bytes_accessed=moved, transcendentals=0),
    )


def struct(shape, dtype):
    return jax.ShapeDtypeStruct(shape, dtype)


def fixed(shape):
    return pl.BlockSpec(shape, lambda i: (0,) * len(shape))


def rowed(rows, columns):
    return pl.BlockSpec((rows, columns), lambda i: (i, 0))


def project_kernel(xa, xb, w, gains, cosine, sine, xn, pre, low, gate):
    x = jnp.where(pl.program_id(0) == 0, xa[...], xb[...]).astype(F32)
    normed = (x * rms_scale(x)).astype(BF16)
    xn[...] = normed
    out = dot(normed, w[...])
    for place in range(3):
        raw = out[:, head(place)]
        pre[:, head(place)] = raw
        unit = raw * rms_scale(raw) * gains[pl.ds(place // 2, 1), :]
        low[:, head(place)] = (unit * cosine[...] + turn(unit) * sine[...]).astype(BF16)
    low[:, head(3)] = out[:, head(3)].astype(BF16)
    gate[...] = out[:, 4 * HD :]


def project(xa, xb, w, gains, cosine, sine):
    half, width = xa.shape
    return call(
        project_kernel,
        (2,),
        [
            fixed((half, width)),
            fixed((half, width)),
            fixed((width, 6 * HD)),
            fixed((2, HD)),
            rowed(half, HD),
            rowed(half, HD),
        ],
        [rowed(half, width), rowed(half, 3 * HD), rowed(half, 4 * HD), rowed(half, 2 * HD)],
        [
            struct((2 * half, width), BF16),
            struct((2 * half, 3 * HD), F32),
            struct((2 * half, 4 * HD), BF16),
            struct((2 * half, 2 * HD), F32),
        ],
        2 * 2 * half * width * 6 * HD,
    )(xa, xb, w, gains, cosine, sine)


def attend_kernel(low, gate, w_out, of_row, of_column, probs, attended, gated, mine, other):
    step = pl.program_id(0)
    half = probs.shape[1]
    rows = pl.ds(step * half, half)
    key, value = low[:, head(2)], low[:, head(3)]
    seg, par, grand, place = (of_row[rows, n : n + 1] for n in range(4))
    key_seg, key_place = of_column[0:1, :], of_column[1:2, :]
    allowed = ((key_seg == seg) | (key_seg == par) | (key_seg == grand)) & (key_place <= place)
    for number in range(2):
        scores = dot_back(low[rows, head(number)], key) * SCALE
        scores = jnp.where(allowed, scores, NEG)
        raised = jnp.exp(scores - jnp.max(scores, axis=-1, keepdims=True))
        share = raised / jnp.sum(raised, axis=-1, keepdims=True)
        probs[number] = share
        seen = dot(share.astype(BF16), value)
        attended[:, head(number)] = seen
        gated[:, head(number)] = (seen * jax.nn.sigmoid(gate[:, head(number)])).astype(BF16)
    out = dot_back(gated[...], w_out[...])

    @pl.when(step == 0)
    def _():
        mine[...] = out

    @pl.when(step == 1)
    def _():
        other[...] = out.astype(BF16)


def attend(low, gate, w, of_row, of_column):
    length = low.shape[0]
    half, width = length // 2, w.shape[0]
    return call(
        attend_kernel,
        (2,),
        [
            fixed((length, 4 * HD)),
            rowed(half, 2 * HD),
            pl.BlockSpec((width, 2 * HD), lambda i: (0, 3)),
            fixed((length, 4)),
            fixed((2, length)),
        ],
        [
            pl.BlockSpec((2, half, length), lambda i: (0, i, 0)),
            rowed(half, 2 * HD),
            rowed(half, 2 * HD),
            fixed((half, width)),
            fixed((half, width)),
        ],
        [
            struct((2, length, length), F32),
            struct((length, 2 * HD), F32),
            struct((length, 2 * HD), BF16),
            struct((half, width), F32),
            struct((half, width), BF16),
        ],
        2 * length * width * 2 * HD + 8 * length * length * HD,
    )(low, gate, w, of_row, of_column)


def feed_kernel(ua, ub, ca, cb, wg, wu, wd, hidden, d_gate, d_up, mine, other, total):
    step = pl.program_id(0)
    half = ua.shape[0]
    for number, (u, cot) in enumerate(((ua, ca), (ub, cb))):
        rows = slice(number * half, (number + 1) * half)
        gate, up = dot(u[...], wg[...]), dot(u[...], wu[...])
        d_hidden = dot(cot[...], wd[...])
        sig = jax.nn.sigmoid(gate)
        silu = gate * sig
        hidden[rows, :] = (silu * up).astype(BF16)
        dg = (d_hidden * up * sig * (1.0 + gate * (1.0 - sig))).astype(BF16)
        du = (d_hidden * silu).astype(BF16)
        d_gate[rows, :] = dg
        d_up[rows, :] = du
        term = dot_back(dg, wg[...]) + dot_back(du, wu[...])

        @pl.when(step == 0)
        def _():
            total[rows, :] = term

        @pl.when(step > 0)
        def _():
            total[rows, :] += term

    @pl.when(step == pl.num_programs(0) - 1)
    def _():
        mine[...] = total[:half, :]
        other[...] = total[half:, :].astype(BF16)


def feed(ua, ub, ca, cb, w):
    half, width = ua.shape
    chunk = 2 * HD
    parts = w.shape[1] // 3 // chunk
    column = lambda shift: pl.BlockSpec((width, chunk), lambda i: (0, shift * parts + i))
    unit = pl.BlockSpec((2 * half, chunk), lambda i: (0, i))
    units = parts * chunk
    return call(
        feed_kernel,
        (parts,),
        [fixed((half, width))] * 4 + [column(0), column(1), column(2)],
        [unit, unit, unit, fixed((half, width)), fixed((half, width))],
        [struct((2 * half, units), BF16)] * 3
        + [struct((half, width), F32), struct((half, width), BF16)],
        2 * 2 * half * width * units * 5,
        scratch=[pltpu.VMEM((2 * half, width), F32)],
    )(ua, ub, ca, cb, w, w, w)


def down_kernel(hidden, w, mine, other):
    out = dot_back(hidden[...], w[...])

    @pl.when(pl.program_id(0) == 0)
    def _():
        mine[...] = out

    @pl.when(pl.program_id(0) == 1)
    def _():
        other[...] = out.astype(BF16)


def down_product(left, w, place):
    length, units = left.shape
    half, width = length // 2, w.shape[0]
    return call(
        down_kernel,
        (2,),
        [rowed(half, units), pl.BlockSpec((width, units), lambda i: (0, place))],
        [fixed((half, width)), fixed((half, width))],
        [struct((half, width), F32), struct((half, width), BF16)],
        2 * length * width * units,
    )(left, w)


def feed_grads_kernel(ua, ub, ca, cb, d_gate, d_up, hidden, out):
    half, units = ua.shape[0], hidden.shape[1]
    pairs = ((ua, ub, d_gate), (ua, ub, d_up), (ca, cb, hidden))
    for number, (first, second, right) in enumerate(pairs):
        term = dot_rows(first[...], right[:half, :]) + dot_rows(second[...], right[half:, :])
        out[:, number * units : (number + 1) * units] = term.astype(BF16)


def feed_grads(ua, ub, ca, cb, d_gate, d_up, hidden):
    half, width = ua.shape
    units = hidden.shape[1]
    chunk = 2 * HD
    slab = pl.BlockSpec((half, chunk), lambda i: (0, i))
    return call(
        feed_grads_kernel,
        (width // chunk,),
        [slab] * 4 + [fixed((2 * half, units))] * 3,
        rowed(chunk, 3 * units),
        struct((width, 3 * units), BF16),
        2 * 2 * half * width * units * 3,
    )(ua, ub, ca, cb, d_gate, d_up, hidden)


def gate_back_kernel(da, db, w_out, gate, attended, d_attended, d_gate):
    half = da.shape[0]
    for number, low in enumerate((da, db)):
        rows = slice(number * half, (number + 1) * half)
        d_gated = dot(low[...], w_out[...])
        sig = jax.nn.sigmoid(gate[rows, :])
        d_attended[rows, :] = (d_gated * sig).astype(BF16)
        d_gate[rows, :] = (d_gated * attended[rows, :] * sig * (1.0 - sig)).astype(BF16)


def gate_back(da, db, w, gate, attended):
    half, width = da.shape
    wide = (2 * half, 2 * HD)
    return call(
        gate_back_kernel,
        (1,),
        [fixed((half, width))] * 2
        + [pl.BlockSpec((width, 2 * HD), lambda i: (0, 3)), fixed(wide), fixed(wide)],
        [fixed(wide), fixed(wide)],
        [struct(wide, BF16), struct(wide, BF16)],
        2 * 2 * half * width * 2 * HD,
    )(da, db, w, gate, attended)


def head_back(grads, inputs, gain):
    factor = rms_scale(inputs)
    scaled = gain * grads
    back = factor * scaled - inputs * factor**3 * jnp.mean(scaled * inputs, axis=-1, keepdims=True)
    return back.astype(BF16), jnp.sum(grads * inputs * factor, axis=0, keepdims=True)


def attend_back_kernel(
    probs, low, d_attended, pre, gains, cosine, sine, out, terms, d_key, d_value
):
    step = pl.program_id(0)
    half = probs.shape[1]
    start = pl.multiple_of(step * half, half)
    rows = pl.ds(start, half)
    key, value = low[:, head(2)], low[:, head(3)]
    cos_rows, sin_rows = cosine[rows, :], sine[rows, :]

    @pl.when(step == 0)
    def _():
        d_key[...] = jnp.zeros_like(d_key)
        d_value[...] = jnp.zeros_like(d_value)
        terms[...] = jnp.zeros_like(terms)

    for number in range(2):
        share = probs[number]
        d_seen = d_attended[:, head(number)]
        d_share = dot_back(d_seen, value)
        d_scores = share * (d_share - jnp.sum(share * d_share, axis=-1, keepdims=True))
        d_scores = d_scores.astype(BF16)
        d_query = dot(d_scores, key) * SCALE
        d_key[...] += dot_rows(d_scores, low[rows, head(number)])
        d_value[...] += dot_rows(share.astype(BF16), d_seen)
        grads = d_query * cos_rows + unturn(d_query * sin_rows)
        back, term = head_back(grads, pre[rows, head(number)], gains[0:1, :])
        out[rows, head(number)] = back
        terms[0:1, :] += term

    @pl.when(step == 1)
    def _():
        grads = d_key[...] * SCALE
        grads = grads * cosine[...] + unturn(grads * sine[...])
        back, term = head_back(grads, pre[:, head(2)], gains[1:2, :])
        out[:, head(2)] = back
        terms[1:2, :] = term
        out[:, head(3)] = d_value[...].astype(BF16)


def attend_back(probs, low, d_attended, pre, gains, cosine, sine):
    length = low.shape[0]
    half = length // 2
    return call(
        attend_back_kernel,
        (2,),
        [
            pl.BlockSpec((2, half, length), lambda i: (0, i, 0)),
            fixed((length, 4 * HD)),
            rowed(half, 2 * HD),
            fixed((length, 3 * HD)),
            fixed((2, HD)),
            fixed((length, HD)),
            fixed((length, HD)),
        ],
        [fixed((length, 4 * HD)), fixed((8, HD))],
        [struct((length, 4 * HD), BF16), struct((8, HD), F32)],
        20 * length * length * HD,
        scratch=[pltpu.VMEM((length, HD), F32), pltpu.VMEM((length, HD), F32)],
    )(probs, low, d_attended, pre, gains, cosine, sine)


def input_back_kernel(d_qkv, d_gate, w, mine, other):
    out = dot_back(d_qkv[...], w[:, : 4 * HD]) + dot_back(d_gate[...], w[:, 4 * HD :])

    @pl.when(pl.program_id(0) == 0)
    def _():
        mine[...] = out

    @pl.when(pl.program_id(0) == 1)
    def _():
        other[...] = out.astype(BF16)


def input_back(d_qkv, d_gate, w):
    length = d_qkv.shape[0]
    half, width = length // 2, w.shape[0]
    return call(
        input_back_kernel,
        (2,),
        [rowed(half, 4 * HD), rowed(half, 2 * HD), fixed((width, 6 * HD))],
        [fixed((half, width)), fixed((half, width))],
        [struct((half, width), F32), struct((half, width), BF16)],
        2 * length * width * 6 * HD,
    )(d_qkv, d_gate, w)


def outer_grads_kernel(xn, da, db, d_gate, gated, out):
    half = da.shape[0]
    split = d_gate.shape[1]
    out[:, :split] = dot_rows(xn[...], d_gate[...]).astype(BF16)
    term = dot_rows(da[...], gated[:half, :]) + dot_rows(db[...], gated[half:, :])
    out[:, split:] = term.astype(BF16)


def outer_grads(xn, da, db, d_gate, gated):
    half, width = da.shape
    chunk = 2 * HD
    slab = pl.BlockSpec((half, chunk), lambda i: (0, i))
    return call(
        outer_grads_kernel,
        (width // chunk,),
        [pl.BlockSpec((2 * half, chunk), lambda i: (0, i)), slab, slab]
        + [fixed((2 * half, 2 * HD))] * 2,
        rowed(chunk, 4 * HD),
        struct((width, 4 * HD), BF16),
        2 * 2 * half * width * 4 * HD,
    )(xn, da, db, d_gate, gated)


def inner_grads_kernel(xn, d_qkv, terms, out):
    term = dot_rows(xn[...], d_qkv[...]).astype(BF16)
    count, block = out.shape[0], out.shape[1] - terms.shape[1]
    for number in range(count):
        out[number, :block] = term[number * block : (number + 1) * block]
        out[number, block:] = terms[number].astype(BF16)


def inner_grads(xn, d_qkv, terms):
    length, width = xn.shape
    columns, extra = d_qkv.shape[1], terms.shape[1]
    owners = terms.shape[0]
    block = width // owners
    return call(
        inner_grads_kernel,
        (owners // 2,),
        [
            pl.BlockSpec((length, 2 * block), lambda i: (0, i)),
            fixed((length, columns)),
            pl.BlockSpec((2, extra, columns), lambda i: (i, 0, 0)),
        ],
        pl.BlockSpec((2, block + extra, columns), lambda i: (i, 0, 0)),
        struct((owners, block + extra, columns), BF16),
        2 * length * width * columns,
    )(xn, d_qkv, terms)


def middle_kernel(parts, x, middle, spread):
    total = x[...].astype(F32) + jnp.sum(parts[...].astype(F32), axis=0)
    middle[...] = total
    low = (total * rms_scale(total)).astype(BF16)
    for number in range(spread.shape[0]):
        spread[number] = low


def middle_step(parts, x):
    shape = x.shape
    return call(
        middle_kernel,
        (1,),
        [fixed(parts.shape), fixed(shape)],
        [fixed(shape), fixed(parts.shape)],
        [struct(shape, F32), struct(parts.shape, BF16)],
        1 << 20,
    )(parts, x)


def norm_back(grads, inputs):
    factor = rms_scale(inputs)
    return factor * grads - inputs * factor**3 * jnp.mean(grads * inputs, axis=-1, keepdims=True)


def d_middle_kernel(parts, middle, cot, d_middle, spread):
    grads = jnp.sum(parts[...].astype(F32), axis=0)
    total = cot[...].astype(F32) + norm_back(grads, middle[...])
    d_middle[...] = total
    for number in range(spread.shape[0]):
        spread[number] = total.astype(BF16)


def d_middle_step(parts, middle, cot):
    shape = cot.shape
    return call(
        d_middle_kernel,
        (1,),
        [fixed(parts.shape), fixed(shape), fixed(shape)],
        [fixed(shape), fixed(parts.shape)],
        [struct(shape, F32), struct(parts.shape, BF16)],
        1 << 20,
    )(parts, middle, cot)


def make_shards(mesh):
    n_shard, n_ctx, n_tp = mesh.shape["shard"], mesh.shape["ctx"], mesh.shape["tp"]
    pairs = n_shard // 2

    def joint(pair, core, tp):
        return (pair * 2 + core) * n_tp + tp

    core_perm = [(i, i ^ 1) for i in range(n_shard)]
    planes = [
        [joint(pair, core, tp) for pair in range(pairs) for tp in range(n_tp)] for core in range(2)
    ]
    swap_perm = [
        edge
        for pair in range(pairs)
        for edge in (
            (joint(pair, 1, 0), joint(pair, 0, 1)),
            (joint(pair, 0, 1), joint(pair, 1, 0)),
        )
    ]
    across_perm = [(joint(pair, t, t), joint(pair, t, 1 - t)) for pair in range(pairs) for t in range(2)]

    def core_swap(value):
        return lax.ppermute(value, "shard", core_perm)

    def ctx_exchange(value):
        return lax.all_to_all(value, "ctx", 0, 0)

    def ctx_gather(value):
        return ctx_exchange(jnp.broadcast_to(value[None], (n_ctx,) + value.shape))

    def flat(value):
        return value.reshape((-1,) + value.shape[2:])

    def tree_rows(spread):
        mine = flat(ctx_exchange(spread))
        return mine, core_swap(mine)

    def tree_sums(mine, other):
        half = (mine + core_swap(other).astype(F32)).astype(BF16)
        return ctx_exchange(half.reshape((n_ctx, -1) + half.shape[1:]))

    def plane_gather(value):
        return lax.all_gather(value, PLANE, axis=0, tiled=True, axis_index_groups=planes)

    def plane_scatter(value):
        return lax.psum_scatter(
            value, PLANE, scatter_dimension=0, tiled=True, axis_index_groups=planes
        )

    def plane_exchange(value):
        parts = lax.all_to_all(value, PLANE, 0, 0, axis_index_groups=planes)
        return jnp.sum(parts.astype(F32), axis=0)

    def shards(
        tokens,
        seg_lengths,
        seg_parents,
        gain_in,
        w_query,
        w_key,
        w_value,
        w_gate_attn,
        w_out,
        gain_query,
        gain_key,
        gain_mid,
        w_gate,
        w_up,
        w_down,
        cotangent,
    ):
        core = lax.axis_index("shard") % 2
        tp = lax.axis_index("tp")
        ctx = lax.axis_index("ctx")
        native = core == tp
        rows = tokens.shape[0] // 2

        def swapped(value):
            return jnp.where(native, value, lax.ppermute(value, PLANE, swap_perm))

        def quarter(weight, axis):
            size = weight.shape[axis] // n_ctx
            return lax.dynamic_slice_in_dim(weight, ctx * size, size, axis)

        gain_one = gain_in.astype(F32)[:, None]
        gain_two = gain_mid.astype(F32)[:, None]
        first = jnp.concatenate(
            [quarter(w, 1) for w in (w_query, w_key, w_value, w_gate_attn)], axis=1
        )
        first = (first.astype(F32) * gain_one).astype(BF16)
        first = jnp.concatenate([first, quarter(w_out, 0).T], axis=1)
        second = jnp.concatenate([quarter(w_gate, 1), quarter(w_up, 1)], axis=1)
        second = (second.astype(F32) * gain_two).astype(BF16)
        second = jnp.concatenate([second, quarter(w_down, 0).T], axis=1)
        w1 = plane_gather(swapped(first))
        w2 = plane_gather(swapped(second))
        head_gains = lax.all_gather(
            jnp.concatenate([gain_query[None], gain_key[None]], axis=0), "shard", axis=1, tiled=True
        ).astype(F32)

        both = jnp.stack([tokens, cotangent])
        keep = lax.dynamic_slice_in_dim(both, core * rows, rows, 1)
        give = lax.dynamic_slice_in_dim(both, (1 - core) * rows, rows, 1)
        own = jnp.where(native, keep, core_swap(give))
        tree = jnp.concatenate([seg_lengths, seg_parents], axis=0)
        tree = jnp.where(native, tree, core_swap(tree))
        own_x, own_cot = own[0], own[1]
        xa, xb = tree_rows(jnp.broadcast_to(own_x[None], (n_ctx,) + own_x.shape))
        ca, cb = tree_rows(jnp.broadcast_to(own_cot[None], (n_ctx,) + own_cot.shape))

        half_at = jnp.where(jnp.arange(2) == 0, core, 1 - core) * rows
        places = (
            half_at[:, None, None]
            + jnp.arange(n_ctx, dtype=jnp.int32)[None, :, None] * (2 * rows)
            + jnp.arange(rows, dtype=jnp.int32)[None, None, :]
        ).reshape(-1)
        segment, parent_seg, grand_seg, position = tree_layout(tree[0], tree[1], places)
        of_row = jnp.stack([segment, parent_seg, grand_seg, places], axis=1)
        of_column = jnp.stack([segment, places], axis=0)
        cosine, sine = rope_tables(position, HD)

        xn, pre, low, gate = project(xa, xb, w1, head_gains, cosine, sine)
        probs, attended, gated, mine, other = attend(low, gate, w1, of_row, of_column)
        middle, spread = middle_step(tree_sums(mine, other), own_x)
        ua, ub = tree_rows(spread)

        hidden, d_gate, d_up, mine, other = feed(ua, ub, ca, cb, w2)
        units = hidden.shape[1]
        grad_ffn = plane_scatter(feed_grads(ua, ub, ca, cb, d_gate, d_up, hidden))
        d_middle, spread = d_middle_step(tree_sums(mine, other), middle, own_cot)
        da, db = tree_rows(spread)
        layer_parts = tree_sums(*down_product(hidden, w2, 2))
        layer_own = middle + jnp.sum(layer_parts.astype(F32), axis=0)

        d_attended, d_gate_pre = gate_back(da, db, w1, gate, attended)
        grad_outer = plane_exchange(
            outer_grads(xn, da, db, d_gate_pre, gated).reshape(n_shard, -1, 4 * HD)
        )
        d_qkv, terms = attend_back(probs, low, d_attended, pre, head_gains, cosine, sine)

        def spread_terms(vector):
            return jnp.pad(vector.reshape(n_shard, 1, -1), ((0, 0), (0, 15), (0, 0)))

        head_rows = gain_query.shape[0]
        wide_terms = jnp.concatenate([spread_terms(terms[0]), spread_terms(terms[1])], axis=2)
        wide_terms = jnp.pad(wide_terms, ((0, 0), (0, 0), (0, 4 * HD - 2 * head_rows)))
        grad_inner = plane_exchange(inner_grads(xn, d_qkv, wide_terms))
        parts = tree_sums(*input_back(d_qkv, d_gate_pre, w1))
        input_own = d_middle + norm_back(
            jnp.sum(parts.astype(F32), axis=0), own_x.astype(F32)
        )

        def owners(block):
            return ctx_gather(swapped(block.astype(BF16))).astype(F32)

        def side(parts):
            return parts.transpose(1, 0, 2).reshape(parts.shape[1], -1)

        def down(parts):
            return parts.transpose(0, 2, 1).reshape(-1, parts.shape[1])

        size = gain_in.shape[0]
        ffn = owners(grad_ffn)
        raw_gate = side(ffn[:, :, :units])
        raw_up = side(ffn[:, :, units : 2 * units])
        grad_down = down(ffn[:, :, 2 * units :])
        outer = owners(grad_outer)
        raw_gate_attn = side(outer[:, :, : 2 * HD])
        grad_out = down(outer[:, :, 2 * HD :])
        ends = grad_inner[size:]
        ends = ends + core_swap(ends.astype(BF16)).astype(F32)
        inner = owners(jnp.concatenate([grad_inner[:size], ends], axis=0))
        raw_query = side(inner[:, :size, : 2 * HD])
        raw_key = side(inner[:, :size, 2 * HD : 3 * HD])
        raw_value = side(inner[:, :size, 3 * HD :])
        head_ends = jnp.sum(inner[:, size, : 2 * head_rows], axis=0)

        def along(weights, raws):
            total = 0.0
            for weight, raw in zip(weights, raws):
                total = total + jnp.sum(weight.astype(F32) * raw, axis=1)
            return total

        gain_terms = jnp.stack(
            [
                along(
                    (w_query, w_key, w_value, w_gate_attn),
                    (raw_query, raw_key, raw_value, raw_gate_attn),
                ),
                along((w_gate, w_up), (raw_gate, raw_up)),
            ]
        )
        gain_terms = gain_terms + lax.ppermute(gain_terms, "tp", [(0, 1), (1, 0)])

        def finish(part):
            low = part.astype(BF16)
            sibling = core_swap(low)
            full = jnp.where(
                core == 0,
                jnp.concatenate([low, sibling], axis=0),
                jnp.concatenate([sibling, low], axis=0),
            )
            return jnp.where(native, full, lax.ppermute(full, PLANE, across_perm)).astype(F32)

        return (
            finish(layer_own),
            finish(input_own),
            gain_terms[0],
            raw_query * gain_one,
            raw_key * gain_one,
            raw_value * gain_one,
            raw_gate_attn * gain_one,
            grad_out,
            head_ends[:head_rows],
            head_ends[head_rows:],
            gain_terms[1],
            raw_gate * gain_two,
            raw_up * gain_two,
            grad_down,
        )

    return shards


def solution(mesh):
    return jax.shard_map(
        make_shards(mesh),
        mesh=mesh,
        in_specs=(
            P(("shard", "ctx"), None),
            P("shard", None),
            P("shard", None),
            P("shard"),
            P("shard", "tp"),
            P("shard", "tp"),
            P("shard", "tp"),
            P("shard", "tp"),
            P("tp", "shard"),
            P("shard"),
            P("shard"),
            P("shard"),
            P("shard", "tp"),
            P("shard", "tp"),
            P("tp", "shard"),
            P(("shard", "ctx"), None),
        ),
        out_specs=(
            P(("shard", "ctx"), None),
            P(("shard", "ctx"), None),
            P("shard"),
            P("shard", "tp"),
            P("shard", "tp"),
            P("shard", "tp"),
            P("shard", "tp"),
            P("tp", "shard"),
            P("shard"),
            P("shard"),
            P("shard"),
            P("shard", "tp"),
            P("shard", "tp"),
            P("tp", "shard"),
        ),
        check_vma=False,
    )
```

time: 612 us -> 453 us (0.74); the launches traced: 601 us -> 451 us
  waiting for transfers between devices: 218 us -> 133 us
  Pallas kernels: 0 us -> 67.8 us
  matrix products: 62.5 us -> 0 us
  blocking collectives: 111 us -> 74.9 us
  local copies, waits for them, and re-layouts: 70.4 us -> 40.1 us
  other arithmetic: 63 us -> 35.1 us
  starting transfers between devices: 60.6 us -> 85.1 us
    unnamed x8 -> x3, waiting for transfers between devices: 93.1 us -> 0.05 us
    pallas_call x0 -> x12, Pallas kernels: none -> 67.8 us  [the longest x1 18.5 us: feed(): call(feed_kernel, (parts,), [fixed((half, width))] * 4 + [column(0), colu...]
    dot_general x17 -> x0, matrix products: 59.1 us -> none  [the longest x4 20.2 us: dot(): return jnp.dot(left, right, preferred_element_type=F32)]
    all_to_all x5 -> x10, waiting for transfers between devices: 63.4 us -> 109 us  [the longest x8 84.7 us: ctx_exchange(): return lax.all_to_all(value, 'ctx', 0, 0)]
    all_gather x4 -> x2, waiting for transfers between devices: 38.7 us -> 0.01 us  [plane_gather(): lax.all_gather(value, PLANE, axis=0, tiled=True, axis_index_groups=planes)]
    all_to_all x5 -> x3, blocking collectives: 85.8 us -> 51 us  [ctx_exchange(): return lax.all_to_all(value, 'ctx', 0, 0)]
    all_to_all x5 -> x10, starting transfers between devices: 20.9 us -> 42.2 us  [the longest x8 32.5 us: ctx_exchange(): return lax.all_to_all(value, 'ctx', 0, 0)]
    concatenate x5 -> x4, other arithmetic: 15.3 us -> 0.18 us  [the longest x1 0.11 us: shards(): jnp.concatenate([spread_terms(terms[0]), spread_terms(terms[1])], axis=2)]
  transfers between devices with their start and end apart: 32 -> 34, of which waited for: 18 -> 17; matrix products, arithmetic and copies ran while one was open for 20% -> 11% of each run, Pallas kernels for 0% -> 9%
where the time goes in v2:
time: 453 us; the launch traced here: 451 us
  waiting for transfers between devices  133 us (29%)
  starting transfers between devices  85.1 us (19%)
  blocking collectives  74.9 us (17%)
  Pallas kernels  67.8 us (15%)
  local copies, waits for them, and re-layouts  40.1 us (9%)
  other arithmetic  35.1 us (8%)
  between operations  14.8 us (3%)
    all_to_all x8, waiting for transfers between devices, ctx_exchange(): return lax.all_to_all(value, 'ctx', 0, 0)  84.7 us
    all_to_all x3, blocking collectives, ctx_exchange(): return lax.all_to_all(value, 'ctx', 0, 0)  51 us
    all_to_all x8, starting transfers between devices, ctx_exchange(): return lax.all_to_all(value, 'ctx', 0, 0)  32.5 us
    all_to_all x2, waiting for transfers between devices, plane_exchange(): parts = lax.all_to_all(value, PLANE, 0, 0, axis_index_groups=planes)  24.7 us
    all_gather x1, blocking collectives, shards(): lax.all_gather(jnp.concatenate([gain_query[None], gain_key[None]], axis=0...  23.9 us
    ppermute x13, starting transfers between devices, core_swap(): return lax.ppermute(value, 'shard', core_perm)  22.8 us
    pallas_call x1, Pallas kernels, feed(): call(feed_kernel, (parts,), [fixed((half, width))] * 4 + [column(0), colu...  18.5 us
    ppermute x5, starting transfers between devices, swapped(): return jnp.where(native, value, lax.ppermute(value, PLANE, swap_perm))  17.4 us
  transfers between devices with their start and end apart: 34, of which 17 were waited for; matrix products, arithmetic and copies ran while one was open for 11% of the time, Pallas kernels for 9%

profile of v2, /device:TPU:1, one launch (start us, length us, event | category | flops | bytes accessed | tf_op | source)
XLA Modules:
  0.0 451.1 jit_solution(4161014800207490027)
XLA Ops:
  10.8 4.6 %collective-permute-start.2 = (bf16[128,1024]{1,0:T(8,128)(2,1)S(1)}, bf16[128,1024]{1,0:T(8,128)(2,1)S(1)}, u32[]{:S(2)}, u32[]{:S(2)}) collective-permute-start(bf16[128,1024]{1,0:T(8,128)(2,1)S(1)} %pad_maximum_fusion.1), channel_id=1, source_target_pairs={{8,1},{1,8},{24,17},{17,24},{40,33},{33,40},{56,49},{49,56},{72,65... | collective-permute-start | bytes 786440 | tf_op jit(solution)/shard_map/ppermute | solution.py:591
  15.4 4.0 collective-permute-done.2
  21.8 3.8 collective-permute-start.7
  25.6 7.6 %collective-permute-done.7 = bf16[128,2304]{1,0:T(8,128)(2,1)S(1)} collective-permute-done((bf16[128,2304]{1,0:T(8,128)(2,1)S(1)}, bf16[128,2304]{1,0:T(8,128)(2,1)S(1)}, u32[]{:S(2)}, u32[]{:S(2)}) %collective-permute-start.7) | collective-permute-done | bytes 589856 | tf_op jit(solution)/shard_map/ppermute | solution.py:591
  35.3 23.9 %all-gather = bf16[16,8,2]{1,2,0:T(2,128)(2,1)S(1)} all-gather(bf16[1,8,2]{1,2,0:T(2,128)(2,1)S(1)} %maximum_bitcast_fusion), channel_id=1, replica_groups=mesh['shard'=16,'ctx'=4,'tp'=2] {'shard'}, dimensions={0}, use_global_device_ids=true | all-gather | bytes 544 | tf_op jit(solution)/shard_map/all_gather | solution.py:609
  60.8 5.4 %all-to-all-start = ((bf16[4,64,2048]{2,1,0:T(8,128)(2,1)}), bf16[4,64,2048]{2,1,0:T(8,128)(2,1)S(1)}, u32[]{:S(2)}, u32[]{:S(2)}) async-start(bf16[4,64,2048]{2,1,0:T(8,128)(2,1)} %broadcast_in_dim.32), calls=%async_computation | async-start | bytes 2097152 | tf_op jit(solution)/shard_map/all_to_all | solution.py:538
  66.8 14.1 %all-to-all-done = bf16[4,64,2048]{2,1,0:T(8,128)(2,1)S(1)} async-done(((bf16[4,64,2048]{2,1,0:T(8,128)(2,1)}), bf16[4,64,2048]{2,1,0:T(8,128)(2,1)S(1)}, u32[]{:S(2)}, u32[]{:S(2)}) %all-to-all-start) | async-done | bytes 1048608 | tf_op jit(solution)/shard_map/all_to_all | solution.py:538
  84.6 5.9 %shard_map.263 = (bf16[512,2048]{1,0:T(8,128)(2,1)}, f32[512,384]{1,0:T(8,128)S(1)}, bf16[512,512]{1,0:T(8,128)(2,1)S(1)}, f32[512,256]{1,0:T(8,128)S(1)}) custom-call(bf16[256,2048]{1,0:T(8,128)(2,1)S(1)} %bitcast.115, bf16[256,2048]{1,0:T(8,128)(2,1)S(1)} %collective-permute-done.1.xb, bf16[2048,1024]{1,0:T(8,128)(2,1)} %all-gather.4.cloned.1.call-done.w.w_out, ...), custom_call_target="tpu_custom_call" | custom-call | flops 1610612736 | bytes 8388608 | tf_op jit(solution)/shard_map/pallas_call | solution.py:122
  91.4 6.6 %shard_map.264 = (f32[2,512,512]{2,1,0:T(8,128)S(1)}, f32[512,256]{1,0:T(8,128)S(1)}, bf16[512,256]{1,0:T(8,128)(2,1)S(1)}, f32[256,2048]{1,0:T(8,128)}, bf16[256,2048]{1,0:T(8,128)(2,1)S(1)}) custom-call(bf16[512,512]{1,0:T(8,128)(2,1)S(1)} %get-tuple-element.40.low, f32[512,256]{1,0:T(8,128)S(1)} %get-tuple-element.41.gate, ...), custom_call_target="tpu_custom_call" | custom-call | flops 805306368 | bytes 8388608 | tf_op jit(solution)/shard_map/pallas_call | solution.py:175
  98.4 2.3 collective-permute-done.4
  100.7 1.9 add_convert_fusion.3
  102.6 17.3 %all_to_all.65.parts = bf16[4,64,2048]{2,1,0:T(8,128)(2,1)S(1)} all-to-all(bf16[4,64,2048]{2,1,0:T(8,128)(2,1)S(1)} %bitcast.122), channel_id=1, replica_groups=mesh['shard'=16,'ctx'=4,'tp'=2] {'ctx'}, dimensions={0} | all-to-all | bytes 2097152 | tf_op jit(solution)/shard_map/all_to_all | solution.py:538
  121.0 3.5 all-to-all-start.3
  126.6 11.8 %all-to-all-done.3 = bf16[4,64,2048]{2,1,0:T(8,128)(2,1)S(1)} async-done(((bf16[4,64,2048]{2,1,0:T(8,128)(2,1)}), bf16[4,64,2048]{2,1,0:T(8,128)(2,1)S(1)}, u32[]{:S(2)}, u32[]{:S(2)}) %all-to-all-start.3) | async-done | bytes 1048608 | tf_op jit(solution)/shard_map/all_to_all | solution.py:538
  138.5 3.5 all-to-all-start.2
  142.0 2.2 collective-permute-start.6
  144.2 10.8 %all-to-all-done.2 = bf16[4,64,2048]{2,1,0:T(8,128)(2,1)S(1)} async-done(((bf16[4,64,2048]{2,1,0:T(8,128)(2,1)}), bf16[4,64,2048]{2,1,0:T(8,128)(2,1)S(1)}, u32[]{:S(2)}, u32[]{:S(2)}) %all-to-all-start.2) | async-done | bytes 1048608 | tf_op jit(solution)/shard_map/all_to_all | solution.py:538
  155.0 3.0 collective-permute-start.5
  158.0 2.3 collective-permute-done.5.ub
  162.5 18.5 %shard_map.266 = (bf16[512,768]{1,0:T(8,128)(2,1)S(1)}, bf16[512,768]{1,0:T(8,128)(2,1)S(1)}, bf16[512,768]{1,0:T(8,128)(2,1)S(1)}, f32[256,2048]{1,0:T(8,128)}, bf16[256,2048]{1,0:T(8,128)(2,1)S(1)}) custom-call(bf16[256,2048]{1,0:T(8,128)(2,1)S(1)} %bitcast.112, bf16[256,2048]{1,0:T(8,128)(2,1)S(1)} %copy-done.15, bf16[256,2048]{1,0:T(8,128)(2,1)} %bitcast.109, ...), custom_call_target="tpu_custom_call" | custom-call | flops 8053063680 | bytes 8388608 | tf_op jit(solution)/shard_map/pallas_call | solution.py:240
  183.2 9.7 %shard_map.274 = bf16[2048,2304]{1,0:T(8,128)(2,1)} custom-call(bf16[256,2048]{1,0:T(8,128)(2,1)S(1)} %bitcast.113, bf16[256,2048]{1,0:T(8,128)(2,1)S(1)} %copy-done.15, bf16[256,2048]{1,0:T(8,128)(2,1)S(1)} %bitcast.110, bf16[256,2048]{1,0:T(8,128)(2,1)} %collective-permute-done.6.cb, bf16[512,768]{1,0:T(8,128)(2,1)S(1)} %get-tuple-element.64.d_gate, ...), custom_call_target="tpu_custom_call" | custom-call | flops 4831838208 | bytes 8388608 | tf_op jit(solution)/shard_map/pallas_call | solution.py:290
  195.4 2.3 collective-permute-done.11
  197.6 1.9 add_convert_fusion.1
  199.6 17.4 %all_to_all.66.parts = bf16[4,64,2048]{2,1,0:T(8,128)(2,1)S(1)} all-to-all(bf16[4,64,2048]{2,1,0:T(8,128)(2,1)S(1)} %bitcast.123), channel_id=1, replica_groups=mesh['shard'=16,'ctx'=4,'tp'=2] {'ctx'}, dimensions={0} | all-to-all | bytes 2097152 | tf_op jit(solution)/shard_map/all_to_all | solution.py:538
  217.5 16.3 %all_to_all.67 = bf16[4,64,2048]{2,1,0:T(8,128)(2,1)S(1)} all-to-all(bf16[4,64,2048]{2,1,0:T(8,128)(2,1)S(1)} %get-tuple-element.53), channel_id=1, replica_groups=mesh['shard'=16,'ctx'=4,'tp'=2] {'ctx'}, dimensions={0} | all-to-all | bytes 2097152 | tf_op jit(solution)/shard_map/all_to_all | solution.py:538
  233.8 2.1 collective-permute-start.12
  236.0 4.2 shard_map.267
  240.4 2.2 shard_map.269
  242.7 3.1 shard_map.270
  245.8 5.3 %shard_map.271 = (f32[256,2048]{1,0:T(8,128)S(1)}, bf16[256,2048]{1,0:T(8,128)(2,1)}) custom-call(bf16[512,512]{1,0:T(8,128)(2,1)S(1)} %get-tuple-element.57.d_qkv, bf16[512,256]{1,0:T(8,128)(2,1)S(1)} %get-tuple-element.58.d_gate, bf16[2048,1024]{1,0:T(8,128)(2,1)} %all-gather.4.cloned.1.call-done.w.w_out), custom_call_target="tpu_custom_call" | custom-call | flops 1610612736 | bytes 8388608 | tf_op jit(solution)/shard_map/pallas_call | solution.py:408
  252.9 4.5 all-to-all-start.4
  257.4 3.1 add_convert_fusion
  260.5 11.5 %all-to-all-done.4 = bf16[4,64,2048]{2,1,0:T(8,128)(2,1)} async-done(((bf16[4,64,2048]{2,1,0:T(8,128)(2,1)}), bf16[4,64,2048]{2,1,0:T(8,128)(2,1)}, u32[]{:S(2)}, u32[]{:S(2)}) %all-to-all-start.4) | async-done | bytes 1048608 | tf_op jit(solution)/shard_map/all_to_all | solution.py:538
  272.0 4.3 all-to-all-start.7
  276.3 6.9 %shard_map.273 = bf16[2048,512]{1,0:T(8,128)(2,1)} custom-call(bf16[512,2048]{1,0:T(8,128)(2,1)} %get-tuple-element.61.xn, bf16[256,2048]{1,0:T(8,128)(2,1)S(1)} %bitcast.107, bf16[256,2048]{1,0:T(8,128)(2,1)S(1)} %collective-permute-done.12.db, bf16[512,256]{1,0:T(8,128)(2,1)S(1)} %copy-done.30, bf16[512,256]{1,0:T(8,128)(2,1)S(1)} %copy-done.28), custom_call_target="tpu_custom_call" | custom-call | flops 1073741824 | bytes 8388608 | tf_op jit(solution)/shard_map/pallas_call | solution.py:430
  283.2 7.0 %all-to-all-done.7 = bf16[4,64,2048]{2,1,0:T(8,128)(2,1)} async-done(((bf16[4,64,2048]{2,1,0:T(8,128)(2,1)}), bf16[4,64,2048]{2,1,0:T(8,128)(2,1)}, u32[]{:S(2)}, u32[]{:S(2)}) %all-to-all-start.7) | async-done | bytes 1048608 | tf_op jit(solution)/shard_map/all_to_all | solution.py:538
  290.2 4.4 all-to-all-start.10
  294.7 1.6 convert_reduce_fusion.2
  296.3 2.2 collective-permute-start.9
  303.3 4.7 %shard_map.272 = bf16[16,144,512]{2,1,0:T(8,128)(2,1)} custom-call(bf16[512,2048]{1,0:T(8,128)(2,1)S(1)} %copy-done.2, bf16[512,512]{1,0:T(8,128)(2,1)S(1)} %copy-done.26, f32[16,16,512]{2,1,0:T(8,128)S(1)} %pad.13.terms), custom_call_target="tpu_custom_call" | custom-call | flops 1073741824 | bytes 8388608 | tf_op jit(solution)/shard_map/pallas_call | solution.py:454
  308.0 12.4 %all-to-all-done.10 = bf16[16,128,512]{2,1,0:T(8,128)(2,1)} async-done(((bf16[16,128,512]{2,1,0:T(8,128)(2,1)}), bf16[16,128,512]{2,1,0:T(8,128)(2,1)}, u32[]{:S(2)}, u32[]{:S(2)}) %all-to-all-start.10) | async-done | bytes 2097184 | tf_op jit(solution)/shard_map/all_to_all | solution.py:563
  320.4 5.3 %all-to-all-start.8 = ((bf16[16,144,512]{2,1,0:T(8,128)(2,1)}), bf16[16,144,512]{2,1,0:T(8,128)(2,1)S(1)}, u32[]{:S(2)}, u32[]{:S(2)}) async-start(bf16[16,144,512]{2,1,0:T(8,128)(2,1)} %shard_map.272), calls=%async_computation.8 | async-start | bytes 4718592 | tf_op jit(solution)/shard_map/all_to_all | solution.py:563
  328.3 2.2 select_convert_fusion.1
  332.3 3.5 collective-permute-start.14
  335.9 1.9 reduce_sum.214
  337.8 3.3 collective-permute-start.18
  341.1 12.4 %all-to-all-done.8 = bf16[16,144,512]{2,1,0:T(8,128)(2,1)S(1)} async-done(((bf16[16,144,512]{2,1,0:T(8,128)(2,1)}), bf16[16,144,512]{2,1,0:T(8,128)(2,1)S(1)}, u32[]{:S(2)}, u32[]{:S(2)}) %all-to-all-start.8) | async-done | bytes 2359328 | tf_op jit(solution)/shard_map/all_to_all | solution.py:563
  353.8 6.2 %collective-permute-start.16 = (bf16[16,512]{1,0:T(8,128)(2,1)S(1)}, bf16[16,512]{1,0:T(8,128)(2,1)S(1)}, u32[]{:S(2)}, u32[]{:S(2)}) collective-permute-start(bf16[16,512]{1,0:T(8,128)(2,1)S(1)} %slice.120), channel_id=1, source_target_pairs={{0,8},{8,0},{16,24},{24,16},{32,40},{40,32},{48,56},{56,48},{64,72... | collective-permute-start | bytes 49160 | tf_op jit(solution)/shard_map/ppermute | solution.py:535
  361.1 3.5 all-to-all-start.11
  365.6 2.2 collective-permute-start.19
  368.6 3.5 collective-permute-start.17
  372.1 2.0 maximum_select_fusion.1
  375.4 3.4 collective-permute-done.17
  379.7 4.2 all-to-all-start.9
  384.2 9.7 %all-to-all-done.9 = bf16[4,144,512]{2,1,0:T(8,128)(2,1)S(1)} async-done(((bf16[4,144,512]{2,1,0:T(8,128)(2,1)}), bf16[4,144,512]{2,1,0:T(8,128)(2,1)S(1)}, u32[]{:S(2)}, u32[]{:S(2)}) %all-to-all-start.9) | async-done | bytes 589856 | tf_op jit(solution)/shard_map/all_to_all | solution.py:538
  394.0 1.7 broadcast_in_dim.42
  395.7 3.6 all-to-all-start.12
  400.4 2.1 select_convert_fusion
  404.9 1.5 convert_element_type.151
  408.5 19.7 %all-to-all-done.12 = bf16[4,128,2304]{1,2,0:T(8,128)(2,1)S(1)} async-done(((bf16[4,128,2304]{1,2,0:T(8,128)(2,1)}), bf16[4,128,2304]{1,2,0:T(8,128)(2,1)S(1)}, u32[]{:S(2)}, u32[]{:S(2)}) %all-to-all-start.12) | async-done | bytes 2359328 | tf_op jit(solution)/shard_map/all_to_all | solution.py:538
  428.2 2.3 fusion.20
  430.5 3.2 copy.121
  433.7 1.6 copy.122
  435.3 4.4 broadcast_multiply_fusion
  (251 shorter events, 52.8 us)
Async XLA Ops:
  7.2 13.1 %copy-start = (bf16[3072,128]{1,0:T(8,128)(2,1)S(1)}, bf16[3072,128]{1,0:T(8,128)(2,1)}, u32[]{:S(2)}) copy-start(bf16[3072,128]{1,0:T(8,128)(2,1)} %param.30) | copy-start | bytes 2359300
  7.2 13.0 %copy-start.57 = (bf16[128]{0:T(256)(128)(2,1)S(1)}, bf16[128]{0:T(256)(128)(2,1)}, u32[]{:S(2)}) copy-start(bf16[128]{0:T(256)(128)(2,1)} %param.27) | copy-start | bytes 772
  7.2 77.4 %all-gather.4.cloned.1.call-start = ((), (), s32[]{:S(2)}) async-start(), calls=%async_computation.14 | async-start | bytes 4456448 | tf_op jit(solution)/shard_map/all_gather | solution.py:555
  10.8 8.6 %collective-permute-start.2 = (bf16[128,1024]{1,0:T(8,128)(2,1)S(1)}, bf16[128,1024]{1,0:T(8,128)(2,1)S(1)}, u32[]{:S(2)}, u32[]{:S(2)}) collective-permute-start(bf16[128,1024]{1,0:T(8,128)(2,1)S(1)} %pad_maximum_fusion.1), channel_id=1, source_target_pairs={{8,1},{1,8},{24,17},{17,24},{40,33},{33,40},{56,49},{49,56},{72,65... | collective-permute-start | bytes 786440 | tf_op jit(solution)/shard_map/ppermute | solution.py:591
  20.2 141.1 %all-gather.6.cloned.1.call-start = ((), (), s32[]{:S(2)}) async-start(), calls=%async_computation.15 | async-start | bytes 10027008 | tf_op jit(solution)/shard_map/all_gather | solution.py:555
  21.5 12.6 %copy-start.39 = (bf16[128,2048]{1,0:T(8,128)(2,1)S(1)}, bf16[128,2048]{1,0:T(8,128)(2,1)}, u32[]{:S(2)}) copy-start(bf16[128,2048]{1,0:T(8,128)(2,1)} %param.16) | copy-start | bytes 1572868
  21.5 12.6 %copy-start.40 = (bf16[128,2048]{1,0:T(8,128)(2,1)S(1)}, bf16[128,2048]{1,0:T(8,128)(2,1)}, u32[]{:S(2)}) copy-start(bf16[128,2048]{1,0:T(8,128)(2,1)} %param.31) | copy-start | bytes 1572868
  21.7 12.5 %copy-start.55 = (s32[1,13]{1,0:T(1,128)S(1)}, s32[1,13]{1,0:T(1,128)}, u32[]{:S(2)}) copy-start(s32[1,13]{1,0:T(1,128)} %param.18) | copy-start | bytes 160
  21.7 12.5 %copy-start.56 = (s32[1,13]{1,0:T(1,128)S(1)}, s32[1,13]{1,0:T(1,128)}, u32[]{:S(2)}) copy-start(s32[1,13]{1,0:T(1,128)} %param.17) | copy-start | bytes 160
  21.7 13.5 %copy-start.58 = (bf16[8]{0:T(256)(128)(2,1)S(1)}, bf16[8]{0:T(256)(128)(2,1)}, u32[]{:S(2)}) copy-start(bf16[8]{0:T(256)(128)(2,1)} %param.26) | copy-start | bytes 52
  21.8 13.5 %copy-start.59 = (bf16[8]{0:T(256)(128)(2,1)S(1)}, bf16[8]{0:T(256)(128)(2,1)}, u32[]{:S(2)}) copy-start(bf16[8]{0:T(256)(128)(2,1)} %param.25) | copy-start | bytes 52
  21.8 11.3 %collective-permute-start.7 = (bf16[128,2304]{1,0:T(8,128)(2,1)S(1)}, bf16[128,2304]{1,0:T(8,128)(2,1)S(1)}, u32[]{:S(2)}, u32[]{:S(2)}) collective-permute-start(bf16[128,2304]{1,0:T(8,128)(2,1)S(1)} %pad_maximum_fusion), channel_id=1, source_target_pairs={{8,1},{1,8},{24,17},{17,24},{40,33},{33,40},{56,49},{49,56},{72,65... | collective-permute-start | bytes 1769480 | tf_op jit(solution)/shard_map/ppermute | solution.py:591
  34.2 25.3 %collective-permute-start = (bf16[2,64,2048]{2,1,0:T(8,128)(2,1)S(1)}, bf16[2,64,2048]{2,1,0:T(8,128)(2,1)S(1)}, u32[]{:S(2)}, u32[]{:S(2)}) collective-permute-start(bf16[2,64,2048]{2,1,0:T(8,128)(2,1)S(1)} %fusion.6), channel_id=1, source_target_pairs={{0,8},{8,0},{16,24},{24,16},{32,40},{40,32},{48,56},{56,48},{64,72... | collective-permute-start | bytes 1572872 | tf_op jit(solution)/shard_map/ppermute | solution.py:535
  34.3 31.9 %collective-permute-start.3 = (s32[2,13]{1,0:T(2,128)S(1)}, s32[2,13]{1,0:T(2,128)S(1)}, u32[]{:S(2)}, u32[]{:S(2)}) collective-permute-start(s32[2,13]{1,0:T(2,128)S(1)} %pad_add_fusion.2), channel_id=1, source_target_pairs={{0,8},{8,0},{16,24},{24,16},{32,40},{40,32},{48,56},{56,48},{64,72... | collective-permute-start | bytes 320 | tf_op jit(solution)/shard_map/ppermute | solution.py:535
  60.8 20.1 %all-to-all-start = ((bf16[4,64,2048]{2,1,0:T(8,128)(2,1)}), bf16[4,64,2048]{2,1,0:T(8,128)(2,1)S(1)}, u32[]{:S(2)}, u32[]{:S(2)}) async-start(bf16[4,64,2048]{2,1,0:T(8,128)(2,1)} %broadcast_in_dim.32), calls=%async_computation | async-start | bytes 2097152 | tf_op jit(solution)/shard_map/all_to_all | solution.py:538
  81.0 3.6 collective-permute-start.1
  91.4 6.6 %copy-start.5 = (f32[512,256]{1,0:T(8,128)}, f32[512,256]{1,0:T(8,128)S(1)}, u32[]{:S(2)}) copy-start(f32[512,256]{1,0:T(8,128)S(1)} %get-tuple-element.41.gate) | copy-start | bytes 1572868
  91.4 6.6 %copy-start.7 = (bf16[512,512]{1,0:T(8,128)(2,1)}, bf16[512,512]{1,0:T(8,128)(2,1)S(1)}, u32[]{:S(2)}) copy-start(bf16[512,512]{1,0:T(8,128)(2,1)S(1)} %get-tuple-element.40.low) | copy-start | bytes 1572868
  98.0 4.6 %copy-start.27 = (bf16[512,256]{1,0:T(8,128)(2,1)}, bf16[512,256]{1,0:T(8,128)(2,1)S(1)}, u32[]{:S(2)}) copy-start(bf16[512,256]{1,0:T(8,128)(2,1)S(1)} %get-tuple-element.63.gated) | copy-start | bytes 786436
  98.0 2.7 collective-permute-start.4
  121.0 17.4 %all-to-all-start.3 = ((bf16[4,64,2048]{2,1,0:T(8,128)(2,1)}), bf16[4,64,2048]{2,1,0:T(8,128)(2,1)S(1)}, u32[]{:S(2)}, u32[]{:S(2)}) async-start(bf16[4,64,2048]{2,1,0:T(8,128)(2,1)} %broadcast_in_dim.39), calls=%async_computation.3 | async-start | bytes 2097152 | tf_op jit(solution)/shard_map/all_to_all | solution.py:538
  138.5 22.8 %copy-start.3 = (bf16[4,64,2048]{2,1,0:T(8,128)(2,1)}, bf16[4,64,2048]{2,1,0:T(8,128)(2,1)S(1)}, u32[]{:S(2)}) copy-start(bf16[4,64,2048]{2,1,0:T(8,128)(2,1)S(1)} %all-to-all-done.3) | copy-start | bytes 3145732
  138.5 16.5 %all-to-all-start.2 = ((bf16[4,64,2048]{2,1,0:T(8,128)(2,1)}), bf16[4,64,2048]{2,1,0:T(8,128)(2,1)S(1)}, u32[]{:S(2)}, u32[]{:S(2)}) async-start(bf16[4,64,2048]{2,1,0:T(8,128)(2,1)} %copy-done.16), calls=%async_computation.2 | async-start | bytes 2097152 | tf_op jit(solution)/shard_map/all_to_all | solution.py:538
  142.0 223.6 %reduce-scatter.2.cloned.1.call-start = ((), (), s32[]{:S(2)}) async-start(), calls=%async_computation.16 | async-start | bytes 10027008 | tf_op jit(solution)/shard_map/reduce_scatter | solution.py:558
  142.0 16.0 %collective-permute-start.6 = (bf16[256,2048]{1,0:T(8,128)(2,1)S(1)}, bf16[256,2048]{1,0:T(8,128)(2,1)}, u32[]{:S(2)}, u32[]{:S(2)}) collective-permute-start(bf16[256,2048]{1,0:T(8,128)(2,1)S(1)} %bitcast.108), channel_id=1, source_target_pairs={{0,8},{8,0},{16,24},{24,16},{32,40},{40,32},{48,56},{56,48},{64,72... | collective-permute-start | bytes 3145736 | tf_op jit(solution)/shard_map/ppermute | solution.py:535
  155.0 5.3 %collective-permute-start.5 = (bf16[256,2048]{1,0:T(8,128)(2,1)S(1)}, bf16[256,2048]{1,0:T(8,128)(2,1)S(1)}, u32[]{:S(2)}, u32[]{:S(2)}) collective-permute-start(bf16[256,2048]{1,0:T(8,128)(2,1)S(1)} %bitcast.111), channel_id=1, source_target_pairs={{0,8},{8,0},{16,24},{24,16},{32,40},{40,32},{48,56},{56,48},{64,72... | collective-permute-start | bytes 3145736 | tf_op jit(solution)/shard_map/ppermute | solution.py:535
  195.0 2.7 collective-permute-start.11
  199.6 17.4 %copy-start.12 = (f32[64,2048]{1,0:T(8,128)S(1)}, f32[64,2048]{1,0:T(8,128)}, u32[]{:S(2)}) copy-start(f32[64,2048]{1,0:T(8,128)} %copy-done.11) | copy-start | bytes 1572868
  217.0 19.0 %copy-start.20 = (bf16[512,768]{1,0:T(8,128)(2,1)S(1)}, bf16[512,768]{1,0:T(8,128)(2,1)}, u32[]{:S(2)}) copy-start(bf16[512,768]{1,0:T(8,128)(2,1)} %copy-done.19) | copy-start | bytes 2359300
  217.5 16.3 %copy-start.23 = (f32[64,2048]{1,0:T(8,128)}, f32[64,2048]{1,0:T(8,128)S(1)}, u32[]{:S(2)}) copy-start(f32[64,2048]{1,0:T(8,128)S(1)} %get-tuple-element.51) | copy-start | bytes 1572868
  233.8 6.5 %copy-start.6 = (f32[512,256]{1,0:T(8,128)S(1)}, f32[512,256]{1,0:T(8,128)}, u32[]{:S(2)}) copy-start(f32[512,256]{1,0:T(8,128)} %copy-done.5) | copy-start | bytes 1572868
  233.8 6.5 %copy-start.22 = (f32[512,256]{1,0:T(8,128)S(1)}, f32[512,256]{1,0:T(8,128)}, u32[]{:S(2)}) copy-start(f32[512,256]{1,0:T(8,128)} %copy-done.21) | copy-start | bytes 1572868
  233.8 6.5 %collective-permute-start.12 = (bf16[256,2048]{1,0:T(8,128)(2,1)S(1)}, bf16[256,2048]{1,0:T(8,128)(2,1)S(1)}, u32[]{:S(2)}, u32[]{:S(2)}) collective-permute-start(bf16[256,2048]{1,0:T(8,128)(2,1)S(1)} %bitcast.105), channel_id=1, source_target_pairs={{0,8},{8,0},{16,24},{24,16},{32,40},{40,32},{48,56},{56,48},{64,72... | collective-permute-start | bytes 3145736 | tf_op jit(solution)/shard_map/ppermute | solution.py:535
  240.2 11.4 %collective-permute-start.8 = (bf16[256,2048]{1,0:T(8,128)(2,1)S(1)}, bf16[256,2048]{1,0:T(8,128)(2,1)S(1)}, u32[]{:S(2)}, u32[]{:S(2)}) collective-permute-start(bf16[256,2048]{1,0:T(8,128)(2,1)S(1)} %get-tuple-element.48), channel_id=1, source_target_pairs={{0,8},{8,0},{16,24},{24,16},{32,40},{40,32},{48,56},{56,48},{64,72... | collective-permute-start | bytes 3145736 | tf_op jit(solution)/shard_map/ppermute | solution.py:535
  245.8 5.3 %copy-start.25 = (bf16[512,512]{1,0:T(8,128)(2,1)}, bf16[512,512]{1,0:T(8,128)(2,1)S(1)}, u32[]{:S(2)}) copy-start(bf16[512,512]{1,0:T(8,128)(2,1)S(1)} %get-tuple-element.57.d_qkv) | copy-start | bytes 1572868
  251.1 6.3 %collective-permute-start.13 = (bf16[256,2048]{1,0:T(8,128)(2,1)}, bf16[256,2048]{1,0:T(8,128)(2,1)}, u32[]{:S(2)}, u32[]{:S(2)}) collective-permute-start(bf16[256,2048]{1,0:T(8,128)(2,1)} %get-tuple-element.60), channel_id=1, source_target_pairs={{0,8},{8,0},{16,24},{24,16},{32,40},{40,32},{48,56},{56,48},{64,72... | collective-permute-start | bytes 3145736 | tf_op jit(solution)/shard_map/ppermute | solution.py:535
  252.9 19.1 %all-to-all-start.4 = ((bf16[4,64,2048]{2,1,0:T(8,128)(2,1)}), bf16[4,64,2048]{2,1,0:T(8,128)(2,1)}, u32[]{:S(2)}, u32[]{:S(2)}) async-start(bf16[4,64,2048]{2,1,0:T(8,128)(2,1)} %bitcast.121), calls=%async_computation.4 | async-start | bytes 2097152 | tf_op jit(solution)/shard_map/all_to_all | solution.py:538
  260.5 15.8 %copy-start.28 = (bf16[512,256]{1,0:T(8,128)(2,1)S(1)}, bf16[512,256]{1,0:T(8,128)(2,1)}, u32[]{:S(2)}) copy-start(bf16[512,256]{1,0:T(8,128)(2,1)} %copy-done.27) | copy-start | bytes 786436
  260.5 15.8 %copy-start.30 = (bf16[512,256]{1,0:T(8,128)(2,1)S(1)}, bf16[512,256]{1,0:T(8,128)(2,1)}, u32[]{:S(2)}) copy-start(bf16[512,256]{1,0:T(8,128)(2,1)} %copy-done.29) | copy-start | bytes 786436
  272.0 18.2 %all-to-all-start.7 = ((bf16[4,64,2048]{2,1,0:T(8,128)(2,1)}), bf16[4,64,2048]{2,1,0:T(8,128)(2,1)}, u32[]{:S(2)}, u32[]{:S(2)}) async-start(bf16[4,64,2048]{2,1,0:T(8,128)(2,1)} %bitcast.120), calls=%async_computation.7 | async-start | bytes 2097152 | tf_op jit(solution)/shard_map/all_to_all | solution.py:538
  290.2 30.2 %all-to-all-start.10 = ((bf16[16,128,512]{2,1,0:T(8,128)(2,1)}), bf16[16,128,512]{2,1,0:T(8,128)(2,1)}, u32[]{:S(2)}, u32[]{:S(2)}) async-start(bf16[16,128,512]{2,1,0:T(8,128)(2,1)} %bitcast.40), calls=%async_computation.10 | async-start | bytes 4194304 | tf_op jit(solution)/shard_map/all_to_all | solution.py:563
  294.7 7.6 %copy-start.2 = (bf16[512,2048]{1,0:T(8,128)(2,1)S(1)}, bf16[512,2048]{1,0:T(8,128)(2,1)}, u32[]{:S(2)}) copy-start(bf16[512,2048]{1,0:T(8,128)(2,1)} %get-tuple-element.61.xn) | copy-start | bytes 6291460
  296.3 3.4 collective-permute-start.9
  300.6 27.7 %collective-permute-start.10 = (bf16[128,2048]{1,0:T(8,128)(2,1)}, bf16[128,2048]{1,0:T(8,128)(2,1)}, u32[]{:S(2)}, u32[]{:S(2)}) collective-permute-start(bf16[128,2048]{1,0:T(8,128)(2,1)} %maximum_select_fusion), channel_id=1, source_target_pairs={{0,1},{9,8},{16,17},{25,24},{32,33},{41,40},{48,49},{57,56},{64,65... | collective-permute-start | bytes 1572872 | tf_op jit(solution)/shard_map/ppermute | solution.py:715
  308.0 17.7 %copy-start.53 = (bf16[128,512]{1,0:T(8,128)(2,1)S(1)}, bf16[128,512]{1,0:T(8,128)(2,1)}, u32[]{:S(2)}) copy-start(bf16[128,512]{1,0:T(8,128)(2,1)} %param.21) | copy-start | bytes 393220
  308.0 17.8 %copy-start.54 = (bf16[128,512]{1,0:T(8,128)(2,1)S(1)}, bf16[128,512]{1,0:T(8,128)(2,1)}, u32[]{:S(2)}) copy-start(bf16[128,512]{1,0:T(8,128)(2,1)} %param.22) | copy-start | bytes 393220
  308.0 18.6 %copy-start.51 = (bf16[128,1024]{1,0:T(8,128)(2,1)S(1)}, bf16[128,1024]{1,0:T(8,128)(2,1)}, u32[]{:S(2)}) copy-start(bf16[128,1024]{1,0:T(8,128)(2,1)} %param.20) | copy-start | bytes 786436
  308.0 19.4 %copy-start.52 = (bf16[128,1024]{1,0:T(8,128)(2,1)S(1)}, bf16[128,1024]{1,0:T(8,128)(2,1)}, u32[]{:S(2)}) copy-start(bf16[128,1024]{1,0:T(8,128)(2,1)} %param.23) | copy-start | bytes 786436
  320.4 33.1 %all-to-all-start.8 = ((bf16[16,144,512]{2,1,0:T(8,128)(2,1)}), bf16[16,144,512]{2,1,0:T(8,128)(2,1)S(1)}, u32[]{:S(2)}, u32[]{:S(2)}) async-start(bf16[16,144,512]{2,1,0:T(8,128)(2,1)} %shard_map.272), calls=%async_computation.8 | async-start | bytes 4718592 | tf_op jit(solution)/shard_map/all_to_all | solution.py:563
  332.3 39.8 %collective-permute-start.14 = (bf16[64,2048]{1,0:T(8,128)(2,1)S(1)}, bf16[64,2048]{1,0:T(8,128)(2,1)}, u32[]{:S(2)}, u32[]{:S(2)}) collective-permute-start(bf16[64,2048]{1,0:T(8,128)(2,1)S(1)} %fusion.4), channel_id=1, source_target_pairs={{0,8},{8,0},{16,24},{24,16},{32,40},{40,32},{48,56},{56,48},{64,72... | collective-permute-start | bytes 786440 | tf_op jit(solution)/shard_map/ppermute | solution.py:535
  337.8 22.3 %collective-permute-start.18 = (bf16[128,512]{1,0:T(8,128)(2,1)S(1)}, bf16[128,512]{1,0:T(8,128)(2,1)S(1)}, u32[]{:S(2)}, u32[]{:S(2)}) collective-permute-start(bf16[128,512]{1,0:T(8,128)(2,1)S(1)} %reduce_sum.214), channel_id=1, source_target_pairs={{8,1},{1,8},{24,17},{17,24},{40,33},{33,40},{56,49},{49,56},{72,65... | collective-permute-start | bytes 393224 | tf_op jit(solution)/shard_map/ppermute | solution.py:591
  353.8 7.3 %copy-start.48 = (f32[144,512]{1,0:T(8,128)}, f32[144,512]{1,0:T(8,128)S(1)}, u32[]{:S(2)}) copy-start(f32[144,512]{1,0:T(8,128)S(1)} %convert_reduce_fusion) | copy-start | bytes 884740
  353.8 14.0 %collective-permute-start.16 = (bf16[16,512]{1,0:T(8,128)(2,1)S(1)}, bf16[16,512]{1,0:T(8,128)(2,1)S(1)}, u32[]{:S(2)}, u32[]{:S(2)}) collective-permute-start(bf16[16,512]{1,0:T(8,128)(2,1)S(1)} %slice.120), channel_id=1, source_target_pairs={{0,8},{8,0},{16,24},{24,16},{32,40},{40,32},{48,56},{56,48},{64,72... | collective-permute-start | bytes 49160 | tf_op jit(solution)/shard_map/ppermute | solution.py:535
  361.1 17.7 %all-to-all-start.11 = ((bf16[4,128,512]{1,2,0:T(8,128)(2,1)}), bf16[4,128,512]{1,2,0:T(8,128)(2,1)S(1)}, u32[]{:S(2)}, u32[]{:S(2)}) async-start(bf16[4,128,512]{1,2,0:T(8,128)(2,1)} %broadcast_in_dim.41), calls=%async_computation.11 | async-start | bytes 1048576 | tf_op jit(solution)/shard_map/all_to_all | solution.py:538
  365.6 18.3 %copy-start.49 = (bf16[128,2304]{1,0:T(8,128)(2,1)S(1)}, bf16[128,2304]{1,0:T(8,128)(2,1)}, u32[]{:S(2)}) copy-start(bf16[128,2304]{1,0:T(8,128)(2,1)} %reduce-scatter.2.cloned.1.call-done) | copy-start | bytes 1769476
  365.6 18.3 %collective-permute-start.19 = (bf16[128,2304]{1,0:T(8,128)(2,1)}, bf16[128,2304]{1,0:T(8,128)(2,1)S(1)}, u32[]{:S(2)}, u32[]{:S(2)}) collective-permute-start(bf16[128,2304]{1,0:T(8,128)(2,1)} %reduce-scatter.2.cloned.1.call-done), channel_id=1, source_target_pairs={{8,1},{1,8},{24,17},{17,24},{40,33},{33,40},{56,49},{49,56},{72,65... | collective-permute-start | bytes 1769480 | tf_op jit(solution)/shard_map/ppermute | solution.py:591
  368.6 10.1 %collective-permute-start.17 = (bf16[144,512]{1,0:T(8,128)(2,1)S(1)}, bf16[144,512]{1,0:T(8,128)(2,1)S(1)}, u32[]{:S(2)}, u32[]{:S(2)}) collective-permute-start(bf16[144,512]{1,0:T(8,128)(2,1)S(1)} %pad_maximum_fusion.3), channel_id=1, source_target_pairs={{8,1},{1,8},{24,17},{17,24},{40,33},{33,40},{56,49},{49,56},{72,65... | collective-permute-start | bytes 442376 | tf_op jit(solution)/shard_map/ppermute | solution.py:591
  374.1 26.3 %collective-permute-start.15 = (bf16[128,2048]{1,0:T(8,128)(2,1)}, bf16[128,2048]{1,0:T(8,128)(2,1)}, u32[]{:S(2)}, u32[]{:S(2)}) collective-permute-start(bf16[128,2048]{1,0:T(8,128)(2,1)} %maximum_select_fusion.1), channel_id=1, source_target_pairs={{0,1},{9,8},{16,17},{25,24},{32,33},{41,40},{48,49},{57,56},{64,65... | collective-permute-start | bytes 1572872 | tf_op jit(solution)/shard_map/ppermute | solution.py:715
  379.7 14.3 %all-to-all-start.9 = ((bf16[4,144,512]{2,1,0:T(8,128)(2,1)}), bf16[4,144,512]{2,1,0:T(8,128)(2,1)S(1)}, u32[]{:S(2)}, u32[]{:S(2)}) async-start(bf16[4,144,512]{2,1,0:T(8,128)(2,1)} %broadcast_in_dim.40), calls=%async_computation.9 | async-start | bytes 1179648 | tf_op jit(solution)/shard_map/all_to_all | solution.py:538
  395.7 32.5 %all-to-all-start.12 = ((bf16[4,128,2304]{1,2,0:T(8,128)(2,1)}), bf16[4,128,2304]{1,2,0:T(8,128)(2,1)S(1)}, u32[]{:S(2)}, u32[]{:S(2)}) async-start(bf16[4,128,2304]{1,2,0:T(8,128)(2,1)} %broadcast_in_dim.42), calls=%async_computation.13 | async-start | bytes 4718592 | tf_op jit(solution)/shard_map/all_to_all | solution.py:538
  435.3 5.1 %copy-start.45 = (f32[128,512]{0,1:T(8,128)S(1)}, f32[128,512]{0,1:T(8,128)}, u32[]{:S(2)}) copy-start(f32[128,512]{0,1:T(8,128)} %get-tuple-element.153) | copy-start | bytes 786436
  435.3 6.7 %copy-start.42 = (f32[128,1024]{0,1:T(8,128)S(1)}, f32[128,1024]{0,1:T(8,128)}, u32[]{:S(2)}) copy-start(f32[128,1024]{0,1:T(8,128)} %get-tuple-element.151) | copy-start | bytes 1572868
  435.3 9.3 %copy-start.1 = (bf16[3072,128]{1,0:T(8,128)(2,1)S(1)}, bf16[3072,128]{1,0:T(8,128)(2,1)}, u32[]{:S(2)}) copy-start(bf16[3072,128]{1,0:T(8,128)(2,1)} %param.30) | copy-start | bytes 2359300
  439.7 4.3 collective-permute-start.20
  (30 other events, 63.9 us)
Sparse Core Ops, SparseCore 0:
  20.3 53.4 all-gather.3
  76.6 75.1 all-gather.5
  193.9 80.6 reduce-scatter.1

commit v3 on v2

--- a/solution.py
+++ b/solution.py
@@ -76,11 +76,16 @@
     return slice(number * HD, (number + 1) * HD)
 
 
-def call(kernel, grid, in_specs, out_specs, out_shape, flops, scratch=(), moved=8 << 20):
-    return pl.pallas_call(
-        kernel,
+def call(kernel, grid, in_specs, out_specs, out_shape, flops, scratch=(), moved=8 << 20, behind=()):
+    count = len(in_specs)
+
+    def body(*refs):
+        kernel(*refs[:count], *refs[count + len(behind) :])
+
+    built = pl.pallas_call(
+        body,
         grid=grid,
-        in_specs=in_specs,
+        in_specs=list(in_specs) + [pl.BlockSpec(memory_space=pl.ANY)] * len(behind),
         out_specs=out_specs,
         out_shape=out_shape,
         scratch_shapes=scratch,
@@ -89,6 +94,7 @@
         ),
         cost_estimate=pl.CostEstimate(flops=flops, bytes_accessed=moved, transcendentals=0),
     )
+    return lambda *operands: built(*operands, *behind)
 
 
 def struct(shape, dtype):
@@ -103,42 +109,61 @@
     return pl.BlockSpec((rows, columns), lambda i: (i, 0))
 
 
-def project_kernel(xa, xb, w, gains, cosine, sine, xn, pre, low, gate):
-    x = jnp.where(pl.program_id(0) == 0, xa[...], xb[...]).astype(F32)
+def piled(shape, which):
+    return pl.BlockSpec((shape[0], shape[1] // 2, shape[2]), lambda i: (0, which, 0))
+
+
+def flat(value):
+    return value.reshape((-1,) + value.shape[2:])
+
+
+def project_kernel(xa, xb, w, ends, cosine, sine, xn, pre, low, gate, gains):
+    x = flat(jnp.where(pl.program_id(0) == 0, xa[...], xb[...])).astype(F32)
     normed = (x * rms_scale(x)).astype(BF16)
     xn[...] = normed
     out = dot(normed, w[...])
+    found = jnp.zeros((16, HD), F32)
+    for start in range(0, ends.shape[0], HD):
+        found = found + ends[start : start + 16, :].astype(F32)
+    gains[...] = found
     for place in range(3):
         raw = out[:, head(place)]
         pre[:, head(place)] = raw
-        unit = raw * rms_scale(raw) * gains[pl.ds(place // 2, 1), :]
+        unit = raw * rms_scale(raw) * found[place // 2 : place // 2 + 1, :]
         low[:, head(place)] = (unit * cosine[...] + turn(unit) * sine[...]).astype(BF16)
     low[:, head(3)] = out[:, head(3)].astype(BF16)
     gate[...] = out[:, 4 * HD :]
 
 
-def project(xa, xb, w, gains, cosine, sine):
-    half, width = xa.shape
+def project(xa, xb, w, cosine, sine):
+    half, width = xa.shape[0] * xa.shape[1] // 2, xa.shape[2]
     return call(
         project_kernel,
         (2,),
         [
-            fixed((half, width)),
-            fixed((half, width)),
+            piled(xa.shape, 0),
+            piled(xb.shape, 0),
             fixed((width, 6 * HD)),
-            fixed((2, HD)),
+            pl.BlockSpec((width, HD), lambda i: (0, 8)),
             rowed(half, HD),
             rowed(half, HD),
         ],
-        [rowed(half, width), rowed(half, 3 * HD), rowed(half, 4 * HD), rowed(half, 2 * HD)],
+        [
+            rowed(half, width),
+            rowed(half, 3 * HD),
+            rowed(half, 4 * HD),
+            rowed(half, 2 * HD),
+            fixed((16, HD)),
+        ],
         [
             struct((2 * half, width), BF16),
             struct((2 * half, 3 * HD), F32),
             struct((2 * half, 4 * HD), BF16),
             struct((2 * half, 2 * HD), F32),
+            struct((16, HD), F32),
         ],
         2 * 2 * half * width * 6 * HD,
-    )(xa, xb, w, gains, cosine, sine)
+    )(xa, xb, w, w, cosine, sine)
 
 
 def attend_kernel(low, gate, w_out, of_row, of_column, probs, attended, gated, mine, other):
@@ -200,29 +225,37 @@
     )(low, gate, w, of_row, of_column)
 
 
-def feed_kernel(ua, ub, ca, cb, wg, wu, wd, hidden, d_gate, d_up, mine, other, total):
+def feed_kernel(
+    ua, ub, ca, cb, wg, wu, wd, hidden, d_gate, d_up, mine, other, total, u_all, c_all
+):
     step = pl.program_id(0)
     half = ua.shape[0]
-    for number, (u, cot) in enumerate(((ua, ca), (ub, cb))):
-        rows = slice(number * half, (number + 1) * half)
-        gate, up = dot(u[...], wg[...]), dot(u[...], wu[...])
-        d_hidden = dot(cot[...], wd[...])
-        sig = jax.nn.sigmoid(gate)
-        silu = gate * sig
-        hidden[rows, :] = (silu * up).astype(BF16)
-        dg = (d_hidden * up * sig * (1.0 + gate * (1.0 - sig))).astype(BF16)
-        du = (d_hidden * silu).astype(BF16)
-        d_gate[rows, :] = dg
-        d_up[rows, :] = du
-        term = dot_back(dg, wg[...]) + dot_back(du, wu[...])
-
-        @pl.when(step == 0)
-        def _():
-            total[rows, :] = term
-
-        @pl.when(step > 0)
-        def _():
-            total[rows, :] += term
+
+    @pl.when(step == 0)
+    def _():
+        u_all[:half, :] = ua[...]
+        u_all[half:, :] = ub[...]
+        c_all[:half, :] = flat(ca[...])
+        c_all[half:, :] = flat(cb[...])
+
+    gate, up = dot(u_all[...], wg[...]), dot(u_all[...], wu[...])
+    d_hidden = dot(c_all[...], wd[...])
+    sig = jax.nn.sigmoid(gate)
+    silu = gate * sig
+    hidden[...] = (silu * up).astype(BF16)
+    dg = (d_hidden * up * sig * (1.0 + gate * (1.0 - sig))).astype(BF16)
+    du = (d_hidden * silu).astype(BF16)
+    d_gate[...] = dg
+    d_up[...] = du
+    term = dot_back(dg, wg[...]) + dot_back(du, wu[...])
+
+    @pl.when(step == 0)
+    def _():
+        total[...] = term
+
+    @pl.when(step > 0)
+    def _():
+        total[...] += term
 
     @pl.when(step == pl.num_programs(0) - 1)
     def _():
@@ -240,12 +273,14 @@
     return call(
         feed_kernel,
         (parts,),
-        [fixed((half, width))] * 4 + [column(0), column(1), column(2)],
+        [fixed((half, width))] * 2
+        + [piled(ca.shape, 1)] * 2
+        + [column(0), column(1), column(2)],
         [unit, unit, unit, fixed((half, width)), fixed((half, width))],
         [struct((2 * half, units), BF16)] * 3
         + [struct((half, width), F32), struct((half, width), BF16)],
         2 * 2 * half * width * units * 5,
-        scratch=[pltpu.VMEM((2 * half, width), F32)],
+        scratch=[pltpu.VMEM((2 * half, width), F32)] + [pltpu.VMEM((2 * half, width), BF16)] * 2,
     )(ua, ub, ca, cb, w, w, w)
 
 
@@ -261,7 +296,7 @@
         other[...] = out.astype(BF16)
 
 
-def down_product(left, w, place):
+def down_product(left, w, place, behind):
     length, units = left.shape
     half, width = length // 2, w.shape[0]
     return call(
@@ -271,6 +306,7 @@
         [fixed((half, width)), fixed((half, width))],
         [struct((half, width), F32), struct((half, width), BF16)],
         2 * length * width * units,
+        behind=behind,
     )(left, w)
 
 
@@ -278,11 +314,14 @@
     half, units = ua.shape[0], hidden.shape[1]
     pairs = ((ua, ub, d_gate), (ua, ub, d_up), (ca, cb, hidden))
     for number, (first, second, right) in enumerate(pairs):
-        term = dot_rows(first[...], right[:half, :]) + dot_rows(second[...], right[half:, :])
+        first, second = first[...], second[...]
+        if number == 2:
+            first, second = flat(first), flat(second)
+        term = dot_rows(first, right[:half, :]) + dot_rows(second, right[half:, :])
         out[:, number * units : (number + 1) * units] = term.astype(BF16)
 
 
-def feed_grads(ua, ub, ca, cb, d_gate, d_up, hidden):
+def feed_grads(ua, ub, ca, cb, d_gate, d_up, hidden, behind):
     half, width = ua.shape
     units = hidden.shape[1]
     chunk = 2 * HD
@@ -290,10 +329,13 @@
     return call(
         feed_grads_kernel,
         (width // chunk,),
-        [slab] * 4 + [fixed((2 * half, units))] * 3,
+        [slab] * 2
+        + [pl.BlockSpec((ca.shape[0], ca.shape[1] // 2, chunk), lambda i: (0, 1, i))] * 2
+        + [fixed((2 * half, units))] * 3,
         rowed(chunk, 3 * units),
         struct((width, 3 * units), BF16),
         2 * 2 * half * width * units * 3,
+        behind=behind,
     )(ua, ub, ca, cb, d_gate, d_up, hidden)
 
 
@@ -368,7 +410,7 @@
         out[:, head(3)] = d_value[...].astype(BF16)
 
 
-def attend_back(probs, low, d_attended, pre, gains, cosine, sine):
+def attend_back(probs, low, d_attended, pre, gains, cosine, sine, behind):
     length = low.shape[0]
     half = length // 2
     return call(
@@ -379,7 +421,7 @@
             fixed((length, 4 * HD)),
             rowed(half, 2 * HD),
             fixed((length, 3 * HD)),
-            fixed((2, HD)),
+            fixed((16, HD)),
             fixed((length, HD)),
             fixed((length, HD)),
         ],
@@ -387,6 +429,7 @@
         [struct((length, 4 * HD), BF16), struct((8, HD), F32)],
         20 * length * length * HD,
         scratch=[pltpu.VMEM((length, HD), F32), pltpu.VMEM((length, HD), F32)],
+        behind=behind,
     )(probs, low, d_attended, pre, gains, cosine, sine)
 
 
@@ -446,7 +489,7 @@
         out[number, block:] = terms[number].astype(BF16)
 
 
-def inner_grads(xn, d_qkv, terms):
+def inner_grads(xn, d_qkv, terms, behind):
     length, width = xn.shape
     columns, extra = d_qkv.shape[1], terms.shape[1]
     owners = terms.shape[0]
@@ -462,6 +505,7 @@
         pl.BlockSpec((2, block + extra, columns), lambda i: (i, 0, 0)),
         struct((owners, block + extra, columns), BF16),
         2 * length * width * columns,
+        behind=behind,
     )(xn, d_qkv, terms)
 
 
@@ -508,6 +552,105 @@
         [struct(shape, F32), struct(parts.shape, BF16)],
         1 << 20,
     )(parts, middle, cot)
+
+
+def input_step_kernel(p0, p1, p2, p3, d_middle, x, out):
+    grads = sum(p[...].astype(F32) for p in (p0, p1, p2, p3))
+    out[...] = (d_middle[...] + norm_back(grads, x[...].astype(F32))).astype(BF16)
+
+
+def input_step(parts, d_middle, x):
+    shape = x.shape
+    return call(
+        input_step_kernel,
+        (1,),
+        [fixed(shape)] * 6,
+        fixed(shape),
+        struct(shape, BF16),
+        1 << 20,
+    )(*parts, d_middle, x)
+
+
+def lanes(value):
+    return sum(value[:, start : start + HD] for start in range(0, value.shape[1], HD))
+
+
+def pick(blocks):
+    step = pl.program_id(0)
+    value = blocks[0][...]
+    for number in range(1, len(blocks)):
+        value = jnp.where(step == number, blocks[number][...], value)
+    return value.astype(F32)
+
+
+def close_feed_kernel(turn_at, b0, b1, b2, b3, w_gate, w_up, gain, g_gate, g_up, g_down, sums):
+    raw = pick((b0, b1, b2, b3))
+    units = w_gate.shape[1]
+    raw_gate, raw_up = raw[:, :units], raw[:, units : 2 * units]
+    g_gate[...] = raw_gate * gain[...]
+    g_up[...] = raw_up * gain[...]
+    g_down[...] = raw[:, 2 * units :].T
+    term = lanes(raw_gate * w_gate[...].astype(F32)) + lanes(raw_up * w_up[...].astype(F32))
+
+    @pl.when(pl.program_id(0) == 0)
+    def _():
+        sums[...] = term
+
+    @pl.when(pl.program_id(0) > 0)
+    def _():
+        sums[...] += term
+
+
+def close_attend_kernel(
+    turn_at, i0, i1, i2, i3, o0, o1, o2, o3, wq, wk, wv, wg, gain, gq, gk, gv, gg, go, sums, ends
+):
+    inner, outer = pick((i0, i1, i2, i3)), pick((o0, o1, o2, o3))
+    block = outer.shape[0]
+    scale = gain[...]
+    raw_q, raw_k, raw_v = inner[:block, : 2 * HD], inner[:block, head(2)], inner[:block, head(3)]
+    raw_g = outer[:, : 2 * HD]
+    gq[...], gk[...], gv[...], gg[...] = raw_q * scale, raw_k * scale, raw_v * scale, raw_g * scale
+    go[...] = outer[:, 2 * HD :].T
+    pairs = ((raw_q, wq), (raw_k, wk), (raw_v, wv), (raw_g, wg))
+    term = sum(lanes(raw * w[...].astype(F32)) for raw, w in pairs)
+    last = inner[block:, :HD]
+
+    @pl.when(pl.program_id(0) == 0)
+    def _():
+        sums[...] = term
+        ends[...] = last
+
+    @pl.when(pl.program_id(0) > 0)
+    def _():
+        sums[...] += term
+        ends[...] += last
+
+
+def close(kernel, turn_at, blocks, weights, gain, out_rows, extra):
+    quarters = 4
+    place = lambda i, at: (at[0] + quarters - i) % quarters
+    whole = lambda value: pl.BlockSpec(value.shape, lambda i, at: (0, 0))
+    columns = lambda w: pl.BlockSpec(
+        (w.shape[0], w.shape[1] // quarters), lambda i, at: (0, place(i, at))
+    )
+    rows, width = out_rows
+    in_specs = [whole(b) for b in blocks] + [columns(w) for w in weights] + [whole(gain)]
+    out_specs = [columns(w) for w in weights]
+    out_specs += [pl.BlockSpec((rows // quarters, width), lambda i, at: (place(i, at), 0))]
+    out_specs += [pl.BlockSpec(shape, lambda i, at: (0, 0)) for shape in extra]
+    out_shape = [struct(w.shape, F32) for w in weights] + [struct(out_rows, F32)]
+    out_shape += [struct(shape, F32) for shape in extra]
+    return pl.pallas_call(
+        kernel,
+        grid_spec=pltpu.PrefetchScalarGridSpec(
+            num_scalar_prefetch=1, grid=(quarters,), in_specs=in_specs, out_specs=out_specs
+        ),
+        out_shape=out_shape,
+        compiler_params=pltpu.CompilerParams(
+            dimension_semantics=("arbitrary",), vmem_limit_bytes=VMEM
+        ),
+        cost_estimate=pl.CostEstimate(flops=1 << 20, bytes_accessed=8 << 20, transcendentals=0),
+    )(turn_at, *blocks, *weights, gain)
 
 
 def make_shards(mesh):
@@ -537,19 +680,16 @@
     def ctx_exchange(value):
         return lax.all_to_all(value, "ctx", 0, 0)
 
-    def ctx_gather(value):
-        return ctx_exchange(jnp.broadcast_to(value[None], (n_ctx,) + value.shape))
-
-    def flat(value):
-        return value.reshape((-1,) + value.shape[2:])
+    def ctx_turn(value, by):
+        return lax.ppermute(value, "ctx", [(i, (i + by) % n_ctx) for i in range(n_ctx)])
 
     def tree_rows(spread):
-        mine = flat(ctx_exchange(spread))
+        mine = ctx_exchange(spread)
         return mine, core_swap(mine)
 
-    def tree_sums(mine, other):
+    def tree_half(mine, other):
         half = (mine + core_swap(other).astype(F32)).astype(BF16)
-        return ctx_exchange(half.reshape((n_ctx, -1) + half.shape[1:]))
+        return half.reshape((n_ctx, -1) + half.shape[1:])
 
     def plane_gather(value):
         return lax.all_gather(value, PLANE, axis=0, tiled=True, axis_index_groups=planes)
@@ -561,7 +701,7 @@
 
     def plane_exchange(value):
         parts = lax.all_to_all(value, PLANE, 0, 0, axis_index_groups=planes)
-        return jnp.sum(parts.astype(F32), axis=0)
+        return jnp.sum(parts.astype(F32), axis=0).astype(BF16)
 
     def shards(
         tokens,
@@ -600,25 +740,29 @@
             [quarter(w, 1) for w in (w_query, w_key, w_value, w_gate_attn)], axis=1
         )
         first = (first.astype(F32) * gain_one).astype(BF16)
-        first = jnp.concatenate([first, quarter(w_out, 0).T], axis=1)
+        head_rows = gain_query.shape[0]
+        ends = lax.dynamic_update_slice(
+            jnp.zeros((gain_in.shape[0], HD), BF16),
+            jnp.stack([gain_query, gain_key]),
+            (0, lax.axis_index("shard") * head_rows),
+        )
+        first = jnp.concatenate([first, quarter(w_out, 0).T, ends], axis=1)
+        w1 = plane_gather(swapped(first))
+
+        def half_rows(place):
+            pieces = [lax.dynamic_slice_in_dim(v, place * rows, rows, 0) for v in (tokens, cotangent)]
+            return jnp.concatenate(pieces, axis=0)
+
+        own = jnp.where(native, half_rows(core), core_swap(half_rows(1 - core)))
+        tree = jnp.concatenate([seg_lengths, seg_parents], axis=0)
+        tree = jnp.where(native, tree, core_swap(tree))
+        own_x, own_cot = own[:rows], own[rows:]
+        xa, xb = tree_rows(jnp.broadcast_to(own[None], (n_ctx,) + own.shape))
+
         second = jnp.concatenate([quarter(w_gate, 1), quarter(w_up, 1)], axis=1)
         second = (second.astype(F32) * gain_two).astype(BF16)
         second = jnp.concatenate([second, quarter(w_down, 0).T], axis=1)
-        w1 = plane_gather(swapped(first))
         w2 = plane_gather(swapped(second))
-        head_gains = lax.all_gather(
-            jnp.concatenate([gain_query[None], gain_key[None]], axis=0), "shard", axis=1, tiled=True
-        ).astype(F32)
-
-        both = jnp.stack([tokens, cotangent])
-        keep = lax.dynamic_slice_in_dim(both, core * rows, rows, 1)
-        give = lax.dynamic_slice_in_dim(both, (1 - core) * rows, rows, 1)
-        own = jnp.where(native, keep, core_swap(give))
-        tree = jnp.concatenate([seg_lengths, seg_parents], axis=0)
-        tree = jnp.where(native, tree, core_swap(tree))
-        own_x, own_cot = own[0], own[1]
-        xa, xb = tree_rows(jnp.broadcast_to(own_x[None], (n_ctx,) + own_x.shape))
-        ca, cb = tree_rows(jnp.broadcast_to(own_cot[None], (n_ctx,) + own_cot.shape))
 
         half_at = jnp.where(jnp.arange(2) == 0, core, 1 - core) * rows
         places = (
@@ -631,77 +775,67 @@
         of_column = jnp.stack([segment, places], axis=0)
         cosine, sine = rope_tables(position, HD)
 
-        xn, pre, low, gate = project(xa, xb, w1, head_gains, cosine, sine)
+        xn, pre, low, gate, gains = project(xa, xb, w1, cosine, sine)
         probs, attended, gated, mine, other = attend(low, gate, w1, of_row, of_column)
-        middle, spread = middle_step(tree_sums(mine, other), own_x)
-        ua, ub = tree_rows(spread)
-
-        hidden, d_gate, d_up, mine, other = feed(ua, ub, ca, cb, w2)
-        units = hidden.shape[1]
-        grad_ffn = plane_scatter(feed_grads(ua, ub, ca, cb, d_gate, d_up, hidden))
-        d_middle, spread = d_middle_step(tree_sums(mine, other), middle, own_cot)
-        da, db = tree_rows(spread)
-        layer_parts = tree_sums(*down_product(hidden, w2, 2))
-        layer_own = middle + jnp.sum(layer_parts.astype(F32), axis=0)
+        middle, spread = middle_step(ctx_exchange(tree_half(mine, other)), own_x)
+        ua, ub = (flat(v) for v in tree_rows(spread))
+
+        hidden, d_gate, d_up, mine, other = feed(ua, ub, xa, xb, w2)
+        half = tree_half(mine, other)
+        ffn = feed_grads(ua, ub, xa, xb, d_gate, d_up, hidden, (half,))
+        d_middle, spread = d_middle_step(ctx_exchange(half), middle, own_cot)
+        da, db = (flat(v) for v in tree_rows(spread))
+        grad_ffn = plane_scatter(ffn)
 
         d_attended, d_gate_pre = gate_back(da, db, w1, gate, attended)
-        grad_outer = plane_exchange(
-            outer_grads(xn, da, db, d_gate_pre, gated).reshape(n_shard, -1, 4 * HD)
-        )
-        d_qkv, terms = attend_back(probs, low, d_attended, pre, head_gains, cosine, sine)
+        outer = outer_grads(xn, da, db, d_gate_pre, gated)
+        grad_outer = plane_exchange(outer.reshape(n_shard, -1, 4 * HD))
+        d_qkv, terms = attend_back(probs, low, d_attended, pre, gains, cosine, sine, (outer,))
+        half = tree_half(*input_back(d_qkv, d_gate_pre, w1))
 
         def spread_terms(vector):
             return jnp.pad(vector.reshape(n_shard, 1, -1), ((0, 0), (0, 15), (0, 0)))
 
-        head_rows = gain_query.shape[0]
         wide_terms = jnp.concatenate([spread_terms(terms[0]), spread_terms(terms[1])], axis=2)
         wide_terms = jnp.pad(wide_terms, ((0, 0), (0, 0), (0, 4 * HD - 2 * head_rows)))
-        grad_inner = plane_exchange(inner_grads(xn, d_qkv, wide_terms))
-        parts = tree_sums(*input_back(d_qkv, d_gate_pre, w1))
-        input_own = d_middle + norm_back(
-            jnp.sum(parts.astype(F32), axis=0), own_x.astype(F32)
+        inner = inner_grads(xn, d_qkv, wide_terms, (half,))
+        grad_inner = plane_exchange(inner)
+        parts = [lax.dynamic_index_in_dim(half, ctx, 0, False)] + [
+            ctx_turn(lax.dynamic_index_in_dim(half, (ctx + by) % n_ctx, 0, False), by)
+            for by in range(1, n_ctx)
+        ]
+        input_own = input_step(parts, d_middle, own_x)
+
+        layer_half = tree_half(*down_product(hidden, w2, 2, (inner,)))
+        layer_own = middle + lax.psum_scatter(
+            flat(layer_half), "ctx", scatter_dimension=0, tiled=True
+        ).astype(F32)
+
+        def owners(block):
+            block = swapped(block)
+            return [block] + [ctx_turn(block, by) for by in range(1, n_ctx)]
+
+        turn_at = ctx.astype(jnp.int32).reshape(1)
+        size = gain_in.shape[0]
+        grad_gate, grad_up, grad_down, mid_sums = close(
+            close_feed_kernel,
+            turn_at,
+            owners(grad_ffn),
+            (w_gate, w_up),
+            gain_two,
+            w_down.shape,
+            [(size, HD)],
         )
-
-        def owners(block):
-            return ctx_gather(swapped(block.astype(BF16))).astype(F32)
-
-        def side(parts):
-            return parts.transpose(1, 0, 2).reshape(parts.shape[1], -1)
-
-        def down(parts):
-            return parts.transpose(0, 2, 1).reshape(-1, parts.shape[1])
-
-        size = gain_in.shape[0]
-        ffn = owners(grad_ffn)
-        raw_gate = side(ffn[:, :, :units])
-        raw_up = side(ffn[:, :, units : 2 * units])
-        grad_down = down(ffn[:, :, 2 * units :])
-        outer = owners(grad_outer)
-        raw_gate_attn = side(outer[:, :, : 2 * HD])
-        grad_out = down(outer[:, :, 2 * HD :])
-        ends = grad_inner[size:]
-        ends = ends + core_swap(ends.astype(BF16)).astype(F32)
-        inner = owners(jnp.concatenate([grad_inner[:size], ends], axis=0))
-        raw_query = side(inner[:, :size, : 2 * HD])
-        raw_key = side(inner[:, :size, 2 * HD : 3 * HD])
-        raw_value = side(inner[:, :size, 3 * HD :])
-        head_ends = jnp.sum(inner[:, size, : 2 * head_rows], axis=0)
-
-        def along(weights, raws):
-            total = 0.0
-            for weight, raw in zip(weights, raws):
-                total = total + jnp.sum(weight.astype(F32) * raw, axis=1)
-            return total
-
-        gain_terms = jnp.stack(
-            [
-                along(
-                    (w_query, w_key, w_value, w_gate_attn),
-                    (raw_query, raw_key, raw_value, raw_gate_attn),
-                ),
-                along((w_gate, w_up), (raw_gate, raw_up)),
-            ]
+        grad_query, grad_key, grad_value, grad_gate_attn, grad_out, in_sums, head_ends = close(
+            close_attend_kernel,
+            turn_at,
+            owners(grad_inner) + owners(grad_outer),
+            (w_query, w_key, w_value, w_gate_attn),
+            gain_one,
+            w_out.shape,
+            [(size, HD), (16, HD)],
         )
+        gain_terms = jnp.stack([jnp.sum(in_sums, axis=1), jnp.sum(mid_sums, axis=1), head_ends[0]])
         gain_terms = gain_terms + lax.ppermute(gain_terms, "tp", [(0, 1), (1, 0)])
 
         def finish(part):
@@ -718,16 +852,16 @@
             finish(layer_own),
             finish(input_own),
             gain_terms[0],
-            raw_query * gain_one,
-            raw_key * gain_one,
-            raw_value * gain_one,
-            raw_gate_attn * gain_one,
+            grad_query,
+            grad_key,
+            grad_value,
+            grad_gate_attn,
             grad_out,
-            head_ends[:head_rows],
-            head_ends[head_rows:],
+            gain_terms[2, :head_rows],
+            gain_terms[2, head_rows : 2 * head_rows],
             gain_terms[1],
-            raw_gate * gain_two,
-            raw_up * gain_two,
+            grad_gate,
+            grad_up,
             grad_down,
         )
 

time: 453 us -> 414 us (0.914)
  blocking collectives: 74.9 us -> 49.9 us
  local copies, waits for them, and re-layouts: 40.1 us -> 21.6 us
  waiting for transfers between devices: 133 us -> 151 us
  starting transfers between devices: 85.1 us -> 69 us
  Pallas kernels: 67.8 us -> 77.7 us
  other arithmetic: 35.1 us -> 28.2 us
    all_to_all x8 -> x2, waiting for transfers between devices: 84.7 us -> 39.1 us  [ctx_exchange(): return lax.all_to_all(value, 'ctx', 0, 0)]
    ppermute x0 -> x12, waiting for transfers between devices: none -> 36.9 us  [ctx_turn(): lax.ppermute(value, 'ctx', [(i, (i + by) % n_ctx) for i in range(n_ctx)])]
    all_gather x1 -> x0, blocking collectives: 23.9 us -> none  [shards(): lax.all_gather(jnp.concatenate([gain_query[None], gain_key[None]], axis=0...]
    all_to_all x8 -> x2, starting transfers between devices: 32.5 us -> 9.4 us  [ctx_exchange(): return lax.all_to_all(value, 'ctx', 0, 0)]
    all_gather x2, waiting for transfers between devices: 0.01 us -> 19.5 us  [plane_gather(): lax.all_gather(value, PLANE, axis=0, tiled=True, axis_index_groups=planes)]
    ppermute x0 -> x12, starting transfers between devices: none -> 13.2 us  [ctx_turn(): lax.ppermute(value, 'ctx', [(i, (i + by) % n_ctx) for i in range(n_ctx)])]
    pallas_call x12 -> x15, Pallas kernels: 67.8 us -> 77.7 us  [the longest x13 70.9 us: call(): return lambda *operands: built(*operands, *behind)]
    ppermute x5, waiting for transfers between devices: 14.9 us -> 23.2 us  [swapped(): return jnp.where(native, value, lax.ppermute(value, PLANE, swap_perm))]
  transfers between devices with their start and end apart: 34 -> 39, of which waited for: 17 -> 19; matrix products, arithmetic and copies ran while one was open for 11% -> 7% of each run, Pallas kernels for 9% -> 11%
where the time goes in v3:
time: 414 us; the launch traced here: 412 us
  waiting for transfers between devices  151 us (36%)
  Pallas kernels  77.7 us (19%)
  starting transfers between devices  69 us (17%)
  blocking collectives  49.9 us (12%)
  other arithmetic  28.2 us (7%)
  local copies, waits for them, and re-layouts  21.6 us (5%)
  between operations  14.7 us (4%)
    pallas_call x13, Pallas kernels, call(): return lambda *operands: built(*operands, *behind)  70.9 us
    all_to_all x3, blocking collectives, ctx_exchange(): return lax.all_to_all(value, 'ctx', 0, 0)  49.9 us
    all_to_all x2, waiting for transfers between devices, ctx_exchange(): return lax.all_to_all(value, 'ctx', 0, 0)  39.1 us
    ppermute x12, waiting for transfers between devices, ctx_turn(): lax.ppermute(value, 'ctx', [(i, (i + by) % n_ctx) for i in range(n_ctx)])  36.9 us
    ppermute x5, waiting for transfers between devices, swapped(): return jnp.where(native, value, lax.ppermute(value, PLANE, swap_perm))  23.2 us
    all_to_all x2, waiting for transfers between devices, plane_exchange(): parts = lax.all_to_all(value, PLANE, 0, 0, axis_index_groups=planes)  19.5 us
    all_gather x2, waiting for transfers between devices, plane_gather(): lax.all_gather(value, PLANE, axis=0, tiled=True, axis_index_groups=planes)  19.5 us
    ppermute x5, starting transfers between devices, swapped(): return jnp.where(native, value, lax.ppermute(value, PLANE, swap_perm))  15.7 us
  transfers between devices with their start and end apart: 39, of which 19 were waited for; matrix products, arithmetic and copies ran while one was open for 7% of the time, Pallas kernels for 11%

profile of v3, /device:TPU:1, one launch (start us, length us, event | category | flops | bytes accessed | tf_op | source)
XLA Modules:
  0.0 412.5 jit_solution(4663159975894025716)
XLA Ops:
  12.0 4.4 %collective-permute-start.2 = (bf16[128,1152]{1,0:T(8,128)(2,1)S(1)}, bf16[128,1152]{1,0:T(8,128)(2,1)S(1)}, u32[]{:S(2)}, u32[]{:S(2)}) collective-permute-start(bf16[128,1152]{1,0:T(8,128)(2,1)S(1)} %pad_maximum_fusion.2), channel_id=1, source_target_pairs={{8,1},{1,8},{24,17},{17,24},{40,33},{33,40},{56,49},{49,56},{72,65... | collective-permute-start | bytes 884744 | tf_op jit(solution)/shard_map/ppermute | solution.py:731
  16.4 4.4 %collective-permute-done.2 = bf16[128,1152]{1,0:T(8,128)(2,1)S(1)} collective-permute-done((bf16[128,1152]{1,0:T(8,128)(2,1)S(1)}, bf16[128,1152]{1,0:T(8,128)(2,1)S(1)}, u32[]{:S(2)}, u32[]{:S(2)}) %collective-permute-start.2) | collective-permute-done | bytes 294944 | tf_op jit(solution)/shard_map/ppermute | solution.py:731
  23.1 3.8 collective-permute-start.6
  26.9 7.6 %collective-permute-done.6 = bf16[128,2304]{1,0:T(8,128)(2,1)S(1)} collective-permute-done((bf16[128,2304]{1,0:T(8,128)(2,1)S(1)}, bf16[128,2304]{1,0:T(8,128)(2,1)S(1)}, u32[]{:S(2)}, u32[]{:S(2)}) %collective-permute-start.6) | collective-permute-done | bytes 589856 | tf_op jit(solution)/shard_map/ppermute | solution.py:731
  35.7 1.9 collective-permute-done
  37.7 1.6 broadcast_in_dim.21
  39.4 5.3 %all-to-all-start = ((bf16[4,128,2048]{2,1,0:T(8,128)(2,1)}), bf16[4,128,2048]{2,1,0:T(8,128)(2,1)}, u32[]{:S(2)}, u32[]{:S(2)}) async-start(bf16[4,128,2048]{2,1,0:T(8,128)(2,1)} %broadcast_in_dim.21), calls=%async_computation | async-start | bytes 4194304 | tf_op jit(solution)/shard_map/all_to_all | solution.py:681
  45.6 25.3 %all-to-all-done.refs_0_.refs_2_ = bf16[4,128,2048]{2,1,0:T(8,128)(2,1)} async-done(((bf16[4,128,2048]{2,1,0:T(8,128)(2,1)}), bf16[4,128,2048]{2,1,0:T(8,128)(2,1)}, u32[]{:S(2)}, u32[]{:S(2)}) %all-to-all-start) | async-done | bytes 2097184 | tf_op jit(solution)/shard_map/all_to_all | solution.py:681
  70.8 1.4 collective-permute-start.1
  74.5 1.9 collective-permute-done.1.refs_1_.refs_3_
  76.3 1.6 all-gather.3.cloned.1.call-done.refs_2_.refs_3_
  77.9 5.5 %shard_map.263 = (bf16[512,2048]{1,0:T(8,128)(2,1)S(1)}, f32[512,384]{1,0:T(8,128)S(1)}, bf16[512,512]{1,0:T(8,128)(2,1)S(1)}, f32[512,256]{1,0:T(8,128)S(1)}, f32[16,128]{1,0:T(8,128)S(1)}) custom-call(bf16[4,128,2048]{2,1,0:T(8,128)(2,1)} %all-to-all-done.refs_0_.refs_2_, bf16[4,128,2048]{2,1,0:T(8,128)(2,1)} %collective-permute-done.1.refs_1_.refs_3_, ...), custom_call_target="tpu_custom_call" | custom-call | flops 1610612736 | bytes 8388608 | tf_op jit(solution)/shard_map/pallas_call | solution.py:97
  83.5 1.4 copy-done.2
  85.7 6.6 %shard_map.264 = (f32[2,512,512]{2,1,0:T(8,128)S(1)}, f32[512,256]{1,0:T(8,128)S(1)}, bf16[512,256]{1,0:T(8,128)(2,1)S(1)}, f32[256,2048]{1,0:T(8,128)}, bf16[256,2048]{1,0:T(8,128)(2,1)S(1)}) custom-call(bf16[512,512]{1,0:T(8,128)(2,1)S(1)} %get-tuple-element.52.refs_0_.refs_1_, f32[512,256]{1,0:T(8,128)S(1)} %get-tuple-element.53.refs_1_.refs_3_, ...), custom_call_target="tpu_custom_call" | custom-call | flops 805306368 | bytes 8388608 | tf_op jit(solution)/shard_map/pallas_call | solution.py:97
  93.1 2.3 collective-permute-done.4
  95.4 2.9 add_convert_fusion.3
  98.3 4.1 %all-to-all-start.1 = ((bf16[4,64,2048]{2,1,0:T(8,128)(2,1)}), bf16[4,64,2048]{2,1,0:T(8,128)(2,1)S(1)}, u32[]{:S(2)}, u32[]{:S(2)}) async-start(bf16[4,64,2048]{2,1,0:T(8,128)(2,1)} %bitcast.16), calls=%async_computation.1 | async-start | bytes 2097152 | tf_op jit(solution)/shard_map/all_to_all | solution.py:681
  103.2 13.8 %all-to-all-done.1.refs_0_ = bf16[4,64,2048]{2,1,0:T(8,128)(2,1)S(1)} async-done(((bf16[4,64,2048]{2,1,0:T(8,128)(2,1)}), bf16[4,64,2048]{2,1,0:T(8,128)(2,1)S(1)}, u32[]{:S(2)}, u32[]{:S(2)}) %all-to-all-start.1) | async-done | bytes 1048608 | tf_op jit(solution)/shard_map/all_to_all | solution.py:681
  117.3 15.9 %all_to_all.35 = bf16[4,64,2048]{2,1,0:T(8,128)(2,1)S(1)} all-to-all(bf16[4,64,2048]{2,1,0:T(8,128)(2,1)S(1)} %get-tuple-element.57), channel_id=1, replica_groups=mesh['shard'=16,'ctx'=4,'tp'=2] {'ctx'}, dimensions={0} | all-to-all | bytes 2097152 | tf_op jit(solution)/shard_map/all_to_all | solution.py:681
  133.2 2.6 collective-permute-start.5
  135.8 2.3 collective-permute-done.5
  138.1 17.9 %all-gather.5.cloned.1.call-done.refs_4_.refs_5_.refs_6_.refs_1_ = bf16[2048,2304]{1,0:T(8,128)(2,1)} async-done(((bf16[128,2304]{1,0:T(8,128)(2,1)}), bf16[2048,2304]{1,0:T(8,128)(2,1)}) %all-gather.5.cloned.1.call-update) | async-done | bytes 9437200 | tf_op jit(solution)/shard_map/all_gather | solution.py:695
  156.0 21.1 %shard_map.266 = (bf16[512,768]{1,0:T(8,128)(2,1)S(1)}, bf16[512,768]{1,0:T(8,128)(2,1)S(1)}, bf16[512,768]{1,0:T(8,128)(2,1)S(1)}, f32[256,2048]{1,0:T(8,128)}, bf16[256,2048]{1,0:T(8,128)(2,1)S(1)}) custom-call(bf16[256,2048]{1,0:T(8,128)(2,1)S(1)} %bitcast.60, bf16[256,2048]{1,0:T(8,128)(2,1)S(1)} %bitcast.68, ...), custom_call_target="tpu_custom_call" | custom-call | flops 8053063680 | bytes 8388608 | tf_op jit(solution)/shard_map/pallas_call | solution.py:97
  177.8 2.3 collective-permute-done.7
  180.1 1.9 add_convert_fusion.2
  182.0 10.4 %shard_map.276 = bf16[2048,2304]{1,0:T(8,128)(2,1)} custom-call(bf16[256,2048]{1,0:T(8,128)(2,1)S(1)} %bitcast.61, bf16[256,2048]{1,0:T(8,128)(2,1)S(1)} %bitcast.69, bf16[4,128,2048]{2,1,0:T(8,128)(2,1)} %all-to-all-done.refs_0_.refs_2_, bf16[4,128,2048]{2,1,0:T(8,128)(2,1)} %collective-permute-done.1.refs_1_.refs_3_, ...), custom_call_target="tpu_custom_call" | custom-call | flops 4831838208 | bytes 8388608 | tf_op jit(solution)/shard_map/pallas_call | solution.py:97
  192.4 18.3 %all_to_all.36.refs_0_ = bf16[4,64,2048]{2,1,0:T(8,128)(2,1)S(1)} all-to-all(bf16[4,64,2048]{2,1,0:T(8,128)(2,1)S(1)} %bitcast.65), channel_id=1, replica_groups=mesh['shard'=16,'ctx'=4,'tp'=2] {'ctx'}, dimensions={0} | all-to-all | bytes 2097152 | tf_op jit(solution)/shard_map/all_to_all | solution.py:681
  211.2 15.7 %all_to_all.37 = bf16[4,64,2048]{2,1,0:T(8,128)(2,1)S(1)} all-to-all(bf16[4,64,2048]{2,1,0:T(8,128)(2,1)S(1)} %get-tuple-element.63), channel_id=1, replica_groups=mesh['shard'=16,'ctx'=4,'tp'=2] {'ctx'}, dimensions={0} | all-to-all | bytes 2097152 | tf_op jit(solution)/shard_map/all_to_all | solution.py:681
  226.9 2.7 collective-permute-start.8
  229.7 2.3 collective-permute-done.8
  232.0 2.1 shard_map.268
  234.1 7.1 %shard_map.269.refs_7_ = bf16[2048,512]{1,0:T(8,128)(2,1)} custom-call(bf16[512,2048]{1,0:T(8,128)(2,1)} %copy-done.2, bf16[256,2048]{1,0:T(8,128)(2,1)S(1)} %bitcast.67, bf16[256,2048]{1,0:T(8,128)(2,1)S(1)} %bitcast.71, bf16[512,256]{1,0:T(8,128)(2,1)S(1)} %get-tuple-element.68.refs_3_.refs_1_, bf16[512,256]{1,0:T(8,128)(2,1)S(1)} %copy-done.36), custom_call_target="tpu_custom_call" | custom-call | flops 1073741824 | bytes 8388608 | tf_op jit(solution)/shard_map/pallas_call | solution.py:97
  241.2 3.1 shard_map.270
  244.3 5.1 %shard_map.271 = (f32[256,2048]{1,0:T(8,128)S(1)}, bf16[256,2048]{1,0:T(8,128)(2,1)}) custom-call(bf16[512,512]{1,0:T(8,128)(2,1)S(1)} %get-tuple-element.70.refs_0_.refs_1_, bf16[512,256]{1,0:T(8,128)(2,1)S(1)} %get-tuple-element.68.refs_3_.refs_1_, bf16[2048,1152]{1,0:T(8,128)(2,1)} %all-gather.3.cloned.1.call-done.refs_2_.refs_3_), custom_call_target="tpu_custom_call" | custom-call | flops 1610612736 | bytes 8388608 | tf_op jit(solution)/shard_map/pallas_call | solution.py:97
  251.1 5.0 %all-to-all-start.6 = ((bf16[16,128,512]{2,1,0:T(8,128)(2,1)}), bf16[16,128,512]{2,1,0:T(8,128)(2,1)}, u32[]{:S(2)}, u32[]{:S(2)}) async-start(bf16[16,128,512]{2,1,0:T(8,128)(2,1)} %bitcast.31), calls=%async_computation.7 | async-start | bytes 4194304 | tf_op jit(solution)/shard_map/all_to_all | solution.py:703
  256.5 2.3 add_convert_fusion.1
  259.0 4.7 %shard_map.272.refs_2_ = bf16[16,144,512]{2,1,0:T(8,128)(2,1)} custom-call(bf16[512,2048]{1,0:T(8,128)(2,1)S(1)} %copy-done.3, bf16[512,512]{1,0:T(8,128)(2,1)S(1)} %get-tuple-element.70.refs_0_.refs_1_, f32[16,16,512]{2,1,0:T(8,128)S(1)} %pad.13.refs_2_, bf16[4,64,2048]{2,1,0:T(8,128)(2,1)S(1)} %bitcast.62), custom_call_target="tpu_custom_call" | custom-call | flops 1073741824 | bytes 8388608 | tf_op jit(solution)/shard_map/pallas_call | solution.py:97
  263.8 4.2 %shard_map.273 = (f32[256,2048]{1,0:T(8,128)S(1)}, bf16[256,2048]{1,0:T(8,128)(2,1)S(1)}) custom-call(bf16[512,768]{1,0:T(8,128)(2,1)S(1)} %copy-done.5, bf16[2048,2304]{1,0:T(8,128)(2,1)} %all-gather.5.cloned.1.call-done.refs_4_.refs_5_.refs_6_.refs_1_, bf16[16,144,512]{2,1,0:T(8,128)(2,1)} %shard_map.272.refs_2_), custom_call_target="tpu_custom_call" | custom-call | flops 1610612736 | bytes 8388608 | tf_op jit(solution)/shard_map/pallas_call | solution.py:97
  268.0 1.4 copy-done.17
  269.9 19.5 %all-to-all-done.6 = bf16[16,128,512]{2,1,0:T(8,128)(2,1)} async-done(((bf16[16,128,512]{2,1,0:T(8,128)(2,1)}), bf16[16,128,512]{2,1,0:T(8,128)(2,1)}, u32[]{:S(2)}, u32[]{:S(2)}) %all-to-all-start.6) | async-done | bytes 2097184 | tf_op jit(solution)/shard_map/all_to_all | solution.py:703
  289.4 6.3 %all-to-all-start.5 = ((bf16[16,144,512]{2,1,0:T(8,128)(2,1)}), bf16[16,144,512]{2,1,0:T(8,128)(2,1)}, u32[]{:S(2)}, u32[]{:S(2)}) async-start(bf16[16,144,512]{2,1,0:T(8,128)(2,1)} %shard_map.272.refs_2_), calls=%async_computation.6 | async-start | bytes 4718592 | tf_op jit(solution)/shard_map/all_to_all | solution.py:703
  295.8 3.1 add_convert_fusion
  299.6 2.2 collective-permute-start.14
  302.4 3.6 collective-permute-done.13.refs_1_
  306.0 5.7 %collective-permute-done.14.refs_2_ = bf16[64,2048]{1,0:T(8,128)(2,1)S(1)} collective-permute-done((bf16[64,2048]{1,0:T(8,128)(2,1)S(1)}, bf16[64,2048]{1,0:T(8,128)(2,1)S(1)}, u32[]{:S(2)}, u32[]{:S(2)}) %collective-permute-start.14) | collective-permute-done | bytes 262176 | tf_op jit(solution)/shard_map/ppermute | solution.py:684
  311.7 4.1 %collective-permute-done.15.refs_3_ = bf16[64,2048]{1,0:T(8,128)(2,1)S(1)} collective-permute-done((bf16[64,2048]{1,0:T(8,128)(2,1)S(1)}, bf16[64,2048]{1,0:T(8,128)(2,1)S(1)}, u32[]{:S(2)}, u32[]{:S(2)}) %collective-permute-start.15) | collective-permute-done | bytes 262176 | tf_op jit(solution)/shard_map/ppermute | solution.py:684
  316.2 4.9 %collective-permute-start.16 = (bf16[64,2048]{1,0:T(8,128)(2,1)S(1)}, bf16[64,2048]{1,0:T(8,128)(2,1)S(1)}, u32[]{:S(2)}, u32[]{:S(2)}) collective-permute-start(bf16[64,2048]{1,0:T(8,128)(2,1)S(1)} %shard_map.274), channel_id=1, source_target_pairs={{0,8},{8,0},{16,24},{24,16},{32,40},{40,32},{48,56},{56,48},{64,72... | collective-permute-start | bytes 786440 | tf_op jit(solution)/shard_map/ppermute | solution.py:678
  322.6 1.9 reduce_sum.129
  324.5 3.5 collective-permute-start.22
  329.5 2.0 reduce_sum.128
  331.5 2.1 collective-permute-start.18
  334.1 2.2 collective-permute-start.24
  336.9 3.0 collective-permute-done.18
  339.9 1.9 collective-permute-start.26
  342.9 8.4 %collective-permute-done.26 = bf16[128,2304]{1,0:T(8,128)(2,1)S(1)} collective-permute-done((bf16[128,2304]{1,0:T(8,128)(2,1)}, bf16[128,2304]{1,0:T(8,128)(2,1)S(1)}, u32[]{:S(2)}, u32[]{:S(2)}) %collective-permute-start.26) | collective-permute-done | bytes 589856 | tf_op jit(solution)/shard_map/ppermute | solution.py:731
  352.1 1.7 collective-permute-start.20
  354.5 1.5 collective-permute-start.27
  357.3 1.8 collective-permute-start.29
  362.3 2.1 select_convert_fusion
  364.3 23.5 %collective-permute-done.21.i3 = bf16[144,512]{1,0:T(8,128)(2,1)S(1)} collective-permute-done((bf16[144,512]{1,0:T(8,128)(2,1)S(1)}, bf16[144,512]{1,0:T(8,128)(2,1)S(1)}, u32[]{:S(2)}, u32[]{:S(2)}) %collective-permute-start.21) | collective-permute-done | bytes 147488 | tf_op jit(solution)/shard_map/ppermute | solution.py:684
  387.9 2.5 shard_map.275
  394.7 4.3 %shard_map.277 = (f32[128,3072]{1,0:T(8,128)}, f32[128,3072]{1,0:T(8,128)}, f32[3072,128]{1,0:T(8,128)}, f32[128,128]{1,0:T(8,128)S(1)}) custom-call(s32[1]{0:T(128)} %bitcast.30.turn_at, bf16[128,2304]{1,0:T(8,128)(2,1)S(1)} %broadcast_select_fusion.b0, bf16[128,2304]{1,0:T(8,128)(2,1)S(1)} %collective-permute-done.27.b1, bf16[128,2304]{1,0:T(8,128)(2,1)S(1)} %copy-done.26, ...), custom_call_target="tpu_custom_call" | custom-call | flops 1048576 | bytes 8388608 | tf_op jit(solution)/shard_map/pallas_call | solution.py:643
  400.6 2.1 collective-permute-start.30
  402.7 2.1 select_convert_fusion.1
  (220 shorter events, 38.0 us)
Async XLA Ops:
  7.2 14.4 %copy-start = (bf16[3072,128]{1,0:T(8,128)(2,1)S(1)}, bf16[3072,128]{1,0:T(8,128)(2,1)}, u32[]{:S(2)}) copy-start(bf16[3072,128]{1,0:T(8,128)(2,1)} %param.30) | copy-start | bytes 2359300
  7.2 70.7 %all-gather.3.cloned.1.call-start = ((), (), s32[]{:S(2)}) async-start(), calls=%async_computation.9 | async-start | bytes 5013504 | tf_op jit(solution)/shard_map/all_gather | solution.py:695
  9.6 13.3 %copy-start.53 = (bf16[128]{0:T(256)(128)(2,1)S(1)}, bf16[128]{0:T(256)(128)(2,1)}, u32[]{:S(2)}) copy-start(bf16[128]{0:T(256)(128)(2,1)} %param.27) | copy-start | bytes 772
  12.0 8.8 %collective-permute-start.2 = (bf16[128,1152]{1,0:T(8,128)(2,1)S(1)}, bf16[128,1152]{1,0:T(8,128)(2,1)S(1)}, u32[]{:S(2)}, u32[]{:S(2)}) collective-permute-start(bf16[128,1152]{1,0:T(8,128)(2,1)S(1)} %pad_maximum_fusion.2), channel_id=1, source_target_pairs={{8,1},{1,8},{24,17},{17,24},{40,33},{33,40},{56,49},{49,56},{72,65... | collective-permute-start | bytes 884744 | tf_op jit(solution)/shard_map/ppermute | solution.py:731
  21.6 134.4 %all-gather.5.cloned.1.call-start = ((), (), s32[]{:S(2)}) async-start(), calls=%async_computation.10 | async-start | bytes 10027008 | tf_op jit(solution)/shard_map/all_gather | solution.py:695
  22.9 12.5 %copy-start.49 = (bf16[128,2048]{1,0:T(8,128)(2,1)S(1)}, bf16[128,2048]{1,0:T(8,128)(2,1)}, u32[]{:S(2)}) copy-start(bf16[128,2048]{1,0:T(8,128)(2,1)} %param.31) | copy-start | bytes 1572868
  22.9 12.5 %copy-start.50 = (bf16[128,2048]{1,0:T(8,128)(2,1)S(1)}, bf16[128,2048]{1,0:T(8,128)(2,1)}, u32[]{:S(2)}) copy-start(bf16[128,2048]{1,0:T(8,128)(2,1)} %param.16) | copy-start | bytes 1572868
  23.1 11.3 %collective-permute-start.6 = (bf16[128,2304]{1,0:T(8,128)(2,1)S(1)}, bf16[128,2304]{1,0:T(8,128)(2,1)S(1)}, u32[]{:S(2)}, u32[]{:S(2)}) collective-permute-start(bf16[128,2304]{1,0:T(8,128)(2,1)S(1)} %pad_maximum_fusion), channel_id=1, source_target_pairs={{8,1},{1,8},{24,17},{17,24},{40,33},{33,40},{56,49},{49,56},{72,65... | collective-permute-start | bytes 1769480 | tf_op jit(solution)/shard_map/ppermute | solution.py:731
  35.6 2.0 collective-permute-start
  39.4 31.5 %all-to-all-start = ((bf16[4,128,2048]{2,1,0:T(8,128)(2,1)}), bf16[4,128,2048]{2,1,0:T(8,128)(2,1)}, u32[]{:S(2)}, u32[]{:S(2)}) async-start(bf16[4,128,2048]{2,1,0:T(8,128)(2,1)} %broadcast_in_dim.21), calls=%async_computation | async-start | bytes 4194304 | tf_op jit(solution)/shard_map/all_to_all | solution.py:681
  44.6 27.6 %collective-permute-start.3 = (s32[2,13]{1,0:T(2,128)S(1)}, s32[2,13]{1,0:T(2,128)S(1)}, u32[]{:S(2)}, u32[]{:S(2)}) collective-permute-start(s32[2,13]{1,0:T(2,128)S(1)} %pad_add_fusion.2), channel_id=1, source_target_pairs={{0,8},{8,0},{16,24},{24,16},{32,40},{40,32},{48,56},{56,48},{64,72... | collective-permute-start | bytes 320 | tf_op jit(solution)/shard_map/ppermute | solution.py:678
  70.8 5.5 %collective-permute-start.1 = (bf16[4,128,2048]{2,1,0:T(8,128)(2,1)}, bf16[4,128,2048]{2,1,0:T(8,128)(2,1)}, u32[]{:S(2)}, u32[]{:S(2)}) collective-permute-start(bf16[4,128,2048]{2,1,0:T(8,128)(2,1)} %all-to-all-done.refs_0_.refs_2_), channel_id=1, source_target_pairs={{0,8},{8,0},{16,24},{24,16},{32,40},{40,32},{48,56},{56,48},{64,72... | collective-permute-start | bytes 6291464 | tf_op jit(solution)/shard_map/ppermute | solution.py:678
  92.3 3.0 collective-permute-start.4
  98.3 18.7 %all-to-all-start.1 = ((bf16[4,64,2048]{2,1,0:T(8,128)(2,1)}), bf16[4,64,2048]{2,1,0:T(8,128)(2,1)S(1)}, u32[]{:S(2)}, u32[]{:S(2)}) async-start(bf16[4,64,2048]{2,1,0:T(8,128)(2,1)} %bitcast.16), calls=%async_computation.1 | async-start | bytes 2097152 | tf_op jit(solution)/shard_map/all_to_all | solution.py:681
  102.4 237.5 %reduce-scatter.5.cloned.1.call-start = ((), (), s32[]{:S(2)}) async-start(), calls=%async_computation.12 | async-start | bytes 10027008 | tf_op jit(solution)/shard_map/reduce_scatter | solution.py:698
  103.2 73.9 %copy-start.8 = (bf16[64,2048]{1,0:T(8,128)(2,1)}, bf16[64,2048]{1,0:T(8,128)(2,1)S(1)}, u32[]{:S(2)}) copy-start(bf16[64,2048]{1,0:T(8,128)(2,1)S(1)} %get-tuple-element.103.refs_1_.refs_5_) | copy-start | bytes 786436
  117.3 15.9 %copy-start.12 = (f32[64,2048]{1,0:T(8,128)}, f32[64,2048]{1,0:T(8,128)S(1)}, u32[]{:S(2)}) copy-start(f32[64,2048]{1,0:T(8,128)S(1)} %get-tuple-element.56.refs_1_) | copy-start | bytes 1572868
  133.2 4.9 %collective-permute-start.5 = (bf16[4,64,2048]{2,1,0:T(8,128)(2,1)S(1)}, bf16[4,64,2048]{2,1,0:T(8,128)(2,1)S(1)}, u32[]{:S(2)}, u32[]{:S(2)}) collective-permute-start(bf16[4,64,2048]{2,1,0:T(8,128)(2,1)S(1)} %all_to_all.35), channel_id=1, source_target_pairs={{0,8},{8,0},{16,24},{24,16},{32,40},{40,32},{48,56},{56,48},{64,72... | collective-permute-start | bytes 3145736 | tf_op jit(solution)/shard_map/ppermute | solution.py:678
  177.1 3.0 collective-permute-start.7
  192.4 18.3 %copy-start.13 = (f32[64,2048]{1,0:T(8,128)S(1)}, f32[64,2048]{1,0:T(8,128)}, u32[]{:S(2)}) copy-start(f32[64,2048]{1,0:T(8,128)} %copy-done.12) | copy-start | bytes 1572868
  192.4 18.3 %copy-start.22 = (bf16[64,2048]{1,0:T(8,128)(2,1)S(1)}, bf16[64,2048]{1,0:T(8,128)(2,1)}, u32[]{:S(2)}) copy-start(bf16[64,2048]{1,0:T(8,128)(2,1)} %get-tuple-element.102.refs_2_) | copy-start | bytes 786436
  210.7 21.3 %copy-start.19 = (f32[512,256]{1,0:T(8,128)S(1)}, f32[512,256]{1,0:T(8,128)}, u32[]{:S(2)}) copy-start(f32[512,256]{1,0:T(8,128)} %copy-done.18) | copy-start | bytes 1572868
  210.7 21.3 %copy-start.30 = (f32[512,256]{1,0:T(8,128)S(1)}, f32[512,256]{1,0:T(8,128)}, u32[]{:S(2)}) copy-start(f32[512,256]{1,0:T(8,128)} %copy-done.29) | copy-start | bytes 1572868
  226.9 5.0 %collective-permute-start.8 = (bf16[4,64,2048]{2,1,0:T(8,128)(2,1)S(1)}, bf16[4,64,2048]{2,1,0:T(8,128)(2,1)S(1)}, u32[]{:S(2)}, u32[]{:S(2)}) collective-permute-start(bf16[4,64,2048]{2,1,0:T(8,128)(2,1)S(1)} %all_to_all.37), channel_id=1, source_target_pairs={{0,8},{8,0},{16,24},{24,16},{32,40},{40,32},{48,56},{56,48},{64,72... | collective-permute-start | bytes 3145736 | tf_op jit(solution)/shard_map/ppermute | solution.py:678
  250.7 5.8 %collective-permute-start.9 = (bf16[256,2048]{1,0:T(8,128)(2,1)}, bf16[256,2048]{1,0:T(8,128)(2,1)}, u32[]{:S(2)}, u32[]{:S(2)}) collective-permute-start(bf16[256,2048]{1,0:T(8,128)(2,1)} %get-tuple-element.73), channel_id=1, source_target_pairs={{0,8},{8,0},{16,24},{24,16},{32,40},{40,32},{48,56},{56,48},{64,72... | collective-permute-start | bytes 3145736 | tf_op jit(solution)/shard_map/ppermute | solution.py:678
  251.1 38.3 %all-to-all-start.6 = ((bf16[16,128,512]{2,1,0:T(8,128)(2,1)}), bf16[16,128,512]{2,1,0:T(8,128)(2,1)}, u32[]{:S(2)}, u32[]{:S(2)}) async-start(bf16[16,128,512]{2,1,0:T(8,128)(2,1)} %bitcast.31), calls=%async_computation.7 | async-start | bytes 4194304 | tf_op jit(solution)/shard_map/all_to_all | solution.py:703
  269.3 26.5 %collective-permute-start.10 = (bf16[256,2048]{1,0:T(8,128)(2,1)S(1)}, bf16[256,2048]{1,0:T(8,128)(2,1)}, u32[]{:S(2)}, u32[]{:S(2)}) collective-permute-start(bf16[256,2048]{1,0:T(8,128)(2,1)S(1)} %get-tuple-element.75), channel_id=1, source_target_pairs={{0,8},{8,0},{16,24},{24,16},{32,40},{40,32},{48,56},{56,48},{64,72... | collective-permute-start | bytes 3145736 | tf_op jit(solution)/shard_map/ppermute | solution.py:678
  289.4 40.0 %all-to-all-start.5 = ((bf16[16,144,512]{2,1,0:T(8,128)(2,1)}), bf16[16,144,512]{2,1,0:T(8,128)(2,1)}, u32[]{:S(2)}, u32[]{:S(2)}) async-start(bf16[16,144,512]{2,1,0:T(8,128)(2,1)} %shard_map.272.refs_2_), calls=%async_computation.6 | async-start | bytes 4718592 | tf_op jit(solution)/shard_map/all_to_all | solution.py:703
  295.8 46.1 %reduce-scatter.3.cloned.1.call-start = ((), (), s32[]{:S(2)}) async-start(), calls=%async_computation.11 | async-start | bytes 1310720 | tf_op jit(solution)/shard_map/reduce_scatter | solution.py:810
  298.9 16.9 %copy-start.9 = (bf16[64,2048]{1,0:T(8,128)(2,1)S(1)}, bf16[64,2048]{1,0:T(8,128)(2,1)}, u32[]{:S(2)}) copy-start(bf16[64,2048]{1,0:T(8,128)(2,1)} %copy-done.8) | copy-start | bytes 786436
  299.1 6.9 %collective-permute-start.13 = (bf16[64,2048]{1,0:T(8,128)(2,1)S(1)}, bf16[64,2048]{1,0:T(8,128)(2,1)S(1)}, u32[]{:S(2)}, u32[]{:S(2)}) collective-permute-start(bf16[64,2048]{1,0:T(8,128)(2,1)S(1)} %get-tuple-element.100), channel_id=1, source_target_pairs={{0,2},{2,4},{4,6},{6,0},{1,3},{3,5},{5,7},{7,1},{8,10},{10,12},{12... | collective-permute-start | bytes 786440 | tf_op jit(solution)/shard_map/ppermute | solution.py:684
  299.6 12.1 %collective-permute-start.14 = (bf16[64,2048]{1,0:T(8,128)(2,1)S(1)}, bf16[64,2048]{1,0:T(8,128)(2,1)S(1)}, u32[]{:S(2)}, u32[]{:S(2)}) collective-permute-start(bf16[64,2048]{1,0:T(8,128)(2,1)S(1)} %get-tuple-element.99), channel_id=1, source_target_pairs={{0,4},{2,6},{4,0},{6,2},{1,5},{3,7},{5,1},{7,3},{8,12},{10,14},{12... | collective-permute-start | bytes 786440 | tf_op jit(solution)/shard_map/ppermute | solution.py:684
  301.8 14.0 %collective-permute-start.15 = (bf16[64,2048]{1,0:T(8,128)(2,1)S(1)}, bf16[64,2048]{1,0:T(8,128)(2,1)S(1)}, u32[]{:S(2)}, u32[]{:S(2)}) collective-permute-start(bf16[64,2048]{1,0:T(8,128)(2,1)S(1)} %get-tuple-element.98), channel_id=1, source_target_pairs={{0,6},{2,0},{4,2},{6,4},{1,7},{3,1},{5,3},{7,5},{8,14},{10,8},{12,... | collective-permute-start | bytes 786440 | tf_op jit(solution)/shard_map/ppermute | solution.py:684
  316.2 11.8 %collective-permute-start.16 = (bf16[64,2048]{1,0:T(8,128)(2,1)S(1)}, bf16[64,2048]{1,0:T(8,128)(2,1)S(1)}, u32[]{:S(2)}, u32[]{:S(2)}) collective-permute-start(bf16[64,2048]{1,0:T(8,128)(2,1)S(1)} %shard_map.274), channel_id=1, source_target_pairs={{0,8},{8,0},{16,24},{24,16},{32,40},{40,32},{48,56},{56,48},{64,72... | collective-permute-start | bytes 786440 | tf_op jit(solution)/shard_map/ppermute | solution.py:678
  324.5 9.1 %collective-permute-start.22 = (bf16[128,512]{1,0:T(8,128)(2,1)S(1)}, bf16[128,512]{1,0:T(8,128)(2,1)S(1)}, u32[]{:S(2)}, u32[]{:S(2)}) collective-permute-start(bf16[128,512]{1,0:T(8,128)(2,1)S(1)} %reduce_sum.129), channel_id=1, source_target_pairs={{8,1},{1,8},{24,17},{17,24},{40,33},{33,40},{56,49},{49,56},{72,65... | collective-permute-start | bytes 393224 | tf_op jit(solution)/shard_map/ppermute | solution.py:731
  328.2 14.7 %copy-start.47 = (bf16[128,2048]{1,0:T(8,128)(2,1)}, bf16[128,2048]{1,0:T(8,128)(2,1)S(1)}, u32[]{:S(2)}) copy-start(bf16[128,2048]{1,0:T(8,128)(2,1)S(1)} %maximum_select_fusion.2) | copy-start | bytes 1572868
  328.2 23.2 %collective-permute-start.17 = (bf16[128,2048]{1,0:T(8,128)(2,1)S(1)}, bf16[128,2048]{1,0:T(8,128)(2,1)}, u32[]{:S(2)}, u32[]{:S(2)}) collective-permute-start(bf16[128,2048]{1,0:T(8,128)(2,1)S(1)} %maximum_select_fusion.2), channel_id=1, source_target_pairs={{0,1},{9,8},{16,17},{25,24},{32,33},{41,40},{48,49},{57,56},{64,65... | collective-permute-start | bytes 1572872 | tf_op jit(solution)/shard_map/ppermute | solution.py:849
  331.5 8.4 %collective-permute-start.18 = (bf16[144,512]{1,0:T(8,128)(2,1)S(1)}, bf16[144,512]{1,0:T(8,128)(2,1)S(1)}, u32[]{:S(2)}, u32[]{:S(2)}) collective-permute-start(bf16[144,512]{1,0:T(8,128)(2,1)S(1)} %reduce_sum.128), channel_id=1, source_target_pairs={{8,1},{1,8},{24,17},{17,24},{40,33},{33,40},{56,49},{49,56},{72,65... | collective-permute-start | bytes 442376 | tf_op jit(solution)/shard_map/ppermute | solution.py:731
  333.6 25.4 %copy-start.27 = (bf16[128,512]{1,0:T(8,128)(2,1)}, bf16[128,512]{1,0:T(8,128)(2,1)S(1)}, u32[]{:S(2)}) copy-start(bf16[128,512]{1,0:T(8,128)(2,1)S(1)} %broadcast_select_fusion.4.o0) | copy-start | bytes 393220
  333.7 17.8 %collective-permute-start.23 = (bf16[128,512]{1,0:T(8,128)(2,1)S(1)}, bf16[128,512]{1,0:T(8,128)(2,1)S(1)}, u32[]{:S(2)}, u32[]{:S(2)}) collective-permute-start(bf16[128,512]{1,0:T(8,128)(2,1)S(1)} %broadcast_select_fusion.4.o0), channel_id=1, source_target_pairs={{0,2},{2,4},{4,6},{6,0},{1,3},{3,5},{5,7},{7,1},{8,10},{10,12},{12... | collective-permute-start | bytes 393224 | tf_op jit(solution)/shard_map/ppermute | solution.py:684
  334.1 19.7 %collective-permute-start.24 = (bf16[128,512]{1,0:T(8,128)(2,1)S(1)}, bf16[128,512]{1,0:T(8,128)(2,1)S(1)}, u32[]{:S(2)}, u32[]{:S(2)}) collective-permute-start(bf16[128,512]{1,0:T(8,128)(2,1)S(1)} %broadcast_select_fusion.4.o0), channel_id=1, source_target_pairs={{0,4},{2,6},{4,0},{6,2},{1,5},{3,7},{5,1},{7,3},{8,12},{10,14},{12... | collective-permute-start | bytes 393224 | tf_op jit(solution)/shard_map/ppermute | solution.py:684
  336.3 19.7 %collective-permute-start.25 = (bf16[128,512]{1,0:T(8,128)(2,1)S(1)}, bf16[128,512]{1,0:T(8,128)(2,1)S(1)}, u32[]{:S(2)}, u32[]{:S(2)}) collective-permute-start(bf16[128,512]{1,0:T(8,128)(2,1)S(1)} %broadcast_select_fusion.4.o0), channel_id=1, source_target_pairs={{0,6},{2,0},{4,2},{6,4},{1,7},{3,1},{5,3},{7,5},{8,14},{10,8},{12,... | collective-permute-start | bytes 393224 | tf_op jit(solution)/shard_map/ppermute | solution.py:684
  339.9 11.4 %collective-permute-start.26 = (bf16[128,2304]{1,0:T(8,128)(2,1)}, bf16[128,2304]{1,0:T(8,128)(2,1)S(1)}, u32[]{:S(2)}, u32[]{:S(2)}) collective-permute-start(bf16[128,2304]{1,0:T(8,128)(2,1)} %reduce-scatter.5.cloned.1.call-done), channel_id=1, source_target_pairs={{8,1},{1,8},{24,17},{17,24},{40,33},{33,40},{56,49},{49,56},{72,65... | collective-permute-start | bytes 1769480 | tf_op jit(solution)/shard_map/ppermute | solution.py:731
  342.9 44.9 %copy-start.31 = (bf16[128,1024]{1,0:T(8,128)(2,1)S(1)}, bf16[128,1024]{1,0:T(8,128)(2,1)}, u32[]{:S(2)}) copy-start(bf16[128,1024]{1,0:T(8,128)(2,1)} %wg.1) | copy-start | bytes 786436
  342.9 44.9 %copy-start.32 = (bf16[128,1024]{1,0:T(8,128)(2,1)S(1)}, bf16[128,1024]{1,0:T(8,128)(2,1)}, u32[]{:S(2)}) copy-start(bf16[128,1024]{1,0:T(8,128)(2,1)} %wq.1) | copy-start | bytes 786436
  342.9 44.9 %copy-start.34 = (f32[128,1]{1,0:T(8,128)S(1)}, f32[128,1]{1,0:T(8,128)}, u32[]{:S(2)}) copy-start(f32[128,1]{1,0:T(8,128)} %copy.58.gain) | copy-start | bytes 1540
  342.9 44.9 %copy-start.37 = (bf16[128,512]{1,0:T(8,128)(2,1)S(1)}, bf16[128,512]{1,0:T(8,128)(2,1)}, u32[]{:S(2)}) copy-start(bf16[128,512]{1,0:T(8,128)(2,1)} %wv.1) | copy-start | bytes 393220
  342.9 44.9 %copy-start.38 = (bf16[128,512]{1,0:T(8,128)(2,1)S(1)}, bf16[128,512]{1,0:T(8,128)(2,1)}, u32[]{:S(2)}) copy-start(bf16[128,512]{1,0:T(8,128)(2,1)} %wk.1) | copy-start | bytes 393220
  351.3 6.0 %collective-permute-start.11 = (bf16[64,2048]{1,0:T(8,128)(2,1)S(1)}, bf16[64,2048]{1,0:T(8,128)(2,1)S(1)}, u32[]{:S(2)}, u32[]{:S(2)}) collective-permute-start(bf16[64,2048]{1,0:T(8,128)(2,1)S(1)} %add_convert_fusion.4), channel_id=1, source_target_pairs={{0,8},{8,0},{16,24},{24,16},{32,40},{40,32},{48,56},{56,48},{64,72... | collective-permute-start | bytes 786440 | tf_op jit(solution)/shard_map/ppermute | solution.py:678
  351.4 8.7 %collective-permute-start.19 = (bf16[144,512]{1,0:T(8,128)(2,1)S(1)}, bf16[144,512]{1,0:T(8,128)(2,1)S(1)}, u32[]{:S(2)}, u32[]{:S(2)}) collective-permute-start(bf16[144,512]{1,0:T(8,128)(2,1)S(1)} %broadcast_select_fusion.3.i0), channel_id=1, source_target_pairs={{0,2},{2,4},{4,6},{6,0},{1,3},{3,5},{5,7},{7,1},{8,10},{10,12},{12... | collective-permute-start | bytes 442376 | tf_op jit(solution)/shard_map/ppermute | solution.py:684
  352.1 8.8 %collective-permute-start.20 = (bf16[144,512]{1,0:T(8,128)(2,1)S(1)}, bf16[144,512]{1,0:T(8,128)(2,1)S(1)}, u32[]{:S(2)}, u32[]{:S(2)}) collective-permute-start(bf16[144,512]{1,0:T(8,128)(2,1)S(1)} %broadcast_select_fusion.3.i0), channel_id=1, source_target_pairs={{0,4},{2,6},{4,0},{6,2},{1,5},{3,7},{5,1},{7,3},{8,12},{10,14},{12... | collective-permute-start | bytes 442376 | tf_op jit(solution)/shard_map/ppermute | solution.py:684
  353.8 34.0 %copy-start.40 = (bf16[128,512]{1,0:T(8,128)(2,1)S(1)}, bf16[128,512]{1,0:T(8,128)(2,1)}, u32[]{:S(2)}) copy-start(bf16[128,512]{1,0:T(8,128)(2,1)} %copy-done.39) | copy-start | bytes 393220
  354.5 37.5 %collective-permute-start.27 = (bf16[128,2304]{1,0:T(8,128)(2,1)S(1)}, bf16[128,2304]{1,0:T(8,128)(2,1)S(1)}, u32[]{:S(2)}, u32[]{:S(2)}) collective-permute-start(bf16[128,2304]{1,0:T(8,128)(2,1)S(1)} %broadcast_select_fusion.b0), channel_id=1, source_target_pairs={{0,2},{2,4},{4,6},{6,0},{1,3},{3,5},{5,7},{7,1},{8,10},{10,12},{12... | collective-permute-start | bytes 1769480 | tf_op jit(solution)/shard_map/ppermute | solution.py:684
  356.0 31.8 %copy-start.42 = (bf16[128,512]{1,0:T(8,128)(2,1)S(1)}, bf16[128,512]{1,0:T(8,128)(2,1)}, u32[]{:S(2)}) copy-start(bf16[128,512]{1,0:T(8,128)(2,1)} %copy-done.41) | copy-start | bytes 393220
  356.7 35.3 %collective-permute-start.28 = (bf16[128,2304]{1,0:T(8,128)(2,1)S(1)}, bf16[128,2304]{1,0:T(8,128)(2,1)S(1)}, u32[]{:S(2)}, u32[]{:S(2)}) collective-permute-start(bf16[128,2304]{1,0:T(8,128)(2,1)S(1)} %broadcast_select_fusion.b0), channel_id=1, source_target_pairs={{0,4},{2,6},{4,0},{6,2},{1,5},{3,7},{5,1},{7,3},{8,12},{10,14},{12... | collective-permute-start | bytes 1769480 | tf_op jit(solution)/shard_map/ppermute | solution.py:684
  357.3 30.6 %copy-start.44 = (bf16[128,512]{1,0:T(8,128)(2,1)S(1)}, bf16[128,512]{1,0:T(8,128)(2,1)}, u32[]{:S(2)}) copy-start(bf16[128,512]{1,0:T(8,128)(2,1)} %copy-done.43) | copy-start | bytes 393220
  357.3 35.5 %collective-permute-start.29 = (bf16[128,2304]{1,0:T(8,128)(2,1)S(1)}, bf16[128,2304]{1,0:T(8,128)(2,1)}, u32[]{:S(2)}, u32[]{:S(2)}) collective-permute-start(bf16[128,2304]{1,0:T(8,128)(2,1)S(1)} %broadcast_select_fusion.b0), channel_id=1, source_target_pairs={{0,6},{2,0},{4,2},{6,4},{1,7},{3,1},{5,3},{7,5},{8,14},{10,8},{12,... | collective-permute-start | bytes 1769480 | tf_op jit(solution)/shard_map/ppermute | solution.py:684
  360.0 27.8 %copy-start.28 = (bf16[128,512]{1,0:T(8,128)(2,1)S(1)}, bf16[128,512]{1,0:T(8,128)(2,1)}, u32[]{:S(2)}) copy-start(bf16[128,512]{1,0:T(8,128)(2,1)} %copy-done.27) | copy-start | bytes 393220
  360.0 32.8 %copy-start.20 = (bf16[128,3072]{1,0:T(8,128)(2,1)S(1)}, bf16[128,3072]{1,0:T(8,128)(2,1)}, u32[]{:S(2)}) copy-start(bf16[128,3072]{1,0:T(8,128)(2,1)} %w_up.1) | copy-start | bytes 2359300
  360.0 32.8 %copy-start.21 = (bf16[128,3072]{1,0:T(8,128)(2,1)S(1)}, bf16[128,3072]{1,0:T(8,128)(2,1)}, u32[]{:S(2)}) copy-start(bf16[128,3072]{1,0:T(8,128)(2,1)} %w_gate.1) | copy-start | bytes 2359300
  360.0 27.8 %collective-permute-start.21 = (bf16[144,512]{1,0:T(8,128)(2,1)S(1)}, bf16[144,512]{1,0:T(8,128)(2,1)S(1)}, u32[]{:S(2)}, u32[]{:S(2)}) collective-permute-start(bf16[144,512]{1,0:T(8,128)(2,1)S(1)} %broadcast_select_fusion.3.i0), channel_id=1, source_target_pairs={{0,6},{2,0},{4,2},{6,4},{1,7},{3,1},{5,3},{7,5},{8,14},{10,8},{12,... | collective-permute-start | bytes 442376 | tf_op jit(solution)/shard_map/ppermute | solution.py:684
  361.0 41.8 %collective-permute-start.12 = (bf16[128,2048]{1,0:T(8,128)(2,1)}, bf16[128,2048]{1,0:T(8,128)(2,1)}, u32[]{:S(2)}, u32[]{:S(2)}) collective-permute-start(bf16[128,2048]{1,0:T(8,128)(2,1)} %maximum_select_fusion.1), channel_id=1, source_target_pairs={{0,1},{9,8},{16,17},{25,24},{32,33},{41,40},{48,49},{57,56},{64,65... | collective-permute-start | bytes 1572872 | tf_op jit(solution)/shard_map/ppermute | solution.py:849
  394.7 11.2 %copy-start.1 = (bf16[3072,128]{1,0:T(8,128)(2,1)S(1)}, bf16[3072,128]{1,0:T(8,128)(2,1)}, u32[]{:S(2)}) copy-start(bf16[3072,128]{1,0:T(8,128)(2,1)} %param.30) | copy-start | bytes 2359300
  400.6 4.2 %collective-permute-start.30 = (f32[3,128]{1,0:T(4,128)S(1)}, f32[3,128]{1,0:T(4,128)S(1)}, u32[]{:S(2)}, u32[]{:S(2)}) collective-permute-start(f32[3,128]{1,0:T(4,128)S(1)} %pad_maximum_fusion.4), channel_id=1, source_target_pairs={{0,1},{1,0},{2,3},{3,2},{4,5},{5,4},{6,7},{7,6},{8,9},{9,8},{10,11... | collective-permute-start | bytes 4616 | tf_op jit(solution)/shard_map/ppermute | solution.py:839
  (29 other events, 115.1 us)
Sparse Core Ops, SparseCore 0:
  21.7 56.1 all-gather.2
  80.7 75.2 all-gather.4
  192.5 102.9 reduce-scatter.4
  299.4 26.4 reduce-scatter.2

commit v4 on v3

--- a/solution.py
+++ b/solution.py
@@ -225,47 +225,42 @@
     )(low, gate, w, of_row, of_column)
 
 
-def feed_kernel(
-    ua, ub, ca, cb, wg, wu, wd, hidden, d_gate, d_up, mine, other, total, u_all, c_all
-):
-    step = pl.program_id(0)
+def flip_kernel(pieces, out):
+    at = 0
+    for piece in pieces:
+        out[:, at : at + piece.shape[0]] = piece[...].T
+        at += piece.shape[0]
+
+
+def flip(*pieces):
+    length, width = sum(piece.shape[0] for piece in pieces), pieces[0].shape[1]
+    chunk = 2 * HD
+    return call(
+        lambda *refs: flip_kernel(refs[:-1], refs[-1]),
+        (width // chunk,),
+        [pl.BlockSpec((piece.shape[0], chunk), lambda i: (0, i)) for piece in pieces],
+        rowed(chunk, length),
+        struct((width, length), BF16),
+        1 << 20,
+    )(*pieces)
+
+
+def feed_kernel(ua, ub, ca, cb, wg, wu, wd, hidden, d_gate, d_up):
     half = ua.shape[0]
-
-    @pl.when(step == 0)
-    def _():
-        u_all[:half, :] = ua[...]
-        u_all[half:, :] = ub[...]
-        c_all[:half, :] = flat(ca[...])
-        c_all[half:, :] = flat(cb[...])
-
-    gate, up = dot(u_all[...], wg[...]), dot(u_all[...], wu[...])
-    d_hidden = dot(c_all[...], wd[...])
-    sig = jax.nn.sigmoid(gate)
-    silu = gate * sig
-    hidden[...] = (silu * up).astype(BF16)
-    dg = (d_hidden * up * sig * (1.0 + gate * (1.0 - sig))).astype(BF16)
-    du = (d_hidden * silu).astype(BF16)
-    d_gate[...] = dg
-    d_up[...] = du
-    term = dot_back(dg, wg[...]) + dot_back(du, wu[...])
-
-    @pl.when(step == 0)
-    def _():
-        total[...] = term
-
-    @pl.when(step > 0)
-    def _():
-        total[...] += term
-
-    @pl.when(step == pl.num_programs(0) - 1)
-    def _():
-        mine[...] = total[:half, :]
-        other[...] = total[half:, :].astype(BF16)
-
-
-def feed(ua, ub, ca, cb, w):
+    for number, (u, cot) in enumerate(((ua, ca), (ub, cb))):
+        rows = slice(number * half, (number + 1) * half)
+        gate, up = dot(u[...], wg[...]), dot(u[...], wu[...])
+        d_hidden = dot(flat(cot[...]), wd[...])
+        sig = jax.nn.sigmoid(gate)
+        silu = gate * sig
+        hidden[rows, :] = (silu * up).astype(BF16)
+        d_gate[rows, :] = (d_hidden * up * sig * (1.0 + gate * (1.0 - sig))).astype(BF16)
+        d_up[rows, :] = (d_hidden * silu).astype(BF16)
+
+
+def feed(ua, ub, ca, cb, w, behind):
     half, width = ua.shape
-    chunk = 2 * HD
+    chunk = 3 * HD
     parts = w.shape[1] // 3 // chunk
     column = lambda shift: pl.BlockSpec((width, chunk), lambda i: (0, shift * parts + i))
     unit = pl.BlockSpec((2 * half, chunk), lambda i: (0, i))
@@ -276,12 +271,37 @@
         [fixed((half, width))] * 2
         + [piled(ca.shape, 1)] * 2
         + [column(0), column(1), column(2)],
-        [unit, unit, unit, fixed((half, width)), fixed((half, width))],
-        [struct((2 * half, units), BF16)] * 3
-        + [struct((half, width), F32), struct((half, width), BF16)],
-        2 * 2 * half * width * units * 5,
-        scratch=[pltpu.VMEM((2 * half, width), F32)] + [pltpu.VMEM((2 * half, width), BF16)] * 2,
+        [unit, unit, unit],
+        [struct((2 * half, units), BF16)] * 3,
+        2 * 2 * half * width * units * 3,
+        behind=behind,
     )(ua, ub, ca, cb, w, w, w)
+
+
+def feed_back_kernel(d_gate, d_up, wg, wu, mine, other):
+    half = mine.shape[0]
+    out = dot_back(d_gate[...], wg[...]) + dot_back(d_up[...], wu[...])
+    mine[...] = out[:half, :]
+    other[...] = out[half:, :].astype(BF16)
+
+
+def feed_back(d_gate, d_up, w):
+    length, units = d_gate.shape
+    half, width = length // 2, w.shape[0]
+    chunk = 4 * HD
+    slab = pl.BlockSpec((half, chunk), lambda i: (0, i))
+    return call(
+        feed_back_kernel,
+        (width // chunk,),
+        [fixed((length, units))] * 2
+        + [
+            pl.BlockSpec((chunk, units), lambda i: (i, 0)),
+            pl.BlockSpec((chunk, units), lambda i: (i, 1)),
+        ],
+        [slab, slab],
+        [struct((half, width), F32), struct((half, width), BF16)],
+        2 * length * width * units * 2,
+    )(d_gate, d_up, w, w)
 
 
 def down_kernel(hidden, w, mine, other):
@@ -310,33 +330,37 @@
     )(left, w)
 
 
-def feed_grads_kernel(ua, ub, ca, cb, d_gate, d_up, hidden, out):
-    half, units = ua.shape[0], hidden.shape[1]
-    pairs = ((ua, ub, d_gate), (ua, ub, d_up), (ca, cb, hidden))
-    for number, (first, second, right) in enumerate(pairs):
-        first, second = first[...], second[...]
-        if number == 2:
-            first, second = flat(first), flat(second)
-        term = dot_rows(first, right[:half, :]) + dot_rows(second, right[half:, :])
-        out[:, number * units : (number + 1) * units] = term.astype(BF16)
-
-
-def feed_grads(ua, ub, ca, cb, d_gate, d_up, hidden, behind):
-    half, width = ua.shape
+def spread_blocks(left, right, out, start):
+    for place in range(left.shape[1] // HD):
+        term = dot_rows(left[:, head(place)], right)
+        for owner in range(right.shape[1] // HD):
+            at = start + place * HD
+            out[owner * HD : (owner + 1) * HD, at : at + HD] = term[:, head(owner)].astype(BF16)
+
+
+def feed_grads_kernel(u_flip, ca, cb, d_gate, d_up, hidden, out):
     units = hidden.shape[1]
-    chunk = 2 * HD
-    slab = pl.BlockSpec((half, chunk), lambda i: (0, i))
+    out[:, :units] = dot(u_flip[...], d_gate[...]).astype(BF16)
+    out[:, units : 2 * units] = dot(u_flip[...], d_up[...]).astype(BF16)
+    cot = jnp.concatenate([flat(ca[...]), flat(cb[...])], axis=0)
+    spread_blocks(hidden, cot, out, 2 * units)
+
+
+def feed_grads(u_flip, ca, cb, d_gate, d_up, hidden, behind):
+    width, length = u_flip.shape
+    units = hidden.shape[1]
+    chunk = 4 * HD
     return call(
         feed_grads_kernel,
         (width // chunk,),
-        [slab] * 2
+        [rowed(chunk, length)]
         + [pl.BlockSpec((ca.shape[0], ca.shape[1] // 2, chunk), lambda i: (0, 1, i))] * 2
-        + [fixed((2 * half, units))] * 3,
+        + [fixed((length, units))] * 3,
         rowed(chunk, 3 * units),
         struct((width, 3 * units), BF16),
-        2 * 2 * half * width * units * 3,
+        2 * length * width * units * 3,
         behind=behind,
-    )(ua, ub, ca, cb, d_gate, d_up, hidden)
+    )(u_flip, ca, cb, d_gate, d_up, hidden)
 
 
 def gate_back_kernel(da, db, w_out, gate, attended, d_attended, d_gate):
@@ -458,55 +482,52 @@
     )(d_qkv, d_gate, w)
 
 
-def outer_grads_kernel(xn, da, db, d_gate, gated, out):
-    half = da.shape[0]
+def outer_grads_kernel(x_flip, da, db, d_gate, gated, out):
     split = d_gate.shape[1]
-    out[:, :split] = dot_rows(xn[...], d_gate[...]).astype(BF16)
-    term = dot_rows(da[...], gated[:half, :]) + dot_rows(db[...], gated[half:, :])
-    out[:, split:] = term.astype(BF16)
-
-
-def outer_grads(xn, da, db, d_gate, gated):
+    out[:, :split] = dot(x_flip[...], d_gate[...]).astype(BF16)
+    spread_blocks(gated, jnp.concatenate([da[...], db[...]], axis=0), out, split)
+
+
+def outer_grads(x_flip, da, db, d_gate, gated):
     half, width = da.shape
-    chunk = 2 * HD
+    chunk = 4 * HD
     slab = pl.BlockSpec((half, chunk), lambda i: (0, i))
     return call(
         outer_grads_kernel,
         (width // chunk,),
-        [pl.BlockSpec((2 * half, chunk), lambda i: (0, i)), slab, slab]
-        + [fixed((2 * half, 2 * HD))] * 2,
+        [rowed(chunk, 2 * half), slab, slab] + [fixed((2 * half, 2 * HD))] * 2,
         rowed(chunk, 4 * HD),
         struct((width, 4 * HD), BF16),
         2 * 2 * half * width * 4 * HD,
-    )(xn, da, db, d_gate, gated)
-
-
-def inner_grads_kernel(xn, d_qkv, terms, out):
-    term = dot_rows(xn[...], d_qkv[...]).astype(BF16)
+    )(x_flip, da, db, d_gate, gated)
+
+
+def inner_grads_kernel(x_flip, d_qkv, terms, out):
+    term = dot(x_flip[...], d_qkv[...]).astype(BF16)
     count, block = out.shape[0], out.shape[1] - terms.shape[1]
     for number in range(count):
         out[number, :block] = term[number * block : (number + 1) * block]
         out[number, block:] = terms[number].astype(BF16)
 
 
-def inner_grads(xn, d_qkv, terms, behind):
-    length, width = xn.shape
+def inner_grads(x_flip, d_qkv, terms, behind):
+    width, length = x_flip.shape
     columns, extra = d_qkv.shape[1], terms.shape[1]
     owners = terms.shape[0]
     block = width // owners
     return call(
         inner_grads_kernel,
-        (owners // 2,),
+        (owners // 4,),
         [
-            pl.BlockSpec((length, 2 * block), lambda i: (0, i)),
+            rowed(4 * block, length),
             fixed((length, columns)),
-            pl.BlockSpec((2, extra, columns), lambda i: (i, 0, 0)),
+            pl.BlockSpec((4, extra, columns), lambda i: (i, 0, 0)),
         ],
-        pl.BlockSpec((2, block + extra, columns), lambda i: (i, 0, 0)),
+        pl.BlockSpec((4, block + extra, columns), lambda i: (i, 0, 0)),
         struct((owners, block + extra, columns), BF16),
         2 * length * width * columns,
         behind=behind,
-    )(xn, d_qkv, terms)
+    )(x_flip, d_qkv, terms)
 
 
 def middle_kernel(parts, x, middle, spread):
@@ -517,7 +538,7 @@
         spread[number] = low
 
 
-def middle_step(parts, x):
+def middle_step(parts, x, behind):
     shape = x.shape
     return call(
         middle_kernel,
@@ -526,6 +547,7 @@
         [fixed(shape), fixed(parts.shape)],
         [struct(shape, F32), struct(parts.shape, BF16)],
         1 << 20,
+        behind=behind,
     )(parts, x)
 
 
@@ -554,21 +576,41 @@
     )(parts, middle, cot)
 
 
-def input_step_kernel(p0, p1, p2, p3, d_middle, x, out):
-    grads = sum(p[...].astype(F32) for p in (p0, p1, p2, p3))
-    out[...] = (d_middle[...] + norm_back(grads, x[...].astype(F32))).astype(BF16)
-
-
-def input_step(parts, d_middle, x):
-    shape = x.shape
-    return call(
-        input_step_kernel,
+def ends_kernel(parts, middle, d_middle, x, out):
+    rows = x.shape[0]
+    total = sum(part[...].astype(F32) for part in parts)
+    out[:rows, :] = (middle[...] + total[:rows, :]).astype(BF16)
+    back = norm_back(total[rows:, :], x[...].astype(F32))
+    out[rows:, :] = (d_middle[...] + back).astype(BF16)
+
+
+def ends_step(parts, middle, d_middle, x):
+    shape, wide = x.shape, parts[0].shape
+    count = len(parts)
+    return call(
+        lambda *refs: ends_kernel(refs[:count], *refs[count:]),
         (1,),
-        [fixed(shape)] * 6,
-        fixed(shape),
-        struct(shape, BF16),
+        [fixed(wide)] * count + [fixed(shape)] * 3,
+        fixed(wide),
+        struct(wide, BF16),
         1 << 20,
-    )(*parts, d_middle, x)
+    )(*parts, middle, d_middle, x)
+
+
+def sum_kernel(parts, out):
+    out[...] = jnp.sum(parts[...].astype(F32), axis=0).astype(BF16)
+
+
+def sum_step(parts, behind):
+    return call(
+        sum_kernel,
+        (1,),
+        [fixed(parts.shape)],
+        fixed(parts.shape[1:]),
+        struct(parts.shape[1:], BF16),
+        1 << 20,
+        behind=behind,
+    )(parts)
 
 
 def lanes(value):
@@ -589,7 +631,8 @@
     raw_gate, raw_up = raw[:, :units], raw[:, units : 2 * units]
     g_gate[...] = raw_gate * gain[...]
     g_up[...] = raw_up * gain[...]
-    g_down[...] = raw[:, 2 * units :].T
+    for place in range(units // HD):
+        g_down[head(place), :] = raw[:, 2 * units + place * HD : 2 * units + (place + 1) * HD]
     term = lanes(raw_gate * w_gate[...].astype(F32)) + lanes(raw_up * w_up[...].astype(F32))
 
     @pl.when(pl.program_id(0) == 0)
@@ -610,7 +653,7 @@
     raw_q, raw_k, raw_v = inner[:block, : 2 * HD], inner[:block, head(2)], inner[:block, head(3)]
     raw_g = outer[:, : 2 * HD]
     gq[...], gk[...], gv[...], gg[...] = raw_q * scale, raw_k * scale, raw_v * scale, raw_g * scale
-    go[...] = outer[:, 2 * HD :].T
+    go[head(0), :], go[head(1), :] = outer[:, head(2)], outer[:, head(3)]
     pairs = ((raw_q, wq), (raw_k, wk), (raw_v, wv), (raw_g, wg))
     term = sum(lanes(raw * w[...].astype(F32)) for raw, w in pairs)
     last = inner[block:, :HD]
@@ -674,6 +717,21 @@
     ]
     across_perm = [(joint(pair, t, t), joint(pair, t, 1 - t)) for pair in range(pairs) for t in range(2)]
 
+    def spot(pair, core, ctx, tp):
+        return ((pair * 2 + core) * n_ctx + ctx) * n_tp + tp
+
+    owner_perms = [
+        [
+            (spot(pair, core, ctx, tp), spot(pair, tp, (ctx + by) % n_ctx, core))
+            for pair in range(pairs)
+            for core in range(2)
+            for ctx in range(n_ctx)
+            for tp in range(n_tp)
+            if by > 0 or core != tp
+        ]
+        for by in range(n_ctx)
+    ]
+
     def core_swap(value):
         return lax.ppermute(value, "shard", core_perm)
 
@@ -700,8 +758,7 @@
         )
 
     def plane_exchange(value):
-        parts = lax.all_to_all(value, PLANE, 0, 0, axis_index_groups=planes)
-        return jnp.sum(parts.astype(F32), axis=0).astype(BF16)
+        return lax.all_to_all(value, PLANE, 0, 0, axis_index_groups=planes)
 
     def shards(
         tokens,
@@ -747,7 +804,7 @@
             (0, lax.axis_index("shard") * head_rows),
         )
         first = jnp.concatenate([first, quarter(w_out, 0).T, ends], axis=1)
-        w1 = plane_gather(swapped(first))
+        found = plane_gather(first)
 
         def half_rows(place):
             pieces = [lax.dynamic_slice_in_dim(v, place * rows, rows, 0) for v in (tokens, cotangent)]
@@ -775,52 +832,84 @@
         of_column = jnp.stack([segment, places], axis=0)
         cosine, sine = rope_tables(position, HD)
 
+        found, xa, xb, of_row, of_column, cosine, sine = lax.optimization_barrier(
+            (found, xa, xb, of_row, of_column, cosine, sine)
+        )
+        found = found.reshape(pairs, n_tp, gain_in.shape[0], -1)
+        mine = lax.dynamic_index_in_dim(found, core, 1, False)
+        other = core_swap(lax.dynamic_index_in_dim(found, 1 - core, 1, False))
+        w1 = jnp.where(
+            core == 0, jnp.stack([mine, other], axis=1), jnp.stack([other, mine], axis=1)
+        ).reshape(-1, first.shape[1])
+
         xn, pre, low, gate, gains = project(xa, xb, w1, cosine, sine)
         probs, attended, gated, mine, other = attend(low, gate, w1, of_row, of_column)
-        middle, spread = middle_step(ctx_exchange(tree_half(mine, other)), own_x)
+        x_flip = flip(xn)
+        middle, spread = middle_step(ctx_exchange(tree_half(mine, other)), own_x, (x_flip,))
         ua, ub = (flat(v) for v in tree_rows(spread))
-
-        hidden, d_gate, d_up, mine, other = feed(ua, ub, xa, xb, w2)
-        half = tree_half(mine, other)
-        ffn = feed_grads(ua, ub, xa, xb, d_gate, d_up, hidden, (half,))
+        u_flip = flip(ua, ub)
+
+        hidden, d_gate, d_up = feed(ua, ub, xa, xb, w2, (u_flip,))
+        half = tree_half(*feed_back(d_gate, d_up, w2))
+        ffn = feed_grads(u_flip, xa, xb, d_gate, d_up, hidden, (half,))
         d_middle, spread = d_middle_step(ctx_exchange(half), middle, own_cot)
         da, db = (flat(v) for v in tree_rows(spread))
         grad_ffn = plane_scatter(ffn)
+        layer_mine, layer_other = down_product(hidden, w2, 2, (half,))
 
         d_attended, d_gate_pre = gate_back(da, db, w1, gate, attended)
-        outer = outer_grads(xn, da, db, d_gate_pre, gated)
-        grad_outer = plane_exchange(outer.reshape(n_shard, -1, 4 * HD))
+        outer = outer_grads(x_flip, da, db, d_gate_pre, gated)
+        outer_parts = plane_exchange(outer.reshape(n_shard, -1, 4 * HD))
         d_qkv, terms = attend_back(probs, low, d_attended, pre, gains, cosine, sine, (outer,))
-        half = tree_half(*input_back(d_qkv, d_gate_pre, w1))
+        in_mine, in_other = input_back(d_qkv, d_gate_pre, w1)
 
         def spread_terms(vector):
             return jnp.pad(vector.reshape(n_shard, 1, -1), ((0, 0), (0, 15), (0, 0)))
 
         wide_terms = jnp.concatenate([spread_terms(terms[0]), spread_terms(terms[1])], axis=2)
         wide_terms = jnp.pad(wide_terms, ((0, 0), (0, 0), (0, 4 * HD - 2 * head_rows)))
-        inner = inner_grads(xn, d_qkv, wide_terms, (half,))
-        grad_inner = plane_exchange(inner)
-        parts = [lax.dynamic_index_in_dim(half, ctx, 0, False)] + [
-            ctx_turn(lax.dynamic_index_in_dim(half, (ctx + by) % n_ctx, 0, False), by)
+        inner_parts = plane_exchange(inner_grads(x_flip, d_qkv, wide_terms, (in_other, outer_parts)))
+
+        both = jnp.concatenate(
+            [tree_half(layer_mine, layer_other), tree_half(in_mine, in_other)], axis=1
+        )
+        parts = [lax.dynamic_index_in_dim(both, ctx, 0, False)] + [
+            ctx_turn(lax.dynamic_index_in_dim(both, (ctx + by) % n_ctx, 0, False), by)
             for by in range(1, n_ctx)
         ]
-        input_own = input_step(parts, d_middle, own_x)
-
-        layer_half = tree_half(*down_product(hidden, w2, 2, (inner,)))
-        layer_own = middle + lax.psum_scatter(
-            flat(layer_half), "ctx", scatter_dimension=0, tiled=True
-        ).astype(F32)
+        ends = ends_step(parts, middle, d_middle, own_x)
+        sibling = core_swap(ends)
+
+        def whole(start):
+            mine, other = ends[start : start + rows], sibling[start : start + rows]
+            return jnp.where(
+                core == 0,
+                jnp.concatenate([mine, other], axis=0),
+                jnp.concatenate([other, mine], axis=0),
+            )
+
+        full = jnp.stack([whole(0), whole(rows)])
+        full = jnp.where(native, full, lax.ppermute(full, PLANE, across_perm))
 
         def owners(block):
             block = swapped(block)
             return [block] + [ctx_turn(block, by) for by in range(1, n_ctx)]
 
+        def owners_at_once(block):
+            moved = [lax.ppermute(block, ("shard", "ctx", "tp"), perm) for perm in owner_perms]
+            return [jnp.where(native, block, moved[0])] + moved[1:]
+
         turn_at = ctx.astype(jnp.int32).reshape(1)
         size = gain_in.shape[0]
+        outer_blocks = owners(sum_step(outer_parts, ()))
+        ffn_blocks = owners(grad_ffn)
+        inner_blocks = owners_at_once(
+            sum_step(inner_parts, (full, *ffn_blocks[1:], *outer_blocks[1:]))
+        )
         grad_gate, grad_up, grad_down, mid_sums = close(
             close_feed_kernel,
             turn_at,
-            owners(grad_ffn),
+            ffn_blocks,
             (w_gate, w_up),
             gain_two,
             w_down.shape,
@@ -829,7 +918,7 @@
         grad_query, grad_key, grad_value, grad_gate_attn, grad_out, in_sums, head_ends = close(
             close_attend_kernel,
             turn_at,
-            owners(grad_inner) + owners(grad_outer),
+            inner_blocks + outer_blocks,
             (w_query, w_key, w_value, w_gate_attn),
             gain_one,
             w_out.shape,
@@ -838,19 +927,9 @@
         gain_terms = jnp.stack([jnp.sum(in_sums, axis=1), jnp.sum(mid_sums, axis=1), head_ends[0]])
         gain_terms = gain_terms + lax.ppermute(gain_terms, "tp", [(0, 1), (1, 0)])
 
-        def finish(part):
-            low = part.astype(BF16)
-            sibling = core_swap(low)
-            full = jnp.where(
-                core == 0,
-                jnp.concatenate([low, sibling], axis=0),
-                jnp.concatenate([sibling, low], axis=0),
-            )
-            return jnp.where(native, full, lax.ppermute(full, PLANE, across_perm)).astype(F32)
-
         return (
-            finish(layer_own),
-            finish(input_own),
+            full[0].astype(F32),
+            full[1].astype(F32),
             gain_terms[0],
             grad_query,
             grad_key,

time: 414 us -> 411 us (level)
  local copies, waits for them, and re-layouts: 21.6 us -> 49.1 us
  waiting for transfers between devices: 151 us -> 130 us
  starting transfers between devices: 69 us -> 61.2 us
    unnamed x110 -> x133, local copies, waits for them, and re-layouts: 11.6 us -> 31.3 us
    all_to_all x2, waiting for transfers between devices: 19.5 us -> 0.01 us  [plane_exchange(): return lax.all_to_all(value, PLANE, 0, 0, axis_index_groups=planes)]
    all_gather x2, waiting for transfers between devices: 19.5 us -> 1.06 us  [plane_gather(): lax.all_gather(value, PLANE, axis=0, tiled=True, axis_index_groups=planes)]
    ppermute x5 -> x3, waiting for transfers between devices: 23.2 us -> 40.5 us  [swapped(): return jnp.where(native, value, lax.ppermute(value, PLANE, swap_perm))]
    select_n x2 -> x5, other arithmetic: 1.03 us -> 8.59 us  [the longest x1 7.31 us: shards(): jnp.where(core == 0, jnp.stack([mine, other], axis=1), jnp.stack([other,...]
    ppermute x2 -> x5, starting transfers between devices: 2.57 us -> 9.07 us  [the longest x4 7.78 us: owners_at_once(): lax.ppermute(block, ('shard', 'ctx', 'tp'), perm)]
    ppermute x5 -> x3, starting transfers between devices: 15.7 us -> 10.2 us  [swapped(): return jnp.where(native, value, lax.ppermute(value, PLANE, swap_perm))]
    dynamic_slice x0 -> x1, local copies, waits for them, and re-layouts: none -> 4.98 us  [shards(): mine = lax.dynamic_index_in_dim(found, core, 1, False)]
  transfers between devices with their start and end apart: 39 -> 36, of which waited for: 19 -> 18; matrix products, arithmetic and copies ran while one was open for 7% -> 9% of each run, Pallas kernels for 11% -> 11%
where the time goes in v4:
time: 411 us; the launch traced here: 407 us
  waiting for transfers between devices  130 us (32%)
  Pallas kernels  77 us (19%)
  starting transfers between devices  61.2 us (15%)
  blocking collectives  49.6 us (12%)
  local copies, waits for them, and re-layouts  49.1 us (12%)
  other arithmetic  24.9 us (6%)
  between operations  14.7 us (4%)
    pallas_call x18, Pallas kernels, call(): return lambda *operands: built(*operands, *behind)  69.4 us
    all_to_all x3, blocking collectives, ctx_exchange(): return lax.all_to_all(value, 'ctx', 0, 0)  49.6 us
    ppermute x3, waiting for transfers between devices, swapped(): return jnp.where(native, value, lax.ppermute(value, PLANE, swap_perm))  40.5 us
    ppermute x9, waiting for transfers between devices, ctx_turn(): lax.ppermute(value, 'ctx', [(i, (i + by) % n_ctx) for i in range(n_ctx)])  36.4 us
    all_to_all x2, waiting for transfers between devices, ctx_exchange(): return lax.all_to_all(value, 'ctx', 0, 0)  36.3 us
    unnamed x133, local copies, waits for them, and re-layouts  31.3 us
    ppermute x11, waiting for transfers between devices, core_swap(): return lax.ppermute(value, 'shard', core_perm)  14.8 us
    all_to_all x2, starting transfers between devices, plane_exchange(): return lax.all_to_all(value, PLANE, 0, 0, axis_index_groups=planes)  12.1 us
  transfers between devices with their start and end apart: 36, of which 18 were waited for; matrix products, arithmetic and copies ran while one was open for 9% of the time, Pallas kernels for 11%

profile of v4, /device:TPU:1, one launch (start us, length us, event | category | flops | bytes accessed | tf_op | source)
XLA Modules:
  0.0 406.6 jit_solution(12951710257196479173)
XLA Ops:
  14.2 4.5 %collective-permute-start.6 = (bf16[128,2304]{1,0:T(8,128)(2,1)S(1)}, bf16[128,2304]{1,0:T(8,128)(2,1)S(1)}, u32[]{:S(2)}, u32[]{:S(2)}) collective-permute-start(bf16[128,2304]{1,0:T(8,128)(2,1)S(1)} %pad_maximum_fusion.1), channel_id=1, source_target_pairs={{8,1},{1,8},{24,17},{17,24},{40,33},{33,40},{56,49},{49,56},{72,65... | collective-permute-start | bytes 1769480 | tf_op jit(solution)/shard_map/ppermute | solution.py:788
  18.8 7.5 %collective-permute-done.6 = bf16[128,2304]{1,0:T(8,128)(2,1)S(1)} collective-permute-done((bf16[128,2304]{1,0:T(8,128)(2,1)S(1)}, bf16[128,2304]{1,0:T(8,128)(2,1)S(1)}, u32[]{:S(2)}, u32[]{:S(2)}) %collective-permute-start.6) | collective-permute-done | bytes 589856 | tf_op jit(solution)/shard_map/ppermute | solution.py:788
  27.5 1.9 collective-permute-done
  30.4 1.6 broadcast_in_dim.20
  31.9 5.3 %all-to-all-start = ((bf16[4,128,2048]{2,1,0:T(8,128)(2,1)}), bf16[4,128,2048]{2,1,0:T(8,128)(2,1)}, u32[]{:S(2)}, u32[]{:S(2)}) async-start(bf16[4,128,2048]{2,1,0:T(8,128)(2,1)} %broadcast_in_dim.20), calls=%async_computation | async-start | bytes 4194304 | tf_op jit(solution)/shard_map/all_to_all | solution.py:739
  37.8 25.6 %all-to-all-done.refs_0_.refs_2_.refs_1_ = bf16[4,128,2048]{2,1,0:T(8,128)(2,1)} async-done(((bf16[4,128,2048]{2,1,0:T(8,128)(2,1)}), bf16[4,128,2048]{2,1,0:T(8,128)(2,1)}, u32[]{:S(2)}, u32[]{:S(2)}) %all-to-all-start) | async-done | bytes 2097184 | tf_op jit(solution)/shard_map/all_to_all | solution.py:739
  63.4 1.4 collective-permute-start.1
  67.2 1.7 collective-permute-done.1.refs_1_.refs_3_.refs_2_
  70.0 5.0 %constant_dynamic-slice_fusion.3 = (bf16[8,1,128,1152]{3,2,1,0:T(8,128)(2,1)}, bf16[8,128,1152]{2,1,0:T(8,128)(2,1)}) fusion(bf16[8,2,128,1152]{3,2,1,0:T(8,128)(2,1)} %bitcast.101, s32[]{:T(128)S(6)} %select_n.185, s32[]{:T(128)S(6)} %select_n.186), kind=kLoop, calls=%fused_computation.67 | loop fusion | bytes 9437192 | tf_op jit(solution)/shard_map/jit(dynamic_index_in_dim)/dynamic_slice | solution.py:839
  75.8 4.4 %collective-permute-done.3 = bf16[8,128,1152]{2,1,0:T(8,128)(2,1)} collective-permute-done((bf16[8,128,1152]{2,1,0:T(8,128)(2,1)}, bf16[8,128,1152]{2,1,0:T(8,128)(2,1)}, u32[]{:S(2)}, u32[]{:S(2)}) %collective-permute-start.3) | collective-permute-done | bytes 2359328 | tf_op jit(solution)/shard_map/ppermute | solution.py:736
  80.1 7.3 %maximum_select_fusion = bf16[8,2,128,1152]{3,2,1,0:T(8,128)(2,1)} fusion(bf16[8,1,128,1152]{3,2,1,0:T(8,128)(2,1)} %bitcast.18, bf16[8,1,128,1152]{3,2,1,0:T(8,128)(2,1)} %get-tuple-element.112, pred[]{:T(512)S(6)} %eq.74), kind=kLoop, calls=%fused_computation | loop fusion | flops 7077888 | bytes 9437185 | tf_op jit(solution)/shard_map/jit(_where)/select_n | solution.py:841
  87.5 5.7 %shard_map.263 = (bf16[512,2048]{1,0:T(8,128)(2,1)S(1)}, f32[512,384]{1,0:T(8,128)S(1)}, bf16[512,512]{1,0:T(8,128)(2,1)S(1)}, f32[512,256]{1,0:T(8,128)S(1)}, f32[16,128]{1,0:T(8,128)S(1)}) custom-call(bf16[4,128,2048]{2,1,0:T(8,128)(2,1)} %all-to-all-done.refs_0_.refs_2_.refs_1_, bf16[4,128,2048]{2,1,0:T(8,128)(2,1)} %collective-permute-done.1.refs_1_.refs_3_.refs_2_, ...), custom_call_target="tpu_custom_call" | custom-call | flops 1610612736 | bytes 8388608 | tf_op jit(solution)/shard_map/pallas_call | solution.py:97
  93.1 1.3 copy-done.24
  95.4 6.6 %shard_map.264 = (f32[2,512,512]{2,1,0:T(8,128)S(1)}, f32[512,256]{1,0:T(8,128)S(1)}, bf16[512,256]{1,0:T(8,128)(2,1)S(1)}, f32[256,2048]{1,0:T(8,128)}, bf16[256,2048]{1,0:T(8,128)(2,1)S(1)}) custom-call(bf16[512,512]{1,0:T(8,128)(2,1)S(1)} %get-tuple-element.64.refs_0_.refs_1_, f32[512,256]{1,0:T(8,128)S(1)} %get-tuple-element.65.refs_1_.refs_3_, ...), custom_call_target="tpu_custom_call" | custom-call | flops 805306368 | bytes 8388608 | tf_op jit(solution)/shard_map/pallas_call | solution.py:97
  102.4 2.3 collective-permute-done.4
  104.7 2.9 add_convert_fusion.3
  107.6 4.2 %all-to-all-start.1 = ((bf16[4,64,2048]{2,1,0:T(8,128)(2,1)}), bf16[4,64,2048]{2,1,0:T(8,128)(2,1)S(1)}, u32[]{:S(2)}, u32[]{:S(2)}) async-start(bf16[4,64,2048]{2,1,0:T(8,128)(2,1)} %bitcast.20), calls=%async_computation.1 | async-start | bytes 2097152 | tf_op jit(solution)/shard_map/all_to_all | solution.py:739
  112.7 1.6 copy-done.25
  115.6 10.8 %all-to-all-done.1.refs_0_ = bf16[4,64,2048]{2,1,0:T(8,128)(2,1)S(1)} async-done(((bf16[4,64,2048]{2,1,0:T(8,128)(2,1)}), bf16[4,64,2048]{2,1,0:T(8,128)(2,1)S(1)}, u32[]{:S(2)}, u32[]{:S(2)}) %all-to-all-start.1) | async-done | bytes 1048608 | tf_op jit(solution)/shard_map/all_to_all | solution.py:739
  128.5 15.9 %all_to_all.35 = bf16[4,64,2048]{2,1,0:T(8,128)(2,1)S(1)} all-to-all(bf16[4,64,2048]{2,1,0:T(8,128)(2,1)S(1)} %get-tuple-element.71), channel_id=1, replica_groups=mesh['shard'=16,'ctx'=4,'tp'=2] {'ctx'}, dimensions={0} | all-to-all | bytes 2097152 | tf_op jit(solution)/shard_map/all_to_all | solution.py:739
  144.4 2.6 collective-permute-start.5
  147.0 2.3 collective-permute-done.5
  149.2 1.3 shard_map.267.refs_7_.refs_0_
  150.6 1.3 copy-done.4
  154.1 10.5 %shard_map.268 = (bf16[512,768]{1,0:T(8,128)(2,1)S(1)}, bf16[512,768]{1,0:T(8,128)(2,1)S(1)}, bf16[512,768]{1,0:T(8,128)(2,1)S(1)}) custom-call(bf16[256,2048]{1,0:T(8,128)(2,1)S(1)} %bitcast.91, bf16[256,2048]{1,0:T(8,128)(2,1)S(1)} %bitcast.95, bf16[4,128,2048]{2,1,0:T(8,128)(2,1)} %all-to-all-done.refs_0_.refs_2_.refs_1_, ...), custom_call_target="tpu_custom_call" | custom-call | flops 4831838208 | bytes 8388608 | tf_op jit(solution)/shard_map/pallas_call | solution.py:97
  164.6 6.3 %shard_map.269 = (f32[256,2048]{1,0:T(8,128)S(1)}, bf16[256,2048]{1,0:T(8,128)(2,1)S(1)}) custom-call(bf16[512,768]{1,0:T(8,128)(2,1)S(1)} %get-tuple-element.73.refs_0_.refs_3_, bf16[512,768]{1,0:T(8,128)(2,1)S(1)} %get-tuple-element.74.refs_1_.refs_4_, bf16[2048,2304]{1,0:T(8,128)(2,1)} %all-gather.5.cloned.1.call-done.refs_4_.refs_5_.refs_6_.refs_2_.refs_3_.refs_1_, ...), custom_call_target="tpu_custom_call" | custom-call | flops 3221225472 | bytes 8388608 | tf_op jit(solution)/shard_map/pallas_call | solution.py:97
  171.4 2.3 collective-permute-done.7
  175.3 8.2 %shard_map.278 = bf16[2048,2304]{1,0:T(8,128)(2,1)} custom-call(bf16[2048,512]{1,0:T(8,128)(2,1)S(1)} %copy-done.5, bf16[4,128,2048]{2,1,0:T(8,128)(2,1)} %all-to-all-done.refs_0_.refs_2_.refs_1_, bf16[4,128,2048]{2,1,0:T(8,128)(2,1)} %collective-permute-done.1.refs_1_.refs_3_.refs_2_, bf16[512,768]{1,0:T(8,128)(2,1)S(1)} %get-tuple-element.73.refs_0_.refs_3_, ...), custom_call_target="tpu_custom_call" | custom-call | flops 4831838208 | bytes 8388608 | tf_op jit(solution)/shard_map/pallas_call | solution.py:97
  183.5 17.4 %all_to_all.36.refs_0_ = bf16[4,64,2048]{2,1,0:T(8,128)(2,1)S(1)} all-to-all(bf16[4,64,2048]{2,1,0:T(8,128)(2,1)S(1)} %bitcast.86), channel_id=1, replica_groups=mesh['shard'=16,'ctx'=4,'tp'=2] {'ctx'}, dimensions={0} | all-to-all | bytes 2097152 | tf_op jit(solution)/shard_map/all_to_all | solution.py:739
  201.4 16.3 %all_to_all.37 = bf16[4,64,2048]{2,1,0:T(8,128)(2,1)S(1)} all-to-all(bf16[4,64,2048]{2,1,0:T(8,128)(2,1)S(1)} %get-tuple-element.81), channel_id=1, replica_groups=mesh['shard'=16,'ctx'=4,'tp'=2] {'ctx'}, dimensions={0} | all-to-all | bytes 2097152 | tf_op jit(solution)/shard_map/all_to_all | solution.py:739
  217.7 2.1 collective-permute-start.9
  219.9 5.2 %shard_map.270 = (f32[256,2048]{1,0:T(8,128)S(1)}, bf16[256,2048]{1,0:T(8,128)(2,1)}) custom-call(bf16[512,768]{1,0:T(8,128)(2,1)S(1)} %copy-done.9, bf16[2048,2304]{1,0:T(8,128)(2,1)} %all-gather.5.cloned.1.call-done.refs_4_.refs_5_.refs_6_.refs_2_.refs_3_.refs_1_, bf16[4,64,2048]{2,1,0:T(8,128)(2,1)S(1)} %bitcast.87), custom_call_target="tpu_custom_call" | custom-call | flops 1610612736 | bytes 8388608 | tf_op jit(solution)/shard_map/pallas_call | solution.py:97
  226.7 2.1 shard_map.272
  228.8 4.8 %shard_map.273.refs_7_ = bf16[2048,512]{1,0:T(8,128)(2,1)} custom-call(bf16[2048,512]{1,0:T(8,128)(2,1)} %copy-done.2, bf16[256,2048]{1,0:T(8,128)(2,1)S(1)} %bitcast.89, bf16[256,2048]{1,0:T(8,128)(2,1)S(1)} %bitcast.93, bf16[512,256]{1,0:T(8,128)(2,1)S(1)} %get-tuple-element.86.refs_3_.refs_1_, bf16[512,256]{1,0:T(8,128)(2,1)S(1)} %copy-done.51), custom_call_target="tpu_custom_call" | custom-call | flops 1073741824 | bytes 8388608 | tf_op jit(solution)/shard_map/pallas_call | solution.py:97
  233.7 3.1 shard_map.274
  236.8 5.3 %shard_map.275 = (f32[256,2048]{1,0:T(8,128)S(1)}, bf16[256,2048]{1,0:T(8,128)(2,1)}) custom-call(bf16[512,512]{1,0:T(8,128)(2,1)S(1)} %get-tuple-element.88.refs_0_.refs_1_, bf16[512,256]{1,0:T(8,128)(2,1)S(1)} %get-tuple-element.86.refs_3_.refs_1_, bf16[2048,1152]{1,0:T(8,128)(2,1)} %bitcast.100), custom_call_target="tpu_custom_call" | custom-call | flops 1610612736 | bytes 8388608 | tf_op jit(solution)/shard_map/pallas_call | solution.py:97
  242.1 1.4 copy-done.22
  243.7 5.5 %all-to-all-start.5 = ((bf16[16,128,512]{2,1,0:T(8,128)(2,1)}), bf16[16,128,512]{2,1,0:T(8,128)(2,1)}, u32[]{:S(2)}, u32[]{:S(2)}) async-start(bf16[16,128,512]{2,1,0:T(8,128)(2,1)} %bitcast.42), calls=%async_computation.5 | async-start | bytes 4194304 | tf_op jit(solution)/shard_map/all_to_all | solution.py:761
  249.2 1.7 add_convert_fusion.1
  251.1 1.5 add_convert_fusion
  252.6 1.4 fusion.1
  254.3 1.7 collective-permute-start.12
  257.1 12.6 %collective-permute-done.11.refs_1_ = bf16[128,2048]{1,0:T(8,128)(2,1)S(1)} collective-permute-done((bf16[128,2048]{1,0:T(8,128)(2,1)}, bf16[128,2048]{1,0:T(8,128)(2,1)S(1)}, u32[]{:S(2)}, u32[]{:S(2)}) %collective-permute-start.11) | collective-permute-done | bytes 524320 | tf_op jit(solution)/shard_map/ppermute | solution.py:742
  270.5 8.6 %collective-permute-done.12.refs_2_ = bf16[128,2048]{1,0:T(8,128)(2,1)S(1)} collective-permute-done((bf16[128,2048]{1,0:T(8,128)(2,1)}, bf16[128,2048]{1,0:T(8,128)(2,1)S(1)}, u32[]{:S(2)}, u32[]{:S(2)}) %collective-permute-start.12) | collective-permute-done | bytes 524320 | tf_op jit(solution)/shard_map/ppermute | solution.py:742
  286.4 1.5 shard_map.276
  287.8 2.3 collective-permute-start.14
  290.1 1.8 slice_bitcast_fusion.5
  292.9 3.0 shard_map.277
  295.9 6.7 %all-to-all-start.6 = ((bf16[16,144,512]{2,1,0:T(8,128)(2,1)}), bf16[16,144,512]{2,1,0:T(8,128)(2,1)}, u32[]{:S(2)}, u32[]{:S(2)}) async-start(bf16[16,144,512]{2,1,0:T(8,128)(2,1)} %shard_map.277), calls=%async_computation.6 | async-start | bytes 4718592 | tf_op jit(solution)/shard_map/all_to_all | solution.py:761
  302.6 1.9 shard_map.279
  304.5 3.7 collective-permute-start.20
  309.4 2.1 collective-permute-start.16
  313.0 17.8 %collective-permute-done.20 = bf16[128,512]{1,0:T(8,128)(2,1)S(1)} collective-permute-done((bf16[128,512]{1,0:T(8,128)(2,1)S(1)}, bf16[128,512]{1,0:T(8,128)(2,1)S(1)}, u32[]{:S(2)}, u32[]{:S(2)}) %collective-permute-start.20) | collective-permute-done | bytes 131104 | tf_op jit(solution)/shard_map/ppermute | solution.py:788
  330.8 15.2 %collective-permute-done.16 = bf16[128,2304]{1,0:T(8,128)(2,1)S(1)} collective-permute-done((bf16[128,2304]{1,0:T(8,128)(2,1)}, bf16[128,2304]{1,0:T(8,128)(2,1)S(1)}, u32[]{:S(2)}, u32[]{:S(2)}) %collective-permute-start.16) | collective-permute-done | bytes 589856 | tf_op jit(solution)/shard_map/ppermute | solution.py:788
  346.2 2.3 collective-permute-start.18
  348.8 2.4 collective-permute-start.22
  352.5 11.1 %collective-permute-done.22.refs_6_.o2 = bf16[128,512]{1,0:T(8,128)(2,1)S(1)} collective-permute-done((bf16[128,512]{1,0:T(8,128)(2,1)S(1)}, bf16[128,512]{1,0:T(8,128)(2,1)S(1)}, u32[]{:S(2)}, u32[]{:S(2)}) %collective-permute-start.22) | collective-permute-done | bytes 131104 | tf_op jit(solution)/shard_map/ppermute | solution.py:742
  363.6 3.7 collective-permute-done.23.refs_7_.o3
  367.3 2.0 shard_map.280
  369.3 3.4 collective-permute-start.24
  374.1 4.4 %collective-permute-start.26 = (bf16[144,512]{1,0:T(8,128)(2,1)S(1)}, bf16[144,512]{1,0:T(8,128)(2,1)}, u32[]{:S(2)}, u32[]{:S(2)}) collective-permute-start(bf16[144,512]{1,0:T(8,128)(2,1)S(1)} %shard_map.280), channel_id=1, source_target_pairs={{0,4},{1,12},{2,6},{3,14},{4,0},{5,8},{6,2},{7,10},{8,5},{9,13},{1... | collective-permute-start | bytes 442376 | tf_op jit(solution)/shard_map/ppermute | solution.py:899
  381.6 4.1 %shard_map.282 = (f32[128,3072]{1,0:T(8,128)}, f32[128,3072]{1,0:T(8,128)}, f32[3072,128]{1,0:T(8,128)}, f32[128,128]{1,0:T(8,128)S(1)}) custom-call(s32[1]{0:T(128)} %bitcast.39.turn_at, bf16[128,2304]{1,0:T(8,128)(2,1)S(1)} %broadcast_select_fusion.1.b0, bf16[128,2304]{1,0:T(8,128)(2,1)S(1)} %collective-permute-done.17.refs_2_.b1, ...), custom_call_target="tpu_custom_call" | custom-call | flops 1048576 | bytes 8388608 | tf_op jit(solution)/shard_map/pallas_call | solution.py:686
  392.9 3.4 shard_map.281
  396.5 1.6 fusion.8
  (242 shorter events, 55.2 us)
Async XLA Ops:
  7.2 5.6 %copy-start = (bf16[3072,128]{1,0:T(8,128)(2,1)S(1)}, bf16[3072,128]{1,0:T(8,128)(2,1)}, u32[]{:S(2)}) copy-start(bf16[3072,128]{1,0:T(8,128)(2,1)} %param.30) | copy-start | bytes 2359300
  7.2 6.8 %copy-start.65 = (bf16[128]{0:T(256)(128)(2,1)S(1)}, bf16[128]{0:T(256)(128)(2,1)}, u32[]{:S(2)}) copy-start(bf16[128]{0:T(256)(128)(2,1)} %param.27) | copy-start | bytes 772
  7.2 62.8 %all-gather.3.cloned.1.call-start = ((), (), s32[]{:S(2)}) async-start(), calls=%async_computation.8 | async-start | bytes 5013504 | tf_op jit(solution)/shard_map/all_gather | solution.py:753
  12.7 140.2 %all-gather.5.cloned.1.call-start = ((), (), s32[]{:S(2)}) async-start(), calls=%async_computation.9 | async-start | bytes 10027008 | tf_op jit(solution)/shard_map/all_gather | solution.py:753
  14.0 13.3 %copy-start.61 = (bf16[128,2048]{1,0:T(8,128)(2,1)S(1)}, bf16[128,2048]{1,0:T(8,128)(2,1)}, u32[]{:S(2)}) copy-start(bf16[128,2048]{1,0:T(8,128)(2,1)} %param.31) | copy-start | bytes 1572868
  14.0 13.3 %copy-start.62 = (bf16[128,2048]{1,0:T(8,128)(2,1)S(1)}, bf16[128,2048]{1,0:T(8,128)(2,1)}, u32[]{:S(2)}) copy-start(bf16[128,2048]{1,0:T(8,128)(2,1)} %param.16) | copy-start | bytes 1572868
  14.2 12.1 %collective-permute-start.6 = (bf16[128,2304]{1,0:T(8,128)(2,1)S(1)}, bf16[128,2304]{1,0:T(8,128)(2,1)S(1)}, u32[]{:S(2)}, u32[]{:S(2)}) collective-permute-start(bf16[128,2304]{1,0:T(8,128)(2,1)S(1)} %pad_maximum_fusion.1), channel_id=1, source_target_pairs={{8,1},{1,8},{24,17},{17,24},{40,33},{33,40},{56,49},{49,56},{72,65... | collective-permute-start | bytes 1769480 | tf_op jit(solution)/shard_map/ppermute | solution.py:788
  27.5 2.0 collective-permute-start
  31.9 5.3 %copy-start.64 = (s32[1,13]{1,0:T(1,128)S(1)}, s32[1,13]{1,0:T(1,128)}, u32[]{:S(2)}) copy-start(s32[1,13]{1,0:T(1,128)} %param.17) | copy-start | bytes 160
  31.9 31.4 %all-to-all-start = ((bf16[4,128,2048]{2,1,0:T(8,128)(2,1)}), bf16[4,128,2048]{2,1,0:T(8,128)(2,1)}, u32[]{:S(2)}, u32[]{:S(2)}) async-start(bf16[4,128,2048]{2,1,0:T(8,128)(2,1)} %broadcast_in_dim.20), calls=%async_computation | async-start | bytes 4194304 | tf_op jit(solution)/shard_map/all_to_all | solution.py:739
  37.2 27.9 %collective-permute-start.2 = (s32[2,13]{1,0:T(2,128)S(1)}, s32[2,13]{1,0:T(2,128)S(1)}, u32[]{:S(2)}, u32[]{:S(2)}) collective-permute-start(s32[2,13]{1,0:T(2,128)S(1)} %pad_add_fusion.2), channel_id=1, source_target_pairs={{0,8},{8,0},{16,24},{24,16},{32,40},{40,32},{48,56},{56,48},{64,72... | collective-permute-start | bytes 320 | tf_op jit(solution)/shard_map/ppermute | solution.py:736
  63.4 5.6 %collective-permute-start.1 = (bf16[4,128,2048]{2,1,0:T(8,128)(2,1)}, bf16[4,128,2048]{2,1,0:T(8,128)(2,1)}, u32[]{:S(2)}, u32[]{:S(2)}) collective-permute-start(bf16[4,128,2048]{2,1,0:T(8,128)(2,1)} %all-to-all-done.refs_0_.refs_2_.refs_1_), channel_id=1, source_target_pairs={{0,8},{8,0},{16,24},{24,16},{32,40},{40,32},{48,56},{56,48},{64,72... | collective-permute-start | bytes 6291464 | tf_op jit(solution)/shard_map/ppermute | solution.py:736
  67.2 20.2 %copy-start.10 = (f32[512,128]{1,0:T(8,128)}, f32[512,128]{1,0:T(8,128)S(1)}, u32[]{:S(2)}) copy-start(f32[512,128]{1,0:T(8,128)S(1)} %get-tuple-element.62.refs_4_.refs_5_) | copy-start | bytes 786436
  75.0 5.2 %collective-permute-start.3 = (bf16[8,128,1152]{2,1,0:T(8,128)(2,1)}, bf16[8,128,1152]{2,1,0:T(8,128)(2,1)}, u32[]{:S(2)}, u32[]{:S(2)}) collective-permute-start(bf16[8,128,1152]{2,1,0:T(8,128)(2,1)} %get-tuple-element.113), channel_id=1, source_target_pairs={{0,8},{8,0},{16,24},{24,16},{32,40},{40,32},{48,56},{56,48},{64,72... | collective-permute-start | bytes 7077896 | tf_op jit(solution)/shard_map/ppermute | solution.py:736
  95.4 6.6 %copy-start.16 = (bf16[512,512]{1,0:T(8,128)(2,1)}, bf16[512,512]{1,0:T(8,128)(2,1)S(1)}, u32[]{:S(2)}) copy-start(bf16[512,512]{1,0:T(8,128)(2,1)S(1)} %get-tuple-element.64.refs_0_.refs_1_) | copy-start | bytes 1572868
  95.4 6.6 %copy-start.27 = (f32[512,256]{1,0:T(8,128)}, f32[512,256]{1,0:T(8,128)S(1)}, u32[]{:S(2)}) copy-start(f32[512,256]{1,0:T(8,128)S(1)} %get-tuple-element.65.refs_1_.refs_3_) | copy-start | bytes 1572868
  102.0 5.6 %copy-start.20 = (f32[2,512,512]{2,1,0:T(8,128)}, f32[2,512,512]{2,1,0:T(8,128)S(1)}, u32[]{:S(2)}) copy-start(f32[2,512,512]{2,1,0:T(8,128)S(1)} %get-tuple-element.79.refs_0_) | copy-start | bytes 6291460
  102.0 5.6 %copy-start.44 = (f32[512,256]{1,0:T(8,128)}, f32[512,256]{1,0:T(8,128)S(1)}, u32[]{:S(2)}) copy-start(f32[512,256]{1,0:T(8,128)S(1)} %get-tuple-element.82.refs_4_) | copy-start | bytes 1572868
  102.0 5.6 %copy-start.50 = (bf16[512,256]{1,0:T(8,128)(2,1)}, bf16[512,256]{1,0:T(8,128)(2,1)S(1)}, u32[]{:S(2)}) copy-start(bf16[512,256]{1,0:T(8,128)(2,1)S(1)} %get-tuple-element.87.refs_4_) | copy-start | bytes 786436
  102.0 2.7 collective-permute-start.4
  107.6 18.8 %all-to-all-start.1 = ((bf16[4,64,2048]{2,1,0:T(8,128)(2,1)}), bf16[4,64,2048]{2,1,0:T(8,128)(2,1)S(1)}, u32[]{:S(2)}, u32[]{:S(2)}) async-start(bf16[4,64,2048]{2,1,0:T(8,128)(2,1)} %bitcast.20), calls=%async_computation.1 | async-start | bytes 2097152 | tf_op jit(solution)/shard_map/all_to_all | solution.py:739
  111.9 197.5 %reduce-scatter.2.cloned.1.call-start = ((), (), s32[]{:S(2)}) async-start(), calls=%async_computation.10 | async-start | bytes 10027008 | tf_op jit(solution)/shard_map/reduce_scatter | solution.py:756
  115.6 28.7 %copy-start.2 = (bf16[2048,512]{1,0:T(8,128)(2,1)}, bf16[2048,512]{1,0:T(8,128)(2,1)S(1)}, u32[]{:S(2)}) copy-start(bf16[2048,512]{1,0:T(8,128)(2,1)S(1)} %shard_map.265.refs_2_.refs_0_) | copy-start | bytes 6291460
  144.4 4.9 %collective-permute-start.5 = (bf16[4,64,2048]{2,1,0:T(8,128)(2,1)S(1)}, bf16[4,64,2048]{2,1,0:T(8,128)(2,1)S(1)}, u32[]{:S(2)}, u32[]{:S(2)}) collective-permute-start(bf16[4,64,2048]{2,1,0:T(8,128)(2,1)S(1)} %all_to_all.35), channel_id=1, source_target_pairs={{0,8},{8,0},{16,24},{24,16},{32,40},{40,32},{48,56},{56,48},{64,72... | collective-permute-start | bytes 3145736 | tf_op jit(solution)/shard_map/ppermute | solution.py:736
  164.6 9.3 %copy-start.8 = (bf16[512,768]{1,0:T(8,128)(2,1)}, bf16[512,768]{1,0:T(8,128)(2,1)S(1)}, u32[]{:S(2)}) copy-start(bf16[512,768]{1,0:T(8,128)(2,1)S(1)} %get-tuple-element.72.refs_0_.refs_5_) | copy-start | bytes 2359300
  170.9 2.7 collective-permute-start.7
  183.4 17.4 %copy-start.15 = (f32[64,2048]{1,0:T(8,128)S(1)}, f32[64,2048]{1,0:T(8,128)}, u32[]{:S(2)}) copy-start(f32[64,2048]{1,0:T(8,128)} %copy-done.14) | copy-start | bytes 1572868
  183.5 17.4 %copy-start.31 = (bf16[64,2048]{1,0:T(8,128)(2,1)S(1)}, bf16[64,2048]{1,0:T(8,128)(2,1)}, u32[]{:S(2)}) copy-start(bf16[64,2048]{1,0:T(8,128)(2,1)} %get-tuple-element.124.refs_2_) | copy-start | bytes 786436
  200.9 19.0 %copy-start.9 = (bf16[512,768]{1,0:T(8,128)(2,1)S(1)}, bf16[512,768]{1,0:T(8,128)(2,1)}, u32[]{:S(2)}) copy-start(bf16[512,768]{1,0:T(8,128)(2,1)} %copy-done.8) | copy-start | bytes 2359300
  201.4 16.4 %copy-start.34 = (f32[64,2048]{1,0:T(8,128)}, f32[64,2048]{1,0:T(8,128)S(1)}, u32[]{:S(2)}) copy-start(f32[64,2048]{1,0:T(8,128)S(1)} %get-tuple-element.91.refs_5_) | copy-start | bytes 1572868
  217.7 8.9 %copy-start.28 = (f32[512,256]{1,0:T(8,128)S(1)}, f32[512,256]{1,0:T(8,128)}, u32[]{:S(2)}) copy-start(f32[512,256]{1,0:T(8,128)} %copy-done.27) | copy-start | bytes 1572868
  217.7 8.9 %copy-start.45 = (f32[512,256]{1,0:T(8,128)S(1)}, f32[512,256]{1,0:T(8,128)}, u32[]{:S(2)}) copy-start(f32[512,256]{1,0:T(8,128)} %copy-done.44) | copy-start | bytes 1572868
  217.7 8.9 %collective-permute-start.9 = (bf16[4,64,2048]{2,1,0:T(8,128)(2,1)S(1)}, bf16[4,64,2048]{2,1,0:T(8,128)(2,1)S(1)}, u32[]{:S(2)}, u32[]{:S(2)}) collective-permute-start(bf16[4,64,2048]{2,1,0:T(8,128)(2,1)S(1)} %all_to_all.37), channel_id=1, source_target_pairs={{0,8},{8,0},{16,24},{24,16},{32,40},{40,32},{48,56},{56,48},{64,72... | collective-permute-start | bytes 3145736 | tf_op jit(solution)/shard_map/ppermute | solution.py:736
  226.3 22.8 %collective-permute-start.8 = (bf16[256,2048]{1,0:T(8,128)(2,1)}, bf16[256,2048]{1,0:T(8,128)(2,1)}, u32[]{:S(2)}, u32[]{:S(2)}) collective-permute-start(bf16[256,2048]{1,0:T(8,128)(2,1)} %get-tuple-element.78), channel_id=1, source_target_pairs={{0,8},{8,0},{16,24},{24,16},{32,40},{40,32},{48,56},{56,48},{64,72... | collective-permute-start | bytes 3145736 | tf_op jit(solution)/shard_map/ppermute | solution.py:736
  236.8 5.3 %copy-start.36 = (bf16[512,512]{1,0:T(8,128)(2,1)}, bf16[512,512]{1,0:T(8,128)(2,1)S(1)}, u32[]{:S(2)}) copy-start(bf16[512,512]{1,0:T(8,128)(2,1)S(1)} %get-tuple-element.88.refs_0_.refs_1_) | copy-start | bytes 1572868
  243.5 7.4 %collective-permute-start.10 = (bf16[256,2048]{1,0:T(8,128)(2,1)}, bf16[256,2048]{1,0:T(8,128)(2,1)}, u32[]{:S(2)}, u32[]{:S(2)}) collective-permute-start(bf16[256,2048]{1,0:T(8,128)(2,1)} %get-tuple-element.90.refs_3_), channel_id=1, source_target_pairs={{0,8},{8,0},{16,24},{24,16},{32,40},{40,32},{48,56},{56,48},{64,72... | collective-permute-start | bytes 3145736 | tf_op jit(solution)/shard_map/ppermute | solution.py:736
  243.7 5.5 %copy-start.19 = (f32[256,2048]{1,0:T(8,128)S(1)}, f32[256,2048]{1,0:T(8,128)}, u32[]{:S(2)}) copy-start(f32[256,2048]{1,0:T(8,128)} %copy-done.18) | copy-start | bytes 6291460
  243.7 48.2 %all-to-all-start.5 = ((bf16[16,128,512]{2,1,0:T(8,128)(2,1)}), bf16[16,128,512]{2,1,0:T(8,128)(2,1)}, u32[]{:S(2)}, u32[]{:S(2)}) async-start(bf16[16,128,512]{2,1,0:T(8,128)(2,1)} %bitcast.42), calls=%async_computation.5 | async-start | bytes 4194304 | tf_op jit(solution)/shard_map/all_to_all | solution.py:761
  252.6 28.5 %copy-start.13 = (bf16[64,2048]{1,0:T(8,128)(2,1)S(1)}, bf16[64,2048]{1,0:T(8,128)(2,1)}, u32[]{:S(2)}) copy-start(bf16[64,2048]{1,0:T(8,128)(2,1)} %get-tuple-element.125.refs_1_.refs_6_) | copy-start | bytes 786436
  254.0 15.7 %collective-permute-start.11 = (bf16[128,2048]{1,0:T(8,128)(2,1)}, bf16[128,2048]{1,0:T(8,128)(2,1)S(1)}, u32[]{:S(2)}, u32[]{:S(2)}) collective-permute-start(bf16[128,2048]{1,0:T(8,128)(2,1)} %get-tuple-element.116), channel_id=1, source_target_pairs={{0,2},{2,4},{4,6},{6,0},{1,3},{3,5},{5,7},{7,1},{8,10},{10,12},{12... | collective-permute-start | bytes 1572872 | tf_op jit(solution)/shard_map/ppermute | solution.py:742
  254.3 24.7 %collective-permute-start.12 = (bf16[128,2048]{1,0:T(8,128)(2,1)}, bf16[128,2048]{1,0:T(8,128)(2,1)S(1)}, u32[]{:S(2)}, u32[]{:S(2)}) collective-permute-start(bf16[128,2048]{1,0:T(8,128)(2,1)} %get-tuple-element.117), channel_id=1, source_target_pairs={{0,4},{2,6},{4,0},{6,2},{1,5},{3,7},{5,1},{7,3},{8,12},{10,14},{12... | collective-permute-start | bytes 1572872 | tf_op jit(solution)/shard_map/ppermute | solution.py:742
  256.0 24.3 %collective-permute-start.13 = (bf16[128,2048]{1,0:T(8,128)(2,1)}, bf16[128,2048]{1,0:T(8,128)(2,1)S(1)}, u32[]{:S(2)}, u32[]{:S(2)}) collective-permute-start(bf16[128,2048]{1,0:T(8,128)(2,1)} %get-tuple-element.114), channel_id=1, source_target_pairs={{0,6},{2,0},{4,2},{6,4},{1,7},{3,1},{5,3},{7,5},{8,14},{10,8},{12,... | collective-permute-start | bytes 1572872 | tf_op jit(solution)/shard_map/ppermute | solution.py:742
  286.4 5.5 %copy-start.3 = (bf16[2048,512]{1,0:T(8,128)(2,1)S(1)}, bf16[2048,512]{1,0:T(8,128)(2,1)}, u32[]{:S(2)}) copy-start(bf16[2048,512]{1,0:T(8,128)(2,1)} %copy-done.2) | copy-start | bytes 6291460
  287.8 20.3 %collective-permute-start.14 = (bf16[128,2048]{1,0:T(8,128)(2,1)}, bf16[128,2048]{1,0:T(8,128)(2,1)}, u32[]{:S(2)}, u32[]{:S(2)}) collective-permute-start(bf16[128,2048]{1,0:T(8,128)(2,1)} %shard_map.276), channel_id=1, source_target_pairs={{0,8},{8,0},{16,24},{24,16},{32,40},{40,32},{48,56},{56,48},{64,72... | collective-permute-start | bytes 1572872 | tf_op jit(solution)/shard_map/ppermute | solution.py:736
  295.9 71.4 %all-to-all-start.6 = ((bf16[16,144,512]{2,1,0:T(8,128)(2,1)}), bf16[16,144,512]{2,1,0:T(8,128)(2,1)}, u32[]{:S(2)}, u32[]{:S(2)}) async-start(bf16[16,144,512]{2,1,0:T(8,128)(2,1)} %shard_map.277), calls=%async_computation.6 | async-start | bytes 4718592 | tf_op jit(solution)/shard_map/all_to_all | solution.py:761
  302.5 6.7 %copy-start.59 = (bf16[1,64,2048]{2,1,0:T(8,128)(2,1)S(1)}, bf16[1,64,2048]{2,1,0:T(8,128)(2,1)}, u32[]{:S(2)}) copy-start(bf16[1,64,2048]{2,1,0:T(8,128)(2,1)} %get-tuple-element.121) | copy-start | bytes 786436
  304.5 26.3 %collective-permute-start.20 = (bf16[128,512]{1,0:T(8,128)(2,1)S(1)}, bf16[128,512]{1,0:T(8,128)(2,1)S(1)}, u32[]{:S(2)}, u32[]{:S(2)}) collective-permute-start(bf16[128,512]{1,0:T(8,128)(2,1)S(1)} %shard_map.279), channel_id=1, source_target_pairs={{8,1},{1,8},{24,17},{17,24},{40,33},{33,40},{56,49},{49,56},{72,65... | collective-permute-start | bytes 393224 | tf_op jit(solution)/shard_map/ppermute | solution.py:788
  309.3 21.5 %copy-start.57 = (bf16[1,128,2048]{2,1,0:T(8,128)(2,1)}, bf16[1,128,2048]{2,1,0:T(8,128)(2,1)S(1)}, u32[]{:S(2)}) copy-start(bf16[1,128,2048]{2,1,0:T(8,128)(2,1)S(1)} %maximum_select_fusion.3) | copy-start | bytes 1572868
  309.4 36.6 %copy-start.60 = (bf16[128,2304]{1,0:T(8,128)(2,1)S(1)}, bf16[128,2304]{1,0:T(8,128)(2,1)}, u32[]{:S(2)}) copy-start(bf16[128,2304]{1,0:T(8,128)(2,1)} %reduce-scatter.2.cloned.1.call-done) | copy-start | bytes 1769476
  309.4 36.6 %collective-permute-start.16 = (bf16[128,2304]{1,0:T(8,128)(2,1)}, bf16[128,2304]{1,0:T(8,128)(2,1)S(1)}, u32[]{:S(2)}, u32[]{:S(2)}) collective-permute-start(bf16[128,2304]{1,0:T(8,128)(2,1)} %reduce-scatter.2.cloned.1.call-done), channel_id=1, source_target_pairs={{8,1},{1,8},{24,17},{17,24},{40,33},{33,40},{56,49},{49,56},{72,65... | collective-permute-start | bytes 1769480 | tf_op jit(solution)/shard_map/ppermute | solution.py:788
  311.7 39.5 %collective-permute-start.15 = (bf16[2,128,2048]{2,1,0:T(8,128)(2,1)S(1)}, bf16[2,128,2048]{2,1,0:T(8,128)(2,1)S(1)}, u32[]{:S(2)}, u32[]{:S(2)}) collective-permute-start(bf16[2,128,2048]{2,1,0:T(8,128)(2,1)S(1)} %pad_maximum_fusion), channel_id=1, source_target_pairs={{0,1},{9,8},{16,17},{25,24},{32,33},{41,40},{48,49},{57,56},{64,65... | collective-permute-start | bytes 3145736 | tf_op jit(solution)/shard_map/ppermute | solution.py:892
  330.8 18.1 %collective-permute-start.21 = (bf16[128,512]{1,0:T(8,128)(2,1)S(1)}, bf16[128,512]{1,0:T(8,128)(2,1)S(1)}, u32[]{:S(2)}, u32[]{:S(2)}) collective-permute-start(bf16[128,512]{1,0:T(8,128)(2,1)S(1)} %broadcast_select_fusion.4.o0), channel_id=1, source_target_pairs={{0,2},{2,4},{4,6},{6,0},{1,3},{3,5},{5,7},{7,1},{8,10},{10,12},{12... | collective-permute-start | bytes 393224 | tf_op jit(solution)/shard_map/ppermute | solution.py:742
  346.0 6.3 %copy-start.58 = (bf16[1,128,2048]{2,1,0:T(8,128)(2,1)S(1)}, bf16[1,128,2048]{2,1,0:T(8,128)(2,1)}, u32[]{:S(2)}) copy-start(bf16[1,128,2048]{2,1,0:T(8,128)(2,1)} %copy-done.57) | copy-start | bytes 1572868
  346.1 21.2 %collective-permute-start.17 = (bf16[128,2304]{1,0:T(8,128)(2,1)S(1)}, bf16[128,2304]{1,0:T(8,128)(2,1)S(1)}, u32[]{:S(2)}, u32[]{:S(2)}) collective-permute-start(bf16[128,2304]{1,0:T(8,128)(2,1)S(1)} %broadcast_select_fusion.1.b0), channel_id=1, source_target_pairs={{0,2},{2,4},{4,6},{6,0},{1,3},{3,5},{5,7},{7,1},{8,10},{10,12},{12... | collective-permute-start | bytes 1769480 | tf_op jit(solution)/shard_map/ppermute | solution.py:742
  346.2 21.1 %collective-permute-start.18 = (bf16[128,2304]{1,0:T(8,128)(2,1)S(1)}, bf16[128,2304]{1,0:T(8,128)(2,1)S(1)}, u32[]{:S(2)}, u32[]{:S(2)}) collective-permute-start(bf16[128,2304]{1,0:T(8,128)(2,1)S(1)} %broadcast_select_fusion.1.b0), channel_id=1, source_target_pairs={{0,4},{2,6},{4,0},{6,2},{1,5},{3,7},{5,1},{7,3},{8,12},{10,14},{12... | collective-permute-start | bytes 1769480 | tf_op jit(solution)/shard_map/ppermute | solution.py:742
  348.5 18.8 %collective-permute-start.19 = (bf16[128,2304]{1,0:T(8,128)(2,1)S(1)}, bf16[128,2304]{1,0:T(8,128)(2,1)}, u32[]{:S(2)}, u32[]{:S(2)}) collective-permute-start(bf16[128,2304]{1,0:T(8,128)(2,1)S(1)} %broadcast_select_fusion.1.b0), channel_id=1, source_target_pairs={{0,6},{2,0},{4,2},{6,4},{1,7},{3,1},{5,3},{7,5},{8,14},{10,8},{12,... | collective-permute-start | bytes 1769480 | tf_op jit(solution)/shard_map/ppermute | solution.py:742
  348.8 14.7 %collective-permute-start.22 = (bf16[128,512]{1,0:T(8,128)(2,1)S(1)}, bf16[128,512]{1,0:T(8,128)(2,1)S(1)}, u32[]{:S(2)}, u32[]{:S(2)}) collective-permute-start(bf16[128,512]{1,0:T(8,128)(2,1)S(1)} %broadcast_select_fusion.4.o0), channel_id=1, source_target_pairs={{0,4},{2,6},{4,0},{6,2},{1,5},{3,7},{5,1},{7,3},{8,12},{10,14},{12... | collective-permute-start | bytes 393224 | tf_op jit(solution)/shard_map/ppermute | solution.py:742
  351.2 16.0 %collective-permute-start.23 = (bf16[128,512]{1,0:T(8,128)(2,1)S(1)}, bf16[128,512]{1,0:T(8,128)(2,1)S(1)}, u32[]{:S(2)}, u32[]{:S(2)}) collective-permute-start(bf16[128,512]{1,0:T(8,128)(2,1)S(1)} %broadcast_select_fusion.4.o0), channel_id=1, source_target_pairs={{0,6},{2,0},{4,2},{6,4},{1,7},{3,1},{5,3},{7,5},{8,14},{10,8},{12,... | collective-permute-start | bytes 393224 | tf_op jit(solution)/shard_map/ppermute | solution.py:742
  369.3 18.1 %collective-permute-start.24 = (bf16[144,512]{1,0:T(8,128)(2,1)S(1)}, bf16[144,512]{1,0:T(8,128)(2,1)}, u32[]{:S(2)}, u32[]{:S(2)}) collective-permute-start(bf16[144,512]{1,0:T(8,128)(2,1)S(1)} %shard_map.280), channel_id=1, source_target_pairs={{1,8},{3,10},{5,12},{7,14},{8,1},{10,3},{12,5},{14,7},{17,24},{19,... | collective-permute-start | bytes 442376 | tf_op jit(solution)/shard_map/ppermute | solution.py:899
  374.1 14.2 %collective-permute-start.25 = (bf16[144,512]{1,0:T(8,128)(2,1)S(1)}, bf16[144,512]{1,0:T(8,128)(2,1)}, u32[]{:S(2)}, u32[]{:S(2)}) collective-permute-start(bf16[144,512]{1,0:T(8,128)(2,1)S(1)} %shard_map.280), channel_id=1, source_target_pairs={{0,2},{1,10},{2,4},{3,12},{4,6},{5,14},{6,0},{7,8},{8,3},{9,11},{1... | collective-permute-start | bytes 442376 | tf_op jit(solution)/shard_map/ppermute | solution.py:899
  374.1 14.2 %collective-permute-start.26 = (bf16[144,512]{1,0:T(8,128)(2,1)S(1)}, bf16[144,512]{1,0:T(8,128)(2,1)}, u32[]{:S(2)}, u32[]{:S(2)}) collective-permute-start(bf16[144,512]{1,0:T(8,128)(2,1)S(1)} %shard_map.280), channel_id=1, source_target_pairs={{0,4},{1,12},{2,6},{3,14},{4,0},{5,8},{6,2},{7,10},{8,5},{9,13},{1... | collective-permute-start | bytes 442376 | tf_op jit(solution)/shard_map/ppermute | solution.py:899
  378.5 9.8 %collective-permute-start.27 = (bf16[144,512]{1,0:T(8,128)(2,1)S(1)}, bf16[144,512]{1,0:T(8,128)(2,1)}, u32[]{:S(2)}, u32[]{:S(2)}) collective-permute-start(bf16[144,512]{1,0:T(8,128)(2,1)S(1)} %shard_map.280), channel_id=1, source_target_pairs={{0,6},{1,14},{2,0},{3,8},{4,2},{5,10},{6,4},{7,12},{8,7},{9,15},{1... | collective-permute-start | bytes 442376 | tf_op jit(solution)/shard_map/ppermute | solution.py:899
  392.8 7.2 %copy-start.1 = (bf16[3072,128]{1,0:T(8,128)(2,1)S(1)}, bf16[3072,128]{1,0:T(8,128)(2,1)}, u32[]{:S(2)}) copy-start(bf16[3072,128]{1,0:T(8,128)(2,1)} %param.30) | copy-start | bytes 2359300
  396.4 2.5 collective-permute-start.28
  (38 other events, 64.2 us)
Sparse Core Ops, SparseCore 0:
  12.8 57.0 all-gather.2
  72.7 75.2 all-gather.4
  183.6 106.1 reduce-scatter.1

commit v5 on v4

--- a/solution.py
+++ b/solution.py
@@ -285,7 +285,7 @@
     other[...] = out[half:, :].astype(BF16)
 
 
-def feed_back(d_gate, d_up, w):
+def feed_back(d_gate, d_up, w, behind):
     length, units = d_gate.shape
     half, width = length // 2, w.shape[0]
     chunk = 4 * HD
@@ -301,6 +301,7 @@
         [slab, slab],
         [struct((half, width), F32), struct((half, width), BF16)],
         2 * length * width * units * 2,
+        behind=behind,
     )(d_gate, d_up, w, w)
 
 
@@ -469,7 +470,7 @@
         other[...] = out.astype(BF16)
 
 
-def input_back(d_qkv, d_gate, w):
+def input_back(d_qkv, d_gate, w, behind):
     length = d_qkv.shape[0]
     half, width = length // 2, w.shape[0]
     return call(
@@ -479,55 +480,49 @@
         [fixed((half, width)), fixed((half, width))],
         [struct((half, width), F32), struct((half, width), BF16)],
         2 * length * width * 6 * HD,
+        behind=behind,
     )(d_qkv, d_gate, w)
 
 
-def outer_grads_kernel(x_flip, da, db, d_gate, gated, out):
-    split = d_gate.shape[1]
-    out[:, :split] = dot(x_flip[...], d_gate[...]).astype(BF16)
-    spread_blocks(gated, jnp.concatenate([da[...], db[...]], axis=0), out, split)
-
-
-def outer_grads(x_flip, da, db, d_gate, gated):
-    half, width = da.shape
-    chunk = 4 * HD
-    slab = pl.BlockSpec((half, chunk), lambda i: (0, i))
-    return call(
-        outer_grads_kernel,
-        (width // chunk,),
-        [rowed(chunk, 2 * half), slab, slab] + [fixed((2 * half, 2 * HD))] * 2,
-        rowed(chunk, 4 * HD),
-        struct((width, 4 * HD), BF16),
-        2 * 2 * half * width * 4 * HD,
-    )(x_flip, da, db, d_gate, gated)
-
-
-def inner_grads_kernel(x_flip, d_qkv, terms, out):
+def attend_grads_kernel(x_flip, da, db, d_qkv, d_gate, gated, terms, out, outer):
+    inner, split = d_qkv.shape[1], d_gate.shape[1]
+    block = out.shape[1] - terms.shape[1]
+    for number in range(out.shape[0]):
+        out[number, block:, :] = terms[number].astype(BF16)
     term = dot(x_flip[...], d_qkv[...]).astype(BF16)
-    count, block = out.shape[0], out.shape[1] - terms.shape[1]
-    for number in range(count):
-        out[number, :block] = term[number * block : (number + 1) * block]
-        out[number, block:] = terms[number].astype(BF16)
-
-
-def inner_grads(x_flip, d_qkv, terms, behind):
+    gates = dot(x_flip[...], d_gate[...]).astype(BF16)
+    spread_blocks(gated, jnp.concatenate([da[...], db[...]], axis=0), outer, 0)
+    for number in range(out.shape[0]):
+        rows = slice(number * block, (number + 1) * block)
+        out[number, :block, :inner] = term[rows]
+        out[number, :block, inner : inner + split] = gates[rows]
+        out[number, :block, inner + split :] = outer[rows, :]
+
+
+def attend_grads(x_flip, da, db, d_qkv, d_gate, gated, terms, behind):
     width, length = x_flip.shape
-    columns, extra = d_qkv.shape[1], terms.shape[1]
-    owners = terms.shape[0]
+    owners, extra, columns = terms.shape
     block = width // owners
-    return call(
-        inner_grads_kernel,
-        (owners // 4,),
+    many = 4
+    slab = pl.BlockSpec((length // 2, many * block), lambda i: (0, i))
+    return call(
+        attend_grads_kernel,
+        (owners // many,),
         [
-            rowed(4 * block, length),
-            fixed((length, columns)),
-            pl.BlockSpec((4, extra, columns), lambda i: (i, 0, 0)),
+            rowed(many * block, length),
+            slab,
+            slab,
+            fixed(d_qkv.shape),
+            fixed(d_gate.shape),
+            fixed(gated.shape),
+            pl.BlockSpec((many, extra, columns), lambda i: (i, 0, 0)),
         ],
-        pl.BlockSpec((4, block + extra, columns), lambda i: (i, 0, 0)),
+        pl.BlockSpec((many, block + extra, columns), lambda i: (i, 0, 0)),
         struct((owners, block + extra, columns), BF16),
         2 * length * width * columns,
+        scratch=[pltpu.VMEM((many * block, gated.shape[1]), BF16)],
         behind=behind,
-    )(x_flip, d_qkv, terms)
+    )(x_flip, da, db, d_qkv, d_gate, gated, terms)
 
 
 def middle_kernel(parts, x, middle, spread):
@@ -611,6 +606,54 @@
         1 << 20,
         behind=behind,
     )(parts)
+
+
+def prefetched(kernel, grid, in_specs, out_specs, out_shape):
+    return pl.pallas_call(
+        kernel,
+        grid_spec=pltpu.PrefetchScalarGridSpec(
+            num_scalar_prefetch=1, grid=grid, in_specs=in_specs, out_specs=out_specs
+        ),
+        out_shape=out_shape,
+        compiler_params=pltpu.CompilerParams(
+            dimension_semantics=("arbitrary",) * len(grid), vmem_limit_bytes=VMEM
+        ),
+        cost_estimate=pl.CostEstimate(flops=1 << 20, bytes_accessed=8 << 20, transcendentals=0),
+    )
+
+
+def copy_kernel(core, source, out):
+    out[...] = source[...]
+
+
+def sibling_part(core, found):
+    pairs, _, rows, columns = found.shape
+    return prefetched(
+        copy_kernel,
+        (pairs // 2,),
+        [pl.BlockSpec((2, None, rows, columns), lambda i, at: (i, 1 - at[0], 0, 0))],
+        pl.BlockSpec((2, rows, columns), lambda i, at: (i, 0, 0)),
+        struct((pairs, rows, columns), found.dtype),
+    )(core, found)
+
+
+def join_kernel(core, mine, other, out):
+    out[:, core[0]] = mine[...]
+    out[:, 1 - core[0]] = other[...]
+
+
+def join_cores(core, found, other):
+    pairs, _, rows, columns = found.shape
+    return prefetched(
+        join_kernel,
+        (pairs // 2,),
+        [
+            pl.BlockSpec((2, None, rows, columns), lambda i, at: (i, at[0], 0, 0)),
+            pl.BlockSpec((2, rows, columns), lambda i, at: (i, 0, 0)),
+        ],
+        pl.BlockSpec((2, 2, rows, columns), lambda i, at: (i, 0, 0, 0)),
+        struct(found.shape, found.dtype),
+    )(core, found, other)
 
 
 def lanes(value):
@@ -645,11 +688,12 @@
 
 
 def close_attend_kernel(
-    turn_at, i0, i1, i2, i3, o0, o1, o2, o3, wq, wk, wv, wg, gain, gq, gk, gv, gg, go, sums, ends
+    turn_at, b0, b1, b2, b3, wq, wk, wv, wg, gain, gq, gk, gv, gg, go, sums, ends
 ):
-    inner, outer = pick((i0, i1, i2, i3)), pick((o0, o1, o2, o3))
-    block = outer.shape[0]
-    scale = gain[...]
+    found = pick((b0, b1, b2, b3))
+    inner, scale = found[:, : 4 * HD], gain[...]
+    block = scale.shape[0]
+    outer = found[:block, 4 * HD :]
     raw_q, raw_k, raw_v = inner[:block, : 2 * HD], inner[:block, head(2)], inner[:block, head(3)]
     raw_g = outer[:, : 2 * HD]
     gq[...], gk[...], gv[...], gg[...] = raw_q * scale, raw_k * scale, raw_v * scale, raw_g * scale
@@ -683,17 +727,9 @@
     out_specs += [pl.BlockSpec(shape, lambda i, at: (0, 0)) for shape in extra]
     out_shape = [struct(w.shape, F32) for w in weights] + [struct(out_rows, F32)]
     out_shape += [struct(shape, F32) for shape in extra]
-    return pl.pallas_call(
-        kernel,
-        grid_spec=pltpu.PrefetchScalarGridSpec(
-            num_scalar_prefetch=1, grid=(quarters,), in_specs=in_specs, out_specs=out_specs
-        ),
-        out_shape=out_shape,
-        compiler_params=pltpu.CompilerParams(
-            dimension_semantics=("arbitrary",), vmem_limit_bytes=VMEM
-        ),
-        cost_estimate=pl.CostEstimate(flops=1 << 20, bytes_accessed=8 << 20, transcendentals=0),
-    )(turn_at, *blocks, *weights, gain)
+    return prefetched(kernel, (quarters,), in_specs, out_specs, out_shape)(
+        turn_at, *blocks, *weights, gain
+    )
 
 
 def make_shards(mesh):
@@ -836,11 +872,9 @@
             (found, xa, xb, of_row, of_column, cosine, sine)
         )
         found = found.reshape(pairs, n_tp, gain_in.shape[0], -1)
-        mine = lax.dynamic_index_in_dim(found, core, 1, False)
-        other = core_swap(lax.dynamic_index_in_dim(found, 1 - core, 1, False))
-        w1 = jnp.where(
-            core == 0, jnp.stack([mine, other], axis=1), jnp.stack([other, mine], axis=1)
-        ).reshape(-1, first.shape[1])
+        core_at = core.astype(jnp.int32).reshape(1)
+        other = core_swap(sibling_part(core_at, found))
+        w1 = join_cores(core_at, found, other).reshape(-1, first.shape[1])
 
         xn, pre, low, gate, gains = project(xa, xb, w1, cosine, sine)
         probs, attended, gated, mine, other = attend(low, gate, w1, of_row, of_column)
@@ -850,25 +884,24 @@
         u_flip = flip(ua, ub)
 
         hidden, d_gate, d_up = feed(ua, ub, xa, xb, w2, (u_flip,))
-        half = tree_half(*feed_back(d_gate, d_up, w2))
-        ffn = feed_grads(u_flip, xa, xb, d_gate, d_up, hidden, (half,))
+        ffn = feed_grads(u_flip, xa, xb, d_gate, d_up, hidden, ())
+        half = tree_half(*feed_back(d_gate, d_up, w2, (ffn,)))
         d_middle, spread = d_middle_step(ctx_exchange(half), middle, own_cot)
         da, db = (flat(v) for v in tree_rows(spread))
         grad_ffn = plane_scatter(ffn)
         layer_mine, layer_other = down_product(hidden, w2, 2, (half,))
 
         d_attended, d_gate_pre = gate_back(da, db, w1, gate, attended)
-        outer = outer_grads(x_flip, da, db, d_gate_pre, gated)
-        outer_parts = plane_exchange(outer.reshape(n_shard, -1, 4 * HD))
-        d_qkv, terms = attend_back(probs, low, d_attended, pre, gains, cosine, sine, (outer,))
-        in_mine, in_other = input_back(d_qkv, d_gate_pre, w1)
+        d_qkv, terms = attend_back(probs, low, d_attended, pre, gains, cosine, sine, ())
 
         def spread_terms(vector):
             return jnp.pad(vector.reshape(n_shard, 1, -1), ((0, 0), (0, 15), (0, 0)))
 
         wide_terms = jnp.concatenate([spread_terms(terms[0]), spread_terms(terms[1])], axis=2)
-        wide_terms = jnp.pad(wide_terms, ((0, 0), (0, 0), (0, 4 * HD - 2 * head_rows)))
-        inner_parts = plane_exchange(inner_grads(x_flip, d_qkv, wide_terms, (in_other, outer_parts)))
+        wide_terms = jnp.pad(wide_terms, ((0, 0), (0, 0), (0, 8 * HD - 2 * head_rows)))
+        attn = attend_grads(x_flip, da, db, d_qkv, d_gate_pre, gated, wide_terms, ())
+        attn_parts = plane_exchange(attn)
+        in_mine, in_other = input_back(d_qkv, d_gate_pre, w1, (attn,))
 
         both = jnp.concatenate(
             [tree_half(layer_mine, layer_other), tree_half(in_mine, in_other)], axis=1
@@ -901,11 +934,7 @@
 
         turn_at = ctx.astype(jnp.int32).reshape(1)
         size = gain_in.shape[0]
-        outer_blocks = owners(sum_step(outer_parts, ()))
         ffn_blocks = owners(grad_ffn)
-        inner_blocks = owners_at_once(
-            sum_step(inner_parts, (full, *ffn_blocks[1:], *outer_blocks[1:]))
-        )
         grad_gate, grad_up, grad_down, mid_sums = close(
             close_feed_kernel,
             turn_at,
@@ -915,10 +944,11 @@
             w_down.shape,
             [(size, HD)],
         )
+        attn_blocks = owners_at_once(sum_step(attn_parts, (full, mid_sums)))
         grad_query, grad_key, grad_value, grad_gate_attn, grad_out, in_sums, head_ends = close(
             close_attend_kernel,
             turn_at,
-            inner_blocks + outer_blocks,
+            attn_blocks,
             (w_query, w_key, w_value, w_gate_attn),
             gain_one,
             w_out.shape,

time: 411 us -> 390 us (0.949)
  the two profiles are of different devices: /device:TPU:1 before, /device:TPU:12 now
where the time goes in v5:
time: 390 us; the launch traced here: 388 us
  waiting for transfers between devices  148 us (38%)
  Pallas kernels  80.7 us (21%)
  blocking collectives  53.4 us (14%)
  starting transfers between devices  47.4 us (12%)
  local copies, waits for them, and re-layouts  26.3 us (7%)
  other arithmetic  17.1 us (4%)
  between operations  14.7 us (4%)
    pallas_call x16, Pallas kernels, call(): return lambda *operands: built(*operands, *behind)  66.4 us
    all_to_all x3, blocking collectives, ctx_exchange(): return lax.all_to_all(value, 'ctx', 0, 0)  53.4 us
    ppermute x2, waiting for transfers between devices, swapped(): return jnp.where(native, value, lax.ppermute(value, PLANE, swap_perm))  40.4 us
    all_to_all x2, waiting for transfers between devices, ctx_exchange(): return lax.all_to_all(value, 'ctx', 0, 0)  37.5 us
    ppermute x6, waiting for transfers between devices, ctx_turn(): lax.ppermute(value, 'ctx', [(i, (i + by) % n_ctx) for i in range(n_ctx)])  35.7 us
    ppermute x11, waiting for transfers between devices, core_swap(): return lax.ppermute(value, 'shard', core_perm)  17.9 us
    unnamed x115, local copies, waits for them, and re-layouts  17.5 us
    ppermute x4, waiting for transfers between devices, owners_at_once(): lax.ppermute(block, ('shard', 'ctx', 'tp'), perm)  13.9 us
  transfers between devices with their start and end apart: 31, of which 21 were waited for; matrix products, arithmetic and copies ran while one was open for 5% of the time, Pallas kernels for 15%

profile of v5, /device:TPU:12, one launch (start us, length us, event | category | flops | bytes accessed | tf_op | source)
XLA Modules:
  0.0 388.0 jit_solution(530086711722807421)
XLA Ops:
  14.2 2.1 collective-permute-start.6
  16.3 9.3 %collective-permute-done.6 = bf16[128,2304]{1,0:T(8,128)(2,1)S(1)} collective-permute-done((bf16[128,2304]{1,0:T(8,128)(2,1)S(1)}, bf16[128,2304]{1,0:T(8,128)(2,1)S(1)}, u32[]{:S(2)}, u32[]{:S(2)}) %collective-permute-start.6) | collective-permute-done | bytes 589856 | tf_op jit(solution)/shard_map/ppermute | solution.py:824
  26.8 1.9 collective-permute-done
  29.6 1.6 broadcast_in_dim.20
  31.2 5.4 %all-to-all-start = ((bf16[4,128,2048]{2,1,0:T(8,128)(2,1)}), bf16[4,128,2048]{2,1,0:T(8,128)(2,1)S(1)}, u32[]{:S(2)}, u32[]{:S(2)}) async-start(bf16[4,128,2048]{2,1,0:T(8,128)(2,1)} %broadcast_in_dim.20), calls=%async_computation | async-start | bytes 4194304 | tf_op jit(solution)/shard_map/all_to_all | solution.py:775
  36.9 26.4 %all-to-all-done.refs_0_.refs_2_.refs_1_ = bf16[4,128,2048]{2,1,0:T(8,128)(2,1)S(1)} async-done(((bf16[4,128,2048]{2,1,0:T(8,128)(2,1)}), bf16[4,128,2048]{2,1,0:T(8,128)(2,1)S(1)}, u32[]{:S(2)}, u32[]{:S(2)}) %all-to-all-start) | async-done | bytes 2097184 | tf_op jit(solution)/shard_map/all_to_all | solution.py:775
  64.6 1.1 fusion.10
  65.8 1.8 collective-permute-done.1.refs_1_.refs_3_.refs_2_
  67.8 2.5 shard_map.263
  70.5 4.5 %collective-permute-done.3.other = bf16[8,128,1152]{2,1,0:T(8,128)(2,1)} collective-permute-done((bf16[8,128,1152]{2,1,0:T(8,128)(2,1)S(1)}, bf16[8,128,1152]{2,1,0:T(8,128)(2,1)}, u32[]{:S(2)}, u32[]{:S(2)}) %collective-permute-start.3) | collective-permute-done | bytes 2359328 | tf_op jit(solution)/shard_map/ppermute | solution.py:772
  75.0 5.0 %shard_map.264 = bf16[8,2,128,1152]{3,2,1,0:T(8,128)(2,1)} custom-call(s32[1]{0:T(128)} %bitcast.16.core, bf16[8,2,128,1152]{3,2,1,0:T(8,128)(2,1)} %bitcast.98, bf16[8,128,1152]{2,1,0:T(8,128)(2,1)} %collective-permute-done.3.other), custom_call_target="tpu_custom_call" | custom-call | flops 1048576 | bytes 8388608 | tf_op jit(solution)/shard_map/pallas_call | solution.py:647
  80.0 5.9 %shard_map.265 = (bf16[512,2048]{1,0:T(8,128)(2,1)S(1)}, f32[512,384]{1,0:T(8,128)S(1)}, bf16[512,512]{1,0:T(8,128)(2,1)S(1)}, f32[512,256]{1,0:T(8,128)S(1)}, f32[16,128]{1,0:T(8,128)S(1)}) custom-call(bf16[4,128,2048]{2,1,0:T(8,128)(2,1)} %copy-done.45, bf16[4,128,2048]{2,1,0:T(8,128)(2,1)} %collective-permute-done.1.refs_1_.refs_3_.refs_2_, ...), custom_call_target="tpu_custom_call" | custom-call | flops 1610612736 | bytes 8388608 | tf_op jit(solution)/shard_map/pallas_call | solution.py:97
  86.0 1.3 copy-done.21
  87.3 6.9 %shard_map.266 = (f32[2,512,512]{2,1,0:T(8,128)S(1)}, f32[512,256]{1,0:T(8,128)S(1)}, bf16[512,256]{1,0:T(8,128)(2,1)S(1)}, f32[256,2048]{1,0:T(8,128)}, bf16[256,2048]{1,0:T(8,128)(2,1)S(1)}) custom-call(bf16[512,512]{1,0:T(8,128)(2,1)S(1)} %get-tuple-element.64.refs_0_.refs_1_, f32[512,256]{1,0:T(8,128)S(1)} %get-tuple-element.65.refs_1_.refs_3_, ...), custom_call_target="tpu_custom_call" | custom-call | flops 805306368 | bytes 8388608 | tf_op jit(solution)/shard_map/pallas_call | solution.py:97
  94.4 2.5 collective-permute-done.4
  96.9 2.9 add_convert_fusion.3
  99.8 4.5 %all-to-all-start.1 = ((bf16[4,64,2048]{2,1,0:T(8,128)(2,1)}), bf16[4,64,2048]{2,1,0:T(8,128)(2,1)S(1)}, u32[]{:S(2)}, u32[]{:S(2)}) async-start(bf16[4,64,2048]{2,1,0:T(8,128)(2,1)} %bitcast.19), calls=%async_computation.1 | async-start | bytes 2097152 | tf_op jit(solution)/shard_map/all_to_all | solution.py:775
  105.2 2.2 copy-done.22
  107.4 1.3 shard_map.267.refs_2_.refs_0_
  108.8 11.0 %all-to-all-done.1.refs_0_ = bf16[4,64,2048]{2,1,0:T(8,128)(2,1)S(1)} async-done(((bf16[4,64,2048]{2,1,0:T(8,128)(2,1)}), bf16[4,64,2048]{2,1,0:T(8,128)(2,1)S(1)}, u32[]{:S(2)}, u32[]{:S(2)}) %all-to-all-start.1) | async-done | bytes 1048608 | tf_op jit(solution)/shard_map/all_to_all | solution.py:775
  121.9 17.0 %all_to_all.30 = bf16[4,64,2048]{2,1,0:T(8,128)(2,1)S(1)} all-to-all(bf16[4,64,2048]{2,1,0:T(8,128)(2,1)S(1)} %get-tuple-element.71), channel_id=1, replica_groups=mesh['shard'=16,'ctx'=4,'tp'=2] {'ctx'}, dimensions={0} | all-to-all | bytes 2097152 | tf_op jit(solution)/shard_map/all_to_all | solution.py:775
  138.8 2.7 collective-permute-done.5
  141.5 1.3 shard_map.269.refs_7_.refs_0_
  142.9 1.3 copy-done.2
  145.9 1.2 copy-done.6
  147.1 10.6 %shard_map.270 = (bf16[512,768]{1,0:T(8,128)(2,1)S(1)}, bf16[512,768]{1,0:T(8,128)(2,1)S(1)}, bf16[512,768]{1,0:T(8,128)(2,1)S(1)}) custom-call(bf16[256,2048]{1,0:T(8,128)(2,1)S(1)} %bitcast.83, bf16[256,2048]{1,0:T(8,128)(2,1)S(1)} %bitcast.89, bf16[4,128,2048]{2,1,0:T(8,128)(2,1)} %copy-done.45, ...), custom_call_target="tpu_custom_call" | custom-call | flops 4831838208 | bytes 8388608 | tf_op jit(solution)/shard_map/pallas_call | solution.py:97
  157.7 8.1 %shard_map.271.refs_4_ = bf16[2048,2304]{1,0:T(8,128)(2,1)} custom-call(bf16[2048,512]{1,0:T(8,128)(2,1)S(1)} %copy-done.3, bf16[4,128,2048]{2,1,0:T(8,128)(2,1)} %copy-done.45, bf16[4,128,2048]{2,1,0:T(8,128)(2,1)} %collective-permute-done.1.refs_1_.refs_3_.refs_2_, bf16[512,768]{1,0:T(8,128)(2,1)S(1)} %get-tuple-element.73.refs_3_.refs_0_, ...), custom_call_target="tpu_custom_call" | custom-call | flops 4831838208 | bytes 8388608 | tf_op jit(solution)/shard_map/pallas_call | solution.py:97
  166.8 6.0 %shard_map.272 = (f32[256,2048]{1,0:T(8,128)S(1)}, bf16[256,2048]{1,0:T(8,128)(2,1)S(1)}) custom-call(bf16[512,768]{1,0:T(8,128)(2,1)S(1)} %get-tuple-element.73.refs_3_.refs_0_, bf16[512,768]{1,0:T(8,128)(2,1)S(1)} %get-tuple-element.74.refs_4_.refs_1_, bf16[2048,2304]{1,0:T(8,128)(2,1)} %all-gather.5.cloned.1.call-done.refs_4_.refs_5_.refs_6_.refs_2_.refs_3_.refs_1_, ...), custom_call_target="tpu_custom_call" | custom-call | flops 3221225472 | bytes 8388608 | tf_op jit(solution)/shard_map/pallas_call | solution.py:97
  172.9 2.6 collective-permute-done.7
  175.8 19.7 %all_to_all.31.refs_0_ = bf16[4,64,2048]{2,1,0:T(8,128)(2,1)S(1)} all-to-all(bf16[4,64,2048]{2,1,0:T(8,128)(2,1)S(1)} %bitcast.86), channel_id=1, replica_groups=mesh['shard'=16,'ctx'=4,'tp'=2] {'ctx'}, dimensions={0} | all-to-all | bytes 2097152 | tf_op jit(solution)/shard_map/all_to_all | solution.py:775
  196.1 16.7 %all_to_all.32 = bf16[4,64,2048]{2,1,0:T(8,128)(2,1)S(1)} all-to-all(bf16[4,64,2048]{2,1,0:T(8,128)(2,1)S(1)} %get-tuple-element.81), channel_id=1, replica_groups=mesh['shard'=16,'ctx'=4,'tp'=2] {'ctx'}, dimensions={0} | all-to-all | bytes 2097152 | tf_op jit(solution)/shard_map/all_to_all | solution.py:775
  212.8 5.3 %shard_map.273 = (f32[256,2048]{1,0:T(8,128)S(1)}, bf16[256,2048]{1,0:T(8,128)(2,1)}) custom-call(bf16[512,768]{1,0:T(8,128)(2,1)S(1)} %copy-done.8, bf16[2048,2304]{1,0:T(8,128)(2,1)} %all-gather.5.cloned.1.call-done.refs_4_.refs_5_.refs_6_.refs_2_.refs_3_.refs_1_, bf16[4,64,2048]{2,1,0:T(8,128)(2,1)S(1)} %bitcast.87), custom_call_target="tpu_custom_call" | custom-call | flops 1610612736 | bytes 8388608 | tf_op jit(solution)/shard_map/pallas_call | solution.py:97
  218.1 1.4 copy-done.15
  219.8 2.1 shard_map.275
  222.2 3.1 shard_map.276
  228.6 5.9 %shard_map.277.refs_3_ = bf16[16,144,1024]{2,1,0:T(8,128)(2,1)} custom-call(bf16[2048,512]{1,0:T(8,128)(2,1)} %copy-done.4, bf16[256,2048]{1,0:T(8,128)(2,1)S(1)} %bitcast.85, bf16[256,2048]{1,0:T(8,128)(2,1)S(1)} %bitcast.91, bf16[512,512]{1,0:T(8,128)(2,1)S(1)} %copy-done.28, bf16[512,256]{1,0:T(8,128)(2,1)S(1)} %get-tuple-element.87.refs_4_.refs_1_, ...), custom_call_target="tpu_custom_call" | custom-call | flops 2147483648 | bytes 8388608 | tf_op jit(solution)/shard_map/pallas_call | solution.py:97
  234.5 5.2 %shard_map.278 = (f32[256,2048]{1,0:T(8,128)S(1)}, bf16[256,2048]{1,0:T(8,128)(2,1)}) custom-call(bf16[512,512]{1,0:T(8,128)(2,1)S(1)} %copy-done.29, bf16[512,256]{1,0:T(8,128)(2,1)S(1)} %get-tuple-element.87.refs_4_.refs_1_, bf16[2048,1152]{1,0:T(8,128)(2,1)} %bitcast.96, bf16[16,144,1024]{2,1,0:T(8,128)(2,1)} %shard_map.277.refs_3_), custom_call_target="tpu_custom_call" | custom-call | flops 1610612736 | bytes 8388608 | tf_op jit(solution)/shard_map/pallas_call | solution.py:97
  239.7 1.4 copy-done.19
  241.3 2.5 add_convert_fusion.1
  243.7 7.1 %all-to-all-start.5 = ((bf16[16,144,1024]{2,1,0:T(8,128)(2,1)}), bf16[16,144,1024]{2,1,0:T(8,128)(2,1)}, u32[]{:S(2)}, u32[]{:S(2)}) async-start(bf16[16,144,1024]{2,1,0:T(8,128)(2,1)} %shard_map.277.refs_3_), calls=%async_computation.5 | async-start | bytes 9437184 | tf_op jit(solution)/shard_map/all_to_all | solution.py:797
  250.9 1.6 add_convert_fusion
  253.3 2.1 collective-permute-start.12
  256.4 22.5 %collective-permute-done.11.refs_1_ = bf16[128,2048]{1,0:T(8,128)(2,1)S(1)} collective-permute-done((bf16[128,2048]{1,0:T(8,128)(2,1)S(1)}, bf16[128,2048]{1,0:T(8,128)(2,1)S(1)}, u32[]{:S(2)}, u32[]{:S(2)}) %collective-permute-start.11) | collective-permute-done | bytes 524320 | tf_op jit(solution)/shard_map/ppermute | solution.py:778
  280.4 1.8 collective-permute-done.14
  282.4 2.3 collective-permute-start.16
  285.0 1.4 collective-permute-start.15
  286.5 31.2 %collective-permute-done.16 = bf16[128,2304]{1,0:T(8,128)(2,1)S(1)} collective-permute-done((bf16[128,2304]{1,0:T(8,128)(2,1)}, bf16[128,2304]{1,0:T(8,128)(2,1)S(1)}, u32[]{:S(2)}, u32[]{:S(2)}) %collective-permute-start.16) | collective-permute-done | bytes 589856 | tf_op jit(solution)/shard_map/ppermute | solution.py:824
  317.7 4.7 %collective-permute-start.17 = (bf16[128,2304]{1,0:T(8,128)(2,1)S(1)}, bf16[128,2304]{1,0:T(8,128)(2,1)}, u32[]{:S(2)}, u32[]{:S(2)}) collective-permute-start(bf16[128,2304]{1,0:T(8,128)(2,1)S(1)} %broadcast_select_fusion.1.b0), channel_id=1, source_target_pairs={{0,2},{2,4},{4,6},{6,0},{1,3},{3,5},{5,7},{7,1},{8,10},{10,12},{12... | collective-permute-start | bytes 1769480 | tf_op jit(solution)/shard_map/ppermute | solution.py:778
  322.4 2.7 collective-permute-start.18
  325.1 1.2 collective-permute-start.19
  326.5 1.7 broadcast_select_fusion.refs_1_
  328.2 3.5 collective-permute-done.17.b1
  331.6 9.1 %collective-permute-done.18.b2 = bf16[128,2304]{1,0:T(8,128)(2,1)} collective-permute-done((bf16[128,2304]{1,0:T(8,128)(2,1)S(1)}, bf16[128,2304]{1,0:T(8,128)(2,1)}, u32[]{:S(2)}, u32[]{:S(2)}) %collective-permute-start.18) | collective-permute-done | bytes 589856 | tf_op jit(solution)/shard_map/ppermute | solution.py:778
  340.7 4.5 %shard_map.280 = (f32[128,3072]{1,0:T(8,128)}, f32[128,3072]{1,0:T(8,128)}, f32[3072,128]{1,0:T(8,128)}, f32[128,128]{1,0:T(8,128)S(1)}) custom-call(s32[1]{0:T(128)} %bitcast.40.turn_at, bf16[128,2304]{1,0:T(8,128)(2,1)S(1)} %broadcast_select_fusion.1.b0, bf16[128,2304]{1,0:T(8,128)(2,1)} %collective-permute-done.17.b1, ...), custom_call_target="tpu_custom_call" | custom-call | flops 1048576 | bytes 8388608 | tf_op jit(solution)/shard_map/pallas_call | solution.py:730
  345.3 3.0 shard_map.281
  348.3 1.9 collective-permute-start.20
  350.2 6.2 %collective-permute-start.21 = (bf16[144,1024]{1,0:T(8,128)(2,1)S(1)}, bf16[144,1024]{1,0:T(8,128)(2,1)S(1)}, u32[]{:S(2)}, u32[]{:S(2)}) collective-permute-start(bf16[144,1024]{1,0:T(8,128)(2,1)S(1)} %shard_map.281), channel_id=1, source_target_pairs={{0,2},{1,10},{2,4},{3,12},{4,6},{5,14},{6,0},{7,8},{8,3},{9,11},{1... | collective-permute-start | bytes 884744 | tf_op jit(solution)/shard_map/ppermute | solution.py:932
  356.4 2.7 collective-permute-start.23
  359.4 1.7 collective-permute-done.21.b1
  361.0 5.4 %collective-permute-done.22.b2 = bf16[144,1024]{1,0:T(8,128)(2,1)S(1)} collective-permute-done((bf16[144,1024]{1,0:T(8,128)(2,1)S(1)}, bf16[144,1024]{1,0:T(8,128)(2,1)S(1)}, u32[]{:S(2)}, u32[]{:S(2)}) %collective-permute-start.22) | collective-permute-done | bytes 294944 | tf_op jit(solution)/shard_map/ppermute | solution.py:932
  366.5 6.8 %collective-permute-done.23.b3 = bf16[144,1024]{1,0:T(8,128)(2,1)S(1)} collective-permute-done((bf16[144,1024]{1,0:T(8,128)(2,1)S(1)}, bf16[144,1024]{1,0:T(8,128)(2,1)S(1)}, u32[]{:S(2)}, u32[]{:S(2)}) %collective-permute-start.23) | collective-permute-done | bytes 294944 | tf_op jit(solution)/shard_map/ppermute | solution.py:932
  374.2 2.4 shard_map.282
  376.7 1.6 fusion.8
  378.3 2.0 collective-permute-done.24
  (211 shorter events, 27.7 us)
Async XLA Ops:
  7.2 5.6 %copy-start = (bf16[3072,128]{1,0:T(8,128)(2,1)S(1)}, bf16[3072,128]{1,0:T(8,128)(2,1)}, u32[]{:S(2)}) copy-start(bf16[3072,128]{1,0:T(8,128)(2,1)} %param.30) | copy-start | bytes 2359300
  7.2 6.8 %copy-start.56 = (bf16[128]{0:T(256)(128)(2,1)S(1)}, bf16[128]{0:T(256)(128)(2,1)}, u32[]{:S(2)}) copy-start(bf16[128]{0:T(256)(128)(2,1)} %param.27) | copy-start | bytes 772
  7.2 60.6 %all-gather.3.cloned.1.call-start = ((), (), s32[]{:S(2)}) async-start(), calls=%async_computation.7 | async-start | bytes 5013504 | tf_op jit(solution)/shard_map/all_gather | solution.py:789
  12.7 133.1 %all-gather.5.cloned.1.call-start = ((), (), s32[]{:S(2)}) async-start(), calls=%async_computation.8 | async-start | bytes 10027008 | tf_op jit(solution)/shard_map/all_gather | solution.py:789
  14.0 12.5 %copy-start.52 = (bf16[128,2048]{1,0:T(8,128)(2,1)S(1)}, bf16[128,2048]{1,0:T(8,128)(2,1)}, u32[]{:S(2)}) copy-start(bf16[128,2048]{1,0:T(8,128)(2,1)} %param.31) | copy-start | bytes 1572868
  14.0 12.5 %copy-start.53 = (bf16[128,2048]{1,0:T(8,128)(2,1)S(1)}, bf16[128,2048]{1,0:T(8,128)(2,1)}, u32[]{:S(2)}) copy-start(bf16[128,2048]{1,0:T(8,128)(2,1)} %param.16) | copy-start | bytes 1572868
  14.2 11.3 %collective-permute-start.6 = (bf16[128,2304]{1,0:T(8,128)(2,1)S(1)}, bf16[128,2304]{1,0:T(8,128)(2,1)S(1)}, u32[]{:S(2)}, u32[]{:S(2)}) collective-permute-start(bf16[128,2304]{1,0:T(8,128)(2,1)S(1)} %pad_maximum_fusion.1), channel_id=1, source_target_pairs={{8,1},{1,8},{24,17},{17,24},{40,33},{33,40},{56,49},{49,56},{72,65... | collective-permute-start | bytes 1769480 | tf_op jit(solution)/shard_map/ppermute | solution.py:824
  26.7 2.0 collective-permute-start
  31.2 5.4 %copy-start.55 = (s32[1,13]{1,0:T(1,128)S(1)}, s32[1,13]{1,0:T(1,128)}, u32[]{:S(2)}) copy-start(s32[1,13]{1,0:T(1,128)} %param.17) | copy-start | bytes 160
  31.2 32.1 %all-to-all-start = ((bf16[4,128,2048]{2,1,0:T(8,128)(2,1)}), bf16[4,128,2048]{2,1,0:T(8,128)(2,1)S(1)}, u32[]{:S(2)}, u32[]{:S(2)}) async-start(bf16[4,128,2048]{2,1,0:T(8,128)(2,1)} %broadcast_in_dim.20), calls=%async_computation | async-start | bytes 4194304 | tf_op jit(solution)/shard_map/all_to_all | solution.py:775
  36.7 27.0 %collective-permute-start.2 = (s32[2,13]{1,0:T(2,128)S(1)}, s32[2,13]{1,0:T(2,128)S(1)}, u32[]{:S(2)}, u32[]{:S(2)}) collective-permute-start(s32[2,13]{1,0:T(2,128)S(1)} %pad_add_fusion.2), channel_id=1, source_target_pairs={{0,8},{8,0},{16,24},{24,16},{32,40},{40,32},{48,56},{56,48},{64,72... | collective-permute-start | bytes 320 | tf_op jit(solution)/shard_map/ppermute | solution.py:772
  63.3 4.3 %collective-permute-start.1 = (bf16[4,128,2048]{2,1,0:T(8,128)(2,1)S(1)}, bf16[4,128,2048]{2,1,0:T(8,128)(2,1)}, u32[]{:S(2)}, u32[]{:S(2)}) collective-permute-start(bf16[4,128,2048]{2,1,0:T(8,128)(2,1)S(1)} %all-to-all-done.refs_0_.refs_2_.refs_1_), channel_id=1, source_target_pairs={{0,8},{8,0},{16,24},{24,16},{32,40},{40,32},{48,56},{56,48},{64,72... | collective-permute-start | bytes 6291464 | tf_op jit(solution)/shard_map/ppermute | solution.py:772
  65.7 14.3 %copy-start.9 = (f32[512,128]{1,0:T(8,128)}, f32[512,128]{1,0:T(8,128)S(1)}, u32[]{:S(2)}) copy-start(f32[512,128]{1,0:T(8,128)S(1)} %get-tuple-element.62.refs_4_.refs_5_) | copy-start | bytes 786436
  70.3 4.7 %collective-permute-start.3 = (bf16[8,128,1152]{2,1,0:T(8,128)(2,1)S(1)}, bf16[8,128,1152]{2,1,0:T(8,128)(2,1)}, u32[]{:S(2)}, u32[]{:S(2)}) collective-permute-start(bf16[8,128,1152]{2,1,0:T(8,128)(2,1)S(1)} %shard_map.263), channel_id=1, source_target_pairs={{0,8},{8,0},{16,24},{24,16},{32,40},{40,32},{48,56},{56,48},{64,72... | collective-permute-start | bytes 7077896 | tf_op jit(solution)/shard_map/ppermute | solution.py:772
  87.3 6.9 %copy-start.23 = (bf16[512,512]{1,0:T(8,128)(2,1)}, bf16[512,512]{1,0:T(8,128)(2,1)S(1)}, u32[]{:S(2)}) copy-start(bf16[512,512]{1,0:T(8,128)(2,1)S(1)} %get-tuple-element.64.refs_0_.refs_1_) | copy-start | bytes 1572868
  87.3 6.9 %copy-start.25 = (f32[512,256]{1,0:T(8,128)}, f32[512,256]{1,0:T(8,128)S(1)}, u32[]{:S(2)}) copy-start(f32[512,256]{1,0:T(8,128)S(1)} %get-tuple-element.65.refs_1_.refs_3_) | copy-start | bytes 1572868
  87.3 6.9 %copy-start.33 = (f32[512,384]{1,0:T(8,128)}, f32[512,384]{1,0:T(8,128)S(1)}, u32[]{:S(2)}) copy-start(f32[512,384]{1,0:T(8,128)S(1)} %get-tuple-element.84.refs_3_) | copy-start | bytes 2359300
  94.2 5.7 %copy-start.17 = (f32[2,512,512]{2,1,0:T(8,128)}, f32[2,512,512]{2,1,0:T(8,128)S(1)}, u32[]{:S(2)}) copy-start(f32[2,512,512]{2,1,0:T(8,128)S(1)} %get-tuple-element.79.refs_0_) | copy-start | bytes 6291460
  94.2 5.7 %copy-start.37 = (f32[512,256]{1,0:T(8,128)}, f32[512,256]{1,0:T(8,128)S(1)}, u32[]{:S(2)}) copy-start(f32[512,256]{1,0:T(8,128)S(1)} %get-tuple-element.82.refs_4_) | copy-start | bytes 1572868
  94.2 5.6 %copy-start.41 = (bf16[512,256]{1,0:T(8,128)(2,1)}, bf16[512,256]{1,0:T(8,128)(2,1)S(1)}, u32[]{:S(2)}) copy-start(bf16[512,256]{1,0:T(8,128)(2,1)S(1)} %get-tuple-element.88.refs_5_) | copy-start | bytes 786436
  94.2 2.7 collective-permute-start.4
  99.8 20.0 %all-to-all-start.1 = ((bf16[4,64,2048]{2,1,0:T(8,128)(2,1)}), bf16[4,64,2048]{2,1,0:T(8,128)(2,1)S(1)}, u32[]{:S(2)}, u32[]{:S(2)}) async-start(bf16[4,64,2048]{2,1,0:T(8,128)(2,1)} %bitcast.19), calls=%async_computation.1 | async-start | bytes 2097152 | tf_op jit(solution)/shard_map/all_to_all | solution.py:775
  104.4 178.0 %reduce-scatter.2.cloned.1.call-start = ((), (), s32[]{:S(2)}) async-start(), calls=%async_computation.9 | async-start | bytes 10027008 | tf_op jit(solution)/shard_map/reduce_scatter | solution.py:792
  108.8 30.1 %copy-start.4 = (bf16[2048,512]{1,0:T(8,128)(2,1)}, bf16[2048,512]{1,0:T(8,128)(2,1)S(1)}, u32[]{:S(2)}) copy-start(bf16[2048,512]{1,0:T(8,128)(2,1)S(1)} %shard_map.267.refs_2_.refs_0_) | copy-start | bytes 6291460
  138.8 2.7 collective-permute-start.5
  147.1 10.6 %copy-start.3 = (bf16[2048,512]{1,0:T(8,128)(2,1)S(1)}, bf16[2048,512]{1,0:T(8,128)(2,1)}, u32[]{:S(2)}) copy-start(bf16[2048,512]{1,0:T(8,128)(2,1)} %copy-done.2) | copy-start | bytes 6291460
  172.8 2.7 collective-permute-start.7
  175.8 19.8 %copy-start.14 = (f32[64,2048]{1,0:T(8,128)S(1)}, f32[64,2048]{1,0:T(8,128)}, u32[]{:S(2)}) copy-start(f32[64,2048]{1,0:T(8,128)} %copy-done.13) | copy-start | bytes 1572868
  175.8 19.8 %copy-start.32 = (bf16[64,2048]{1,0:T(8,128)(2,1)S(1)}, bf16[64,2048]{1,0:T(8,128)(2,1)}, u32[]{:S(2)}) copy-start(bf16[64,2048]{1,0:T(8,128)(2,1)} %get-tuple-element.122.refs_2_) | copy-start | bytes 786436
  195.6 17.2 %copy-start.8 = (bf16[512,768]{1,0:T(8,128)(2,1)S(1)}, bf16[512,768]{1,0:T(8,128)(2,1)}, u32[]{:S(2)}) copy-start(bf16[512,768]{1,0:T(8,128)(2,1)} %copy-done.7) | copy-start | bytes 2359300
  196.1 16.7 %copy-start.35 = (f32[64,2048]{1,0:T(8,128)}, f32[64,2048]{1,0:T(8,128)S(1)}, u32[]{:S(2)}) copy-start(f32[64,2048]{1,0:T(8,128)S(1)} %get-tuple-element.92.refs_5_) | copy-start | bytes 1572868
  212.7 7.1 %copy-start.26 = (f32[512,256]{1,0:T(8,128)S(1)}, f32[512,256]{1,0:T(8,128)}, u32[]{:S(2)}) copy-start(f32[512,256]{1,0:T(8,128)} %copy-done.25) | copy-start | bytes 1572868
  212.7 7.1 %copy-start.38 = (f32[512,256]{1,0:T(8,128)S(1)}, f32[512,256]{1,0:T(8,128)}, u32[]{:S(2)}) copy-start(f32[512,256]{1,0:T(8,128)} %copy-done.37) | copy-start | bytes 1572868
  212.7 7.1 %collective-permute-start.9 = (bf16[4,64,2048]{2,1,0:T(8,128)(2,1)S(1)}, bf16[4,64,2048]{2,1,0:T(8,128)(2,1)S(1)}, u32[]{:S(2)}, u32[]{:S(2)}) collective-permute-start(bf16[4,64,2048]{2,1,0:T(8,128)(2,1)S(1)} %all_to_all.32), channel_id=1, source_target_pairs={{0,8},{8,0},{16,24},{24,16},{32,40},{40,32},{48,56},{56,48},{64,72... | collective-permute-start | bytes 3145736 | tf_op jit(solution)/shard_map/ppermute | solution.py:772
  219.4 21.8 %collective-permute-start.8 = (bf16[256,2048]{1,0:T(8,128)(2,1)}, bf16[256,2048]{1,0:T(8,128)(2,1)}, u32[]{:S(2)}, u32[]{:S(2)}) collective-permute-start(bf16[256,2048]{1,0:T(8,128)(2,1)} %get-tuple-element.78), channel_id=1, source_target_pairs={{0,8},{8,0},{16,24},{24,16},{32,40},{40,32},{48,56},{56,48},{64,72... | collective-permute-start | bytes 3145736 | tf_op jit(solution)/shard_map/ppermute | solution.py:772
  228.6 5.9 %copy-start.29 = (bf16[512,512]{1,0:T(8,128)(2,1)S(1)}, bf16[512,512]{1,0:T(8,128)(2,1)}, u32[]{:S(2)}) copy-start(bf16[512,512]{1,0:T(8,128)(2,1)} %copy-done.27) | copy-start | bytes 1572868
  234.5 6.8 %copy-start.16 = (f32[256,2048]{1,0:T(8,128)S(1)}, f32[256,2048]{1,0:T(8,128)}, u32[]{:S(2)}) copy-start(f32[256,2048]{1,0:T(8,128)} %copy-done.15) | copy-start | bytes 6291460
  241.1 9.8 %collective-permute-start.10 = (bf16[256,2048]{1,0:T(8,128)(2,1)}, bf16[256,2048]{1,0:T(8,128)(2,1)}, u32[]{:S(2)}, u32[]{:S(2)}) collective-permute-start(bf16[256,2048]{1,0:T(8,128)(2,1)} %get-tuple-element.91), channel_id=1, source_target_pairs={{0,8},{8,0},{16,24},{24,16},{32,40},{40,32},{48,56},{56,48},{64,72... | collective-permute-start | bytes 3145736 | tf_op jit(solution)/shard_map/ppermute | solution.py:772
  243.7 7.1 %copy-start.20 = (f32[256,2048]{1,0:T(8,128)S(1)}, f32[256,2048]{1,0:T(8,128)}, u32[]{:S(2)}) copy-start(f32[256,2048]{1,0:T(8,128)} %copy-done.19) | copy-start | bytes 6291460
  243.7 101.5 %all-to-all-start.5 = ((bf16[16,144,1024]{2,1,0:T(8,128)(2,1)}), bf16[16,144,1024]{2,1,0:T(8,128)(2,1)}, u32[]{:S(2)}, u32[]{:S(2)}) async-start(bf16[16,144,1024]{2,1,0:T(8,128)(2,1)} %shard_map.277.refs_3_), calls=%async_computation.5 | async-start | bytes 9437184 | tf_op jit(solution)/shard_map/all_to_all | solution.py:797
  252.5 27.0 %copy-start.12 = (bf16[64,2048]{1,0:T(8,128)(2,1)S(1)}, bf16[64,2048]{1,0:T(8,128)(2,1)}, u32[]{:S(2)}) copy-start(bf16[64,2048]{1,0:T(8,128)(2,1)} %get-tuple-element.123.refs_1_.refs_6_) | copy-start | bytes 786436
  252.5 27.0 %copy-start.36 = (f32[64,2048]{1,0:T(8,128)S(1)}, f32[64,2048]{1,0:T(8,128)}, u32[]{:S(2)}) copy-start(f32[64,2048]{1,0:T(8,128)} %copy-done.35) | copy-start | bytes 1572868
  252.8 26.1 %collective-permute-start.11 = (bf16[128,2048]{1,0:T(8,128)(2,1)S(1)}, bf16[128,2048]{1,0:T(8,128)(2,1)S(1)}, u32[]{:S(2)}, u32[]{:S(2)}) collective-permute-start(bf16[128,2048]{1,0:T(8,128)(2,1)S(1)} %get-tuple-element.114), channel_id=1, source_target_pairs={{0,2},{2,4},{4,6},{6,0},{1,3},{3,5},{5,7},{7,1},{8,10},{10,12},{12... | collective-permute-start | bytes 1572872 | tf_op jit(solution)/shard_map/ppermute | solution.py:778
  253.3 25.6 %collective-permute-start.12 = (bf16[128,2048]{1,0:T(8,128)(2,1)S(1)}, bf16[128,2048]{1,0:T(8,128)(2,1)S(1)}, u32[]{:S(2)}, u32[]{:S(2)}) collective-permute-start(bf16[128,2048]{1,0:T(8,128)(2,1)S(1)} %get-tuple-element.115), channel_id=1, source_target_pairs={{0,4},{2,6},{4,0},{6,2},{1,5},{3,7},{5,1},{7,3},{8,12},{10,14},{12... | collective-permute-start | bytes 1572872 | tf_op jit(solution)/shard_map/ppermute | solution.py:778
  255.4 24.2 %collective-permute-start.13 = (bf16[128,2048]{1,0:T(8,128)(2,1)S(1)}, bf16[128,2048]{1,0:T(8,128)(2,1)S(1)}, u32[]{:S(2)}, u32[]{:S(2)}) collective-permute-start(bf16[128,2048]{1,0:T(8,128)(2,1)S(1)} %get-tuple-element.112), channel_id=1, source_target_pairs={{0,6},{2,0},{4,2},{6,4},{1,7},{3,1},{5,3},{7,5},{8,14},{10,8},{12,... | collective-permute-start | bytes 1572872 | tf_op jit(solution)/shard_map/ppermute | solution.py:778
  280.2 2.0 collective-permute-start.14
  282.4 35.2 %copy-start.51 = (bf16[128,2304]{1,0:T(8,128)(2,1)S(1)}, bf16[128,2304]{1,0:T(8,128)(2,1)}, u32[]{:S(2)}) copy-start(bf16[128,2304]{1,0:T(8,128)(2,1)} %reduce-scatter.2.cloned.1.call-done) | copy-start | bytes 1769476
  282.4 35.2 %collective-permute-start.16 = (bf16[128,2304]{1,0:T(8,128)(2,1)}, bf16[128,2304]{1,0:T(8,128)(2,1)S(1)}, u32[]{:S(2)}, u32[]{:S(2)}) collective-permute-start(bf16[128,2304]{1,0:T(8,128)(2,1)} %reduce-scatter.2.cloned.1.call-done), channel_id=1, source_target_pairs={{8,1},{1,8},{24,17},{17,24},{40,33},{33,40},{56,49},{49,56},{72,65... | collective-permute-start | bytes 1769480 | tf_op jit(solution)/shard_map/ppermute | solution.py:824
  284.9 41.5 %copy-start.49 = (bf16[1,128,2048]{2,1,0:T(8,128)(2,1)}, bf16[1,128,2048]{2,1,0:T(8,128)(2,1)S(1)}, u32[]{:S(2)}) copy-start(bf16[1,128,2048]{2,1,0:T(8,128)(2,1)S(1)} %maximum_select_fusion.1) | copy-start | bytes 1572868
  285.0 55.7 %copy-start.30 = (bf16[128,3072]{1,0:T(8,128)(2,1)S(1)}, bf16[128,3072]{1,0:T(8,128)(2,1)}, u32[]{:S(2)}) copy-start(bf16[128,3072]{1,0:T(8,128)(2,1)} %w_up.1) | copy-start | bytes 2359300
  285.0 55.7 %copy-start.31 = (bf16[128,3072]{1,0:T(8,128)(2,1)S(1)}, bf16[128,3072]{1,0:T(8,128)(2,1)}, u32[]{:S(2)}) copy-start(bf16[128,3072]{1,0:T(8,128)(2,1)} %w_gate.1) | copy-start | bytes 2359300
  285.0 41.5 %collective-permute-start.15 = (bf16[2,128,2048]{2,1,0:T(8,128)(2,1)S(1)}, bf16[2,128,2048]{2,1,0:T(8,128)(2,1)}, u32[]{:S(2)}, u32[]{:S(2)}) collective-permute-start(bf16[2,128,2048]{2,1,0:T(8,128)(2,1)S(1)} %pad_maximum_fusion), channel_id=1, source_target_pairs={{0,1},{9,8},{16,17},{25,24},{32,33},{41,40},{48,49},{57,56},{64,65... | collective-permute-start | bytes 3145736 | tf_op jit(solution)/shard_map/ppermute | solution.py:925
  317.7 13.9 %collective-permute-start.17 = (bf16[128,2304]{1,0:T(8,128)(2,1)S(1)}, bf16[128,2304]{1,0:T(8,128)(2,1)}, u32[]{:S(2)}, u32[]{:S(2)}) collective-permute-start(bf16[128,2304]{1,0:T(8,128)(2,1)S(1)} %broadcast_select_fusion.1.b0), channel_id=1, source_target_pairs={{0,2},{2,4},{4,6},{6,0},{1,3},{3,5},{5,7},{7,1},{8,10},{10,12},{12... | collective-permute-start | bytes 1769480 | tf_op jit(solution)/shard_map/ppermute | solution.py:778
  322.4 18.3 %collective-permute-start.18 = (bf16[128,2304]{1,0:T(8,128)(2,1)S(1)}, bf16[128,2304]{1,0:T(8,128)(2,1)}, u32[]{:S(2)}, u32[]{:S(2)}) collective-permute-start(bf16[128,2304]{1,0:T(8,128)(2,1)S(1)} %broadcast_select_fusion.1.b0), channel_id=1, source_target_pairs={{0,4},{2,6},{4,0},{6,2},{1,5},{3,7},{5,1},{7,3},{8,12},{10,14},{12... | collective-permute-start | bytes 1769480 | tf_op jit(solution)/shard_map/ppermute | solution.py:778
  325.1 15.6 %collective-permute-start.19 = (bf16[128,2304]{1,0:T(8,128)(2,1)S(1)}, bf16[128,2304]{1,0:T(8,128)(2,1)}, u32[]{:S(2)}, u32[]{:S(2)}) collective-permute-start(bf16[128,2304]{1,0:T(8,128)(2,1)S(1)} %broadcast_select_fusion.1.b0), channel_id=1, source_target_pairs={{0,6},{2,0},{4,2},{6,4},{1,7},{3,1},{5,3},{7,5},{8,14},{10,8},{12,... | collective-permute-start | bytes 1769480 | tf_op jit(solution)/shard_map/ppermute | solution.py:778
  345.2 28.0 %copy-start.39 = (bf16[128,1024]{1,0:T(8,128)(2,1)S(1)}, bf16[128,1024]{1,0:T(8,128)(2,1)}, u32[]{:S(2)}) copy-start(bf16[128,1024]{1,0:T(8,128)(2,1)} %wg.1) | copy-start | bytes 786436
  345.2 28.0 %copy-start.40 = (bf16[128,1024]{1,0:T(8,128)(2,1)S(1)}, bf16[128,1024]{1,0:T(8,128)(2,1)}, u32[]{:S(2)}) copy-start(bf16[128,1024]{1,0:T(8,128)(2,1)} %wq.1) | copy-start | bytes 786436
  345.2 28.0 %copy-start.43 = (bf16[128,512]{1,0:T(8,128)(2,1)S(1)}, bf16[128,512]{1,0:T(8,128)(2,1)}, u32[]{:S(2)}) copy-start(bf16[128,512]{1,0:T(8,128)(2,1)} %wv.1) | copy-start | bytes 393220
  348.3 11.1 %collective-permute-start.20 = (bf16[144,1024]{1,0:T(8,128)(2,1)S(1)}, bf16[144,1024]{1,0:T(8,128)(2,1)S(1)}, u32[]{:S(2)}, u32[]{:S(2)}) collective-permute-start(bf16[144,1024]{1,0:T(8,128)(2,1)S(1)} %shard_map.281), channel_id=1, source_target_pairs={{1,8},{3,10},{5,12},{7,14},{8,1},{10,3},{12,5},{14,7},{17,24},{19,... | collective-permute-start | bytes 884744 | tf_op jit(solution)/shard_map/ppermute | solution.py:932
  350.2 10.9 %collective-permute-start.21 = (bf16[144,1024]{1,0:T(8,128)(2,1)S(1)}, bf16[144,1024]{1,0:T(8,128)(2,1)S(1)}, u32[]{:S(2)}, u32[]{:S(2)}) collective-permute-start(bf16[144,1024]{1,0:T(8,128)(2,1)S(1)} %shard_map.281), channel_id=1, source_target_pairs={{0,2},{1,10},{2,4},{3,12},{4,6},{5,14},{6,0},{7,8},{8,3},{9,11},{1... | collective-permute-start | bytes 884744 | tf_op jit(solution)/shard_map/ppermute | solution.py:932
  356.4 10.1 %collective-permute-start.22 = (bf16[144,1024]{1,0:T(8,128)(2,1)S(1)}, bf16[144,1024]{1,0:T(8,128)(2,1)S(1)}, u32[]{:S(2)}, u32[]{:S(2)}) collective-permute-start(bf16[144,1024]{1,0:T(8,128)(2,1)S(1)} %shard_map.281), channel_id=1, source_target_pairs={{0,4},{1,12},{2,6},{3,14},{4,0},{5,8},{6,2},{7,10},{8,5},{9,13},{1... | collective-permute-start | bytes 884744 | tf_op jit(solution)/shard_map/ppermute | solution.py:932
  356.4 16.9 %collective-permute-start.23 = (bf16[144,1024]{1,0:T(8,128)(2,1)S(1)}, bf16[144,1024]{1,0:T(8,128)(2,1)S(1)}, u32[]{:S(2)}, u32[]{:S(2)}) collective-permute-start(bf16[144,1024]{1,0:T(8,128)(2,1)S(1)} %shard_map.281), channel_id=1, source_target_pairs={{0,6},{1,14},{2,0},{3,8},{4,2},{5,10},{6,4},{7,12},{8,7},{9,15},{1... | collective-permute-start | bytes 884744 | tf_op jit(solution)/shard_map/ppermute | solution.py:932
  374.2 7.3 %copy-start.1 = (bf16[3072,128]{1,0:T(8,128)(2,1)S(1)}, bf16[3072,128]{1,0:T(8,128)(2,1)}, u32[]{:S(2)}) copy-start(bf16[3072,128]{1,0:T(8,128)(2,1)} %param.30) | copy-start | bytes 2359300
  376.6 3.7 collective-permute-start.24
  (24 other events, 46.2 us)
Sparse Core Ops, SparseCore 0:
  12.8 54.8 all-gather.2
  70.5 75.2 all-gather.4
  166.9 86.2 reduce-scatter.1

commit v6 on v5

--- a/solution.py
+++ b/solution.py
@@ -187,7 +187,7 @@
 
     @pl.when(step == 0)
     def _():
-        mine[...] = out
+        mine[...] = out.astype(BF16)
 
     @pl.when(step == 1)
     def _():
@@ -218,7 +218,7 @@
             struct((2, length, length), F32),
             struct((length, 2 * HD), F32),
             struct((length, 2 * HD), BF16),
-            struct((half, width), F32),
+            struct((half, width), BF16),
             struct((half, width), BF16),
         ],
         2 * length * width * 2 * HD + 8 * length * length * HD,
@@ -281,7 +281,7 @@
 def feed_back_kernel(d_gate, d_up, wg, wu, mine, other):
     half = mine.shape[0]
     out = dot_back(d_gate[...], wg[...]) + dot_back(d_up[...], wu[...])
-    mine[...] = out[:half, :]
+    mine[...] = out[:half, :].astype(BF16)
     other[...] = out[half:, :].astype(BF16)
 
 
@@ -299,7 +299,7 @@
             pl.BlockSpec((chunk, units), lambda i: (i, 1)),
         ],
         [slab, slab],
-        [struct((half, width), F32), struct((half, width), BF16)],
+        [struct((half, width), BF16), struct((half, width), BF16)],
         2 * length * width * units * 2,
         behind=behind,
     )(d_gate, d_up, w, w)
@@ -310,7 +310,7 @@
 
     @pl.when(pl.program_id(0) == 0)
     def _():
-        mine[...] = out
+        mine[...] = out.astype(BF16)
 
     @pl.when(pl.program_id(0) == 1)
     def _():
@@ -325,7 +325,7 @@
         (2,),
         [rowed(half, units), pl.BlockSpec((width, units), lambda i: (0, place))],
         [fixed((half, width)), fixed((half, width))],
-        [struct((half, width), F32), struct((half, width), BF16)],
+        [struct((half, width), BF16), struct((half, width), BF16)],
         2 * length * width * units,
         behind=behind,
     )(left, w)
@@ -463,7 +463,7 @@
 
     @pl.when(pl.program_id(0) == 0)
     def _():
-        mine[...] = out
+        mine[...] = out.astype(BF16)
 
     @pl.when(pl.program_id(0) == 1)
     def _():
@@ -478,7 +478,7 @@
         (2,),
         [rowed(half, 4 * HD), rowed(half, 2 * HD), fixed((width, 6 * HD))],
         [fixed((half, width)), fixed((half, width))],
-        [struct((half, width), F32), struct((half, width), BF16)],
+        [struct((half, width), BF16), struct((half, width), BF16)],
         2 * length * width * 6 * HD,
         behind=behind,
     )(d_qkv, d_gate, w)
@@ -777,12 +777,14 @@
     def ctx_turn(value, by):
         return lax.ppermute(value, "ctx", [(i, (i + by) % n_ctx) for i in range(n_ctx)])
 
-    def tree_rows(spread):
+    def tree_rows(spread, *before):
         mine = ctx_exchange(spread)
-        return mine, core_swap(mine)
+        if before:
+            mine, *before = lax.optimization_barrier((mine, *before))
+        return mine, core_swap(mine), *before
 
     def tree_half(mine, other):
-        half = (mine + core_swap(other).astype(F32)).astype(BF16)
+        half = (mine.astype(F32) + core_swap(other).astype(F32)).astype(BF16)
         return half.reshape((n_ctx, -1) + half.shape[1:])
 
     def plane_gather(value):
@@ -887,9 +889,10 @@
         ffn = feed_grads(u_flip, xa, xb, d_gate, d_up, hidden, ())
         half = tree_half(*feed_back(d_gate, d_up, w2, (ffn,)))
         d_middle, spread = d_middle_step(ctx_exchange(half), middle, own_cot)
-        da, db = (flat(v) for v in tree_rows(spread))
+        layer_mine, layer_other = down_product(hidden, w2, 2, (half,))
+        da, db, layer_mine, layer_other = tree_rows(spread, layer_mine, layer_other)
+        da, db = flat(da), flat(db)
         grad_ffn = plane_scatter(ffn)
-        layer_mine, layer_other = down_product(hidden, w2, 2, (half,))
 
         d_attended, d_gate_pre = gate_back(da, db, w1, gate, attended)
         d_qkv, terms = attend_back(probs, low, d_attended, pre, gains, cosine, sine, ())
@@ -900,17 +903,32 @@
         wide_terms = jnp.concatenate([spread_terms(terms[0]), spread_terms(terms[1])], axis=2)
         wide_terms = jnp.pad(wide_terms, ((0, 0), (0, 0), (0, 8 * HD - 2 * head_rows)))
         attn = attend_grads(x_flip, da, db, d_qkv, d_gate_pre, gated, wide_terms, ())
+        in_mine, in_other = input_back(d_qkv, d_gate_pre, w1, (attn,))
+        layer_half, in_half = tree_half(layer_mine, layer_other), tree_half(in_mine, in_other)
+        attn, layer_half, in_half, grad_ffn = lax.optimization_barrier(
+            (attn, layer_half, in_half, grad_ffn)
+        )
         attn_parts = plane_exchange(attn)
-        in_mine, in_other = input_back(d_qkv, d_gate_pre, w1, (attn,))
+
+        def owners(block):
+            block = swapped(block)
+            return [block] + [ctx_turn(block, by) for by in range(1, n_ctx)]
+
+        def owners_at_once(block):
+            moved = [lax.ppermute(block, ("shard", "ctx", "tp"), perm) for perm in owner_perms]
+            return [jnp.where(native, block, moved[0])] + moved[1:]
 
         both = jnp.concatenate(
-            [tree_half(layer_mine, layer_other), tree_half(in_mine, in_other)], axis=1
+            [layer_half, in_half], axis=1
         )
         parts = [lax.dynamic_index_in_dim(both, ctx, 0, False)] + [
             ctx_turn(lax.dynamic_index_in_dim(both, (ctx + by) % n_ctx, 0, False), by)
             for by in range(1, n_ctx)
         ]
         ends = ends_step(parts, middle, d_middle, own_x)
+        ffn_blocks = owners(grad_ffn)
+        attn_sum = sum_step(attn_parts, (ends, ffn_blocks[0]))
+        ends, attn_sum = lax.optimization_barrier((ends, attn_sum))
         sibling = core_swap(ends)
 
         def whole(start):
@@ -924,17 +942,8 @@
         full = jnp.stack([whole(0), whole(rows)])
         full = jnp.where(native, full, lax.ppermute(full, PLANE, across_perm))
 
-        def owners(block):
-            block = swapped(block)
-            return [block] + [ctx_turn(block, by) for by in range(1, n_ctx)]
-
-        def owners_at_once(block):
-            moved = [lax.ppermute(block, ("shard", "ctx", "tp"), perm) for perm in owner_perms]
-            return [jnp.where(native, block, moved[0])] + moved[1:]
-
         turn_at = ctx.astype(jnp.int32).reshape(1)
         size = gain_in.shape[0]
-        ffn_blocks = owners(grad_ffn)
         grad_gate, grad_up, grad_down, mid_sums = close(
             close_feed_kernel,
             turn_at,
@@ -944,7 +953,7 @@
             w_down.shape,
             [(size, HD)],
         )
-        attn_blocks = owners_at_once(sum_step(attn_parts, (full, mid_sums)))
+        attn_blocks = owners(attn_sum)
         grad_query, grad_key, grad_value, grad_gate_attn, grad_out, in_sums, head_ends = close(
             close_attend_kernel,
             turn_at,

time: 390 us -> 378 us (0.969)
  the two profiles are of different devices: /device:TPU:12 before, /device:TPU:1 now
where the time goes in v6:
time: 378 us; the launch traced here: 371 us
  waiting for transfers between devices  140 us (37%)
  Pallas kernels  80.1 us (21%)
  starting transfers between devices  54.6 us (14%)
  blocking collectives  34.2 us (9%)
  local copies, waits for them, and re-layouts  31.8 us (8%)
  other arithmetic  15.5 us (4%)
  between operations  14.7 us (4%)
    pallas_call x16, Pallas kernels, call(): return lambda *operands: built(*operands, *behind)  64.9 us
    all_to_all x3, waiting for transfers between devices, ctx_exchange(): return lax.all_to_all(value, 'ctx', 0, 0)  43.1 us
    ppermute x3, waiting for transfers between devices, swapped(): return jnp.where(native, value, lax.ppermute(value, PLANE, swap_perm))  35.7 us
    all_to_all x2, blocking collectives, ctx_exchange(): return lax.all_to_all(value, 'ctx', 0, 0)  34.2 us
    ppermute x9, waiting for transfers between devices, ctx_turn(): lax.ppermute(value, 'ctx', [(i, (i + by) % n_ctx) for i in range(n_ctx)])  25.8 us
    unnamed x110, local copies, waits for them, and re-layouts  21.8 us
    ppermute x11, waiting for transfers between devices, core_swap(): return lax.ppermute(value, 'shard', core_perm)  18.8 us
    all_to_all x3, starting transfers between devices, ctx_exchange(): return lax.all_to_all(value, 'ctx', 0, 0)  13 us
  transfers between devices with their start and end apart: 32, of which 22 were waited for; matrix products, arithmetic and copies ran while one was open for 5% of the time, Pallas kernels for 17%

profile of v6, /device:TPU:1, one launch (start us, length us, event | category | flops | bytes accessed | tf_op | source)
XLA Modules:
  0.0 371.5 jit_solution(1657805111697881464)
XLA Ops:
  14.2 4.5 %collective-permute-start.6 = (bf16[128,2304]{1,0:T(8,128)(2,1)S(1)}, bf16[128,2304]{1,0:T(8,128)(2,1)S(1)}, u32[]{:S(2)}, u32[]{:S(2)}) collective-permute-start(bf16[128,2304]{1,0:T(8,128)(2,1)S(1)} %pad_maximum_fusion.1), channel_id=1, source_target_pairs={{8,1},{1,8},{24,17},{17,24},{40,33},{33,40},{56,49},{49,56},{72,65... | collective-permute-start | bytes 1769480 | tf_op jit(solution)/shard_map/ppermute | solution.py:826
  18.8 7.5 %collective-permute-done.6 = bf16[128,2304]{1,0:T(8,128)(2,1)S(1)} collective-permute-done((bf16[128,2304]{1,0:T(8,128)(2,1)S(1)}, bf16[128,2304]{1,0:T(8,128)(2,1)S(1)}, u32[]{:S(2)}, u32[]{:S(2)}) %collective-permute-start.6) | collective-permute-done | bytes 589856 | tf_op jit(solution)/shard_map/ppermute | solution.py:826
  27.5 1.9 collective-permute-done
  30.4 1.6 broadcast_in_dim.20
  31.9 5.3 %all-to-all-start = ((bf16[4,128,2048]{2,1,0:T(8,128)(2,1)}), bf16[4,128,2048]{2,1,0:T(8,128)(2,1)S(1)}, u32[]{:S(2)}, u32[]{:S(2)}) async-start(bf16[4,128,2048]{2,1,0:T(8,128)(2,1)} %broadcast_in_dim.20), calls=%async_computation | async-start | bytes 4194304 | tf_op jit(solution)/shard_map/all_to_all | solution.py:775
  37.8 25.4 %all-to-all-done.refs_0_.refs_2_.refs_1_ = bf16[4,128,2048]{2,1,0:T(8,128)(2,1)S(1)} async-done(((bf16[4,128,2048]{2,1,0:T(8,128)(2,1)}), bf16[4,128,2048]{2,1,0:T(8,128)(2,1)S(1)}, u32[]{:S(2)}, u32[]{:S(2)}) %all-to-all-start) | async-done | bytes 2097184 | tf_op jit(solution)/shard_map/all_to_all | solution.py:775
  63.2 1.3 collective-permute-start.1
  66.9 1.5 collective-permute-done.1.refs_1_.refs_3_.refs_2_
  68.4 1.6 all-gather.3.cloned.1.call-done
  70.0 2.5 shard_map.263
  73.4 4.1 %collective-permute-done.3.other = bf16[8,128,1152]{2,1,0:T(8,128)(2,1)} collective-permute-done((bf16[8,128,1152]{2,1,0:T(8,128)(2,1)S(1)}, bf16[8,128,1152]{2,1,0:T(8,128)(2,1)}, u32[]{:S(2)}, u32[]{:S(2)}) %collective-permute-start.3) | collective-permute-done | bytes 2359328 | tf_op jit(solution)/shard_map/ppermute | solution.py:772
  77.5 5.0 %shard_map.264 = bf16[8,2,128,1152]{3,2,1,0:T(8,128)(2,1)} custom-call(s32[1]{0:T(128)} %bitcast.16.core, bf16[8,2,128,1152]{3,2,1,0:T(8,128)(2,1)} %bitcast.98, bf16[8,128,1152]{2,1,0:T(8,128)(2,1)} %collective-permute-done.3.other), custom_call_target="tpu_custom_call" | custom-call | flops 1048576 | bytes 8388608 | tf_op jit(solution)/shard_map/pallas_call | solution.py:647
  82.5 5.8 %shard_map.265 = (bf16[512,2048]{1,0:T(8,128)(2,1)S(1)}, f32[512,384]{1,0:T(8,128)S(1)}, bf16[512,512]{1,0:T(8,128)(2,1)S(1)}, f32[512,256]{1,0:T(8,128)S(1)}, f32[16,128]{1,0:T(8,128)S(1)}) custom-call(bf16[4,128,2048]{2,1,0:T(8,128)(2,1)} %copy-done.44, bf16[4,128,2048]{2,1,0:T(8,128)(2,1)} %collective-permute-done.1.refs_1_.refs_3_.refs_2_, ...), custom_call_target="tpu_custom_call" | custom-call | flops 1610612736 | bytes 8388608 | tf_op jit(solution)/shard_map/pallas_call | solution.py:97
  88.3 1.3 copy-done.17
  89.7 6.4 %shard_map.267 = (f32[2,512,512]{2,1,0:T(8,128)}, f32[512,256]{1,0:T(8,128)S(1)}, bf16[512,256]{1,0:T(8,128)(2,1)S(1)}, bf16[256,2048]{1,0:T(8,128)(2,1)S(1)}, bf16[256,2048]{1,0:T(8,128)(2,1)S(1)}) custom-call(bf16[512,512]{1,0:T(8,128)(2,1)S(1)} %get-tuple-element.74.refs_0_.refs_1_, f32[512,256]{1,0:T(8,128)S(1)} %get-tuple-element.75.refs_1_.refs_3_, ...), custom_call_target="tpu_custom_call" | custom-call | flops 805306368 | bytes 8388608 | tf_op jit(solution)/shard_map/pallas_call | solution.py:97
  96.6 2.3 collective-permute-done.4
  98.9 1.4 add_convert_fusion.3
  100.2 4.2 %all-to-all-start.1 = ((bf16[4,64,2048]{2,1,0:T(8,128)(2,1)}), bf16[4,64,2048]{2,1,0:T(8,128)(2,1)S(1)}, u32[]{:S(2)}, u32[]{:S(2)}) async-start(bf16[4,64,2048]{2,1,0:T(8,128)(2,1)} %bitcast.19), calls=%async_computation.1 | async-start | bytes 2097152 | tf_op jit(solution)/shard_map/all_to_all | solution.py:775
  105.3 1.6 copy-done.18
  106.9 1.3 shard_map.266.refs_2_.refs_0_
  108.2 10.8 %all-to-all-done.1.refs_0_ = bf16[4,64,2048]{2,1,0:T(8,128)(2,1)S(1)} async-done(((bf16[4,64,2048]{2,1,0:T(8,128)(2,1)}), bf16[4,64,2048]{2,1,0:T(8,128)(2,1)S(1)}, u32[]{:S(2)}, u32[]{:S(2)}) %all-to-all-start.1) | async-done | bytes 1048608 | tf_op jit(solution)/shard_map/all_to_all | solution.py:775
  121.1 15.9 %all_to_all.30 = bf16[4,64,2048]{2,1,0:T(8,128)(2,1)S(1)} all-to-all(bf16[4,64,2048]{2,1,0:T(8,128)(2,1)S(1)} %get-tuple-element.80), channel_id=1, replica_groups=mesh['shard'=16,'ctx'=4,'tp'=2] {'ctx'}, dimensions={0} | all-to-all | bytes 2097152 | tf_op jit(solution)/shard_map/all_to_all | solution.py:775
  136.9 2.6 collective-permute-start.5
  139.5 2.3 collective-permute-done.5
  141.8 1.3 shard_map.269.refs_7_.refs_0_
  143.2 1.3 copy-done.2
  145.5 2.6 all-gather.5.cloned.1.call-done.refs_4_.refs_5_.refs_6_.refs_2_.refs_3_.refs_1_
  149.3 10.6 %shard_map.270 = (bf16[512,768]{1,0:T(8,128)(2,1)S(1)}, bf16[512,768]{1,0:T(8,128)(2,1)S(1)}, bf16[512,768]{1,0:T(8,128)(2,1)S(1)}) custom-call(bf16[256,2048]{1,0:T(8,128)(2,1)S(1)} %bitcast.83, bf16[256,2048]{1,0:T(8,128)(2,1)S(1)} %bitcast.89, bf16[4,128,2048]{2,1,0:T(8,128)(2,1)} %copy-done.44, ...), custom_call_target="tpu_custom_call" | custom-call | flops 4831838208 | bytes 8388608 | tf_op jit(solution)/shard_map/pallas_call | solution.py:97
  159.9 8.1 %shard_map.271.refs_4_ = bf16[2048,2304]{1,0:T(8,128)(2,1)} custom-call(bf16[2048,512]{1,0:T(8,128)(2,1)S(1)} %copy-done.3, bf16[4,128,2048]{2,1,0:T(8,128)(2,1)} %copy-done.44, bf16[4,128,2048]{2,1,0:T(8,128)(2,1)} %collective-permute-done.1.refs_1_.refs_3_.refs_2_, bf16[512,768]{1,0:T(8,128)(2,1)S(1)} %get-tuple-element.81.refs_3_.refs_0_, ...), custom_call_target="tpu_custom_call" | custom-call | flops 4831838208 | bytes 8388608 | tf_op jit(solution)/shard_map/pallas_call | solution.py:97
  169.0 6.0 %shard_map.272 = (bf16[256,2048]{1,0:T(8,128)(2,1)S(1)}, bf16[256,2048]{1,0:T(8,128)(2,1)S(1)}) custom-call(bf16[512,768]{1,0:T(8,128)(2,1)S(1)} %get-tuple-element.81.refs_3_.refs_0_, bf16[512,768]{1,0:T(8,128)(2,1)S(1)} %get-tuple-element.82.refs_4_.refs_1_, bf16[2048,2304]{1,0:T(8,128)(2,1)} %all-gather.5.cloned.1.call-done.refs_4_.refs_5_.refs_6_.refs_2_.refs_3_.refs_1_, ...), custom_call_target="tpu_custom_call" | custom-call | flops 3221225472 | bytes 8388608 | tf_op jit(solution)/shard_map/pallas_call | solution.py:97
  175.7 2.3 collective-permute-done.7
  178.4 18.4 %all_to_all.31.refs_0_ = bf16[4,64,2048]{2,1,0:T(8,128)(2,1)S(1)} all-to-all(bf16[4,64,2048]{2,1,0:T(8,128)(2,1)S(1)} %bitcast.86), channel_id=1, replica_groups=mesh['shard'=16,'ctx'=4,'tp'=2] {'ctx'}, dimensions={0} | all-to-all | bytes 2097152 | tf_op jit(solution)/shard_map/all_to_all | solution.py:775
  199.0 3.5 all-to-all-start.4
  202.5 4.5 %shard_map.274 = (bf16[256,2048]{1,0:T(8,128)(2,1)S(1)}, bf16[256,2048]{1,0:T(8,128)(2,1)S(1)}) custom-call(bf16[512,768]{1,0:T(8,128)(2,1)S(1)} %copy-done.8, bf16[2048,2304]{1,0:T(8,128)(2,1)} %all-gather.5.cloned.1.call-done.refs_4_.refs_5_.refs_6_.refs_2_.refs_3_.refs_1_, bf16[4,64,2048]{2,1,0:T(8,128)(2,1)S(1)} %bitcast.87), custom_call_target="tpu_custom_call" | custom-call | flops 1610612736 | bytes 8388608 | tf_op jit(solution)/shard_map/pallas_call | solution.py:97
  208.9 6.9 %all-to-all-done.4 = bf16[4,64,2048]{2,1,0:T(8,128)(2,1)S(1)} async-done(((bf16[4,64,2048]{2,1,0:T(8,128)(2,1)}), bf16[4,64,2048]{2,1,0:T(8,128)(2,1)S(1)}, u32[]{:S(2)}, u32[]{:S(2)}) %all-to-all-start.4) | async-done | bytes 1048608 | tf_op jit(solution)/shard_map/all_to_all | solution.py:775
  215.9 2.7 collective-permute-start.8
  218.5 3.7 %collective-permute-done.8 = bf16[4,64,2048]{2,1,0:T(8,128)(2,1)S(1)} collective-permute-done((bf16[4,64,2048]{2,1,0:T(8,128)(2,1)S(1)}, bf16[4,64,2048]{2,1,0:T(8,128)(2,1)S(1)}, u32[]{:S(2)}, u32[]{:S(2)}) %collective-permute-start.8) | collective-permute-done | bytes 1048608 | tf_op jit(solution)/shard_map/ppermute | solution.py:772
  224.4 2.2 shard_map.275
  226.8 3.1 shard_map.276
  231.3 5.9 %shard_map.277.refs_3_ = bf16[16,144,1024]{2,1,0:T(8,128)(2,1)} custom-call(bf16[2048,512]{1,0:T(8,128)(2,1)} %copy-done.4, bf16[256,2048]{1,0:T(8,128)(2,1)S(1)} %bitcast.85, bf16[256,2048]{1,0:T(8,128)(2,1)S(1)} %bitcast.91, bf16[512,512]{1,0:T(8,128)(2,1)S(1)} %get-tuple-element.96.refs_3_.refs_0_, ...), custom_call_target="tpu_custom_call" | custom-call | flops 2147483648 | bytes 8388608 | tf_op jit(solution)/shard_map/pallas_call | solution.py:97
  237.2 4.2 %shard_map.278 = (bf16[256,2048]{1,0:T(8,128)(2,1)S(1)}, bf16[256,2048]{1,0:T(8,128)(2,1)S(1)}) custom-call(bf16[512,512]{1,0:T(8,128)(2,1)S(1)} %get-tuple-element.96.refs_3_.refs_0_, bf16[512,256]{1,0:T(8,128)(2,1)S(1)} %get-tuple-element.97.refs_4_.refs_1_, bf16[2048,1152]{1,0:T(8,128)(2,1)} %bitcast.96, bf16[16,144,1024]{2,1,0:T(8,128)(2,1)} %shard_map.277.refs_3_), custom_call_target="tpu_custom_call" | custom-call | flops 1610612736 | bytes 8388608 | tf_op jit(solution)/shard_map/pallas_call | solution.py:97
  241.9 1.6 add_convert_fusion.1
  244.6 10.4 %reduce-scatter.2.cloned.1.call-done = bf16[128,2304]{1,0:T(8,128)(2,1)} async-done(((bf16[2048,2304]{1,0:T(8,128)(2,1)}), bf16[128,2304]{1,0:T(8,128)(2,1)}) %reduce-scatter.2.cloned.1.call-update) | async-done | bytes 589840 | tf_op jit(solution)/shard_map/reduce_scatter | solution.py:794
  255.0 4.7 %all-to-all-start.5 = ((bf16[16,144,1024]{2,1,0:T(8,128)(2,1)}), bf16[16,144,1024]{2,1,0:T(8,128)(2,1)}, u32[]{:S(2)}, u32[]{:S(2)}) async-start(bf16[16,144,1024]{2,1,0:T(8,128)(2,1)} %shard_map.277.refs_3_), calls=%async_computation.6 | async-start | bytes 9437184 | tf_op jit(solution)/shard_map/all_to_all | solution.py:799
  259.7 5.3 %collective-permute-start.14 = (bf16[128,2304]{1,0:T(8,128)(2,1)}, bf16[128,2304]{1,0:T(8,128)(2,1)}, u32[]{:S(2)}, u32[]{:S(2)}) collective-permute-start(bf16[128,2304]{1,0:T(8,128)(2,1)} %reduce-scatter.2.cloned.1.call-done), channel_id=1, source_target_pairs={{8,1},{1,8},{24,17},{17,24},{40,33},{33,40},{56,49},{49,56},{72,65... | collective-permute-start | bytes 1769480 | tf_op jit(solution)/shard_map/ppermute | solution.py:826
  266.5 1.3 collective-permute-start.11
  267.8 2.6 collective-permute-start.12
  271.4 9.4 %collective-permute-done.11.refs_1_ = bf16[128,2048]{1,0:T(8,128)(2,1)S(1)} collective-permute-done((bf16[128,2048]{1,0:T(8,128)(2,1)}, bf16[128,2048]{1,0:T(8,128)(2,1)S(1)}, u32[]{:S(2)}, u32[]{:S(2)}) %collective-permute-start.11) | collective-permute-done | bytes 524320 | tf_op jit(solution)/shard_map/ppermute | solution.py:778
  280.9 12.1 %collective-permute-done.12.refs_2_ = bf16[128,2048]{1,0:T(8,128)(2,1)S(1)} collective-permute-done((bf16[128,2048]{1,0:T(8,128)(2,1)}, bf16[128,2048]{1,0:T(8,128)(2,1)S(1)}, u32[]{:S(2)}, u32[]{:S(2)}) %collective-permute-start.12) | collective-permute-done | bytes 524320 | tf_op jit(solution)/shard_map/ppermute | solution.py:778
  294.9 1.7 shard_map.279.refs_1_
  296.6 22.9 %collective-permute-done.14 = bf16[128,2304]{1,0:T(8,128)(2,1)} collective-permute-done((bf16[128,2304]{1,0:T(8,128)(2,1)}, bf16[128,2304]{1,0:T(8,128)(2,1)}, u32[]{:S(2)}, u32[]{:S(2)}) %collective-permute-start.14) | collective-permute-done | bytes 589856 | tf_op jit(solution)/shard_map/ppermute | solution.py:826
  320.6 1.4 collective-permute-start.21
  321.9 2.6 collective-permute-start.22
  325.6 2.9 shard_map.280
  328.5 3.1 collective-permute-start.17
  331.8 5.2 %collective-permute-done.17 = bf16[144,1024]{1,0:T(8,128)(2,1)S(1)} collective-permute-done((bf16[144,1024]{1,0:T(8,128)(2,1)S(1)}, bf16[144,1024]{1,0:T(8,128)(2,1)S(1)}, u32[]{:S(2)}, u32[]{:S(2)}) %collective-permute-start.17) | collective-permute-done | bytes 294944 | tf_op jit(solution)/shard_map/ppermute | solution.py:826
  338.6 1.8 collective-permute-start.20
  341.8 1.3 collective-permute-start.16
  343.4 4.3 %shard_map.282 = (f32[128,3072]{1,0:T(8,128)}, f32[128,3072]{1,0:T(8,128)}, f32[3072,128]{1,0:T(8,128)}, f32[128,128]{1,0:T(8,128)S(1)}) custom-call(s32[1]{0:T(128)} %bitcast.40.turn_at, bf16[128,2304]{1,0:T(8,128)(2,1)S(1)} %broadcast_select_fusion.1.refs_2_.b0, bf16[128,2304]{1,0:T(8,128)(2,1)S(1)} %collective-permute-done.21.b1, ...), custom_call_target="tpu_custom_call" | custom-call | flops 1048576 | bytes 8388608 | tf_op jit(solution)/shard_map/pallas_call | solution.py:730
  347.8 3.8 %collective-permute-done.18.b1 = bf16[144,1024]{1,0:T(8,128)(2,1)} collective-permute-done((bf16[144,1024]{1,0:T(8,128)(2,1)S(1)}, bf16[144,1024]{1,0:T(8,128)(2,1)}, u32[]{:S(2)}, u32[]{:S(2)}) %collective-permute-start.18) | collective-permute-done | bytes 294944 | tf_op jit(solution)/shard_map/ppermute | solution.py:778
  354.5 3.4 shard_map.281
  358.1 2.4 collective-permute-done.24
  361.7 1.7 broadcast_select_fusion
  363.4 1.6 fusion
  (208 shorter events, 44.0 us)
Async XLA Ops:
  7.2 5.6 %copy-start = (bf16[3072,128]{1,0:T(8,128)(2,1)S(1)}, bf16[3072,128]{1,0:T(8,128)(2,1)}, u32[]{:S(2)}) copy-start(bf16[3072,128]{1,0:T(8,128)(2,1)} %param.30) | copy-start | bytes 2359300
  7.2 6.8 %copy-start.53 = (bf16[128]{0:T(256)(128)(2,1)S(1)}, bf16[128]{0:T(256)(128)(2,1)}, u32[]{:S(2)}) copy-start(bf16[128]{0:T(256)(128)(2,1)} %param.27) | copy-start | bytes 772
  7.2 62.8 %all-gather.3.cloned.1.call-start = ((), (), s32[]{:S(2)}) async-start(), calls=%async_computation.7 | async-start | bytes 5013504 | tf_op jit(solution)/shard_map/all_gather | solution.py:791
  12.7 135.4 %all-gather.5.cloned.1.call-start = ((), (), s32[]{:S(2)}) async-start(), calls=%async_computation.8 | async-start | bytes 10027008 | tf_op jit(solution)/shard_map/all_gather | solution.py:791
  14.0 13.3 %copy-start.49 = (bf16[128,2048]{1,0:T(8,128)(2,1)S(1)}, bf16[128,2048]{1,0:T(8,128)(2,1)}, u32[]{:S(2)}) copy-start(bf16[128,2048]{1,0:T(8,128)(2,1)} %param.31) | copy-start | bytes 1572868
  14.0 13.3 %copy-start.50 = (bf16[128,2048]{1,0:T(8,128)(2,1)S(1)}, bf16[128,2048]{1,0:T(8,128)(2,1)}, u32[]{:S(2)}) copy-start(bf16[128,2048]{1,0:T(8,128)(2,1)} %param.16) | copy-start | bytes 1572868
  14.2 12.1 %collective-permute-start.6 = (bf16[128,2304]{1,0:T(8,128)(2,1)S(1)}, bf16[128,2304]{1,0:T(8,128)(2,1)S(1)}, u32[]{:S(2)}, u32[]{:S(2)}) collective-permute-start(bf16[128,2304]{1,0:T(8,128)(2,1)S(1)} %pad_maximum_fusion.1), channel_id=1, source_target_pairs={{8,1},{1,8},{24,17},{17,24},{40,33},{33,40},{56,49},{49,56},{72,65... | collective-permute-start | bytes 1769480 | tf_op jit(solution)/shard_map/ppermute | solution.py:826
  27.4 2.0 collective-permute-start
  31.9 5.3 %copy-start.51 = (s32[1,13]{1,0:T(1,128)S(1)}, s32[1,13]{1,0:T(1,128)}, u32[]{:S(2)}) copy-start(s32[1,13]{1,0:T(1,128)} %param.18) | copy-start | bytes 160
  31.9 5.3 %copy-start.52 = (s32[1,13]{1,0:T(1,128)S(1)}, s32[1,13]{1,0:T(1,128)}, u32[]{:S(2)}) copy-start(s32[1,13]{1,0:T(1,128)} %param.17) | copy-start | bytes 160
  31.9 31.3 %all-to-all-start = ((bf16[4,128,2048]{2,1,0:T(8,128)(2,1)}), bf16[4,128,2048]{2,1,0:T(8,128)(2,1)S(1)}, u32[]{:S(2)}, u32[]{:S(2)}) async-start(bf16[4,128,2048]{2,1,0:T(8,128)(2,1)} %broadcast_in_dim.20), calls=%async_computation | async-start | bytes 4194304 | tf_op jit(solution)/shard_map/all_to_all | solution.py:775
  37.2 27.6 %collective-permute-start.2 = (s32[2,13]{1,0:T(2,128)S(1)}, s32[2,13]{1,0:T(2,128)S(1)}, u32[]{:S(2)}, u32[]{:S(2)}) collective-permute-start(s32[2,13]{1,0:T(2,128)S(1)} %pad_add_fusion.2), channel_id=1, source_target_pairs={{0,8},{8,0},{16,24},{24,16},{32,40},{40,32},{48,56},{56,48},{64,72... | collective-permute-start | bytes 320 | tf_op jit(solution)/shard_map/ppermute | solution.py:772
  63.2 6.8 %copy-start.44 = (bf16[4,128,2048]{2,1,0:T(8,128)(2,1)}, bf16[4,128,2048]{2,1,0:T(8,128)(2,1)S(1)}, u32[]{:S(2)}) copy-start(bf16[4,128,2048]{2,1,0:T(8,128)(2,1)S(1)} %all-to-all-done.refs_0_.refs_2_.refs_1_) | copy-start | bytes 6291460
  63.2 5.2 %collective-permute-start.1 = (bf16[4,128,2048]{2,1,0:T(8,128)(2,1)S(1)}, bf16[4,128,2048]{2,1,0:T(8,128)(2,1)}, u32[]{:S(2)}, u32[]{:S(2)}) collective-permute-start(bf16[4,128,2048]{2,1,0:T(8,128)(2,1)S(1)} %all-to-all-done.refs_0_.refs_2_.refs_1_), channel_id=1, source_target_pairs={{0,8},{8,0},{16,24},{24,16},{32,40},{40,32},{48,56},{56,48},{64,72... | collective-permute-start | bytes 6291464 | tf_op jit(solution)/shard_map/ppermute | solution.py:772
  66.9 15.6 %copy-start.9 = (f32[512,128]{1,0:T(8,128)}, f32[512,128]{1,0:T(8,128)S(1)}, u32[]{:S(2)}) copy-start(f32[512,128]{1,0:T(8,128)S(1)} %get-tuple-element.71.refs_4_.refs_5_) | copy-start | bytes 786436
  72.5 5.0 %collective-permute-start.3 = (bf16[8,128,1152]{2,1,0:T(8,128)(2,1)S(1)}, bf16[8,128,1152]{2,1,0:T(8,128)(2,1)}, u32[]{:S(2)}, u32[]{:S(2)}) collective-permute-start(bf16[8,128,1152]{2,1,0:T(8,128)(2,1)S(1)} %shard_map.263), channel_id=1, source_target_pairs={{0,8},{8,0},{16,24},{24,16},{32,40},{40,32},{48,56},{56,48},{64,72... | collective-permute-start | bytes 7077896 | tf_op jit(solution)/shard_map/ppermute | solution.py:772
  89.7 6.4 %copy-start.19 = (bf16[512,512]{1,0:T(8,128)(2,1)}, bf16[512,512]{1,0:T(8,128)(2,1)S(1)}, u32[]{:S(2)}) copy-start(bf16[512,512]{1,0:T(8,128)(2,1)S(1)} %get-tuple-element.74.refs_0_.refs_1_) | copy-start | bytes 1572868
  89.7 6.4 %copy-start.21 = (f32[512,256]{1,0:T(8,128)}, f32[512,256]{1,0:T(8,128)S(1)}, u32[]{:S(2)}) copy-start(f32[512,256]{1,0:T(8,128)S(1)} %get-tuple-element.75.refs_1_.refs_3_) | copy-start | bytes 1572868
  89.7 6.4 %copy-start.29 = (f32[512,384]{1,0:T(8,128)}, f32[512,384]{1,0:T(8,128)S(1)}, u32[]{:S(2)}) copy-start(f32[512,384]{1,0:T(8,128)S(1)} %get-tuple-element.94.refs_3_) | copy-start | bytes 2359300
  96.1 4.1 %copy-start.35 = (f32[512,256]{1,0:T(8,128)}, f32[512,256]{1,0:T(8,128)S(1)}, u32[]{:S(2)}) copy-start(f32[512,256]{1,0:T(8,128)S(1)} %get-tuple-element.92.refs_4_) | copy-start | bytes 1572868
  96.1 4.1 %copy-start.39 = (bf16[512,256]{1,0:T(8,128)(2,1)}, bf16[512,256]{1,0:T(8,128)(2,1)S(1)}, u32[]{:S(2)}) copy-start(bf16[512,256]{1,0:T(8,128)(2,1)S(1)} %get-tuple-element.98.refs_5_) | copy-start | bytes 786436
  96.1 2.8 collective-permute-start.4
  98.9 5.6 %copy-start.46 = (bf16[128,2048]{1,0:T(8,128)(2,1)S(1)}, bf16[128,2048]{1,0:T(8,128)(2,1)}, u32[]{:S(2)}) copy-start(bf16[128,2048]{1,0:T(8,128)(2,1)} %copy-done.45) | copy-start | bytes 1572868
  100.2 18.7 %all-to-all-start.1 = ((bf16[4,64,2048]{2,1,0:T(8,128)(2,1)}), bf16[4,64,2048]{2,1,0:T(8,128)(2,1)S(1)}, u32[]{:S(2)}, u32[]{:S(2)}) async-start(bf16[4,64,2048]{2,1,0:T(8,128)(2,1)} %bitcast.19), calls=%async_computation.1 | async-start | bytes 2097152 | tf_op jit(solution)/shard_map/all_to_all | solution.py:775
  104.4 150.6 %reduce-scatter.2.cloned.1.call-start = ((), (), s32[]{:S(2)}) async-start(), calls=%async_computation.9 | async-start | bytes 10027008 | tf_op jit(solution)/shard_map/reduce_scatter | solution.py:794
  108.2 28.8 %copy-start.4 = (bf16[2048,512]{1,0:T(8,128)(2,1)}, bf16[2048,512]{1,0:T(8,128)(2,1)S(1)}, u32[]{:S(2)}) copy-start(bf16[2048,512]{1,0:T(8,128)(2,1)S(1)} %shard_map.266.refs_2_.refs_0_) | copy-start | bytes 6291460
  136.9 4.9 %collective-permute-start.5 = (bf16[4,64,2048]{2,1,0:T(8,128)(2,1)S(1)}, bf16[4,64,2048]{2,1,0:T(8,128)(2,1)S(1)}, u32[]{:S(2)}, u32[]{:S(2)}) collective-permute-start(bf16[4,64,2048]{2,1,0:T(8,128)(2,1)S(1)} %all_to_all.30), channel_id=1, source_target_pairs={{0,8},{8,0},{16,24},{24,16},{32,40},{40,32},{48,56},{56,48},{64,72... | collective-permute-start | bytes 3145736 | tf_op jit(solution)/shard_map/ppermute | solution.py:772
  149.3 10.6 %copy-start.3 = (bf16[2048,512]{1,0:T(8,128)(2,1)S(1)}, bf16[2048,512]{1,0:T(8,128)(2,1)}, u32[]{:S(2)}) copy-start(bf16[2048,512]{1,0:T(8,128)(2,1)} %copy-done.2) | copy-start | bytes 6291460
  174.9 3.0 collective-permute-start.7
  178.0 18.8 %copy-start.14 = (f32[64,2048]{1,0:T(8,128)S(1)}, f32[64,2048]{1,0:T(8,128)}, u32[]{:S(2)}) copy-start(f32[64,2048]{1,0:T(8,128)} %copy-done.13) | copy-start | bytes 1572868
  178.0 18.8 %copy-start.28 = (bf16[64,2048]{1,0:T(8,128)(2,1)S(1)}, bf16[64,2048]{1,0:T(8,128)(2,1)}, u32[]{:S(2)}) copy-start(bf16[64,2048]{1,0:T(8,128)(2,1)} %get-tuple-element.140.refs_2_) | copy-start | bytes 786436
  196.7 5.8 %copy-start.8 = (bf16[512,768]{1,0:T(8,128)(2,1)S(1)}, bf16[512,768]{1,0:T(8,128)(2,1)}, u32[]{:S(2)}) copy-start(bf16[512,768]{1,0:T(8,128)(2,1)} %copy-done.7) | copy-start | bytes 2359300
  199.0 16.9 %all-to-all-start.4 = ((bf16[4,64,2048]{2,1,0:T(8,128)(2,1)}), bf16[4,64,2048]{2,1,0:T(8,128)(2,1)S(1)}, u32[]{:S(2)}, u32[]{:S(2)}) async-start(bf16[4,64,2048]{2,1,0:T(8,128)(2,1)} %copy-done.27), calls=%async_computation.4 | async-start | bytes 2097152 | tf_op jit(solution)/shard_map/all_to_all | solution.py:775
  215.9 6.4 %collective-permute-start.8 = (bf16[4,64,2048]{2,1,0:T(8,128)(2,1)S(1)}, bf16[4,64,2048]{2,1,0:T(8,128)(2,1)S(1)}, u32[]{:S(2)}, u32[]{:S(2)}) collective-permute-start(bf16[4,64,2048]{2,1,0:T(8,128)(2,1)S(1)} %all-to-all-done.4), channel_id=1, source_target_pairs={{0,8},{8,0},{16,24},{24,16},{32,40},{40,32},{48,56},{56,48},{64,72... | collective-permute-start | bytes 3145736 | tf_op jit(solution)/shard_map/ppermute | solution.py:772
  218.5 23.4 %collective-permute-start.9 = (bf16[256,2048]{1,0:T(8,128)(2,1)}, bf16[256,2048]{1,0:T(8,128)(2,1)}, u32[]{:S(2)}, u32[]{:S(2)}) collective-permute-start(bf16[256,2048]{1,0:T(8,128)(2,1)} %copy-done.43), channel_id=1, source_target_pairs={{0,8},{8,0},{16,24},{24,16},{32,40},{40,32},{48,56},{56,48},{64,72... | collective-permute-start | bytes 3145736 | tf_op jit(solution)/shard_map/ppermute | solution.py:772
  224.4 2.2 copy-start.16
  224.4 2.2 copy-start.20
  224.4 2.4 copy-start.30
  237.2 4.7 %copy-start.26 = (bf16[256,2048]{1,0:T(8,128)(2,1)S(1)}, bf16[256,2048]{1,0:T(8,128)(2,1)}, u32[]{:S(2)}) copy-start(bf16[256,2048]{1,0:T(8,128)(2,1)} %copy-done.25) | copy-start | bytes 3145732
  241.4 2.8 collective-permute-start.10
  255.0 70.6 %all-to-all-start.5 = ((bf16[16,144,1024]{2,1,0:T(8,128)(2,1)}), bf16[16,144,1024]{2,1,0:T(8,128)(2,1)}, u32[]{:S(2)}, u32[]{:S(2)}) async-start(bf16[16,144,1024]{2,1,0:T(8,128)(2,1)} %shard_map.277.refs_3_), calls=%async_computation.6 | async-start | bytes 9437184 | tf_op jit(solution)/shard_map/all_to_all | solution.py:799
  259.7 59.7 %collective-permute-start.14 = (bf16[128,2304]{1,0:T(8,128)(2,1)}, bf16[128,2304]{1,0:T(8,128)(2,1)}, u32[]{:S(2)}, u32[]{:S(2)}) collective-permute-start(bf16[128,2304]{1,0:T(8,128)(2,1)} %reduce-scatter.2.cloned.1.call-done), channel_id=1, source_target_pairs={{8,1},{1,8},{24,17},{17,24},{40,33},{33,40},{56,49},{49,56},{72,65... | collective-permute-start | bytes 1769480 | tf_op jit(solution)/shard_map/ppermute | solution.py:826
  265.3 28.5 %copy-start.12 = (bf16[64,2048]{1,0:T(8,128)(2,1)S(1)}, bf16[64,2048]{1,0:T(8,128)(2,1)}, u32[]{:S(2)}) copy-start(bf16[64,2048]{1,0:T(8,128)(2,1)} %get-tuple-element.141.refs_1_.refs_6_) | copy-start | bytes 786436
  265.3 28.5 %copy-start.15 = (f32[64,2048]{1,0:T(8,128)S(1)}, f32[64,2048]{1,0:T(8,128)}, u32[]{:S(2)}) copy-start(f32[64,2048]{1,0:T(8,128)} %copy-done.13) | copy-start | bytes 1572868
  265.3 28.5 %copy-start.32 = (f32[64,2048]{1,0:T(8,128)S(1)}, f32[64,2048]{1,0:T(8,128)}, u32[]{:S(2)}) copy-start(f32[64,2048]{1,0:T(8,128)} %copy-done.31) | copy-start | bytes 1572868
  266.5 14.3 %collective-permute-start.11 = (bf16[128,2048]{1,0:T(8,128)(2,1)}, bf16[128,2048]{1,0:T(8,128)(2,1)S(1)}, u32[]{:S(2)}, u32[]{:S(2)}) collective-permute-start(bf16[128,2048]{1,0:T(8,128)(2,1)} %get-tuple-element.132), channel_id=1, source_target_pairs={{0,2},{2,4},{4,6},{6,0},{1,3},{3,5},{5,7},{7,1},{8,10},{10,12},{12... | collective-permute-start | bytes 1572872 | tf_op jit(solution)/shard_map/ppermute | solution.py:778
  267.8 25.2 %collective-permute-start.12 = (bf16[128,2048]{1,0:T(8,128)(2,1)}, bf16[128,2048]{1,0:T(8,128)(2,1)S(1)}, u32[]{:S(2)}, u32[]{:S(2)}) collective-permute-start(bf16[128,2048]{1,0:T(8,128)(2,1)} %get-tuple-element.131), channel_id=1, source_target_pairs={{0,4},{2,6},{4,0},{6,2},{1,5},{3,7},{5,1},{7,3},{8,12},{10,14},{12... | collective-permute-start | bytes 1572872 | tf_op jit(solution)/shard_map/ppermute | solution.py:778
  270.4 23.4 %collective-permute-start.13 = (bf16[128,2048]{1,0:T(8,128)(2,1)}, bf16[128,2048]{1,0:T(8,128)(2,1)}, u32[]{:S(2)}, u32[]{:S(2)}) collective-permute-start(bf16[128,2048]{1,0:T(8,128)(2,1)} %get-tuple-element.130), channel_id=1, source_target_pairs={{0,6},{2,0},{4,2},{6,4},{1,7},{3,1},{5,3},{7,5},{8,14},{10,8},{12,... | collective-permute-start | bytes 1572872 | tf_op jit(solution)/shard_map/ppermute | solution.py:778
  320.6 18.0 %collective-permute-start.21 = (bf16[128,2304]{1,0:T(8,128)(2,1)S(1)}, bf16[128,2304]{1,0:T(8,128)(2,1)S(1)}, u32[]{:S(2)}, u32[]{:S(2)}) collective-permute-start(bf16[128,2304]{1,0:T(8,128)(2,1)S(1)} %broadcast_select_fusion.1.refs_2_.b0), channel_id=1, source_target_pairs={{0,2},{2,4},{4,6},{6,0},{1,3},{3,5},{5,7},{7,1},{8,10},{10,12},{12... | collective-permute-start | bytes 1769480 | tf_op jit(solution)/shard_map/ppermute | solution.py:778
  321.9 19.9 %collective-permute-start.22 = (bf16[128,2304]{1,0:T(8,128)(2,1)S(1)}, bf16[128,2304]{1,0:T(8,128)(2,1)}, u32[]{:S(2)}, u32[]{:S(2)}) collective-permute-start(bf16[128,2304]{1,0:T(8,128)(2,1)S(1)} %broadcast_select_fusion.1.refs_2_.b0), channel_id=1, source_target_pairs={{0,4},{2,6},{4,0},{6,2},{1,5},{3,7},{5,1},{7,3},{8,12},{10,14},{12... | collective-permute-start | bytes 1769480 | tf_op jit(solution)/shard_map/ppermute | solution.py:778
  324.5 18.9 %collective-permute-start.23 = (bf16[128,2304]{1,0:T(8,128)(2,1)S(1)}, bf16[128,2304]{1,0:T(8,128)(2,1)}, u32[]{:S(2)}, u32[]{:S(2)}) collective-permute-start(bf16[128,2304]{1,0:T(8,128)(2,1)S(1)} %broadcast_select_fusion.1.refs_2_.b0), channel_id=1, source_target_pairs={{0,6},{2,0},{4,2},{6,4},{1,7},{3,1},{5,3},{7,5},{8,14},{10,8},{12,... | collective-permute-start | bytes 1769480 | tf_op jit(solution)/shard_map/ppermute | solution.py:778
  328.5 8.4 %collective-permute-start.17 = (bf16[144,1024]{1,0:T(8,128)(2,1)S(1)}, bf16[144,1024]{1,0:T(8,128)(2,1)S(1)}, u32[]{:S(2)}, u32[]{:S(2)}) collective-permute-start(bf16[144,1024]{1,0:T(8,128)(2,1)S(1)} %shard_map.280), channel_id=1, source_target_pairs={{8,1},{1,8},{24,17},{17,24},{40,33},{33,40},{56,49},{49,56},{72,65... | collective-permute-start | bytes 884744 | tf_op jit(solution)/shard_map/ppermute | solution.py:826
  331.6 5.8 %collective-permute-start.15 = (bf16[128,2048]{1,0:T(8,128)(2,1)S(1)}, bf16[128,2048]{1,0:T(8,128)(2,1)S(1)}, u32[]{:S(2)}, u32[]{:S(2)}) collective-permute-start(bf16[128,2048]{1,0:T(8,128)(2,1)S(1)} %shard_map.279.refs_1_), channel_id=1, source_target_pairs={{0,8},{8,0},{16,24},{24,16},{32,40},{40,32},{48,56},{56,48},{64,72... | collective-permute-start | bytes 1572872 | tf_op jit(solution)/shard_map/ppermute | solution.py:772
  337.0 14.7 %collective-permute-start.18 = (bf16[144,1024]{1,0:T(8,128)(2,1)S(1)}, bf16[144,1024]{1,0:T(8,128)(2,1)}, u32[]{:S(2)}, u32[]{:S(2)}) collective-permute-start(bf16[144,1024]{1,0:T(8,128)(2,1)S(1)} %broadcast_select_fusion.3.b0), channel_id=1, source_target_pairs={{0,2},{2,4},{4,6},{6,0},{1,3},{3,5},{5,7},{7,1},{8,10},{10,12},{12... | collective-permute-start | bytes 884744 | tf_op jit(solution)/shard_map/ppermute | solution.py:778
  337.5 14.2 %collective-permute-start.19 = (bf16[144,1024]{1,0:T(8,128)(2,1)S(1)}, bf16[144,1024]{1,0:T(8,128)(2,1)}, u32[]{:S(2)}, u32[]{:S(2)}) collective-permute-start(bf16[144,1024]{1,0:T(8,128)(2,1)S(1)} %broadcast_select_fusion.3.b0), channel_id=1, source_target_pairs={{0,4},{2,6},{4,0},{6,2},{1,5},{3,7},{5,1},{7,3},{8,12},{10,14},{12... | collective-permute-start | bytes 884744 | tf_op jit(solution)/shard_map/ppermute | solution.py:778
  338.3 5.1 %copy-start.23 = (bf16[128,3072]{1,0:T(8,128)(2,1)S(1)}, bf16[128,3072]{1,0:T(8,128)(2,1)}, u32[]{:S(2)}) copy-start(bf16[128,3072]{1,0:T(8,128)(2,1)} %w_up.1) | copy-start | bytes 2359300
  338.3 5.1 %copy-start.24 = (bf16[128,3072]{1,0:T(8,128)(2,1)S(1)}, bf16[128,3072]{1,0:T(8,128)(2,1)}, u32[]{:S(2)}) copy-start(bf16[128,3072]{1,0:T(8,128)(2,1)} %w_gate.1) | copy-start | bytes 2359300
  338.5 4.7 %copy-start.47 = (bf16[1,128,2048]{2,1,0:T(8,128)(2,1)}, bf16[1,128,2048]{2,1,0:T(8,128)(2,1)S(1)}, u32[]{:S(2)}) copy-start(bf16[1,128,2048]{2,1,0:T(8,128)(2,1)S(1)} %maximum_select_fusion.1) | copy-start | bytes 1572868
  338.6 4.6 %copy-start.48 = (bf16[1,128,2048]{2,1,0:T(8,128)(2,1)}, bf16[1,128,2048]{2,1,0:T(8,128)(2,1)S(1)}, u32[]{:S(2)}) copy-start(bf16[1,128,2048]{2,1,0:T(8,128)(2,1)S(1)} %maximum_select_fusion.2) | copy-start | bytes 1572868
  338.6 13.1 %collective-permute-start.20 = (bf16[144,1024]{1,0:T(8,128)(2,1)S(1)}, bf16[144,1024]{1,0:T(8,128)(2,1)}, u32[]{:S(2)}, u32[]{:S(2)}) collective-permute-start(bf16[144,1024]{1,0:T(8,128)(2,1)S(1)} %broadcast_select_fusion.3.b0), channel_id=1, source_target_pairs={{0,6},{2,0},{4,2},{6,4},{1,7},{3,1},{5,3},{7,5},{8,14},{10,8},{12,... | collective-permute-start | bytes 884744 | tf_op jit(solution)/shard_map/ppermute | solution.py:778
  341.8 19.8 %collective-permute-start.16 = (bf16[2,128,2048]{2,1,0:T(8,128)(2,1)}, bf16[2,128,2048]{2,1,0:T(8,128)(2,1)}, u32[]{:S(2)}, u32[]{:S(2)}) collective-permute-start(bf16[2,128,2048]{2,1,0:T(8,128)(2,1)} %pad_maximum_fusion), channel_id=1, source_target_pairs={{0,1},{9,8},{16,17},{25,24},{32,33},{41,40},{48,49},{57,56},{64,65... | collective-permute-start | bytes 3145736 | tf_op jit(solution)/shard_map/ppermute | solution.py:943
  343.1 8.6 %copy-start.37 = (bf16[128,1024]{1,0:T(8,128)(2,1)S(1)}, bf16[128,1024]{1,0:T(8,128)(2,1)}, u32[]{:S(2)}) copy-start(bf16[128,1024]{1,0:T(8,128)(2,1)} %wg.1) | copy-start | bytes 786436
  358.0 2.5 collective-permute-start.24
  361.7 3.3 copy-start.1
  (22 other events, 23.4 us)
Sparse Core Ops, SparseCore 0:
  12.8 57.1 all-gather.2
  72.7 75.2 all-gather.4
  169.1 85.8 reduce-scatter.1

commit v7 on v6

--- a/solution.py
+++ b/solution.py
@@ -93,6 +93,32 @@
             dimension_semantics=("arbitrary",) * len(grid), vmem_limit_bytes=VMEM
         ),
         cost_estimate=pl.CostEstimate(flops=flops, bytes_accessed=moved, transcendentals=0),
+    )
+    return lambda *operands: built(*operands, *behind)
+
+
+def prefetched(
+    kernel, grid, in_specs, out_specs, out_shape, flops=1 << 20, scratch=(), behind=()
+):
+    count = len(in_specs) + 1
+
+    def body(*refs):
+        kernel(*refs[:count], *refs[count + len(behind) :])
+
+    built = pl.pallas_call(
+        body,
+        grid_spec=pltpu.PrefetchScalarGridSpec(
+            num_scalar_prefetch=1,
+            grid=grid,
+            in_specs=list(in_specs) + [pl.BlockSpec(memory_space=pl.ANY)] * len(behind),
+            out_specs=out_specs,
+            scratch_shapes=scratch,
+        ),
+        out_shape=out_shape,
+        compiler_params=pltpu.CompilerParams(
+            dimension_semantics=("arbitrary",) * len(grid), vmem_limit_bytes=VMEM
+        ),
+        cost_estimate=pl.CostEstimate(flops=flops, bytes_accessed=8 << 20, transcendentals=0),
     )
     return lambda *operands: built(*operands, *behind)
 
@@ -484,45 +510,104 @@
     )(d_qkv, d_gate, w)
 
 
-def attend_grads_kernel(x_flip, da, db, d_qkv, d_gate, gated, terms, out, outer):
+SIDE = 4
+
+
+def attend_grads_kernel(at, x_flip, da, db, d_qkv, d_gate, gated, terms, *refs):
+    first, second, (whole, outer) = refs[:SIDE], refs[SIDE : 2 * SIDE], refs[2 * SIDE :]
+    step = pl.program_id(0)
+    x = (at[0] + step) % SIDE
     inner, split = d_qkv.shape[1], d_gate.shape[1]
-    block = out.shape[1] - terms.shape[1]
-    for number in range(out.shape[0]):
-        out[number, block:, :] = terms[number].astype(BF16)
+    block = second[0].shape[1]
     term = dot(x_flip[...], d_qkv[...]).astype(BF16)
+    for owner in range(SIDE):
+        whole[owner, :block, :inner] = term[owner * block : (owner + 1) * block]
+        whole[owner, block:, :inner] = terms[owner].astype(BF16)
     gates = dot(x_flip[...], d_gate[...]).astype(BF16)
     spread_blocks(gated, jnp.concatenate([da[...], db[...]], axis=0), outer, 0)
-    for number in range(out.shape[0]):
-        rows = slice(number * block, (number + 1) * block)
-        out[number, :block, :inner] = term[rows]
-        out[number, :block, inner : inner + split] = gates[rows]
-        out[number, :block, inner + split :] = outer[rows, :]
-
-
-def attend_grads(x_flip, da, db, d_qkv, d_gate, gated, terms, behind):
+    for owner in range(SIDE):
+        rows = slice(owner * block, (owner + 1) * block)
+        whole[owner, :block, inner : inner + split] = gates[rows]
+        whole[owner, :block, inner + split :] = outer[rows, :]
+    for turn_by in range(SIDE):
+
+        @pl.when(step == turn_by)
+        def _():
+            first[turn_by][...] = whole[:, :, :inner]
+
+        second[turn_by][x] = whole[(at[1] + turn_by) % SIDE, :block, inner:]
+
+
+def attend_grads(at, x_flip, da, db, d_qkv, d_gate, gated, terms):
     width, length = x_flip.shape
-    owners, extra, columns = terms.shape
-    block = width // owners
-    many = 4
-    slab = pl.BlockSpec((length // 2, many * block), lambda i: (0, i))
-    return call(
+    owners, extra, inner = terms.shape
+    block, outer = width // owners, d_gate.shape[1] + gated.shape[1]
+    place = lambda i, at: (at[0] + i) % SIDE
+    slab = pl.BlockSpec((length // 2, SIDE * block), lambda i, at: (0, place(i, at)))
+    whole = lambda value: pl.BlockSpec(value.shape, lambda i, at: (0, 0))
+    piece = lambda shape: pl.BlockSpec(shape, lambda i, at: (0, 0, 0))
+    shapes = [(SIDE, block + extra, inner)] * SIDE + [(SIDE, block, outer)] * SIDE
+    found = prefetched(
         attend_grads_kernel,
-        (owners // many,),
+        (SIDE,),
         [
-            rowed(many * block, length),
+            pl.BlockSpec((SIDE * block, length), lambda i, at: (place(i, at), 0)),
             slab,
             slab,
-            fixed(d_qkv.shape),
-            fixed(d_gate.shape),
-            fixed(gated.shape),
-            pl.BlockSpec((many, extra, columns), lambda i: (i, 0, 0)),
+            whole(d_qkv),
+            whole(d_gate),
+            whole(gated),
+            pl.BlockSpec((SIDE, extra, inner), lambda i, at: (place(i, at), 0, 0)),
         ],
-        pl.BlockSpec((many, block + extra, columns), lambda i: (i, 0, 0)),
-        struct((owners, block + extra, columns), BF16),
-        2 * length * width * columns,
-        scratch=[pltpu.VMEM((many * block, gated.shape[1]), BF16)],
+        [piece(shape) for shape in shapes],
+        [struct(shape, BF16) for shape in shapes],
+        2 * length * width * (inner + outer),
+        scratch=[
+            pltpu.VMEM((SIDE, block + extra, inner + outer), BF16),
+            pltpu.VMEM((SIDE * block, gated.shape[1]), BF16),
+        ],
+    )(at, x_flip, da, db, d_qkv, d_gate, gated, terms)
+    return found[:SIDE], found[SIDE:]
+
+
+def turn_sums_kernel(at, *refs):
+    parts, outs = refs[:SIDE], refs[SIDE:]
+    for turn_by in range(SIDE):
+        place = (at[0] + turn_by) % SIDE
+        total = sum(part[place].astype(F32) for part in parts)
+        outs[turn_by][...] = total.astype(BF16)
+
+
+def turn_sums(at, parts):
+    shape = parts[0].shape
+    return prefetched(
+        turn_sums_kernel,
+        (1,),
+        [pl.BlockSpec(shape, lambda i, at: (0, 0, 0))] * SIDE,
+        [pl.BlockSpec(shape[1:], lambda i, at: (0, 0))] * SIDE,
+        [struct(shape[1:], BF16)] * SIDE,
+    )(at, *parts)
+
+
+def both_sums_kernel(first, second, out):
+    columns, rows = first[0].shape[1], second[0].shape[0]
+    out[:, :columns] = sum(part[...].astype(F32) for part in first).astype(BF16)
+    out[:rows, columns:] = sum(part[...].astype(F32) for part in second).astype(BF16)
+    out[rows:, columns:] = jnp.zeros((out.shape[0] - rows, out.shape[1] - columns), BF16)
+
+
+def both_sums(first, second, behind):
+    rows, columns = first[0].shape
+    wide = (rows, columns + second[0].shape[1])
+    return call(
+        lambda *refs: both_sums_kernel(refs[:SIDE], refs[SIDE : 2 * SIDE], refs[-1]),
+        (1,),
+        [fixed(part.shape) for part in (*first, *second)],
+        fixed(wide),
+        struct(wide, BF16),
+        1 << 20,
         behind=behind,
-    )(x_flip, da, db, d_qkv, d_gate, gated, terms)
+    )(*first, *second)
 
 
 def middle_kernel(parts, x, middle, spread):
@@ -590,36 +675,6 @@
         struct(wide, BF16),
         1 << 20,
     )(*parts, middle, d_middle, x)
-
-
-def sum_kernel(parts, out):
-    out[...] = jnp.sum(parts[...].astype(F32), axis=0).astype(BF16)
-
-
-def sum_step(parts, behind):
-    return call(
-        sum_kernel,
-        (1,),
-        [fixed(parts.shape)],
-        fixed(parts.shape[1:]),
-        struct(parts.shape[1:], BF16),
-        1 << 20,
-        behind=behind,
-    )(parts)
-
-
-def prefetched(kernel, grid, in_specs, out_specs, out_shape):
-    return pl.pallas_call(
-        kernel,
-        grid_spec=pltpu.PrefetchScalarGridSpec(
-            num_scalar_prefetch=1, grid=grid, in_specs=in_specs, out_specs=out_specs
-        ),
-        out_shape=out_shape,
-        compiler_params=pltpu.CompilerParams(
-            dimension_semantics=("arbitrary",) * len(grid), vmem_limit_bytes=VMEM
-        ),
-        cost_estimate=pl.CostEstimate(flops=1 << 20, bytes_accessed=8 << 20, transcendentals=0),
-    )
 
 
 def copy_kernel(core, source, out):
@@ -795,8 +850,21 @@
             value, PLANE, scatter_dimension=0, tiled=True, axis_index_groups=planes
         )
 
-    def plane_exchange(value):
-        return lax.all_to_all(value, PLANE, 0, 0, axis_index_groups=planes)
+    def x_turn(value, by):
+        perm = [(s, (s + by * SIDE) % n_shard) for s in range(n_shard)]
+        return lax.ppermute(value, "shard", perm)
+
+    def y_turn(value, by):
+        perm = []
+        for s in range(n_shard):
+            for tp in range(n_tp):
+                y = (s // 2 % 2) * n_tp + tp
+                to = (y + by) % SIDE
+                perm.append((s * n_tp + tp, (s // 4 * 4 + to // n_tp * 2 + s % 2) * n_tp + to % n_tp))
+        return lax.ppermute(value, PLANE, perm)
+
+    def turned(turn_along, pieces):
+        return [pieces[0]] + [turn_along(pieces[by], by) for by in range(1, SIDE)]
 
     def shards(
         tokens,
@@ -901,14 +969,18 @@
             return jnp.pad(vector.reshape(n_shard, 1, -1), ((0, 0), (0, 15), (0, 0)))
 
         wide_terms = jnp.concatenate([spread_terms(terms[0]), spread_terms(terms[1])], axis=2)
-        wide_terms = jnp.pad(wide_terms, ((0, 0), (0, 0), (0, 8 * HD - 2 * head_rows)))
-        attn = attend_grads(x_flip, da, db, d_qkv, d_gate_pre, gated, wide_terms, ())
-        in_mine, in_other = input_back(d_qkv, d_gate_pre, w1, (attn,))
+        wide_terms = jnp.pad(wide_terms, ((0, 0), (0, 0), (0, 4 * HD - 2 * head_rows)))
+        x_at = (lax.axis_index("shard") // SIDE).astype(jnp.int32)
+        y_at = (lax.axis_index("shard") // 2 % 2 * n_tp + tp).astype(jnp.int32)
+        first, second = attend_grads(
+            jnp.stack([x_at, y_at]), x_flip, da, db, d_qkv, d_gate_pre, gated, wide_terms
+        )
+        in_mine, in_other = input_back(d_qkv, d_gate_pre, w1, (first[0],))
         layer_half, in_half = tree_half(layer_mine, layer_other), tree_half(in_mine, in_other)
-        attn, layer_half, in_half, grad_ffn = lax.optimization_barrier(
-            (attn, layer_half, in_half, grad_ffn)
-        )
-        attn_parts = plane_exchange(attn)
+        first = turn_sums(y_at.reshape(1), turned(x_turn, first))
+        second = turn_sums(x_at.reshape(1), turned(y_turn, second))
+        first, second, grad_ffn = lax.optimization_barrier((first, second, grad_ffn))
+        first, second = turned(y_turn, first), turned(x_turn, second)
 
         def owners(block):
             block = swapped(block)
@@ -927,7 +999,7 @@
         ]
         ends = ends_step(parts, middle, d_middle, own_x)
         ffn_blocks = owners(grad_ffn)
-        attn_sum = sum_step(attn_parts, (ends, ffn_blocks[0]))
+        attn_sum = both_sums(first, second, (ends, ffn_blocks[0]))
         ends, attn_sum = lax.optimization_barrier((ends, attn_sum))
         sibling = core_swap(ends)
 

time: 378 us -> 407 us (1.077)
  starting transfers between devices: 54.6 us -> 72.7 us
  other arithmetic: 15.5 us -> 22.7 us
  local copies, waits for them, and re-layouts: 31.8 us -> 37.7 us
    ppermute x0 -> x12, waiting for transfers between devices: none -> 24.1 us  [the longest x6 21.2 us: y_turn(): return lax.ppermute(value, PLANE, perm)]
    ppermute x0 -> x12, starting transfers between devices: none -> 23.8 us  [the longest x6 17.2 us: x_turn(): return lax.ppermute(value, 'shard', perm)]
    ppermute x3, waiting for transfers between devices: 35.7 us -> 12.1 us  [swapped(): return jnp.where(native, value, lax.ppermute(value, PLANE, swap_perm))]
    ppermute x9, waiting for transfers between devices: 25.8 us -> 36.6 us  [ctx_turn(): lax.ppermute(value, 'ctx', [(i, (i + by) % n_ctx) for i in range(n_ctx)])]
    reduce_scatter x1, waiting for transfers between devices: 10.4 us -> 0.01 us  [plane_scatter(): lax.psum_scatter(value, PLANE, scatter_dimension=0, tiled=True, axis_inde...]
    pallas_call x4 -> x7, Pallas kernels: 15.2 us -> 25.5 us  [prefetched(): return lambda *operands: built(*operands, *behind)]
    pallas_call x16 -> x15, Pallas kernels: 64.9 us -> 56.9 us  [call(): return lambda *operands: built(*operands, *behind)]
    unnamed x110 -> x163, local copies, waits for them, and re-layouts: 21.8 us -> 28.9 us
  transfers between devices with their start and end apart: 32 -> 43, of which waited for: 22 -> 26; matrix products, arithmetic and copies ran while one was open for 5% -> 6% of each run, Pallas kernels for 17% -> 16%
where the time goes in v7:
time: 407 us; the launch traced here: 403 us
  waiting for transfers between devices  139 us (34%)
  Pallas kernels  82.4 us (20%)
  starting transfers between devices  72.7 us (18%)
  local copies, waits for them, and re-layouts  37.7 us (9%)
  blocking collectives  34.1 us (8%)
  other arithmetic  22.7 us (6%)
  between operations  14.7 us (4%)
    pallas_call x15, Pallas kernels, call(): return lambda *operands: built(*operands, *behind)  56.9 us
    all_to_all x3, waiting for transfers between devices, ctx_exchange(): return lax.all_to_all(value, 'ctx', 0, 0)  43.2 us
    ppermute x9, waiting for transfers between devices, ctx_turn(): lax.ppermute(value, 'ctx', [(i, (i + by) % n_ctx) for i in range(n_ctx)])  36.6 us
    all_to_all x2, blocking collectives, ctx_exchange(): return lax.all_to_all(value, 'ctx', 0, 0)  34.1 us
    unnamed x163, local copies, waits for them, and re-layouts  28.9 us
    pallas_call x7, Pallas kernels, prefetched(): return lambda *operands: built(*operands, *behind)  25.5 us
    ppermute x6, waiting for transfers between devices, y_turn(): return lax.ppermute(value, PLANE, perm)  21.2 us
    ppermute x6, starting transfers between devices, x_turn(): return lax.ppermute(value, 'shard', perm)  17.2 us
  transfers between devices with their start and end apart: 43, of which 26 were waited for; matrix products, arithmetic and copies ran while one was open for 6% of the time, Pallas kernels for 16%

profile of v7, /device:TPU:1, one launch (start us, length us, event | category | flops | bytes accessed | tf_op | source)
XLA Modules:
  0.0 402.9 jit_solution(8988959708327801907)
XLA Ops:
  15.2 4.5 %collective-permute-start.6 = (bf16[128,2304]{1,0:T(8,128)(2,1)S(1)}, bf16[128,2304]{1,0:T(8,128)(2,1)S(1)}, u32[]{:S(2)}, u32[]{:S(2)}) collective-permute-start(bf16[128,2304]{1,0:T(8,128)(2,1)S(1)} %pad_maximum_fusion.1), channel_id=1, source_target_pairs={{8,1},{1,8},{24,17},{17,24},{40,33},{33,40},{56,49},{49,56},{72,65... | collective-permute-start | bytes 1769480 | tf_op jit(solution)/shard_map/ppermute | solution.py:894
  19.8 7.5 %collective-permute-done.6 = bf16[128,2304]{1,0:T(8,128)(2,1)S(1)} collective-permute-done((bf16[128,2304]{1,0:T(8,128)(2,1)S(1)}, bf16[128,2304]{1,0:T(8,128)(2,1)S(1)}, u32[]{:S(2)}, u32[]{:S(2)}) %collective-permute-start.6) | collective-permute-done | bytes 589856 | tf_op jit(solution)/shard_map/ppermute | solution.py:894
  28.5 1.9 collective-permute-done
  31.4 1.7 broadcast_in_dim.20
  33.0 5.3 %all-to-all-start = ((bf16[4,128,2048]{2,1,0:T(8,128)(2,1)}), bf16[4,128,2048]{2,1,0:T(8,128)(2,1)S(1)}, u32[]{:S(2)}, u32[]{:S(2)}) async-start(bf16[4,128,2048]{2,1,0:T(8,128)(2,1)} %broadcast_in_dim.20), calls=%async_computation | async-start | bytes 4194304 | tf_op jit(solution)/shard_map/all_to_all | solution.py:830
  38.9 25.4 %all-to-all-done.refs_0_.refs_2_.refs_1_ = bf16[4,128,2048]{2,1,0:T(8,128)(2,1)S(1)} async-done(((bf16[4,128,2048]{2,1,0:T(8,128)(2,1)}), bf16[4,128,2048]{2,1,0:T(8,128)(2,1)S(1)}, u32[]{:S(2)}, u32[]{:S(2)}) %all-to-all-start) | async-done | bytes 2097184 | tf_op jit(solution)/shard_map/all_to_all | solution.py:830
  68.0 1.5 collective-permute-done.1.refs_1_.refs_3_.refs_2_
  70.5 2.5 shard_map.263
  73.8 4.1 %collective-permute-done.3.refs_2_ = bf16[8,128,1152]{2,1,0:T(8,128)(2,1)} collective-permute-done((bf16[8,128,1152]{2,1,0:T(8,128)(2,1)S(1)}, bf16[8,128,1152]{2,1,0:T(8,128)(2,1)}, u32[]{:S(2)}, u32[]{:S(2)}) %collective-permute-start.3) | collective-permute-done | bytes 2359328 | tf_op jit(solution)/shard_map/ppermute | solution.py:827
  78.0 5.1 %shard_map.264 = bf16[8,2,128,1152]{3,2,1,0:T(8,128)(2,1)} custom-call(s32[1]{0:T(128)} %bitcast.16.refs_0_, bf16[8,2,128,1152]{3,2,1,0:T(8,128)(2,1)} %bitcast.100, bf16[8,128,1152]{2,1,0:T(8,128)(2,1)} %collective-permute-done.3.refs_2_), custom_call_target="tpu_custom_call" | custom-call | flops 1048576 | bytes 8388608 | tf_op jit(solution)/shard_map/pallas_call | solution.py:123
  83.1 5.8 %shard_map.265 = (bf16[512,2048]{1,0:T(8,128)(2,1)S(1)}, f32[512,384]{1,0:T(8,128)S(1)}, bf16[512,512]{1,0:T(8,128)(2,1)S(1)}, f32[512,256]{1,0:T(8,128)S(1)}, f32[16,128]{1,0:T(8,128)S(1)}) custom-call(bf16[4,128,2048]{2,1,0:T(8,128)(2,1)} %copy-done.68, bf16[4,128,2048]{2,1,0:T(8,128)(2,1)} %collective-permute-done.1.refs_1_.refs_3_.refs_2_, ...), custom_call_target="tpu_custom_call" | custom-call | flops 1610612736 | bytes 8388608 | tf_op jit(solution)/shard_map/pallas_call | solution.py:97
  90.3 6.4 %shard_map.266 = (f32[2,512,512]{2,1,0:T(8,128)}, f32[512,256]{1,0:T(8,128)S(1)}, bf16[512,256]{1,0:T(8,128)(2,1)S(1)}, bf16[256,2048]{1,0:T(8,128)(2,1)S(1)}, bf16[256,2048]{1,0:T(8,128)(2,1)S(1)}) custom-call(bf16[512,512]{1,0:T(8,128)(2,1)S(1)} %get-tuple-element.94.refs_0_.refs_1_, f32[512,256]{1,0:T(8,128)S(1)} %get-tuple-element.95.refs_1_.refs_3_, ...), custom_call_target="tpu_custom_call" | custom-call | flops 805306368 | bytes 8388608 | tf_op jit(solution)/shard_map/pallas_call | solution.py:97
  97.2 2.3 collective-permute-done.4
  100.8 4.2 %all-to-all-start.1 = ((bf16[4,64,2048]{2,1,0:T(8,128)(2,1)}), bf16[4,64,2048]{2,1,0:T(8,128)(2,1)S(1)}, u32[]{:S(2)}, u32[]{:S(2)}) async-start(bf16[4,64,2048]{2,1,0:T(8,128)(2,1)} %bitcast.19), calls=%async_computation.1 | async-start | bytes 2097152 | tf_op jit(solution)/shard_map/all_to_all | solution.py:830
  105.8 1.6 copy-done.19
  108.8 10.8 %all-to-all-done.1.refs_0_ = bf16[4,64,2048]{2,1,0:T(8,128)(2,1)S(1)} async-done(((bf16[4,64,2048]{2,1,0:T(8,128)(2,1)}), bf16[4,64,2048]{2,1,0:T(8,128)(2,1)S(1)}, u32[]{:S(2)}, u32[]{:S(2)}) %all-to-all-start.1) | async-done | bytes 1048608 | tf_op jit(solution)/shard_map/all_to_all | solution.py:830
  121.6 15.9 %all_to_all.25 = bf16[4,64,2048]{2,1,0:T(8,128)(2,1)S(1)} all-to-all(bf16[4,64,2048]{2,1,0:T(8,128)(2,1)S(1)} %get-tuple-element.101), channel_id=1, replica_groups=mesh['shard'=16,'ctx'=4,'tp'=2] {'ctx'}, dimensions={0} | all-to-all | bytes 2097152 | tf_op jit(solution)/shard_map/all_to_all | solution.py:830
  137.5 2.6 collective-permute-start.5
  140.1 2.3 collective-permute-done.5
  146.0 2.6 all-gather.5.cloned.1.call-done.refs_4_.refs_5_.refs_6_.refs_2_.refs_3_.refs_1_
  149.8 10.6 %shard_map.270 = (bf16[512,768]{1,0:T(8,128)(2,1)S(1)}, bf16[512,768]{1,0:T(8,128)(2,1)S(1)}, bf16[512,768]{1,0:T(8,128)(2,1)S(1)}) custom-call(bf16[256,2048]{1,0:T(8,128)(2,1)S(1)} %bitcast.85, bf16[256,2048]{1,0:T(8,128)(2,1)S(1)} %bitcast.91, bf16[4,128,2048]{2,1,0:T(8,128)(2,1)} %copy-done.68, ...), custom_call_target="tpu_custom_call" | custom-call | flops 4831838208 | bytes 8388608 | tf_op jit(solution)/shard_map/pallas_call | solution.py:97
  160.4 8.2 %shard_map.271.refs_4_ = bf16[2048,2304]{1,0:T(8,128)(2,1)} custom-call(bf16[2048,512]{1,0:T(8,128)(2,1)S(1)} %copy-done.3, bf16[4,128,2048]{2,1,0:T(8,128)(2,1)} %copy-done.68, bf16[4,128,2048]{2,1,0:T(8,128)(2,1)} %collective-permute-done.1.refs_1_.refs_3_.refs_2_, bf16[512,768]{1,0:T(8,128)(2,1)S(1)} %get-tuple-element.102.refs_3_.refs_0_, ...), custom_call_target="tpu_custom_call" | custom-call | flops 4831838208 | bytes 8388608 | tf_op jit(solution)/shard_map/pallas_call | solution.py:97
  170.6 6.0 %shard_map.272 = (bf16[256,2048]{1,0:T(8,128)(2,1)S(1)}, bf16[256,2048]{1,0:T(8,128)(2,1)S(1)}) custom-call(bf16[512,768]{1,0:T(8,128)(2,1)S(1)} %get-tuple-element.102.refs_3_.refs_0_, bf16[512,768]{1,0:T(8,128)(2,1)S(1)} %copy-done.9, bf16[2048,2304]{1,0:T(8,128)(2,1)} %all-gather.5.cloned.1.call-done.refs_4_.refs_5_.refs_6_.refs_2_.refs_3_.refs_1_, ...), custom_call_target="tpu_custom_call" | custom-call | flops 3221225472 | bytes 8388608 | tf_op jit(solution)/shard_map/pallas_call | solution.py:97
  177.3 2.3 collective-permute-done.7
  180.0 18.2 %all_to_all.26.refs_0_ = bf16[4,64,2048]{2,1,0:T(8,128)(2,1)S(1)} all-to-all(bf16[4,64,2048]{2,1,0:T(8,128)(2,1)S(1)} %bitcast.86), channel_id=1, replica_groups=mesh['shard'=16,'ctx'=4,'tp'=2] {'ctx'}, dimensions={0} | all-to-all | bytes 2097152 | tf_op jit(solution)/shard_map/all_to_all | solution.py:830
  200.4 3.5 all-to-all-start.4
  204.0 4.3 %shard_map.274 = (bf16[256,2048]{1,0:T(8,128)(2,1)S(1)}, bf16[256,2048]{1,0:T(8,128)(2,1)S(1)}) custom-call(bf16[512,768]{1,0:T(8,128)(2,1)S(1)} %get-tuple-element.104.refs_5_.refs_0_, bf16[2048,2304]{1,0:T(8,128)(2,1)} %all-gather.5.cloned.1.call-done.refs_4_.refs_5_.refs_6_.refs_2_.refs_3_.refs_1_, bf16[4,64,2048]{2,1,0:T(8,128)(2,1)S(1)} %bitcast.87), custom_call_target="tpu_custom_call" | custom-call | flops 1610612736 | bytes 8388608 | tf_op jit(solution)/shard_map/pallas_call | solution.py:97
  210.3 7.0 %all-to-all-done.4 = bf16[4,64,2048]{2,1,0:T(8,128)(2,1)S(1)} async-done(((bf16[4,64,2048]{2,1,0:T(8,128)(2,1)}), bf16[4,64,2048]{2,1,0:T(8,128)(2,1)S(1)}, u32[]{:S(2)}, u32[]{:S(2)}) %all-to-all-start.4) | async-done | bytes 1048608 | tf_op jit(solution)/shard_map/all_to_all | solution.py:830
  217.3 2.7 collective-permute-start.9
  220.1 2.8 collective-permute-done.9
  222.8 1.4 copy-done.23
  225.3 2.2 shard_map.275
  227.7 3.1 shard_map.276
  232.1 7.0 %shard_map.277 = (bf16[4,144,512]{2,1,0:T(8,128)(2,1)S(1)}, bf16[4,144,512]{2,1,0:T(8,128)(2,1)}, bf16[4,144,512]{2,1,0:T(8,128)(2,1)}, bf16[4,144,512]{2,1,0:T(...) custom-call(s32[2]{0:T(128)S(1)} %pad_add_fusion.3.refs_0_, ...), custom_call_target="tpu_custom_call" | custom-call | flops 2147483648 | bytes 8388608 | tf_op jit(solution)/shard_map/pallas_call | solution.py:123
  239.1 1.4 collective-permute-start.17
  240.5 2.4 collective-permute-start.18
  243.9 5.2 %shard_map.278 = (bf16[256,2048]{1,0:T(8,128)(2,1)S(1)}, bf16[256,2048]{1,0:T(8,128)(2,1)}) custom-call(bf16[512,512]{1,0:T(8,128)(2,1)S(1)} %copy-done.42, bf16[512,256]{1,0:T(8,128)(2,1)S(1)} %copy-done.49, bf16[2048,1152]{1,0:T(8,128)(2,1)} %bitcast.98, bf16[4,144,512]{2,1,0:T(8,128)(2,1)S(1)} %get-tuple-element.123.refs_3_.refs_1_), custom_call_target="tpu_custom_call" | custom-call | flops 1610612736 | bytes 8388608 | tf_op jit(solution)/shard_map/pallas_call | solution.py:97
  250.3 1.7 collective-permute-start.15
  251.9 11.5 %collective-permute-done.17.refs_2_ = bf16[4,128,512]{2,1,0:T(8,128)(2,1)S(1)} collective-permute-done((bf16[4,128,512]{2,1,0:T(8,128)(2,1)S(1)}, bf16[4,128,512]{2,1,0:T(8,128)(2,1)S(1)}, u32[]{:S(2)}, u32[]{:S(2)}) %collective-permute-start.17) | collective-permute-done | bytes 524320 | tf_op jit(solution)/shard_map/ppermute | solution.py:864
  264.3 13.5 %collective-permute-start.16 = (bf16[4,144,512]{2,1,0:T(8,128)(2,1)}, bf16[4,144,512]{2,1,0:T(8,128)(2,1)}, u32[]{:S(2)}, u32[]{:S(2)}) collective-permute-start(bf16[4,144,512]{2,1,0:T(8,128)(2,1)} %get-tuple-element.129), channel_id=1, source_target_pairs={{0,96},{8,104},{16,112},{24,120},{32,0},{40,8},{48,16},{56,24},{64... | collective-permute-start | bytes 1769480 | tf_op jit(solution)/shard_map/ppermute | solution.py:855
  277.8 2.7 add_convert_fusion.1
  280.5 9.7 %collective-permute-done.19.refs_4_ = bf16[4,128,512]{2,1,0:T(8,128)(2,1)S(1)} collective-permute-done((bf16[4,128,512]{2,1,0:T(8,128)(2,1)}, bf16[4,128,512]{2,1,0:T(8,128)(2,1)S(1)}, u32[]{:S(2)}, u32[]{:S(2)}) %collective-permute-start.19) | collective-permute-done | bytes 524320 | tf_op jit(solution)/shard_map/ppermute | solution.py:864
  290.1 1.9 shard_map.281
  294.0 1.5 shard_map.280
  297.5 2.6 add_convert_fusion
  300.1 3.4 collective-permute-start.26
  303.5 2.8 fusion.1
  306.3 2.7 collective-permute-start.13
  309.0 23.2 %collective-permute-done.11.refs_1_ = bf16[128,2048]{1,0:T(8,128)(2,1)S(1)} collective-permute-done((bf16[128,2048]{1,0:T(8,128)(2,1)}, bf16[128,2048]{1,0:T(8,128)(2,1)S(1)}, u32[]{:S(2)}, u32[]{:S(2)}) %collective-permute-start.11) | collective-permute-done | bytes 524320 | tf_op jit(solution)/shard_map/ppermute | solution.py:833
  333.4 2.6 collective-permute-start.22
  339.0 2.7 collective-permute-done.24.refs_6_
  342.7 2.7 collective-permute-start.34
  346.5 5.2 %collective-permute-start.29 = (bf16[144,1024]{1,0:T(8,128)(2,1)S(1)}, bf16[144,1024]{1,0:T(8,128)(2,1)S(1)}, u32[]{:S(2)}, u32[]{:S(2)}) collective-permute-start(bf16[144,1024]{1,0:T(8,128)(2,1)S(1)} %shard_map.282), channel_id=1, source_target_pairs={{8,1},{1,8},{24,17},{17,24},{40,33},{33,40},{56,49},{49,56},{72,65... | collective-permute-start | bytes 884744 | tf_op jit(solution)/shard_map/ppermute | solution.py:894
  351.9 4.5 %collective-permute-done.29 = bf16[144,1024]{1,0:T(8,128)(2,1)S(1)} collective-permute-done((bf16[144,1024]{1,0:T(8,128)(2,1)S(1)}, bf16[144,1024]{1,0:T(8,128)(2,1)S(1)}, u32[]{:S(2)}, u32[]{:S(2)}) %collective-permute-start.29) | collective-permute-done | bytes 294944 | tf_op jit(solution)/shard_map/ppermute | solution.py:894
  356.5 1.9 collective-permute-start.30
  359.0 2.2 collective-permute-start.32
  362.3 6.8 %collective-permute-done.34.refs_3_ = bf16[128,2304]{1,0:T(8,128)(2,1)S(1)} collective-permute-done((bf16[128,2304]{1,0:T(8,128)(2,1)S(1)}, bf16[128,2304]{1,0:T(8,128)(2,1)S(1)}, u32[]{:S(2)}, u32[]{:S(2)}) %collective-permute-start.34) | collective-permute-done | bytes 589856 | tf_op jit(solution)/shard_map/ppermute | solution.py:833
  371.5 1.7 collective-permute-done.35.refs_4_
  374.3 4.1 %shard_map.284 = (f32[128,3072]{1,0:T(8,128)}, f32[128,3072]{1,0:T(8,128)}, f32[3072,128]{1,0:T(8,128)}, f32[128,128]{1,0:T(8,128)S(1)}) custom-call(s32[1]{0:T(128)} %bitcast.42.refs_0_, bf16[128,2304]{1,0:T(8,128)(2,1)S(1)} %broadcast_select_fusion.1.refs_9_.refs_1_, bf16[128,2304]{1,0:T(8,128)(2,1)S(1)} %collective-permute-done.33.refs_2_, ...), custom_call_target="tpu_custom_call" | custom-call | flops 1048576 | bytes 8388608 | tf_op jit(solution)/shard_map/pallas_call | solution.py:123
  378.7 3.2 collective-permute-done.31.refs_3_
  385.8 3.4 shard_map.283
  390.1 1.9 collective-permute-done.36
  393.0 1.7 broadcast_select_fusion
  394.8 1.6 fusion.8
  (285 shorter events, 62.8 us)
Async XLA Ops:
  7.2 63.3 %all-gather.3.cloned.1.call-start = ((), (), s32[]{:S(2)}) async-start(), calls=%async_computation.6 | async-start | bytes 5013504 | tf_op jit(solution)/shard_map/all_gather | solution.py:846
  13.2 135.3 %all-gather.5.cloned.1.call-start = ((), (), s32[]{:S(2)}) async-start(), calls=%async_computation.7 | async-start | bytes 10027008 | tf_op jit(solution)/shard_map/all_gather | solution.py:846
  15.0 13.2 %copy-start.74 = (bf16[128,2048]{1,0:T(8,128)(2,1)S(1)}, bf16[128,2048]{1,0:T(8,128)(2,1)}, u32[]{:S(2)}) copy-start(bf16[128,2048]{1,0:T(8,128)(2,1)} %param.31) | copy-start | bytes 1572868
  15.0 13.3 %copy-start.75 = (bf16[128,2048]{1,0:T(8,128)(2,1)S(1)}, bf16[128,2048]{1,0:T(8,128)(2,1)}, u32[]{:S(2)}) copy-start(bf16[128,2048]{1,0:T(8,128)(2,1)} %param.16) | copy-start | bytes 1572868
  15.2 12.1 %collective-permute-start.6 = (bf16[128,2304]{1,0:T(8,128)(2,1)S(1)}, bf16[128,2304]{1,0:T(8,128)(2,1)S(1)}, u32[]{:S(2)}, u32[]{:S(2)}) collective-permute-start(bf16[128,2304]{1,0:T(8,128)(2,1)S(1)} %pad_maximum_fusion.1), channel_id=1, source_target_pairs={{8,1},{1,8},{24,17},{17,24},{40,33},{33,40},{56,49},{49,56},{72,65... | collective-permute-start | bytes 1769480 | tf_op jit(solution)/shard_map/ppermute | solution.py:894
  28.4 2.0 collective-permute-start
  33.0 31.3 %all-to-all-start = ((bf16[4,128,2048]{2,1,0:T(8,128)(2,1)}), bf16[4,128,2048]{2,1,0:T(8,128)(2,1)S(1)}, u32[]{:S(2)}, u32[]{:S(2)}) async-start(bf16[4,128,2048]{2,1,0:T(8,128)(2,1)} %broadcast_in_dim.20), calls=%async_computation | async-start | bytes 4194304 | tf_op jit(solution)/shard_map/all_to_all | solution.py:830
  38.3 27.6 %collective-permute-start.2 = (s32[2,13]{1,0:T(2,128)S(1)}, s32[2,13]{1,0:T(2,128)S(1)}, u32[]{:S(2)}, u32[]{:S(2)}) collective-permute-start(s32[2,13]{1,0:T(2,128)S(1)} %pad_add_fusion.2), channel_id=1, source_target_pairs={{0,8},{8,0},{16,24},{24,16},{32,40},{40,32},{48,56},{56,48},{64,72... | collective-permute-start | bytes 320 | tf_op jit(solution)/shard_map/ppermute | solution.py:827
  64.3 5.2 %collective-permute-start.1 = (bf16[4,128,2048]{2,1,0:T(8,128)(2,1)S(1)}, bf16[4,128,2048]{2,1,0:T(8,128)(2,1)}, u32[]{:S(2)}, u32[]{:S(2)}) collective-permute-start(bf16[4,128,2048]{2,1,0:T(8,128)(2,1)S(1)} %all-to-all-done.refs_0_.refs_2_.refs_1_), channel_id=1, source_target_pairs={{0,8},{8,0},{16,24},{24,16},{32,40},{40,32},{48,56},{56,48},{64,72... | collective-permute-start | bytes 6291464 | tf_op jit(solution)/shard_map/ppermute | solution.py:827
  68.0 15.1 %copy-start.10 = (f32[512,128]{1,0:T(8,128)}, f32[512,128]{1,0:T(8,128)S(1)}, u32[]{:S(2)}) copy-start(f32[512,128]{1,0:T(8,128)S(1)} %get-tuple-element.92.refs_4_.refs_5_) | copy-start | bytes 786436
  72.9 5.0 %collective-permute-start.3 = (bf16[8,128,1152]{2,1,0:T(8,128)(2,1)S(1)}, bf16[8,128,1152]{2,1,0:T(8,128)(2,1)}, u32[]{:S(2)}, u32[]{:S(2)}) collective-permute-start(bf16[8,128,1152]{2,1,0:T(8,128)(2,1)S(1)} %shard_map.263), channel_id=1, source_target_pairs={{0,8},{8,0},{16,24},{24,16},{32,40},{40,32},{48,56},{56,48},{64,72... | collective-permute-start | bytes 7077896 | tf_op jit(solution)/shard_map/ppermute | solution.py:827
  96.7 2.8 collective-permute-start.4
  100.8 18.7 %all-to-all-start.1 = ((bf16[4,64,2048]{2,1,0:T(8,128)(2,1)}), bf16[4,64,2048]{2,1,0:T(8,128)(2,1)S(1)}, u32[]{:S(2)}, u32[]{:S(2)}) async-start(bf16[4,64,2048]{2,1,0:T(8,128)(2,1)} %bitcast.19), calls=%async_computation.1 | async-start | bytes 2097152 | tf_op jit(solution)/shard_map/all_to_all | solution.py:830
  105.0 195.1 %reduce-scatter.2.cloned.1.call-start = ((), (), s32[]{:S(2)}) async-start(), calls=%async_computation.8 | async-start | bytes 10027008 | tf_op jit(solution)/shard_map/reduce_scatter | solution.py:849
  108.8 28.8 %copy-start.4 = (bf16[2048,512]{1,0:T(8,128)(2,1)}, bf16[2048,512]{1,0:T(8,128)(2,1)S(1)}, u32[]{:S(2)}) copy-start(bf16[2048,512]{1,0:T(8,128)(2,1)S(1)} %shard_map.267.refs_2_.refs_1_) | copy-start | bytes 6291460
  137.5 4.8 %collective-permute-start.5 = (bf16[4,64,2048]{2,1,0:T(8,128)(2,1)S(1)}, bf16[4,64,2048]{2,1,0:T(8,128)(2,1)S(1)}, u32[]{:S(2)}, u32[]{:S(2)}) collective-permute-start(bf16[4,64,2048]{2,1,0:T(8,128)(2,1)S(1)} %all_to_all.25), channel_id=1, source_target_pairs={{0,8},{8,0},{16,24},{24,16},{32,40},{40,32},{48,56},{56,48},{64,72... | collective-permute-start | bytes 3145736 | tf_op jit(solution)/shard_map/ppermute | solution.py:827
  176.5 3.0 collective-permute-start.7
  179.6 18.6 %copy-start.15 = (f32[64,2048]{1,0:T(8,128)S(1)}, f32[64,2048]{1,0:T(8,128)}, u32[]{:S(2)}) copy-start(f32[64,2048]{1,0:T(8,128)} %copy-done.14) | copy-start | bytes 1572868
  179.6 18.6 %copy-start.30 = (bf16[64,2048]{1,0:T(8,128)(2,1)S(1)}, bf16[64,2048]{1,0:T(8,128)(2,1)}, u32[]{:S(2)}) copy-start(bf16[64,2048]{1,0:T(8,128)(2,1)} %get-tuple-element.182.refs_2_) | copy-start | bytes 786436
  200.4 16.8 %all-to-all-start.4 = ((bf16[4,64,2048]{2,1,0:T(8,128)(2,1)}), bf16[4,64,2048]{2,1,0:T(8,128)(2,1)S(1)}, u32[]{:S(2)}, u32[]{:S(2)}) async-start(bf16[4,64,2048]{2,1,0:T(8,128)(2,1)} %copy-done.29), calls=%async_computation.4 | async-start | bytes 2097152 | tf_op jit(solution)/shard_map/all_to_all | solution.py:830
  217.3 5.5 %collective-permute-start.9 = (bf16[4,64,2048]{2,1,0:T(8,128)(2,1)S(1)}, bf16[4,64,2048]{2,1,0:T(8,128)(2,1)S(1)}, u32[]{:S(2)}, u32[]{:S(2)}) collective-permute-start(bf16[4,64,2048]{2,1,0:T(8,128)(2,1)S(1)} %all-to-all-done.4), channel_id=1, source_target_pairs={{0,8},{8,0},{16,24},{24,16},{32,40},{40,32},{48,56},{56,48},{64,72... | collective-permute-start | bytes 3145736 | tf_op jit(solution)/shard_map/ppermute | solution.py:827
  220.1 30.2 %collective-permute-start.8 = (bf16[256,2048]{1,0:T(8,128)(2,1)}, bf16[256,2048]{1,0:T(8,128)(2,1)}, u32[]{:S(2)}, u32[]{:S(2)}) collective-permute-start(bf16[256,2048]{1,0:T(8,128)(2,1)} %copy-done.54), channel_id=1, source_target_pairs={{0,8},{8,0},{16,24},{24,16},{32,40},{40,32},{48,56},{56,48},{64,72... | collective-permute-start | bytes 3145736 | tf_op jit(solution)/shard_map/ppermute | solution.py:827
  239.1 24.4 %copy-start.55 = (bf16[4,128,512]{2,1,0:T(8,128)(2,1)}, bf16[4,128,512]{2,1,0:T(8,128)(2,1)S(1)}, u32[]{:S(2)}) copy-start(bf16[4,128,512]{2,1,0:T(8,128)(2,1)S(1)} %get-tuple-element.137) | copy-start | bytes 1572868
  239.1 24.4 %collective-permute-start.17 = (bf16[4,128,512]{2,1,0:T(8,128)(2,1)S(1)}, bf16[4,128,512]{2,1,0:T(8,128)(2,1)S(1)}, u32[]{:S(2)}, u32[]{:S(2)}) collective-permute-start(bf16[4,128,512]{2,1,0:T(8,128)(2,1)S(1)} %get-tuple-element.135), channel_id=1, source_target_pairs={{0,1},{1,16},{8,9},{9,24},{16,17},{17,0},{24,25},{25,8},{32,33},{3... | collective-permute-start | bytes 1572872 | tf_op jit(solution)/shard_map/ppermute | solution.py:864
  240.5 37.3 %collective-permute-start.18 = (bf16[4,128,512]{2,1,0:T(8,128)(2,1)}, bf16[4,128,512]{2,1,0:T(8,128)(2,1)}, u32[]{:S(2)}, u32[]{:S(2)}) collective-permute-start(bf16[4,128,512]{2,1,0:T(8,128)(2,1)} %get-tuple-element.136), channel_id=1, source_target_pairs={{0,16},{1,17},{8,24},{9,25},{16,0},{17,1},{24,8},{25,9},{32,48},{3... | collective-permute-start | bytes 1572872 | tf_op jit(solution)/shard_map/ppermute | solution.py:864
  243.9 33.9 %copy-start.27 = (bf16[256,2048]{1,0:T(8,128)(2,1)S(1)}, bf16[256,2048]{1,0:T(8,128)(2,1)}, u32[]{:S(2)}) copy-start(bf16[256,2048]{1,0:T(8,128)(2,1)} %copy-done.26) | copy-start | bytes 3145732
  249.1 48.4 %collective-permute-start.10 = (bf16[256,2048]{1,0:T(8,128)(2,1)}, bf16[256,2048]{1,0:T(8,128)(2,1)}, u32[]{:S(2)}, u32[]{:S(2)}) collective-permute-start(bf16[256,2048]{1,0:T(8,128)(2,1)} %get-tuple-element.125), channel_id=1, source_target_pairs={{0,8},{8,0},{16,24},{24,16},{32,40},{40,32},{48,56},{56,48},{64,72... | collective-permute-start | bytes 3145736 | tf_op jit(solution)/shard_map/ppermute | solution.py:827
  250.1 43.9 %collective-permute-start.14 = (bf16[4,144,512]{2,1,0:T(8,128)(2,1)}, bf16[4,144,512]{2,1,0:T(8,128)(2,1)S(1)}, u32[]{:S(2)}, u32[]{:S(2)}) collective-permute-start(bf16[4,144,512]{2,1,0:T(8,128)(2,1)} %get-tuple-element.127), channel_id=1, source_target_pairs={{0,32},{8,40},{16,48},{24,56},{32,64},{40,72},{48,80},{56,88},{64,... | collective-permute-start | bytes 1769480 | tf_op jit(solution)/shard_map/ppermute | solution.py:855
  250.3 43.7 %collective-permute-start.15 = (bf16[4,144,512]{2,1,0:T(8,128)(2,1)}, bf16[4,144,512]{2,1,0:T(8,128)(2,1)}, u32[]{:S(2)}, u32[]{:S(2)}) collective-permute-start(bf16[4,144,512]{2,1,0:T(8,128)(2,1)} %get-tuple-element.128), channel_id=1, source_target_pairs={{0,64},{8,72},{16,80},{24,88},{32,96},{40,104},{48,112},{56,120},{... | collective-permute-start | bytes 1769480 | tf_op jit(solution)/shard_map/ppermute | solution.py:855
  264.3 29.7 %collective-permute-start.16 = (bf16[4,144,512]{2,1,0:T(8,128)(2,1)}, bf16[4,144,512]{2,1,0:T(8,128)(2,1)}, u32[]{:S(2)}, u32[]{:S(2)}) collective-permute-start(bf16[4,144,512]{2,1,0:T(8,128)(2,1)} %get-tuple-element.129), channel_id=1, source_target_pairs={{0,96},{8,104},{16,112},{24,120},{32,0},{40,8},{48,16},{56,24},{64... | collective-permute-start | bytes 1769480 | tf_op jit(solution)/shard_map/ppermute | solution.py:855
  277.8 12.3 %collective-permute-start.19 = (bf16[4,128,512]{2,1,0:T(8,128)(2,1)}, bf16[4,128,512]{2,1,0:T(8,128)(2,1)S(1)}, u32[]{:S(2)}, u32[]{:S(2)}) collective-permute-start(bf16[4,128,512]{2,1,0:T(8,128)(2,1)} %copy-done.55), channel_id=1, source_target_pairs={{0,17},{1,0},{8,25},{9,8},{16,1},{17,16},{24,9},{25,24},{32,49},{3... | collective-permute-start | bytes 1572872 | tf_op jit(solution)/shard_map/ppermute | solution.py:864
  300.1 36.8 %collective-permute-start.26 = (bf16[128,2304]{1,0:T(8,128)(2,1)}, bf16[128,2304]{1,0:T(8,128)(2,1)}, u32[]{:S(2)}, u32[]{:S(2)}) collective-permute-start(bf16[128,2304]{1,0:T(8,128)(2,1)} %reduce-scatter.2.cloned.1.call-done), channel_id=1, source_target_pairs={{8,1},{1,8},{24,17},{17,24},{40,33},{33,40},{56,49},{49,56},{72,65... | collective-permute-start | bytes 1769480 | tf_op jit(solution)/shard_map/ppermute | solution.py:894
  303.4 29.1 %copy-start.13 = (bf16[64,2048]{1,0:T(8,128)(2,1)S(1)}, bf16[64,2048]{1,0:T(8,128)(2,1)}, u32[]{:S(2)}) copy-start(bf16[64,2048]{1,0:T(8,128)(2,1)} %get-tuple-element.183.refs_1_.refs_6_) | copy-start | bytes 786436
  303.5 29.1 %copy-start.16 = (f32[64,2048]{1,0:T(8,128)S(1)}, f32[64,2048]{1,0:T(8,128)}, u32[]{:S(2)}) copy-start(f32[64,2048]{1,0:T(8,128)} %copy-done.14) | copy-start | bytes 1572868
  303.5 29.1 %copy-start.36 = (f32[64,2048]{1,0:T(8,128)S(1)}, f32[64,2048]{1,0:T(8,128)}, u32[]{:S(2)}) copy-start(f32[64,2048]{1,0:T(8,128)} %copy-done.35) | copy-start | bytes 1572868
  306.3 25.9 %collective-permute-start.11 = (bf16[128,2048]{1,0:T(8,128)(2,1)}, bf16[128,2048]{1,0:T(8,128)(2,1)S(1)}, u32[]{:S(2)}, u32[]{:S(2)}) collective-permute-start(bf16[128,2048]{1,0:T(8,128)(2,1)} %get-tuple-element.174), channel_id=1, source_target_pairs={{0,2},{2,4},{4,6},{6,0},{1,3},{3,5},{5,7},{7,1},{8,10},{10,12},{12... | collective-permute-start | bytes 1572872 | tf_op jit(solution)/shard_map/ppermute | solution.py:833
  306.3 25.9 %collective-permute-start.12 = (bf16[128,2048]{1,0:T(8,128)(2,1)}, bf16[128,2048]{1,0:T(8,128)(2,1)S(1)}, u32[]{:S(2)}, u32[]{:S(2)}) collective-permute-start(bf16[128,2048]{1,0:T(8,128)(2,1)} %get-tuple-element.175), channel_id=1, source_target_pairs={{0,4},{2,6},{4,0},{6,2},{1,5},{3,7},{5,1},{7,3},{8,12},{10,14},{12... | collective-permute-start | bytes 1572872 | tf_op jit(solution)/shard_map/ppermute | solution.py:833
  306.3 26.2 %collective-permute-start.13 = (bf16[128,2048]{1,0:T(8,128)(2,1)}, bf16[128,2048]{1,0:T(8,128)(2,1)S(1)}, u32[]{:S(2)}, u32[]{:S(2)}) collective-permute-start(bf16[128,2048]{1,0:T(8,128)(2,1)} %get-tuple-element.172), channel_id=1, source_target_pairs={{0,6},{2,0},{4,2},{6,4},{1,7},{3,1},{5,3},{7,5},{8,14},{10,8},{12,... | collective-permute-start | bytes 1572872 | tf_op jit(solution)/shard_map/ppermute | solution.py:833
  309.0 27.1 %collective-permute-start.23 = (bf16[128,512]{1,0:T(8,128)(2,1)}, bf16[128,512]{1,0:T(8,128)(2,1)}, u32[]{:S(2)}, u32[]{:S(2)}) collective-permute-start(bf16[128,512]{1,0:T(8,128)(2,1)} %get-tuple-element.147), channel_id=1, source_target_pairs={{0,32},{8,40},{16,48},{24,56},{32,64},{40,72},{48,80},{56,88},{64,... | collective-permute-start | bytes 393224 | tf_op jit(solution)/shard_map/ppermute | solution.py:855
  309.0 24.2 %copy-start.63 = (bf16[144,512]{1,0:T(8,128)(2,1)S(1)}, bf16[144,512]{1,0:T(8,128)(2,1)}, u32[]{:S(2)}) copy-start(bf16[144,512]{1,0:T(8,128)(2,1)} %copy-done.62) | copy-start | bytes 442372
  309.0 24.3 %copy-start.61 = (bf16[144,512]{1,0:T(8,128)(2,1)S(1)}, bf16[144,512]{1,0:T(8,128)(2,1)}, u32[]{:S(2)}) copy-start(bf16[144,512]{1,0:T(8,128)(2,1)} %copy-done.60) | copy-start | bytes 442372
  309.0 24.4 %copy-start.59 = (bf16[144,512]{1,0:T(8,128)(2,1)S(1)}, bf16[144,512]{1,0:T(8,128)(2,1)}, u32[]{:S(2)}) copy-start(bf16[144,512]{1,0:T(8,128)(2,1)} %copy-done.58) | copy-start | bytes 442372
  309.0 27.1 %copy-start.67 = (bf16[128,512]{1,0:T(8,128)(2,1)S(1)}, bf16[128,512]{1,0:T(8,128)(2,1)}, u32[]{:S(2)}) copy-start(bf16[128,512]{1,0:T(8,128)(2,1)} %copy-done.66) | copy-start | bytes 393220
  309.0 27.9 %copy-start.65 = (bf16[128,512]{1,0:T(8,128)(2,1)S(1)}, bf16[128,512]{1,0:T(8,128)(2,1)}, u32[]{:S(2)}) copy-start(bf16[128,512]{1,0:T(8,128)(2,1)} %copy-done.64) | copy-start | bytes 393220
  309.0 28.9 %copy-start.73 = (bf16[128,2304]{1,0:T(8,128)(2,1)S(1)}, bf16[128,2304]{1,0:T(8,128)(2,1)}, u32[]{:S(2)}) copy-start(bf16[128,2304]{1,0:T(8,128)(2,1)} %reduce-scatter.2.cloned.1.call-done) | copy-start | bytes 1769476
  332.5 12.9 %copy-start.53 = (bf16[128,512]{1,0:T(8,128)(2,1)S(1)}, bf16[128,512]{1,0:T(8,128)(2,1)}, u32[]{:S(2)}) copy-start(bf16[128,512]{1,0:T(8,128)(2,1)} %copy-done.52) | copy-start | bytes 393220
  333.2 12.2 %collective-permute-start.20 = (bf16[144,512]{1,0:T(8,128)(2,1)S(1)}, bf16[144,512]{1,0:T(8,128)(2,1)S(1)}, u32[]{:S(2)}, u32[]{:S(2)}) collective-permute-start(bf16[144,512]{1,0:T(8,128)(2,1)S(1)} %copy-done.63), channel_id=1, source_target_pairs={{0,1},{1,16},{8,9},{9,24},{16,17},{17,0},{24,25},{25,8},{32,33},{3... | collective-permute-start | bytes 442376 | tf_op jit(solution)/shard_map/ppermute | solution.py:864
  333.3 12.1 %collective-permute-start.21 = (bf16[144,512]{1,0:T(8,128)(2,1)S(1)}, bf16[144,512]{1,0:T(8,128)(2,1)S(1)}, u32[]{:S(2)}, u32[]{:S(2)}) collective-permute-start(bf16[144,512]{1,0:T(8,128)(2,1)S(1)} %copy-done.61), channel_id=1, source_target_pairs={{0,16},{1,17},{8,24},{9,25},{16,0},{17,1},{24,8},{25,9},{32,48},{3... | collective-permute-start | bytes 442376 | tf_op jit(solution)/shard_map/ppermute | solution.py:864
  333.4 12.0 %collective-permute-start.22 = (bf16[144,512]{1,0:T(8,128)(2,1)S(1)}, bf16[144,512]{1,0:T(8,128)(2,1)S(1)}, u32[]{:S(2)}, u32[]{:S(2)}) collective-permute-start(bf16[144,512]{1,0:T(8,128)(2,1)S(1)} %copy-done.59), channel_id=1, source_target_pairs={{0,17},{1,0},{8,25},{9,8},{16,1},{17,16},{24,9},{25,24},{32,49},{3... | collective-permute-start | bytes 442376 | tf_op jit(solution)/shard_map/ppermute | solution.py:864
  336.0 5.6 %collective-permute-start.24 = (bf16[128,512]{1,0:T(8,128)(2,1)S(1)}, bf16[128,512]{1,0:T(8,128)(2,1)S(1)}, u32[]{:S(2)}, u32[]{:S(2)}) collective-permute-start(bf16[128,512]{1,0:T(8,128)(2,1)S(1)} %copy-done.67), channel_id=1, source_target_pairs={{0,64},{8,72},{16,80},{24,88},{32,96},{40,104},{48,112},{56,120},{... | collective-permute-start | bytes 393224 | tf_op jit(solution)/shard_map/ppermute | solution.py:855
  336.9 5.8 %collective-permute-start.25 = (bf16[128,512]{1,0:T(8,128)(2,1)S(1)}, bf16[128,512]{1,0:T(8,128)(2,1)S(1)}, u32[]{:S(2)}, u32[]{:S(2)}) collective-permute-start(bf16[128,512]{1,0:T(8,128)(2,1)S(1)} %copy-done.65), channel_id=1, source_target_pairs={{0,96},{8,104},{16,112},{24,120},{32,0},{40,8},{48,16},{56,24},{64... | collective-permute-start | bytes 393224 | tf_op jit(solution)/shard_map/ppermute | solution.py:855
  341.7 17.4 %collective-permute-start.33 = (bf16[128,2304]{1,0:T(8,128)(2,1)S(1)}, bf16[128,2304]{1,0:T(8,128)(2,1)S(1)}, u32[]{:S(2)}, u32[]{:S(2)}) collective-permute-start(bf16[128,2304]{1,0:T(8,128)(2,1)S(1)} %broadcast_select_fusion.1.refs_9_.refs_1_), channel_id=1, source_target_pairs={{0,2},{2,4},{4,6},{6,0},{1,3},{3,5},{5,7},{7,1},{8,10},{10,12},{12... | collective-permute-start | bytes 1769480 | tf_op jit(solution)/shard_map/ppermute | solution.py:833
  342.7 26.5 %collective-permute-start.34 = (bf16[128,2304]{1,0:T(8,128)(2,1)S(1)}, bf16[128,2304]{1,0:T(8,128)(2,1)S(1)}, u32[]{:S(2)}, u32[]{:S(2)}) collective-permute-start(bf16[128,2304]{1,0:T(8,128)(2,1)S(1)} %broadcast_select_fusion.1.refs_9_.refs_1_), channel_id=1, source_target_pairs={{0,4},{2,6},{4,0},{6,2},{1,5},{3,7},{5,1},{7,3},{8,12},{10,14},{12... | collective-permute-start | bytes 1769480 | tf_op jit(solution)/shard_map/ppermute | solution.py:833
  345.4 27.8 %collective-permute-start.35 = (bf16[128,2304]{1,0:T(8,128)(2,1)S(1)}, bf16[128,2304]{1,0:T(8,128)(2,1)}, u32[]{:S(2)}, u32[]{:S(2)}) collective-permute-start(bf16[128,2304]{1,0:T(8,128)(2,1)S(1)} %broadcast_select_fusion.1.refs_9_.refs_1_), channel_id=1, source_target_pairs={{0,6},{2,0},{4,2},{6,4},{1,7},{3,1},{5,3},{7,5},{8,14},{10,8},{12,... | collective-permute-start | bytes 1769480 | tf_op jit(solution)/shard_map/ppermute | solution.py:833
  346.5 9.9 %collective-permute-start.29 = (bf16[144,1024]{1,0:T(8,128)(2,1)S(1)}, bf16[144,1024]{1,0:T(8,128)(2,1)S(1)}, u32[]{:S(2)}, u32[]{:S(2)}) collective-permute-start(bf16[144,1024]{1,0:T(8,128)(2,1)S(1)} %shard_map.282), channel_id=1, source_target_pairs={{8,1},{1,8},{24,17},{17,24},{40,33},{33,40},{56,49},{49,56},{72,65... | collective-permute-start | bytes 884744 | tf_op jit(solution)/shard_map/ppermute | solution.py:894
  351.7 6.6 %collective-permute-start.27 = (bf16[128,2048]{1,0:T(8,128)(2,1)S(1)}, bf16[128,2048]{1,0:T(8,128)(2,1)S(1)}, u32[]{:S(2)}, u32[]{:S(2)}) collective-permute-start(bf16[128,2048]{1,0:T(8,128)(2,1)S(1)} %shard_map.279.refs_8_), channel_id=1, source_target_pairs={{0,8},{8,0},{16,24},{24,16},{32,40},{40,32},{48,56},{56,48},{64,72... | collective-permute-start | bytes 1572872 | tf_op jit(solution)/shard_map/ppermute | solution.py:827
  356.5 22.2 %collective-permute-start.30 = (bf16[144,1024]{1,0:T(8,128)(2,1)S(1)}, bf16[144,1024]{1,0:T(8,128)(2,1)}, u32[]{:S(2)}, u32[]{:S(2)}) collective-permute-start(bf16[144,1024]{1,0:T(8,128)(2,1)S(1)} %broadcast_select_fusion.3.refs_1_), channel_id=1, source_target_pairs={{0,2},{2,4},{4,6},{6,0},{1,3},{3,5},{5,7},{7,1},{8,10},{10,12},{12... | collective-permute-start | bytes 884744 | tf_op jit(solution)/shard_map/ppermute | solution.py:833
  358.4 23.5 %collective-permute-start.31 = (bf16[144,1024]{1,0:T(8,128)(2,1)S(1)}, bf16[144,1024]{1,0:T(8,128)(2,1)}, u32[]{:S(2)}, u32[]{:S(2)}) collective-permute-start(bf16[144,1024]{1,0:T(8,128)(2,1)S(1)} %broadcast_select_fusion.3.refs_1_), channel_id=1, source_target_pairs={{0,4},{2,6},{4,0},{6,2},{1,5},{3,7},{5,1},{7,3},{8,12},{10,14},{12... | collective-permute-start | bytes 884744 | tf_op jit(solution)/shard_map/ppermute | solution.py:833
  358.8 14.5 %copy-start.24 = (bf16[128,3072]{1,0:T(8,128)(2,1)S(1)}, bf16[128,3072]{1,0:T(8,128)(2,1)}, u32[]{:S(2)}) copy-start(bf16[128,3072]{1,0:T(8,128)(2,1)} %refs_6_.3) | copy-start | bytes 2359300
  358.8 14.5 %copy-start.25 = (bf16[128,3072]{1,0:T(8,128)(2,1)S(1)}, bf16[128,3072]{1,0:T(8,128)(2,1)}, u32[]{:S(2)}) copy-start(bf16[128,3072]{1,0:T(8,128)(2,1)} %refs_5_.3) | copy-start | bytes 2359300
  359.0 24.0 %collective-permute-start.32 = (bf16[144,1024]{1,0:T(8,128)(2,1)S(1)}, bf16[144,1024]{1,0:T(8,128)(2,1)}, u32[]{:S(2)}, u32[]{:S(2)}) collective-permute-start(bf16[144,1024]{1,0:T(8,128)(2,1)S(1)} %broadcast_select_fusion.3.refs_1_), channel_id=1, source_target_pairs={{0,6},{2,0},{4,2},{6,4},{1,7},{3,1},{5,3},{7,5},{8,14},{10,8},{12,... | collective-permute-start | bytes 884744 | tf_op jit(solution)/shard_map/ppermute | solution.py:833
  361.3 21.8 %copy-start.45 = (bf16[128,1024]{1,0:T(8,128)(2,1)S(1)}, bf16[128,1024]{1,0:T(8,128)(2,1)}, u32[]{:S(2)}) copy-start(bf16[128,1024]{1,0:T(8,128)(2,1)} %refs_8_.1) | copy-start | bytes 786436
  370.0 23.1 %collective-permute-start.28 = (bf16[2,128,2048]{2,1,0:T(8,128)(2,1)}, bf16[2,128,2048]{2,1,0:T(8,128)(2,1)}, u32[]{:S(2)}, u32[]{:S(2)}) collective-permute-start(bf16[2,128,2048]{2,1,0:T(8,128)(2,1)} %pad_maximum_fusion), channel_id=1, source_target_pairs={{0,1},{9,8},{16,17},{25,24},{32,33},{41,40},{48,49},{57,56},{64,65... | collective-permute-start | bytes 3145736 | tf_op jit(solution)/shard_map/ppermute | solution.py:1015
  389.4 2.5 collective-permute-start.36
  (60 other events, 239.9 us)
Sparse Core Ops, SparseCore 0:
  13.3 57.0 all-gather.2
  73.2 75.2 all-gather.4
  169.6 94.2 reduce-scatter.1

commit v8 on v6

--- a/solution.py
+++ b/solution.py
@@ -260,7 +260,7 @@
 
 def feed(ua, ub, ca, cb, w, behind):
     half, width = ua.shape
-    chunk = 3 * HD
+    chunk = 2 * HD
     parts = w.shape[1] // 3 // chunk
     column = lambda shift: pl.BlockSpec((width, chunk), lambda i: (0, shift * parts + i))
     unit = pl.BlockSpec((2 * half, chunk), lambda i: (0, i))
@@ -331,20 +331,24 @@
     )(left, w)
 
 
-def spread_blocks(left, right, out, start):
-    for place in range(left.shape[1] // HD):
-        term = dot_rows(left[:, head(place)], right)
+def spread_blocks(flipped, right, out, start):
+    term = dot(flipped, right).astype(BF16)
+    for place in range(flipped.shape[0] // HD):
         for owner in range(right.shape[1] // HD):
             at = start + place * HD
-            out[owner * HD : (owner + 1) * HD, at : at + HD] = term[:, head(owner)].astype(BF16)
-
-
-def feed_grads_kernel(u_flip, ca, cb, d_gate, d_up, hidden, out):
+            out[owner * HD : (owner + 1) * HD, at : at + HD] = term[head(place), head(owner)]
+
+
+def feed_grads_kernel(u_flip, ca, cb, d_gate, d_up, hidden, out, flipped):
+    @pl.when(pl.program_id(0) == 0)
+    def _():
+        flipped[...] = hidden[...].T
+
     units = hidden.shape[1]
     out[:, :units] = dot(u_flip[...], d_gate[...]).astype(BF16)
     out[:, units : 2 * units] = dot(u_flip[...], d_up[...]).astype(BF16)
     cot = jnp.concatenate([flat(ca[...]), flat(cb[...])], axis=0)
-    spread_blocks(hidden, cot, out, 2 * units)
+    spread_blocks(flipped[...], cot, out, 2 * units)
 
 
 def feed_grads(u_flip, ca, cb, d_gate, d_up, hidden, behind):
@@ -360,6 +364,7 @@
         rowed(chunk, 3 * units),
         struct((width, 3 * units), BF16),
         2 * length * width * units * 3,
+        scratch=[pltpu.VMEM((units, length), BF16)],
         behind=behind,
     )(u_flip, ca, cb, d_gate, d_up, hidden)
 
@@ -484,45 +489,41 @@
     )(d_qkv, d_gate, w)
 
 
-def attend_grads_kernel(x_flip, da, db, d_qkv, d_gate, gated, terms, out, outer):
+def attend_grads_kernel(x_flip, da, db, d_qkv, d_gate, gated, out, flipped):
+    @pl.when(pl.program_id(0) == 0)
+    def _():
+        flipped[...] = gated[...].T
+
     inner, split = d_qkv.shape[1], d_gate.shape[1]
-    block = out.shape[1] - terms.shape[1]
-    for number in range(out.shape[0]):
-        out[number, block:, :] = terms[number].astype(BF16)
-    term = dot(x_flip[...], d_qkv[...]).astype(BF16)
-    gates = dot(x_flip[...], d_gate[...]).astype(BF16)
-    spread_blocks(gated, jnp.concatenate([da[...], db[...]], axis=0), outer, 0)
-    for number in range(out.shape[0]):
-        rows = slice(number * block, (number + 1) * block)
-        out[number, :block, :inner] = term[rows]
-        out[number, :block, inner : inner + split] = gates[rows]
-        out[number, :block, inner + split :] = outer[rows, :]
-
-
-def attend_grads(x_flip, da, db, d_qkv, d_gate, gated, terms, behind):
+    out[:, :inner] = dot(x_flip[...], d_qkv[...]).astype(BF16)
+    out[:, inner : inner + split] = dot(x_flip[...], d_gate[...]).astype(BF16)
+    spread_blocks(
+        flipped[...], jnp.concatenate([da[...], db[...]], axis=0), out, inner + split
+    )
+
+
+def attend_grads(x_flip, da, db, d_qkv, d_gate, gated, behind):
     width, length = x_flip.shape
-    owners, extra, columns = terms.shape
-    block = width // owners
-    many = 4
-    slab = pl.BlockSpec((length // 2, many * block), lambda i: (0, i))
+    columns = d_qkv.shape[1] + d_gate.shape[1] + gated.shape[1]
+    chunk = 4 * HD
+    slab = pl.BlockSpec((length // 2, chunk), lambda i: (0, i))
     return call(
         attend_grads_kernel,
-        (owners // many,),
+        (width // chunk,),
         [
-            rowed(many * block, length),
+            rowed(chunk, length),
             slab,
             slab,
             fixed(d_qkv.shape),
             fixed(d_gate.shape),
             fixed(gated.shape),
-            pl.BlockSpec((many, extra, columns), lambda i: (i, 0, 0)),
         ],
-        pl.BlockSpec((many, block + extra, columns), lambda i: (i, 0, 0)),
-        struct((owners, block + extra, columns), BF16),
+        rowed(chunk, columns),
+        struct((width, columns), BF16),
         2 * length * width * columns,
-        scratch=[pltpu.VMEM((many * block, gated.shape[1]), BF16)],
+        scratch=[pltpu.VMEM(gated.shape[::-1], BF16)],
         behind=behind,
-    )(x_flip, da, db, d_qkv, d_gate, gated, terms)
+    )(x_flip, da, db, d_qkv, d_gate, gated)
 
 
 def middle_kernel(parts, x, middle, spread):
@@ -688,29 +689,24 @@
 
 
 def close_attend_kernel(
-    turn_at, b0, b1, b2, b3, wq, wk, wv, wg, gain, gq, gk, gv, gg, go, sums, ends
+    turn_at, b0, b1, b2, b3, wq, wk, wv, wg, gain, gq, gk, gv, gg, go, sums
 ):
     found = pick((b0, b1, b2, b3))
-    inner, scale = found[:, : 4 * HD], gain[...]
-    block = scale.shape[0]
-    outer = found[:block, 4 * HD :]
-    raw_q, raw_k, raw_v = inner[:block, : 2 * HD], inner[:block, head(2)], inner[:block, head(3)]
+    inner, outer, scale = found[:, : 4 * HD], found[:, 4 * HD :], gain[...]
+    raw_q, raw_k, raw_v = inner[:, : 2 * HD], inner[:, head(2)], inner[:, head(3)]
     raw_g = outer[:, : 2 * HD]
     gq[...], gk[...], gv[...], gg[...] = raw_q * scale, raw_k * scale, raw_v * scale, raw_g * scale
     go[head(0), :], go[head(1), :] = outer[:, head(2)], outer[:, head(3)]
     pairs = ((raw_q, wq), (raw_k, wk), (raw_v, wv), (raw_g, wg))
     term = sum(lanes(raw * w[...].astype(F32)) for raw, w in pairs)
-    last = inner[block:, :HD]
 
     @pl.when(pl.program_id(0) == 0)
     def _():
         sums[...] = term
-        ends[...] = last
 
     @pl.when(pl.program_id(0) > 0)
     def _():
         sums[...] += term
-        ends[...] += last
 
 
 def close(kernel, turn_at, blocks, weights, gain, out_rows, extra):
@@ -897,18 +893,23 @@
         d_attended, d_gate_pre = gate_back(da, db, w1, gate, attended)
         d_qkv, terms = attend_back(probs, low, d_attended, pre, gains, cosine, sine, ())
 
-        def spread_terms(vector):
-            return jnp.pad(vector.reshape(n_shard, 1, -1), ((0, 0), (0, 15), (0, 0)))
-
-        wide_terms = jnp.concatenate([spread_terms(terms[0]), spread_terms(terms[1])], axis=2)
-        wide_terms = jnp.pad(wide_terms, ((0, 0), (0, 0), (0, 8 * HD - 2 * head_rows)))
-        attn = attend_grads(x_flip, da, db, d_qkv, d_gate_pre, gated, wide_terms, ())
+        pieces = jnp.concatenate(
+            [terms[0].reshape(n_shard, -1), terms[1].reshape(n_shard, -1)], axis=1
+        )
+        copies = n_ctx * n_tp
+        pieces = jnp.pad(pieces, ((0, 0), (0, HD - pieces.shape[1]))).astype(BF16)
+        pieces = jnp.broadcast_to(pieces[:, None, None], (n_shard, copies, 8, HD))
+        pieces = lax.all_to_all(
+            pieces.reshape(n_shard * copies, 8, HD), ("shard", "ctx", "tp"), 0, 0
+        )
+        head_ends = jnp.sum(pieces.astype(F32), axis=0)
+        attn = attend_grads(x_flip, da, db, d_qkv, d_gate_pre, gated, ())
         in_mine, in_other = input_back(d_qkv, d_gate_pre, w1, (attn,))
         layer_half, in_half = tree_half(layer_mine, layer_other), tree_half(in_mine, in_other)
-        attn, layer_half, in_half, grad_ffn = lax.optimization_barrier(
-            (attn, layer_half, in_half, grad_ffn)
-        )
-        attn_parts = plane_exchange(attn)
+        attn, layer_half, in_half, grad_ffn, head_ends = lax.optimization_barrier(
+            (attn, layer_half, in_half, grad_ffn, head_ends)
+        )
+        attn_parts = plane_exchange(attn.reshape(n_shard, -1, attn.shape[1]))
 
         def owners(block):
             block = swapped(block)
@@ -927,8 +928,6 @@
         ]
         ends = ends_step(parts, middle, d_middle, own_x)
         ffn_blocks = owners(grad_ffn)
-        attn_sum = sum_step(attn_parts, (ends, ffn_blocks[0]))
-        ends, attn_sum = lax.optimization_barrier((ends, attn_sum))
         sibling = core_swap(ends)
 
         def whole(start):
@@ -940,6 +939,8 @@
             )
 
         full = jnp.stack([whole(0), whole(rows)])
+        attn_sum = sum_step(attn_parts, (full, ffn_blocks[0]))
+        full, attn_sum = lax.optimization_barrier((full, attn_sum))
         full = jnp.where(native, full, lax.ppermute(full, PLANE, across_perm))
 
         turn_at = ctx.astype(jnp.int32).reshape(1)
@@ -954,16 +955,16 @@
             [(size, HD)],
         )
         attn_blocks = owners(attn_sum)
-        grad_query, grad_key, grad_value, grad_gate_attn, grad_out, in_sums, head_ends = close(
+        grad_query, grad_key, grad_value, grad_gate_attn, grad_out, in_sums = close(
             close_attend_kernel,
             turn_at,
             attn_blocks,
             (w_query, w_key, w_value, w_gate_attn),
             gain_one,
             w_out.shape,
-            [(size, HD), (16, HD)],
-        )
-        gain_terms = jnp.stack([jnp.sum(in_sums, axis=1), jnp.sum(mid_sums, axis=1), head_ends[0]])
+            [(size, HD)],
+        )
+        gain_terms = jnp.stack([jnp.sum(in_sums, axis=1), jnp.sum(mid_sums, axis=1)])
         gain_terms = gain_terms + lax.ppermute(gain_terms, "tp", [(0, 1), (1, 0)])
 
         return (
@@ -975,8 +976,8 @@
             grad_value,
             grad_gate_attn,
             grad_out,
-            gain_terms[2, :head_rows],
-            gain_terms[2, head_rows : 2 * head_rows],
+            head_ends[0, :head_rows],
+            head_ends[0, head_rows : 2 * head_rows],
             gain_terms[1],
             grad_gate,
             grad_up,

time: 378 us -> 385 us (1.019)
  local copies, waits for them, and re-layouts: 31.8 us -> 37.1 us
  Pallas kernels: 80.1 us -> 75.6 us
  waiting for transfers between devices: 140 us -> 144 us
    reduce_scatter x1, waiting for transfers between devices: 10.4 us -> 0.02 us  [plane_scatter(): lax.psum_scatter(value, PLANE, scatter_dimension=0, tiled=True, axis_inde...]
    all_to_all x0 -> x1, waiting for transfers between devices: none -> 9.96 us  [shards(): lax.all_to_all(pieces.reshape(n_shard * copies, 8, HD), ('shard', 'ctx',...]
    all_to_all x0 -> x1, starting transfers between devices: none -> 5.42 us  [shards(): lax.all_to_all(pieces.reshape(n_shard * copies, 8, HD), ('shard', 'ctx',...]
    pallas_call x16, Pallas kernels: 64.9 us -> 60.1 us  [call(): return lambda *operands: built(*operands, *behind)]
    unnamed x110 -> x114, local copies, waits for them, and re-layouts: 21.8 us -> 26.3 us
  transfers between devices with their start and end apart: 32 -> 33, of which waited for: 22 -> 24; matrix products, arithmetic and copies ran while one was open for 5% -> 5% of each run, Pallas kernels for 17% -> 15%
where the time goes in v8:
time: 385 us; the launch traced here: 379 us
  waiting for transfers between devices  144 us (37%)
  Pallas kernels  75.6 us (20%)
  starting transfers between devices  56.2 us (15%)
  local copies, waits for them, and re-layouts  37.1 us (10%)
  blocking collectives  34.1 us (9%)
  other arithmetic  17.3 us (4%)
  between operations  14.6 us (4%)
    pallas_call x16, Pallas kernels, call(): return lambda *operands: built(*operands, *behind)  60.1 us
    all_to_all x3, waiting for transfers between devices, ctx_exchange(): return lax.all_to_all(value, 'ctx', 0, 0)  41 us
    ppermute x3, waiting for transfers between devices, swapped(): return jnp.where(native, value, lax.ppermute(value, PLANE, swap_perm))  37.9 us
    all_to_all x2, blocking collectives, ctx_exchange(): return lax.all_to_all(value, 'ctx', 0, 0)  34.1 us
    ppermute x9, waiting for transfers between devices, ctx_turn(): lax.ppermute(value, 'ctx', [(i, (i + by) % n_ctx) for i in range(n_ctx)])  28.3 us
    unnamed x114, local copies, waits for them, and re-layouts  26.3 us
    ppermute x11, waiting for transfers between devices, core_swap(): return lax.ppermute(value, 'shard', core_perm)  18.1 us
    all_to_all x3, starting transfers between devices, ctx_exchange(): return lax.all_to_all(value, 'ctx', 0, 0)  13 us
  transfers between devices with their start and end apart: 33, of which 24 were waited for; matrix products, arithmetic and copies ran while one was open for 5% of the time, Pallas kernels for 15%

profile of v8, /device:TPU:1, one launch (start us, length us, event | category | flops | bytes accessed | tf_op | source)
XLA Modules:
  0.0 379.4 jit_solution(6220861301500181590)
XLA Ops:
  14.2 4.5 %collective-permute-start.6 = (bf16[128,2304]{1,0:T(8,128)(2,1)S(1)}, bf16[128,2304]{1,0:T(8,128)(2,1)S(1)}, u32[]{:S(2)}, u32[]{:S(2)}) collective-permute-start(bf16[128,2304]{1,0:T(8,128)(2,1)S(1)} %pad_maximum_fusion.1), channel_id=1, source_target_pairs={{8,1},{1,8},{24,17},{17,24},{40,33},{33,40},{56,49},{49,56},{72,65... | collective-permute-start | bytes 1769480 | tf_op jit(solution)/shard_map/ppermute | solution.py:822
  18.8 7.5 %collective-permute-done.6 = bf16[128,2304]{1,0:T(8,128)(2,1)S(1)} collective-permute-done((bf16[128,2304]{1,0:T(8,128)(2,1)S(1)}, bf16[128,2304]{1,0:T(8,128)(2,1)S(1)}, u32[]{:S(2)}, u32[]{:S(2)}) %collective-permute-start.6) | collective-permute-done | bytes 589856 | tf_op jit(solution)/shard_map/ppermute | solution.py:822
  27.5 1.9 collective-permute-done
  30.4 1.6 broadcast_in_dim.26
  31.9 5.3 %all-to-all-start = ((bf16[4,128,2048]{2,1,0:T(8,128)(2,1)}), bf16[4,128,2048]{2,1,0:T(8,128)(2,1)S(1)}, u32[]{:S(2)}, u32[]{:S(2)}) async-start(bf16[4,128,2048]{2,1,0:T(8,128)(2,1)} %broadcast_in_dim.26), calls=%async_computation | async-start | bytes 4194304 | tf_op jit(solution)/shard_map/all_to_all | solution.py:771
  37.8 25.4 %all-to-all-done.refs_0_.refs_2_.refs_1_ = bf16[4,128,2048]{2,1,0:T(8,128)(2,1)S(1)} async-done(((bf16[4,128,2048]{2,1,0:T(8,128)(2,1)}), bf16[4,128,2048]{2,1,0:T(8,128)(2,1)S(1)}, u32[]{:S(2)}, u32[]{:S(2)}) %all-to-all-start) | async-done | bytes 2097184 | tf_op jit(solution)/shard_map/all_to_all | solution.py:771
  66.9 1.5 collective-permute-done.1.refs_1_.refs_3_.refs_2_
  68.4 1.6 all-gather.3.cloned.1.call-done
  70.0 2.5 shard_map.263
  73.4 4.1 %collective-permute-done.3.other = bf16[8,128,1152]{2,1,0:T(8,128)(2,1)} collective-permute-done((bf16[8,128,1152]{2,1,0:T(8,128)(2,1)S(1)}, bf16[8,128,1152]{2,1,0:T(8,128)(2,1)}, u32[]{:S(2)}, u32[]{:S(2)}) %collective-permute-start.3) | collective-permute-done | bytes 2359328 | tf_op jit(solution)/shard_map/ppermute | solution.py:768
  77.5 5.0 %shard_map.264 = bf16[8,2,128,1152]{3,2,1,0:T(8,128)(2,1)} custom-call(s32[1]{0:T(128)} %bitcast.16.core, bf16[8,2,128,1152]{3,2,1,0:T(8,128)(2,1)} %bitcast.100, bf16[8,128,1152]{2,1,0:T(8,128)(2,1)} %collective-permute-done.3.other), custom_call_target="tpu_custom_call" | custom-call | flops 1048576 | bytes 8388608 | tf_op jit(solution)/shard_map/pallas_call | solution.py:648
  82.5 5.8 %shard_map.265 = (bf16[512,2048]{1,0:T(8,128)(2,1)S(1)}, f32[512,384]{1,0:T(8,128)S(1)}, bf16[512,512]{1,0:T(8,128)(2,1)S(1)}, f32[512,256]{1,0:T(8,128)S(1)}, f32[16,128]{1,0:T(8,128)S(1)}) custom-call(bf16[4,128,2048]{2,1,0:T(8,128)(2,1)} %copy-done.47, bf16[4,128,2048]{2,1,0:T(8,128)(2,1)} %collective-permute-done.1.refs_1_.refs_3_.refs_2_, ...), custom_call_target="tpu_custom_call" | custom-call | flops 1610612736 | bytes 8388608 | tf_op jit(solution)/shard_map/pallas_call | solution.py:97
  89.7 6.4 %shard_map.267 = (f32[2,512,512]{2,1,0:T(8,128)}, f32[512,256]{1,0:T(8,128)S(1)}, bf16[512,256]{1,0:T(8,128)(2,1)S(1)}, bf16[256,2048]{1,0:T(8,128)(2,1)S(1)}, bf16[256,2048]{1,0:T(8,128)(2,1)S(1)}) custom-call(bf16[512,512]{1,0:T(8,128)(2,1)S(1)} %get-tuple-element.74.refs_0_.refs_1_, f32[512,256]{1,0:T(8,128)S(1)} %get-tuple-element.75.refs_1_.refs_3_, ...), custom_call_target="tpu_custom_call" | custom-call | flops 805306368 | bytes 8388608 | tf_op jit(solution)/shard_map/pallas_call | solution.py:97
  96.6 2.3 collective-permute-done.4
  98.9 1.4 add_convert_fusion.3
  100.3 4.2 %all-to-all-start.1 = ((bf16[4,64,2048]{2,1,0:T(8,128)(2,1)}), bf16[4,64,2048]{2,1,0:T(8,128)(2,1)S(1)}, u32[]{:S(2)}, u32[]{:S(2)}) async-start(bf16[4,64,2048]{2,1,0:T(8,128)(2,1)} %bitcast.19), calls=%async_computation.1 | async-start | bytes 2097152 | tf_op jit(solution)/shard_map/all_to_all | solution.py:771
  105.3 1.6 copy-done.23
  108.2 10.8 %all-to-all-done.1.refs_0_ = bf16[4,64,2048]{2,1,0:T(8,128)(2,1)S(1)} async-done(((bf16[4,64,2048]{2,1,0:T(8,128)(2,1)}), bf16[4,64,2048]{2,1,0:T(8,128)(2,1)S(1)}, u32[]{:S(2)}, u32[]{:S(2)}) %all-to-all-start.1) | async-done | bytes 1048608 | tf_op jit(solution)/shard_map/all_to_all | solution.py:771
  121.1 15.9 %all_to_all.35 = bf16[4,64,2048]{2,1,0:T(8,128)(2,1)S(1)} all-to-all(bf16[4,64,2048]{2,1,0:T(8,128)(2,1)S(1)} %get-tuple-element.80), channel_id=1, replica_groups=mesh['shard'=16,'ctx'=4,'tp'=2] {'ctx'}, dimensions={0} | all-to-all | bytes 2097152 | tf_op jit(solution)/shard_map/all_to_all | solution.py:771
  137.0 2.6 collective-permute-start.5
  139.5 2.3 collective-permute-done.5
  145.5 2.6 all-gather.5.cloned.1.call-done.refs_4_.refs_5_.refs_6_.refs_2_.refs_3_.refs_1_
  149.3 8.6 %shard_map.270 = (bf16[512,768]{1,0:T(8,128)(2,1)S(1)}, bf16[512,768]{1,0:T(8,128)(2,1)S(1)}, bf16[512,768]{1,0:T(8,128)(2,1)S(1)}) custom-call(bf16[256,2048]{1,0:T(8,128)(2,1)S(1)} %bitcast.86, bf16[256,2048]{1,0:T(8,128)(2,1)S(1)} %bitcast.92, bf16[4,128,2048]{2,1,0:T(8,128)(2,1)} %copy-done.47, ...), custom_call_target="tpu_custom_call" | custom-call | flops 4831838208 | bytes 8388608 | tf_op jit(solution)/shard_map/pallas_call | solution.py:97
  157.9 8.4 %shard_map.271.refs_4_ = bf16[2048,2304]{1,0:T(8,128)(2,1)} custom-call(bf16[2048,512]{1,0:T(8,128)(2,1)S(1)} %copy-done.3, bf16[4,128,2048]{2,1,0:T(8,128)(2,1)} %copy-done.47, bf16[4,128,2048]{2,1,0:T(8,128)(2,1)} %collective-permute-done.1.refs_1_.refs_3_.refs_2_, bf16[512,768]{1,0:T(8,128)(2,1)S(1)} %get-tuple-element.81.refs_3_.refs_0_, ...), custom_call_target="tpu_custom_call" | custom-call | flops 4831838208 | bytes 8388608 | tf_op jit(solution)/shard_map/pallas_call | solution.py:97
  171.2 6.0 %shard_map.272 = (bf16[256,2048]{1,0:T(8,128)(2,1)S(1)}, bf16[256,2048]{1,0:T(8,128)(2,1)S(1)}) custom-call(bf16[512,768]{1,0:T(8,128)(2,1)S(1)} %copy-done.11, bf16[512,768]{1,0:T(8,128)(2,1)S(1)} %copy-done.13, bf16[2048,2304]{1,0:T(8,128)(2,1)} %all-gather.5.cloned.1.call-done.refs_4_.refs_5_.refs_6_.refs_2_.refs_3_.refs_1_, ...), custom_call_target="tpu_custom_call" | custom-call | flops 3221225472 | bytes 8388608 | tf_op jit(solution)/shard_map/pallas_call | solution.py:97
  177.9 2.3 collective-permute-done.7
  180.6 18.2 %all_to_all.36.refs_0_ = bf16[4,64,2048]{2,1,0:T(8,128)(2,1)S(1)} all-to-all(bf16[4,64,2048]{2,1,0:T(8,128)(2,1)S(1)} %bitcast.87), channel_id=1, replica_groups=mesh['shard'=16,'ctx'=4,'tp'=2] {'ctx'}, dimensions={0} | all-to-all | bytes 2097152 | tf_op jit(solution)/shard_map/all_to_all | solution.py:771
  202.1 3.5 all-to-all-start.4
  208.0 4.2 %shard_map.274 = (bf16[256,2048]{1,0:T(8,128)(2,1)S(1)}, bf16[256,2048]{1,0:T(8,128)(2,1)S(1)}) custom-call(bf16[512,768]{1,0:T(8,128)(2,1)S(1)} %copy-done.9, bf16[2048,2304]{1,0:T(8,128)(2,1)} %all-gather.5.cloned.1.call-done.refs_4_.refs_5_.refs_6_.refs_2_.refs_3_.refs_1_, bf16[4,64,2048]{2,1,0:T(8,128)(2,1)S(1)} %bitcast.88), custom_call_target="tpu_custom_call" | custom-call | flops 1610612736 | bytes 8388608 | tf_op jit(solution)/shard_map/pallas_call | solution.py:97
  214.1 4.8 %all-to-all-done.4 = bf16[4,64,2048]{2,1,0:T(8,128)(2,1)S(1)} async-done(((bf16[4,64,2048]{2,1,0:T(8,128)(2,1)}), bf16[4,64,2048]{2,1,0:T(8,128)(2,1)S(1)}, u32[]{:S(2)}, u32[]{:S(2)}) %all-to-all-start.4) | async-done | bytes 1048608 | tf_op jit(solution)/shard_map/all_to_all | solution.py:771
  218.9 2.7 collective-permute-start.8
  221.6 3.8 collective-permute-done.8
  227.5 2.1 shard_map.275
  229.8 3.2 shard_map.276
  233.0 4.4 %shard_map.277.refs_3_ = bf16[2048,1024]{1,0:T(8,128)(2,1)} custom-call(bf16[2048,512]{1,0:T(8,128)(2,1)S(1)} %shard_map.266.refs_2_.refs_0_, bf16[256,2048]{1,0:T(8,128)(2,1)S(1)} %bitcast.84, bf16[256,2048]{1,0:T(8,128)(2,1)S(1)} %bitcast.90, bf16[512,512]{1,0:T(8,128)(2,1)S(1)} %get-tuple-element.96.refs_3_.refs_0_, ...), custom_call_target="tpu_custom_call" | custom-call | flops 2147483648 | bytes 8388608 | tf_op jit(solution)/shard_map/pallas_call | solution.py:97
  237.4 4.2 %shard_map.278 = (bf16[256,2048]{1,0:T(8,128)(2,1)S(1)}, bf16[256,2048]{1,0:T(8,128)(2,1)S(1)}) custom-call(bf16[512,512]{1,0:T(8,128)(2,1)S(1)} %get-tuple-element.96.refs_3_.refs_0_, bf16[512,256]{1,0:T(8,128)(2,1)S(1)} %get-tuple-element.97.refs_4_.refs_1_, bf16[2048,1152]{1,0:T(8,128)(2,1)} %bitcast.97, bf16[2048,1024]{1,0:T(8,128)(2,1)} %shard_map.277.refs_3_), custom_call_target="tpu_custom_call" | custom-call | flops 1610612736 | bytes 8388608 | tf_op jit(solution)/shard_map/pallas_call | solution.py:97
  243.2 5.4 %all-to-all-start.5 = ((bf16[128,8,128]{2,1,0:T(8,128)(2,1)}), bf16[128,8,128]{2,1,0:T(8,128)(2,1)S(1)}, u32[]{:S(2)}, u32[]{:S(2)}) async-start(bf16[128,8,128]{2,1,0:T(8,128)(2,1)} %broadcast_in_dim.56), calls=%async_computation.6 | async-start | bytes 524288 | tf_op jit(solution)/shard_map/all_to_all | solution.py:902
  248.6 2.6 add_convert_fusion.1
  251.2 10.0 %all-to-all-done.5 = bf16[128,8,128]{2,1,0:T(8,128)(2,1)S(1)} async-done(((bf16[128,8,128]{2,1,0:T(8,128)(2,1)}), bf16[128,8,128]{2,1,0:T(8,128)(2,1)S(1)}, u32[]{:S(2)}, u32[]{:S(2)}) %all-to-all-start.5) | async-done | bytes 262176 | tf_op jit(solution)/shard_map/all_to_all | solution.py:902
  261.3 1.6 add_convert_fusion
  263.0 4.7 %all-to-all-start.6 = ((bf16[16,128,1024]{2,1,0:T(8,128)(2,1)}), bf16[16,128,1024]{2,1,0:T(8,128)(2,1)}, u32[]{:S(2)}, u32[]{:S(2)}) async-start(bf16[16,128,1024]{2,1,0:T(8,128)(2,1)} %bitcast.98), calls=%async_computation.7 | async-start | bytes 8388608 | tf_op jit(solution)/shard_map/all_to_all | solution.py:795
  269.3 1.5 collective-permute-start.12
  270.8 1.7 collective-permute-start.13
  272.5 4.0 %collective-permute-start.15 = (bf16[128,2304]{1,0:T(8,128)(2,1)}, bf16[128,2304]{1,0:T(8,128)(2,1)}, u32[]{:S(2)}, u32[]{:S(2)}) collective-permute-start(bf16[128,2304]{1,0:T(8,128)(2,1)} %reduce-scatter.2.cloned.1.call-done), channel_id=1, source_target_pairs={{8,1},{1,8},{24,17},{17,24},{40,33},{33,40},{56,49},{49,56},{72,65... | collective-permute-start | bytes 1769480 | tf_op jit(solution)/shard_map/ppermute | solution.py:822
  276.5 7.6 %collective-permute-done.11.refs_1_ = bf16[128,2048]{1,0:T(8,128)(2,1)S(1)} collective-permute-done((bf16[128,2048]{1,0:T(8,128)(2,1)}, bf16[128,2048]{1,0:T(8,128)(2,1)S(1)}, u32[]{:S(2)}, u32[]{:S(2)}) %collective-permute-start.11) | collective-permute-done | bytes 524320 | tf_op jit(solution)/shard_map/ppermute | solution.py:774
  284.1 9.7 %collective-permute-done.12.refs_2_ = bf16[128,2048]{1,0:T(8,128)(2,1)S(1)} collective-permute-done((bf16[128,2048]{1,0:T(8,128)(2,1)}, bf16[128,2048]{1,0:T(8,128)(2,1)S(1)}, u32[]{:S(2)}, u32[]{:S(2)}) %collective-permute-start.12) | collective-permute-done | bytes 524320 | tf_op jit(solution)/shard_map/ppermute | solution.py:774
  293.8 1.6 collective-permute-done.13.refs_3_
  296.0 1.5 collective-permute-start.14
  297.6 24.3 %collective-permute-done.15 = bf16[128,2304]{1,0:T(8,128)(2,1)} collective-permute-done((bf16[128,2304]{1,0:T(8,128)(2,1)}, bf16[128,2304]{1,0:T(8,128)(2,1)}, u32[]{:S(2)}, u32[]{:S(2)}) %collective-permute-start.15) | collective-permute-done | bytes 589856 | tf_op jit(solution)/shard_map/ppermute | solution.py:822
  323.0 1.8 collective-permute-start.21
  324.8 2.2 collective-permute-start.22
  327.4 3.1 all-to-all-done.6.refs_0_
  330.5 2.7 shard_map.280
  333.2 1.9 collective-permute-start.17
  336.5 6.1 %collective-permute-done.17 = bf16[128,1024]{1,0:T(8,128)(2,1)S(1)} collective-permute-done((bf16[128,1024]{1,0:T(8,128)(2,1)S(1)}, bf16[128,1024]{1,0:T(8,128)(2,1)S(1)}, u32[]{:S(2)}, u32[]{:S(2)}) %collective-permute-start.17) | collective-permute-done | bytes 262176 | tf_op jit(solution)/shard_map/ppermute | solution.py:822
  343.4 2.7 collective-permute-start.20
  346.3 2.8 collective-permute-done.23.b3
  349.2 4.5 %shard_map.282 = (f32[128,3072]{1,0:T(8,128)}, f32[128,3072]{1,0:T(8,128)}, f32[3072,128]{1,0:T(8,128)}, f32[128,128]{1,0:T(8,128)S(1)}) custom-call(s32[1]{0:T(128)} %bitcast.40.turn_at, bf16[128,2304]{1,0:T(8,128)(2,1)S(1)} %broadcast_select_fusion.1.refs_2_.b0, bf16[128,2304]{1,0:T(8,128)(2,1)} %collective-permute-done.21.b1, ...), custom_call_target="tpu_custom_call" | custom-call | flops 1048576 | bytes 8388608 | tf_op jit(solution)/shard_map/pallas_call | solution.py:726
  353.8 2.9 collective-permute-done.18.b1
  356.6 3.8 %collective-permute-done.20.b3 = bf16[128,1024]{1,0:T(8,128)(2,1)} collective-permute-done((bf16[128,1024]{1,0:T(8,128)(2,1)}, bf16[128,1024]{1,0:T(8,128)(2,1)}, u32[]{:S(2)}, u32[]{:S(2)}) %collective-permute-start.20) | collective-permute-done | bytes 262176 | tf_op jit(solution)/shard_map/ppermute | solution.py:774
  363.3 3.5 shard_map.281
  367.5 1.8 collective-permute-done.24
  369.9 1.4 broadcast_select_fusion
  371.3 1.6 fusion
  (216 shorter events, 52.8 us)
Async XLA Ops:
  7.2 5.6 %copy-start = (bf16[3072,128]{1,0:T(8,128)(2,1)S(1)}, bf16[3072,128]{1,0:T(8,128)(2,1)}, u32[]{:S(2)}) copy-start(bf16[3072,128]{1,0:T(8,128)(2,1)} %param.30) | copy-start | bytes 2359300
  7.2 6.8 %copy-start.55 = (bf16[128]{0:T(256)(128)(2,1)S(1)}, bf16[128]{0:T(256)(128)(2,1)}, u32[]{:S(2)}) copy-start(bf16[128]{0:T(256)(128)(2,1)} %param.27) | copy-start | bytes 772
  7.2 62.8 %all-gather.3.cloned.1.call-start = ((), (), s32[]{:S(2)}) async-start(), calls=%async_computation.8 | async-start | bytes 5013504 | tf_op jit(solution)/shard_map/all_gather | solution.py:787
  12.7 135.4 %all-gather.5.cloned.1.call-start = ((), (), s32[]{:S(2)}) async-start(), calls=%async_computation.9 | async-start | bytes 10027008 | tf_op jit(solution)/shard_map/all_gather | solution.py:787
  14.0 13.3 %copy-start.51 = (bf16[128,2048]{1,0:T(8,128)(2,1)S(1)}, bf16[128,2048]{1,0:T(8,128)(2,1)}, u32[]{:S(2)}) copy-start(bf16[128,2048]{1,0:T(8,128)(2,1)} %param.31) | copy-start | bytes 1572868
  14.0 13.3 %copy-start.52 = (bf16[128,2048]{1,0:T(8,128)(2,1)S(1)}, bf16[128,2048]{1,0:T(8,128)(2,1)}, u32[]{:S(2)}) copy-start(bf16[128,2048]{1,0:T(8,128)(2,1)} %param.16) | copy-start | bytes 1572868
  14.2 12.1 %collective-permute-start.6 = (bf16[128,2304]{1,0:T(8,128)(2,1)S(1)}, bf16[128,2304]{1,0:T(8,128)(2,1)S(1)}, u32[]{:S(2)}, u32[]{:S(2)}) collective-permute-start(bf16[128,2304]{1,0:T(8,128)(2,1)S(1)} %pad_maximum_fusion.1), channel_id=1, source_target_pairs={{8,1},{1,8},{24,17},{17,24},{40,33},{33,40},{56,49},{49,56},{72,65... | collective-permute-start | bytes 1769480 | tf_op jit(solution)/shard_map/ppermute | solution.py:822
  27.4 2.0 collective-permute-start
  31.9 5.3 %copy-start.53 = (s32[1,13]{1,0:T(1,128)S(1)}, s32[1,13]{1,0:T(1,128)}, u32[]{:S(2)}) copy-start(s32[1,13]{1,0:T(1,128)} %param.18) | copy-start | bytes 160
  31.9 5.3 %copy-start.54 = (s32[1,13]{1,0:T(1,128)S(1)}, s32[1,13]{1,0:T(1,128)}, u32[]{:S(2)}) copy-start(s32[1,13]{1,0:T(1,128)} %param.17) | copy-start | bytes 160
  31.9 31.3 %all-to-all-start = ((bf16[4,128,2048]{2,1,0:T(8,128)(2,1)}), bf16[4,128,2048]{2,1,0:T(8,128)(2,1)S(1)}, u32[]{:S(2)}, u32[]{:S(2)}) async-start(bf16[4,128,2048]{2,1,0:T(8,128)(2,1)} %broadcast_in_dim.26), calls=%async_computation | async-start | bytes 4194304 | tf_op jit(solution)/shard_map/all_to_all | solution.py:771
  37.2 27.6 %collective-permute-start.2 = (s32[2,13]{1,0:T(2,128)S(1)}, s32[2,13]{1,0:T(2,128)S(1)}, u32[]{:S(2)}, u32[]{:S(2)}) collective-permute-start(s32[2,13]{1,0:T(2,128)S(1)} %pad_add_fusion.2), channel_id=1, source_target_pairs={{0,8},{8,0},{16,24},{24,16},{32,40},{40,32},{48,56},{56,48},{64,72... | collective-permute-start | bytes 320 | tf_op jit(solution)/shard_map/ppermute | solution.py:768
  63.2 6.8 %copy-start.47 = (bf16[4,128,2048]{2,1,0:T(8,128)(2,1)}, bf16[4,128,2048]{2,1,0:T(8,128)(2,1)S(1)}, u32[]{:S(2)}) copy-start(bf16[4,128,2048]{2,1,0:T(8,128)(2,1)S(1)} %all-to-all-done.refs_0_.refs_2_.refs_1_) | copy-start | bytes 6291460
  63.2 5.2 %collective-permute-start.1 = (bf16[4,128,2048]{2,1,0:T(8,128)(2,1)S(1)}, bf16[4,128,2048]{2,1,0:T(8,128)(2,1)}, u32[]{:S(2)}, u32[]{:S(2)}) collective-permute-start(bf16[4,128,2048]{2,1,0:T(8,128)(2,1)S(1)} %all-to-all-done.refs_0_.refs_2_.refs_1_), channel_id=1, source_target_pairs={{0,8},{8,0},{16,24},{24,16},{32,40},{40,32},{48,56},{56,48},{64,72... | collective-permute-start | bytes 6291464 | tf_op jit(solution)/shard_map/ppermute | solution.py:768
  66.9 15.6 %copy-start.14 = (f32[512,128]{1,0:T(8,128)}, f32[512,128]{1,0:T(8,128)S(1)}, u32[]{:S(2)}) copy-start(f32[512,128]{1,0:T(8,128)S(1)} %get-tuple-element.71.refs_4_.refs_5_) | copy-start | bytes 786436
  72.5 5.0 %collective-permute-start.3 = (bf16[8,128,1152]{2,1,0:T(8,128)(2,1)S(1)}, bf16[8,128,1152]{2,1,0:T(8,128)(2,1)}, u32[]{:S(2)}, u32[]{:S(2)}) collective-permute-start(bf16[8,128,1152]{2,1,0:T(8,128)(2,1)S(1)} %shard_map.263), channel_id=1, source_target_pairs={{0,8},{8,0},{16,24},{24,16},{32,40},{40,32},{48,56},{56,48},{64,72... | collective-permute-start | bytes 7077896 | tf_op jit(solution)/shard_map/ppermute | solution.py:768
  89.7 6.4 %copy-start.24 = (bf16[512,512]{1,0:T(8,128)(2,1)}, bf16[512,512]{1,0:T(8,128)(2,1)S(1)}, u32[]{:S(2)}) copy-start(bf16[512,512]{1,0:T(8,128)(2,1)S(1)} %get-tuple-element.74.refs_0_.refs_1_) | copy-start | bytes 1572868
  89.7 6.4 %copy-start.26 = (f32[512,256]{1,0:T(8,128)}, f32[512,256]{1,0:T(8,128)S(1)}, u32[]{:S(2)}) copy-start(f32[512,256]{1,0:T(8,128)S(1)} %get-tuple-element.75.refs_1_.refs_3_) | copy-start | bytes 1572868
  89.7 6.4 %copy-start.34 = (f32[512,384]{1,0:T(8,128)}, f32[512,384]{1,0:T(8,128)S(1)}, u32[]{:S(2)}) copy-start(f32[512,384]{1,0:T(8,128)S(1)} %get-tuple-element.94.refs_3_) | copy-start | bytes 2359300
  96.1 4.1 %copy-start.38 = (f32[512,256]{1,0:T(8,128)}, f32[512,256]{1,0:T(8,128)S(1)}, u32[]{:S(2)}) copy-start(f32[512,256]{1,0:T(8,128)S(1)} %get-tuple-element.92.refs_4_) | copy-start | bytes 1572868
  96.1 4.1 %copy-start.42 = (bf16[512,256]{1,0:T(8,128)(2,1)}, bf16[512,256]{1,0:T(8,128)(2,1)S(1)}, u32[]{:S(2)}) copy-start(bf16[512,256]{1,0:T(8,128)(2,1)S(1)} %get-tuple-element.98.refs_5_) | copy-start | bytes 786436
  96.2 2.8 collective-permute-start.4
  98.9 5.6 %copy-start.49 = (bf16[128,2048]{1,0:T(8,128)(2,1)S(1)}, bf16[128,2048]{1,0:T(8,128)(2,1)}, u32[]{:S(2)}) copy-start(bf16[128,2048]{1,0:T(8,128)(2,1)} %copy-done.48) | copy-start | bytes 1572868
  100.3 18.7 %all-to-all-start.1 = ((bf16[4,64,2048]{2,1,0:T(8,128)(2,1)}), bf16[4,64,2048]{2,1,0:T(8,128)(2,1)S(1)}, u32[]{:S(2)}, u32[]{:S(2)}) async-start(bf16[4,64,2048]{2,1,0:T(8,128)(2,1)} %bitcast.19), calls=%async_computation.1 | async-start | bytes 2097152 | tf_op jit(solution)/shard_map/all_to_all | solution.py:771
  104.5 158.5 %reduce-scatter.2.cloned.1.call-start = ((), (), s32[]{:S(2)}) async-start(), calls=%async_computation.10 | async-start | bytes 10027008 | tf_op jit(solution)/shard_map/reduce_scatter | solution.py:790
  137.0 4.9 %collective-permute-start.5 = (bf16[4,64,2048]{2,1,0:T(8,128)(2,1)S(1)}, bf16[4,64,2048]{2,1,0:T(8,128)(2,1)S(1)}, u32[]{:S(2)}, u32[]{:S(2)}) collective-permute-start(bf16[4,64,2048]{2,1,0:T(8,128)(2,1)S(1)} %all_to_all.35), channel_id=1, source_target_pairs={{0,8},{8,0},{16,24},{24,16},{32,40},{40,32},{48,56},{56,48},{64,72... | collective-permute-start | bytes 3145736 | tf_op jit(solution)/shard_map/ppermute | solution.py:768
  149.3 8.6 %copy-start.3 = (bf16[2048,512]{1,0:T(8,128)(2,1)S(1)}, bf16[2048,512]{1,0:T(8,128)(2,1)}, u32[]{:S(2)}) copy-start(bf16[2048,512]{1,0:T(8,128)(2,1)} %copy-done.2) | copy-start | bytes 6291460
  177.2 3.0 collective-permute-start.7
  180.2 19.6 %copy-start.19 = (f32[64,2048]{1,0:T(8,128)S(1)}, f32[64,2048]{1,0:T(8,128)}, u32[]{:S(2)}) copy-start(f32[64,2048]{1,0:T(8,128)} %copy-done.18) | copy-start | bytes 1572868
  180.2 19.6 %copy-start.33 = (bf16[64,2048]{1,0:T(8,128)(2,1)S(1)}, bf16[64,2048]{1,0:T(8,128)(2,1)}, u32[]{:S(2)}) copy-start(bf16[64,2048]{1,0:T(8,128)(2,1)} %get-tuple-element.140.refs_2_) | copy-start | bytes 786436
  202.1 16.9 %all-to-all-start.4 = ((bf16[4,64,2048]{2,1,0:T(8,128)(2,1)}), bf16[4,64,2048]{2,1,0:T(8,128)(2,1)S(1)}, u32[]{:S(2)}, u32[]{:S(2)}) async-start(bf16[4,64,2048]{2,1,0:T(8,128)(2,1)} %copy-done.32), calls=%async_computation.4 | async-start | bytes 2097152 | tf_op jit(solution)/shard_map/all_to_all | solution.py:771
  218.9 6.4 %collective-permute-start.8 = (bf16[4,64,2048]{2,1,0:T(8,128)(2,1)S(1)}, bf16[4,64,2048]{2,1,0:T(8,128)(2,1)S(1)}, u32[]{:S(2)}, u32[]{:S(2)}) collective-permute-start(bf16[4,64,2048]{2,1,0:T(8,128)(2,1)S(1)} %all-to-all-done.4), channel_id=1, source_target_pairs={{0,8},{8,0},{16,24},{24,16},{32,40},{40,32},{48,56},{56,48},{64,72... | collective-permute-start | bytes 3145736 | tf_op jit(solution)/shard_map/ppermute | solution.py:768
  221.6 27.0 %collective-permute-start.9 = (bf16[256,2048]{1,0:T(8,128)(2,1)}, bf16[256,2048]{1,0:T(8,128)(2,1)}, u32[]{:S(2)}, u32[]{:S(2)}) collective-permute-start(bf16[256,2048]{1,0:T(8,128)(2,1)} %copy-done.46), channel_id=1, source_target_pairs={{0,8},{8,0},{16,24},{24,16},{32,40},{40,32},{48,56},{56,48},{64,72... | collective-permute-start | bytes 3145736 | tf_op jit(solution)/shard_map/ppermute | solution.py:768
  227.5 2.2 copy-start.15
  227.5 2.2 copy-start.21
  227.5 2.2 copy-start.25
  227.5 2.3 copy-start.35
  229.8 3.2 copy-start.43
  237.4 11.2 %copy-start.31 = (bf16[256,2048]{1,0:T(8,128)(2,1)S(1)}, bf16[256,2048]{1,0:T(8,128)(2,1)}, u32[]{:S(2)}) copy-start(bf16[256,2048]{1,0:T(8,128)(2,1)} %copy-done.30) | copy-start | bytes 3145732
  241.6 19.7 %collective-permute-start.10 = (bf16[256,2048]{1,0:T(8,128)(2,1)S(1)}, bf16[256,2048]{1,0:T(8,128)(2,1)}, u32[]{:S(2)}, u32[]{:S(2)}) collective-permute-start(bf16[256,2048]{1,0:T(8,128)(2,1)S(1)} %get-tuple-element.102), channel_id=1, source_target_pairs={{0,8},{8,0},{16,24},{24,16},{32,40},{40,32},{48,56},{56,48},{64,72... | collective-permute-start | bytes 3145736 | tf_op jit(solution)/shard_map/ppermute | solution.py:768
  243.2 18.0 %all-to-all-start.5 = ((bf16[128,8,128]{2,1,0:T(8,128)(2,1)}), bf16[128,8,128]{2,1,0:T(8,128)(2,1)S(1)}, u32[]{:S(2)}, u32[]{:S(2)}) async-start(bf16[128,8,128]{2,1,0:T(8,128)(2,1)} %broadcast_in_dim.56), calls=%async_computation.6 | async-start | bytes 524288 | tf_op jit(solution)/shard_map/all_to_all | solution.py:902
  263.0 4.8 %copy-start.50 = (bf16[256,2048]{1,0:T(8,128)(2,1)S(1)}, bf16[256,2048]{1,0:T(8,128)(2,1)}, u32[]{:S(2)}) copy-start(bf16[256,2048]{1,0:T(8,128)(2,1)} %add_convert_fusion.1) | copy-start | bytes 3145732
  263.0 67.5 %all-to-all-start.6 = ((bf16[16,128,1024]{2,1,0:T(8,128)(2,1)}), bf16[16,128,1024]{2,1,0:T(8,128)(2,1)}, u32[]{:S(2)}, u32[]{:S(2)}) async-start(bf16[16,128,1024]{2,1,0:T(8,128)(2,1)} %bitcast.98), calls=%async_computation.7 | async-start | bytes 8388608 | tf_op jit(solution)/shard_map/all_to_all | solution.py:795
  268.0 27.4 %copy-start.17 = (bf16[64,2048]{1,0:T(8,128)(2,1)S(1)}, bf16[64,2048]{1,0:T(8,128)(2,1)}, u32[]{:S(2)}) copy-start(bf16[64,2048]{1,0:T(8,128)(2,1)} %get-tuple-element.141.refs_1_.refs_6_) | copy-start | bytes 786436
  268.0 27.4 %copy-start.20 = (f32[64,2048]{1,0:T(8,128)S(1)}, f32[64,2048]{1,0:T(8,128)}, u32[]{:S(2)}) copy-start(f32[64,2048]{1,0:T(8,128)} %copy-done.18) | copy-start | bytes 1572868
  268.0 27.4 %copy-start.37 = (f32[64,2048]{1,0:T(8,128)S(1)}, f32[64,2048]{1,0:T(8,128)}, u32[]{:S(2)}) copy-start(f32[64,2048]{1,0:T(8,128)} %copy-done.36) | copy-start | bytes 1572868
  269.2 14.9 %collective-permute-start.11 = (bf16[128,2048]{1,0:T(8,128)(2,1)}, bf16[128,2048]{1,0:T(8,128)(2,1)S(1)}, u32[]{:S(2)}, u32[]{:S(2)}) collective-permute-start(bf16[128,2048]{1,0:T(8,128)(2,1)} %get-tuple-element.132), channel_id=1, source_target_pairs={{0,2},{2,4},{4,6},{6,0},{1,3},{3,5},{5,7},{7,1},{8,10},{10,12},{12... | collective-permute-start | bytes 1572872 | tf_op jit(solution)/shard_map/ppermute | solution.py:774
  269.3 24.5 %collective-permute-start.12 = (bf16[128,2048]{1,0:T(8,128)(2,1)}, bf16[128,2048]{1,0:T(8,128)(2,1)S(1)}, u32[]{:S(2)}, u32[]{:S(2)}) collective-permute-start(bf16[128,2048]{1,0:T(8,128)(2,1)} %get-tuple-element.131), channel_id=1, source_target_pairs={{0,4},{2,6},{4,0},{6,2},{1,5},{3,7},{5,1},{7,3},{8,12},{10,14},{12... | collective-permute-start | bytes 1572872 | tf_op jit(solution)/shard_map/ppermute | solution.py:774
  270.8 24.6 %collective-permute-start.13 = (bf16[128,2048]{1,0:T(8,128)(2,1)}, bf16[128,2048]{1,0:T(8,128)(2,1)S(1)}, u32[]{:S(2)}, u32[]{:S(2)}) collective-permute-start(bf16[128,2048]{1,0:T(8,128)(2,1)} %get-tuple-element.130), channel_id=1, source_target_pairs={{0,6},{2,0},{4,2},{6,4},{1,7},{3,1},{5,3},{7,5},{8,14},{10,8},{12,... | collective-permute-start | bytes 1572872 | tf_op jit(solution)/shard_map/ppermute | solution.py:774
  272.5 49.3 %collective-permute-start.15 = (bf16[128,2304]{1,0:T(8,128)(2,1)}, bf16[128,2304]{1,0:T(8,128)(2,1)}, u32[]{:S(2)}, u32[]{:S(2)}) collective-permute-start(bf16[128,2304]{1,0:T(8,128)(2,1)} %reduce-scatter.2.cloned.1.call-done), channel_id=1, source_target_pairs={{8,1},{1,8},{24,17},{17,24},{40,33},{33,40},{56,49},{49,56},{72,65... | collective-permute-start | bytes 1769480 | tf_op jit(solution)/shard_map/ppermute | solution.py:822
  296.0 31.0 %collective-permute-start.14 = (bf16[128,2048]{1,0:T(8,128)(2,1)S(1)}, bf16[128,2048]{1,0:T(8,128)(2,1)S(1)}, u32[]{:S(2)}, u32[]{:S(2)}) collective-permute-start(bf16[128,2048]{1,0:T(8,128)(2,1)S(1)} %shard_map.279), channel_id=1, source_target_pairs={{0,8},{8,0},{16,24},{24,16},{32,40},{40,32},{48,56},{56,48},{64,72... | collective-permute-start | bytes 1572872 | tf_op jit(solution)/shard_map/ppermute | solution.py:768
  323.0 20.4 %collective-permute-start.21 = (bf16[128,2304]{1,0:T(8,128)(2,1)S(1)}, bf16[128,2304]{1,0:T(8,128)(2,1)}, u32[]{:S(2)}, u32[]{:S(2)}) collective-permute-start(bf16[128,2304]{1,0:T(8,128)(2,1)S(1)} %broadcast_select_fusion.1.refs_2_.b0), channel_id=1, source_target_pairs={{0,2},{2,4},{4,6},{6,0},{1,3},{3,5},{5,7},{7,1},{8,10},{10,12},{12... | collective-permute-start | bytes 1769480 | tf_op jit(solution)/shard_map/ppermute | solution.py:774
  324.8 18.5 %collective-permute-start.22 = (bf16[128,2304]{1,0:T(8,128)(2,1)S(1)}, bf16[128,2304]{1,0:T(8,128)(2,1)}, u32[]{:S(2)}, u32[]{:S(2)}) collective-permute-start(bf16[128,2304]{1,0:T(8,128)(2,1)S(1)} %broadcast_select_fusion.1.refs_2_.b0), channel_id=1, source_target_pairs={{0,4},{2,6},{4,0},{6,2},{1,5},{3,7},{5,1},{7,3},{8,12},{10,14},{12... | collective-permute-start | bytes 1769480 | tf_op jit(solution)/shard_map/ppermute | solution.py:774
  327.4 21.8 %copy-start.28 = (bf16[128,3072]{1,0:T(8,128)(2,1)S(1)}, bf16[128,3072]{1,0:T(8,128)(2,1)}, u32[]{:S(2)}) copy-start(bf16[128,3072]{1,0:T(8,128)(2,1)} %w_up.1) | copy-start | bytes 2359300
  327.4 21.8 %copy-start.29 = (bf16[128,3072]{1,0:T(8,128)(2,1)S(1)}, bf16[128,3072]{1,0:T(8,128)(2,1)}, u32[]{:S(2)}) copy-start(bf16[128,3072]{1,0:T(8,128)(2,1)} %w_gate.1) | copy-start | bytes 2359300
  333.2 9.4 %collective-permute-start.17 = (bf16[128,1024]{1,0:T(8,128)(2,1)S(1)}, bf16[128,1024]{1,0:T(8,128)(2,1)S(1)}, u32[]{:S(2)}, u32[]{:S(2)}) collective-permute-start(bf16[128,1024]{1,0:T(8,128)(2,1)S(1)} %shard_map.280), channel_id=1, source_target_pairs={{8,1},{1,8},{24,17},{17,24},{40,33},{33,40},{56,49},{49,56},{72,65... | collective-permute-start | bytes 786440 | tf_op jit(solution)/shard_map/ppermute | solution.py:822
  335.2 14.0 %collective-permute-start.23 = (bf16[128,2304]{1,0:T(8,128)(2,1)S(1)}, bf16[128,2304]{1,0:T(8,128)(2,1)}, u32[]{:S(2)}, u32[]{:S(2)}) collective-permute-start(bf16[128,2304]{1,0:T(8,128)(2,1)S(1)} %broadcast_select_fusion.1.refs_2_.b0), channel_id=1, source_target_pairs={{0,6},{2,0},{4,2},{6,4},{1,7},{3,1},{5,3},{7,5},{8,14},{10,8},{12,... | collective-permute-start | bytes 1769480 | tf_op jit(solution)/shard_map/ppermute | solution.py:774
  335.2 34.6 %collective-permute-start.16 = (bf16[2,128,2048]{2,1,0:T(8,128)(2,1)S(1)}, bf16[2,128,2048]{2,1,0:T(8,128)(2,1)}, u32[]{:S(2)}, u32[]{:S(2)}) collective-permute-start(bf16[2,128,2048]{2,1,0:T(8,128)(2,1)S(1)} %pad_maximum_fusion.refs_1_), channel_id=1, source_target_pairs={{0,1},{9,8},{16,17},{25,24},{32,33},{41,40},{48,49},{57,56},{64,65... | collective-permute-start | bytes 3145736 | tf_op jit(solution)/shard_map/ppermute | solution.py:944
  343.4 13.3 %collective-permute-start.18 = (bf16[128,1024]{1,0:T(8,128)(2,1)}, bf16[128,1024]{1,0:T(8,128)(2,1)}, u32[]{:S(2)}, u32[]{:S(2)}) collective-permute-start(bf16[128,1024]{1,0:T(8,128)(2,1)} %broadcast_select_fusion.3.b0), channel_id=1, source_target_pairs={{0,2},{2,4},{4,6},{6,0},{1,3},{3,5},{5,7},{7,1},{8,10},{10,12},{12... | collective-permute-start | bytes 786440 | tf_op jit(solution)/shard_map/ppermute | solution.py:774
  343.4 13.3 %collective-permute-start.19 = (bf16[128,1024]{1,0:T(8,128)(2,1)}, bf16[128,1024]{1,0:T(8,128)(2,1)}, u32[]{:S(2)}, u32[]{:S(2)}) collective-permute-start(bf16[128,1024]{1,0:T(8,128)(2,1)} %broadcast_select_fusion.3.b0), channel_id=1, source_target_pairs={{0,4},{2,6},{4,0},{6,2},{1,5},{3,7},{5,1},{7,3},{8,12},{10,14},{12... | collective-permute-start | bytes 786440 | tf_op jit(solution)/shard_map/ppermute | solution.py:774
  343.4 17.1 %collective-permute-start.20 = (bf16[128,1024]{1,0:T(8,128)(2,1)}, bf16[128,1024]{1,0:T(8,128)(2,1)}, u32[]{:S(2)}, u32[]{:S(2)}) collective-permute-start(bf16[128,1024]{1,0:T(8,128)(2,1)} %broadcast_select_fusion.3.b0), channel_id=1, source_target_pairs={{0,6},{2,0},{4,2},{6,4},{1,7},{3,1},{5,3},{7,5},{8,14},{10,8},{12,... | collective-permute-start | bytes 786440 | tf_op jit(solution)/shard_map/ppermute | solution.py:774
  346.1 14.3 %copy-start.44 = (bf16[128,512]{1,0:T(8,128)(2,1)S(1)}, bf16[128,512]{1,0:T(8,128)(2,1)}, u32[]{:S(2)}) copy-start(bf16[128,512]{1,0:T(8,128)(2,1)} %wv.1) | copy-start | bytes 393220
  366.9 2.5 collective-permute-start.24
  369.9 3.0 copy-start.1
  (25 other events, 25.9 us)
Sparse Core Ops, SparseCore 0:
  12.8 57.1 all-gather.2
  72.7 75.2 all-gather.4
  169.1 88.2 reduce-scatter.1

commit v9 on v8

--- a/solution.py
+++ b/solution.py
@@ -728,6 +728,48 @@
     )
 
 
+def column(row):
+    shape = (HD, HD)
+    there = lax.broadcasted_iota(jnp.int32, shape, 0) == lax.broadcasted_iota(jnp.int32, shape, 1)
+    return jnp.sum(jnp.where(there, jnp.broadcast_to(row, shape), 0.0), axis=1, keepdims=True)
+
+
+def first_kernel(at, wq, wk, wv, wg, wo, gain, gain_q, gain_k, out):
+    scale = column(gain[...].astype(F32))
+    start = 0
+    for w in (wq, wk, wv, wg):
+        stop = start + w.shape[1]
+        out[:, start:stop] = (w[...].astype(F32) * scale).astype(BF16)
+        start = stop
+    out[:, start : start + wo.shape[0]] = wo[...].T
+    start += wo.shape[0]
+    count = gain_q.shape[1]
+    lane = lax.broadcasted_iota(jnp.int32, (count, HD), 1)
+    spot = lax.broadcasted_iota(jnp.int32, (count, HD), 0) + at[1] * count
+    there = jnp.where(lane == spot, 1.0, 0.0)
+    ends = [dot(g[...].astype(F32), there) for g in (gain_q, gain_k)]
+    ends = jnp.concatenate(ends + [jnp.zeros((14, HD), F32)], axis=0)
+    out[:16, start:] = ends.astype(BF16)
+    out[16:, start:] = jnp.zeros((HD - 16, HD), BF16)
+
+
+def first_columns(at, wq, wk, wv, wg, wo, gain, gain_q, gain_k):
+    quarter = lambda w: pl.BlockSpec((w.shape[0], w.shape[1] // 4), lambda i, at: (0, at[0]))
+    row = lambda g: pl.BlockSpec(g.shape, lambda i, at: (0, 0))
+    rows = wq.shape[0]
+    heads = wo.shape[0] // 4
+    columns = sum(w.shape[1] // 4 for w in (wq, wk, wv, wg)) + heads + HD
+    return prefetched(
+        first_kernel,
+        (1,),
+        [quarter(w) for w in (wq, wk, wv, wg)]
+        + [pl.BlockSpec((heads, rows), lambda i, at: (at[0], 0))]
+        + [row(g) for g in (gain, gain_q, gain_k)],
+        pl.BlockSpec((rows, columns), lambda i, at: (0, 0)),
+        struct((rows, columns), BF16),
+    )(at, wq, wk, wv, wg, wo, gain, gain_q, gain_k)
+
+
 def make_shards(mesh):
     n_shard, n_ctx, n_tp = mesh.shape["shard"], mesh.shape["ctx"], mesh.shape["tp"]
     pairs = n_shard // 2
@@ -748,21 +790,6 @@
         )
     ]
     across_perm = [(joint(pair, t, t), joint(pair, t, 1 - t)) for pair in range(pairs) for t in range(2)]
-
-    def spot(pair, core, ctx, tp):
-        return ((pair * 2 + core) * n_ctx + ctx) * n_tp + tp
-
-    owner_perms = [
-        [
-            (spot(pair, core, ctx, tp), spot(pair, tp, (ctx + by) % n_ctx, core))
-            for pair in range(pairs)
-            for core in range(2)
-            for ctx in range(n_ctx)
-            for tp in range(n_tp)
-            if by > 0 or core != tp
-        ]
-        for by in range(n_ctx)
-    ]
 
     def core_swap(value):
         return lax.ppermute(value, "shard", core_perm)
@@ -827,17 +854,18 @@
 
         gain_one = gain_in.astype(F32)[:, None]
         gain_two = gain_mid.astype(F32)[:, None]
-        first = jnp.concatenate(
-            [quarter(w, 1) for w in (w_query, w_key, w_value, w_gate_attn)], axis=1
+        head_rows = gain_query.shape[0]
+        first = first_columns(
+            jnp.stack([ctx, lax.axis_index("shard")]).astype(jnp.int32),
+            w_query,
+            w_key,
+            w_value,
+            w_gate_attn,
+            w_out,
+            gain_in[None],
+            gain_query[None],
+            gain_key[None],
         )
-        first = (first.astype(F32) * gain_one).astype(BF16)
-        head_rows = gain_query.shape[0]
-        ends = lax.dynamic_update_slice(
-            jnp.zeros((gain_in.shape[0], HD), BF16),
-            jnp.stack([gain_query, gain_key]),
-            (0, lax.axis_index("shard") * head_rows),
-        )
-        first = jnp.concatenate([first, quarter(w_out, 0).T, ends], axis=1)
         found = plane_gather(first)
 
         def half_rows(place):
@@ -906,18 +934,15 @@
         attn = attend_grads(x_flip, da, db, d_qkv, d_gate_pre, gated, ())
         in_mine, in_other = input_back(d_qkv, d_gate_pre, w1, (attn,))
         layer_half, in_half = tree_half(layer_mine, layer_other), tree_half(in_mine, in_other)
-        attn, layer_half, in_half, grad_ffn, head_ends = lax.optimization_barrier(
-            (attn, layer_half, in_half, grad_ffn, head_ends)
+        own_ffn = swapped(grad_ffn)
+        attn, layer_half, in_half, own_ffn, head_ends = lax.optimization_barrier(
+            (attn, layer_half, in_half, own_ffn, head_ends)
         )
         attn_parts = plane_exchange(attn.reshape(n_shard, -1, attn.shape[1]))
 
         def owners(block):
-            block = swapped(block)
             return [block] + [ctx_turn(block, by) for by in range(1, n_ctx)]
 
-        def owners_at_once(block):
-            moved = [lax.ppermute(block, ("shard", "ctx", "tp"), perm) for perm in owner_perms]
-            return [jnp.where(native, block, moved[0])] + moved[1:]
 
         both = jnp.concatenate(
             [layer_half, in_half], axis=1
@@ -927,7 +952,7 @@
             for by in range(1, n_ctx)
         ]
         ends = ends_step(parts, middle, d_middle, own_x)
-        ffn_blocks = owners(grad_ffn)
+        ffn_blocks = owners(own_ffn)
         sibling = core_swap(ends)
 
         def whole(start):
@@ -939,10 +964,6 @@
             )
 
         full = jnp.stack([whole(0), whole(rows)])
-        attn_sum = sum_step(attn_parts, (full, ffn_blocks[0]))
-        full, attn_sum = lax.optimization_barrier((full, attn_sum))
-        full = jnp.where(native, full, lax.ppermute(full, PLANE, across_perm))
-
         turn_at = ctx.astype(jnp.int32).reshape(1)
         size = gain_in.shape[0]
         grad_gate, grad_up, grad_down, mid_sums = close(
@@ -954,7 +975,11 @@
             w_down.shape,
             [(size, HD)],
         )
-        attn_blocks = owners(attn_sum)
+        attn_sum = sum_step(attn_parts, (full, mid_sums))
+        full, attn_sum = lax.optimization_barrier((full, attn_sum))
+        full = jnp.where(native, full, lax.ppermute(full, PLANE, across_perm))
+
+        attn_blocks = owners(swapped(attn_sum))
         grad_query, grad_key, grad_value, grad_gate_attn, grad_out, in_sums = close(
             close_attend_kernel,
             turn_at,

time: 385 us -> 387 us (level)
    ppermute x9, waiting for transfers between devices: 28.3 us -> 50.1 us  [ctx_turn(): lax.ppermute(value, 'ctx', [(i, (i + by) % n_ctx) for i in range(n_ctx)])]
    ppermute x3, waiting for transfers between devices: 37.9 us -> 19.2 us  [swapped(): return jnp.where(native, value, lax.ppermute(value, PLANE, swap_perm))]
    all_to_all x1, waiting for transfers between devices: 9.96 us -> 0.01 us  [shards(): lax.all_to_all(pieces.reshape(n_shard * copies, 8, HD), ('shard', 'ctx',...]
    reduce_scatter x1, waiting for transfers between devices: 0.02 us -> 6.03 us  [plane_scatter(): lax.psum_scatter(value, PLANE, scatter_dimension=0, tiled=True, axis_inde...]
    unnamed x114 -> x134, local copies, waits for them, and re-layouts: 26.3 us -> 30.2 us
  transfers between devices with their start and end apart: 33 -> 33, of which waited for: 24 -> 25; matrix products, arithmetic and copies ran while one was open for 5% -> 5% of each run, Pallas kernels for 15% -> 14%
where the time goes in v9:
time: 387 us; the launch traced here: 381 us
  waiting for transfers between devices  144 us (37%)
  Pallas kernels  75.8 us (20%)
  starting transfers between devices  59.6 us (15%)
  local copies, waits for them, and re-layouts  37.8 us (10%)
  blocking collectives  34.1 us (9%)
  between operations  14.6 us (4%)
  other arithmetic  14.5 us (4%)
    pallas_call x16, Pallas kernels, call(): return lambda *operands: built(*operands, *behind)  60.2 us
    ppermute x9, waiting for transfers between devices, ctx_turn(): lax.ppermute(value, 'ctx', [(i, (i + by) % n_ctx) for i in range(n_ctx)])  50.1 us
    all_to_all x3, waiting for transfers between devices, ctx_exchange(): return lax.all_to_all(value, 'ctx', 0, 0)  41 us
    all_to_all x2, blocking collectives, ctx_exchange(): return lax.all_to_all(value, 'ctx', 0, 0)  34.1 us
    unnamed x134, local copies, waits for them, and re-layouts  30.2 us
    ppermute x3, waiting for transfers between devices, swapped(): return jnp.where(native, value, lax.ppermute(value, PLANE, swap_perm))  19.2 us
    ppermute x11, waiting for transfers between devices, core_swap(): return lax.ppermute(value, 'shard', core_perm)  18.1 us
    all_to_all x3, starting transfers between devices, ctx_exchange(): return lax.all_to_all(value, 'ctx', 0, 0)  12.9 us
  transfers between devices with their start and end apart: 33, of which 25 were waited for; matrix products, arithmetic and copies ran while one was open for 5% of the time, Pallas kernels for 14%

profile of v9, /device:TPU:1, one launch (start us, length us, event | category | flops | bytes accessed | tf_op | source)
XLA Modules:
  0.0 380.6 jit_solution(8922097815544658062)
XLA Ops:
  14.0 1.4 shard_map.263
  17.0 4.7 %collective-permute-start.6 = (bf16[128,2304]{1,0:T(8,128)(2,1)S(1)}, bf16[128,2304]{1,0:T(8,128)(2,1)S(1)}, u32[]{:S(2)}, u32[]{:S(2)}) collective-permute-start(bf16[128,2304]{1,0:T(8,128)(2,1)S(1)} %pad_maximum_fusion.1), channel_id=1, source_target_pairs={{8,1},{1,8},{24,17},{17,24},{40,33},{33,40},{56,49},{49,56},{72,65... | collective-permute-start | bytes 1769480 | tf_op jit(solution)/shard_map/ppermute | solution.py:849
  21.7 7.5 %collective-permute-done.6 = bf16[128,2304]{1,0:T(8,128)(2,1)S(1)} collective-permute-done((bf16[128,2304]{1,0:T(8,128)(2,1)S(1)}, bf16[128,2304]{1,0:T(8,128)(2,1)S(1)}, u32[]{:S(2)}, u32[]{:S(2)}) %collective-permute-start.6) | collective-permute-done | bytes 589856 | tf_op jit(solution)/shard_map/ppermute | solution.py:849
  30.5 1.9 collective-permute-done
  33.3 1.6 broadcast_in_dim.61
  34.9 5.2 %all-to-all-start = ((bf16[4,128,2048]{2,1,0:T(8,128)(2,1)}), bf16[4,128,2048]{2,1,0:T(8,128)(2,1)S(1)}, u32[]{:S(2)}, u32[]{:S(2)}) async-start(bf16[4,128,2048]{2,1,0:T(8,128)(2,1)} %broadcast_in_dim.61), calls=%async_computation | async-start | bytes 4194304 | tf_op jit(solution)/shard_map/all_to_all | solution.py:798
  40.7 25.4 %all-to-all-done.refs_0_.refs_2_.refs_1_ = bf16[4,128,2048]{2,1,0:T(8,128)(2,1)S(1)} async-done(((bf16[4,128,2048]{2,1,0:T(8,128)(2,1)}), bf16[4,128,2048]{2,1,0:T(8,128)(2,1)S(1)}, u32[]{:S(2)}, u32[]{:S(2)}) %all-to-all-start) | async-done | bytes 2097184 | tf_op jit(solution)/shard_map/all_to_all | solution.py:798
  69.8 1.5 collective-permute-done.1.refs_1_.refs_3_.refs_2_
  71.3 1.4 all-gather.3.cloned.1.call-done
  72.7 2.5 shard_map.264
  76.1 4.1 %collective-permute-done.3.other = bf16[8,128,1152]{2,1,0:T(8,128)(2,1)} collective-permute-done((bf16[8,128,1152]{2,1,0:T(8,128)(2,1)S(1)}, bf16[8,128,1152]{2,1,0:T(8,128)(2,1)}, u32[]{:S(2)}, u32[]{:S(2)}) %collective-permute-start.3) | collective-permute-done | bytes 2359328 | tf_op jit(solution)/shard_map/ppermute | solution.py:795
  80.2 5.0 %shard_map.265 = bf16[8,2,128,1152]{3,2,1,0:T(8,128)(2,1)} custom-call(s32[1]{0:T(128)} %bitcast.18.core, bf16[8,2,128,1152]{3,2,1,0:T(8,128)(2,1)} %bitcast.104, bf16[8,128,1152]{2,1,0:T(8,128)(2,1)} %collective-permute-done.3.other), custom_call_target="tpu_custom_call" | custom-call | flops 1048576 | bytes 8388608 | tf_op jit(solution)/shard_map/pallas_call | solution.py:648
  85.3 5.8 %shard_map.266 = (bf16[512,2048]{1,0:T(8,128)(2,1)S(1)}, f32[512,384]{1,0:T(8,128)S(1)}, bf16[512,512]{1,0:T(8,128)(2,1)S(1)}, f32[512,256]{1,0:T(8,128)S(1)}, f32[16,128]{1,0:T(8,128)S(1)}) custom-call(bf16[4,128,2048]{2,1,0:T(8,128)(2,1)} %copy-done.56, bf16[4,128,2048]{2,1,0:T(8,128)(2,1)} %collective-permute-done.1.refs_1_.refs_3_.refs_2_, ...), custom_call_target="tpu_custom_call" | custom-call | flops 1610612736 | bytes 8388608 | tf_op jit(solution)/shard_map/pallas_call | solution.py:97
  91.1 1.3 copy-done.22
  92.5 6.4 %shard_map.268 = (f32[2,512,512]{2,1,0:T(8,128)}, f32[512,256]{1,0:T(8,128)S(1)}, bf16[512,256]{1,0:T(8,128)(2,1)S(1)}, bf16[256,2048]{1,0:T(8,128)(2,1)S(1)}, bf16[256,2048]{1,0:T(8,128)(2,1)S(1)}) custom-call(bf16[512,512]{1,0:T(8,128)(2,1)S(1)} %get-tuple-element.74.refs_0_.refs_1_, f32[512,256]{1,0:T(8,128)S(1)} %get-tuple-element.75.refs_1_.refs_3_, ...), custom_call_target="tpu_custom_call" | custom-call | flops 805306368 | bytes 8388608 | tf_op jit(solution)/shard_map/pallas_call | solution.py:97
  99.4 2.3 collective-permute-done.4
  101.7 1.4 add_convert_fusion.3
  103.1 4.2 %all-to-all-start.1 = ((bf16[4,64,2048]{2,1,0:T(8,128)(2,1)}), bf16[4,64,2048]{2,1,0:T(8,128)(2,1)S(1)}, u32[]{:S(2)}, u32[]{:S(2)}) async-start(bf16[4,64,2048]{2,1,0:T(8,128)(2,1)} %bitcast.21), calls=%async_computation.1 | async-start | bytes 2097152 | tf_op jit(solution)/shard_map/all_to_all | solution.py:798
  108.1 1.6 copy-done.23
  111.0 10.8 %all-to-all-done.1.refs_0_ = bf16[4,64,2048]{2,1,0:T(8,128)(2,1)S(1)} async-done(((bf16[4,64,2048]{2,1,0:T(8,128)(2,1)}), bf16[4,64,2048]{2,1,0:T(8,128)(2,1)S(1)}, u32[]{:S(2)}, u32[]{:S(2)}) %all-to-all-start.1) | async-done | bytes 1048608 | tf_op jit(solution)/shard_map/all_to_all | solution.py:798
  123.9 15.9 %all_to_all.35 = bf16[4,64,2048]{2,1,0:T(8,128)(2,1)S(1)} all-to-all(bf16[4,64,2048]{2,1,0:T(8,128)(2,1)S(1)} %get-tuple-element.80), channel_id=1, replica_groups=mesh['shard'=16,'ctx'=4,'tp'=2] {'ctx'}, dimensions={0} | all-to-all | bytes 2097152 | tf_op jit(solution)/shard_map/all_to_all | solution.py:798
  139.7 2.6 collective-permute-start.5
  142.3 2.3 collective-permute-done.5
  146.0 1.3 copy-done.2
  148.3 2.5 all-gather.5.cloned.1.call-done.refs_4_.refs_5_.refs_6_.refs_2_.refs_3_.refs_1_
  152.0 8.6 %shard_map.271 = (bf16[512,768]{1,0:T(8,128)(2,1)S(1)}, bf16[512,768]{1,0:T(8,128)(2,1)S(1)}, bf16[512,768]{1,0:T(8,128)(2,1)S(1)}) custom-call(bf16[256,2048]{1,0:T(8,128)(2,1)S(1)} %bitcast.87, bf16[256,2048]{1,0:T(8,128)(2,1)S(1)} %bitcast.93, bf16[4,128,2048]{2,1,0:T(8,128)(2,1)} %copy-done.56, ...), custom_call_target="tpu_custom_call" | custom-call | flops 4831838208 | bytes 8388608 | tf_op jit(solution)/shard_map/pallas_call | solution.py:97
  160.6 8.4 %shard_map.272.refs_4_ = bf16[2048,2304]{1,0:T(8,128)(2,1)} custom-call(bf16[2048,512]{1,0:T(8,128)(2,1)S(1)} %copy-done.3, bf16[4,128,2048]{2,1,0:T(8,128)(2,1)} %copy-done.56, bf16[4,128,2048]{2,1,0:T(8,128)(2,1)} %collective-permute-done.1.refs_1_.refs_3_.refs_2_, bf16[512,768]{1,0:T(8,128)(2,1)S(1)} %get-tuple-element.81.refs_3_.refs_0_, ...), custom_call_target="tpu_custom_call" | custom-call | flops 4831838208 | bytes 8388608 | tf_op jit(solution)/shard_map/pallas_call | solution.py:97
  173.9 6.0 %shard_map.273 = (bf16[256,2048]{1,0:T(8,128)(2,1)S(1)}, bf16[256,2048]{1,0:T(8,128)(2,1)S(1)}) custom-call(bf16[512,768]{1,0:T(8,128)(2,1)S(1)} %copy-done.11, bf16[512,768]{1,0:T(8,128)(2,1)S(1)} %copy-done.13, bf16[2048,2304]{1,0:T(8,128)(2,1)} %all-gather.5.cloned.1.call-done.refs_4_.refs_5_.refs_6_.refs_2_.refs_3_.refs_1_, ...), custom_call_target="tpu_custom_call" | custom-call | flops 3221225472 | bytes 8388608 | tf_op jit(solution)/shard_map/pallas_call | solution.py:97
  180.6 2.3 collective-permute-done.7
  183.3 18.2 %all_to_all.36.refs_0_ = bf16[4,64,2048]{2,1,0:T(8,128)(2,1)S(1)} all-to-all(bf16[4,64,2048]{2,1,0:T(8,128)(2,1)S(1)} %bitcast.88), channel_id=1, replica_groups=mesh['shard'=16,'ctx'=4,'tp'=2] {'ctx'}, dimensions={0} | all-to-all | bytes 2097152 | tf_op jit(solution)/shard_map/all_to_all | solution.py:798
  204.8 3.5 all-to-all-start.4
  210.7 4.2 %shard_map.275 = (bf16[256,2048]{1,0:T(8,128)(2,1)S(1)}, bf16[256,2048]{1,0:T(8,128)(2,1)S(1)}) custom-call(bf16[512,768]{1,0:T(8,128)(2,1)S(1)} %copy-done.9, bf16[2048,2304]{1,0:T(8,128)(2,1)} %all-gather.5.cloned.1.call-done.refs_4_.refs_5_.refs_6_.refs_2_.refs_3_.refs_1_, bf16[4,64,2048]{2,1,0:T(8,128)(2,1)S(1)} %bitcast.89), custom_call_target="tpu_custom_call" | custom-call | flops 1610612736 | bytes 8388608 | tf_op jit(solution)/shard_map/pallas_call | solution.py:97
  216.8 4.8 %all-to-all-done.4 = bf16[4,64,2048]{2,1,0:T(8,128)(2,1)S(1)} async-done(((bf16[4,64,2048]{2,1,0:T(8,128)(2,1)}), bf16[4,64,2048]{2,1,0:T(8,128)(2,1)S(1)}, u32[]{:S(2)}, u32[]{:S(2)}) %all-to-all-start.4) | async-done | bytes 1048608 | tf_op jit(solution)/shard_map/all_to_all | solution.py:798
  221.6 2.7 collective-permute-start.8
  224.3 3.8 collective-permute-done.8
  230.2 2.1 shard_map.276
  232.5 3.1 shard_map.277
  235.7 4.4 %shard_map.278.refs_3_ = bf16[2048,1024]{1,0:T(8,128)(2,1)} custom-call(bf16[2048,512]{1,0:T(8,128)(2,1)S(1)} %shard_map.267.refs_2_.refs_0_, bf16[256,2048]{1,0:T(8,128)(2,1)S(1)} %bitcast.85, bf16[256,2048]{1,0:T(8,128)(2,1)S(1)} %bitcast.91, bf16[512,512]{1,0:T(8,128)(2,1)S(1)} %get-tuple-element.96.refs_3_.refs_0_, ...), custom_call_target="tpu_custom_call" | custom-call | flops 2147483648 | bytes 8388608 | tf_op jit(solution)/shard_map/pallas_call | solution.py:97
  240.1 4.2 %shard_map.279 = (bf16[256,2048]{1,0:T(8,128)(2,1)S(1)}, bf16[256,2048]{1,0:T(8,128)(2,1)S(1)}) custom-call(bf16[512,512]{1,0:T(8,128)(2,1)S(1)} %get-tuple-element.96.refs_3_.refs_0_, bf16[512,256]{1,0:T(8,128)(2,1)S(1)} %get-tuple-element.97.refs_4_.refs_1_, bf16[2048,1152]{1,0:T(8,128)(2,1)} %bitcast.101, bf16[2048,1024]{1,0:T(8,128)(2,1)} %shard_map.278.refs_3_), custom_call_target="tpu_custom_call" | custom-call | flops 1610612736 | bytes 8388608 | tf_op jit(solution)/shard_map/pallas_call | solution.py:97
  245.9 5.4 %all-to-all-start.5 = ((bf16[128,8,128]{2,1,0:T(8,128)(2,1)}), bf16[128,8,128]{2,1,0:T(8,128)(2,1)S(1)}, u32[]{:S(2)}, u32[]{:S(2)}) async-start(bf16[128,8,128]{2,1,0:T(8,128)(2,1)} %broadcast_in_dim.66), calls=%async_computation.6 | async-start | bytes 524288 | tf_op jit(solution)/shard_map/all_to_all | solution.py:930
  251.3 2.6 add_convert_fusion.1
  253.9 6.0 %reduce-scatter.2.cloned.1.call-done = bf16[128,2304]{1,0:T(8,128)(2,1)} async-done(((bf16[2048,2304]{1,0:T(8,128)(2,1)}), bf16[128,2304]{1,0:T(8,128)(2,1)}) %reduce-scatter.2.cloned.1.call-update) | async-done | bytes 589840 | tf_op jit(solution)/shard_map/reduce_scatter | solution.py:817
  260.0 4.2 %collective-permute-start.11 = (bf16[128,2304]{1,0:T(8,128)(2,1)}, bf16[128,2304]{1,0:T(8,128)(2,1)}, u32[]{:S(2)}, u32[]{:S(2)}) collective-permute-start(bf16[128,2304]{1,0:T(8,128)(2,1)} %reduce-scatter.2.cloned.1.call-done), channel_id=1, source_target_pairs={{8,1},{1,8},{24,17},{17,24},{40,33},{33,40},{56,49},{49,56},{72,65... | collective-permute-start | bytes 1769480 | tf_op jit(solution)/shard_map/ppermute | solution.py:849
  264.3 1.6 add_convert_fusion
  266.0 5.8 %collective-permute-done.11 = bf16[128,2304]{1,0:T(8,128)(2,1)} collective-permute-done((bf16[128,2304]{1,0:T(8,128)(2,1)}, bf16[128,2304]{1,0:T(8,128)(2,1)}, u32[]{:S(2)}, u32[]{:S(2)}) %collective-permute-start.11) | collective-permute-done | bytes 589856 | tf_op jit(solution)/shard_map/ppermute | solution.py:849
  273.0 5.0 %all-to-all-start.6 = ((bf16[16,128,1024]{2,1,0:T(8,128)(2,1)}), bf16[16,128,1024]{2,1,0:T(8,128)(2,1)}, u32[]{:S(2)}, u32[]{:S(2)}) async-start(bf16[16,128,1024]{2,1,0:T(8,128)(2,1)} %bitcast.102), calls=%async_computation.7 | async-start | bytes 8388608 | tf_op jit(solution)/shard_map/all_to_all | solution.py:822
  279.7 2.4 collective-permute-start.13
  284.4 7.9 %collective-permute-done.12.refs_1_ = bf16[128,2048]{1,0:T(8,128)(2,1)S(1)} collective-permute-done((bf16[128,2048]{1,0:T(8,128)(2,1)S(1)}, bf16[128,2048]{1,0:T(8,128)(2,1)S(1)}, u32[]{:S(2)}, u32[]{:S(2)}) %collective-permute-start.12) | collective-permute-done | bytes 524320 | tf_op jit(solution)/shard_map/ppermute | solution.py:801
  293.5 11.0 %collective-permute-done.13.refs_2_ = bf16[128,2048]{1,0:T(8,128)(2,1)S(1)} collective-permute-done((bf16[128,2048]{1,0:T(8,128)(2,1)S(1)}, bf16[128,2048]{1,0:T(8,128)(2,1)S(1)}, u32[]{:S(2)}, u32[]{:S(2)}) %collective-permute-start.13) | collective-permute-done | bytes 524320 | tf_op jit(solution)/shard_map/ppermute | solution.py:801
  306.1 2.3 collective-permute-start.15
  308.6 7.5 %collective-permute-done.16.b1 = bf16[128,2304]{1,0:T(8,128)(2,1)S(1)} collective-permute-done((bf16[128,2304]{1,0:T(8,128)(2,1)S(1)}, bf16[128,2304]{1,0:T(8,128)(2,1)S(1)}, u32[]{:S(2)}, u32[]{:S(2)}) %collective-permute-start.16) | collective-permute-done | bytes 589856 | tf_op jit(solution)/shard_map/ppermute | solution.py:801
  316.1 13.7 %collective-permute-done.17.b2 = bf16[128,2304]{1,0:T(8,128)(2,1)} collective-permute-done((bf16[128,2304]{1,0:T(8,128)(2,1)S(1)}, bf16[128,2304]{1,0:T(8,128)(2,1)}, u32[]{:S(2)}, u32[]{:S(2)}) %collective-permute-start.17) | collective-permute-done | bytes 589856 | tf_op jit(solution)/shard_map/ppermute | solution.py:801
  329.8 4.3 %shard_map.281 = (f32[128,3072]{1,0:T(8,128)}, f32[128,3072]{1,0:T(8,128)}, f32[3072,128]{1,0:T(8,128)}, f32[128,128]{1,0:T(8,128)S(1)}) custom-call(s32[1]{0:T(128)} %bitcast.turn_at, bf16[128,2304]{1,0:T(8,128)(2,1)S(1)} %broadcast_select_fusion.1.b0, bf16[128,2304]{1,0:T(8,128)(2,1)S(1)} %collective-permute-done.16.b1, ...), custom_call_target="tpu_custom_call" | custom-call | flops 1048576 | bytes 8388608 | tf_op jit(solution)/shard_map/pallas_call | solution.py:726
  335.6 3.6 all-to-all-done.6.refs_0_
  339.2 2.8 shard_map.282
  342.0 1.9 collective-permute-start.20
  345.2 5.9 %collective-permute-done.20 = bf16[128,1024]{1,0:T(8,128)(2,1)S(1)} collective-permute-done((bf16[128,1024]{1,0:T(8,128)(2,1)S(1)}, bf16[128,1024]{1,0:T(8,128)(2,1)S(1)}, u32[]{:S(2)}, u32[]{:S(2)}) %collective-permute-start.20) | collective-permute-done | bytes 262176 | tf_op jit(solution)/shard_map/ppermute | solution.py:849
  352.4 2.4 collective-permute-start.22
  356.2 3.7 collective-permute-done.21.b1
  359.9 5.4 %collective-permute-done.22.b2 = bf16[128,1024]{1,0:T(8,128)(2,1)S(1)} collective-permute-done((bf16[128,1024]{1,0:T(8,128)(2,1)S(1)}, bf16[128,1024]{1,0:T(8,128)(2,1)S(1)}, u32[]{:S(2)}, u32[]{:S(2)}) %collective-permute-start.22) | collective-permute-done | bytes 262176 | tf_op jit(solution)/shard_map/ppermute | solution.py:801
  365.3 2.4 shard_map.283
  368.5 2.1 collective-permute-done.24
  371.1 1.4 broadcast_select_fusion
  372.6 1.6 fusion
  (228 shorter events, 56.1 us)
Async XLA Ops:
  7.2 8.3 %copy-start = (bf16[3072,128]{1,0:T(8,128)(2,1)S(1)}, bf16[3072,128]{1,0:T(8,128)(2,1)}, u32[]{:S(2)}) copy-start(bf16[3072,128]{1,0:T(8,128)(2,1)} %param.30) | copy-start | bytes 2359300
  7.2 9.6 %copy-start.65 = (bf16[128]{0:T(256)(128)(2,1)S(1)}, bf16[128]{0:T(256)(128)(2,1)}, u32[]{:S(2)}) copy-start(bf16[128]{0:T(256)(128)(2,1)} %param.27) | copy-start | bytes 772
  7.2 65.5 %all-gather.3.cloned.1.call-start = ((), (), s32[]{:S(2)}) async-start(), calls=%async_computation.8 | async-start | bytes 5013504 | tf_op jit(solution)/shard_map/all_gather | solution.py:814
  15.4 135.4 %all-gather.5.cloned.1.call-start = ((), (), s32[]{:S(2)}) async-start(), calls=%async_computation.9 | async-start | bytes 10027008 | tf_op jit(solution)/shard_map/all_gather | solution.py:814
  16.8 13.5 %copy-start.61 = (bf16[128,2048]{1,0:T(8,128)(2,1)S(1)}, bf16[128,2048]{1,0:T(8,128)(2,1)}, u32[]{:S(2)}) copy-start(bf16[128,2048]{1,0:T(8,128)(2,1)} %param.31) | copy-start | bytes 1572868
  16.8 13.5 %copy-start.62 = (bf16[128,2048]{1,0:T(8,128)(2,1)S(1)}, bf16[128,2048]{1,0:T(8,128)(2,1)}, u32[]{:S(2)}) copy-start(bf16[128,2048]{1,0:T(8,128)(2,1)} %param.16) | copy-start | bytes 1572868
  17.0 12.3 %collective-permute-start.6 = (bf16[128,2304]{1,0:T(8,128)(2,1)S(1)}, bf16[128,2304]{1,0:T(8,128)(2,1)S(1)}, u32[]{:S(2)}, u32[]{:S(2)}) collective-permute-start(bf16[128,2304]{1,0:T(8,128)(2,1)S(1)} %pad_maximum_fusion.1), channel_id=1, source_target_pairs={{8,1},{1,8},{24,17},{17,24},{40,33},{33,40},{56,49},{49,56},{72,65... | collective-permute-start | bytes 1769480 | tf_op jit(solution)/shard_map/ppermute | solution.py:849
  30.4 2.0 collective-permute-start
  34.9 5.2 %copy-start.63 = (s32[1,13]{1,0:T(1,128)S(1)}, s32[1,13]{1,0:T(1,128)}, u32[]{:S(2)}) copy-start(s32[1,13]{1,0:T(1,128)} %param.18) | copy-start | bytes 160
  34.9 5.2 %copy-start.64 = (s32[1,13]{1,0:T(1,128)S(1)}, s32[1,13]{1,0:T(1,128)}, u32[]{:S(2)}) copy-start(s32[1,13]{1,0:T(1,128)} %param.17) | copy-start | bytes 160
  34.9 31.2 %all-to-all-start = ((bf16[4,128,2048]{2,1,0:T(8,128)(2,1)}), bf16[4,128,2048]{2,1,0:T(8,128)(2,1)S(1)}, u32[]{:S(2)}, u32[]{:S(2)}) async-start(bf16[4,128,2048]{2,1,0:T(8,128)(2,1)} %broadcast_in_dim.61), calls=%async_computation | async-start | bytes 4194304 | tf_op jit(solution)/shard_map/all_to_all | solution.py:798
  40.1 27.6 %collective-permute-start.2 = (s32[2,13]{1,0:T(2,128)S(1)}, s32[2,13]{1,0:T(2,128)S(1)}, u32[]{:S(2)}, u32[]{:S(2)}) collective-permute-start(s32[2,13]{1,0:T(2,128)S(1)} %pad_add_fusion.2), channel_id=1, source_target_pairs={{0,8},{8,0},{16,24},{24,16},{32,40},{40,32},{48,56},{56,48},{64,72... | collective-permute-start | bytes 320 | tf_op jit(solution)/shard_map/ppermute | solution.py:795
  66.1 6.6 %copy-start.56 = (bf16[4,128,2048]{2,1,0:T(8,128)(2,1)}, bf16[4,128,2048]{2,1,0:T(8,128)(2,1)S(1)}, u32[]{:S(2)}) copy-start(bf16[4,128,2048]{2,1,0:T(8,128)(2,1)S(1)} %all-to-all-done.refs_0_.refs_2_.refs_1_) | copy-start | bytes 6291460
  66.1 5.2 %collective-permute-start.1 = (bf16[4,128,2048]{2,1,0:T(8,128)(2,1)S(1)}, bf16[4,128,2048]{2,1,0:T(8,128)(2,1)}, u32[]{:S(2)}, u32[]{:S(2)}) collective-permute-start(bf16[4,128,2048]{2,1,0:T(8,128)(2,1)S(1)} %all-to-all-done.refs_0_.refs_2_.refs_1_), channel_id=1, source_target_pairs={{0,8},{8,0},{16,24},{24,16},{32,40},{40,32},{48,56},{56,48},{64,72... | collective-permute-start | bytes 6291464 | tf_op jit(solution)/shard_map/ppermute | solution.py:795
  69.8 15.5 %copy-start.14 = (f32[512,128]{1,0:T(8,128)}, f32[512,128]{1,0:T(8,128)S(1)}, u32[]{:S(2)}) copy-start(f32[512,128]{1,0:T(8,128)S(1)} %get-tuple-element.71.refs_4_.refs_5_) | copy-start | bytes 786436
  75.2 5.0 %collective-permute-start.3 = (bf16[8,128,1152]{2,1,0:T(8,128)(2,1)S(1)}, bf16[8,128,1152]{2,1,0:T(8,128)(2,1)}, u32[]{:S(2)}, u32[]{:S(2)}) collective-permute-start(bf16[8,128,1152]{2,1,0:T(8,128)(2,1)S(1)} %shard_map.264), channel_id=1, source_target_pairs={{0,8},{8,0},{16,24},{24,16},{32,40},{40,32},{48,56},{56,48},{64,72... | collective-permute-start | bytes 7077896 | tf_op jit(solution)/shard_map/ppermute | solution.py:795
  92.4 6.4 %copy-start.24 = (bf16[512,512]{1,0:T(8,128)(2,1)}, bf16[512,512]{1,0:T(8,128)(2,1)S(1)}, u32[]{:S(2)}) copy-start(bf16[512,512]{1,0:T(8,128)(2,1)S(1)} %get-tuple-element.74.refs_0_.refs_1_) | copy-start | bytes 1572868
  92.4 6.4 %copy-start.26 = (f32[512,256]{1,0:T(8,128)}, f32[512,256]{1,0:T(8,128)S(1)}, u32[]{:S(2)}) copy-start(f32[512,256]{1,0:T(8,128)S(1)} %get-tuple-element.75.refs_1_.refs_3_) | copy-start | bytes 1572868
  92.4 6.4 %copy-start.38 = (f32[512,384]{1,0:T(8,128)}, f32[512,384]{1,0:T(8,128)S(1)}, u32[]{:S(2)}) copy-start(f32[512,384]{1,0:T(8,128)S(1)} %get-tuple-element.94.refs_3_) | copy-start | bytes 2359300
  98.9 4.1 %copy-start.46 = (f32[512,256]{1,0:T(8,128)}, f32[512,256]{1,0:T(8,128)S(1)}, u32[]{:S(2)}) copy-start(f32[512,256]{1,0:T(8,128)S(1)} %get-tuple-element.92.refs_4_) | copy-start | bytes 1572868
  98.9 4.1 %copy-start.48 = (bf16[512,256]{1,0:T(8,128)(2,1)}, bf16[512,256]{1,0:T(8,128)(2,1)S(1)}, u32[]{:S(2)}) copy-start(bf16[512,256]{1,0:T(8,128)(2,1)S(1)} %get-tuple-element.98.refs_5_) | copy-start | bytes 786436
  98.9 2.8 collective-permute-start.4
  101.7 5.6 %copy-start.58 = (bf16[128,2048]{1,0:T(8,128)(2,1)S(1)}, bf16[128,2048]{1,0:T(8,128)(2,1)}, u32[]{:S(2)}) copy-start(bf16[128,2048]{1,0:T(8,128)(2,1)} %copy-done.57) | copy-start | bytes 1572868
  103.1 18.7 %all-to-all-start.1 = ((bf16[4,64,2048]{2,1,0:T(8,128)(2,1)}), bf16[4,64,2048]{2,1,0:T(8,128)(2,1)S(1)}, u32[]{:S(2)}, u32[]{:S(2)}) async-start(bf16[4,64,2048]{2,1,0:T(8,128)(2,1)} %bitcast.21), calls=%async_computation.1 | async-start | bytes 2097152 | tf_op jit(solution)/shard_map/all_to_all | solution.py:798
  107.2 152.7 %reduce-scatter.2.cloned.1.call-start = ((), (), s32[]{:S(2)}) async-start(), calls=%async_computation.10 | async-start | bytes 10027008 | tf_op jit(solution)/shard_map/reduce_scatter | solution.py:817
  139.7 4.9 %collective-permute-start.5 = (bf16[4,64,2048]{2,1,0:T(8,128)(2,1)S(1)}, bf16[4,64,2048]{2,1,0:T(8,128)(2,1)S(1)}, u32[]{:S(2)}, u32[]{:S(2)}) collective-permute-start(bf16[4,64,2048]{2,1,0:T(8,128)(2,1)S(1)} %all_to_all.35), channel_id=1, source_target_pairs={{0,8},{8,0},{16,24},{24,16},{32,40},{40,32},{48,56},{56,48},{64,72... | collective-permute-start | bytes 3145736 | tf_op jit(solution)/shard_map/ppermute | solution.py:795
  152.0 8.6 %copy-start.3 = (bf16[2048,512]{1,0:T(8,128)(2,1)S(1)}, bf16[2048,512]{1,0:T(8,128)(2,1)}, u32[]{:S(2)}) copy-start(bf16[2048,512]{1,0:T(8,128)(2,1)} %copy-done.2) | copy-start | bytes 6291460
  179.9 3.0 collective-permute-start.7
  182.9 19.6 %copy-start.19 = (f32[64,2048]{1,0:T(8,128)S(1)}, f32[64,2048]{1,0:T(8,128)}, u32[]{:S(2)}) copy-start(f32[64,2048]{1,0:T(8,128)} %copy-done.18) | copy-start | bytes 1572868
  182.9 19.6 %copy-start.33 = (bf16[64,2048]{1,0:T(8,128)(2,1)S(1)}, bf16[64,2048]{1,0:T(8,128)(2,1)}, u32[]{:S(2)}) copy-start(bf16[64,2048]{1,0:T(8,128)(2,1)} %get-tuple-element.140.refs_2_) | copy-start | bytes 786436
  204.8 16.9 %all-to-all-start.4 = ((bf16[4,64,2048]{2,1,0:T(8,128)(2,1)}), bf16[4,64,2048]{2,1,0:T(8,128)(2,1)S(1)}, u32[]{:S(2)}, u32[]{:S(2)}) async-start(bf16[4,64,2048]{2,1,0:T(8,128)(2,1)} %copy-done.32), calls=%async_computation.4 | async-start | bytes 2097152 | tf_op jit(solution)/shard_map/all_to_all | solution.py:798
  221.6 6.4 %collective-permute-start.8 = (bf16[4,64,2048]{2,1,0:T(8,128)(2,1)S(1)}, bf16[4,64,2048]{2,1,0:T(8,128)(2,1)S(1)}, u32[]{:S(2)}, u32[]{:S(2)}) collective-permute-start(bf16[4,64,2048]{2,1,0:T(8,128)(2,1)S(1)} %all-to-all-done.4), channel_id=1, source_target_pairs={{0,8},{8,0},{16,24},{24,16},{32,40},{40,32},{48,56},{56,48},{64,72... | collective-permute-start | bytes 3145736 | tf_op jit(solution)/shard_map/ppermute | solution.py:795
  224.3 27.0 %collective-permute-start.9 = (bf16[256,2048]{1,0:T(8,128)(2,1)}, bf16[256,2048]{1,0:T(8,128)(2,1)}, u32[]{:S(2)}, u32[]{:S(2)}) collective-permute-start(bf16[256,2048]{1,0:T(8,128)(2,1)} %copy-done.55), channel_id=1, source_target_pairs={{0,8},{8,0},{16,24},{24,16},{32,40},{40,32},{48,56},{56,48},{64,72... | collective-permute-start | bytes 3145736 | tf_op jit(solution)/shard_map/ppermute | solution.py:795
  232.5 3.2 copy-start.49
  240.1 11.2 %copy-start.31 = (bf16[256,2048]{1,0:T(8,128)(2,1)S(1)}, bf16[256,2048]{1,0:T(8,128)(2,1)}, u32[]{:S(2)}) copy-start(bf16[256,2048]{1,0:T(8,128)(2,1)} %copy-done.30) | copy-start | bytes 3145732
  244.3 20.0 %collective-permute-start.10 = (bf16[256,2048]{1,0:T(8,128)(2,1)S(1)}, bf16[256,2048]{1,0:T(8,128)(2,1)}, u32[]{:S(2)}, u32[]{:S(2)}) collective-permute-start(bf16[256,2048]{1,0:T(8,128)(2,1)S(1)} %get-tuple-element.102), channel_id=1, source_target_pairs={{0,8},{8,0},{16,24},{24,16},{32,40},{40,32},{48,56},{56,48},{64,72... | collective-permute-start | bytes 3145736 | tf_op jit(solution)/shard_map/ppermute | solution.py:795
  245.9 18.3 %all-to-all-start.5 = ((bf16[128,8,128]{2,1,0:T(8,128)(2,1)}), bf16[128,8,128]{2,1,0:T(8,128)(2,1)S(1)}, u32[]{:S(2)}, u32[]{:S(2)}) async-start(bf16[128,8,128]{2,1,0:T(8,128)(2,1)} %broadcast_in_dim.66), calls=%async_computation.6 | async-start | bytes 524288 | tf_op jit(solution)/shard_map/all_to_all | solution.py:930
  260.0 11.9 %collective-permute-start.11 = (bf16[128,2304]{1,0:T(8,128)(2,1)}, bf16[128,2304]{1,0:T(8,128)(2,1)}, u32[]{:S(2)}, u32[]{:S(2)}) collective-permute-start(bf16[128,2304]{1,0:T(8,128)(2,1)} %reduce-scatter.2.cloned.1.call-done), channel_id=1, source_target_pairs={{8,1},{1,8},{24,17},{17,24},{40,33},{33,40},{56,49},{49,56},{72,65... | collective-permute-start | bytes 1769480 | tf_op jit(solution)/shard_map/ppermute | solution.py:849
  264.2 7.6 %copy-start.60 = (bf16[128,2304]{1,0:T(8,128)(2,1)S(1)}, bf16[128,2304]{1,0:T(8,128)(2,1)}, u32[]{:S(2)}) copy-start(bf16[128,2304]{1,0:T(8,128)(2,1)} %reduce-scatter.2.cloned.1.call-done) | copy-start | bytes 1769476
  273.0 5.0 %copy-start.59 = (bf16[256,2048]{1,0:T(8,128)(2,1)S(1)}, bf16[256,2048]{1,0:T(8,128)(2,1)}, u32[]{:S(2)}) copy-start(bf16[256,2048]{1,0:T(8,128)(2,1)} %add_convert_fusion.1) | copy-start | bytes 3145732
  273.0 66.2 %all-to-all-start.6 = ((bf16[16,128,1024]{2,1,0:T(8,128)(2,1)}), bf16[16,128,1024]{2,1,0:T(8,128)(2,1)}, u32[]{:S(2)}, u32[]{:S(2)}) async-start(bf16[16,128,1024]{2,1,0:T(8,128)(2,1)} %bitcast.102), calls=%async_computation.7 | async-start | bytes 8388608 | tf_op jit(solution)/shard_map/all_to_all | solution.py:822
  278.2 27.3 %copy-start.17 = (bf16[64,2048]{1,0:T(8,128)(2,1)S(1)}, bf16[64,2048]{1,0:T(8,128)(2,1)}, u32[]{:S(2)}) copy-start(bf16[64,2048]{1,0:T(8,128)(2,1)} %get-tuple-element.141.refs_1_.refs_6_) | copy-start | bytes 786436
  278.2 27.2 %copy-start.20 = (f32[64,2048]{1,0:T(8,128)S(1)}, f32[64,2048]{1,0:T(8,128)}, u32[]{:S(2)}) copy-start(f32[64,2048]{1,0:T(8,128)} %copy-done.18) | copy-start | bytes 1572868
  278.2 27.2 %copy-start.41 = (f32[64,2048]{1,0:T(8,128)S(1)}, f32[64,2048]{1,0:T(8,128)}, u32[]{:S(2)}) copy-start(f32[64,2048]{1,0:T(8,128)} %copy-done.40) | copy-start | bytes 1572868
  278.4 13.9 %collective-permute-start.12 = (bf16[128,2048]{1,0:T(8,128)(2,1)S(1)}, bf16[128,2048]{1,0:T(8,128)(2,1)S(1)}, u32[]{:S(2)}, u32[]{:S(2)}) collective-permute-start(bf16[128,2048]{1,0:T(8,128)(2,1)S(1)} %get-tuple-element.132), channel_id=1, source_target_pairs={{0,2},{2,4},{4,6},{6,0},{1,3},{3,5},{5,7},{7,1},{8,10},{10,12},{12... | collective-permute-start | bytes 1572872 | tf_op jit(solution)/shard_map/ppermute | solution.py:801
  279.7 24.8 %collective-permute-start.13 = (bf16[128,2048]{1,0:T(8,128)(2,1)S(1)}, bf16[128,2048]{1,0:T(8,128)(2,1)S(1)}, u32[]{:S(2)}, u32[]{:S(2)}) collective-permute-start(bf16[128,2048]{1,0:T(8,128)(2,1)S(1)} %get-tuple-element.131), channel_id=1, source_target_pairs={{0,4},{2,6},{4,0},{6,2},{1,5},{3,7},{5,1},{7,3},{8,12},{10,14},{12... | collective-permute-start | bytes 1572872 | tf_op jit(solution)/shard_map/ppermute | solution.py:801
  282.1 23.3 %collective-permute-start.14 = (bf16[128,2048]{1,0:T(8,128)(2,1)S(1)}, bf16[128,2048]{1,0:T(8,128)(2,1)S(1)}, u32[]{:S(2)}, u32[]{:S(2)}) collective-permute-start(bf16[128,2048]{1,0:T(8,128)(2,1)S(1)} %get-tuple-element.130), channel_id=1, source_target_pairs={{0,6},{2,0},{4,2},{6,4},{1,7},{3,1},{5,3},{7,5},{8,14},{10,8},{12,... | collective-permute-start | bytes 1572872 | tf_op jit(solution)/shard_map/ppermute | solution.py:801
  283.2 32.9 %collective-permute-start.16 = (bf16[128,2304]{1,0:T(8,128)(2,1)S(1)}, bf16[128,2304]{1,0:T(8,128)(2,1)S(1)}, u32[]{:S(2)}, u32[]{:S(2)}) collective-permute-start(bf16[128,2304]{1,0:T(8,128)(2,1)S(1)} %broadcast_select_fusion.1.b0), channel_id=1, source_target_pairs={{0,2},{2,4},{4,6},{6,0},{1,3},{3,5},{5,7},{7,1},{8,10},{10,12},{12... | collective-permute-start | bytes 1769480 | tf_op jit(solution)/shard_map/ppermute | solution.py:801
  283.6 46.2 %collective-permute-start.17 = (bf16[128,2304]{1,0:T(8,128)(2,1)S(1)}, bf16[128,2304]{1,0:T(8,128)(2,1)}, u32[]{:S(2)}, u32[]{:S(2)}) collective-permute-start(bf16[128,2304]{1,0:T(8,128)(2,1)S(1)} %broadcast_select_fusion.1.b0), channel_id=1, source_target_pairs={{0,4},{2,6},{4,0},{6,2},{1,5},{3,7},{5,1},{7,3},{8,12},{10,14},{12... | collective-permute-start | bytes 1769480 | tf_op jit(solution)/shard_map/ppermute | solution.py:801
  292.3 37.5 %collective-permute-start.18 = (bf16[128,2304]{1,0:T(8,128)(2,1)S(1)}, bf16[128,2304]{1,0:T(8,128)(2,1)}, u32[]{:S(2)}, u32[]{:S(2)}) collective-permute-start(bf16[128,2304]{1,0:T(8,128)(2,1)S(1)} %broadcast_select_fusion.1.b0), channel_id=1, source_target_pairs={{0,6},{2,0},{4,2},{6,4},{1,7},{3,1},{5,3},{7,5},{8,14},{10,8},{12,... | collective-permute-start | bytes 1769480 | tf_op jit(solution)/shard_map/ppermute | solution.py:801
  305.4 24.4 %copy-start.28 = (bf16[128,3072]{1,0:T(8,128)(2,1)S(1)}, bf16[128,3072]{1,0:T(8,128)(2,1)}, u32[]{:S(2)}) copy-start(bf16[128,3072]{1,0:T(8,128)(2,1)} %w_up.1) | copy-start | bytes 2359300
  305.4 24.4 %copy-start.29 = (bf16[128,3072]{1,0:T(8,128)(2,1)S(1)}, bf16[128,3072]{1,0:T(8,128)(2,1)}, u32[]{:S(2)}) copy-start(bf16[128,3072]{1,0:T(8,128)(2,1)} %w_gate.1) | copy-start | bytes 2359300
  306.1 28.0 %collective-permute-start.15 = (bf16[128,2048]{1,0:T(8,128)(2,1)S(1)}, bf16[128,2048]{1,0:T(8,128)(2,1)}, u32[]{:S(2)}, u32[]{:S(2)}) collective-permute-start(bf16[128,2048]{1,0:T(8,128)(2,1)S(1)} %shard_map.280), channel_id=1, source_target_pairs={{0,8},{8,0},{16,24},{24,16},{32,40},{40,32},{48,56},{56,48},{64,72... | collective-permute-start | bytes 1572872 | tf_op jit(solution)/shard_map/ppermute | solution.py:795
  339.2 16.8 %copy-start.54 = (bf16[128]{0:T(256)(128)(2,1)S(1)}, bf16[128]{0:T(256)(128)(2,1)}, u32[]{:S(2)}) copy-start(bf16[128]{0:T(256)(128)(2,1)} %param.19) | copy-start | bytes 772
  339.2 26.1 %copy-start.35 = (bf16[128,1024]{1,0:T(8,128)(2,1)S(1)}, bf16[128,1024]{1,0:T(8,128)(2,1)}, u32[]{:S(2)}) copy-start(bf16[128,1024]{1,0:T(8,128)(2,1)} %wq.3) | copy-start | bytes 786436
  339.2 26.1 %copy-start.37 = (bf16[128,1024]{1,0:T(8,128)(2,1)S(1)}, bf16[128,1024]{1,0:T(8,128)(2,1)}, u32[]{:S(2)}) copy-start(bf16[128,1024]{1,0:T(8,128)(2,1)} %wg.3) | copy-start | bytes 786436
  339.2 26.1 %copy-start.43 = (bf16[128,512]{1,0:T(8,128)(2,1)S(1)}, bf16[128,512]{1,0:T(8,128)(2,1)}, u32[]{:S(2)}) copy-start(bf16[128,512]{1,0:T(8,128)(2,1)} %wk.3) | copy-start | bytes 393220
  339.2 26.1 %copy-start.45 = (bf16[128,512]{1,0:T(8,128)(2,1)S(1)}, bf16[128,512]{1,0:T(8,128)(2,1)}, u32[]{:S(2)}) copy-start(bf16[128,512]{1,0:T(8,128)(2,1)} %wv.3) | copy-start | bytes 393220
  342.0 9.1 %collective-permute-start.20 = (bf16[128,1024]{1,0:T(8,128)(2,1)S(1)}, bf16[128,1024]{1,0:T(8,128)(2,1)S(1)}, u32[]{:S(2)}, u32[]{:S(2)}) collective-permute-start(bf16[128,1024]{1,0:T(8,128)(2,1)S(1)} %shard_map.282), channel_id=1, source_target_pairs={{8,1},{1,8},{24,17},{17,24},{40,33},{33,40},{56,49},{49,56},{72,65... | collective-permute-start | bytes 786440 | tf_op jit(solution)/shard_map/ppermute | solution.py:849
  343.9 27.2 %collective-permute-start.19 = (bf16[2,128,2048]{2,1,0:T(8,128)(2,1)S(1)}, bf16[2,128,2048]{2,1,0:T(8,128)(2,1)}, u32[]{:S(2)}, u32[]{:S(2)}) collective-permute-start(bf16[2,128,2048]{2,1,0:T(8,128)(2,1)S(1)} %pad_maximum_fusion.refs_1_), channel_id=1, source_target_pairs={{0,1},{9,8},{16,17},{25,24},{32,33},{41,40},{48,49},{57,56},{64,65... | collective-permute-start | bytes 3145736 | tf_op jit(solution)/shard_map/ppermute | solution.py:980
  351.1 8.7 %collective-permute-start.21 = (bf16[128,1024]{1,0:T(8,128)(2,1)S(1)}, bf16[128,1024]{1,0:T(8,128)(2,1)S(1)}, u32[]{:S(2)}, u32[]{:S(2)}) collective-permute-start(bf16[128,1024]{1,0:T(8,128)(2,1)S(1)} %broadcast_select_fusion.3.b0), channel_id=1, source_target_pairs={{0,2},{2,4},{4,6},{6,0},{1,3},{3,5},{5,7},{7,1},{8,10},{10,12},{12... | collective-permute-start | bytes 786440 | tf_op jit(solution)/shard_map/ppermute | solution.py:801
  352.4 12.9 %collective-permute-start.22 = (bf16[128,1024]{1,0:T(8,128)(2,1)S(1)}, bf16[128,1024]{1,0:T(8,128)(2,1)S(1)}, u32[]{:S(2)}, u32[]{:S(2)}) collective-permute-start(bf16[128,1024]{1,0:T(8,128)(2,1)S(1)} %broadcast_select_fusion.3.b0), channel_id=1, source_target_pairs={{0,4},{2,6},{4,0},{6,2},{1,5},{3,7},{5,1},{7,3},{8,12},{10,14},{12... | collective-permute-start | bytes 786440 | tf_op jit(solution)/shard_map/ppermute | solution.py:801
  354.8 10.5 %collective-permute-start.23 = (bf16[128,1024]{1,0:T(8,128)(2,1)S(1)}, bf16[128,1024]{1,0:T(8,128)(2,1)S(1)}, u32[]{:S(2)}, u32[]{:S(2)}) collective-permute-start(bf16[128,1024]{1,0:T(8,128)(2,1)S(1)} %broadcast_select_fusion.3.b0), channel_id=1, source_target_pairs={{0,6},{2,0},{4,2},{6,4},{1,7},{3,1},{5,3},{7,5},{8,14},{10,8},{12,... | collective-permute-start | bytes 786440 | tf_op jit(solution)/shard_map/ppermute | solution.py:801
  367.9 2.7 collective-permute-start.24
  (35 other events, 41.6 us)
Sparse Core Ops, SparseCore 0:
  15.6 57.1 all-gather.2
  75.5 75.2 all-gather.4
  171.8 88.1 reduce-scatter.1

commit v10 on v8

--- a/solution.py
+++ b/solution.py
@@ -16,6 +16,7 @@
 PLANE = ("shard", "tp")
 SCALE = 1.0 / math.sqrt(HD)
 VMEM = 48 << 20
+ALL_VMEM = 60 << 20
 
 
 def lookup(onehot, table):
@@ -117,25 +118,21 @@
     return value.reshape((-1,) + value.shape[2:])
 
 
-def project_kernel(xa, xb, w, ends, cosine, sine, xn, pre, low, gate, gains):
+def project_kernel(xa, xb, w, gains, cosine, sine, xn, pre, low, gate):
     x = flat(jnp.where(pl.program_id(0) == 0, xa[...], xb[...])).astype(F32)
     normed = (x * rms_scale(x)).astype(BF16)
     xn[...] = normed
     out = dot(normed, w[...])
-    found = jnp.zeros((16, HD), F32)
-    for start in range(0, ends.shape[0], HD):
-        found = found + ends[start : start + 16, :].astype(F32)
-    gains[...] = found
     for place in range(3):
         raw = out[:, head(place)]
         pre[:, head(place)] = raw
-        unit = raw * rms_scale(raw) * found[place // 2 : place // 2 + 1, :]
+        unit = raw * rms_scale(raw) * gains[place // 2 : place // 2 + 1, :]
         low[:, head(place)] = (unit * cosine[...] + turn(unit) * sine[...]).astype(BF16)
     low[:, head(3)] = out[:, head(3)].astype(BF16)
     gate[...] = out[:, 4 * HD :]
 
 
-def project(xa, xb, w, cosine, sine):
+def project(xa, xb, w, gains, cosine, sine):
     half, width = xa.shape[0] * xa.shape[1] // 2, xa.shape[2]
     return call(
         project_kernel,
@@ -144,7 +141,7 @@
             piled(xa.shape, 0),
             piled(xb.shape, 0),
             fixed((width, 6 * HD)),
-            pl.BlockSpec((width, HD), lambda i: (0, 8)),
+            fixed(gains.shape),
             rowed(half, HD),
             rowed(half, HD),
         ],
@@ -153,17 +150,15 @@
             rowed(half, 3 * HD),
             rowed(half, 4 * HD),
             rowed(half, 2 * HD),
-            fixed((16, HD)),
         ],
         [
             struct((2 * half, width), BF16),
             struct((2 * half, 3 * HD), F32),
             struct((2 * half, 4 * HD), BF16),
             struct((2 * half, 2 * HD), F32),
-            struct((16, HD), F32),
         ],
         2 * 2 * half * width * 6 * HD,
-    )(xa, xb, w, w, cosine, sine)
+    )(xa, xb, w, gains, cosine, sine)
 
 
 def attend_kernel(low, gate, w_out, of_row, of_column, probs, attended, gated, mine, other):
@@ -451,7 +446,7 @@
             fixed((length, 4 * HD)),
             rowed(half, 2 * HD),
             fixed((length, 3 * HD)),
-            fixed((16, HD)),
+            fixed((8, HD)),
             fixed((length, HD)),
             fixed((length, HD)),
         ],
@@ -572,12 +567,15 @@
     )(parts, middle, cot)
 
 
-def ends_kernel(parts, middle, d_middle, x, out):
+def ends_kernel(parts, middle, d_middle, x, out, terms):
     rows = x.shape[0]
     total = sum(part[...].astype(F32) for part in parts)
     out[:rows, :] = (middle[...] + total[:rows, :]).astype(BF16)
-    back = norm_back(total[rows:, :], x[...].astype(F32))
-    out[rows:, :] = (d_middle[...] + back).astype(BF16)
+    inputs = x[...].astype(F32)
+    grads = total[rows:, :]
+    out[rows:, :] = (d_middle[...] + norm_back(grads, inputs)).astype(BF16)
+    found = jnp.sum(grads * inputs * rms_scale(inputs), axis=0, keepdims=True)
+    terms[...] = jnp.broadcast_to(found, terms.shape)
 
 
 def ends_step(parts, middle, d_middle, x):
@@ -587,29 +585,13 @@
         lambda *refs: ends_kernel(refs[:count], *refs[count:]),
         (1,),
         [fixed(wide)] * count + [fixed(shape)] * 3,
-        fixed(wide),
-        struct(wide, BF16),
+        [fixed(wide), fixed((8, shape[1]))],
+        [struct(wide, BF16), struct((8, shape[1]), F32)],
         1 << 20,
     )(*parts, middle, d_middle, x)
 
 
-def sum_kernel(parts, out):
-    out[...] = jnp.sum(parts[...].astype(F32), axis=0).astype(BF16)
-
-
-def sum_step(parts, behind):
-    return call(
-        sum_kernel,
-        (1,),
-        [fixed(parts.shape)],
-        fixed(parts.shape[1:]),
-        struct(parts.shape[1:], BF16),
-        1 << 20,
-        behind=behind,
-    )(parts)
-
-
-def prefetched(kernel, grid, in_specs, out_specs, out_shape):
+def prefetched(kernel, grid, in_specs, out_specs, out_shape, vmem=VMEM):
     return pl.pallas_call(
         kernel,
         grid_spec=pltpu.PrefetchScalarGridSpec(
@@ -617,7 +599,7 @@
         ),
         out_shape=out_shape,
         compiler_params=pltpu.CompilerParams(
-            dimension_semantics=("arbitrary",) * len(grid), vmem_limit_bytes=VMEM
+            dimension_semantics=("arbitrary",) * len(grid), vmem_limit_bytes=vmem
         ),
         cost_estimate=pl.CostEstimate(flops=1 << 20, bytes_accessed=8 << 20, transcendentals=0),
     )
@@ -688,28 +670,14 @@
         sums[...] += term
 
 
-def close_attend_kernel(
-    turn_at, b0, b1, b2, b3, wq, wk, wv, wg, gain, gq, gk, gv, gg, go, sums
-):
-    found = pick((b0, b1, b2, b3))
-    inner, outer, scale = found[:, : 4 * HD], found[:, 4 * HD :], gain[...]
-    raw_q, raw_k, raw_v = inner[:, : 2 * HD], inner[:, head(2)], inner[:, head(3)]
-    raw_g = outer[:, : 2 * HD]
-    gq[...], gk[...], gv[...], gg[...] = raw_q * scale, raw_k * scale, raw_v * scale, raw_g * scale
-    go[head(0), :], go[head(1), :] = outer[:, head(2)], outer[:, head(3)]
-    pairs = ((raw_q, wq), (raw_k, wk), (raw_v, wv), (raw_g, wg))
-    term = sum(lanes(raw * w[...].astype(F32)) for raw, w in pairs)
-
-    @pl.when(pl.program_id(0) == 0)
-    def _():
-        sums[...] = term
-
-    @pl.when(pl.program_id(0) > 0)
-    def _():
-        sums[...] += term
-
-
-def close(kernel, turn_at, blocks, weights, gain, out_rows, extra):
+def close_attend_kernel(turn_at, b0, b1, b2, b3, gain, gq, gk, gv, gg, go):
+    found, scale = pick((b0, b1, b2, b3)), gain[...]
+    gq[...], gk[...] = found[:, : 2 * HD] * scale, found[:, head(2)] * scale
+    gv[...], gg[...] = found[:, head(3)] * scale, found[:, 4 * HD : 6 * HD] * scale
+    go[...] = jnp.concatenate([found[:, head(6)], found[:, head(7)]], axis=0)
+
+
+def close(kernel, turn_at, blocks, weights, gain, out_rows, extra, read):
     quarters = 4
     place = lambda i, at: (at[0] + quarters - i) % quarters
     whole = lambda value: pl.BlockSpec(value.shape, lambda i, at: (0, 0))
@@ -717,15 +685,49 @@
         (w.shape[0], w.shape[1] // quarters), lambda i, at: (0, place(i, at))
     )
     rows, width = out_rows
-    in_specs = [whole(b) for b in blocks] + [columns(w) for w in weights] + [whole(gain)]
+    operands = weights if read else ()
+    in_specs = [whole(b) for b in blocks] + [columns(w) for w in operands] + [whole(gain)]
     out_specs = [columns(w) for w in weights]
     out_specs += [pl.BlockSpec((rows // quarters, width), lambda i, at: (place(i, at), 0))]
     out_specs += [pl.BlockSpec(shape, lambda i, at: (0, 0)) for shape in extra]
     out_shape = [struct(w.shape, F32) for w in weights] + [struct(out_rows, F32)]
     out_shape += [struct(shape, F32) for shape in extra]
-    return prefetched(kernel, (quarters,), in_specs, out_specs, out_shape)(
-        turn_at, *blocks, *weights, gain
+    return prefetched(kernel, (quarters,), in_specs, out_specs, out_shape, vmem=ALL_VMEM)(
+        turn_at, *blocks, *operands, gain
     )
+
+
+def column(row):
+    shape = (HD, HD)
+    there = lax.broadcasted_iota(jnp.int32, shape, 0) == lax.broadcasted_iota(jnp.int32, shape, 1)
+    return jnp.sum(jnp.where(there, jnp.broadcast_to(row, shape), 0.0), axis=1, keepdims=True)
+
+
+def first_kernel(at, wq, wk, wv, wg, wo, gain, out):
+    scale = column(gain[...].astype(F32))
+    start = 0
+    for w in (wq, wk, wv, wg):
+        stop = start + w.shape[1]
+        out[:, start:stop] = (w[...].astype(F32) * scale).astype(BF16)
+        start = stop
+    out[:, start:] = wo[...].T
+
+
+def first_columns(at, wq, wk, wv, wg, wo, gain):
+    quarter = lambda w: pl.BlockSpec((w.shape[0], w.shape[1] // 4), lambda i, at: (0, at[0]))
+    rows = wq.shape[0]
+    heads = wo.shape[0] // 4
+    columns = sum(w.shape[1] // 4 for w in (wq, wk, wv, wg)) + heads
+    return prefetched(
+        first_kernel,
+        (1,),
+        [quarter(w) for w in (wq, wk, wv, wg)]
+        + [pl.BlockSpec((heads, rows), lambda i, at: (at[0], 0))]
+        + [pl.BlockSpec(gain.shape, lambda i, at: (0, 0))],
+        pl.BlockSpec((rows, columns), lambda i, at: (0, 0)),
+        struct((rows, columns), BF16),
+        vmem=ALL_VMEM,
+    )(at, wq, wk, wv, wg, wo, gain)
 
 
 def make_shards(mesh):
@@ -790,9 +792,6 @@
         return lax.psum_scatter(
             value, PLANE, scatter_dimension=0, tiled=True, axis_index_groups=planes
         )
-
-    def plane_exchange(value):
-        return lax.all_to_all(value, PLANE, 0, 0, axis_index_groups=planes)
 
     def shards(
         tokens,
@@ -827,18 +826,16 @@
 
         gain_one = gain_in.astype(F32)[:, None]
         gain_two = gain_mid.astype(F32)[:, None]
-        first = jnp.concatenate(
-            [quarter(w, 1) for w in (w_query, w_key, w_value, w_gate_attn)], axis=1
-        )
-        first = (first.astype(F32) * gain_one).astype(BF16)
         head_rows = gain_query.shape[0]
-        ends = lax.dynamic_update_slice(
-            jnp.zeros((gain_in.shape[0], HD), BF16),
-            jnp.stack([gain_query, gain_key]),
-            (0, lax.axis_index("shard") * head_rows),
-        )
-        first = jnp.concatenate([first, quarter(w_out, 0).T, ends], axis=1)
+        first = first_columns(
+            ctx.astype(jnp.int32).reshape(1), w_query, w_key, w_value, w_gate_attn, w_out, gain_in[None]
+        )
         found = plane_gather(first)
+        both_gains = jnp.pad(jnp.stack([gain_query, gain_key]), ((0, 6), (0, HD - head_rows)))
+        both_gains = lax.all_to_all(
+            jnp.broadcast_to(both_gains[None], (n_shard, 8, HD)), "shard", 0, 0
+        )
+        gains = both_gains[:, :, :head_rows].astype(F32).transpose(1, 0, 2).reshape(8, HD)
 
         def half_rows(place):
             pieces = [lax.dynamic_slice_in_dim(v, place * rows, rows, 0) for v in (tokens, cotangent)]
@@ -874,7 +871,7 @@
         other = core_swap(sibling_part(core_at, found))
         w1 = join_cores(core_at, found, other).reshape(-1, first.shape[1])
 
-        xn, pre, low, gate, gains = project(xa, xb, w1, cosine, sine)
+        xn, pre, low, gate = project(xa, xb, w1, gains, cosine, sine)
         probs, attended, gated, mine, other = attend(low, gate, w1, of_row, of_column)
         x_flip = flip(xn)
         middle, spread = middle_step(ctx_exchange(tree_half(mine, other)), own_x, (x_flip,))
@@ -893,23 +890,10 @@
         d_attended, d_gate_pre = gate_back(da, db, w1, gate, attended)
         d_qkv, terms = attend_back(probs, low, d_attended, pre, gains, cosine, sine, ())
 
-        pieces = jnp.concatenate(
-            [terms[0].reshape(n_shard, -1), terms[1].reshape(n_shard, -1)], axis=1
-        )
-        copies = n_ctx * n_tp
-        pieces = jnp.pad(pieces, ((0, 0), (0, HD - pieces.shape[1]))).astype(BF16)
-        pieces = jnp.broadcast_to(pieces[:, None, None], (n_shard, copies, 8, HD))
-        pieces = lax.all_to_all(
-            pieces.reshape(n_shard * copies, 8, HD), ("shard", "ctx", "tp"), 0, 0
-        )
-        head_ends = jnp.sum(pieces.astype(F32), axis=0)
         attn = attend_grads(x_flip, da, db, d_qkv, d_gate_pre, gated, ())
         in_mine, in_other = input_back(d_qkv, d_gate_pre, w1, (attn,))
         layer_half, in_half = tree_half(layer_mine, layer_other), tree_half(in_mine, in_other)
-        attn, layer_half, in_half, grad_ffn, head_ends = lax.optimization_barrier(
-            (attn, layer_half, in_half, grad_ffn, head_ends)
-        )
-        attn_parts = plane_exchange(attn.reshape(n_shard, -1, attn.shape[1]))
+        grad_attn = plane_scatter(attn)
 
         def owners(block):
             block = swapped(block)
@@ -918,6 +902,7 @@
         def owners_at_once(block):
             moved = [lax.ppermute(block, ("shard", "ctx", "tp"), perm) for perm in owner_perms]
             return [jnp.where(native, block, moved[0])] + moved[1:]
+
 
         both = jnp.concatenate(
             [layer_half, in_half], axis=1
@@ -926,7 +911,20 @@
             ctx_turn(lax.dynamic_index_in_dim(both, (ctx + by) % n_ctx, 0, False), by)
             for by in range(1, n_ctx)
         ]
-        ends = ends_step(parts, middle, d_middle, own_x)
+        ends, in_terms = ends_step(parts, middle, d_middle, own_x)
+        pieces = jnp.concatenate(
+            [terms[0].reshape(n_shard, -1), terms[1].reshape(n_shard, -1)], axis=1
+        )
+        pieces = jnp.pad(pieces, ((0, 0), (0, HD - pieces.shape[1])))
+        pieces = jnp.stack([in_terms[0].reshape(n_shard, HD), pieces], axis=1).astype(BF16)
+        copies = n_ctx * n_tp
+        pieces = jnp.broadcast_to(
+            jnp.pad(pieces, ((0, 0), (0, 6), (0, 0)))[:, None], (n_shard, copies, 8, HD)
+        )
+        pieces = lax.all_to_all(
+            pieces.reshape(n_shard * copies, 8, HD), ("shard", "ctx", "tp"), 0, 0
+        )
+        end_sums = jnp.sum(pieces.astype(F32), axis=0)
         ffn_blocks = owners(grad_ffn)
         sibling = core_swap(ends)
 
@@ -939,10 +937,6 @@
             )
 
         full = jnp.stack([whole(0), whole(rows)])
-        attn_sum = sum_step(attn_parts, (full, ffn_blocks[0]))
-        full, attn_sum = lax.optimization_barrier((full, attn_sum))
-        full = jnp.where(native, full, lax.ppermute(full, PLANE, across_perm))
-
         turn_at = ctx.astype(jnp.int32).reshape(1)
         size = gain_in.shape[0]
         grad_gate, grad_up, grad_down, mid_sums = close(
@@ -953,32 +947,36 @@
             gain_two,
             w_down.shape,
             [(size, HD)],
-        )
-        attn_blocks = owners(attn_sum)
-        grad_query, grad_key, grad_value, grad_gate_attn, grad_out, in_sums = close(
+            True,
+        )
+        mid_terms = jnp.sum(mid_sums, axis=1)
+        mid_terms = mid_terms + lax.ppermute(mid_terms, "tp", [(0, 1), (1, 0)])
+        full = jnp.where(native, full, lax.ppermute(full, PLANE, across_perm))
+        full = full.astype(F32)
+        grad_attn, mid_terms, full = lax.optimization_barrier((grad_attn, mid_terms, full))
+        grad_query, grad_key, grad_value, grad_gate_attn, grad_out = close(
             close_attend_kernel,
             turn_at,
-            attn_blocks,
+            owners_at_once(grad_attn),
             (w_query, w_key, w_value, w_gate_attn),
             gain_one,
             w_out.shape,
-            [(size, HD)],
-        )
-        gain_terms = jnp.stack([jnp.sum(in_sums, axis=1), jnp.sum(mid_sums, axis=1)])
-        gain_terms = gain_terms + lax.ppermute(gain_terms, "tp", [(0, 1), (1, 0)])
+            [],
+            False,
+        )
 
         return (
-            full[0].astype(F32),
-            full[1].astype(F32),
-            gain_terms[0],
+            full[0],
+            full[1],
+            end_sums[0] / gain_one[:, 0],
             grad_query,
             grad_key,
             grad_value,
             grad_gate_attn,
             grad_out,
-            head_ends[0, :head_rows],
-            head_ends[0, head_rows : 2 * head_rows],
-            gain_terms[1],
+            end_sums[1, :head_rows],
+            end_sums[1, head_rows : 2 * head_rows],
+            mid_terms,
             grad_gate,
             grad_up,
             grad_down,

time: 385 us -> 368 us (0.956); the launches traced: 379 us -> 366 us
  waiting for transfers between devices: 144 us -> 123 us
  blocking collectives: 34.1 us -> 46.9 us
    all_to_all x0 -> x1, blocking collectives: none -> 13.3 us  [shards(): lax.all_to_all(jnp.broadcast_to(both_gains[None], (n_shard, 8, HD)), 'sha...]
    ppermute x1 -> x5, starting transfers between devices: 0.09 us -> 10.5 us  [the longest x4 10.4 us: owners_at_once(): lax.ppermute(block, ('shard', 'ctx', 'tp'), perm)]
    ppermute x3 -> x2, waiting for transfers between devices: 37.9 us -> 27.7 us  [swapped(): return jnp.where(native, value, lax.ppermute(value, PLANE, swap_perm))]
    all_to_all x1, waiting for transfers between devices: 9.96 us -> 0.01 us  [shards(): lax.all_to_all(pieces.reshape(n_shard * copies, 8, HD), ('shard', 'ctx',...]
    ppermute x1 -> x5, waiting for transfers between devices: 1.82 us -> 6.79 us  [the longest x4 5.82 us: owners_at_once(): lax.ppermute(block, ('shard', 'ctx', 'tp'), perm)]
    ppermute x9 -> x6, waiting for transfers between devices: 28.3 us -> 33.1 us  [ctx_turn(): lax.ppermute(value, 'ctx', [(i, (i + by) % n_ctx) for i in range(n_ctx)])]
    all_to_all x1 -> x0, starting transfers between devices: 4.7 us -> none  [plane_exchange(): return lax.all_to_all(value, PLANE, 0, 0, axis_index_groups=planes)]
    ppermute x11, waiting for transfers between devices: 18.1 us -> 13.6 us  [core_swap(): return lax.ppermute(value, 'shard', core_perm)]
  transfers between devices with their start and end apart: 33 -> 33, of which waited for: 24 -> 22; matrix products, arithmetic and copies ran while one was open for 5% -> 6% of each run, Pallas kernels for 15% -> 15%
where the time goes in v10:
time: 368 us; the launch traced here: 366 us
  waiting for transfers between devices  123 us (33%)
  Pallas kernels  76.7 us (21%)
  starting transfers between devices  55.3 us (15%)
  blocking collectives  46.9 us (13%)
  local copies, waits for them, and re-layouts  35.3 us (10%)
  between operations  14.6 us (4%)
  other arithmetic  14.4 us (4%)
    pallas_call x15, Pallas kernels, call(): return lambda *operands: built(*operands, *behind)  59.1 us
    all_to_all x3, waiting for transfers between devices, ctx_exchange(): return lax.all_to_all(value, 'ctx', 0, 0)  41.5 us
    all_to_all x2, blocking collectives, ctx_exchange(): return lax.all_to_all(value, 'ctx', 0, 0)  33.5 us
    ppermute x6, waiting for transfers between devices, ctx_turn(): lax.ppermute(value, 'ctx', [(i, (i + by) % n_ctx) for i in range(n_ctx)])  33.1 us
    ppermute x2, waiting for transfers between devices, swapped(): return jnp.where(native, value, lax.ppermute(value, PLANE, swap_perm))  27.7 us
    unnamed x128, local copies, waits for them, and re-layouts  26.6 us
    ppermute x11, waiting for transfers between devices, core_swap(): return lax.ppermute(value, 'shard', core_perm)  13.6 us
    all_to_all x1, blocking collectives, shards(): lax.all_to_all(jnp.broadcast_to(both_gains[None], (n_shard, 8, HD)), 'sha...  13.3 us
  transfers between devices with their start and end apart: 33, of which 22 were waited for; matrix products, arithmetic and copies ran while one was open for 6% of the time, Pallas kernels for 15%

profile of v10, /device:TPU:1, one launch (start us, length us, event | category | flops | bytes accessed | tf_op | source)
XLA Modules:
  0.0 366.3 jit_solution(18027803454521678281)
XLA Ops:
  7.3 1.8 shard_map.263
  10.6 4.7 %collective-permute-start.6 = (bf16[128,2304]{1,0:T(8,128)(2,1)S(1)}, bf16[128,2304]{1,0:T(8,128)(2,1)S(1)}, u32[]{:S(2)}, u32[]{:S(2)}) collective-permute-start(bf16[128,2304]{1,0:T(8,128)(2,1)S(1)} %pad_maximum_fusion.1), channel_id=1, source_target_pairs={{8,1},{1,8},{24,17},{17,24},{40,33},{33,40},{56,49},{49,56},{72,65... | collective-permute-start | bytes 1769480 | tf_op jit(solution)/shard_map/ppermute | solution.py:821
  15.4 7.5 %collective-permute-done.6 = bf16[128,2304]{1,0:T(8,128)(2,1)S(1)} collective-permute-done((bf16[128,2304]{1,0:T(8,128)(2,1)S(1)}, bf16[128,2304]{1,0:T(8,128)(2,1)S(1)}, u32[]{:S(2)}, u32[]{:S(2)}) %collective-permute-start.6) | collective-permute-done | bytes 589856 | tf_op jit(solution)/shard_map/ppermute | solution.py:821
  24.2 1.9 collective-permute-done
  27.0 1.6 broadcast_in_dim.24
  28.6 5.2 %all-to-all-start = ((bf16[4,128,2048]{2,1,0:T(8,128)(2,1)}), bf16[4,128,2048]{2,1,0:T(8,128)(2,1)S(1)}, u32[]{:S(2)}, u32[]{:S(2)}) async-start(bf16[4,128,2048]{2,1,0:T(8,128)(2,1)} %broadcast_in_dim.24), calls=%async_computation | async-start | bytes 4194304 | tf_op jit(solution)/shard_map/all_to_all | solution.py:773
  34.3 25.4 %all-to-all-done.refs_0_.refs_2_.refs_1_ = bf16[4,128,2048]{2,1,0:T(8,128)(2,1)S(1)} async-done(((bf16[4,128,2048]{2,1,0:T(8,128)(2,1)}), bf16[4,128,2048]{2,1,0:T(8,128)(2,1)S(1)}, u32[]{:S(2)}, u32[]{:S(2)}) %all-to-all-start) | async-done | bytes 2097184 | tf_op jit(solution)/shard_map/all_to_all | solution.py:773
  59.8 1.3 collective-permute-start.1
  63.5 1.5 collective-permute-done.1.refs_1_.refs_3_.refs_2_
  65.4 2.4 shard_map.264
  68.6 13.3 %all_to_all.35 = bf16[16,8,128]{2,1,0:T(8,128)(2,1)S(1)} all-to-all(bf16[16,8,128]{2,1,0:T(8,128)(2,1)S(1)} %broadcast_in_dim.27), channel_id=1, replica_groups=mesh['shard'=16,'ctx'=4,'tp'=2] {'shard'}, dimensions={0} | all-to-all | bytes 65536 | tf_op jit(solution)/shard_map/all_to_all | solution.py:835
  82.2 4.8 %shard_map.265 = bf16[8,2,128,1024]{3,2,1,0:T(8,128)(2,1)} custom-call(s32[1]{0:T(128)} %bitcast.15.core, bf16[8,2,128,1024]{3,2,1,0:T(8,128)(2,1)} %bitcast.90, bf16[8,128,1024]{2,1,0:T(8,128)(2,1)} %collective-permute-done.3.other), custom_call_target="tpu_custom_call" | custom-call | flops 1048576 | bytes 8388608 | tf_op jit(solution)/shard_map/pallas_call | solution.py:630
  87.0 5.6 %shard_map.266 = (bf16[512,2048]{1,0:T(8,128)(2,1)S(1)}, f32[512,384]{1,0:T(8,128)S(1)}, bf16[512,512]{1,0:T(8,128)(2,1)S(1)}, f32[512,256]{1,0:T(8,128)S(1)}) custom-call(bf16[4,128,2048]{2,1,0:T(8,128)(2,1)} %copy-done.46, bf16[4,128,2048]{2,1,0:T(8,128)(2,1)} %collective-permute-done.1.refs_1_.refs_3_.refs_2_, bf16[2048,1024]{1,0:T(8,128)(2,1)} %bitcast.85, ...), custom_call_target="tpu_custom_call" | custom-call | flops 1610612736 | bytes 8388608 | tf_op jit(solution)/shard_map/pallas_call | solution.py:98
  92.6 1.3 copy-done.25
  93.9 6.4 %shard_map.268 = (f32[2,512,512]{2,1,0:T(8,128)}, f32[512,256]{1,0:T(8,128)S(1)}, bf16[512,256]{1,0:T(8,128)(2,1)S(1)}, bf16[256,2048]{1,0:T(8,128)(2,1)S(1)}, bf16[256,2048]{1,0:T(8,128)(2,1)S(1)}) custom-call(bf16[512,512]{1,0:T(8,128)(2,1)S(1)} %get-tuple-element.70.refs_0_.refs_1_, f32[512,256]{1,0:T(8,128)S(1)} %get-tuple-element.71.refs_1_.refs_3_, ...), custom_call_target="tpu_custom_call" | custom-call | flops 805306368 | bytes 8388608 | tf_op jit(solution)/shard_map/pallas_call | solution.py:98
  100.8 2.3 collective-permute-done.4
  103.1 1.4 add_convert_fusion.3
  104.5 3.5 all-to-all-start.2
  108.9 1.7 copy-done.26
  110.6 1.3 shard_map.267.refs_2_.refs_0_
  111.9 10.9 %all-to-all-done.2.refs_0_ = bf16[4,64,2048]{2,1,0:T(8,128)(2,1)S(1)} async-done(((bf16[4,64,2048]{2,1,0:T(8,128)(2,1)}), bf16[4,64,2048]{2,1,0:T(8,128)(2,1)S(1)}, u32[]{:S(2)}, u32[]{:S(2)}) %all-to-all-start.2) | async-done | bytes 1048608 | tf_op jit(solution)/shard_map/all_to_all | solution.py:773
  124.9 16.3 %all_to_all.36 = bf16[4,64,2048]{2,1,0:T(8,128)(2,1)S(1)} all-to-all(bf16[4,64,2048]{2,1,0:T(8,128)(2,1)S(1)} %get-tuple-element.76), channel_id=1, replica_groups=mesh['shard'=16,'ctx'=4,'tp'=2] {'ctx'}, dimensions={0} | all-to-all | bytes 2097152 | tf_op jit(solution)/shard_map/all_to_all | solution.py:773
  141.2 2.1 collective-permute-start.5
  143.4 2.3 collective-permute-done.5
  145.6 1.3 shard_map.270.refs_7_.refs_0_
  147.0 1.3 copy-done.2
  150.6 8.6 %shard_map.271 = (bf16[512,768]{1,0:T(8,128)(2,1)S(1)}, bf16[512,768]{1,0:T(8,128)(2,1)S(1)}, bf16[512,768]{1,0:T(8,128)(2,1)S(1)}) custom-call(bf16[256,2048]{1,0:T(8,128)(2,1)S(1)} %bitcast.78, bf16[256,2048]{1,0:T(8,128)(2,1)S(1)} %bitcast.84, bf16[4,128,2048]{2,1,0:T(8,128)(2,1)} %copy-done.46, ...), custom_call_target="tpu_custom_call" | custom-call | flops 4831838208 | bytes 8388608 | tf_op jit(solution)/shard_map/pallas_call | solution.py:98
  159.2 8.4 %shard_map.272.refs_4_ = bf16[2048,2304]{1,0:T(8,128)(2,1)} custom-call(bf16[2048,512]{1,0:T(8,128)(2,1)S(1)} %copy-done.3, bf16[4,128,2048]{2,1,0:T(8,128)(2,1)} %copy-done.46, bf16[4,128,2048]{2,1,0:T(8,128)(2,1)} %collective-permute-done.1.refs_1_.refs_3_.refs_2_, bf16[512,768]{1,0:T(8,128)(2,1)S(1)} %get-tuple-element.77.refs_3_.refs_0_, ...), custom_call_target="tpu_custom_call" | custom-call | flops 4831838208 | bytes 8388608 | tf_op jit(solution)/shard_map/pallas_call | solution.py:98
  172.5 6.0 %shard_map.273 = (bf16[256,2048]{1,0:T(8,128)(2,1)S(1)}, bf16[256,2048]{1,0:T(8,128)(2,1)S(1)}) custom-call(bf16[512,768]{1,0:T(8,128)(2,1)S(1)} %copy-done.11, bf16[512,768]{1,0:T(8,128)(2,1)S(1)} %copy-done.13, bf16[2048,2304]{1,0:T(8,128)(2,1)} %all-gather.5.cloned.1.call-done.refs_4_.refs_5_.refs_6_.refs_2_.refs_3_.refs_1_, ...), custom_call_target="tpu_custom_call" | custom-call | flops 3221225472 | bytes 8388608 | tf_op jit(solution)/shard_map/pallas_call | solution.py:98
  178.9 2.3 collective-permute-done.7
  181.6 17.2 %all_to_all.37.refs_0_ = bf16[4,64,2048]{2,1,0:T(8,128)(2,1)S(1)} all-to-all(bf16[4,64,2048]{2,1,0:T(8,128)(2,1)S(1)} %bitcast.79), channel_id=1, replica_groups=mesh['shard'=16,'ctx'=4,'tp'=2] {'ctx'}, dimensions={0} | all-to-all | bytes 2097152 | tf_op jit(solution)/shard_map/all_to_all | solution.py:773
  202.1 3.5 all-to-all-start.5
  208.1 5.2 %shard_map.275 = (bf16[256,2048]{1,0:T(8,128)(2,1)S(1)}, bf16[256,2048]{1,0:T(8,128)(2,1)}) custom-call(bf16[512,768]{1,0:T(8,128)(2,1)S(1)} %copy-done.9, bf16[2048,2304]{1,0:T(8,128)(2,1)} %all-gather.5.cloned.1.call-done.refs_4_.refs_5_.refs_6_.refs_2_.refs_3_.refs_1_, bf16[4,64,2048]{2,1,0:T(8,128)(2,1)S(1)} %bitcast.80), custom_call_target="tpu_custom_call" | custom-call | flops 1610612736 | bytes 8388608 | tf_op jit(solution)/shard_map/pallas_call | solution.py:98
  214.2 5.2 %all-to-all-done.5 = bf16[4,64,2048]{2,1,0:T(8,128)(2,1)S(1)} async-done(((bf16[4,64,2048]{2,1,0:T(8,128)(2,1)}), bf16[4,64,2048]{2,1,0:T(8,128)(2,1)S(1)}, u32[]{:S(2)}, u32[]{:S(2)}) %all-to-all-start.5) | async-done | bytes 1048608 | tf_op jit(solution)/shard_map/all_to_all | solution.py:773
  219.4 2.2 collective-permute-start.8
  221.6 2.3 collective-permute-done.8
  226.0 2.1 shard_map.276
  228.3 3.1 shard_map.277
  231.5 4.4 %shard_map.278.refs_3_ = bf16[2048,1024]{1,0:T(8,128)(2,1)} custom-call(bf16[2048,512]{1,0:T(8,128)(2,1)S(1)} %shard_map.267.refs_2_.refs_0_, bf16[256,2048]{1,0:T(8,128)(2,1)S(1)} %bitcast.76, bf16[256,2048]{1,0:T(8,128)(2,1)S(1)} %bitcast.82, bf16[512,512]{1,0:T(8,128)(2,1)S(1)} %get-tuple-element.91.refs_3_.refs_0_, ...), custom_call_target="tpu_custom_call" | custom-call | flops 2147483648 | bytes 8388608 | tf_op jit(solution)/shard_map/pallas_call | solution.py:98
  237.9 5.1 %shard_map.280 = (bf16[256,2048]{1,0:T(8,128)(2,1)S(1)}, bf16[256,2048]{1,0:T(8,128)(2,1)}) custom-call(bf16[512,512]{1,0:T(8,128)(2,1)S(1)} %copy-done.23, bf16[512,256]{1,0:T(8,128)(2,1)S(1)} %copy-done.33, bf16[2048,1024]{1,0:T(8,128)(2,1)} %bitcast.88, bf16[2048,1024]{1,0:T(8,128)(2,1)} %shard_map.278.refs_3_), custom_call_target="tpu_custom_call" | custom-call | flops 1610612736 | bytes 8388608 | tf_op jit(solution)/shard_map/pallas_call | solution.py:98
  243.4 1.6 add_convert_fusion.1
  246.0 1.6 add_convert_fusion
  249.3 2.0 collective-permute-start.17
  252.0 11.7 %collective-permute-done.16.refs_1_ = bf16[128,2048]{1,0:T(8,128)(2,1)S(1)} collective-permute-done((bf16[128,2048]{1,0:T(8,128)(2,1)}, bf16[128,2048]{1,0:T(8,128)(2,1)S(1)}, u32[]{:S(2)}, u32[]{:S(2)}) %collective-permute-start.16) | collective-permute-done | bytes 524320 | tf_op jit(solution)/shard_map/ppermute | solution.py:776
  263.7 10.7 %collective-permute-done.17.refs_2_ = bf16[128,2048]{1,0:T(8,128)(2,1)S(1)} collective-permute-done((bf16[128,2048]{1,0:T(8,128)(2,1)}, bf16[128,2048]{1,0:T(8,128)(2,1)S(1)}, u32[]{:S(2)}, u32[]{:S(2)}) %collective-permute-start.17) | collective-permute-done | bytes 524320 | tf_op jit(solution)/shard_map/ppermute | solution.py:776
  277.6 1.6 collective-permute-start.19
  280.0 4.7 %all-to-all-start.6 = ((bf16[128,8,128]{2,1,0:T(8,128)(2,1)}), bf16[128,8,128]{2,1,0:T(8,128)(2,1)S(1)}, u32[]{:S(2)}, u32[]{:S(2)}) async-start(bf16[128,8,128]{2,1,0:T(8,128)(2,1)} %bitcast.42), calls=%async_computation.8 | async-start | bytes 524288 | tf_op jit(solution)/shard_map/all_to_all | solution.py:924
  284.8 3.5 collective-permute-start.9
  288.7 1.3 collective-permute-start.20
  290.0 20.1 %collective-permute-done.9 = bf16[128,2304]{1,0:T(8,128)(2,1)S(1)} collective-permute-done((bf16[128,2304]{1,0:T(8,128)(2,1)}, bf16[128,2304]{1,0:T(8,128)(2,1)S(1)}, u32[]{:S(2)}, u32[]{:S(2)}) %collective-permute-start.9) | collective-permute-done | bytes 589856 | tf_op jit(solution)/shard_map/ppermute | solution.py:821
  310.2 1.5 collective-permute-start.10
  311.7 2.7 collective-permute-start.11
  318.0 2.6 collective-permute-done.10.b1
  320.6 7.5 %collective-permute-done.11.b2 = bf16[128,2304]{1,0:T(8,128)(2,1)} collective-permute-done((bf16[128,2304]{1,0:T(8,128)(2,1)S(1)}, bf16[128,2304]{1,0:T(8,128)(2,1)}, u32[]{:S(2)}, u32[]{:S(2)}) %collective-permute-start.11) | collective-permute-done | bytes 589856 | tf_op jit(solution)/shard_map/ppermute | solution.py:776
  328.1 5.5 %shard_map.279 = (f32[128,3072]{1,0:T(8,128)}, f32[128,3072]{1,0:T(8,128)}, f32[3072,128]{1,0:T(8,128)}, f32[128,128]{1,0:T(8,128)}) custom-call(s32[1]{0:T(128)} %bitcast.at.turn_at, bf16[128,2304]{1,0:T(8,128)(2,1)} %copy-done.49, bf16[128,2304]{1,0:T(8,128)(2,1)} %collective-permute-done.10.b1, bf16[128,2304]{1,0:T(8,128)(2,1)} %collective-permute-done.11.b2, ...), custom_call_target="tpu_custom_call" | custom-call | flops 1048576 | bytes 8388608 | tf_op jit(solution)/shard_map/pallas_call | solution.py:695
  334.6 1.4 select_convert_fusion
  337.5 4.8 %collective-permute-start.21 = (bf16[128,1024]{1,0:T(8,128)(2,1)}, bf16[128,1024]{1,0:T(8,128)(2,1)S(1)}, u32[]{:S(2)}, u32[]{:S(2)}) collective-permute-start(bf16[128,1024]{1,0:T(8,128)(2,1)} %reduce-scatter.3.cloned.1.call-done), channel_id=1, source_target_pairs={{1,8},{3,10},{5,12},{7,14},{8,1},{10,3},{12,5},{14,7},{17,24},{19,... | collective-permute-start | bytes 786440 | tf_op jit(solution)/shard_map/ppermute | solution.py:903
  343.4 3.3 collective-permute-start.23
  346.7 1.3 collective-permute-start.24
  347.9 1.5 slice_bitcast_fusion
  350.1 1.9 collective-permute-done.22.b1
  352.0 2.6 collective-permute-done.23.b2
  354.6 1.4 collective-permute-done.24.b3
  356.7 3.1 shard_map.282
  (227 shorter events, 47.0 us)
Async XLA Ops:
  7.2 3.2 copy-start.62
  7.2 58.2 %all-gather.3.cloned.1.call-start = ((), (), s32[]{:S(2)}) async-start(), calls=%async_computation.9 | async-start | bytes 4456448 | tf_op jit(solution)/shard_map/all_gather | solution.py:789
  9.1 140.2 %all-gather.5.cloned.1.call-start = ((), (), s32[]{:S(2)}) async-start(), calls=%async_computation.10 | async-start | bytes 10027008 | tf_op jit(solution)/shard_map/all_gather | solution.py:789
  10.4 13.5 %copy-start.51 = (bf16[128,2048]{1,0:T(8,128)(2,1)S(1)}, bf16[128,2048]{1,0:T(8,128)(2,1)}, u32[]{:S(2)}) copy-start(bf16[128,2048]{1,0:T(8,128)(2,1)} %param.31) | copy-start | bytes 1572868
  10.4 13.5 %copy-start.52 = (bf16[128,2048]{1,0:T(8,128)(2,1)S(1)}, bf16[128,2048]{1,0:T(8,128)(2,1)}, u32[]{:S(2)}) copy-start(bf16[128,2048]{1,0:T(8,128)(2,1)} %param.16) | copy-start | bytes 1572868
  10.6 12.3 %collective-permute-start.6 = (bf16[128,2304]{1,0:T(8,128)(2,1)S(1)}, bf16[128,2304]{1,0:T(8,128)(2,1)S(1)}, u32[]{:S(2)}, u32[]{:S(2)}) collective-permute-start(bf16[128,2304]{1,0:T(8,128)(2,1)S(1)} %pad_maximum_fusion.1), channel_id=1, source_target_pairs={{8,1},{1,8},{24,17},{17,24},{40,33},{33,40},{56,49},{49,56},{72,65... | collective-permute-start | bytes 1769480 | tf_op jit(solution)/shard_map/ppermute | solution.py:821
  24.1 2.0 collective-permute-start
  28.6 5.2 %copy-start.57 = (s32[1,13]{1,0:T(1,128)S(1)}, s32[1,13]{1,0:T(1,128)}, u32[]{:S(2)}) copy-start(s32[1,13]{1,0:T(1,128)} %param.18) | copy-start | bytes 160
  28.6 5.2 %copy-start.58 = (s32[1,13]{1,0:T(1,128)S(1)}, s32[1,13]{1,0:T(1,128)}, u32[]{:S(2)}) copy-start(s32[1,13]{1,0:T(1,128)} %param.17) | copy-start | bytes 160
  28.6 31.2 %all-to-all-start = ((bf16[4,128,2048]{2,1,0:T(8,128)(2,1)}), bf16[4,128,2048]{2,1,0:T(8,128)(2,1)S(1)}, u32[]{:S(2)}, u32[]{:S(2)}) async-start(bf16[4,128,2048]{2,1,0:T(8,128)(2,1)} %broadcast_in_dim.24), calls=%async_computation | async-start | bytes 4194304 | tf_op jit(solution)/shard_map/all_to_all | solution.py:773
  33.8 27.6 %collective-permute-start.2 = (s32[2,13]{1,0:T(2,128)S(1)}, s32[2,13]{1,0:T(2,128)S(1)}, u32[]{:S(2)}, u32[]{:S(2)}) collective-permute-start(s32[2,13]{1,0:T(2,128)S(1)} %pad_add_fusion.2), channel_id=1, source_target_pairs={{0,8},{8,0},{16,24},{24,16},{32,40},{40,32},{48,56},{56,48},{64,72... | collective-permute-start | bytes 320 | tf_op jit(solution)/shard_map/ppermute | solution.py:770
  59.8 5.7 %copy-start.46 = (bf16[4,128,2048]{2,1,0:T(8,128)(2,1)}, bf16[4,128,2048]{2,1,0:T(8,128)(2,1)S(1)}, u32[]{:S(2)}) copy-start(bf16[4,128,2048]{2,1,0:T(8,128)(2,1)S(1)} %all-to-all-done.refs_0_.refs_2_.refs_1_) | copy-start | bytes 6291460
  59.8 5.2 %collective-permute-start.1 = (bf16[4,128,2048]{2,1,0:T(8,128)(2,1)S(1)}, bf16[4,128,2048]{2,1,0:T(8,128)(2,1)}, u32[]{:S(2)}, u32[]{:S(2)}) collective-permute-start(bf16[4,128,2048]{2,1,0:T(8,128)(2,1)S(1)} %all-to-all-done.refs_0_.refs_2_.refs_1_), channel_id=1, source_target_pairs={{0,8},{8,0},{16,24},{24,16},{32,40},{40,32},{48,56},{56,48},{64,72... | collective-permute-start | bytes 6291464 | tf_op jit(solution)/shard_map/ppermute | solution.py:770
  63.5 23.5 %copy-start.14 = (f32[512,128]{1,0:T(8,128)}, f32[512,128]{1,0:T(8,128)S(1)}, u32[]{:S(2)}) copy-start(f32[512,128]{1,0:T(8,128)S(1)} %get-tuple-element.67.refs_4_.refs_5_) | copy-start | bytes 786436
  65.4 3.2 copy-start.60
  65.4 3.2 copy-start.61
  67.8 14.4 %collective-permute-start.3 = (bf16[8,128,1024]{2,1,0:T(8,128)(2,1)S(1)}, bf16[8,128,1024]{2,1,0:T(8,128)(2,1)}, u32[]{:S(2)}, u32[]{:S(2)}) collective-permute-start(bf16[8,128,1024]{2,1,0:T(8,128)(2,1)S(1)} %shard_map.264), channel_id=1, source_target_pairs={{0,8},{8,0},{16,24},{24,16},{32,40},{40,32},{48,56},{56,48},{64,72... | collective-permute-start | bytes 6291464 | tf_op jit(solution)/shard_map/ppermute | solution.py:770
  93.9 6.4 %copy-start.18 = (f32[512,256]{1,0:T(8,128)}, f32[512,256]{1,0:T(8,128)S(1)}, u32[]{:S(2)}) copy-start(f32[512,256]{1,0:T(8,128)S(1)} %get-tuple-element.71.refs_1_.refs_3_) | copy-start | bytes 1572868
  93.9 6.4 %copy-start.20 = (bf16[512,512]{1,0:T(8,128)(2,1)}, bf16[512,512]{1,0:T(8,128)(2,1)S(1)}, u32[]{:S(2)}) copy-start(bf16[512,512]{1,0:T(8,128)(2,1)S(1)} %get-tuple-element.70.refs_0_.refs_1_) | copy-start | bytes 1572868
  93.9 6.4 %copy-start.36 = (f32[512,384]{1,0:T(8,128)}, f32[512,384]{1,0:T(8,128)S(1)}, u32[]{:S(2)}) copy-start(f32[512,384]{1,0:T(8,128)S(1)} %get-tuple-element.90.refs_3_) | copy-start | bytes 2359300
  100.4 4.1 %copy-start.38 = (f32[512,256]{1,0:T(8,128)}, f32[512,256]{1,0:T(8,128)S(1)}, u32[]{:S(2)}) copy-start(f32[512,256]{1,0:T(8,128)S(1)} %get-tuple-element.88.refs_4_) | copy-start | bytes 1572868
  100.4 4.1 %copy-start.44 = (bf16[512,256]{1,0:T(8,128)(2,1)}, bf16[512,256]{1,0:T(8,128)(2,1)S(1)}, u32[]{:S(2)}) copy-start(bf16[512,256]{1,0:T(8,128)(2,1)S(1)} %get-tuple-element.93.refs_5_) | copy-start | bytes 786436
  100.4 2.7 collective-permute-start.4
  103.1 4.9 %copy-start.48 = (bf16[128,2048]{1,0:T(8,128)(2,1)S(1)}, bf16[128,2048]{1,0:T(8,128)(2,1)}, u32[]{:S(2)}) copy-start(bf16[128,2048]{1,0:T(8,128)(2,1)} %copy-done.47) | copy-start | bytes 1572868
  104.5 18.4 %all-to-all-start.2 = ((bf16[4,64,2048]{2,1,0:T(8,128)(2,1)}), bf16[4,64,2048]{2,1,0:T(8,128)(2,1)S(1)}, u32[]{:S(2)}, u32[]{:S(2)}) async-start(bf16[4,64,2048]{2,1,0:T(8,128)(2,1)} %bitcast.21), calls=%async_computation.2 | async-start | bytes 2097152 | tf_op jit(solution)/shard_map/all_to_all | solution.py:773
  108.0 176.8 %reduce-scatter.5.cloned.1.call-start = ((), (), s32[]{:S(2)}) async-start(), calls=%async_computation.12 | async-start | bytes 10027008 | tf_op jit(solution)/shard_map/reduce_scatter | solution.py:792
  141.2 4.4 %collective-permute-start.5 = (bf16[4,64,2048]{2,1,0:T(8,128)(2,1)S(1)}, bf16[4,64,2048]{2,1,0:T(8,128)(2,1)S(1)}, u32[]{:S(2)}, u32[]{:S(2)}) collective-permute-start(bf16[4,64,2048]{2,1,0:T(8,128)(2,1)S(1)} %all_to_all.36), channel_id=1, source_target_pairs={{0,8},{8,0},{16,24},{24,16},{32,40},{40,32},{48,56},{56,48},{64,72... | collective-permute-start | bytes 3145736 | tf_op jit(solution)/shard_map/ppermute | solution.py:770
  150.6 8.6 %copy-start.3 = (bf16[2048,512]{1,0:T(8,128)(2,1)S(1)}, bf16[2048,512]{1,0:T(8,128)(2,1)}, u32[]{:S(2)}) copy-start(bf16[2048,512]{1,0:T(8,128)(2,1)} %copy-done.2) | copy-start | bytes 6291460
  178.4 2.7 collective-permute-start.7
  181.2 18.6 %copy-start.28 = (f32[64,2048]{1,0:T(8,128)S(1)}, f32[64,2048]{1,0:T(8,128)}, u32[]{:S(2)}) copy-start(f32[64,2048]{1,0:T(8,128)} %copy-done.27) | copy-start | bytes 1572868
  181.2 18.6 %copy-start.35 = (bf16[64,2048]{1,0:T(8,128)(2,1)S(1)}, bf16[64,2048]{1,0:T(8,128)(2,1)}, u32[]{:S(2)}) copy-start(bf16[64,2048]{1,0:T(8,128)(2,1)} %get-tuple-element.132.refs_2_) | copy-start | bytes 786436
  202.1 17.3 %all-to-all-start.5 = ((bf16[4,64,2048]{2,1,0:T(8,128)(2,1)}), bf16[4,64,2048]{2,1,0:T(8,128)(2,1)S(1)}, u32[]{:S(2)}, u32[]{:S(2)}) async-start(bf16[4,64,2048]{2,1,0:T(8,128)(2,1)} %copy-done.34), calls=%async_computation.5 | async-start | bytes 2097152 | tf_op jit(solution)/shard_map/all_to_all | solution.py:773
  205.6 131.9 %reduce-scatter.3.cloned.1.call-start = ((), (), s32[]{:S(2)}) async-start(), calls=%async_computation.11 | async-start | bytes 4456448 | tf_op jit(solution)/shard_map/reduce_scatter | solution.py:792
  219.4 4.5 %collective-permute-start.8 = (bf16[4,64,2048]{2,1,0:T(8,128)(2,1)S(1)}, bf16[4,64,2048]{2,1,0:T(8,128)(2,1)S(1)}, u32[]{:S(2)}, u32[]{:S(2)}) collective-permute-start(bf16[4,64,2048]{2,1,0:T(8,128)(2,1)S(1)} %all-to-all-done.5), channel_id=1, source_target_pairs={{0,8},{8,0},{16,24},{24,16},{32,40},{40,32},{48,56},{56,48},{64,72... | collective-permute-start | bytes 3145736 | tf_op jit(solution)/shard_map/ppermute | solution.py:770
  226.0 2.3 copy-start.37
  228.2 3.3 copy-start.32
  228.3 3.1 copy-start.45
  236.7 6.7 %copy-start.31 = (bf16[256,2048]{1,0:T(8,128)(2,1)S(1)}, bf16[256,2048]{1,0:T(8,128)(2,1)}, u32[]{:S(2)}) copy-start(bf16[256,2048]{1,0:T(8,128)(2,1)} %copy-done.30) | copy-start | bytes 3145732
  236.7 6.7 %collective-permute-start.14 = (bf16[256,2048]{1,0:T(8,128)(2,1)}, bf16[256,2048]{1,0:T(8,128)(2,1)}, u32[]{:S(2)}, u32[]{:S(2)}) collective-permute-start(bf16[256,2048]{1,0:T(8,128)(2,1)} %get-tuple-element.96), channel_id=1, source_target_pairs={{0,8},{8,0},{16,24},{24,16},{32,40},{40,32},{48,56},{56,48},{64,72... | collective-permute-start | bytes 3145736 | tf_op jit(solution)/shard_map/ppermute | solution.py:770
  243.0 3.1 collective-permute-start.15
  247.7 28.2 %copy-start.17 = (bf16[64,2048]{1,0:T(8,128)(2,1)S(1)}, bf16[64,2048]{1,0:T(8,128)(2,1)}, u32[]{:S(2)}) copy-start(bf16[64,2048]{1,0:T(8,128)(2,1)} %get-tuple-element.133.refs_1_.refs_6_) | copy-start | bytes 786436
  247.7 28.2 %copy-start.29 = (f32[64,2048]{1,0:T(8,128)S(1)}, f32[64,2048]{1,0:T(8,128)}, u32[]{:S(2)}) copy-start(f32[64,2048]{1,0:T(8,128)} %copy-done.27) | copy-start | bytes 1572868
  247.7 28.1 %copy-start.41 = (f32[64,2048]{1,0:T(8,128)S(1)}, f32[64,2048]{1,0:T(8,128)}, u32[]{:S(2)}) copy-start(f32[64,2048]{1,0:T(8,128)} %copy-done.40) | copy-start | bytes 1572868
  248.9 14.8 %collective-permute-start.16 = (bf16[128,2048]{1,0:T(8,128)(2,1)}, bf16[128,2048]{1,0:T(8,128)(2,1)S(1)}, u32[]{:S(2)}, u32[]{:S(2)}) collective-permute-start(bf16[128,2048]{1,0:T(8,128)(2,1)} %get-tuple-element.126), channel_id=1, source_target_pairs={{0,2},{2,4},{4,6},{6,0},{1,3},{3,5},{5,7},{7,1},{8,10},{10,12},{12... | collective-permute-start | bytes 1572872 | tf_op jit(solution)/shard_map/ppermute | solution.py:776
  249.3 25.2 %collective-permute-start.17 = (bf16[128,2048]{1,0:T(8,128)(2,1)}, bf16[128,2048]{1,0:T(8,128)(2,1)S(1)}, u32[]{:S(2)}, u32[]{:S(2)}) collective-permute-start(bf16[128,2048]{1,0:T(8,128)(2,1)} %get-tuple-element.127), channel_id=1, source_target_pairs={{0,4},{2,6},{4,0},{6,2},{1,5},{3,7},{5,1},{7,3},{8,12},{10,14},{12... | collective-permute-start | bytes 1572872 | tf_op jit(solution)/shard_map/ppermute | solution.py:776
  251.3 23.7 %collective-permute-start.18 = (bf16[128,2048]{1,0:T(8,128)(2,1)}, bf16[128,2048]{1,0:T(8,128)(2,1)S(1)}, u32[]{:S(2)}, u32[]{:S(2)}) collective-permute-start(bf16[128,2048]{1,0:T(8,128)(2,1)} %get-tuple-element.124), channel_id=1, source_target_pairs={{0,6},{2,0},{4,2},{6,4},{1,7},{3,1},{5,3},{7,5},{8,14},{10,8},{12,... | collective-permute-start | bytes 1572872 | tf_op jit(solution)/shard_map/ppermute | solution.py:776
  277.6 7.1 %collective-permute-start.19 = (bf16[128,2048]{1,0:T(8,128)(2,1)S(1)}, bf16[128,2048]{1,0:T(8,128)(2,1)S(1)}, u32[]{:S(2)}, u32[]{:S(2)}) collective-permute-start(bf16[128,2048]{1,0:T(8,128)(2,1)S(1)} %get-tuple-element.100), channel_id=1, source_target_pairs={{0,8},{8,0},{16,24},{24,16},{32,40},{40,32},{48,56},{56,48},{64,72... | collective-permute-start | bytes 1572872 | tf_op jit(solution)/shard_map/ppermute | solution.py:770
  280.0 36.8 %all-to-all-start.6 = ((bf16[128,8,128]{2,1,0:T(8,128)(2,1)}), bf16[128,8,128]{2,1,0:T(8,128)(2,1)S(1)}, u32[]{:S(2)}, u32[]{:S(2)}) async-start(bf16[128,8,128]{2,1,0:T(8,128)(2,1)} %bitcast.42), calls=%async_computation.8 | async-start | bytes 524288 | tf_op jit(solution)/shard_map/all_to_all | solution.py:924
  284.8 25.3 %collective-permute-start.9 = (bf16[128,2304]{1,0:T(8,128)(2,1)}, bf16[128,2304]{1,0:T(8,128)(2,1)S(1)}, u32[]{:S(2)}, u32[]{:S(2)}) collective-permute-start(bf16[128,2304]{1,0:T(8,128)(2,1)} %reduce-scatter.5.cloned.1.call-done), channel_id=1, source_target_pairs={{8,1},{1,8},{24,17},{17,24},{40,33},{33,40},{56,49},{49,56},{72,65... | collective-permute-start | bytes 1769480 | tf_op jit(solution)/shard_map/ppermute | solution.py:821
  288.4 21.8 %copy-start.50 = (bf16[128,2304]{1,0:T(8,128)(2,1)S(1)}, bf16[128,2304]{1,0:T(8,128)(2,1)}, u32[]{:S(2)}) copy-start(bf16[128,2304]{1,0:T(8,128)(2,1)} %reduce-scatter.5.cloned.1.call-done) | copy-start | bytes 1769476
  288.6 26.7 %copy-start.59 = (bf16[128]{0:T(256)(128)(2,1)S(1)}, bf16[128]{0:T(256)(128)(2,1)}, u32[]{:S(2)}) copy-start(bf16[128]{0:T(256)(128)(2,1)} %param.19) | copy-start | bytes 772
  288.7 45.9 %collective-permute-start.20 = (bf16[2,128,2048]{2,1,0:T(8,128)(2,1)S(1)}, bf16[2,128,2048]{2,1,0:T(8,128)(2,1)}, u32[]{:S(2)}, u32[]{:S(2)}) collective-permute-start(bf16[2,128,2048]{2,1,0:T(8,128)(2,1)S(1)} %pad_maximum_fusion), channel_id=1, source_target_pairs={{0,1},{9,8},{16,17},{25,24},{32,33},{41,40},{48,49},{57,56},{64,65... | collective-permute-start | bytes 3145736 | tf_op jit(solution)/shard_map/ppermute | solution.py:954
  310.2 17.9 %copy-start.49 = (bf16[128,2304]{1,0:T(8,128)(2,1)}, bf16[128,2304]{1,0:T(8,128)(2,1)S(1)}, u32[]{:S(2)}) copy-start(bf16[128,2304]{1,0:T(8,128)(2,1)S(1)} %broadcast_select_fusion.b0) | copy-start | bytes 1769476
  310.2 10.4 %collective-permute-start.10 = (bf16[128,2304]{1,0:T(8,128)(2,1)S(1)}, bf16[128,2304]{1,0:T(8,128)(2,1)}, u32[]{:S(2)}, u32[]{:S(2)}) collective-permute-start(bf16[128,2304]{1,0:T(8,128)(2,1)S(1)} %broadcast_select_fusion.b0), channel_id=1, source_target_pairs={{0,2},{2,4},{4,6},{6,0},{1,3},{3,5},{5,7},{7,1},{8,10},{10,12},{12... | collective-permute-start | bytes 1769480 | tf_op jit(solution)/shard_map/ppermute | solution.py:776
  311.7 16.4 %collective-permute-start.11 = (bf16[128,2304]{1,0:T(8,128)(2,1)S(1)}, bf16[128,2304]{1,0:T(8,128)(2,1)}, u32[]{:S(2)}, u32[]{:S(2)}) collective-permute-start(bf16[128,2304]{1,0:T(8,128)(2,1)S(1)} %broadcast_select_fusion.b0), channel_id=1, source_target_pairs={{0,4},{2,6},{4,0},{6,2},{1,5},{3,7},{5,1},{7,3},{8,12},{10,14},{12... | collective-permute-start | bytes 1769480 | tf_op jit(solution)/shard_map/ppermute | solution.py:776
  314.4 13.7 %collective-permute-start.12 = (bf16[128,2304]{1,0:T(8,128)(2,1)S(1)}, bf16[128,2304]{1,0:T(8,128)(2,1)}, u32[]{:S(2)}, u32[]{:S(2)}) collective-permute-start(bf16[128,2304]{1,0:T(8,128)(2,1)S(1)} %broadcast_select_fusion.b0), channel_id=1, source_target_pairs={{0,6},{2,0},{4,2},{6,4},{1,7},{3,1},{5,3},{7,5},{8,14},{10,8},{12,... | collective-permute-start | bytes 1769480 | tf_op jit(solution)/shard_map/ppermute | solution.py:776
  334.5 2.5 collective-permute-start.13
  337.0 22.8 %copy-start.1 = (bf16[3072,128]{1,0:T(8,128)(2,1)S(1)}, bf16[3072,128]{1,0:T(8,128)(2,1)}, u32[]{:S(2)}) copy-start(bf16[3072,128]{1,0:T(8,128)(2,1)} %param.30) | copy-start | bytes 2359300
  337.5 11.9 %copy-start.53 = (bf16[128,1024]{1,0:T(8,128)(2,1)S(1)}, bf16[128,1024]{1,0:T(8,128)(2,1)}, u32[]{:S(2)}) copy-start(bf16[128,1024]{1,0:T(8,128)(2,1)} %reduce-scatter.3.cloned.1.call-done) | copy-start | bytes 786436
  337.5 11.9 %collective-permute-start.21 = (bf16[128,1024]{1,0:T(8,128)(2,1)}, bf16[128,1024]{1,0:T(8,128)(2,1)S(1)}, u32[]{:S(2)}, u32[]{:S(2)}) collective-permute-start(bf16[128,1024]{1,0:T(8,128)(2,1)} %reduce-scatter.3.cloned.1.call-done), channel_id=1, source_target_pairs={{1,8},{3,10},{5,12},{7,14},{8,1},{10,3},{12,5},{14,7},{17,24},{19,... | collective-permute-start | bytes 786440 | tf_op jit(solution)/shard_map/ppermute | solution.py:903
  342.3 9.7 %collective-permute-start.22 = (bf16[128,1024]{1,0:T(8,128)(2,1)}, bf16[128,1024]{1,0:T(8,128)(2,1)S(1)}, u32[]{:S(2)}, u32[]{:S(2)}) collective-permute-start(bf16[128,1024]{1,0:T(8,128)(2,1)} %reduce-scatter.3.cloned.1.call-done), channel_id=1, source_target_pairs={{0,2},{1,10},{2,4},{3,12},{4,6},{5,14},{6,0},{7,8},{8,3},{9,11},{1... | collective-permute-start | bytes 786440 | tf_op jit(solution)/shard_map/ppermute | solution.py:903
  343.4 11.2 %collective-permute-start.23 = (bf16[128,1024]{1,0:T(8,128)(2,1)}, bf16[128,1024]{1,0:T(8,128)(2,1)S(1)}, u32[]{:S(2)}, u32[]{:S(2)}) collective-permute-start(bf16[128,1024]{1,0:T(8,128)(2,1)} %reduce-scatter.3.cloned.1.call-done), channel_id=1, source_target_pairs={{0,4},{1,12},{2,6},{3,14},{4,0},{5,8},{6,2},{7,10},{8,5},{9,13},{1... | collective-permute-start | bytes 786440 | tf_op jit(solution)/shard_map/ppermute | solution.py:903
  346.7 9.3 %collective-permute-start.24 = (bf16[128,1024]{1,0:T(8,128)(2,1)}, bf16[128,1024]{1,0:T(8,128)(2,1)S(1)}, u32[]{:S(2)}, u32[]{:S(2)}) collective-permute-start(bf16[128,1024]{1,0:T(8,128)(2,1)} %reduce-scatter.3.cloned.1.call-done), channel_id=1, source_target_pairs={{0,6},{1,14},{2,0},{3,8},{4,2},{5,10},{6,4},{7,12},{8,7},{9,15},{1... | collective-permute-start | bytes 786440 | tf_op jit(solution)/shard_map/ppermute | solution.py:903
  352.0 4.0 %copy-start.54 = (bf16[128,1024]{1,0:T(8,128)(2,1)}, bf16[128,1024]{1,0:T(8,128)(2,1)S(1)}, u32[]{:S(2)}) copy-start(bf16[128,1024]{1,0:T(8,128)(2,1)S(1)} %collective-permute-done.22.b1) | copy-start | bytes 786436
  (32 other events, 37.8 us)
Sparse Core Ops, SparseCore 0:
  10.8 54.5 all-gather.2
  68.2 75.1 all-gather.4
  170.3 81.4 reduce-scatter.4
  255.4 78.1 reduce-scatter.2

commit v11 on v10

--- a/solution.py
+++ b/solution.py
@@ -77,7 +77,9 @@
     return slice(number * HD, (number + 1) * HD)
 
 
-def call(kernel, grid, in_specs, out_specs, out_shape, flops, scratch=(), moved=8 << 20, behind=()):
+def call(
+    kernel, grid, in_specs, out_specs, out_shape, flops, scratch=(), moved=8 << 20, behind=(), vmem=VMEM
+):
     count = len(in_specs)
 
     def body(*refs):
@@ -91,7 +93,7 @@
         out_shape=out_shape,
         scratch_shapes=scratch,
         compiler_params=pltpu.CompilerParams(
-            dimension_semantics=("arbitrary",) * len(grid), vmem_limit_bytes=VMEM
+            dimension_semantics=("arbitrary",) * len(grid), vmem_limit_bytes=vmem
         ),
         cost_estimate=pl.CostEstimate(flops=flops, bytes_accessed=moved, transcendentals=0),
     )
@@ -270,6 +272,7 @@
         [struct((2 * half, units), BF16)] * 3,
         2 * 2 * half * width * units * 3,
         behind=behind,
+        vmem=60 << 20,
     )(ua, ub, ca, cb, w, w, w)
 
 
@@ -297,6 +300,7 @@
         [struct((half, width), BF16), struct((half, width), BF16)],
         2 * length * width * units * 2,
         behind=behind,
+        vmem=48 << 20,
     )(d_gate, d_up, w, w)
 
 
@@ -360,6 +364,7 @@
         struct((width, 3 * units), BF16),
         2 * length * width * units * 3,
         scratch=[pltpu.VMEM((units, length), BF16)],
+        vmem=56 << 20,
         behind=behind,
     )(u_flip, ca, cb, d_gate, d_up, hidden)
 
@@ -835,7 +840,6 @@
         both_gains = lax.all_to_all(
             jnp.broadcast_to(both_gains[None], (n_shard, 8, HD)), "shard", 0, 0
         )
-        gains = both_gains[:, :, :head_rows].astype(F32).transpose(1, 0, 2).reshape(8, HD)
 
         def half_rows(place):
             pieces = [lax.dynamic_slice_in_dim(v, place * rows, rows, 0) for v in (tokens, cotangent)]
@@ -844,14 +848,18 @@
         own = jnp.where(native, half_rows(core), core_swap(half_rows(1 - core)))
         tree = jnp.concatenate([seg_lengths, seg_parents], axis=0)
         tree = jnp.where(native, tree, core_swap(tree))
+        own, both_gains = lax.optimization_barrier((own, both_gains))
         own_x, own_cot = own[:rows], own[rows:]
         xa, xb = tree_rows(jnp.broadcast_to(own[None], (n_ctx,) + own.shape))
 
         second = jnp.concatenate([quarter(w_gate, 1), quarter(w_up, 1)], axis=1)
         second = (second.astype(F32) * gain_two).astype(BF16)
         second = jnp.concatenate([second, quarter(w_down, 0).T], axis=1)
-        w2 = plane_gather(swapped(second))
-
+        moved = lax.ppermute(second, PLANE, swap_perm)
+        moved, xa = lax.optimization_barrier((moved, xa))
+        w2 = plane_gather(jnp.where(native, second, moved))
+
+        gains = both_gains[:, :, :head_rows].astype(F32).transpose(1, 0, 2).reshape(8, HD)
         half_at = jnp.where(jnp.arange(2) == 0, core, 1 - core) * rows
         places = (
             half_at[:, None, None]
@@ -894,6 +902,7 @@
         in_mine, in_other = input_back(d_qkv, d_gate_pre, w1, (attn,))
         layer_half, in_half = tree_half(layer_mine, layer_other), tree_half(in_mine, in_other)
         grad_attn = plane_scatter(attn)
+        layer_half, in_half, grad_ffn = lax.optimization_barrier((layer_half, in_half, grad_ffn))
 
         def owners(block):
             block = swapped(block)

time: 368 us -> 367 us (level)
  starting transfers between devices: 55.3 us -> 71.2 us
  blocking collectives: 46.9 us -> 34.8 us
  waiting for transfers between devices: 123 us -> 112 us
  other arithmetic: 14.4 us -> 18.4 us
    ppermute x2 -> x1, waiting for transfers between devices: 27.7 us -> 0.01 us  [swapped(): return jnp.where(native, value, lax.ppermute(value, PLANE, swap_perm))]
    all_to_all x1 -> x0, blocking collectives: 13.3 us -> none  [shards(): lax.all_to_all(jnp.broadcast_to(both_gains[None], (n_shard, 8, HD)), 'sha...]
    all_to_all x3, waiting for transfers between devices: 41.5 us -> 28.4 us  [ctx_exchange(): return lax.all_to_all(value, 'ctx', 0, 0)]
    ppermute x0 -> x1, waiting for transfers between devices: none -> 8.72 us  [shards(): moved = lax.ppermute(second, PLANE, swap_perm)]
    all_to_all x0 -> x1, waiting for transfers between devices: none -> 7.15 us  [shards(): lax.all_to_all(jnp.broadcast_to(both_gains[None], (n_shard, 8, HD)), 'sha...]
    all_to_all x0 -> x1, starting transfers between devices: none -> 7.14 us  [shards(): lax.all_to_all(jnp.broadcast_to(both_gains[None], (n_shard, 8, HD)), 'sha...]
    reduce_scatter x2, waiting for transfers between devices: 0.02 us -> 6.48 us  [plane_scatter(): lax.psum_scatter(value, PLANE, scatter_dimension=0, tiled=True, axis_inde...]
    ppermute x2 -> x1, starting transfers between devices: 8.27 us -> 5.25 us  [swapped(): return jnp.where(native, value, lax.ppermute(value, PLANE, swap_perm))]
  transfers between devices with their start and end apart: 33 -> 34, of which waited for: 22 -> 25; matrix products, arithmetic and copies ran while one was open for 6% -> 8% of each run, Pallas kernels for 15% -> 15%
where the time goes in v11:
time: 367 us; the launch traced here: 365 us
  waiting for transfers between devices  112 us (31%)
  Pallas kernels  79.4 us (22%)
  starting transfers between devices  71.2 us (19%)
  local copies, waits for them, and re-layouts  35.5 us (10%)
  blocking collectives  34.8 us (9%)
  other arithmetic  18.4 us (5%)
  between operations  14.5 us (4%)
    pallas_call x15, Pallas kernels, call(): return lambda *operands: built(*operands, *behind)  61.7 us
    ppermute x6, waiting for transfers between devices, ctx_turn(): lax.ppermute(value, 'ctx', [(i, (i + by) % n_ctx) for i in range(n_ctx)])  36.7 us
    all_to_all x2, blocking collectives, ctx_exchange(): return lax.all_to_all(value, 'ctx', 0, 0)  34.8 us
    all_to_all x3, waiting for transfers between devices, ctx_exchange(): return lax.all_to_all(value, 'ctx', 0, 0)  28.4 us
    unnamed x123, local copies, waits for them, and re-layouts  23.8 us
    ppermute x11, waiting for transfers between devices, core_swap(): return lax.ppermute(value, 'shard', core_perm)  15.2 us
    all_to_all x3, starting transfers between devices, ctx_exchange(): return lax.all_to_all(value, 'ctx', 0, 0)  12.1 us
    ppermute x11, starting transfers between devices, core_swap(): return lax.ppermute(value, 'shard', core_perm)  11.9 us
  transfers between devices with their start and end apart: 34, of which 25 were waited for; matrix products, arithmetic and copies ran while one was open for 8% of the time, Pallas kernels for 15%

profile of v11, /device:TPU:1, one launch (start us, length us, event | category | flops | bytes accessed | tf_op | source)
XLA Modules:
  0.0 365.4 jit_solution(18249707029195216918)
XLA Ops:
  7.3 1.8 shard_map.263
  10.5 1.5 collective-permute-start.1
  12.6 7.1 %all-to-all-start = ((bf16[16,8,128]{2,1,0:T(8,128)(2,1)}), bf16[16,8,128]{2,1,0:T(8,128)(2,1)S(1)}, u32[]{:S(2)}, u32[]{:S(2)}) async-start(bf16[16,8,128]{2,1,0:T(8,128)(2,1)} %broadcast_in_dim.24), calls=%async_computation | async-start | bytes 65536 | tf_op jit(solution)/shard_map/all_to_all | solution.py:840
  19.9 7.2 %all-to-all-done = bf16[16,8,128]{2,1,0:T(8,128)(2,1)S(1)} async-done(((bf16[16,8,128]{2,1,0:T(8,128)(2,1)}), bf16[16,8,128]{2,1,0:T(8,128)(2,1)S(1)}, u32[]{:S(2)}, u32[]{:S(2)}) %all-to-all-start) | async-done | bytes 32800 | tf_op jit(solution)/shard_map/all_to_all | solution.py:840
  27.1 1.6 broadcast_in_dim.25
  28.7 5.0 %all-to-all-start.1 = ((bf16[4,128,2048]{2,1,0:T(8,128)(2,1)}), bf16[4,128,2048]{2,1,0:T(8,128)(2,1)}, u32[]{:S(2)}, u32[]{:S(2)}) async-start(bf16[4,128,2048]{2,1,0:T(8,128)(2,1)} %broadcast_in_dim.25), calls=%async_computation.1 | async-start | bytes 4194304 | tf_op jit(solution)/shard_map/all_to_all | solution.py:778
  35.1 2.9 collective-permute-start
  38.0 8.7 %collective-permute-done = bf16[128,2304]{1,0:T(8,128)(2,1)S(1)} collective-permute-done((bf16[128,2304]{1,0:T(8,128)(2,1)S(1)}, bf16[128,2304]{1,0:T(8,128)(2,1)S(1)}, u32[]{:S(2)}, u32[]{:S(2)}) %collective-permute-start) | collective-permute-done | bytes 589856 | tf_op jit(solution)/shard_map/ppermute | solution.py:858
  46.8 13.0 %all-to-all-done.1.refs_0_.refs_2_.refs_1_ = bf16[4,128,2048]{2,1,0:T(8,128)(2,1)} async-done(((bf16[4,128,2048]{2,1,0:T(8,128)(2,1)}), bf16[4,128,2048]{2,1,0:T(8,128)(2,1)}, u32[]{:S(2)}, u32[]{:S(2)}) %all-to-all-start.1) | async-done | bytes 2097184 | tf_op jit(solution)/shard_map/all_to_all | solution.py:778
  60.7 1.6 collective-permute-start.3
  65.3 1.5 collective-permute-done.2.refs_1_.refs_3_.refs_2_
  68.1 2.4 shard_map.264
  71.0 3.9 %collective-permute-done.4.other = bf16[8,128,1024]{2,1,0:T(8,128)(2,1)} collective-permute-done((bf16[8,128,1024]{2,1,0:T(8,128)(2,1)S(1)}, bf16[8,128,1024]{2,1,0:T(8,128)(2,1)}, u32[]{:S(2)}, u32[]{:S(2)}) %collective-permute-start.4) | collective-permute-done | bytes 2097184 | tf_op jit(solution)/shard_map/ppermute | solution.py:775
  74.9 4.8 %shard_map.265 = bf16[8,2,128,1024]{3,2,1,0:T(8,128)(2,1)} custom-call(s32[1]{0:T(128)} %bitcast.18.core, bf16[8,2,128,1024]{3,2,1,0:T(8,128)(2,1)} %bitcast.90, bf16[8,128,1024]{2,1,0:T(8,128)(2,1)} %collective-permute-done.4.other), custom_call_target="tpu_custom_call" | custom-call | flops 1048576 | bytes 8388608 | tf_op jit(solution)/shard_map/pallas_call | solution.py:635
  79.6 5.5 %shard_map.266 = (bf16[512,2048]{1,0:T(8,128)(2,1)S(1)}, f32[512,384]{1,0:T(8,128)S(1)}, bf16[512,512]{1,0:T(8,128)(2,1)S(1)}, f32[512,256]{1,0:T(8,128)S(1)}) custom-call(bf16[4,128,2048]{2,1,0:T(8,128)(2,1)} %all-to-all-done.1.refs_0_.refs_2_.refs_1_, bf16[4,128,2048]{2,1,0:T(8,128)(2,1)} %copy-done.42, bf16[2048,1024]{1,0:T(8,128)(2,1)} %bitcast.85, ...), custom_call_target="tpu_custom_call" | custom-call | flops 1610612736 | bytes 8388608 | tf_op jit(solution)/shard_map/pallas_call | solution.py:100
  85.1 1.3 copy-done.21
  86.5 6.4 %shard_map.268 = (f32[2,512,512]{2,1,0:T(8,128)}, f32[512,256]{1,0:T(8,128)S(1)}, bf16[512,256]{1,0:T(8,128)(2,1)S(1)}, bf16[256,2048]{1,0:T(8,128)(2,1)S(1)}, bf16[256,2048]{1,0:T(8,128)(2,1)S(1)}) custom-call(bf16[512,512]{1,0:T(8,128)(2,1)S(1)} %get-tuple-element.80.refs_0_.refs_1_, f32[512,256]{1,0:T(8,128)S(1)} %get-tuple-element.81.refs_1_.refs_3_, ...), custom_call_target="tpu_custom_call" | custom-call | flops 805306368 | bytes 8388608 | tf_op jit(solution)/shard_map/pallas_call | solution.py:100
  93.1 2.5 collective-permute-done.5
  95.7 1.4 add_convert_fusion.3
  97.0 3.5 all-to-all-start.2
  101.4 2.2 copy-done.22
  103.7 1.3 shard_map.267.refs_2_.refs_0_
  105.0 10.6 %all-to-all-done.2.refs_0_ = bf16[4,64,2048]{2,1,0:T(8,128)(2,1)S(1)} async-done(((bf16[4,64,2048]{2,1,0:T(8,128)(2,1)}), bf16[4,64,2048]{2,1,0:T(8,128)(2,1)S(1)}, u32[]{:S(2)}, u32[]{:S(2)}) %all-to-all-start.2) | async-done | bytes 1048608 | tf_op jit(solution)/shard_map/all_to_all | solution.py:778
  117.7 16.6 %all_to_all.35 = bf16[4,64,2048]{2,1,0:T(8,128)(2,1)S(1)} all-to-all(bf16[4,64,2048]{2,1,0:T(8,128)(2,1)S(1)} %get-tuple-element.86), channel_id=1, replica_groups=mesh['shard'=16,'ctx'=4,'tp'=2] {'ctx'}, dimensions={0} | all-to-all | bytes 2097152 | tf_op jit(solution)/shard_map/all_to_all | solution.py:778
  134.3 1.9 collective-permute-start.6
  136.2 2.3 collective-permute-done.6
  138.4 1.3 shard_map.270.refs_7_.refs_0_
  143.3 9.9 %shard_map.271 = (bf16[512,768]{1,0:T(8,128)(2,1)}, bf16[512,768]{1,0:T(8,128)(2,1)}, bf16[512,768]{1,0:T(8,128)(2,1)}) custom-call(bf16[256,2048]{1,0:T(8,128)(2,1)} %bitcast.78, bf16[256,2048]{1,0:T(8,128)(2,1)} %bitcast.84, bf16[4,128,2048]{2,1,0:T(8,128)(2,1)} %all-to-all-done.1.refs_0_.refs_2_.refs_1_, bf16[4,128,2048]{2,1,0:T(8,128)(2,1)} %copy-done.42, ...), custom_call_target="tpu_custom_call" | custom-call | flops 4831838208 | bytes 8388608 | tf_op jit(solution)/shard_map/pallas_call | solution.py:100
  153.2 9.9 %shard_map.272.refs_4_ = bf16[2048,2304]{1,0:T(8,128)(2,1)} custom-call(bf16[2048,512]{1,0:T(8,128)(2,1)} %copy-done.2, bf16[4,128,2048]{2,1,0:T(8,128)(2,1)} %all-to-all-done.1.refs_0_.refs_2_.refs_1_, bf16[4,128,2048]{2,1,0:T(8,128)(2,1)} %copy-done.42, bf16[512,768]{1,0:T(8,128)(2,1)} %get-tuple-element.88.refs_3_.refs_0_, ...), custom_call_target="tpu_custom_call" | custom-call | flops 4831838208 | bytes 8388608 | tf_op jit(solution)/shard_map/pallas_call | solution.py:100
  165.4 6.0 %shard_map.273 = (bf16[256,2048]{1,0:T(8,128)(2,1)S(1)}, bf16[256,2048]{1,0:T(8,128)(2,1)S(1)}) custom-call(bf16[512,768]{1,0:T(8,128)(2,1)S(1)} %copy-done.8, bf16[512,768]{1,0:T(8,128)(2,1)S(1)} %copy-done.9, bf16[2048,2304]{1,0:T(8,128)(2,1)} %all-gather.5.cloned.1.call-done.refs_4_.refs_5_.refs_6_.refs_2_.refs_3_.refs_1_, ...), custom_call_target="tpu_custom_call" | custom-call | flops 3221225472 | bytes 8388608 | tf_op jit(solution)/shard_map/pallas_call | solution.py:100
  172.1 2.3 collective-permute-done.7
  174.8 18.2 %all_to_all.36.refs_0_ = bf16[4,64,2048]{2,1,0:T(8,128)(2,1)S(1)} all-to-all(bf16[4,64,2048]{2,1,0:T(8,128)(2,1)S(1)} %bitcast.79), channel_id=1, replica_groups=mesh['shard'=16,'ctx'=4,'tp'=2] {'ctx'}, dimensions={0} | all-to-all | bytes 2097152 | tf_op jit(solution)/shard_map/all_to_all | solution.py:778
  196.2 3.5 all-to-all-start.5
  202.2 5.2 %shard_map.275 = (bf16[256,2048]{1,0:T(8,128)(2,1)S(1)}, bf16[256,2048]{1,0:T(8,128)(2,1)}) custom-call(bf16[512,768]{1,0:T(8,128)(2,1)S(1)} %copy-done.7, bf16[2048,2304]{1,0:T(8,128)(2,1)} %all-gather.5.cloned.1.call-done.refs_4_.refs_5_.refs_6_.refs_2_.refs_3_.refs_1_, bf16[4,64,2048]{2,1,0:T(8,128)(2,1)S(1)} %bitcast.80), custom_call_target="tpu_custom_call" | custom-call | flops 1610612736 | bytes 8388608 | tf_op jit(solution)/shard_map/pallas_call | solution.py:100
  208.3 4.8 %all-to-all-done.5 = bf16[4,64,2048]{2,1,0:T(8,128)(2,1)S(1)} async-done(((bf16[4,64,2048]{2,1,0:T(8,128)(2,1)}), bf16[4,64,2048]{2,1,0:T(8,128)(2,1)S(1)}, u32[]{:S(2)}, u32[]{:S(2)}) %all-to-all-start.5) | async-done | bytes 1048608 | tf_op jit(solution)/shard_map/all_to_all | solution.py:778
  213.1 2.7 collective-permute-start.8
  215.8 2.3 collective-permute-done.8
  220.2 2.2 shard_map.276
  222.6 3.1 shard_map.277
  225.7 4.4 %shard_map.278.refs_3_ = bf16[2048,1024]{1,0:T(8,128)(2,1)} custom-call(bf16[2048,512]{1,0:T(8,128)(2,1)S(1)} %shard_map.267.refs_2_.refs_0_, bf16[256,2048]{1,0:T(8,128)(2,1)S(1)} %bitcast.76, bf16[256,2048]{1,0:T(8,128)(2,1)S(1)} %bitcast.82, bf16[512,512]{1,0:T(8,128)(2,1)S(1)} %get-tuple-element.102.refs_3_.refs_0_, ...), custom_call_target="tpu_custom_call" | custom-call | flops 2147483648 | bytes 8388608 | tf_op jit(solution)/shard_map/pallas_call | solution.py:100
  232.0 5.1 %shard_map.279 = (bf16[256,2048]{1,0:T(8,128)(2,1)S(1)}, bf16[256,2048]{1,0:T(8,128)(2,1)}) custom-call(bf16[512,512]{1,0:T(8,128)(2,1)S(1)} %copy-done.19, bf16[512,256]{1,0:T(8,128)(2,1)S(1)} %copy-done.29, bf16[2048,1024]{1,0:T(8,128)(2,1)} %bitcast.88, bf16[2048,1024]{1,0:T(8,128)(2,1)} %shard_map.278.refs_3_), custom_call_target="tpu_custom_call" | custom-call | flops 1610612736 | bytes 8388608 | tf_op jit(solution)/shard_map/pallas_call | solution.py:100
  237.5 2.6 add_convert_fusion.1
  240.1 2.7 add_convert_fusion
  242.8 6.5 %reduce-scatter.5.cloned.1.call-done = bf16[128,2304]{1,0:T(8,128)(2,1)} async-done(((bf16[2048,2304]{1,0:T(8,128)(2,1)}), bf16[128,2304]{1,0:T(8,128)(2,1)}) %reduce-scatter.5.cloned.1.call-update) | async-done | bytes 589840 | tf_op jit(solution)/shard_map/reduce_scatter | solution.py:797
  252.0 2.6 collective-permute-start.17
  256.0 5.2 %collective-permute-start.11 = (bf16[128,2304]{1,0:T(8,128)(2,1)}, bf16[128,2304]{1,0:T(8,128)(2,1)}, u32[]{:S(2)}, u32[]{:S(2)}) collective-permute-start(bf16[128,2304]{1,0:T(8,128)(2,1)} %reduce-scatter.5.cloned.1.call-done), channel_id=1, source_target_pairs={{8,1},{1,8},{24,17},{17,24},{40,33},{33,40},{56,49},{49,56},{72,65... | collective-permute-start | bytes 1769480 | tf_op jit(solution)/shard_map/ppermute | solution.py:826
  261.3 2.6 collective-permute-done.16.refs_1_
  263.8 12.4 %collective-permute-done.17.refs_2_ = bf16[128,2048]{1,0:T(8,128)(2,1)S(1)} collective-permute-done((bf16[128,2048]{1,0:T(8,128)(2,1)}, bf16[128,2048]{1,0:T(8,128)(2,1)S(1)}, u32[]{:S(2)}, u32[]{:S(2)}) %collective-permute-start.17) | collective-permute-done | bytes 524320 | tf_op jit(solution)/shard_map/ppermute | solution.py:781
  279.5 2.1 collective-permute-start.19
  282.4 6.5 %all-to-all-start.6 = ((bf16[128,8,128]{2,1,0:T(8,128)(2,1)}), bf16[128,8,128]{2,1,0:T(8,128)(2,1)S(1)}, u32[]{:S(2)}, u32[]{:S(2)}) async-start(bf16[128,8,128]{2,1,0:T(8,128)(2,1)} %bitcast.42), calls=%async_computation.8 | async-start | bytes 524288 | tf_op jit(solution)/shard_map/all_to_all | solution.py:933
  293.7 1.6 collective-permute-start.12
  295.2 3.0 collective-permute-start.13
  302.1 7.9 %collective-permute-done.12.b1 = bf16[128,2304]{1,0:T(8,128)(2,1)S(1)} collective-permute-done((bf16[128,2304]{1,0:T(8,128)(2,1)S(1)}, bf16[128,2304]{1,0:T(8,128)(2,1)S(1)}, u32[]{:S(2)}, u32[]{:S(2)}) %collective-permute-start.12) | collective-permute-done | bytes 589856 | tf_op jit(solution)/shard_map/ppermute | solution.py:781
  310.0 12.6 %collective-permute-done.13.b2 = bf16[128,2304]{1,0:T(8,128)(2,1)} collective-permute-done((bf16[128,2304]{1,0:T(8,128)(2,1)S(1)}, bf16[128,2304]{1,0:T(8,128)(2,1)}, u32[]{:S(2)}, u32[]{:S(2)}) %collective-permute-start.13) | collective-permute-done | bytes 589856 | tf_op jit(solution)/shard_map/ppermute | solution.py:781
  323.2 5.6 %shard_map.280 = (f32[128,3072]{1,0:T(8,128)}, f32[128,3072]{1,0:T(8,128)}, f32[3072,128]{1,0:T(8,128)}, f32[128,128]{1,0:T(8,128)}) custom-call(s32[1]{0:T(128)} %bitcast.at.turn_at, bf16[128,2304]{1,0:T(8,128)(2,1)} %copy-done.47, bf16[128,2304]{1,0:T(8,128)(2,1)} %copy-done.49, bf16[128,2304]{1,0:T(8,128)(2,1)} %collective-permute-done.13.b2, ...), custom_call_target="tpu_custom_call" | custom-call | flops 1048576 | bytes 8388608 | tf_op jit(solution)/shard_map/pallas_call | solution.py:700
  329.7 3.6 collective-permute-start.15
  334.8 1.6 select_convert_fusion
  336.5 4.9 %collective-permute-start.21 = (bf16[128,1024]{1,0:T(8,128)(2,1)}, bf16[128,1024]{1,0:T(8,128)(2,1)S(1)}, u32[]{:S(2)}, u32[]{:S(2)}) collective-permute-start(bf16[128,1024]{1,0:T(8,128)(2,1)} %reduce-scatter.3.cloned.1.call-done), channel_id=1, source_target_pairs={{1,8},{3,10},{5,12},{7,14},{8,1},{10,3},{12,5},{14,7},{17,24},{19,... | collective-permute-start | bytes 786440 | tf_op jit(solution)/shard_map/ppermute | solution.py:912
  342.1 3.6 collective-permute-start.23
  346.6 1.5 slice_bitcast_fusion
  348.7 1.9 collective-permute-done.22.b1
  350.6 2.6 collective-permute-done.23.b2
  353.2 1.8 collective-permute-done.24.b3
  355.7 3.1 shard_map.282
  (224 shorter events, 53.2 us)
Async XLA Ops:
  7.2 26.5 %copy-start = (bf16[3072,128]{1,0:T(8,128)(2,1)S(1)}, bf16[3072,128]{1,0:T(8,128)(2,1)}, u32[]{:S(2)}) copy-start(bf16[3072,128]{1,0:T(8,128)(2,1)} %param.30) | copy-start | bytes 2359300
  7.2 59.6 %all-gather.3.cloned.1.call-start = ((), (), s32[]{:S(2)}) async-start(), calls=%async_computation.9 | async-start | bytes 4456448 | tf_op jit(solution)/shard_map/all_gather | solution.py:794
  7.3 4.7 %copy-start.57 = (bf16[8]{0:T(256)(128)(2,1)S(1)}, bf16[8]{0:T(256)(128)(2,1)}, u32[]{:S(2)}) copy-start(bf16[8]{0:T(256)(128)(2,1)} %param.26) | copy-start | bytes 52
  7.3 4.7 %copy-start.58 = (bf16[8]{0:T(256)(128)(2,1)S(1)}, bf16[8]{0:T(256)(128)(2,1)}, u32[]{:S(2)}) copy-start(bf16[8]{0:T(256)(128)(2,1)} %param.25) | copy-start | bytes 52
  9.1 10.6 %copy-start.59 = (bf16[128]{0:T(256)(128)(2,1)S(1)}, bf16[128]{0:T(256)(128)(2,1)}, u32[]{:S(2)}) copy-start(bf16[128]{0:T(256)(128)(2,1)} %param.27) | copy-start | bytes 772
  10.5 9.3 %collective-permute-start.1 = (bf16[128,2048]{1,0:T(8,128)(2,1)S(1)}, bf16[128,2048]{1,0:T(8,128)(2,1)S(1)}, u32[]{:S(2)}, u32[]{:S(2)}) collective-permute-start(bf16[128,2048]{1,0:T(8,128)(2,1)S(1)} %pad_maximum_fusion.2), channel_id=1, source_target_pairs={{0,8},{8,0},{16,24},{24,16},{32,40},{40,32},{48,56},{56,48},{64,72... | collective-permute-start | bytes 1572872 | tf_op jit(solution)/shard_map/ppermute | solution.py:775
  12.6 14.5 %all-to-all-start = ((bf16[16,8,128]{2,1,0:T(8,128)(2,1)}), bf16[16,8,128]{2,1,0:T(8,128)(2,1)S(1)}, u32[]{:S(2)}, u32[]{:S(2)}) async-start(bf16[16,8,128]{2,1,0:T(8,128)(2,1)} %broadcast_in_dim.24), calls=%async_computation | async-start | bytes 65536 | tf_op jit(solution)/shard_map/all_to_all | solution.py:840
  19.9 8.7 %copy-start.43 = (bf16[128,2048]{1,0:T(8,128)(2,1)}, bf16[128,2048]{1,0:T(8,128)(2,1)S(1)}, u32[]{:S(2)}) copy-start(bf16[128,2048]{1,0:T(8,128)(2,1)S(1)} %maximum_select_fusion) | copy-start | bytes 1572868
  28.7 31.1 %all-to-all-start.1 = ((bf16[4,128,2048]{2,1,0:T(8,128)(2,1)}), bf16[4,128,2048]{2,1,0:T(8,128)(2,1)}, u32[]{:S(2)}, u32[]{:S(2)}) async-start(bf16[4,128,2048]{2,1,0:T(8,128)(2,1)} %broadcast_in_dim.25), calls=%async_computation.1 | async-start | bytes 4194304 | tf_op jit(solution)/shard_map/all_to_all | solution.py:778
  33.7 109.6 %all-gather.5.cloned.1.call-start = ((), (), s32[]{:S(2)}) async-start(), calls=%async_computation.10 | async-start | bytes 10027008 | tf_op jit(solution)/shard_map/all_gather | solution.py:794
  34.9 25.8 %copy-start.54 = (s32[1,13]{1,0:T(1,128)S(1)}, s32[1,13]{1,0:T(1,128)}, u32[]{:S(2)}) copy-start(s32[1,13]{1,0:T(1,128)} %param.18) | copy-start | bytes 160
  34.9 25.8 %copy-start.55 = (s32[1,13]{1,0:T(1,128)S(1)}, s32[1,13]{1,0:T(1,128)}, u32[]{:S(2)}) copy-start(s32[1,13]{1,0:T(1,128)} %param.17) | copy-start | bytes 160
  35.1 11.6 %collective-permute-start = (bf16[128,2304]{1,0:T(8,128)(2,1)S(1)}, bf16[128,2304]{1,0:T(8,128)(2,1)S(1)}, u32[]{:S(2)}, u32[]{:S(2)}) collective-permute-start(bf16[128,2304]{1,0:T(8,128)(2,1)S(1)} %pad_maximum_fusion.1), channel_id=1, source_target_pairs={{8,1},{1,8},{24,17},{17,24},{40,33},{33,40},{56,49},{49,56},{72,65... | collective-permute-start | bytes 1769480 | tf_op jit(solution)/shard_map/ppermute | solution.py:858
  60.7 2.4 collective-permute-start.3
  62.4 4.4 %collective-permute-start.2 = (bf16[4,128,2048]{2,1,0:T(8,128)(2,1)}, bf16[4,128,2048]{2,1,0:T(8,128)(2,1)S(1)}, u32[]{:S(2)}, u32[]{:S(2)}) collective-permute-start(bf16[4,128,2048]{2,1,0:T(8,128)(2,1)} %all-to-all-done.1.refs_0_.refs_2_.refs_1_), channel_id=1, source_target_pairs={{0,8},{8,0},{16,24},{24,16},{32,40},{40,32},{48,56},{56,48},{64,72... | collective-permute-start | bytes 6291464 | tf_op jit(solution)/shard_map/ppermute | solution.py:775
  65.2 14.4 %copy-start.10 = (f32[512,128]{1,0:T(8,128)}, f32[512,128]{1,0:T(8,128)S(1)}, u32[]{:S(2)}) copy-start(f32[512,128]{1,0:T(8,128)S(1)} %get-tuple-element.77.refs_4_.refs_5_) | copy-start | bytes 786436
  70.5 4.4 %collective-permute-start.4 = (bf16[8,128,1024]{2,1,0:T(8,128)(2,1)S(1)}, bf16[8,128,1024]{2,1,0:T(8,128)(2,1)}, u32[]{:S(2)}, u32[]{:S(2)}) collective-permute-start(bf16[8,128,1024]{2,1,0:T(8,128)(2,1)S(1)} %shard_map.264), channel_id=1, source_target_pairs={{0,8},{8,0},{16,24},{24,16},{32,40},{40,32},{48,56},{56,48},{64,72... | collective-permute-start | bytes 6291464 | tf_op jit(solution)/shard_map/ppermute | solution.py:775
  86.5 6.4 %copy-start.14 = (f32[512,256]{1,0:T(8,128)}, f32[512,256]{1,0:T(8,128)S(1)}, u32[]{:S(2)}) copy-start(f32[512,256]{1,0:T(8,128)S(1)} %get-tuple-element.81.refs_1_.refs_3_) | copy-start | bytes 1572868
  86.5 6.4 %copy-start.16 = (bf16[512,512]{1,0:T(8,128)(2,1)}, bf16[512,512]{1,0:T(8,128)(2,1)S(1)}, u32[]{:S(2)}) copy-start(bf16[512,512]{1,0:T(8,128)(2,1)S(1)} %get-tuple-element.80.refs_0_.refs_1_) | copy-start | bytes 1572868
  86.5 6.4 %copy-start.32 = (f32[512,384]{1,0:T(8,128)}, f32[512,384]{1,0:T(8,128)S(1)}, u32[]{:S(2)}) copy-start(f32[512,384]{1,0:T(8,128)S(1)} %get-tuple-element.101.refs_3_) | copy-start | bytes 2359300
  92.9 4.1 %copy-start.34 = (f32[512,256]{1,0:T(8,128)}, f32[512,256]{1,0:T(8,128)S(1)}, u32[]{:S(2)}) copy-start(f32[512,256]{1,0:T(8,128)S(1)} %get-tuple-element.99.refs_4_) | copy-start | bytes 1572868
  92.9 4.1 %copy-start.40 = (bf16[512,256]{1,0:T(8,128)(2,1)}, bf16[512,256]{1,0:T(8,128)(2,1)S(1)}, u32[]{:S(2)}) copy-start(bf16[512,256]{1,0:T(8,128)(2,1)S(1)} %get-tuple-element.104.refs_5_) | copy-start | bytes 786436
  92.9 2.7 collective-permute-start.5
  95.7 4.9 %copy-start.44 = (bf16[128,2048]{1,0:T(8,128)(2,1)S(1)}, bf16[128,2048]{1,0:T(8,128)(2,1)}, u32[]{:S(2)}) copy-start(bf16[128,2048]{1,0:T(8,128)(2,1)} %copy-done.43) | copy-start | bytes 1572868
  97.0 18.6 %all-to-all-start.2 = ((bf16[4,64,2048]{2,1,0:T(8,128)(2,1)}), bf16[4,64,2048]{2,1,0:T(8,128)(2,1)S(1)}, u32[]{:S(2)}, u32[]{:S(2)}) async-start(bf16[4,64,2048]{2,1,0:T(8,128)(2,1)} %bitcast.22), calls=%async_computation.2 | async-start | bytes 2097152 | tf_op jit(solution)/shard_map/all_to_all | solution.py:778
  100.6 148.7 %reduce-scatter.5.cloned.1.call-start = ((), (), s32[]{:S(2)}) async-start(), calls=%async_computation.12 | async-start | bytes 10027008 | tf_op jit(solution)/shard_map/reduce_scatter | solution.py:797
  134.3 5.5 %copy-start.3 = (bf16[4,64,2048]{2,1,0:T(8,128)(2,1)}, bf16[4,64,2048]{2,1,0:T(8,128)(2,1)S(1)}, u32[]{:S(2)}) copy-start(bf16[4,64,2048]{2,1,0:T(8,128)(2,1)S(1)} %all_to_all.35) | copy-start | bytes 3145732
  134.3 4.2 %collective-permute-start.6 = (bf16[4,64,2048]{2,1,0:T(8,128)(2,1)S(1)}, bf16[4,64,2048]{2,1,0:T(8,128)(2,1)S(1)}, u32[]{:S(2)}, u32[]{:S(2)}) collective-permute-start(bf16[4,64,2048]{2,1,0:T(8,128)(2,1)S(1)} %all_to_all.35), channel_id=1, source_target_pairs={{0,8},{8,0},{16,24},{24,16},{32,40},{40,32},{48,56},{56,48},{64,72... | collective-permute-start | bytes 3145736 | tf_op jit(solution)/shard_map/ppermute | solution.py:775
  171.3 3.0 collective-permute-start.7
  174.4 19.6 %copy-start.24 = (f32[64,2048]{1,0:T(8,128)S(1)}, f32[64,2048]{1,0:T(8,128)}, u32[]{:S(2)}) copy-start(f32[64,2048]{1,0:T(8,128)} %copy-done.23) | copy-start | bytes 1572868
  174.4 19.6 %copy-start.31 = (bf16[64,2048]{1,0:T(8,128)(2,1)S(1)}, bf16[64,2048]{1,0:T(8,128)(2,1)}, u32[]{:S(2)}) copy-start(bf16[64,2048]{1,0:T(8,128)(2,1)} %get-tuple-element.146.refs_2_) | copy-start | bytes 786436
  196.2 16.9 %all-to-all-start.5 = ((bf16[4,64,2048]{2,1,0:T(8,128)(2,1)}), bf16[4,64,2048]{2,1,0:T(8,128)(2,1)S(1)}, u32[]{:S(2)}, u32[]{:S(2)}) async-start(bf16[4,64,2048]{2,1,0:T(8,128)(2,1)} %copy-done.30), calls=%async_computation.5 | async-start | bytes 2097152 | tf_op jit(solution)/shard_map/all_to_all | solution.py:778
  199.8 136.7 %reduce-scatter.3.cloned.1.call-start = ((), (), s32[]{:S(2)}) async-start(), calls=%async_computation.11 | async-start | bytes 4456448 | tf_op jit(solution)/shard_map/reduce_scatter | solution.py:797
  213.1 5.0 %collective-permute-start.8 = (bf16[4,64,2048]{2,1,0:T(8,128)(2,1)S(1)}, bf16[4,64,2048]{2,1,0:T(8,128)(2,1)S(1)}, u32[]{:S(2)}, u32[]{:S(2)}) collective-permute-start(bf16[4,64,2048]{2,1,0:T(8,128)(2,1)S(1)} %all-to-all-done.5), channel_id=1, source_target_pairs={{0,8},{8,0},{16,24},{24,16},{32,40},{40,32},{48,56},{56,48},{64,72... | collective-permute-start | bytes 3145736 | tf_op jit(solution)/shard_map/ppermute | solution.py:775
  230.9 6.6 %copy-start.27 = (bf16[256,2048]{1,0:T(8,128)(2,1)S(1)}, bf16[256,2048]{1,0:T(8,128)(2,1)}, u32[]{:S(2)}) copy-start(bf16[256,2048]{1,0:T(8,128)(2,1)} %copy-done.26) | copy-start | bytes 3145732
  230.9 6.6 %collective-permute-start.9 = (bf16[256,2048]{1,0:T(8,128)(2,1)}, bf16[256,2048]{1,0:T(8,128)(2,1)}, u32[]{:S(2)}, u32[]{:S(2)}) collective-permute-start(bf16[256,2048]{1,0:T(8,128)(2,1)} %get-tuple-element.106), channel_id=1, source_target_pairs={{0,8},{8,0},{16,24},{24,16},{32,40},{40,32},{48,56},{56,48},{64,72... | collective-permute-start | bytes 3145736 | tf_op jit(solution)/shard_map/ppermute | solution.py:775
  237.1 3.1 collective-permute-start.10
  240.1 9.2 %copy-start.45 = (bf16[256,2048]{1,0:T(8,128)(2,1)S(1)}, bf16[256,2048]{1,0:T(8,128)(2,1)}, u32[]{:S(2)}) copy-start(bf16[256,2048]{1,0:T(8,128)(2,1)} %add_convert_fusion.1) | copy-start | bytes 3145732
  242.8 6.6 %copy-start.46 = (bf16[256,2048]{1,0:T(8,128)(2,1)S(1)}, bf16[256,2048]{1,0:T(8,128)(2,1)}, u32[]{:S(2)}) copy-start(bf16[256,2048]{1,0:T(8,128)(2,1)} %add_convert_fusion) | copy-start | bytes 3145732
  249.5 28.2 %copy-start.13 = (bf16[64,2048]{1,0:T(8,128)(2,1)S(1)}, bf16[64,2048]{1,0:T(8,128)(2,1)}, u32[]{:S(2)}) copy-start(bf16[64,2048]{1,0:T(8,128)(2,1)} %get-tuple-element.147.refs_1_.refs_6_) | copy-start | bytes 786436
  249.5 28.2 %copy-start.25 = (f32[64,2048]{1,0:T(8,128)S(1)}, f32[64,2048]{1,0:T(8,128)}, u32[]{:S(2)}) copy-start(f32[64,2048]{1,0:T(8,128)} %copy-done.23) | copy-start | bytes 1572868
  249.6 28.2 %copy-start.37 = (f32[64,2048]{1,0:T(8,128)S(1)}, f32[64,2048]{1,0:T(8,128)}, u32[]{:S(2)}) copy-start(f32[64,2048]{1,0:T(8,128)} %copy-done.36) | copy-start | bytes 1572868
  250.8 13.1 %collective-permute-start.16 = (bf16[128,2048]{1,0:T(8,128)(2,1)}, bf16[128,2048]{1,0:T(8,128)(2,1)S(1)}, u32[]{:S(2)}, u32[]{:S(2)}) collective-permute-start(bf16[128,2048]{1,0:T(8,128)(2,1)} %get-tuple-element.140), channel_id=1, source_target_pairs={{0,2},{2,4},{4,6},{6,0},{1,3},{3,5},{5,7},{7,1},{8,10},{10,12},{12... | collective-permute-start | bytes 1572872 | tf_op jit(solution)/shard_map/ppermute | solution.py:781
  252.0 24.2 %collective-permute-start.17 = (bf16[128,2048]{1,0:T(8,128)(2,1)}, bf16[128,2048]{1,0:T(8,128)(2,1)S(1)}, u32[]{:S(2)}, u32[]{:S(2)}) collective-permute-start(bf16[128,2048]{1,0:T(8,128)(2,1)} %get-tuple-element.139), channel_id=1, source_target_pairs={{0,4},{2,6},{4,0},{6,2},{1,5},{3,7},{5,1},{7,3},{8,12},{10,14},{12... | collective-permute-start | bytes 1572872 | tf_op jit(solution)/shard_map/ppermute | solution.py:781
  254.6 22.3 %collective-permute-start.18 = (bf16[128,2048]{1,0:T(8,128)(2,1)}, bf16[128,2048]{1,0:T(8,128)(2,1)S(1)}, u32[]{:S(2)}, u32[]{:S(2)}) collective-permute-start(bf16[128,2048]{1,0:T(8,128)(2,1)} %get-tuple-element.138), channel_id=1, source_target_pairs={{0,6},{2,0},{4,2},{6,4},{1,7},{3,1},{5,3},{7,5},{8,14},{10,8},{12,... | collective-permute-start | bytes 1572872 | tf_op jit(solution)/shard_map/ppermute | solution.py:781
  256.0 36.5 %collective-permute-start.11 = (bf16[128,2304]{1,0:T(8,128)(2,1)}, bf16[128,2304]{1,0:T(8,128)(2,1)}, u32[]{:S(2)}, u32[]{:S(2)}) collective-permute-start(bf16[128,2304]{1,0:T(8,128)(2,1)} %reduce-scatter.5.cloned.1.call-done), channel_id=1, source_target_pairs={{8,1},{1,8},{24,17},{17,24},{40,33},{33,40},{56,49},{49,56},{72,65... | collective-permute-start | bytes 1769480 | tf_op jit(solution)/shard_map/ppermute | solution.py:826
  279.5 9.5 %collective-permute-start.19 = (bf16[128,2048]{1,0:T(8,128)(2,1)S(1)}, bf16[128,2048]{1,0:T(8,128)(2,1)S(1)}, u32[]{:S(2)}, u32[]{:S(2)}) collective-permute-start(bf16[128,2048]{1,0:T(8,128)(2,1)S(1)} %get-tuple-element.114), channel_id=1, source_target_pairs={{0,8},{8,0},{16,24},{24,16},{32,40},{40,32},{48,56},{56,48},{64,72... | collective-permute-start | bytes 1572872 | tf_op jit(solution)/shard_map/ppermute | solution.py:775
  282.4 19.0 %all-to-all-start.6 = ((bf16[128,8,128]{2,1,0:T(8,128)(2,1)}), bf16[128,8,128]{2,1,0:T(8,128)(2,1)S(1)}, u32[]{:S(2)}, u32[]{:S(2)}) async-start(bf16[128,8,128]{2,1,0:T(8,128)(2,1)} %bitcast.42), calls=%async_computation.8 | async-start | bytes 524288 | tf_op jit(solution)/shard_map/all_to_all | solution.py:933
  289.0 3.5 copy-start.48
  290.0 9.8 %copy-start.56 = (bf16[128]{0:T(256)(128)(2,1)S(1)}, bf16[128]{0:T(256)(128)(2,1)}, u32[]{:S(2)}) copy-start(bf16[128]{0:T(256)(128)(2,1)} %param.19) | copy-start | bytes 772
  291.2 43.6 %collective-permute-start.20 = (bf16[2,128,2048]{2,1,0:T(8,128)(2,1)S(1)}, bf16[2,128,2048]{2,1,0:T(8,128)(2,1)}, u32[]{:S(2)}, u32[]{:S(2)}) collective-permute-start(bf16[2,128,2048]{2,1,0:T(8,128)(2,1)S(1)} %pad_maximum_fusion), channel_id=1, source_target_pairs={{0,1},{9,8},{16,17},{25,24},{32,33},{41,40},{48,49},{57,56},{64,65... | collective-permute-start | bytes 3145736 | tf_op jit(solution)/shard_map/ppermute | solution.py:963
  293.7 29.6 %copy-start.47 = (bf16[128,2304]{1,0:T(8,128)(2,1)}, bf16[128,2304]{1,0:T(8,128)(2,1)S(1)}, u32[]{:S(2)}) copy-start(bf16[128,2304]{1,0:T(8,128)(2,1)S(1)} %broadcast_select_fusion.b0) | copy-start | bytes 1769476
  293.7 16.4 %collective-permute-start.12 = (bf16[128,2304]{1,0:T(8,128)(2,1)S(1)}, bf16[128,2304]{1,0:T(8,128)(2,1)S(1)}, u32[]{:S(2)}, u32[]{:S(2)}) collective-permute-start(bf16[128,2304]{1,0:T(8,128)(2,1)S(1)} %broadcast_select_fusion.b0), channel_id=1, source_target_pairs={{0,2},{2,4},{4,6},{6,0},{1,3},{3,5},{5,7},{7,1},{8,10},{10,12},{12... | collective-permute-start | bytes 1769480 | tf_op jit(solution)/shard_map/ppermute | solution.py:781
  295.2 27.4 %collective-permute-start.13 = (bf16[128,2304]{1,0:T(8,128)(2,1)S(1)}, bf16[128,2304]{1,0:T(8,128)(2,1)}, u32[]{:S(2)}, u32[]{:S(2)}) collective-permute-start(bf16[128,2304]{1,0:T(8,128)(2,1)S(1)} %broadcast_select_fusion.b0), channel_id=1, source_target_pairs={{0,4},{2,6},{4,0},{6,2},{1,5},{3,7},{5,1},{7,3},{8,12},{10,14},{12... | collective-permute-start | bytes 1769480 | tf_op jit(solution)/shard_map/ppermute | solution.py:781
  298.2 25.0 %collective-permute-start.14 = (bf16[128,2304]{1,0:T(8,128)(2,1)S(1)}, bf16[128,2304]{1,0:T(8,128)(2,1)}, u32[]{:S(2)}, u32[]{:S(2)}) collective-permute-start(bf16[128,2304]{1,0:T(8,128)(2,1)S(1)} %broadcast_select_fusion.b0), channel_id=1, source_target_pairs={{0,6},{2,0},{4,2},{6,4},{1,7},{3,1},{5,3},{7,5},{8,14},{10,8},{12,... | collective-permute-start | bytes 1769480 | tf_op jit(solution)/shard_map/ppermute | solution.py:781
  310.0 13.2 %copy-start.49 = (bf16[128,2304]{1,0:T(8,128)(2,1)}, bf16[128,2304]{1,0:T(8,128)(2,1)S(1)}, u32[]{:S(2)}) copy-start(bf16[128,2304]{1,0:T(8,128)(2,1)S(1)} %collective-permute-done.12.b1) | copy-start | bytes 1769476
  329.7 4.6 %collective-permute-start.15 = (f32[128]{0:T(128)S(1)}, f32[128]{0:T(128)S(1)}, u32[]{:S(2)}, u32[]{:S(2)}) collective-permute-start(f32[128]{0:T(128)S(1)} %reduce_sum.104), channel_id=1, source_target_pairs={{0,1},{1,0},{2,3},{3,2},{4,5},{5,4},{6,7},{7,6},{8,9},{9,8},{10,11... | collective-permute-start | bytes 1544 | tf_op jit(solution)/shard_map/ppermute | solution.py:962
  334.8 24.0 %copy-start.1 = (bf16[3072,128]{1,0:T(8,128)(2,1)S(1)}, bf16[3072,128]{1,0:T(8,128)(2,1)}, u32[]{:S(2)}) copy-start(bf16[3072,128]{1,0:T(8,128)(2,1)} %param.30) | copy-start | bytes 2359300
  336.5 11.6 %copy-start.50 = (bf16[128,1024]{1,0:T(8,128)(2,1)S(1)}, bf16[128,1024]{1,0:T(8,128)(2,1)}, u32[]{:S(2)}) copy-start(bf16[128,1024]{1,0:T(8,128)(2,1)} %reduce-scatter.3.cloned.1.call-done) | copy-start | bytes 786436
  336.5 11.6 %collective-permute-start.21 = (bf16[128,1024]{1,0:T(8,128)(2,1)}, bf16[128,1024]{1,0:T(8,128)(2,1)S(1)}, u32[]{:S(2)}, u32[]{:S(2)}) collective-permute-start(bf16[128,1024]{1,0:T(8,128)(2,1)} %reduce-scatter.3.cloned.1.call-done), channel_id=1, source_target_pairs={{1,8},{3,10},{5,12},{7,14},{8,1},{10,3},{12,5},{14,7},{17,24},{19,... | collective-permute-start | bytes 786440 | tf_op jit(solution)/shard_map/ppermute | solution.py:912
  341.4 9.2 %collective-permute-start.22 = (bf16[128,1024]{1,0:T(8,128)(2,1)}, bf16[128,1024]{1,0:T(8,128)(2,1)S(1)}, u32[]{:S(2)}, u32[]{:S(2)}) collective-permute-start(bf16[128,1024]{1,0:T(8,128)(2,1)} %reduce-scatter.3.cloned.1.call-done), channel_id=1, source_target_pairs={{0,2},{1,10},{2,4},{3,12},{4,6},{5,14},{6,0},{7,8},{8,3},{9,11},{1... | collective-permute-start | bytes 786440 | tf_op jit(solution)/shard_map/ppermute | solution.py:912
  342.1 11.1 %collective-permute-start.23 = (bf16[128,1024]{1,0:T(8,128)(2,1)}, bf16[128,1024]{1,0:T(8,128)(2,1)S(1)}, u32[]{:S(2)}, u32[]{:S(2)}) collective-permute-start(bf16[128,1024]{1,0:T(8,128)(2,1)} %reduce-scatter.3.cloned.1.call-done), channel_id=1, source_target_pairs={{0,4},{1,12},{2,6},{3,14},{4,0},{5,8},{6,2},{7,10},{8,5},{9,13},{1... | collective-permute-start | bytes 786440 | tf_op jit(solution)/shard_map/ppermute | solution.py:912
  345.7 9.4 %collective-permute-start.24 = (bf16[128,1024]{1,0:T(8,128)(2,1)}, bf16[128,1024]{1,0:T(8,128)(2,1)S(1)}, u32[]{:S(2)}, u32[]{:S(2)}) collective-permute-start(bf16[128,1024]{1,0:T(8,128)(2,1)} %reduce-scatter.3.cloned.1.call-done), channel_id=1, source_target_pairs={{0,6},{1,14},{2,0},{3,8},{4,2},{5,10},{6,4},{7,12},{8,7},{9,15},{1... | collective-permute-start | bytes 786440 | tf_op jit(solution)/shard_map/ppermute | solution.py:912
  350.6 4.4 %copy-start.51 = (bf16[128,1024]{1,0:T(8,128)(2,1)}, bf16[128,1024]{1,0:T(8,128)(2,1)S(1)}, u32[]{:S(2)}) copy-start(bf16[128,1024]{1,0:T(8,128)(2,1)S(1)} %collective-permute-done.22.b1) | copy-start | bytes 786436
  (30 other events, 42.2 us)
Sparse Core Ops, SparseCore 0:
  10.7 54.5 all-gather.2
  68.1 75.1 all-gather.4
  163.2 86.0 reduce-scatter.4
  252.9 77.8 reduce-scatter.2

commit v12 on v11

--- a/solution.py
+++ b/solution.py
@@ -583,7 +583,7 @@
     terms[...] = jnp.broadcast_to(found, terms.shape)
 
 
-def ends_step(parts, middle, d_middle, x):
+def ends_step(parts, middle, d_middle, x, behind):
     shape, wide = x.shape, parts[0].shape
     count = len(parts)
     return call(
@@ -593,6 +593,7 @@
         [fixed(wide), fixed((8, shape[1]))],
         [struct(wide, BF16), struct((8, shape[1]), F32)],
         1 << 20,
+        behind=behind,
     )(*parts, middle, d_middle, x)
 
 
@@ -920,7 +921,9 @@
             ctx_turn(lax.dynamic_index_in_dim(both, (ctx + by) % n_ctx, 0, False), by)
             for by in range(1, n_ctx)
         ]
-        ends, in_terms = ends_step(parts, middle, d_middle, own_x)
+        ffn_blocks = owners(grad_ffn)
+        ends, in_terms = ends_step(parts, middle, d_middle, own_x, (ffn_blocks[0],))
+        ends, in_terms, ffn_blocks[1] = lax.optimization_barrier((ends, in_terms, ffn_blocks[1]))
         pieces = jnp.concatenate(
             [terms[0].reshape(n_shard, -1), terms[1].reshape(n_shard, -1)], axis=1
         )
@@ -934,7 +937,6 @@
             pieces.reshape(n_shard * copies, 8, HD), ("shard", "ctx", "tp"), 0, 0
         )
         end_sums = jnp.sum(pieces.astype(F32), axis=0)
-        ffn_blocks = owners(grad_ffn)
         sibling = core_swap(ends)
 
         def whole(start):

time: 367 us -> 364 us (level)
  waiting for transfers between devices: 112 us -> 127 us
  starting transfers between devices: 71.2 us -> 60.7 us
  other arithmetic: 18.4 us -> 10.9 us
    ppermute x1, waiting for transfers between devices: 0.01 us -> 7.89 us  [swapped(): return jnp.where(native, value, lax.ppermute(value, PLANE, swap_perm))]
    convert_element_type x4, other arithmetic: 7.02 us -> 2.52 us  [tree_half(): half = (mine.astype(F32) + core_swap(other).astype(F32)).astype(BF16)]
    unnamed x123 -> x119, local copies, waits for them, and re-layouts: 23.8 us -> 23.5 us
  transfers between devices with their start and end apart: 34 -> 34, of which waited for: 25 -> 25; matrix products, arithmetic and copies ran while one was open for 8% -> 6% of each run, Pallas kernels for 15% -> 15%
where the time goes in v12:
time: 364 us; the launch traced here: 361 us
  waiting for transfers between devices  127 us (35%)
  Pallas kernels  78.6 us (22%)
  starting transfers between devices  60.7 us (17%)
  local copies, waits for them, and re-layouts  35.3 us (10%)
  blocking collectives  34.8 us (10%)
  between operations  14.6 us (4%)
  other arithmetic  10.9 us (3%)
    pallas_call x15, Pallas kernels, call(): return lambda *operands: built(*operands, *behind)  61 us
    ppermute x6, waiting for transfers between devices, ctx_turn(): lax.ppermute(value, 'ctx', [(i, (i + by) % n_ctx) for i in range(n_ctx)])  35.5 us
    all_to_all x2, blocking collectives, ctx_exchange(): return lax.all_to_all(value, 'ctx', 0, 0)  34.8 us
    all_to_all x3, waiting for transfers between devices, ctx_exchange(): return lax.all_to_all(value, 'ctx', 0, 0)  28.3 us
    unnamed x119, local copies, waits for them, and re-layouts  23.5 us
    ppermute x11, waiting for transfers between devices, core_swap(): return lax.ppermute(value, 'shard', core_perm)  18.4 us
    all_to_all x3, starting transfers between devices, ctx_exchange(): return lax.all_to_all(value, 'ctx', 0, 0)  12.1 us
    ppermute x11, starting transfers between devices, core_swap(): return lax.ppermute(value, 'shard', core_perm)  9.79 us
  transfers between devices with their start and end apart: 34, of which 25 were waited for; matrix products, arithmetic and copies ran while one was open for 6% of the time, Pallas kernels for 15%

profile of v12, /device:TPU:1, one launch (start us, length us, event | category | flops | bytes accessed | tf_op | source)
XLA Modules:
  0.0 361.5 jit_solution(11612579246833976973)
XLA Ops:
  7.3 1.8 shard_map.263
  10.5 1.5 collective-permute-start.1
  12.6 7.1 %all-to-all-start = ((bf16[16,8,128]{2,1,0:T(8,128)(2,1)}), bf16[16,8,128]{2,1,0:T(8,128)(2,1)S(1)}, u32[]{:S(2)}, u32[]{:S(2)}) async-start(bf16[16,8,128]{2,1,0:T(8,128)(2,1)} %broadcast_in_dim.24), calls=%async_computation | async-start | bytes 65536 | tf_op jit(solution)/shard_map/all_to_all | solution.py:841
  19.9 7.2 %all-to-all-done = bf16[16,8,128]{2,1,0:T(8,128)(2,1)S(1)} async-done(((bf16[16,8,128]{2,1,0:T(8,128)(2,1)}), bf16[16,8,128]{2,1,0:T(8,128)(2,1)S(1)}, u32[]{:S(2)}, u32[]{:S(2)}) %all-to-all-start) | async-done | bytes 32800 | tf_op jit(solution)/shard_map/all_to_all | solution.py:841
  27.1 1.6 broadcast_in_dim.25
  28.7 5.0 %all-to-all-start.1 = ((bf16[4,128,2048]{2,1,0:T(8,128)(2,1)}), bf16[4,128,2048]{2,1,0:T(8,128)(2,1)}, u32[]{:S(2)}, u32[]{:S(2)}) async-start(bf16[4,128,2048]{2,1,0:T(8,128)(2,1)} %broadcast_in_dim.25), calls=%async_computation.1 | async-start | bytes 4194304 | tf_op jit(solution)/shard_map/all_to_all | solution.py:779
  35.2 2.9 collective-permute-start
  38.0 8.7 %collective-permute-done = bf16[128,2304]{1,0:T(8,128)(2,1)S(1)} collective-permute-done((bf16[128,2304]{1,0:T(8,128)(2,1)S(1)}, bf16[128,2304]{1,0:T(8,128)(2,1)S(1)}, u32[]{:S(2)}, u32[]{:S(2)}) %collective-permute-start) | collective-permute-done | bytes 589856 | tf_op jit(solution)/shard_map/ppermute | solution.py:859
  46.8 13.0 %all-to-all-done.1.refs_0_.refs_2_.refs_1_ = bf16[4,128,2048]{2,1,0:T(8,128)(2,1)} async-done(((bf16[4,128,2048]{2,1,0:T(8,128)(2,1)}), bf16[4,128,2048]{2,1,0:T(8,128)(2,1)}, u32[]{:S(2)}, u32[]{:S(2)}) %all-to-all-start.1) | async-done | bytes 2097184 | tf_op jit(solution)/shard_map/all_to_all | solution.py:779
  60.7 1.6 collective-permute-start.3
  65.3 1.5 collective-permute-done.2.refs_1_.refs_3_.refs_2_
  68.1 2.4 shard_map.264
  71.0 3.9 %collective-permute-done.4.other = bf16[8,128,1024]{2,1,0:T(8,128)(2,1)} collective-permute-done((bf16[8,128,1024]{2,1,0:T(8,128)(2,1)S(1)}, bf16[8,128,1024]{2,1,0:T(8,128)(2,1)}, u32[]{:S(2)}, u32[]{:S(2)}) %collective-permute-start.4) | collective-permute-done | bytes 2097184 | tf_op jit(solution)/shard_map/ppermute | solution.py:776
  74.9 4.8 %shard_map.265 = bf16[8,2,128,1024]{3,2,1,0:T(8,128)(2,1)} custom-call(s32[1]{0:T(128)} %bitcast.18.core, bf16[8,2,128,1024]{3,2,1,0:T(8,128)(2,1)} %bitcast.90, bf16[8,128,1024]{2,1,0:T(8,128)(2,1)} %collective-permute-done.4.other), custom_call_target="tpu_custom_call" | custom-call | flops 1048576 | bytes 8388608 | tf_op jit(solution)/shard_map/pallas_call | solution.py:636
  79.7 5.5 %shard_map.266 = (bf16[512,2048]{1,0:T(8,128)(2,1)S(1)}, f32[512,384]{1,0:T(8,128)S(1)}, bf16[512,512]{1,0:T(8,128)(2,1)S(1)}, f32[512,256]{1,0:T(8,128)S(1)}) custom-call(bf16[4,128,2048]{2,1,0:T(8,128)(2,1)} %all-to-all-done.1.refs_0_.refs_2_.refs_1_, bf16[4,128,2048]{2,1,0:T(8,128)(2,1)} %copy-done.43, bf16[2048,1024]{1,0:T(8,128)(2,1)} %bitcast.85, ...), custom_call_target="tpu_custom_call" | custom-call | flops 1610612736 | bytes 8388608 | tf_op jit(solution)/shard_map/pallas_call | solution.py:100
  86.5 6.4 %shard_map.268 = (f32[2,512,512]{2,1,0:T(8,128)}, f32[512,256]{1,0:T(8,128)S(1)}, bf16[512,256]{1,0:T(8,128)(2,1)S(1)}, bf16[256,2048]{1,0:T(8,128)(2,1)S(1)}, bf16[256,2048]{1,0:T(8,128)(2,1)S(1)}) custom-call(bf16[512,512]{1,0:T(8,128)(2,1)S(1)} %get-tuple-element.83.refs_0_.refs_1_, f32[512,256]{1,0:T(8,128)S(1)} %get-tuple-element.84.refs_1_.refs_3_, ...), custom_call_target="tpu_custom_call" | custom-call | flops 805306368 | bytes 8388608 | tf_op jit(solution)/shard_map/pallas_call | solution.py:100
  93.2 2.5 collective-permute-done.5
  95.7 1.4 add_convert_fusion.3
  97.1 3.5 all-to-all-start.2
  101.5 2.2 copy-done.26
  105.0 10.6 %all-to-all-done.2.refs_0_ = bf16[4,64,2048]{2,1,0:T(8,128)(2,1)S(1)} async-done(((bf16[4,64,2048]{2,1,0:T(8,128)(2,1)}), bf16[4,64,2048]{2,1,0:T(8,128)(2,1)S(1)}, u32[]{:S(2)}, u32[]{:S(2)}) %all-to-all-start.2) | async-done | bytes 1048608 | tf_op jit(solution)/shard_map/all_to_all | solution.py:779
  117.7 16.6 %all_to_all.35 = bf16[4,64,2048]{2,1,0:T(8,128)(2,1)S(1)} all-to-all(bf16[4,64,2048]{2,1,0:T(8,128)(2,1)S(1)} %get-tuple-element.89), channel_id=1, replica_groups=mesh['shard'=16,'ctx'=4,'tp'=2] {'ctx'}, dimensions={0} | all-to-all | bytes 2097152 | tf_op jit(solution)/shard_map/all_to_all | solution.py:779
  134.3 1.9 collective-permute-start.6
  136.2 2.3 collective-permute-done.6
  138.5 1.3 shard_map.270.refs_7_.refs_0_
  142.1 1.4 all-gather.5.cloned.1.call-done.refs_4_.refs_5_.refs_6_.refs_2_.refs_3_.refs_1_
  143.5 10.0 %shard_map.271 = (bf16[512,768]{1,0:T(8,128)(2,1)}, bf16[512,768]{1,0:T(8,128)(2,1)}, bf16[512,768]{1,0:T(8,128)(2,1)}) custom-call(bf16[256,2048]{1,0:T(8,128)(2,1)} %bitcast.78, bf16[256,2048]{1,0:T(8,128)(2,1)} %bitcast.84, bf16[4,128,2048]{2,1,0:T(8,128)(2,1)} %all-to-all-done.1.refs_0_.refs_2_.refs_1_, bf16[4,128,2048]{2,1,0:T(8,128)(2,1)} %copy-done.43, ...), custom_call_target="tpu_custom_call" | custom-call | flops 4831838208 | bytes 8388608 | tf_op jit(solution)/shard_map/pallas_call | solution.py:100
  153.4 9.9 %shard_map.272.refs_4_ = bf16[2048,2304]{1,0:T(8,128)(2,1)} custom-call(bf16[2048,512]{1,0:T(8,128)(2,1)} %copy-done.2, bf16[4,128,2048]{2,1,0:T(8,128)(2,1)} %all-to-all-done.1.refs_0_.refs_2_.refs_1_, bf16[4,128,2048]{2,1,0:T(8,128)(2,1)} %copy-done.43, bf16[512,768]{1,0:T(8,128)(2,1)} %get-tuple-element.91.refs_3_.refs_0_, ...), custom_call_target="tpu_custom_call" | custom-call | flops 4831838208 | bytes 8388608 | tf_op jit(solution)/shard_map/pallas_call | solution.py:100
  165.6 6.0 %shard_map.273 = (bf16[256,2048]{1,0:T(8,128)(2,1)S(1)}, bf16[256,2048]{1,0:T(8,128)(2,1)S(1)}) custom-call(bf16[512,768]{1,0:T(8,128)(2,1)S(1)} %copy-done.9, bf16[512,768]{1,0:T(8,128)(2,1)S(1)} %copy-done.10, bf16[2048,2304]{1,0:T(8,128)(2,1)} %all-gather.5.cloned.1.call-done.refs_4_.refs_5_.refs_6_.refs_2_.refs_3_.refs_1_, ...), custom_call_target="tpu_custom_call" | custom-call | flops 3221225472 | bytes 8388608 | tf_op jit(solution)/shard_map/pallas_call | solution.py:100
  172.3 2.3 collective-permute-done.7
  175.0 18.2 %all_to_all.36.refs_0_ = bf16[4,64,2048]{2,1,0:T(8,128)(2,1)S(1)} all-to-all(bf16[4,64,2048]{2,1,0:T(8,128)(2,1)S(1)} %bitcast.79), channel_id=1, replica_groups=mesh['shard'=16,'ctx'=4,'tp'=2] {'ctx'}, dimensions={0} | all-to-all | bytes 2097152 | tf_op jit(solution)/shard_map/all_to_all | solution.py:779
  196.5 3.5 all-to-all-start.5
  202.4 4.2 %shard_map.275 = (bf16[256,2048]{1,0:T(8,128)(2,1)S(1)}, bf16[256,2048]{1,0:T(8,128)(2,1)S(1)}) custom-call(bf16[512,768]{1,0:T(8,128)(2,1)S(1)} %copy-done.8, bf16[2048,2304]{1,0:T(8,128)(2,1)} %all-gather.5.cloned.1.call-done.refs_4_.refs_5_.refs_6_.refs_2_.refs_3_.refs_1_, bf16[4,64,2048]{2,1,0:T(8,128)(2,1)S(1)} %bitcast.80), custom_call_target="tpu_custom_call" | custom-call | flops 1610612736 | bytes 8388608 | tf_op jit(solution)/shard_map/pallas_call | solution.py:100
  208.6 4.8 %all-to-all-done.5 = bf16[4,64,2048]{2,1,0:T(8,128)(2,1)S(1)} async-done(((bf16[4,64,2048]{2,1,0:T(8,128)(2,1)}), bf16[4,64,2048]{2,1,0:T(8,128)(2,1)S(1)}, u32[]{:S(2)}, u32[]{:S(2)}) %all-to-all-start.5) | async-done | bytes 1048608 | tf_op jit(solution)/shard_map/all_to_all | solution.py:779
  213.3 2.7 collective-permute-start.8
  216.0 2.3 collective-permute-done.8
  220.4 2.2 shard_map.276
  222.8 3.1 shard_map.277
  226.0 4.4 %shard_map.278.refs_3_ = bf16[2048,1024]{1,0:T(8,128)(2,1)} custom-call(bf16[2048,512]{1,0:T(8,128)(2,1)S(1)} %shard_map.267.refs_2_.refs_0_, bf16[256,2048]{1,0:T(8,128)(2,1)S(1)} %bitcast.76, bf16[256,2048]{1,0:T(8,128)(2,1)S(1)} %bitcast.82, bf16[512,512]{1,0:T(8,128)(2,1)S(1)} %get-tuple-element.105.refs_3_.refs_0_, ...), custom_call_target="tpu_custom_call" | custom-call | flops 2147483648 | bytes 8388608 | tf_op jit(solution)/shard_map/pallas_call | solution.py:100
  232.8 4.1 %shard_map.279 = (bf16[256,2048]{1,0:T(8,128)(2,1)S(1)}, bf16[256,2048]{1,0:T(8,128)(2,1)S(1)}) custom-call(bf16[512,512]{1,0:T(8,128)(2,1)S(1)} %copy-done.23, bf16[512,256]{1,0:T(8,128)(2,1)S(1)} %copy-done.30, bf16[2048,1024]{1,0:T(8,128)(2,1)} %bitcast.88, bf16[2048,1024]{1,0:T(8,128)(2,1)} %shard_map.278.refs_3_), custom_call_target="tpu_custom_call" | custom-call | flops 1610612736 | bytes 8388608 | tf_op jit(solution)/shard_map/pallas_call | solution.py:100
  237.7 2.0 collective-permute-done.10
  240.1 9.4 %reduce-scatter.5.cloned.1.call-done = bf16[128,2304]{1,0:T(8,128)(2,1)} async-done(((bf16[2048,2304]{1,0:T(8,128)(2,1)}), bf16[128,2304]{1,0:T(8,128)(2,1)}) %reduce-scatter.5.cloned.1.call-update) | async-done | bytes 589840 | tf_op jit(solution)/shard_map/reduce_scatter | solution.py:798
  249.5 4.4 %collective-permute-start.11 = (bf16[128,2304]{1,0:T(8,128)(2,1)}, bf16[128,2304]{1,0:T(8,128)(2,1)S(1)}, u32[]{:S(2)}, u32[]{:S(2)}) collective-permute-start(bf16[128,2304]{1,0:T(8,128)(2,1)} %reduce-scatter.5.cloned.1.call-done), channel_id=1, source_target_pairs={{8,1},{1,8},{24,17},{17,24},{40,33},{33,40},{56,49},{49,56},{72,65... | collective-permute-start | bytes 1769480 | tf_op jit(solution)/shard_map/ppermute | solution.py:827
  254.2 7.9 %collective-permute-done.11 = bf16[128,2304]{1,0:T(8,128)(2,1)S(1)} collective-permute-done((bf16[128,2304]{1,0:T(8,128)(2,1)}, bf16[128,2304]{1,0:T(8,128)(2,1)S(1)}, u32[]{:S(2)}, u32[]{:S(2)}) %collective-permute-start.11) | collective-permute-done | bytes 589856 | tf_op jit(solution)/shard_map/ppermute | solution.py:827
  262.2 1.6 collective-permute-start.15
  266.2 1.4 collective-permute-start.13
  267.6 2.0 collective-permute-start.14
  269.9 17.5 %collective-permute-done.12.refs_1_ = bf16[128,2048]{1,0:T(8,128)(2,1)S(1)} collective-permute-done((bf16[128,2048]{1,0:T(8,128)(2,1)}, bf16[128,2048]{1,0:T(8,128)(2,1)S(1)}, u32[]{:S(2)}, u32[]{:S(2)}) %collective-permute-start.12) | collective-permute-done | bytes 524320 | tf_op jit(solution)/shard_map/ppermute | solution.py:782
  287.3 6.5 %collective-permute-done.13.refs_2_ = bf16[128,2048]{1,0:T(8,128)(2,1)S(1)} collective-permute-done((bf16[128,2048]{1,0:T(8,128)(2,1)}, bf16[128,2048]{1,0:T(8,128)(2,1)S(1)}, u32[]{:S(2)}, u32[]{:S(2)}) %collective-permute-start.13) | collective-permute-done | bytes 524320 | tf_op jit(solution)/shard_map/ppermute | solution.py:782
  293.9 1.8 shard_map.280
  300.1 7.5 %all-to-all-start.6 = ((bf16[128,8,128]{2,1,0:T(8,128)(2,1)}), bf16[128,8,128]{2,1,0:T(8,128)(2,1)S(1)}, u32[]{:S(2)}, u32[]{:S(2)}) async-start(bf16[128,8,128]{2,1,0:T(8,128)(2,1)} %bitcast.42), calls=%async_computation.8 | async-start | bytes 524288 | tf_op jit(solution)/shard_map/all_to_all | solution.py:936
  308.4 3.5 collective-permute-done.16.b2
  311.9 8.0 %collective-permute-done.17.b3 = bf16[128,2304]{1,0:T(8,128)(2,1)} collective-permute-done((bf16[128,2304]{1,0:T(8,128)(2,1)S(1)}, bf16[128,2304]{1,0:T(8,128)(2,1)}, u32[]{:S(2)}, u32[]{:S(2)}) %collective-permute-start.17) | collective-permute-done | bytes 589856 | tf_op jit(solution)/shard_map/ppermute | solution.py:782
  319.9 5.5 %shard_map.281 = (f32[128,3072]{1,0:T(8,128)}, f32[128,3072]{1,0:T(8,128)}, f32[3072,128]{1,0:T(8,128)}, f32[128,128]{1,0:T(8,128)}) custom-call(s32[1]{0:T(128)} %bitcast.at.turn_at, bf16[128,2304]{1,0:T(8,128)(2,1)} %copy-done.6, bf16[128,2304]{1,0:T(8,128)(2,1)} %collective-permute-done.15.b1, bf16[128,2304]{1,0:T(8,128)(2,1)} %collective-permute-done.16.b2, ...), custom_call_target="tpu_custom_call" | custom-call | flops 1048576 | bytes 8388608 | tf_op jit(solution)/shard_map/pallas_call | solution.py:701
  327.2 2.0 collective-permute-done.18
  330.9 1.6 select_convert_fusion
  332.6 3.8 %collective-permute-start.21 = (bf16[128,1024]{1,0:T(8,128)(2,1)}, bf16[128,1024]{1,0:T(8,128)(2,1)S(1)}, u32[]{:S(2)}, u32[]{:S(2)}) collective-permute-start(bf16[128,1024]{1,0:T(8,128)(2,1)} %reduce-scatter.3.cloned.1.call-done), channel_id=1, source_target_pairs={{1,8},{3,10},{5,12},{7,14},{8,1},{10,3},{12,5},{14,7},{17,24},{19,... | collective-permute-start | bytes 786440 | tf_op jit(solution)/shard_map/ppermute | solution.py:913
  336.4 1.6 collective-permute-start.22
  338.0 3.2 collective-permute-start.23
  341.2 1.5 slice_bitcast_fusion
  343.4 3.8 %collective-permute-done.22.b1 = bf16[128,1024]{1,0:T(8,128)(2,1)S(1)} collective-permute-done((bf16[128,1024]{1,0:T(8,128)(2,1)}, bf16[128,1024]{1,0:T(8,128)(2,1)S(1)}, u32[]{:S(2)}, u32[]{:S(2)}) %collective-permute-start.22) | collective-permute-done | bytes 262176 | tf_op jit(solution)/shard_map/ppermute | solution.py:913
  347.2 2.0 collective-permute-done.23.b2
  349.2 1.9 collective-permute-done.24.b3
  351.8 3.1 shard_map.282
  (220 shorter events, 47.2 us)
Async XLA Ops:
  7.2 26.5 %copy-start = (bf16[3072,128]{1,0:T(8,128)(2,1)S(1)}, bf16[3072,128]{1,0:T(8,128)(2,1)}, u32[]{:S(2)}) copy-start(bf16[3072,128]{1,0:T(8,128)(2,1)} %param.30) | copy-start | bytes 2359300
  7.2 59.6 %all-gather.3.cloned.1.call-start = ((), (), s32[]{:S(2)}) async-start(), calls=%async_computation.9 | async-start | bytes 4456448 | tf_op jit(solution)/shard_map/all_gather | solution.py:795
  7.3 4.7 %copy-start.55 = (bf16[8]{0:T(256)(128)(2,1)S(1)}, bf16[8]{0:T(256)(128)(2,1)}, u32[]{:S(2)}) copy-start(bf16[8]{0:T(256)(128)(2,1)} %param.26) | copy-start | bytes 52
  7.3 4.7 %copy-start.56 = (bf16[8]{0:T(256)(128)(2,1)S(1)}, bf16[8]{0:T(256)(128)(2,1)}, u32[]{:S(2)}) copy-start(bf16[8]{0:T(256)(128)(2,1)} %param.25) | copy-start | bytes 52
  9.1 10.6 %copy-start.57 = (bf16[128]{0:T(256)(128)(2,1)S(1)}, bf16[128]{0:T(256)(128)(2,1)}, u32[]{:S(2)}) copy-start(bf16[128]{0:T(256)(128)(2,1)} %param.27) | copy-start | bytes 772
  10.5 9.3 %collective-permute-start.1 = (bf16[128,2048]{1,0:T(8,128)(2,1)S(1)}, bf16[128,2048]{1,0:T(8,128)(2,1)S(1)}, u32[]{:S(2)}, u32[]{:S(2)}) collective-permute-start(bf16[128,2048]{1,0:T(8,128)(2,1)S(1)} %pad_maximum_fusion.2), channel_id=1, source_target_pairs={{0,8},{8,0},{16,24},{24,16},{32,40},{40,32},{48,56},{56,48},{64,72... | collective-permute-start | bytes 1572872 | tf_op jit(solution)/shard_map/ppermute | solution.py:776
  12.6 14.5 %all-to-all-start = ((bf16[16,8,128]{2,1,0:T(8,128)(2,1)}), bf16[16,8,128]{2,1,0:T(8,128)(2,1)S(1)}, u32[]{:S(2)}, u32[]{:S(2)}) async-start(bf16[16,8,128]{2,1,0:T(8,128)(2,1)} %broadcast_in_dim.24), calls=%async_computation | async-start | bytes 65536 | tf_op jit(solution)/shard_map/all_to_all | solution.py:841
  19.9 8.7 %copy-start.44 = (bf16[128,2048]{1,0:T(8,128)(2,1)}, bf16[128,2048]{1,0:T(8,128)(2,1)S(1)}, u32[]{:S(2)}) copy-start(bf16[128,2048]{1,0:T(8,128)(2,1)S(1)} %maximum_select_fusion) | copy-start | bytes 1572868
  28.7 31.1 %all-to-all-start.1 = ((bf16[4,128,2048]{2,1,0:T(8,128)(2,1)}), bf16[4,128,2048]{2,1,0:T(8,128)(2,1)}, u32[]{:S(2)}, u32[]{:S(2)}) async-start(bf16[4,128,2048]{2,1,0:T(8,128)(2,1)} %broadcast_in_dim.25), calls=%async_computation.1 | async-start | bytes 4194304 | tf_op jit(solution)/shard_map/all_to_all | solution.py:779
  33.7 109.8 %all-gather.5.cloned.1.call-start = ((), (), s32[]{:S(2)}) async-start(), calls=%async_computation.10 | async-start | bytes 10027008 | tf_op jit(solution)/shard_map/all_gather | solution.py:795
  34.9 25.7 %copy-start.52 = (s32[1,13]{1,0:T(1,128)S(1)}, s32[1,13]{1,0:T(1,128)}, u32[]{:S(2)}) copy-start(s32[1,13]{1,0:T(1,128)} %param.18) | copy-start | bytes 160
  35.0 25.7 %copy-start.53 = (s32[1,13]{1,0:T(1,128)S(1)}, s32[1,13]{1,0:T(1,128)}, u32[]{:S(2)}) copy-start(s32[1,13]{1,0:T(1,128)} %param.17) | copy-start | bytes 160
  35.2 11.6 %collective-permute-start = (bf16[128,2304]{1,0:T(8,128)(2,1)S(1)}, bf16[128,2304]{1,0:T(8,128)(2,1)S(1)}, u32[]{:S(2)}, u32[]{:S(2)}) collective-permute-start(bf16[128,2304]{1,0:T(8,128)(2,1)S(1)} %pad_maximum_fusion.1), channel_id=1, source_target_pairs={{8,1},{1,8},{24,17},{17,24},{40,33},{33,40},{56,49},{49,56},{72,65... | collective-permute-start | bytes 1769480 | tf_op jit(solution)/shard_map/ppermute | solution.py:859
  60.7 2.5 collective-permute-start.3
  62.4 4.4 %collective-permute-start.2 = (bf16[4,128,2048]{2,1,0:T(8,128)(2,1)}, bf16[4,128,2048]{2,1,0:T(8,128)(2,1)S(1)}, u32[]{:S(2)}, u32[]{:S(2)}) collective-permute-start(bf16[4,128,2048]{2,1,0:T(8,128)(2,1)} %all-to-all-done.1.refs_0_.refs_2_.refs_1_), channel_id=1, source_target_pairs={{0,8},{8,0},{16,24},{24,16},{32,40},{40,32},{48,56},{56,48},{64,72... | collective-permute-start | bytes 6291464 | tf_op jit(solution)/shard_map/ppermute | solution.py:776
  65.3 14.4 %copy-start.11 = (f32[512,128]{1,0:T(8,128)}, f32[512,128]{1,0:T(8,128)S(1)}, u32[]{:S(2)}) copy-start(f32[512,128]{1,0:T(8,128)S(1)} %get-tuple-element.80.refs_4_.refs_5_) | copy-start | bytes 786436
  70.5 4.4 %collective-permute-start.4 = (bf16[8,128,1024]{2,1,0:T(8,128)(2,1)S(1)}, bf16[8,128,1024]{2,1,0:T(8,128)(2,1)}, u32[]{:S(2)}, u32[]{:S(2)}) collective-permute-start(bf16[8,128,1024]{2,1,0:T(8,128)(2,1)S(1)} %shard_map.264), channel_id=1, source_target_pairs={{0,8},{8,0},{16,24},{24,16},{32,40},{40,32},{48,56},{56,48},{64,72... | collective-permute-start | bytes 6291464 | tf_op jit(solution)/shard_map/ppermute | solution.py:776
  86.5 6.4 %copy-start.15 = (f32[512,256]{1,0:T(8,128)}, f32[512,256]{1,0:T(8,128)S(1)}, u32[]{:S(2)}) copy-start(f32[512,256]{1,0:T(8,128)S(1)} %get-tuple-element.84.refs_1_.refs_3_) | copy-start | bytes 1572868
  86.5 6.4 %copy-start.20 = (bf16[512,512]{1,0:T(8,128)(2,1)}, bf16[512,512]{1,0:T(8,128)(2,1)S(1)}, u32[]{:S(2)}) copy-start(bf16[512,512]{1,0:T(8,128)(2,1)S(1)} %get-tuple-element.83.refs_0_.refs_1_) | copy-start | bytes 1572868
  86.5 6.4 %copy-start.33 = (f32[512,384]{1,0:T(8,128)}, f32[512,384]{1,0:T(8,128)S(1)}, u32[]{:S(2)}) copy-start(f32[512,384]{1,0:T(8,128)S(1)} %get-tuple-element.104.refs_3_) | copy-start | bytes 2359300
  92.9 4.1 %copy-start.35 = (f32[512,256]{1,0:T(8,128)}, f32[512,256]{1,0:T(8,128)S(1)}, u32[]{:S(2)}) copy-start(f32[512,256]{1,0:T(8,128)S(1)} %get-tuple-element.102.refs_4_) | copy-start | bytes 1572868
  92.9 4.1 %copy-start.39 = (bf16[512,256]{1,0:T(8,128)(2,1)}, bf16[512,256]{1,0:T(8,128)(2,1)S(1)}, u32[]{:S(2)}) copy-start(bf16[512,256]{1,0:T(8,128)(2,1)S(1)} %get-tuple-element.107.refs_5_) | copy-start | bytes 786436
  93.0 2.7 collective-permute-start.5
  95.7 4.9 %copy-start.45 = (bf16[128,2048]{1,0:T(8,128)(2,1)S(1)}, bf16[128,2048]{1,0:T(8,128)(2,1)}, u32[]{:S(2)}) copy-start(bf16[128,2048]{1,0:T(8,128)(2,1)} %copy-done.44) | copy-start | bytes 1572868
  97.1 18.6 %all-to-all-start.2 = ((bf16[4,64,2048]{2,1,0:T(8,128)(2,1)}), bf16[4,64,2048]{2,1,0:T(8,128)(2,1)S(1)}, u32[]{:S(2)}, u32[]{:S(2)}) async-start(bf16[4,64,2048]{2,1,0:T(8,128)(2,1)} %bitcast.22), calls=%async_computation.2 | async-start | bytes 2097152 | tf_op jit(solution)/shard_map/all_to_all | solution.py:779
  100.6 148.9 %reduce-scatter.5.cloned.1.call-start = ((), (), s32[]{:S(2)}) async-start(), calls=%async_computation.12 | async-start | bytes 10027008 | tf_op jit(solution)/shard_map/reduce_scatter | solution.py:798
  134.3 5.5 %copy-start.3 = (bf16[4,64,2048]{2,1,0:T(8,128)(2,1)}, bf16[4,64,2048]{2,1,0:T(8,128)(2,1)S(1)}, u32[]{:S(2)}) copy-start(bf16[4,64,2048]{2,1,0:T(8,128)(2,1)S(1)} %all_to_all.35) | copy-start | bytes 3145732
  134.3 4.2 %collective-permute-start.6 = (bf16[4,64,2048]{2,1,0:T(8,128)(2,1)S(1)}, bf16[4,64,2048]{2,1,0:T(8,128)(2,1)S(1)}, u32[]{:S(2)}, u32[]{:S(2)}) collective-permute-start(bf16[4,64,2048]{2,1,0:T(8,128)(2,1)S(1)} %all_to_all.35), channel_id=1, source_target_pairs={{0,8},{8,0},{16,24},{24,16},{32,40},{40,32},{48,56},{56,48},{64,72... | collective-permute-start | bytes 3145736 | tf_op jit(solution)/shard_map/ppermute | solution.py:776
  171.6 3.0 collective-permute-start.7
  174.6 19.6 %copy-start.18 = (f32[64,2048]{1,0:T(8,128)S(1)}, f32[64,2048]{1,0:T(8,128)}, u32[]{:S(2)}) copy-start(f32[64,2048]{1,0:T(8,128)} %copy-done.17) | copy-start | bytes 1572868
  174.6 19.6 %copy-start.32 = (bf16[64,2048]{1,0:T(8,128)(2,1)S(1)}, bf16[64,2048]{1,0:T(8,128)(2,1)}, u32[]{:S(2)}) copy-start(bf16[64,2048]{1,0:T(8,128)(2,1)} %get-tuple-element.152.refs_2_) | copy-start | bytes 786436
  196.5 16.9 %all-to-all-start.5 = ((bf16[4,64,2048]{2,1,0:T(8,128)(2,1)}), bf16[4,64,2048]{2,1,0:T(8,128)(2,1)S(1)}, u32[]{:S(2)}, u32[]{:S(2)}) async-start(bf16[4,64,2048]{2,1,0:T(8,128)(2,1)} %copy-done.31), calls=%async_computation.5 | async-start | bytes 2097152 | tf_op jit(solution)/shard_map/all_to_all | solution.py:779
  200.0 132.6 %reduce-scatter.3.cloned.1.call-start = ((), (), s32[]{:S(2)}) async-start(), calls=%async_computation.11 | async-start | bytes 4456448 | tf_op jit(solution)/shard_map/reduce_scatter | solution.py:798
  213.3 5.0 %collective-permute-start.8 = (bf16[4,64,2048]{2,1,0:T(8,128)(2,1)S(1)}, bf16[4,64,2048]{2,1,0:T(8,128)(2,1)S(1)}, u32[]{:S(2)}, u32[]{:S(2)}) collective-permute-start(bf16[4,64,2048]{2,1,0:T(8,128)(2,1)S(1)} %all-to-all-done.5), channel_id=1, source_target_pairs={{0,8},{8,0},{16,24},{24,16},{32,40},{40,32},{48,56},{56,48},{64,72... | collective-permute-start | bytes 3145736 | tf_op jit(solution)/shard_map/ppermute | solution.py:776
  222.6 3.3 copy-start.29
  222.8 3.1 copy-start.40
  232.4 5.0 %copy-start.28 = (bf16[256,2048]{1,0:T(8,128)(2,1)S(1)}, bf16[256,2048]{1,0:T(8,128)(2,1)}, u32[]{:S(2)}) copy-start(bf16[256,2048]{1,0:T(8,128)(2,1)} %copy-done.27) | copy-start | bytes 3145732
  232.4 5.0 %collective-permute-start.9 = (bf16[256,2048]{1,0:T(8,128)(2,1)S(1)}, bf16[256,2048]{1,0:T(8,128)(2,1)S(1)}, u32[]{:S(2)}, u32[]{:S(2)}) collective-permute-start(bf16[256,2048]{1,0:T(8,128)(2,1)S(1)} %copy-done.42), channel_id=1, source_target_pairs={{0,8},{8,0},{16,24},{24,16},{32,40},{40,32},{48,56},{56,48},{64,72... | collective-permute-start | bytes 3145736 | tf_op jit(solution)/shard_map/ppermute | solution.py:776
  237.0 2.7 collective-permute-start.10
  249.5 12.6 %collective-permute-start.11 = (bf16[128,2304]{1,0:T(8,128)(2,1)}, bf16[128,2304]{1,0:T(8,128)(2,1)S(1)}, u32[]{:S(2)}, u32[]{:S(2)}) collective-permute-start(bf16[128,2304]{1,0:T(8,128)(2,1)} %reduce-scatter.5.cloned.1.call-done), channel_id=1, source_target_pairs={{8,1},{1,8},{24,17},{17,24},{40,33},{33,40},{56,49},{49,56},{72,65... | collective-permute-start | bytes 1769480 | tf_op jit(solution)/shard_map/ppermute | solution.py:827
  253.9 8.1 %copy-start.47 = (bf16[128,2304]{1,0:T(8,128)(2,1)S(1)}, bf16[128,2304]{1,0:T(8,128)(2,1)}, u32[]{:S(2)}) copy-start(bf16[128,2304]{1,0:T(8,128)(2,1)} %reduce-scatter.5.cloned.1.call-done) | copy-start | bytes 1769476
  262.1 34.2 %copy-start.6 = (bf16[128,2304]{1,0:T(8,128)(2,1)}, bf16[128,2304]{1,0:T(8,128)(2,1)S(1)}, u32[]{:S(2)}) copy-start(bf16[128,2304]{1,0:T(8,128)(2,1)S(1)} %broadcast_select_fusion.refs_7_.b0) | copy-start | bytes 1769476
  262.1 31.7 %copy-start.14 = (bf16[64,2048]{1,0:T(8,128)(2,1)S(1)}, bf16[64,2048]{1,0:T(8,128)(2,1)}, u32[]{:S(2)}) copy-start(bf16[64,2048]{1,0:T(8,128)(2,1)} %get-tuple-element.153.refs_1_.refs_6_) | copy-start | bytes 786436
  262.1 31.7 %copy-start.19 = (f32[64,2048]{1,0:T(8,128)S(1)}, f32[64,2048]{1,0:T(8,128)}, u32[]{:S(2)}) copy-start(f32[64,2048]{1,0:T(8,128)} %copy-done.17) | copy-start | bytes 1572868
  262.2 31.7 %copy-start.38 = (f32[64,2048]{1,0:T(8,128)S(1)}, f32[64,2048]{1,0:T(8,128)}, u32[]{:S(2)}) copy-start(f32[64,2048]{1,0:T(8,128)} %copy-done.37) | copy-start | bytes 1572868
  262.2 33.5 %collective-permute-start.15 = (bf16[128,2304]{1,0:T(8,128)(2,1)S(1)}, bf16[128,2304]{1,0:T(8,128)(2,1)}, u32[]{:S(2)}, u32[]{:S(2)}) collective-permute-start(bf16[128,2304]{1,0:T(8,128)(2,1)S(1)} %broadcast_select_fusion.refs_7_.b0), channel_id=1, source_target_pairs={{0,2},{2,4},{4,6},{6,0},{1,3},{3,5},{5,7},{7,1},{8,10},{10,12},{12... | collective-permute-start | bytes 1769480 | tf_op jit(solution)/shard_map/ppermute | solution.py:782
  265.0 22.3 %collective-permute-start.12 = (bf16[128,2048]{1,0:T(8,128)(2,1)}, bf16[128,2048]{1,0:T(8,128)(2,1)S(1)}, u32[]{:S(2)}, u32[]{:S(2)}) collective-permute-start(bf16[128,2048]{1,0:T(8,128)(2,1)} %get-tuple-element.146), channel_id=1, source_target_pairs={{0,2},{2,4},{4,6},{6,0},{1,3},{3,5},{5,7},{7,1},{8,10},{10,12},{12... | collective-permute-start | bytes 1572872 | tf_op jit(solution)/shard_map/ppermute | solution.py:782
  266.2 27.7 %collective-permute-start.13 = (bf16[128,2048]{1,0:T(8,128)(2,1)}, bf16[128,2048]{1,0:T(8,128)(2,1)S(1)}, u32[]{:S(2)}, u32[]{:S(2)}) collective-permute-start(bf16[128,2048]{1,0:T(8,128)(2,1)} %get-tuple-element.145), channel_id=1, source_target_pairs={{0,4},{2,6},{4,0},{6,2},{1,5},{3,7},{5,1},{7,3},{8,12},{10,14},{12... | collective-permute-start | bytes 1572872 | tf_op jit(solution)/shard_map/ppermute | solution.py:782
  267.6 26.3 %collective-permute-start.14 = (bf16[128,2048]{1,0:T(8,128)(2,1)}, bf16[128,2048]{1,0:T(8,128)(2,1)}, u32[]{:S(2)}, u32[]{:S(2)}) collective-permute-start(bf16[128,2048]{1,0:T(8,128)(2,1)} %get-tuple-element.144), channel_id=1, source_target_pairs={{0,6},{2,0},{4,2},{6,4},{1,7},{3,1},{5,3},{7,5},{8,14},{10,8},{12,... | collective-permute-start | bytes 1572872 | tf_op jit(solution)/shard_map/ppermute | solution.py:782
  295.7 2.0 collective-permute-start.19
  295.8 16.0 %collective-permute-start.16 = (bf16[128,2304]{1,0:T(8,128)(2,1)S(1)}, bf16[128,2304]{1,0:T(8,128)(2,1)}, u32[]{:S(2)}, u32[]{:S(2)}) collective-permute-start(bf16[128,2304]{1,0:T(8,128)(2,1)S(1)} %broadcast_select_fusion.refs_7_.b0), channel_id=1, source_target_pairs={{0,4},{2,6},{4,0},{6,2},{1,5},{3,7},{5,1},{7,3},{8,12},{10,14},{12... | collective-permute-start | bytes 1769480 | tf_op jit(solution)/shard_map/ppermute | solution.py:782
  296.4 23.5 %collective-permute-start.17 = (bf16[128,2304]{1,0:T(8,128)(2,1)S(1)}, bf16[128,2304]{1,0:T(8,128)(2,1)}, u32[]{:S(2)}, u32[]{:S(2)}) collective-permute-start(bf16[128,2304]{1,0:T(8,128)(2,1)S(1)} %broadcast_select_fusion.refs_7_.b0), channel_id=1, source_target_pairs={{0,6},{2,0},{4,2},{6,4},{1,7},{3,1},{5,3},{7,5},{8,14},{10,8},{12,... | collective-permute-start | bytes 1769480 | tf_op jit(solution)/shard_map/ppermute | solution.py:782
  297.9 33.0 %copy-start.46 = (bf16[1,128,2048]{2,1,0:T(8,128)(2,1)}, bf16[1,128,2048]{2,1,0:T(8,128)(2,1)S(1)}, u32[]{:S(2)}) copy-start(bf16[1,128,2048]{2,1,0:T(8,128)(2,1)S(1)} %maximum_select_fusion.2) | copy-start | bytes 1572868
  298.0 32.9 %collective-permute-start.20 = (bf16[2,128,2048]{2,1,0:T(8,128)(2,1)S(1)}, bf16[2,128,2048]{2,1,0:T(8,128)(2,1)}, u32[]{:S(2)}, u32[]{:S(2)}) collective-permute-start(bf16[2,128,2048]{2,1,0:T(8,128)(2,1)S(1)} %pad_maximum_fusion), channel_id=1, source_target_pairs={{0,1},{9,8},{16,17},{25,24},{32,33},{41,40},{48,49},{57,56},{64,65... | collective-permute-start | bytes 3145736 | tf_op jit(solution)/shard_map/ppermute | solution.py:965
  300.1 29.5 %all-to-all-start.6 = ((bf16[128,8,128]{2,1,0:T(8,128)(2,1)}), bf16[128,8,128]{2,1,0:T(8,128)(2,1)S(1)}, u32[]{:S(2)}, u32[]{:S(2)}) async-start(bf16[128,8,128]{2,1,0:T(8,128)(2,1)} %bitcast.42), calls=%async_computation.8 | async-start | bytes 524288 | tf_op jit(solution)/shard_map/all_to_all | solution.py:936
  307.6 18.8 %copy-start.54 = (bf16[128]{0:T(256)(128)(2,1)S(1)}, bf16[128]{0:T(256)(128)(2,1)}, u32[]{:S(2)}) copy-start(bf16[128]{0:T(256)(128)(2,1)} %param.19) | copy-start | bytes 772
  326.3 2.9 collective-permute-start.18
  330.9 24.0 %copy-start.1 = (bf16[3072,128]{1,0:T(8,128)(2,1)S(1)}, bf16[3072,128]{1,0:T(8,128)(2,1)}, u32[]{:S(2)}) copy-start(bf16[3072,128]{1,0:T(8,128)(2,1)} %param.30) | copy-start | bytes 2359300
  332.6 10.1 %copy-start.48 = (bf16[128,1024]{1,0:T(8,128)(2,1)S(1)}, bf16[128,1024]{1,0:T(8,128)(2,1)}, u32[]{:S(2)}) copy-start(bf16[128,1024]{1,0:T(8,128)(2,1)} %reduce-scatter.3.cloned.1.call-done) | copy-start | bytes 786436
  332.6 10.1 %collective-permute-start.21 = (bf16[128,1024]{1,0:T(8,128)(2,1)}, bf16[128,1024]{1,0:T(8,128)(2,1)S(1)}, u32[]{:S(2)}, u32[]{:S(2)}) collective-permute-start(bf16[128,1024]{1,0:T(8,128)(2,1)} %reduce-scatter.3.cloned.1.call-done), channel_id=1, source_target_pairs={{1,8},{3,10},{5,12},{7,14},{8,1},{10,3},{12,5},{14,7},{17,24},{19,... | collective-permute-start | bytes 786440 | tf_op jit(solution)/shard_map/ppermute | solution.py:913
  336.4 10.8 %collective-permute-start.22 = (bf16[128,1024]{1,0:T(8,128)(2,1)}, bf16[128,1024]{1,0:T(8,128)(2,1)S(1)}, u32[]{:S(2)}, u32[]{:S(2)}) collective-permute-start(bf16[128,1024]{1,0:T(8,128)(2,1)} %reduce-scatter.3.cloned.1.call-done), channel_id=1, source_target_pairs={{0,2},{1,10},{2,4},{3,12},{4,6},{5,14},{6,0},{7,8},{8,3},{9,11},{1... | collective-permute-start | bytes 786440 | tf_op jit(solution)/shard_map/ppermute | solution.py:913
  338.0 11.2 %collective-permute-start.23 = (bf16[128,1024]{1,0:T(8,128)(2,1)}, bf16[128,1024]{1,0:T(8,128)(2,1)S(1)}, u32[]{:S(2)}, u32[]{:S(2)}) collective-permute-start(bf16[128,1024]{1,0:T(8,128)(2,1)} %reduce-scatter.3.cloned.1.call-done), channel_id=1, source_target_pairs={{0,4},{1,12},{2,6},{3,14},{4,0},{5,8},{6,2},{7,10},{8,5},{9,13},{1... | collective-permute-start | bytes 786440 | tf_op jit(solution)/shard_map/ppermute | solution.py:913
  341.2 9.9 %collective-permute-start.24 = (bf16[128,1024]{1,0:T(8,128)(2,1)}, bf16[128,1024]{1,0:T(8,128)(2,1)S(1)}, u32[]{:S(2)}, u32[]{:S(2)}) collective-permute-start(bf16[128,1024]{1,0:T(8,128)(2,1)} %reduce-scatter.3.cloned.1.call-done), channel_id=1, source_target_pairs={{0,6},{1,14},{2,0},{3,8},{4,2},{5,10},{6,4},{7,12},{8,7},{9,15},{1... | collective-permute-start | bytes 786440 | tf_op jit(solution)/shard_map/ppermute | solution.py:913
  347.2 3.9 %copy-start.49 = (bf16[128,1024]{1,0:T(8,128)(2,1)}, bf16[128,1024]{1,0:T(8,128)(2,1)S(1)}, u32[]{:S(2)}) copy-start(bf16[128,1024]{1,0:T(8,128)(2,1)S(1)} %collective-permute-done.22.b1) | copy-start | bytes 786436
  (28 other events, 37.3 us)
Sparse Core Ops, SparseCore 0:
  10.7 54.5 all-gather.2
  68.2 75.2 all-gather.4
  163.5 85.9 reduce-scatter.4
  253.0 76.2 reduce-scatter.2

commit v13 on v12

--- a/solution.py
+++ b/solution.py
@@ -242,38 +242,63 @@
     )(*pieces)
 
 
-def feed_kernel(ua, ub, ca, cb, wg, wu, wd, hidden, d_gate, d_up):
-    half = ua.shape[0]
-    for number, (u, cot) in enumerate(((ua, ca), (ub, cb))):
-        rows = slice(number * half, (number + 1) * half)
-        gate, up = dot(u[...], wg[...]), dot(u[...], wu[...])
-        d_hidden = dot(flat(cot[...]), wd[...])
-        sig = jax.nn.sigmoid(gate)
-        silu = gate * sig
-        hidden[rows, :] = (silu * up).astype(BF16)
-        d_gate[rows, :] = (d_hidden * up * sig * (1.0 + gate * (1.0 - sig))).astype(BF16)
-        d_up[rows, :] = (d_hidden * silu).astype(BF16)
-
-
-def feed(ua, ub, ca, cb, w, behind):
+FEED_STEPS = 3
+
+
+def feed_kernel(
+    ua, ub, ca, cb, wg, wu, wd, u_flip, sa, sb, hidden, d_gate, d_up, out, flipped
+):
+    step = pl.program_id(0)
+    half, chunk, units = ua.shape[0], wg.shape[1], hidden.shape[1]
+
+    @pl.when(step < FEED_STEPS)
+    def _():
+        columns = pl.ds(pl.multiple_of(step * chunk, chunk), chunk)
+        for number, (u, cot) in enumerate(((ua, ca), (ub, cb))):
+            rows = slice(number * half, (number + 1) * half)
+            gate, up = dot(u[...], wg[...]), dot(u[...], wu[...])
+            d_hidden = dot(flat(cot[...]), wd[...])
+            sig = jax.nn.sigmoid(gate)
+            silu = gate * sig
+            hidden[rows, columns] = (silu * up).astype(BF16)
+            d_gate[rows, columns] = (d_hidden * up * sig * (1.0 + gate * (1.0 - sig))).astype(BF16)
+            d_up[rows, columns] = (d_hidden * silu).astype(BF16)
+
+    @pl.when(step == FEED_STEPS)
+    def _():
+        flipped[...] = hidden[...].T
+
+    @pl.when(step >= FEED_STEPS)
+    def _():
+        out[:, :units] = dot(u_flip[...], d_gate[...]).astype(BF16)
+        out[:, units : 2 * units] = dot(u_flip[...], d_up[...]).astype(BF16)
+        cot = jnp.concatenate([flat(sa[...]), flat(sb[...])], axis=0)
+        spread_blocks(flipped[...], cot, out, 2 * units)
+
+
+def feed(ua, ub, ca, cb, w, u_flip):
     half, width = ua.shape
-    chunk = 2 * HD
-    parts = w.shape[1] // 3 // chunk
-    column = lambda shift: pl.BlockSpec((width, chunk), lambda i: (0, shift * parts + i))
-    unit = pl.BlockSpec((2 * half, chunk), lambda i: (0, i))
-    units = parts * chunk
+    length, units = 2 * half, w.shape[1] // 3
+    chunk, slab = units // FEED_STEPS, 4 * HD
+    early = lambda i: jnp.minimum(i, FEED_STEPS - 1)
+    late = lambda i: jnp.maximum(i - FEED_STEPS, 0)
+    column = lambda shift: pl.BlockSpec(
+        (width, chunk), lambda i: (0, shift * FEED_STEPS + early(i))
+    )
+    piece = pl.BlockSpec((ca.shape[0], ca.shape[1] // 2, slab), lambda i: (0, 1, late(i)))
     return call(
         feed_kernel,
-        (parts,),
+        (FEED_STEPS + width // slab,),
         [fixed((half, width))] * 2
         + [piled(ca.shape, 1)] * 2
-        + [column(0), column(1), column(2)],
-        [unit, unit, unit],
-        [struct((2 * half, units), BF16)] * 3,
-        2 * 2 * half * width * units * 3,
-        behind=behind,
+        + [column(0), column(1), column(2)]
+        + [pl.BlockSpec((slab, length), lambda i: (late(i), 0)), piece, piece],
+        [fixed((length, units))] * 3 + [pl.BlockSpec((slab, 3 * units), lambda i: (late(i), 0))],
+        [struct((length, units), BF16)] * 3 + [struct((width, 3 * units), BF16)],
+        2 * length * width * units * 6,
+        scratch=[pltpu.VMEM((units, length), BF16)],
         vmem=60 << 20,
-    )(ua, ub, ca, cb, w, w, w)
+    )(ua, ub, ca, cb, w, w, w, u_flip, ca, cb)
 
 
 def feed_back_kernel(d_gate, d_up, wg, wu, mine, other):
@@ -336,37 +361,6 @@
         for owner in range(right.shape[1] // HD):
             at = start + place * HD
             out[owner * HD : (owner + 1) * HD, at : at + HD] = term[head(place), head(owner)]
-
-
-def feed_grads_kernel(u_flip, ca, cb, d_gate, d_up, hidden, out, flipped):
-    @pl.when(pl.program_id(0) == 0)
-    def _():
-        flipped[...] = hidden[...].T
-
-    units = hidden.shape[1]
-    out[:, :units] = dot(u_flip[...], d_gate[...]).astype(BF16)
-    out[:, units : 2 * units] = dot(u_flip[...], d_up[...]).astype(BF16)
-    cot = jnp.concatenate([flat(ca[...]), flat(cb[...])], axis=0)
-    spread_blocks(flipped[...], cot, out, 2 * units)
-
-
-def feed_grads(u_flip, ca, cb, d_gate, d_up, hidden, behind):
-    width, length = u_flip.shape
-    units = hidden.shape[1]
-    chunk = 4 * HD
-    return call(
-        feed_grads_kernel,
-        (width // chunk,),
-        [rowed(chunk, length)]
-        + [pl.BlockSpec((ca.shape[0], ca.shape[1] // 2, chunk), lambda i: (0, 1, i))] * 2
-        + [fixed((length, units))] * 3,
-        rowed(chunk, 3 * units),
-        struct((width, 3 * units), BF16),
-        2 * length * width * units * 3,
-        scratch=[pltpu.VMEM((units, length), BF16)],
-        vmem=56 << 20,
-        behind=behind,
-    )(u_flip, ca, cb, d_gate, d_up, hidden)
 
 
 def gate_back_kernel(da, db, w_out, gate, attended, d_attended, d_gate):
@@ -887,9 +881,8 @@
         ua, ub = (flat(v) for v in tree_rows(spread))
         u_flip = flip(ua, ub)
 
-        hidden, d_gate, d_up = feed(ua, ub, xa, xb, w2, (u_flip,))
-        ffn = feed_grads(u_flip, xa, xb, d_gate, d_up, hidden, ())
-        half = tree_half(*feed_back(d_gate, d_up, w2, (ffn,)))
+        hidden, d_gate, d_up, ffn = feed(ua, ub, xa, xb, w2, u_flip)
+        half = tree_half(*feed_back(d_gate, d_up, w2, ()))
         d_middle, spread = d_middle_step(ctx_exchange(half), middle, own_cot)
         layer_mine, layer_other = down_product(hidden, w2, 2, (half,))
         da, db, layer_mine, layer_other = tree_rows(spread, layer_mine, layer_other)
@@ -961,14 +954,19 @@
             True,
         )
         mid_terms = jnp.sum(mid_sums, axis=1)
+        grad_attn, mid_terms = lax.optimization_barrier((grad_attn, mid_terms))
+        full = jnp.where(native, full, lax.ppermute(full, PLANE, across_perm))
+        outputs = [full[0].astype(F32), full[1].astype(F32)]
+        attn_blocks = owners_at_once(grad_attn)
+        attn_blocks[1], mid_terms = lax.optimization_barrier((attn_blocks[1], mid_terms))
         mid_terms = mid_terms + lax.ppermute(mid_terms, "tp", [(0, 1), (1, 0)])
-        full = jnp.where(native, full, lax.ppermute(full, PLANE, across_perm))
-        full = full.astype(F32)
-        grad_attn, mid_terms, full = lax.optimization_barrier((grad_attn, mid_terms, full))
+        *outputs, attn_blocks[3], end_sums = lax.optimization_barrier(
+            (*outputs, attn_blocks[3], end_sums)
+        )
         grad_query, grad_key, grad_value, grad_gate_attn, grad_out = close(
             close_attend_kernel,
             turn_at,
-            owners_at_once(grad_attn),
+            attn_blocks,
             (w_query, w_key, w_value, w_gate_attn),
             gain_one,
             w_out.shape,
@@ -977,8 +975,7 @@
         )
 
         return (
-            full[0],
-            full[1],
+            *outputs,
             end_sums[0] / gain_one[:, 0],
             grad_query,
             grad_key,

time: 364 us -> 361 us (level)
  waiting for transfers between devices: 127 us -> 122 us
  other arithmetic: 10.9 us -> 15.1 us
    ppermute x4, waiting for transfers between devices: 7.7 us -> 1.54 us  [owners_at_once(): lax.ppermute(block, ('shard', 'ctx', 'tp'), perm)]
    pallas_call x15 -> x14, Pallas kernels: 61 us -> 58.5 us  [call(): return lambda *operands: built(*operands, *behind)]
    unnamed x119 -> x117, local copies, waits for them, and re-layouts: 23.5 us -> 24.2 us
  transfers between devices with their start and end apart: 34 -> 34, of which waited for: 25 -> 25; matrix products, arithmetic and copies ran while one was open for 6% -> 7% of each run, Pallas kernels for 15% -> 15%
where the time goes in v13:
time: 361 us; the launch traced here: 358 us
  waiting for transfers between devices  122 us (34%)
  Pallas kernels  76.2 us (21%)
  starting transfers between devices  61.5 us (17%)
  blocking collectives  34.8 us (10%)
  local copies, waits for them, and re-layouts  33.5 us (9%)
  other arithmetic  15.1 us (4%)
  between operations  14.6 us (4%)
    pallas_call x14, Pallas kernels, call(): return lambda *operands: built(*operands, *behind)  58.5 us
    ppermute x6, waiting for transfers between devices, ctx_turn(): lax.ppermute(value, 'ctx', [(i, (i + by) % n_ctx) for i in range(n_ctx)])  36.7 us
    all_to_all x2, blocking collectives, ctx_exchange(): return lax.all_to_all(value, 'ctx', 0, 0)  34.8 us
    all_to_all x3, waiting for transfers between devices, ctx_exchange(): return lax.all_to_all(value, 'ctx', 0, 0)  28.3 us
    unnamed x117, local copies, waits for them, and re-layouts  24.2 us
    ppermute x11, waiting for transfers between devices, core_swap(): return lax.ppermute(value, 'shard', core_perm)  17.5 us
    all_to_all x3, starting transfers between devices, ctx_exchange(): return lax.all_to_all(value, 'ctx', 0, 0)  12.1 us
    reduce_scatter x2, waiting for transfers between devices, plane_scatter(): lax.psum_scatter(value, PLANE, scatter_dimension=0, tiled=True, axis_inde...  11.2 us
  transfers between devices with their start and end apart: 34, of which 25 were waited for; matrix products, arithmetic and copies ran while one was open for 7% of the time, Pallas kernels for 15%

profile of v13, /device:TPU:1, one launch (start us, length us, event | category | flops | bytes accessed | tf_op | source)
XLA Modules:
  0.0 357.7 jit_solution(9009109884060135331)
XLA Ops:
  7.3 1.8 shard_map.263
  10.5 1.5 collective-permute-start.1
  12.6 7.1 %all-to-all-start = ((bf16[16,8,128]{2,1,0:T(8,128)(2,1)}), bf16[16,8,128]{2,1,0:T(8,128)(2,1)S(1)}, u32[]{:S(2)}, u32[]{:S(2)}) async-start(bf16[16,8,128]{2,1,0:T(8,128)(2,1)} %broadcast_in_dim.24), calls=%async_computation | async-start | bytes 65536 | tf_op jit(solution)/shard_map/all_to_all | solution.py:835
  19.9 7.2 %all-to-all-done = bf16[16,8,128]{2,1,0:T(8,128)(2,1)S(1)} async-done(((bf16[16,8,128]{2,1,0:T(8,128)(2,1)}), bf16[16,8,128]{2,1,0:T(8,128)(2,1)S(1)}, u32[]{:S(2)}, u32[]{:S(2)}) %all-to-all-start) | async-done | bytes 32800 | tf_op jit(solution)/shard_map/all_to_all | solution.py:835
  27.1 1.6 broadcast_in_dim.25
  28.7 5.0 %all-to-all-start.1 = ((bf16[4,128,2048]{2,1,0:T(8,128)(2,1)}), bf16[4,128,2048]{2,1,0:T(8,128)(2,1)}, u32[]{:S(2)}, u32[]{:S(2)}) async-start(bf16[4,128,2048]{2,1,0:T(8,128)(2,1)} %broadcast_in_dim.25), calls=%async_computation.1 | async-start | bytes 4194304 | tf_op jit(solution)/shard_map/all_to_all | solution.py:773
  35.2 2.9 collective-permute-start
  38.0 8.7 %collective-permute-done = bf16[128,2304]{1,0:T(8,128)(2,1)S(1)} collective-permute-done((bf16[128,2304]{1,0:T(8,128)(2,1)S(1)}, bf16[128,2304]{1,0:T(8,128)(2,1)S(1)}, u32[]{:S(2)}, u32[]{:S(2)}) %collective-permute-start) | collective-permute-done | bytes 589856 | tf_op jit(solution)/shard_map/ppermute | solution.py:853
  46.8 13.0 %all-to-all-done.1.refs_0_.refs_2_.refs_8_ = bf16[4,128,2048]{2,1,0:T(8,128)(2,1)} async-done(((bf16[4,128,2048]{2,1,0:T(8,128)(2,1)}), bf16[4,128,2048]{2,1,0:T(8,128)(2,1)}, u32[]{:S(2)}, u32[]{:S(2)}) %all-to-all-start.1) | async-done | bytes 2097184 | tf_op jit(solution)/shard_map/all_to_all | solution.py:773
  60.8 1.6 collective-permute-start.3
  65.3 1.5 collective-permute-done.2.refs_1_.refs_3_.refs_9_
  68.1 2.4 shard_map.264
  71.0 3.9 %collective-permute-done.4.other = bf16[8,128,1024]{2,1,0:T(8,128)(2,1)} collective-permute-done((bf16[8,128,1024]{2,1,0:T(8,128)(2,1)S(1)}, bf16[8,128,1024]{2,1,0:T(8,128)(2,1)}, u32[]{:S(2)}, u32[]{:S(2)}) %collective-permute-start.4) | collective-permute-done | bytes 2097184 | tf_op jit(solution)/shard_map/ppermute | solution.py:770
  74.9 4.8 %shard_map.265 = bf16[8,2,128,1024]{3,2,1,0:T(8,128)(2,1)} custom-call(s32[1]{0:T(128)} %bitcast.18.core, bf16[8,2,128,1024]{3,2,1,0:T(8,128)(2,1)} %bitcast.96, bf16[8,128,1024]{2,1,0:T(8,128)(2,1)} %collective-permute-done.4.other), custom_call_target="tpu_custom_call" | custom-call | flops 1048576 | bytes 8388608 | tf_op jit(solution)/shard_map/pallas_call | solution.py:630
  79.7 5.5 %shard_map.266 = (bf16[512,2048]{1,0:T(8,128)(2,1)S(1)}, f32[512,384]{1,0:T(8,128)S(1)}, bf16[512,512]{1,0:T(8,128)(2,1)S(1)}, f32[512,256]{1,0:T(8,128)S(1)}) custom-call(bf16[4,128,2048]{2,1,0:T(8,128)(2,1)} %all-to-all-done.1.refs_0_.refs_2_.refs_8_, bf16[4,128,2048]{2,1,0:T(8,128)(2,1)} %copy-done.43, bf16[2048,1024]{1,0:T(8,128)(2,1)} %bitcast.91, ...), custom_call_target="tpu_custom_call" | custom-call | flops 1610612736 | bytes 8388608 | tf_op jit(solution)/shard_map/pallas_call | solution.py:100
  85.2 1.3 copy-done.22
  86.5 6.5 %shard_map.267 = (f32[2,512,512]{2,1,0:T(8,128)}, f32[512,256]{1,0:T(8,128)S(1)}, bf16[512,256]{1,0:T(8,128)(2,1)S(1)}, bf16[256,2048]{1,0:T(8,128)(2,1)S(1)}, bf16[256,2048]{1,0:T(8,128)(2,1)S(1)}) custom-call(bf16[512,512]{1,0:T(8,128)(2,1)S(1)} %get-tuple-element.88.refs_0_.refs_1_, f32[512,256]{1,0:T(8,128)S(1)} %get-tuple-element.89.refs_1_.refs_3_, ...), custom_call_target="tpu_custom_call" | custom-call | flops 805306368 | bytes 8388608 | tf_op jit(solution)/shard_map/pallas_call | solution.py:100
  93.2 2.6 collective-permute-done.5
  95.8 1.4 add_convert_fusion.3
  97.1 3.5 all-to-all-start.2
  101.5 2.2 copy-done.23
  103.7 1.3 shard_map.268.refs_2_.refs_0_
  105.1 10.6 %all-to-all-done.2.refs_0_ = bf16[4,64,2048]{2,1,0:T(8,128)(2,1)S(1)} async-done(((bf16[4,64,2048]{2,1,0:T(8,128)(2,1)}), bf16[4,64,2048]{2,1,0:T(8,128)(2,1)S(1)}, u32[]{:S(2)}, u32[]{:S(2)}) %all-to-all-start.2) | async-done | bytes 1048608 | tf_op jit(solution)/shard_map/all_to_all | solution.py:773
  117.8 16.6 %all_to_all.35 = bf16[4,64,2048]{2,1,0:T(8,128)(2,1)S(1)} all-to-all(bf16[4,64,2048]{2,1,0:T(8,128)(2,1)S(1)} %get-tuple-element.95), channel_id=1, replica_groups=mesh['shard'=16,'ctx'=4,'tp'=2] {'ctx'}, dimensions={0} | all-to-all | bytes 2097152 | tf_op jit(solution)/shard_map/all_to_all | solution.py:773
  134.4 1.9 collective-permute-start.6
  136.3 2.3 collective-permute-done.6
  138.5 1.3 shard_map.270.refs_7_
  143.5 18.4 %shard_map.271 = (bf16[512,768]{1,0:T(8,128)(2,1)}, bf16[512,768]{1,0:T(8,128)(2,1)}, bf16[512,768]{1,0:T(8,128)(2,1)}, bf16[2048,2304]{1,0:T(8,128)(2,1)}) custom-call(bf16[256,2048]{1,0:T(8,128)(2,1)} %bitcast.84, bf16[256,2048]{1,0:T(8,128)(2,1)} %bitcast.90, bf16[4,128,2048]{2,1,0:T(8,128)(2,1)} %all-to-all-done.1.refs_0_.refs_2_.refs_8_, ...), custom_call_target="tpu_custom_call" | custom-call | flops 9663676416 | bytes 8388608 | tf_op jit(solution)/shard_map/pallas_call | solution.py:100
  164.1 6.0 %shard_map.272 = (bf16[256,2048]{1,0:T(8,128)(2,1)S(1)}, bf16[256,2048]{1,0:T(8,128)(2,1)S(1)}) custom-call(bf16[512,768]{1,0:T(8,128)(2,1)S(1)} %copy-done.30, bf16[512,768]{1,0:T(8,128)(2,1)S(1)} %copy-done.31, bf16[2048,2304]{1,0:T(8,128)(2,1)} %all-gather.5.cloned.1.call-done.refs_4_.refs_5_.refs_6_.refs_2_.refs_3_.refs_1_, ...), custom_call_target="tpu_custom_call" | custom-call | flops 3221225472 | bytes 8388608 | tf_op jit(solution)/shard_map/pallas_call | solution.py:100
  170.9 2.3 collective-permute-done.7
  173.5 18.2 %all_to_all.36.refs_0_ = bf16[4,64,2048]{2,1,0:T(8,128)(2,1)S(1)} all-to-all(bf16[4,64,2048]{2,1,0:T(8,128)(2,1)S(1)} %bitcast.85), channel_id=1, replica_groups=mesh['shard'=16,'ctx'=4,'tp'=2] {'ctx'}, dimensions={0} | all-to-all | bytes 2097152 | tf_op jit(solution)/shard_map/all_to_all | solution.py:773
  195.0 3.5 all-to-all-start.5
  201.0 4.2 %shard_map.274 = (bf16[256,2048]{1,0:T(8,128)(2,1)S(1)}, bf16[256,2048]{1,0:T(8,128)(2,1)S(1)}) custom-call(bf16[512,768]{1,0:T(8,128)(2,1)S(1)} %copy-done.34, bf16[2048,2304]{1,0:T(8,128)(2,1)} %all-gather.5.cloned.1.call-done.refs_4_.refs_5_.refs_6_.refs_2_.refs_3_.refs_1_, bf16[4,64,2048]{2,1,0:T(8,128)(2,1)S(1)} %bitcast.86), custom_call_target="tpu_custom_call" | custom-call | flops 1610612736 | bytes 8388608 | tf_op jit(solution)/shard_map/pallas_call | solution.py:100
  207.1 4.7 %all-to-all-done.5 = bf16[4,64,2048]{2,1,0:T(8,128)(2,1)S(1)} async-done(((bf16[4,64,2048]{2,1,0:T(8,128)(2,1)}), bf16[4,64,2048]{2,1,0:T(8,128)(2,1)S(1)}, u32[]{:S(2)}, u32[]{:S(2)}) %all-to-all-start.5) | async-done | bytes 1048608 | tf_op jit(solution)/shard_map/all_to_all | solution.py:773
  211.9 2.7 collective-permute-start.9
  214.6 2.3 collective-permute-done.9
  218.9 2.2 shard_map.275
  221.3 3.1 shard_map.276
  224.5 4.4 %shard_map.277.refs_3_ = bf16[2048,1024]{1,0:T(8,128)(2,1)} custom-call(bf16[2048,512]{1,0:T(8,128)(2,1)S(1)} %shard_map.268.refs_2_.refs_0_, bf16[256,2048]{1,0:T(8,128)(2,1)S(1)} %bitcast.82, bf16[256,2048]{1,0:T(8,128)(2,1)S(1)} %bitcast.88, bf16[512,512]{1,0:T(8,128)(2,1)S(1)} %get-tuple-element.113.refs_3_.refs_0_, ...), custom_call_target="tpu_custom_call" | custom-call | flops 2147483648 | bytes 8388608 | tf_op jit(solution)/shard_map/pallas_call | solution.py:100
  231.3 4.1 %shard_map.278 = (bf16[256,2048]{1,0:T(8,128)(2,1)S(1)}, bf16[256,2048]{1,0:T(8,128)(2,1)S(1)}) custom-call(bf16[512,512]{1,0:T(8,128)(2,1)S(1)} %copy-done.20, bf16[512,256]{1,0:T(8,128)(2,1)S(1)} %copy-done.27, bf16[2048,1024]{1,0:T(8,128)(2,1)} %bitcast.94, bf16[2048,1024]{1,0:T(8,128)(2,1)} %shard_map.277.refs_3_), custom_call_target="tpu_custom_call" | custom-call | flops 1610612736 | bytes 8388608 | tf_op jit(solution)/shard_map/pallas_call | solution.py:100
  235.9 1.4 add_convert_fusion.1
  238.2 1.4 add_convert_fusion
  239.6 8.5 %reduce-scatter.3.cloned.1.call-done = bf16[128,2304]{1,0:T(8,128)(2,1)} async-done(((bf16[2048,2304]{1,0:T(8,128)(2,1)}), bf16[128,2304]{1,0:T(8,128)(2,1)}) %reduce-scatter.3.cloned.1.call-update) | async-done | bytes 589840 | tf_op jit(solution)/shard_map/reduce_scatter | solution.py:792
  248.1 4.5 %collective-permute-start.14 = (bf16[128,2304]{1,0:T(8,128)(2,1)}, bf16[128,2304]{1,0:T(8,128)(2,1)}, u32[]{:S(2)}, u32[]{:S(2)}) collective-permute-start(bf16[128,2304]{1,0:T(8,128)(2,1)} %reduce-scatter.3.cloned.1.call-done), channel_id=1, source_target_pairs={{8,1},{1,8},{24,17},{17,24},{40,33},{33,40},{56,49},{49,56},{72,65... | collective-permute-start | bytes 1769480 | tf_op jit(solution)/shard_map/ppermute | solution.py:821
  252.6 1.4 constant_dynamic-update-slice_fusion.1
  254.3 6.4 %collective-permute-done.14 = bf16[128,2304]{1,0:T(8,128)(2,1)} collective-permute-done((bf16[128,2304]{1,0:T(8,128)(2,1)}, bf16[128,2304]{1,0:T(8,128)(2,1)}, u32[]{:S(2)}, u32[]{:S(2)}) %collective-permute-start.14) | collective-permute-done | bytes 589856 | tf_op jit(solution)/shard_map/ppermute | solution.py:821
  261.8 1.5 collective-permute-start.15
  263.5 1.3 collective-permute-start.11
  264.8 1.5 collective-permute-start.12
  266.3 2.0 collective-permute-start.13
  268.3 18.8 %collective-permute-done.11.refs_1_ = bf16[128,2048]{1,0:T(8,128)(2,1)S(1)} collective-permute-done((bf16[128,2048]{1,0:T(8,128)(2,1)S(1)}, bf16[128,2048]{1,0:T(8,128)(2,1)S(1)}, u32[]{:S(2)}, u32[]{:S(2)}) %collective-permute-start.11) | collective-permute-done | bytes 524320 | tf_op jit(solution)/shard_map/ppermute | solution.py:776
  287.1 6.8 %collective-permute-done.12.refs_2_ = bf16[128,2048]{1,0:T(8,128)(2,1)S(1)} collective-permute-done((bf16[128,2048]{1,0:T(8,128)(2,1)S(1)}, bf16[128,2048]{1,0:T(8,128)(2,1)S(1)}, u32[]{:S(2)}, u32[]{:S(2)}) %collective-permute-start.12) | collective-permute-done | bytes 524320 | tf_op jit(solution)/shard_map/ppermute | solution.py:776
  300.4 6.5 %all-to-all-start.6 = ((bf16[128,8,128]{2,1,0:T(8,128)(2,1)}), bf16[128,8,128]{2,1,0:T(8,128)(2,1)S(1)}, u32[]{:S(2)}, u32[]{:S(2)}) async-start(bf16[128,8,128]{2,1,0:T(8,128)(2,1)} %bitcast.42), calls=%async_computation.8 | async-start | bytes 524288 | tf_op jit(solution)/shard_map/all_to_all | solution.py:929
  307.7 3.3 collective-permute-done.18.b2
  310.9 7.9 %collective-permute-done.19.b3 = bf16[128,2304]{1,0:T(8,128)(2,1)} collective-permute-done((bf16[128,2304]{1,0:T(8,128)(2,1)S(1)}, bf16[128,2304]{1,0:T(8,128)(2,1)}, u32[]{:S(2)}, u32[]{:S(2)}) %collective-permute-start.19) | collective-permute-done | bytes 589856 | tf_op jit(solution)/shard_map/ppermute | solution.py:776
  318.8 5.5 %shard_map.280 = (f32[128,3072]{1,0:T(8,128)}, f32[128,3072]{1,0:T(8,128)}, f32[3072,128]{1,0:T(8,128)}, f32[128,128]{1,0:T(8,128)}) custom-call(s32[1]{0:T(128)} %bitcast.at.turn_at, bf16[128,2304]{1,0:T(8,128)(2,1)} %copy-done.6, bf16[128,2304]{1,0:T(8,128)(2,1)} %copy-done.48, bf16[128,2304]{1,0:T(8,128)(2,1)} %collective-permute-done.18.b2, ...), custom_call_target="tpu_custom_call" | custom-call | flops 1048576 | bytes 8388608 | tf_op jit(solution)/shard_map/pallas_call | solution.py:695
  325.3 2.6 reduce-scatter.5.cloned.1.call-done
  327.9 4.1 %collective-permute-start.22 = (bf16[128,1024]{1,0:T(8,128)(2,1)}, bf16[128,1024]{1,0:T(8,128)(2,1)S(1)}, u32[]{:S(2)}, u32[]{:S(2)}) collective-permute-start(bf16[128,1024]{1,0:T(8,128)(2,1)} %reduce-scatter.5.cloned.1.call-done), channel_id=1, source_target_pairs={{0,2},{1,10},{2,4},{3,12},{4,6},{5,14},{6,0},{7,8},{8,3},{9,11},{1... | collective-permute-start | bytes 786440 | tf_op jit(solution)/shard_map/ppermute | solution.py:906
  332.0 1.9 collective-permute-start.21
  334.7 2.9 collective-permute-start.20
  337.6 1.4 collective-permute-start.23
  341.0 3.1 collective-permute-done.24
  344.7 1.6 fusion
  348.0 3.2 shard_map.281
  (217 shorter events, 47.7 us)
Async XLA Ops:
  7.2 26.5 %copy-start = (bf16[3072,128]{1,0:T(8,128)(2,1)S(1)}, bf16[3072,128]{1,0:T(8,128)(2,1)}, u32[]{:S(2)}) copy-start(bf16[3072,128]{1,0:T(8,128)(2,1)} %param.30) | copy-start | bytes 2359300
  7.2 59.6 %all-gather.3.cloned.1.call-start = ((), (), s32[]{:S(2)}) async-start(), calls=%async_computation.9 | async-start | bytes 4456448 | tf_op jit(solution)/shard_map/all_gather | solution.py:789
  7.3 4.7 %copy-start.54 = (bf16[8]{0:T(256)(128)(2,1)S(1)}, bf16[8]{0:T(256)(128)(2,1)}, u32[]{:S(2)}) copy-start(bf16[8]{0:T(256)(128)(2,1)} %param.26) | copy-start | bytes 52
  7.3 4.7 %copy-start.55 = (bf16[8]{0:T(256)(128)(2,1)S(1)}, bf16[8]{0:T(256)(128)(2,1)}, u32[]{:S(2)}) copy-start(bf16[8]{0:T(256)(128)(2,1)} %param.25) | copy-start | bytes 52
  9.1 10.6 %copy-start.56 = (bf16[128]{0:T(256)(128)(2,1)S(1)}, bf16[128]{0:T(256)(128)(2,1)}, u32[]{:S(2)}) copy-start(bf16[128]{0:T(256)(128)(2,1)} %param.27) | copy-start | bytes 772
  10.5 9.3 %collective-permute-start.1 = (bf16[128,2048]{1,0:T(8,128)(2,1)S(1)}, bf16[128,2048]{1,0:T(8,128)(2,1)S(1)}, u32[]{:S(2)}, u32[]{:S(2)}) collective-permute-start(bf16[128,2048]{1,0:T(8,128)(2,1)S(1)} %pad_maximum_fusion.2), channel_id=1, source_target_pairs={{0,8},{8,0},{16,24},{24,16},{32,40},{40,32},{48,56},{56,48},{64,72... | collective-permute-start | bytes 1572872 | tf_op jit(solution)/shard_map/ppermute | solution.py:770
  12.6 14.5 %all-to-all-start = ((bf16[16,8,128]{2,1,0:T(8,128)(2,1)}), bf16[16,8,128]{2,1,0:T(8,128)(2,1)S(1)}, u32[]{:S(2)}, u32[]{:S(2)}) async-start(bf16[16,8,128]{2,1,0:T(8,128)(2,1)} %broadcast_in_dim.24), calls=%async_computation | async-start | bytes 65536 | tf_op jit(solution)/shard_map/all_to_all | solution.py:835
  19.9 8.8 %copy-start.44 = (bf16[128,2048]{1,0:T(8,128)(2,1)}, bf16[128,2048]{1,0:T(8,128)(2,1)S(1)}, u32[]{:S(2)}) copy-start(bf16[128,2048]{1,0:T(8,128)(2,1)S(1)} %maximum_select_fusion) | copy-start | bytes 1572868
  28.7 31.1 %all-to-all-start.1 = ((bf16[4,128,2048]{2,1,0:T(8,128)(2,1)}), bf16[4,128,2048]{2,1,0:T(8,128)(2,1)}, u32[]{:S(2)}, u32[]{:S(2)}) async-start(bf16[4,128,2048]{2,1,0:T(8,128)(2,1)} %broadcast_in_dim.25), calls=%async_computation.1 | async-start | bytes 4194304 | tf_op jit(solution)/shard_map/all_to_all | solution.py:773
  33.7 109.8 %all-gather.5.cloned.1.call-start = ((), (), s32[]{:S(2)}) async-start(), calls=%async_computation.10 | async-start | bytes 10027008 | tf_op jit(solution)/shard_map/all_gather | solution.py:789
  35.0 25.8 %copy-start.51 = (s32[1,13]{1,0:T(1,128)S(1)}, s32[1,13]{1,0:T(1,128)}, u32[]{:S(2)}) copy-start(s32[1,13]{1,0:T(1,128)} %param.18) | copy-start | bytes 160
  35.0 25.8 %copy-start.52 = (s32[1,13]{1,0:T(1,128)S(1)}, s32[1,13]{1,0:T(1,128)}, u32[]{:S(2)}) copy-start(s32[1,13]{1,0:T(1,128)} %param.17) | copy-start | bytes 160
  35.2 11.6 %collective-permute-start = (bf16[128,2304]{1,0:T(8,128)(2,1)S(1)}, bf16[128,2304]{1,0:T(8,128)(2,1)S(1)}, u32[]{:S(2)}, u32[]{:S(2)}) collective-permute-start(bf16[128,2304]{1,0:T(8,128)(2,1)S(1)} %pad_maximum_fusion.1), channel_id=1, source_target_pairs={{8,1},{1,8},{24,17},{17,24},{40,33},{33,40},{56,49},{49,56},{72,65... | collective-permute-start | bytes 1769480 | tf_op jit(solution)/shard_map/ppermute | solution.py:853
  60.8 2.4 collective-permute-start.3
  62.4 4.4 %collective-permute-start.2 = (bf16[4,128,2048]{2,1,0:T(8,128)(2,1)}, bf16[4,128,2048]{2,1,0:T(8,128)(2,1)S(1)}, u32[]{:S(2)}, u32[]{:S(2)}) collective-permute-start(bf16[4,128,2048]{2,1,0:T(8,128)(2,1)} %all-to-all-done.1.refs_0_.refs_2_.refs_8_), channel_id=1, source_target_pairs={{0,8},{8,0},{16,24},{24,16},{32,40},{40,32},{48,56},{56,48},{64,72... | collective-permute-start | bytes 6291464 | tf_op jit(solution)/shard_map/ppermute | solution.py:770
  65.3 14.4 %copy-start.8 = (f32[512,128]{1,0:T(8,128)}, f32[512,128]{1,0:T(8,128)S(1)}, u32[]{:S(2)}) copy-start(f32[512,128]{1,0:T(8,128)S(1)} %get-tuple-element.86.refs_4_.refs_5_) | copy-start | bytes 786436
  70.5 4.4 %collective-permute-start.4 = (bf16[8,128,1024]{2,1,0:T(8,128)(2,1)S(1)}, bf16[8,128,1024]{2,1,0:T(8,128)(2,1)}, u32[]{:S(2)}, u32[]{:S(2)}) collective-permute-start(bf16[8,128,1024]{2,1,0:T(8,128)(2,1)S(1)} %shard_map.264), channel_id=1, source_target_pairs={{0,8},{8,0},{16,24},{24,16},{32,40},{40,32},{48,56},{56,48},{64,72... | collective-permute-start | bytes 6291464 | tf_op jit(solution)/shard_map/ppermute | solution.py:770
  86.5 6.5 %copy-start.12 = (f32[512,256]{1,0:T(8,128)}, f32[512,256]{1,0:T(8,128)S(1)}, u32[]{:S(2)}) copy-start(f32[512,256]{1,0:T(8,128)S(1)} %get-tuple-element.89.refs_1_.refs_3_) | copy-start | bytes 1572868
  86.5 6.5 %copy-start.17 = (bf16[512,512]{1,0:T(8,128)(2,1)}, bf16[512,512]{1,0:T(8,128)(2,1)S(1)}, u32[]{:S(2)}) copy-start(bf16[512,512]{1,0:T(8,128)(2,1)S(1)} %get-tuple-element.88.refs_0_.refs_1_) | copy-start | bytes 1572868
  86.5 6.5 %copy-start.32 = (f32[512,384]{1,0:T(8,128)}, f32[512,384]{1,0:T(8,128)S(1)}, u32[]{:S(2)}) copy-start(f32[512,384]{1,0:T(8,128)S(1)} %get-tuple-element.112.refs_3_) | copy-start | bytes 2359300
  93.0 4.1 %copy-start.35 = (f32[512,256]{1,0:T(8,128)}, f32[512,256]{1,0:T(8,128)S(1)}, u32[]{:S(2)}) copy-start(f32[512,256]{1,0:T(8,128)S(1)} %get-tuple-element.110.refs_4_) | copy-start | bytes 1572868
  93.0 4.1 %copy-start.39 = (bf16[512,256]{1,0:T(8,128)(2,1)}, bf16[512,256]{1,0:T(8,128)(2,1)S(1)}, u32[]{:S(2)}) copy-start(bf16[512,256]{1,0:T(8,128)(2,1)S(1)} %get-tuple-element.115.refs_5_) | copy-start | bytes 786436
  93.0 2.7 collective-permute-start.5
  95.8 4.9 %copy-start.45 = (bf16[128,2048]{1,0:T(8,128)(2,1)S(1)}, bf16[128,2048]{1,0:T(8,128)(2,1)}, u32[]{:S(2)}) copy-start(bf16[128,2048]{1,0:T(8,128)(2,1)} %copy-done.44) | copy-start | bytes 1572868
  97.1 18.6 %all-to-all-start.2 = ((bf16[4,64,2048]{2,1,0:T(8,128)(2,1)}), bf16[4,64,2048]{2,1,0:T(8,128)(2,1)S(1)}, u32[]{:S(2)}, u32[]{:S(2)}) async-start(bf16[4,64,2048]{2,1,0:T(8,128)(2,1)} %bitcast.22), calls=%async_computation.2 | async-start | bytes 2097152 | tf_op jit(solution)/shard_map/all_to_all | solution.py:773
  100.7 147.4 %reduce-scatter.3.cloned.1.call-start = ((), (), s32[]{:S(2)}) async-start(), calls=%async_computation.11 | async-start | bytes 10027008 | tf_op jit(solution)/shard_map/reduce_scatter | solution.py:792
  134.4 5.5 %copy-start.2 = (bf16[4,64,2048]{2,1,0:T(8,128)(2,1)}, bf16[4,64,2048]{2,1,0:T(8,128)(2,1)S(1)}, u32[]{:S(2)}) copy-start(bf16[4,64,2048]{2,1,0:T(8,128)(2,1)S(1)} %all_to_all.35) | copy-start | bytes 3145732
  134.4 4.2 %collective-permute-start.6 = (bf16[4,64,2048]{2,1,0:T(8,128)(2,1)S(1)}, bf16[4,64,2048]{2,1,0:T(8,128)(2,1)S(1)}, u32[]{:S(2)}, u32[]{:S(2)}) collective-permute-start(bf16[4,64,2048]{2,1,0:T(8,128)(2,1)S(1)} %all_to_all.35), channel_id=1, source_target_pairs={{0,8},{8,0},{16,24},{24,16},{32,40},{40,32},{48,56},{56,48},{64,72... | collective-permute-start | bytes 3145736 | tf_op jit(solution)/shard_map/ppermute | solution.py:770
  170.1 3.0 collective-permute-start.7
  173.1 19.6 %copy-start.15 = (f32[64,2048]{1,0:T(8,128)S(1)}, f32[64,2048]{1,0:T(8,128)}, u32[]{:S(2)}) copy-start(f32[64,2048]{1,0:T(8,128)} %copy-done.14) | copy-start | bytes 1572868
  173.1 19.6 %copy-start.29 = (bf16[64,2048]{1,0:T(8,128)(2,1)S(1)}, bf16[64,2048]{1,0:T(8,128)(2,1)}, u32[]{:S(2)}) copy-start(bf16[64,2048]{1,0:T(8,128)(2,1)} %get-tuple-element.164.refs_2_) | copy-start | bytes 786436
  195.0 16.9 %all-to-all-start.5 = ((bf16[4,64,2048]{2,1,0:T(8,128)(2,1)}), bf16[4,64,2048]{2,1,0:T(8,128)(2,1)S(1)}, u32[]{:S(2)}, u32[]{:S(2)}) async-start(bf16[4,64,2048]{2,1,0:T(8,128)(2,1)} %copy-done.28), calls=%async_computation.5 | async-start | bytes 2097152 | tf_op jit(solution)/shard_map/all_to_all | solution.py:773
  198.5 129.4 %reduce-scatter.5.cloned.1.call-start = ((), (), s32[]{:S(2)}) async-start(), calls=%async_computation.12 | async-start | bytes 4456448 | tf_op jit(solution)/shard_map/reduce_scatter | solution.py:792
  211.9 5.0 %collective-permute-start.9 = (bf16[4,64,2048]{2,1,0:T(8,128)(2,1)S(1)}, bf16[4,64,2048]{2,1,0:T(8,128)(2,1)S(1)}, u32[]{:S(2)}, u32[]{:S(2)}) collective-permute-start(bf16[4,64,2048]{2,1,0:T(8,128)(2,1)S(1)} %all-to-all-done.5), channel_id=1, source_target_pairs={{0,8},{8,0},{16,24},{24,16},{32,40},{40,32},{48,56},{56,48},{64,72... | collective-permute-start | bytes 3145736 | tf_op jit(solution)/shard_map/ppermute | solution.py:770
  218.9 2.4 copy-start.33
  221.1 3.3 copy-start.26
  221.3 3.1 copy-start.40
  230.9 5.0 %copy-start.25 = (bf16[256,2048]{1,0:T(8,128)(2,1)S(1)}, bf16[256,2048]{1,0:T(8,128)(2,1)}, u32[]{:S(2)}) copy-start(bf16[256,2048]{1,0:T(8,128)(2,1)} %copy-done.24) | copy-start | bytes 3145732
  230.9 5.0 %collective-permute-start.8 = (bf16[256,2048]{1,0:T(8,128)(2,1)S(1)}, bf16[256,2048]{1,0:T(8,128)(2,1)S(1)}, u32[]{:S(2)}, u32[]{:S(2)}) collective-permute-start(bf16[256,2048]{1,0:T(8,128)(2,1)S(1)} %copy-done.42), channel_id=1, source_target_pairs={{0,8},{8,0},{16,24},{24,16},{32,40},{40,32},{48,56},{56,48},{64,72... | collective-permute-start | bytes 3145736 | tf_op jit(solution)/shard_map/ppermute | solution.py:770
  235.5 2.7 collective-permute-start.10
  248.1 12.5 %collective-permute-start.14 = (bf16[128,2304]{1,0:T(8,128)(2,1)}, bf16[128,2304]{1,0:T(8,128)(2,1)}, u32[]{:S(2)}, u32[]{:S(2)}) collective-permute-start(bf16[128,2304]{1,0:T(8,128)(2,1)} %reduce-scatter.3.cloned.1.call-done), channel_id=1, source_target_pairs={{8,1},{1,8},{24,17},{17,24},{40,33},{33,40},{56,49},{49,56},{72,65... | collective-permute-start | bytes 1769480 | tf_op jit(solution)/shard_map/ppermute | solution.py:821
  252.6 8.0 %copy-start.47 = (bf16[128,2304]{1,0:T(8,128)(2,1)S(1)}, bf16[128,2304]{1,0:T(8,128)(2,1)}, u32[]{:S(2)}) copy-start(bf16[128,2304]{1,0:T(8,128)(2,1)} %reduce-scatter.3.cloned.1.call-done) | copy-start | bytes 1769476
  261.8 33.5 %copy-start.6 = (bf16[128,2304]{1,0:T(8,128)(2,1)}, bf16[128,2304]{1,0:T(8,128)(2,1)S(1)}, u32[]{:S(2)}) copy-start(bf16[128,2304]{1,0:T(8,128)(2,1)S(1)} %broadcast_select_fusion.1.refs_7_.b0) | copy-start | bytes 1769476
  261.8 32.1 %copy-start.11 = (bf16[64,2048]{1,0:T(8,128)(2,1)S(1)}, bf16[64,2048]{1,0:T(8,128)(2,1)}, u32[]{:S(2)}) copy-start(bf16[64,2048]{1,0:T(8,128)(2,1)} %get-tuple-element.165.refs_1_.refs_6_) | copy-start | bytes 786436
  261.8 32.0 %copy-start.16 = (f32[64,2048]{1,0:T(8,128)S(1)}, f32[64,2048]{1,0:T(8,128)}, u32[]{:S(2)}) copy-start(f32[64,2048]{1,0:T(8,128)} %copy-done.14) | copy-start | bytes 1572868
  261.8 32.0 %copy-start.38 = (f32[64,2048]{1,0:T(8,128)S(1)}, f32[64,2048]{1,0:T(8,128)}, u32[]{:S(2)}) copy-start(f32[64,2048]{1,0:T(8,128)} %copy-done.37) | copy-start | bytes 1572868
  261.8 32.8 %collective-permute-start.15 = (bf16[128,2304]{1,0:T(8,128)(2,1)S(1)}, bf16[128,2304]{1,0:T(8,128)(2,1)S(1)}, u32[]{:S(2)}, u32[]{:S(2)}) collective-permute-start(bf16[128,2304]{1,0:T(8,128)(2,1)S(1)} %broadcast_select_fusion.1.refs_7_.b0), channel_id=1, source_target_pairs={{0,2},{2,4},{4,6},{6,0},{1,3},{3,5},{5,7},{7,1},{8,10},{10,12},{12... | collective-permute-start | bytes 1769480 | tf_op jit(solution)/shard_map/ppermute | solution.py:776
  263.5 23.5 %collective-permute-start.11 = (bf16[128,2048]{1,0:T(8,128)(2,1)S(1)}, bf16[128,2048]{1,0:T(8,128)(2,1)S(1)}, u32[]{:S(2)}, u32[]{:S(2)}) collective-permute-start(bf16[128,2048]{1,0:T(8,128)(2,1)S(1)} %get-tuple-element.156), channel_id=1, source_target_pairs={{0,2},{2,4},{4,6},{6,0},{1,3},{3,5},{5,7},{7,1},{8,10},{10,12},{12... | collective-permute-start | bytes 1572872 | tf_op jit(solution)/shard_map/ppermute | solution.py:776
  264.8 29.0 %collective-permute-start.12 = (bf16[128,2048]{1,0:T(8,128)(2,1)S(1)}, bf16[128,2048]{1,0:T(8,128)(2,1)S(1)}, u32[]{:S(2)}, u32[]{:S(2)}) collective-permute-start(bf16[128,2048]{1,0:T(8,128)(2,1)S(1)} %get-tuple-element.155), channel_id=1, source_target_pairs={{0,4},{2,6},{4,0},{6,2},{1,5},{3,7},{5,1},{7,3},{8,12},{10,14},{12... | collective-permute-start | bytes 1572872 | tf_op jit(solution)/shard_map/ppermute | solution.py:776
  266.3 27.5 %collective-permute-start.13 = (bf16[128,2048]{1,0:T(8,128)(2,1)S(1)}, bf16[128,2048]{1,0:T(8,128)(2,1)S(1)}, u32[]{:S(2)}, u32[]{:S(2)}) collective-permute-start(bf16[128,2048]{1,0:T(8,128)(2,1)S(1)} %get-tuple-element.154), channel_id=1, source_target_pairs={{0,6},{2,0},{4,2},{6,4},{1,7},{3,1},{5,3},{7,5},{8,14},{10,8},{12,... | collective-permute-start | bytes 1572872 | tf_op jit(solution)/shard_map/ppermute | solution.py:776
  294.6 2.3 copy-start.48
  294.6 2.0 collective-permute-start.16
  294.7 16.2 %collective-permute-start.18 = (bf16[128,2304]{1,0:T(8,128)(2,1)S(1)}, bf16[128,2304]{1,0:T(8,128)(2,1)}, u32[]{:S(2)}, u32[]{:S(2)}) collective-permute-start(bf16[128,2304]{1,0:T(8,128)(2,1)S(1)} %broadcast_select_fusion.1.refs_7_.b0), channel_id=1, source_target_pairs={{0,4},{2,6},{4,0},{6,2},{1,5},{3,7},{5,1},{7,3},{8,12},{10,14},{12... | collective-permute-start | bytes 1769480 | tf_op jit(solution)/shard_map/ppermute | solution.py:776
  295.3 23.5 %collective-permute-start.19 = (bf16[128,2304]{1,0:T(8,128)(2,1)S(1)}, bf16[128,2304]{1,0:T(8,128)(2,1)}, u32[]{:S(2)}, u32[]{:S(2)}) collective-permute-start(bf16[128,2304]{1,0:T(8,128)(2,1)S(1)} %broadcast_select_fusion.1.refs_7_.b0), channel_id=1, source_target_pairs={{0,6},{2,0},{4,2},{6,4},{1,7},{3,1},{5,3},{7,5},{8,14},{10,8},{12,... | collective-permute-start | bytes 1769480 | tf_op jit(solution)/shard_map/ppermute | solution.py:776
  298.0 46.6 %collective-permute-start.17 = (bf16[2,128,2048]{2,1,0:T(8,128)(2,1)}, bf16[2,128,2048]{2,1,0:T(8,128)(2,1)S(1)}, u32[]{:S(2)}, u32[]{:S(2)}) collective-permute-start(bf16[2,128,2048]{2,1,0:T(8,128)(2,1)} %pad_maximum_fusion), channel_id=1, source_target_pairs={{0,1},{9,8},{16,17},{25,24},{32,33},{41,40},{48,49},{57,56},{64,65... | collective-permute-start | bytes 3145736 | tf_op jit(solution)/shard_map/ppermute | solution.py:958
  300.4 38.6 %all-to-all-start.6 = ((bf16[128,8,128]{2,1,0:T(8,128)(2,1)}), bf16[128,8,128]{2,1,0:T(8,128)(2,1)S(1)}, u32[]{:S(2)}, u32[]{:S(2)}) async-start(bf16[128,8,128]{2,1,0:T(8,128)(2,1)} %bitcast.42), calls=%async_computation.8 | async-start | bytes 524288 | tf_op jit(solution)/shard_map/all_to_all | solution.py:929
  306.9 27.0 %copy-start.53 = (bf16[128]{0:T(256)(128)(2,1)S(1)}, bf16[128]{0:T(256)(128)(2,1)}, u32[]{:S(2)}) copy-start(bf16[128]{0:T(256)(128)(2,1)} %param.19) | copy-start | bytes 772
  327.9 11.2 %collective-permute-start.22 = (bf16[128,1024]{1,0:T(8,128)(2,1)}, bf16[128,1024]{1,0:T(8,128)(2,1)S(1)}, u32[]{:S(2)}, u32[]{:S(2)}) collective-permute-start(bf16[128,1024]{1,0:T(8,128)(2,1)} %reduce-scatter.5.cloned.1.call-done), channel_id=1, source_target_pairs={{0,2},{1,10},{2,4},{3,12},{4,6},{5,14},{6,0},{7,8},{8,3},{9,11},{1... | collective-permute-start | bytes 786440 | tf_op jit(solution)/shard_map/ppermute | solution.py:906
  332.0 8.2 %collective-permute-start.21 = (bf16[128,1024]{1,0:T(8,128)(2,1)}, bf16[128,1024]{1,0:T(8,128)(2,1)S(1)}, u32[]{:S(2)}, u32[]{:S(2)}) collective-permute-start(bf16[128,1024]{1,0:T(8,128)(2,1)} %reduce-scatter.5.cloned.1.call-done), channel_id=1, source_target_pairs={{1,8},{3,10},{5,12},{7,14},{8,1},{10,3},{12,5},{14,7},{17,24},{19,... | collective-permute-start | bytes 786440 | tf_op jit(solution)/shard_map/ppermute | solution.py:906
  334.7 11.6 %collective-permute-start.20 = (bf16[128,1024]{1,0:T(8,128)(2,1)}, bf16[128,1024]{1,0:T(8,128)(2,1)S(1)}, u32[]{:S(2)}, u32[]{:S(2)}) collective-permute-start(bf16[128,1024]{1,0:T(8,128)(2,1)} %reduce-scatter.5.cloned.1.call-done), channel_id=1, source_target_pairs={{0,6},{1,14},{2,0},{3,8},{4,2},{5,10},{6,4},{7,12},{8,7},{9,15},{1... | collective-permute-start | bytes 786440 | tf_op jit(solution)/shard_map/ppermute | solution.py:906
  337.6 10.4 %collective-permute-start.23 = (bf16[128,1024]{1,0:T(8,128)(2,1)}, bf16[128,1024]{1,0:T(8,128)(2,1)}, u32[]{:S(2)}, u32[]{:S(2)}) collective-permute-start(bf16[128,1024]{1,0:T(8,128)(2,1)} %reduce-scatter.5.cloned.1.call-done), channel_id=1, source_target_pairs={{0,4},{1,12},{2,6},{3,14},{4,0},{5,8},{6,2},{7,10},{8,5},{9,13},{1... | collective-permute-start | bytes 786440 | tf_op jit(solution)/shard_map/ppermute | solution.py:906
  339.1 7.2 %copy-start.49 = (bf16[128,1024]{1,0:T(8,128)(2,1)}, bf16[128,1024]{1,0:T(8,128)(2,1)S(1)}, u32[]{:S(2)}) copy-start(bf16[128,1024]{1,0:T(8,128)(2,1)S(1)} %collective-permute-done.22.b1) | copy-start | bytes 786436
  339.1 5.0 %collective-permute-start.24 = (f32[128]{0:T(128)S(1)}, f32[128]{0:T(128)S(1)}, u32[]{:S(2)}, u32[]{:S(2)}) collective-permute-start(f32[128]{0:T(128)S(1)} %reduce_sum.104), channel_id=1, source_target_pairs={{0,1},{1,0},{2,3},{3,2},{4,5},{5,4},{6,7},{7,6},{8,9},{9,8},{10,11... | collective-permute-start | bytes 1544 | tf_op jit(solution)/shard_map/ppermute | solution.py:962
  344.6 6.6 %copy-start.1 = (bf16[3072,128]{1,0:T(8,128)(2,1)S(1)}, bf16[3072,128]{1,0:T(8,128)(2,1)}, u32[]{:S(2)}) copy-start(bf16[3072,128]{1,0:T(8,128)(2,1)} %param.30) | copy-start | bytes 2359300
  (27 other events, 35.6 us)
Sparse Core Ops, SparseCore 0:
  10.7 54.5 all-gather.2
  68.2 75.2 all-gather.4
  162.0 86.0 reduce-scatter.2
  251.7 76.2 reduce-scatter.4

commit v14 on v13

--- a/solution.py
+++ b/solution.py
@@ -954,12 +954,11 @@
             True,
         )
         mid_terms = jnp.sum(mid_sums, axis=1)
+        mid_terms = mid_terms + lax.ppermute(mid_terms, "tp", [(0, 1), (1, 0)])
         grad_attn, mid_terms = lax.optimization_barrier((grad_attn, mid_terms))
         full = jnp.where(native, full, lax.ppermute(full, PLANE, across_perm))
         outputs = [full[0].astype(F32), full[1].astype(F32)]
         attn_blocks = owners_at_once(grad_attn)
-        attn_blocks[1], mid_terms = lax.optimization_barrier((attn_blocks[1], mid_terms))
-        mid_terms = mid_terms + lax.ppermute(mid_terms, "tp", [(0, 1), (1, 0)])
         *outputs, attn_blocks[3], end_sums = lax.optimization_barrier(
             (*outputs, attn_blocks[3], end_sums)
         )

time: 361 us -> 362 us (level)
    ppermute x4, waiting for transfers between devices: 1.54 us -> 6.13 us  [owners_at_once(): lax.ppermute(block, ('shard', 'ctx', 'tp'), perm)]
  transfers between devices with their start and end apart: 34 -> 34, of which waited for: 25 -> 24; matrix products, arithmetic and copies ran while one was open for 7% -> 7% of each run, Pallas kernels for 15% -> 15%
where the time goes in v14:
time: 362 us; the launch traced here: 359 us
  waiting for transfers between devices  124 us (34%)
  Pallas kernels  76.2 us (21%)
  starting transfers between devices  60.8 us (17%)
  blocking collectives  34.8 us (10%)
  local copies, waits for them, and re-layouts  33.5 us (9%)
  other arithmetic  15.1 us (4%)
  between operations  14.6 us (4%)
    pallas_call x14, Pallas kernels, call(): return lambda *operands: built(*operands, *behind)  58.5 us
    ppermute x6, waiting for transfers between devices, ctx_turn(): lax.ppermute(value, 'ctx', [(i, (i + by) % n_ctx) for i in range(n_ctx)])  36.7 us
    all_to_all x2, blocking collectives, ctx_exchange(): return lax.all_to_all(value, 'ctx', 0, 0)  34.8 us
    all_to_all x3, waiting for transfers between devices, ctx_exchange(): return lax.all_to_all(value, 'ctx', 0, 0)  28.3 us
    unnamed x117, local copies, waits for them, and re-layouts  24.2 us
    ppermute x11, waiting for transfers between devices, core_swap(): return lax.ppermute(value, 'shard', core_perm)  17.5 us
    all_to_all x3, starting transfers between devices, ctx_exchange(): return lax.all_to_all(value, 'ctx', 0, 0)  12.1 us
    ppermute x11, starting transfers between devices, core_swap(): return lax.ppermute(value, 'shard', core_perm)  9.79 us
  transfers between devices with their start and end apart: 34, of which 24 were waited for; matrix products, arithmetic and copies ran while one was open for 7% of the time, Pallas kernels for 15%

profile of v14, /device:TPU:1, one launch (start us, length us, event | category | flops | bytes accessed | tf_op | source)
XLA Modules:
  0.0 358.6 jit_solution(982259454534335025)
XLA Ops:
  7.3 1.8 shard_map.263
  10.5 1.5 collective-permute-start.1
  12.6 7.1 %all-to-all-start = ((bf16[16,8,128]{2,1,0:T(8,128)(2,1)}), bf16[16,8,128]{2,1,0:T(8,128)(2,1)S(1)}, u32[]{:S(2)}, u32[]{:S(2)}) async-start(bf16[16,8,128]{2,1,0:T(8,128)(2,1)} %broadcast_in_dim.24), calls=%async_computation | async-start | bytes 65536 | tf_op jit(solution)/shard_map/all_to_all | solution.py:835
  19.9 7.2 %all-to-all-done = bf16[16,8,128]{2,1,0:T(8,128)(2,1)S(1)} async-done(((bf16[16,8,128]{2,1,0:T(8,128)(2,1)}), bf16[16,8,128]{2,1,0:T(8,128)(2,1)S(1)}, u32[]{:S(2)}, u32[]{:S(2)}) %all-to-all-start) | async-done | bytes 32800 | tf_op jit(solution)/shard_map/all_to_all | solution.py:835
  27.1 1.6 broadcast_in_dim.25
  28.7 5.0 %all-to-all-start.1 = ((bf16[4,128,2048]{2,1,0:T(8,128)(2,1)}), bf16[4,128,2048]{2,1,0:T(8,128)(2,1)}, u32[]{:S(2)}, u32[]{:S(2)}) async-start(bf16[4,128,2048]{2,1,0:T(8,128)(2,1)} %broadcast_in_dim.25), calls=%async_computation.1 | async-start | bytes 4194304 | tf_op jit(solution)/shard_map/all_to_all | solution.py:773
  35.2 2.9 collective-permute-start
  38.0 8.7 %collective-permute-done = bf16[128,2304]{1,0:T(8,128)(2,1)S(1)} collective-permute-done((bf16[128,2304]{1,0:T(8,128)(2,1)S(1)}, bf16[128,2304]{1,0:T(8,128)(2,1)S(1)}, u32[]{:S(2)}, u32[]{:S(2)}) %collective-permute-start) | collective-permute-done | bytes 589856 | tf_op jit(solution)/shard_map/ppermute | solution.py:853
  46.8 13.0 %all-to-all-done.1.refs_0_.refs_2_.refs_8_ = bf16[4,128,2048]{2,1,0:T(8,128)(2,1)} async-done(((bf16[4,128,2048]{2,1,0:T(8,128)(2,1)}), bf16[4,128,2048]{2,1,0:T(8,128)(2,1)}, u32[]{:S(2)}, u32[]{:S(2)}) %all-to-all-start.1) | async-done | bytes 2097184 | tf_op jit(solution)/shard_map/all_to_all | solution.py:773
  60.8 1.6 collective-permute-start.3
  65.3 1.5 collective-permute-done.2.refs_1_.refs_3_.refs_9_
  68.1 2.4 shard_map.264
  71.0 3.9 %collective-permute-done.4.other = bf16[8,128,1024]{2,1,0:T(8,128)(2,1)} collective-permute-done((bf16[8,128,1024]{2,1,0:T(8,128)(2,1)S(1)}, bf16[8,128,1024]{2,1,0:T(8,128)(2,1)}, u32[]{:S(2)}, u32[]{:S(2)}) %collective-permute-start.4) | collective-permute-done | bytes 2097184 | tf_op jit(solution)/shard_map/ppermute | solution.py:770
  74.9 4.8 %shard_map.265 = bf16[8,2,128,1024]{3,2,1,0:T(8,128)(2,1)} custom-call(s32[1]{0:T(128)} %bitcast.18.core, bf16[8,2,128,1024]{3,2,1,0:T(8,128)(2,1)} %bitcast.96, bf16[8,128,1024]{2,1,0:T(8,128)(2,1)} %collective-permute-done.4.other), custom_call_target="tpu_custom_call" | custom-call | flops 1048576 | bytes 8388608 | tf_op jit(solution)/shard_map/pallas_call | solution.py:630
  79.7 5.5 %shard_map.266 = (bf16[512,2048]{1,0:T(8,128)(2,1)S(1)}, f32[512,384]{1,0:T(8,128)S(1)}, bf16[512,512]{1,0:T(8,128)(2,1)S(1)}, f32[512,256]{1,0:T(8,128)S(1)}) custom-call(bf16[4,128,2048]{2,1,0:T(8,128)(2,1)} %all-to-all-done.1.refs_0_.refs_2_.refs_8_, bf16[4,128,2048]{2,1,0:T(8,128)(2,1)} %copy-done.43, bf16[2048,1024]{1,0:T(8,128)(2,1)} %bitcast.91, ...), custom_call_target="tpu_custom_call" | custom-call | flops 1610612736 | bytes 8388608 | tf_op jit(solution)/shard_map/pallas_call | solution.py:100
  85.2 1.3 copy-done.22
  86.5 6.5 %shard_map.267 = (f32[2,512,512]{2,1,0:T(8,128)}, f32[512,256]{1,0:T(8,128)S(1)}, bf16[512,256]{1,0:T(8,128)(2,1)S(1)}, bf16[256,2048]{1,0:T(8,128)(2,1)S(1)}, bf16[256,2048]{1,0:T(8,128)(2,1)S(1)}) custom-call(bf16[512,512]{1,0:T(8,128)(2,1)S(1)} %get-tuple-element.86.refs_0_.refs_1_, f32[512,256]{1,0:T(8,128)S(1)} %get-tuple-element.87.refs_1_.refs_3_, ...), custom_call_target="tpu_custom_call" | custom-call | flops 805306368 | bytes 8388608 | tf_op jit(solution)/shard_map/pallas_call | solution.py:100
  93.2 2.6 collective-permute-done.5
  95.8 1.4 add_convert_fusion.3
  97.1 3.5 all-to-all-start.2
  101.5 2.2 copy-done.23
  103.7 1.3 shard_map.268.refs_2_.refs_0_
  105.1 10.6 %all-to-all-done.2.refs_0_ = bf16[4,64,2048]{2,1,0:T(8,128)(2,1)S(1)} async-done(((bf16[4,64,2048]{2,1,0:T(8,128)(2,1)}), bf16[4,64,2048]{2,1,0:T(8,128)(2,1)S(1)}, u32[]{:S(2)}, u32[]{:S(2)}) %all-to-all-start.2) | async-done | bytes 1048608 | tf_op jit(solution)/shard_map/all_to_all | solution.py:773
  117.8 16.6 %all_to_all.35 = bf16[4,64,2048]{2,1,0:T(8,128)(2,1)S(1)} all-to-all(bf16[4,64,2048]{2,1,0:T(8,128)(2,1)S(1)} %get-tuple-element.93), channel_id=1, replica_groups=mesh['shard'=16,'ctx'=4,'tp'=2] {'ctx'}, dimensions={0} | all-to-all | bytes 2097152 | tf_op jit(solution)/shard_map/all_to_all | solution.py:773
  134.4 1.9 collective-permute-start.6
  136.3 2.3 collective-permute-done.6
  138.5 1.3 shard_map.270.refs_7_
  143.5 18.4 %shard_map.271 = (bf16[512,768]{1,0:T(8,128)(2,1)}, bf16[512,768]{1,0:T(8,128)(2,1)}, bf16[512,768]{1,0:T(8,128)(2,1)}, bf16[2048,2304]{1,0:T(8,128)(2,1)}) custom-call(bf16[256,2048]{1,0:T(8,128)(2,1)} %bitcast.84, bf16[256,2048]{1,0:T(8,128)(2,1)} %bitcast.90, bf16[4,128,2048]{2,1,0:T(8,128)(2,1)} %all-to-all-done.1.refs_0_.refs_2_.refs_8_, ...), custom_call_target="tpu_custom_call" | custom-call | flops 9663676416 | bytes 8388608 | tf_op jit(solution)/shard_map/pallas_call | solution.py:100
  164.1 6.0 %shard_map.272 = (bf16[256,2048]{1,0:T(8,128)(2,1)S(1)}, bf16[256,2048]{1,0:T(8,128)(2,1)S(1)}) custom-call(bf16[512,768]{1,0:T(8,128)(2,1)S(1)} %copy-done.30, bf16[512,768]{1,0:T(8,128)(2,1)S(1)} %copy-done.31, bf16[2048,2304]{1,0:T(8,128)(2,1)} %all-gather.5.cloned.1.call-done.refs_4_.refs_5_.refs_6_.refs_2_.refs_3_.refs_1_, ...), custom_call_target="tpu_custom_call" | custom-call | flops 3221225472 | bytes 8388608 | tf_op jit(solution)/shard_map/pallas_call | solution.py:100
  170.9 2.3 collective-permute-done.7
  173.5 18.2 %all_to_all.36.refs_0_ = bf16[4,64,2048]{2,1,0:T(8,128)(2,1)S(1)} all-to-all(bf16[4,64,2048]{2,1,0:T(8,128)(2,1)S(1)} %bitcast.85), channel_id=1, replica_groups=mesh['shard'=16,'ctx'=4,'tp'=2] {'ctx'}, dimensions={0} | all-to-all | bytes 2097152 | tf_op jit(solution)/shard_map/all_to_all | solution.py:773
  195.0 3.5 all-to-all-start.5
  201.0 4.2 %shard_map.274 = (bf16[256,2048]{1,0:T(8,128)(2,1)S(1)}, bf16[256,2048]{1,0:T(8,128)(2,1)S(1)}) custom-call(bf16[512,768]{1,0:T(8,128)(2,1)S(1)} %copy-done.34, bf16[2048,2304]{1,0:T(8,128)(2,1)} %all-gather.5.cloned.1.call-done.refs_4_.refs_5_.refs_6_.refs_2_.refs_3_.refs_1_, bf16[4,64,2048]{2,1,0:T(8,128)(2,1)S(1)} %bitcast.86), custom_call_target="tpu_custom_call" | custom-call | flops 1610612736 | bytes 8388608 | tf_op jit(solution)/shard_map/pallas_call | solution.py:100
  207.1 4.7 %all-to-all-done.5 = bf16[4,64,2048]{2,1,0:T(8,128)(2,1)S(1)} async-done(((bf16[4,64,2048]{2,1,0:T(8,128)(2,1)}), bf16[4,64,2048]{2,1,0:T(8,128)(2,1)S(1)}, u32[]{:S(2)}, u32[]{:S(2)}) %all-to-all-start.5) | async-done | bytes 1048608 | tf_op jit(solution)/shard_map/all_to_all | solution.py:773
  211.9 2.7 collective-permute-start.9
  214.6 2.3 collective-permute-done.9
  218.9 2.2 shard_map.275
  221.3 3.1 shard_map.276
  224.5 4.4 %shard_map.277.refs_3_ = bf16[2048,1024]{1,0:T(8,128)(2,1)} custom-call(bf16[2048,512]{1,0:T(8,128)(2,1)S(1)} %shard_map.268.refs_2_.refs_0_, bf16[256,2048]{1,0:T(8,128)(2,1)S(1)} %bitcast.82, bf16[256,2048]{1,0:T(8,128)(2,1)S(1)} %bitcast.88, bf16[512,512]{1,0:T(8,128)(2,1)S(1)} %get-tuple-element.111.refs_3_.refs_0_, ...), custom_call_target="tpu_custom_call" | custom-call | flops 2147483648 | bytes 8388608 | tf_op jit(solution)/shard_map/pallas_call | solution.py:100
  231.3 4.1 %shard_map.278 = (bf16[256,2048]{1,0:T(8,128)(2,1)S(1)}, bf16[256,2048]{1,0:T(8,128)(2,1)S(1)}) custom-call(bf16[512,512]{1,0:T(8,128)(2,1)S(1)} %copy-done.20, bf16[512,256]{1,0:T(8,128)(2,1)S(1)} %copy-done.27, bf16[2048,1024]{1,0:T(8,128)(2,1)} %bitcast.94, bf16[2048,1024]{1,0:T(8,128)(2,1)} %shard_map.277.refs_3_), custom_call_target="tpu_custom_call" | custom-call | flops 1610612736 | bytes 8388608 | tf_op jit(solution)/shard_map/pallas_call | solution.py:100
  235.9 1.4 add_convert_fusion.1
  238.2 1.4 add_convert_fusion
  239.6 8.5 %reduce-scatter.3.cloned.1.call-done = bf16[128,2304]{1,0:T(8,128)(2,1)} async-done(((bf16[2048,2304]{1,0:T(8,128)(2,1)}), bf16[128,2304]{1,0:T(8,128)(2,1)}) %reduce-scatter.3.cloned.1.call-update) | async-done | bytes 589840 | tf_op jit(solution)/shard_map/reduce_scatter | solution.py:792
  248.1 4.5 %collective-permute-start.14 = (bf16[128,2304]{1,0:T(8,128)(2,1)}, bf16[128,2304]{1,0:T(8,128)(2,1)}, u32[]{:S(2)}, u32[]{:S(2)}) collective-permute-start(bf16[128,2304]{1,0:T(8,128)(2,1)} %reduce-scatter.3.cloned.1.call-done), channel_id=1, source_target_pairs={{8,1},{1,8},{24,17},{17,24},{40,33},{33,40},{56,49},{49,56},{72,65... | collective-permute-start | bytes 1769480 | tf_op jit(solution)/shard_map/ppermute | solution.py:821
  252.6 1.4 constant_dynamic-update-slice_fusion.1
  254.3 6.4 %collective-permute-done.14 = bf16[128,2304]{1,0:T(8,128)(2,1)} collective-permute-done((bf16[128,2304]{1,0:T(8,128)(2,1)}, bf16[128,2304]{1,0:T(8,128)(2,1)}, u32[]{:S(2)}, u32[]{:S(2)}) %collective-permute-start.14) | collective-permute-done | bytes 589856 | tf_op jit(solution)/shard_map/ppermute | solution.py:821
  261.8 1.5 collective-permute-start.15
  263.5 1.3 collective-permute-start.11
  264.8 1.5 collective-permute-start.12
  266.3 2.0 collective-permute-start.13
  268.3 18.8 %collective-permute-done.11.refs_1_ = bf16[128,2048]{1,0:T(8,128)(2,1)S(1)} collective-permute-done((bf16[128,2048]{1,0:T(8,128)(2,1)S(1)}, bf16[128,2048]{1,0:T(8,128)(2,1)S(1)}, u32[]{:S(2)}, u32[]{:S(2)}) %collective-permute-start.11) | collective-permute-done | bytes 524320 | tf_op jit(solution)/shard_map/ppermute | solution.py:776
  287.1 6.8 %collective-permute-done.12.refs_2_ = bf16[128,2048]{1,0:T(8,128)(2,1)S(1)} collective-permute-done((bf16[128,2048]{1,0:T(8,128)(2,1)S(1)}, bf16[128,2048]{1,0:T(8,128)(2,1)S(1)}, u32[]{:S(2)}, u32[]{:S(2)}) %collective-permute-start.12) | collective-permute-done | bytes 524320 | tf_op jit(solution)/shard_map/ppermute | solution.py:776
  300.4 6.5 %all-to-all-start.6 = ((bf16[128,8,128]{2,1,0:T(8,128)(2,1)}), bf16[128,8,128]{2,1,0:T(8,128)(2,1)S(1)}, u32[]{:S(2)}, u32[]{:S(2)}) async-start(bf16[128,8,128]{2,1,0:T(8,128)(2,1)} %bitcast.42), calls=%async_computation.8 | async-start | bytes 524288 | tf_op jit(solution)/shard_map/all_to_all | solution.py:929
  307.7 3.3 collective-permute-done.18.b2
  310.9 7.9 %collective-permute-done.19.b3 = bf16[128,2304]{1,0:T(8,128)(2,1)} collective-permute-done((bf16[128,2304]{1,0:T(8,128)(2,1)S(1)}, bf16[128,2304]{1,0:T(8,128)(2,1)}, u32[]{:S(2)}, u32[]{:S(2)}) %collective-permute-start.19) | collective-permute-done | bytes 589856 | tf_op jit(solution)/shard_map/ppermute | solution.py:776
  318.8 5.5 %shard_map.280 = (f32[128,3072]{1,0:T(8,128)}, f32[128,3072]{1,0:T(8,128)}, f32[3072,128]{1,0:T(8,128)}, f32[128,128]{1,0:T(8,128)}) custom-call(s32[1]{0:T(128)} %bitcast.at.turn_at, bf16[128,2304]{1,0:T(8,128)(2,1)} %copy-done.6, bf16[128,2304]{1,0:T(8,128)(2,1)} %copy-done.48, bf16[128,2304]{1,0:T(8,128)(2,1)} %collective-permute-done.18.b2, ...), custom_call_target="tpu_custom_call" | custom-call | flops 1048576 | bytes 8388608 | tf_op jit(solution)/shard_map/pallas_call | solution.py:695
  325.4 2.8 collective-permute-done.20
  328.7 4.3 %collective-permute-start.22 = (bf16[128,1024]{1,0:T(8,128)(2,1)}, bf16[128,1024]{1,0:T(8,128)(2,1)S(1)}, u32[]{:S(2)}, u32[]{:S(2)}) collective-permute-start(bf16[128,1024]{1,0:T(8,128)(2,1)} %reduce-scatter.5.cloned.1.call-done), channel_id=1, source_target_pairs={{1,8},{3,10},{5,12},{7,14},{8,1},{10,3},{12,5},{14,7},{17,24},{19,... | collective-permute-start | bytes 786440 | tf_op jit(solution)/shard_map/ppermute | solution.py:906
  333.7 2.4 collective-permute-start.21
  336.4 2.6 collective-permute-start.24
  340.0 1.6 fusion
  342.7 3.6 collective-permute-done.23.b1
  346.2 2.6 collective-permute-done.24.b2
  348.8 3.2 shard_map.281
  (217 shorter events, 46.4 us)
Async XLA Ops:
  7.2 26.5 %copy-start = (bf16[3072,128]{1,0:T(8,128)(2,1)S(1)}, bf16[3072,128]{1,0:T(8,128)(2,1)}, u32[]{:S(2)}) copy-start(bf16[3072,128]{1,0:T(8,128)(2,1)} %param.30) | copy-start | bytes 2359300
  7.2 59.6 %all-gather.3.cloned.1.call-start = ((), (), s32[]{:S(2)}) async-start(), calls=%async_computation.9 | async-start | bytes 4456448 | tf_op jit(solution)/shard_map/all_gather | solution.py:789
  7.3 4.7 %copy-start.54 = (bf16[8]{0:T(256)(128)(2,1)S(1)}, bf16[8]{0:T(256)(128)(2,1)}, u32[]{:S(2)}) copy-start(bf16[8]{0:T(256)(128)(2,1)} %param.26) | copy-start | bytes 52
  7.3 4.7 %copy-start.55 = (bf16[8]{0:T(256)(128)(2,1)S(1)}, bf16[8]{0:T(256)(128)(2,1)}, u32[]{:S(2)}) copy-start(bf16[8]{0:T(256)(128)(2,1)} %param.25) | copy-start | bytes 52
  9.1 10.6 %copy-start.56 = (bf16[128]{0:T(256)(128)(2,1)S(1)}, bf16[128]{0:T(256)(128)(2,1)}, u32[]{:S(2)}) copy-start(bf16[128]{0:T(256)(128)(2,1)} %param.27) | copy-start | bytes 772
  10.5 9.3 %collective-permute-start.1 = (bf16[128,2048]{1,0:T(8,128)(2,1)S(1)}, bf16[128,2048]{1,0:T(8,128)(2,1)S(1)}, u32[]{:S(2)}, u32[]{:S(2)}) collective-permute-start(bf16[128,2048]{1,0:T(8,128)(2,1)S(1)} %pad_maximum_fusion.2), channel_id=1, source_target_pairs={{0,8},{8,0},{16,24},{24,16},{32,40},{40,32},{48,56},{56,48},{64,72... | collective-permute-start | bytes 1572872 | tf_op jit(solution)/shard_map/ppermute | solution.py:770
  12.6 14.5 %all-to-all-start = ((bf16[16,8,128]{2,1,0:T(8,128)(2,1)}), bf16[16,8,128]{2,1,0:T(8,128)(2,1)S(1)}, u32[]{:S(2)}, u32[]{:S(2)}) async-start(bf16[16,8,128]{2,1,0:T(8,128)(2,1)} %broadcast_in_dim.24), calls=%async_computation | async-start | bytes 65536 | tf_op jit(solution)/shard_map/all_to_all | solution.py:835
  19.9 8.8 %copy-start.44 = (bf16[128,2048]{1,0:T(8,128)(2,1)}, bf16[128,2048]{1,0:T(8,128)(2,1)S(1)}, u32[]{:S(2)}) copy-start(bf16[128,2048]{1,0:T(8,128)(2,1)S(1)} %maximum_select_fusion) | copy-start | bytes 1572868
  28.7 31.1 %all-to-all-start.1 = ((bf16[4,128,2048]{2,1,0:T(8,128)(2,1)}), bf16[4,128,2048]{2,1,0:T(8,128)(2,1)}, u32[]{:S(2)}, u32[]{:S(2)}) async-start(bf16[4,128,2048]{2,1,0:T(8,128)(2,1)} %broadcast_in_dim.25), calls=%async_computation.1 | async-start | bytes 4194304 | tf_op jit(solution)/shard_map/all_to_all | solution.py:773
  33.7 109.8 %all-gather.5.cloned.1.call-start = ((), (), s32[]{:S(2)}) async-start(), calls=%async_computation.10 | async-start | bytes 10027008 | tf_op jit(solution)/shard_map/all_gather | solution.py:789
  35.0 25.8 %copy-start.51 = (s32[1,13]{1,0:T(1,128)S(1)}, s32[1,13]{1,0:T(1,128)}, u32[]{:S(2)}) copy-start(s32[1,13]{1,0:T(1,128)} %param.18) | copy-start | bytes 160
  35.0 25.8 %copy-start.52 = (s32[1,13]{1,0:T(1,128)S(1)}, s32[1,13]{1,0:T(1,128)}, u32[]{:S(2)}) copy-start(s32[1,13]{1,0:T(1,128)} %param.17) | copy-start | bytes 160
  35.2 11.6 %collective-permute-start = (bf16[128,2304]{1,0:T(8,128)(2,1)S(1)}, bf16[128,2304]{1,0:T(8,128)(2,1)S(1)}, u32[]{:S(2)}, u32[]{:S(2)}) collective-permute-start(bf16[128,2304]{1,0:T(8,128)(2,1)S(1)} %pad_maximum_fusion.1), channel_id=1, source_target_pairs={{8,1},{1,8},{24,17},{17,24},{40,33},{33,40},{56,49},{49,56},{72,65... | collective-permute-start | bytes 1769480 | tf_op jit(solution)/shard_map/ppermute | solution.py:853
  60.8 2.4 collective-permute-start.3
  62.4 4.4 %collective-permute-start.2 = (bf16[4,128,2048]{2,1,0:T(8,128)(2,1)}, bf16[4,128,2048]{2,1,0:T(8,128)(2,1)S(1)}, u32[]{:S(2)}, u32[]{:S(2)}) collective-permute-start(bf16[4,128,2048]{2,1,0:T(8,128)(2,1)} %all-to-all-done.1.refs_0_.refs_2_.refs_8_), channel_id=1, source_target_pairs={{0,8},{8,0},{16,24},{24,16},{32,40},{40,32},{48,56},{56,48},{64,72... | collective-permute-start | bytes 6291464 | tf_op jit(solution)/shard_map/ppermute | solution.py:770
  65.3 14.4 %copy-start.8 = (f32[512,128]{1,0:T(8,128)}, f32[512,128]{1,0:T(8,128)S(1)}, u32[]{:S(2)}) copy-start(f32[512,128]{1,0:T(8,128)S(1)} %get-tuple-element.84.refs_4_.refs_5_) | copy-start | bytes 786436
  70.5 4.4 %collective-permute-start.4 = (bf16[8,128,1024]{2,1,0:T(8,128)(2,1)S(1)}, bf16[8,128,1024]{2,1,0:T(8,128)(2,1)}, u32[]{:S(2)}, u32[]{:S(2)}) collective-permute-start(bf16[8,128,1024]{2,1,0:T(8,128)(2,1)S(1)} %shard_map.264), channel_id=1, source_target_pairs={{0,8},{8,0},{16,24},{24,16},{32,40},{40,32},{48,56},{56,48},{64,72... | collective-permute-start | bytes 6291464 | tf_op jit(solution)/shard_map/ppermute | solution.py:770
  86.5 6.5 %copy-start.12 = (f32[512,256]{1,0:T(8,128)}, f32[512,256]{1,0:T(8,128)S(1)}, u32[]{:S(2)}) copy-start(f32[512,256]{1,0:T(8,128)S(1)} %get-tuple-element.87.refs_1_.refs_3_) | copy-start | bytes 1572868
  86.5 6.5 %copy-start.17 = (bf16[512,512]{1,0:T(8,128)(2,1)}, bf16[512,512]{1,0:T(8,128)(2,1)S(1)}, u32[]{:S(2)}) copy-start(bf16[512,512]{1,0:T(8,128)(2,1)S(1)} %get-tuple-element.86.refs_0_.refs_1_) | copy-start | bytes 1572868
  86.5 6.5 %copy-start.32 = (f32[512,384]{1,0:T(8,128)}, f32[512,384]{1,0:T(8,128)S(1)}, u32[]{:S(2)}) copy-start(f32[512,384]{1,0:T(8,128)S(1)} %get-tuple-element.110.refs_3_) | copy-start | bytes 2359300
  93.0 4.1 %copy-start.35 = (f32[512,256]{1,0:T(8,128)}, f32[512,256]{1,0:T(8,128)S(1)}, u32[]{:S(2)}) copy-start(f32[512,256]{1,0:T(8,128)S(1)} %get-tuple-element.108.refs_4_) | copy-start | bytes 1572868
  93.0 4.1 %copy-start.39 = (bf16[512,256]{1,0:T(8,128)(2,1)}, bf16[512,256]{1,0:T(8,128)(2,1)S(1)}, u32[]{:S(2)}) copy-start(bf16[512,256]{1,0:T(8,128)(2,1)S(1)} %get-tuple-element.113.refs_5_) | copy-start | bytes 786436
  93.0 2.7 collective-permute-start.5
  95.8 4.9 %copy-start.45 = (bf16[128,2048]{1,0:T(8,128)(2,1)S(1)}, bf16[128,2048]{1,0:T(8,128)(2,1)}, u32[]{:S(2)}) copy-start(bf16[128,2048]{1,0:T(8,128)(2,1)} %copy-done.44) | copy-start | bytes 1572868
  97.1 18.6 %all-to-all-start.2 = ((bf16[4,64,2048]{2,1,0:T(8,128)(2,1)}), bf16[4,64,2048]{2,1,0:T(8,128)(2,1)S(1)}, u32[]{:S(2)}, u32[]{:S(2)}) async-start(bf16[4,64,2048]{2,1,0:T(8,128)(2,1)} %bitcast.22), calls=%async_computation.2 | async-start | bytes 2097152 | tf_op jit(solution)/shard_map/all_to_all | solution.py:773
  100.7 147.4 %reduce-scatter.3.cloned.1.call-start = ((), (), s32[]{:S(2)}) async-start(), calls=%async_computation.11 | async-start | bytes 10027008 | tf_op jit(solution)/shard_map/reduce_scatter | solution.py:792
  134.4 5.5 %copy-start.2 = (bf16[4,64,2048]{2,1,0:T(8,128)(2,1)}, bf16[4,64,2048]{2,1,0:T(8,128)(2,1)S(1)}, u32[]{:S(2)}) copy-start(bf16[4,64,2048]{2,1,0:T(8,128)(2,1)S(1)} %all_to_all.35) | copy-start | bytes 3145732
  134.4 4.2 %collective-permute-start.6 = (bf16[4,64,2048]{2,1,0:T(8,128)(2,1)S(1)}, bf16[4,64,2048]{2,1,0:T(8,128)(2,1)S(1)}, u32[]{:S(2)}, u32[]{:S(2)}) collective-permute-start(bf16[4,64,2048]{2,1,0:T(8,128)(2,1)S(1)} %all_to_all.35), channel_id=1, source_target_pairs={{0,8},{8,0},{16,24},{24,16},{32,40},{40,32},{48,56},{56,48},{64,72... | collective-permute-start | bytes 3145736 | tf_op jit(solution)/shard_map/ppermute | solution.py:770
  170.1 3.0 collective-permute-start.7
  173.1 19.6 %copy-start.15 = (f32[64,2048]{1,0:T(8,128)S(1)}, f32[64,2048]{1,0:T(8,128)}, u32[]{:S(2)}) copy-start(f32[64,2048]{1,0:T(8,128)} %copy-done.14) | copy-start | bytes 1572868
  173.1 19.6 %copy-start.29 = (bf16[64,2048]{1,0:T(8,128)(2,1)S(1)}, bf16[64,2048]{1,0:T(8,128)(2,1)}, u32[]{:S(2)}) copy-start(bf16[64,2048]{1,0:T(8,128)(2,1)} %get-tuple-element.160.refs_2_) | copy-start | bytes 786436
  195.0 16.9 %all-to-all-start.5 = ((bf16[4,64,2048]{2,1,0:T(8,128)(2,1)}), bf16[4,64,2048]{2,1,0:T(8,128)(2,1)S(1)}, u32[]{:S(2)}, u32[]{:S(2)}) async-start(bf16[4,64,2048]{2,1,0:T(8,128)(2,1)} %copy-done.28), calls=%async_computation.5 | async-start | bytes 2097152 | tf_op jit(solution)/shard_map/all_to_all | solution.py:773
  198.5 130.1 %reduce-scatter.5.cloned.1.call-start = ((), (), s32[]{:S(2)}) async-start(), calls=%async_computation.12 | async-start | bytes 4456448 | tf_op jit(solution)/shard_map/reduce_scatter | solution.py:792
  211.9 5.0 %collective-permute-start.9 = (bf16[4,64,2048]{2,1,0:T(8,128)(2,1)S(1)}, bf16[4,64,2048]{2,1,0:T(8,128)(2,1)S(1)}, u32[]{:S(2)}, u32[]{:S(2)}) collective-permute-start(bf16[4,64,2048]{2,1,0:T(8,128)(2,1)S(1)} %all-to-all-done.5), channel_id=1, source_target_pairs={{0,8},{8,0},{16,24},{24,16},{32,40},{40,32},{48,56},{56,48},{64,72... | collective-permute-start | bytes 3145736 | tf_op jit(solution)/shard_map/ppermute | solution.py:770
  218.9 2.4 copy-start.33
  221.1 3.3 copy-start.26
  221.3 3.1 copy-start.40
  230.9 5.0 %copy-start.25 = (bf16[256,2048]{1,0:T(8,128)(2,1)S(1)}, bf16[256,2048]{1,0:T(8,128)(2,1)}, u32[]{:S(2)}) copy-start(bf16[256,2048]{1,0:T(8,128)(2,1)} %copy-done.24) | copy-start | bytes 3145732
  230.9 5.0 %collective-permute-start.8 = (bf16[256,2048]{1,0:T(8,128)(2,1)S(1)}, bf16[256,2048]{1,0:T(8,128)(2,1)S(1)}, u32[]{:S(2)}, u32[]{:S(2)}) collective-permute-start(bf16[256,2048]{1,0:T(8,128)(2,1)S(1)} %copy-done.42), channel_id=1, source_target_pairs={{0,8},{8,0},{16,24},{24,16},{32,40},{40,32},{48,56},{56,48},{64,72... | collective-permute-start | bytes 3145736 | tf_op jit(solution)/shard_map/ppermute | solution.py:770
  235.5 2.7 collective-permute-start.10
  248.1 12.5 %collective-permute-start.14 = (bf16[128,2304]{1,0:T(8,128)(2,1)}, bf16[128,2304]{1,0:T(8,128)(2,1)}, u32[]{:S(2)}, u32[]{:S(2)}) collective-permute-start(bf16[128,2304]{1,0:T(8,128)(2,1)} %reduce-scatter.3.cloned.1.call-done), channel_id=1, source_target_pairs={{8,1},{1,8},{24,17},{17,24},{40,33},{33,40},{56,49},{49,56},{72,65... | collective-permute-start | bytes 1769480 | tf_op jit(solution)/shard_map/ppermute | solution.py:821
  252.6 8.0 %copy-start.47 = (bf16[128,2304]{1,0:T(8,128)(2,1)S(1)}, bf16[128,2304]{1,0:T(8,128)(2,1)}, u32[]{:S(2)}) copy-start(bf16[128,2304]{1,0:T(8,128)(2,1)} %reduce-scatter.3.cloned.1.call-done) | copy-start | bytes 1769476
  261.8 33.5 %copy-start.6 = (bf16[128,2304]{1,0:T(8,128)(2,1)}, bf16[128,2304]{1,0:T(8,128)(2,1)S(1)}, u32[]{:S(2)}) copy-start(bf16[128,2304]{1,0:T(8,128)(2,1)S(1)} %broadcast_select_fusion.1.refs_7_.b0) | copy-start | bytes 1769476
  261.8 32.1 %copy-start.11 = (bf16[64,2048]{1,0:T(8,128)(2,1)S(1)}, bf16[64,2048]{1,0:T(8,128)(2,1)}, u32[]{:S(2)}) copy-start(bf16[64,2048]{1,0:T(8,128)(2,1)} %get-tuple-element.161.refs_1_.refs_6_) | copy-start | bytes 786436
  261.8 32.0 %copy-start.16 = (f32[64,2048]{1,0:T(8,128)S(1)}, f32[64,2048]{1,0:T(8,128)}, u32[]{:S(2)}) copy-start(f32[64,2048]{1,0:T(8,128)} %copy-done.14) | copy-start | bytes 1572868
  261.8 32.0 %copy-start.38 = (f32[64,2048]{1,0:T(8,128)S(1)}, f32[64,2048]{1,0:T(8,128)}, u32[]{:S(2)}) copy-start(f32[64,2048]{1,0:T(8,128)} %copy-done.37) | copy-start | bytes 1572868
  261.8 32.8 %collective-permute-start.15 = (bf16[128,2304]{1,0:T(8,128)(2,1)S(1)}, bf16[128,2304]{1,0:T(8,128)(2,1)S(1)}, u32[]{:S(2)}, u32[]{:S(2)}) collective-permute-start(bf16[128,2304]{1,0:T(8,128)(2,1)S(1)} %broadcast_select_fusion.1.refs_7_.b0), channel_id=1, source_target_pairs={{0,2},{2,4},{4,6},{6,0},{1,3},{3,5},{5,7},{7,1},{8,10},{10,12},{12... | collective-permute-start | bytes 1769480 | tf_op jit(solution)/shard_map/ppermute | solution.py:776
  263.5 23.5 %collective-permute-start.11 = (bf16[128,2048]{1,0:T(8,128)(2,1)S(1)}, bf16[128,2048]{1,0:T(8,128)(2,1)S(1)}, u32[]{:S(2)}, u32[]{:S(2)}) collective-permute-start(bf16[128,2048]{1,0:T(8,128)(2,1)S(1)} %get-tuple-element.152), channel_id=1, source_target_pairs={{0,2},{2,4},{4,6},{6,0},{1,3},{3,5},{5,7},{7,1},{8,10},{10,12},{12... | collective-permute-start | bytes 1572872 | tf_op jit(solution)/shard_map/ppermute | solution.py:776
  264.8 29.0 %collective-permute-start.12 = (bf16[128,2048]{1,0:T(8,128)(2,1)S(1)}, bf16[128,2048]{1,0:T(8,128)(2,1)S(1)}, u32[]{:S(2)}, u32[]{:S(2)}) collective-permute-start(bf16[128,2048]{1,0:T(8,128)(2,1)S(1)} %get-tuple-element.151), channel_id=1, source_target_pairs={{0,4},{2,6},{4,0},{6,2},{1,5},{3,7},{5,1},{7,3},{8,12},{10,14},{12... | collective-permute-start | bytes 1572872 | tf_op jit(solution)/shard_map/ppermute | solution.py:776
  266.3 27.5 %collective-permute-start.13 = (bf16[128,2048]{1,0:T(8,128)(2,1)S(1)}, bf16[128,2048]{1,0:T(8,128)(2,1)S(1)}, u32[]{:S(2)}, u32[]{:S(2)}) collective-permute-start(bf16[128,2048]{1,0:T(8,128)(2,1)S(1)} %get-tuple-element.150), channel_id=1, source_target_pairs={{0,6},{2,0},{4,2},{6,4},{1,7},{3,1},{5,3},{7,5},{8,14},{10,8},{12,... | collective-permute-start | bytes 1572872 | tf_op jit(solution)/shard_map/ppermute | solution.py:776
  294.6 2.0 collective-permute-start.16
  294.7 16.2 %collective-permute-start.18 = (bf16[128,2304]{1,0:T(8,128)(2,1)S(1)}, bf16[128,2304]{1,0:T(8,128)(2,1)}, u32[]{:S(2)}, u32[]{:S(2)}) collective-permute-start(bf16[128,2304]{1,0:T(8,128)(2,1)S(1)} %broadcast_select_fusion.1.refs_7_.b0), channel_id=1, source_target_pairs={{0,4},{2,6},{4,0},{6,2},{1,5},{3,7},{5,1},{7,3},{8,12},{10,14},{12... | collective-permute-start | bytes 1769480 | tf_op jit(solution)/shard_map/ppermute | solution.py:776
  295.3 23.5 %collective-permute-start.19 = (bf16[128,2304]{1,0:T(8,128)(2,1)S(1)}, bf16[128,2304]{1,0:T(8,128)(2,1)}, u32[]{:S(2)}, u32[]{:S(2)}) collective-permute-start(bf16[128,2304]{1,0:T(8,128)(2,1)S(1)} %broadcast_select_fusion.1.refs_7_.b0), channel_id=1, source_target_pairs={{0,6},{2,0},{4,2},{6,4},{1,7},{3,1},{5,3},{7,5},{8,14},{10,8},{12,... | collective-permute-start | bytes 1769480 | tf_op jit(solution)/shard_map/ppermute | solution.py:776
  298.0 41.9 %collective-permute-start.17 = (bf16[2,128,2048]{2,1,0:T(8,128)(2,1)}, bf16[2,128,2048]{2,1,0:T(8,128)(2,1)S(1)}, u32[]{:S(2)}, u32[]{:S(2)}) collective-permute-start(bf16[2,128,2048]{2,1,0:T(8,128)(2,1)} %pad_maximum_fusion), channel_id=1, source_target_pairs={{0,1},{9,8},{16,17},{25,24},{32,33},{41,40},{48,49},{57,56},{64,65... | collective-permute-start | bytes 3145736 | tf_op jit(solution)/shard_map/ppermute | solution.py:959
  300.4 38.6 %all-to-all-start.6 = ((bf16[128,8,128]{2,1,0:T(8,128)(2,1)}), bf16[128,8,128]{2,1,0:T(8,128)(2,1)S(1)}, u32[]{:S(2)}, u32[]{:S(2)}) async-start(bf16[128,8,128]{2,1,0:T(8,128)(2,1)} %bitcast.42), calls=%async_computation.8 | async-start | bytes 524288 | tf_op jit(solution)/shard_map/all_to_all | solution.py:929
  306.9 26.0 %copy-start.53 = (bf16[128]{0:T(256)(128)(2,1)S(1)}, bf16[128]{0:T(256)(128)(2,1)}, u32[]{:S(2)}) copy-start(bf16[128]{0:T(256)(128)(2,1)} %param.19) | copy-start | bytes 772
  325.3 2.9 collective-permute-start.20
  328.7 10.4 %collective-permute-start.22 = (bf16[128,1024]{1,0:T(8,128)(2,1)}, bf16[128,1024]{1,0:T(8,128)(2,1)S(1)}, u32[]{:S(2)}, u32[]{:S(2)}) collective-permute-start(bf16[128,1024]{1,0:T(8,128)(2,1)} %reduce-scatter.5.cloned.1.call-done), channel_id=1, source_target_pairs={{1,8},{3,10},{5,12},{7,14},{8,1},{10,3},{12,5},{14,7},{17,24},{19,... | collective-permute-start | bytes 786440 | tf_op jit(solution)/shard_map/ppermute | solution.py:906
  333.7 7.8 %collective-permute-start.21 = (bf16[128,1024]{1,0:T(8,128)(2,1)}, bf16[128,1024]{1,0:T(8,128)(2,1)S(1)}, u32[]{:S(2)}, u32[]{:S(2)}) collective-permute-start(bf16[128,1024]{1,0:T(8,128)(2,1)} %reduce-scatter.5.cloned.1.call-done), channel_id=1, source_target_pairs={{0,6},{1,14},{2,0},{3,8},{4,2},{5,10},{6,4},{7,12},{8,7},{9,15},{1... | collective-permute-start | bytes 786440 | tf_op jit(solution)/shard_map/ppermute | solution.py:906
  336.1 10.1 %collective-permute-start.23 = (bf16[128,1024]{1,0:T(8,128)(2,1)}, bf16[128,1024]{1,0:T(8,128)(2,1)S(1)}, u32[]{:S(2)}, u32[]{:S(2)}) collective-permute-start(bf16[128,1024]{1,0:T(8,128)(2,1)} %reduce-scatter.5.cloned.1.call-done), channel_id=1, source_target_pairs={{0,2},{1,10},{2,4},{3,12},{4,6},{5,14},{6,0},{7,8},{8,3},{9,11},{1... | collective-permute-start | bytes 786440 | tf_op jit(solution)/shard_map/ppermute | solution.py:906
  336.4 12.5 %collective-permute-start.24 = (bf16[128,1024]{1,0:T(8,128)(2,1)}, bf16[128,1024]{1,0:T(8,128)(2,1)}, u32[]{:S(2)}, u32[]{:S(2)}) collective-permute-start(bf16[128,1024]{1,0:T(8,128)(2,1)} %reduce-scatter.5.cloned.1.call-done), channel_id=1, source_target_pairs={{0,4},{1,12},{2,6},{3,14},{4,0},{5,8},{6,2},{7,10},{8,5},{9,13},{1... | collective-permute-start | bytes 786440 | tf_op jit(solution)/shard_map/ppermute | solution.py:906
  339.9 12.2 %copy-start.1 = (bf16[3072,128]{1,0:T(8,128)(2,1)S(1)}, bf16[3072,128]{1,0:T(8,128)(2,1)}, u32[]{:S(2)}) copy-start(bf16[3072,128]{1,0:T(8,128)(2,1)} %param.30) | copy-start | bytes 2359300
  341.6 7.3 %copy-start.49 = (bf16[128,1024]{1,0:T(8,128)(2,1)}, bf16[128,1024]{1,0:T(8,128)(2,1)S(1)}, u32[]{:S(2)}) copy-start(bf16[128,1024]{1,0:T(8,128)(2,1)S(1)} %collective-permute-done.21.b3) | copy-start | bytes 786436
  346.2 2.6 copy-start.50
  (27 other events, 36.2 us)
Sparse Core Ops, SparseCore 0:
  10.7 54.5 all-gather.2
  68.2 75.2 all-gather.4
  162.0 86.0 reduce-scatter.2
  251.7 76.2 reduce-scatter.4

commit v15 on v13

--- a/solution.py
+++ b/solution.py
@@ -279,7 +279,7 @@
 def feed(ua, ub, ca, cb, w, u_flip):
     half, width = ua.shape
     length, units = 2 * half, w.shape[1] // 3
-    chunk, slab = units // FEED_STEPS, 4 * HD
+    chunk, slab = units // FEED_STEPS, 8 * HD
     early = lambda i: jnp.minimum(i, FEED_STEPS - 1)
     late = lambda i: jnp.maximum(i - FEED_STEPS, 0)
     column = lambda shift: pl.BlockSpec(

time: 361 us -> 360 us (level)
  no operation moved by 1% of the time
where the time goes in v15:
time: 360 us; the launch traced here: 357 us
  waiting for transfers between devices  122 us (34%)
  Pallas kernels  76.1 us (21%)
  starting transfers between devices  61.5 us (17%)
  blocking collectives  34.8 us (10%)
  local copies, waits for them, and re-layouts  33.5 us (9%)
  other arithmetic  15.1 us (4%)
  between operations  14.6 us (4%)
    pallas_call x14, Pallas kernels, call(): return lambda *operands: built(*operands, *behind)  58.4 us
    ppermute x6, waiting for transfers between devices, ctx_turn(): lax.ppermute(value, 'ctx', [(i, (i + by) % n_ctx) for i in range(n_ctx)])  36.7 us
    all_to_all x2, blocking collectives, ctx_exchange(): return lax.all_to_all(value, 'ctx', 0, 0)  34.8 us
    all_to_all x3, waiting for transfers between devices, ctx_exchange(): return lax.all_to_all(value, 'ctx', 0, 0)  28.4 us
    unnamed x117, local copies, waits for them, and re-layouts  24.2 us
    ppermute x11, waiting for transfers between devices, core_swap(): return lax.ppermute(value, 'shard', core_perm)  17.5 us
    all_to_all x3, starting transfers between devices, ctx_exchange(): return lax.all_to_all(value, 'ctx', 0, 0)  12.1 us
    reduce_scatter x2, waiting for transfers between devices, plane_scatter(): lax.psum_scatter(value, PLANE, scatter_dimension=0, tiled=True, axis_inde...  10.8 us
  transfers between devices with their start and end apart: 34, of which 25 were waited for; matrix products, arithmetic and copies ran while one was open for 7% of the time, Pallas kernels for 15%

profile of v15, /device:TPU:1, one launch (start us, length us, event | category | flops | bytes accessed | tf_op | source)
XLA Modules:
  0.0 357.3 jit_solution(17193028947947520523)
XLA Ops:
  7.3 1.8 shard_map.263
  10.5 1.5 collective-permute-start.1
  12.6 7.1 %all-to-all-start = ((bf16[16,8,128]{2,1,0:T(8,128)(2,1)}), bf16[16,8,128]{2,1,0:T(8,128)(2,1)S(1)}, u32[]{:S(2)}, u32[]{:S(2)}) async-start(bf16[16,8,128]{2,1,0:T(8,128)(2,1)} %broadcast_in_dim.24), calls=%async_computation | async-start | bytes 65536 | tf_op jit(solution)/shard_map/all_to_all | solution.py:835
  19.9 7.2 %all-to-all-done = bf16[16,8,128]{2,1,0:T(8,128)(2,1)S(1)} async-done(((bf16[16,8,128]{2,1,0:T(8,128)(2,1)}), bf16[16,8,128]{2,1,0:T(8,128)(2,1)S(1)}, u32[]{:S(2)}, u32[]{:S(2)}) %all-to-all-start) | async-done | bytes 32800 | tf_op jit(solution)/shard_map/all_to_all | solution.py:835
  27.1 1.6 broadcast_in_dim.25
  28.7 5.0 %all-to-all-start.1 = ((bf16[4,128,2048]{2,1,0:T(8,128)(2,1)}), bf16[4,128,2048]{2,1,0:T(8,128)(2,1)}, u32[]{:S(2)}, u32[]{:S(2)}) async-start(bf16[4,128,2048]{2,1,0:T(8,128)(2,1)} %broadcast_in_dim.25), calls=%async_computation.1 | async-start | bytes 4194304 | tf_op jit(solution)/shard_map/all_to_all | solution.py:773
  35.2 2.9 collective-permute-start
  38.0 8.7 %collective-permute-done = bf16[128,2304]{1,0:T(8,128)(2,1)S(1)} collective-permute-done((bf16[128,2304]{1,0:T(8,128)(2,1)S(1)}, bf16[128,2304]{1,0:T(8,128)(2,1)S(1)}, u32[]{:S(2)}, u32[]{:S(2)}) %collective-permute-start) | collective-permute-done | bytes 589856 | tf_op jit(solution)/shard_map/ppermute | solution.py:853
  46.8 13.0 %all-to-all-done.1.refs_0_.refs_2_.refs_8_ = bf16[4,128,2048]{2,1,0:T(8,128)(2,1)} async-done(((bf16[4,128,2048]{2,1,0:T(8,128)(2,1)}), bf16[4,128,2048]{2,1,0:T(8,128)(2,1)}, u32[]{:S(2)}, u32[]{:S(2)}) %all-to-all-start.1) | async-done | bytes 2097184 | tf_op jit(solution)/shard_map/all_to_all | solution.py:773
  60.8 1.6 collective-permute-start.3
  65.3 1.5 collective-permute-done.2.refs_1_.refs_3_.refs_9_
  68.1 2.4 shard_map.264
  71.0 3.9 %collective-permute-done.4.other = bf16[8,128,1024]{2,1,0:T(8,128)(2,1)} collective-permute-done((bf16[8,128,1024]{2,1,0:T(8,128)(2,1)S(1)}, bf16[8,128,1024]{2,1,0:T(8,128)(2,1)}, u32[]{:S(2)}, u32[]{:S(2)}) %collective-permute-start.4) | collective-permute-done | bytes 2097184 | tf_op jit(solution)/shard_map/ppermute | solution.py:770
  74.9 4.8 %shard_map.265 = bf16[8,2,128,1024]{3,2,1,0:T(8,128)(2,1)} custom-call(s32[1]{0:T(128)} %bitcast.18.core, bf16[8,2,128,1024]{3,2,1,0:T(8,128)(2,1)} %bitcast.96, bf16[8,128,1024]{2,1,0:T(8,128)(2,1)} %collective-permute-done.4.other), custom_call_target="tpu_custom_call" | custom-call | flops 1048576 | bytes 8388608 | tf_op jit(solution)/shard_map/pallas_call | solution.py:630
  79.7 5.5 %shard_map.266 = (bf16[512,2048]{1,0:T(8,128)(2,1)S(1)}, f32[512,384]{1,0:T(8,128)S(1)}, bf16[512,512]{1,0:T(8,128)(2,1)S(1)}, f32[512,256]{1,0:T(8,128)S(1)}) custom-call(bf16[4,128,2048]{2,1,0:T(8,128)(2,1)} %all-to-all-done.1.refs_0_.refs_2_.refs_8_, bf16[4,128,2048]{2,1,0:T(8,128)(2,1)} %copy-done.43, bf16[2048,1024]{1,0:T(8,128)(2,1)} %bitcast.91, ...), custom_call_target="tpu_custom_call" | custom-call | flops 1610612736 | bytes 8388608 | tf_op jit(solution)/shard_map/pallas_call | solution.py:100
  85.2 1.3 copy-done.22
  86.5 6.5 %shard_map.267 = (f32[2,512,512]{2,1,0:T(8,128)}, f32[512,256]{1,0:T(8,128)S(1)}, bf16[512,256]{1,0:T(8,128)(2,1)S(1)}, bf16[256,2048]{1,0:T(8,128)(2,1)S(1)}, bf16[256,2048]{1,0:T(8,128)(2,1)S(1)}) custom-call(bf16[512,512]{1,0:T(8,128)(2,1)S(1)} %get-tuple-element.88.refs_0_.refs_1_, f32[512,256]{1,0:T(8,128)S(1)} %get-tuple-element.89.refs_1_.refs_3_, ...), custom_call_target="tpu_custom_call" | custom-call | flops 805306368 | bytes 8388608 | tf_op jit(solution)/shard_map/pallas_call | solution.py:100
  93.2 2.6 collective-permute-done.5
  95.8 1.4 add_convert_fusion.3
  97.1 3.5 all-to-all-start.2
  101.5 2.2 copy-done.23
  103.7 1.3 shard_map.268.refs_2_.refs_0_
  105.1 10.6 %all-to-all-done.2.refs_0_ = bf16[4,64,2048]{2,1,0:T(8,128)(2,1)S(1)} async-done(((bf16[4,64,2048]{2,1,0:T(8,128)(2,1)}), bf16[4,64,2048]{2,1,0:T(8,128)(2,1)S(1)}, u32[]{:S(2)}, u32[]{:S(2)}) %all-to-all-start.2) | async-done | bytes 1048608 | tf_op jit(solution)/shard_map/all_to_all | solution.py:773
  117.8 16.6 %all_to_all.35 = bf16[4,64,2048]{2,1,0:T(8,128)(2,1)S(1)} all-to-all(bf16[4,64,2048]{2,1,0:T(8,128)(2,1)S(1)} %get-tuple-element.95), channel_id=1, replica_groups=mesh['shard'=16,'ctx'=4,'tp'=2] {'ctx'}, dimensions={0} | all-to-all | bytes 2097152 | tf_op jit(solution)/shard_map/all_to_all | solution.py:773
  134.4 1.9 collective-permute-start.6
  136.3 2.3 collective-permute-done.6
  138.5 1.3 shard_map.270.refs_7_
  139.9 1.3 copy-done.5
  143.5 18.3 %shard_map.271 = (bf16[512,768]{1,0:T(8,128)(2,1)}, bf16[512,768]{1,0:T(8,128)(2,1)}, bf16[512,768]{1,0:T(8,128)(2,1)}, bf16[2048,2304]{1,0:T(8,128)(2,1)}) custom-call(bf16[256,2048]{1,0:T(8,128)(2,1)} %bitcast.84, bf16[256,2048]{1,0:T(8,128)(2,1)} %bitcast.90, bf16[4,128,2048]{2,1,0:T(8,128)(2,1)} %all-to-all-done.1.refs_0_.refs_2_.refs_8_, ...), custom_call_target="tpu_custom_call" | custom-call | flops 9663676416 | bytes 8388608 | tf_op jit(solution)/shard_map/pallas_call | solution.py:100
  164.0 6.0 %shard_map.272 = (bf16[256,2048]{1,0:T(8,128)(2,1)S(1)}, bf16[256,2048]{1,0:T(8,128)(2,1)S(1)}) custom-call(bf16[512,768]{1,0:T(8,128)(2,1)S(1)} %copy-done.30, bf16[512,768]{1,0:T(8,128)(2,1)S(1)} %copy-done.31, bf16[2048,2304]{1,0:T(8,128)(2,1)} %all-gather.5.cloned.1.call-done.refs_4_.refs_5_.refs_6_.refs_2_.refs_3_.refs_1_, ...), custom_call_target="tpu_custom_call" | custom-call | flops 3221225472 | bytes 8388608 | tf_op jit(solution)/shard_map/pallas_call | solution.py:100
  170.8 2.3 collective-permute-done.7
  173.4 18.2 %all_to_all.36.refs_0_ = bf16[4,64,2048]{2,1,0:T(8,128)(2,1)S(1)} all-to-all(bf16[4,64,2048]{2,1,0:T(8,128)(2,1)S(1)} %bitcast.85), channel_id=1, replica_groups=mesh['shard'=16,'ctx'=4,'tp'=2] {'ctx'}, dimensions={0} | all-to-all | bytes 2097152 | tf_op jit(solution)/shard_map/all_to_all | solution.py:773
  194.9 3.5 all-to-all-start.5
  200.9 4.2 %shard_map.274 = (bf16[256,2048]{1,0:T(8,128)(2,1)S(1)}, bf16[256,2048]{1,0:T(8,128)(2,1)S(1)}) custom-call(bf16[512,768]{1,0:T(8,128)(2,1)S(1)} %copy-done.34, bf16[2048,2304]{1,0:T(8,128)(2,1)} %all-gather.5.cloned.1.call-done.refs_4_.refs_5_.refs_6_.refs_2_.refs_3_.refs_1_, bf16[4,64,2048]{2,1,0:T(8,128)(2,1)S(1)} %bitcast.86), custom_call_target="tpu_custom_call" | custom-call | flops 1610612736 | bytes 8388608 | tf_op jit(solution)/shard_map/pallas_call | solution.py:100
  207.0 4.8 %all-to-all-done.5 = bf16[4,64,2048]{2,1,0:T(8,128)(2,1)S(1)} async-done(((bf16[4,64,2048]{2,1,0:T(8,128)(2,1)}), bf16[4,64,2048]{2,1,0:T(8,128)(2,1)S(1)}, u32[]{:S(2)}, u32[]{:S(2)}) %all-to-all-start.5) | async-done | bytes 1048608 | tf_op jit(solution)/shard_map/all_to_all | solution.py:773
  211.8 2.7 collective-permute-start.9
  214.5 2.3 collective-permute-done.9
  218.9 2.2 shard_map.275
  221.2 3.1 shard_map.276
  224.4 4.4 %shard_map.277.refs_3_ = bf16[2048,1024]{1,0:T(8,128)(2,1)} custom-call(bf16[2048,512]{1,0:T(8,128)(2,1)S(1)} %shard_map.268.refs_2_.refs_0_, bf16[256,2048]{1,0:T(8,128)(2,1)S(1)} %bitcast.82, bf16[256,2048]{1,0:T(8,128)(2,1)S(1)} %bitcast.88, bf16[512,512]{1,0:T(8,128)(2,1)S(1)} %get-tuple-element.113.refs_3_.refs_0_, ...), custom_call_target="tpu_custom_call" | custom-call | flops 2147483648 | bytes 8388608 | tf_op jit(solution)/shard_map/pallas_call | solution.py:100
  231.2 4.2 %shard_map.278 = (bf16[256,2048]{1,0:T(8,128)(2,1)S(1)}, bf16[256,2048]{1,0:T(8,128)(2,1)S(1)}) custom-call(bf16[512,512]{1,0:T(8,128)(2,1)S(1)} %copy-done.20, bf16[512,256]{1,0:T(8,128)(2,1)S(1)} %copy-done.27, bf16[2048,1024]{1,0:T(8,128)(2,1)} %bitcast.94, bf16[2048,1024]{1,0:T(8,128)(2,1)} %shard_map.277.refs_3_), custom_call_target="tpu_custom_call" | custom-call | flops 1610612736 | bytes 8388608 | tf_op jit(solution)/shard_map/pallas_call | solution.py:100
  236.0 1.4 add_convert_fusion.1
  238.4 1.4 add_convert_fusion
  239.8 8.1 %reduce-scatter.3.cloned.1.call-done = bf16[128,2304]{1,0:T(8,128)(2,1)} async-done(((bf16[2048,2304]{1,0:T(8,128)(2,1)}), bf16[128,2304]{1,0:T(8,128)(2,1)}) %reduce-scatter.3.cloned.1.call-update) | async-done | bytes 589840 | tf_op jit(solution)/shard_map/reduce_scatter | solution.py:792
  247.8 4.5 %collective-permute-start.14 = (bf16[128,2304]{1,0:T(8,128)(2,1)}, bf16[128,2304]{1,0:T(8,128)(2,1)}, u32[]{:S(2)}, u32[]{:S(2)}) collective-permute-start(bf16[128,2304]{1,0:T(8,128)(2,1)} %reduce-scatter.3.cloned.1.call-done), channel_id=1, source_target_pairs={{8,1},{1,8},{24,17},{17,24},{40,33},{33,40},{56,49},{49,56},{72,65... | collective-permute-start | bytes 1769480 | tf_op jit(solution)/shard_map/ppermute | solution.py:821
  252.3 1.4 constant_dynamic-update-slice_fusion.1
  254.0 6.4 %collective-permute-done.14 = bf16[128,2304]{1,0:T(8,128)(2,1)} collective-permute-done((bf16[128,2304]{1,0:T(8,128)(2,1)}, bf16[128,2304]{1,0:T(8,128)(2,1)}, u32[]{:S(2)}, u32[]{:S(2)}) %collective-permute-start.14) | collective-permute-done | bytes 589856 | tf_op jit(solution)/shard_map/ppermute | solution.py:821
  263.0 1.3 collective-permute-start.11
  264.4 1.4 collective-permute-start.12
  265.7 2.0 collective-permute-start.13
  267.7 18.8 %collective-permute-done.11.refs_1_ = bf16[128,2048]{1,0:T(8,128)(2,1)S(1)} collective-permute-done((bf16[128,2048]{1,0:T(8,128)(2,1)S(1)}, bf16[128,2048]{1,0:T(8,128)(2,1)S(1)}, u32[]{:S(2)}, u32[]{:S(2)}) %collective-permute-start.11) | collective-permute-done | bytes 524320 | tf_op jit(solution)/shard_map/ppermute | solution.py:776
  286.6 6.8 %collective-permute-done.12.refs_2_ = bf16[128,2048]{1,0:T(8,128)(2,1)S(1)} collective-permute-done((bf16[128,2048]{1,0:T(8,128)(2,1)S(1)}, bf16[128,2048]{1,0:T(8,128)(2,1)S(1)}, u32[]{:S(2)}, u32[]{:S(2)}) %collective-permute-start.12) | collective-permute-done | bytes 524320 | tf_op jit(solution)/shard_map/ppermute | solution.py:776
  299.9 6.7 %all-to-all-start.6 = ((bf16[128,8,128]{2,1,0:T(8,128)(2,1)}), bf16[128,8,128]{2,1,0:T(8,128)(2,1)S(1)}, u32[]{:S(2)}, u32[]{:S(2)}) async-start(bf16[128,8,128]{2,1,0:T(8,128)(2,1)} %bitcast.42), calls=%async_computation.8 | async-start | bytes 524288 | tf_op jit(solution)/shard_map/all_to_all | solution.py:929
  307.4 3.1 collective-permute-done.18.b2
  310.4 7.9 %collective-permute-done.19.b3 = bf16[128,2304]{1,0:T(8,128)(2,1)} collective-permute-done((bf16[128,2304]{1,0:T(8,128)(2,1)S(1)}, bf16[128,2304]{1,0:T(8,128)(2,1)}, u32[]{:S(2)}, u32[]{:S(2)}) %collective-permute-start.19) | collective-permute-done | bytes 589856 | tf_op jit(solution)/shard_map/ppermute | solution.py:776
  318.4 5.5 %shard_map.280 = (f32[128,3072]{1,0:T(8,128)}, f32[128,3072]{1,0:T(8,128)}, f32[3072,128]{1,0:T(8,128)}, f32[128,128]{1,0:T(8,128)}) custom-call(s32[1]{0:T(128)} %bitcast.at.turn_at, bf16[128,2304]{1,0:T(8,128)(2,1)} %copy-done.6, bf16[128,2304]{1,0:T(8,128)(2,1)} %copy-done.48, bf16[128,2304]{1,0:T(8,128)(2,1)} %collective-permute-done.18.b2, ...), custom_call_target="tpu_custom_call" | custom-call | flops 1048576 | bytes 8388608 | tf_op jit(solution)/shard_map/pallas_call | solution.py:695
  324.8 2.8 reduce-scatter.5.cloned.1.call-done
  327.6 4.1 %collective-permute-start.22 = (bf16[128,1024]{1,0:T(8,128)(2,1)}, bf16[128,1024]{1,0:T(8,128)(2,1)S(1)}, u32[]{:S(2)}, u32[]{:S(2)}) collective-permute-start(bf16[128,1024]{1,0:T(8,128)(2,1)} %reduce-scatter.5.cloned.1.call-done), channel_id=1, source_target_pairs={{0,2},{1,10},{2,4},{3,12},{4,6},{5,14},{6,0},{7,8},{8,3},{9,11},{1... | collective-permute-start | bytes 786440 | tf_op jit(solution)/shard_map/ppermute | solution.py:906
  331.7 1.9 collective-permute-start.21
  334.4 2.9 collective-permute-start.20
  337.2 1.4 collective-permute-start.23
  340.6 3.1 collective-permute-done.24
  344.4 1.6 fusion
  347.6 3.2 shard_map.281
  (217 shorter events, 47.9 us)
Async XLA Ops:
  7.2 26.5 %copy-start = (bf16[3072,128]{1,0:T(8,128)(2,1)S(1)}, bf16[3072,128]{1,0:T(8,128)(2,1)}, u32[]{:S(2)}) copy-start(bf16[3072,128]{1,0:T(8,128)(2,1)} %param.30) | copy-start | bytes 2359300
  7.2 59.6 %all-gather.3.cloned.1.call-start = ((), (), s32[]{:S(2)}) async-start(), calls=%async_computation.9 | async-start | bytes 4456448 | tf_op jit(solution)/shard_map/all_gather | solution.py:789
  7.3 4.7 %copy-start.54 = (bf16[8]{0:T(256)(128)(2,1)S(1)}, bf16[8]{0:T(256)(128)(2,1)}, u32[]{:S(2)}) copy-start(bf16[8]{0:T(256)(128)(2,1)} %param.26) | copy-start | bytes 52
  7.3 4.7 %copy-start.55 = (bf16[8]{0:T(256)(128)(2,1)S(1)}, bf16[8]{0:T(256)(128)(2,1)}, u32[]{:S(2)}) copy-start(bf16[8]{0:T(256)(128)(2,1)} %param.25) | copy-start | bytes 52
  9.1 10.6 %copy-start.56 = (bf16[128]{0:T(256)(128)(2,1)S(1)}, bf16[128]{0:T(256)(128)(2,1)}, u32[]{:S(2)}) copy-start(bf16[128]{0:T(256)(128)(2,1)} %param.27) | copy-start | bytes 772
  10.5 9.3 %collective-permute-start.1 = (bf16[128,2048]{1,0:T(8,128)(2,1)S(1)}, bf16[128,2048]{1,0:T(8,128)(2,1)S(1)}, u32[]{:S(2)}, u32[]{:S(2)}) collective-permute-start(bf16[128,2048]{1,0:T(8,128)(2,1)S(1)} %pad_maximum_fusion.2), channel_id=1, source_target_pairs={{0,8},{8,0},{16,24},{24,16},{32,40},{40,32},{48,56},{56,48},{64,72... | collective-permute-start | bytes 1572872 | tf_op jit(solution)/shard_map/ppermute | solution.py:770
  12.6 14.5 %all-to-all-start = ((bf16[16,8,128]{2,1,0:T(8,128)(2,1)}), bf16[16,8,128]{2,1,0:T(8,128)(2,1)S(1)}, u32[]{:S(2)}, u32[]{:S(2)}) async-start(bf16[16,8,128]{2,1,0:T(8,128)(2,1)} %broadcast_in_dim.24), calls=%async_computation | async-start | bytes 65536 | tf_op jit(solution)/shard_map/all_to_all | solution.py:835
  19.9 8.8 %copy-start.44 = (bf16[128,2048]{1,0:T(8,128)(2,1)}, bf16[128,2048]{1,0:T(8,128)(2,1)S(1)}, u32[]{:S(2)}) copy-start(bf16[128,2048]{1,0:T(8,128)(2,1)S(1)} %maximum_select_fusion) | copy-start | bytes 1572868
  28.7 31.1 %all-to-all-start.1 = ((bf16[4,128,2048]{2,1,0:T(8,128)(2,1)}), bf16[4,128,2048]{2,1,0:T(8,128)(2,1)}, u32[]{:S(2)}, u32[]{:S(2)}) async-start(bf16[4,128,2048]{2,1,0:T(8,128)(2,1)} %broadcast_in_dim.25), calls=%async_computation.1 | async-start | bytes 4194304 | tf_op jit(solution)/shard_map/all_to_all | solution.py:773
  33.7 109.8 %all-gather.5.cloned.1.call-start = ((), (), s32[]{:S(2)}) async-start(), calls=%async_computation.10 | async-start | bytes 10027008 | tf_op jit(solution)/shard_map/all_gather | solution.py:789
  35.0 25.8 %copy-start.51 = (s32[1,13]{1,0:T(1,128)S(1)}, s32[1,13]{1,0:T(1,128)}, u32[]{:S(2)}) copy-start(s32[1,13]{1,0:T(1,128)} %param.18) | copy-start | bytes 160
  35.0 25.8 %copy-start.52 = (s32[1,13]{1,0:T(1,128)S(1)}, s32[1,13]{1,0:T(1,128)}, u32[]{:S(2)}) copy-start(s32[1,13]{1,0:T(1,128)} %param.17) | copy-start | bytes 160
  35.2 11.6 %collective-permute-start = (bf16[128,2304]{1,0:T(8,128)(2,1)S(1)}, bf16[128,2304]{1,0:T(8,128)(2,1)S(1)}, u32[]{:S(2)}, u32[]{:S(2)}) collective-permute-start(bf16[128,2304]{1,0:T(8,128)(2,1)S(1)} %pad_maximum_fusion.1), channel_id=1, source_target_pairs={{8,1},{1,8},{24,17},{17,24},{40,33},{33,40},{56,49},{49,56},{72,65... | collective-permute-start | bytes 1769480 | tf_op jit(solution)/shard_map/ppermute | solution.py:853
  60.8 2.4 collective-permute-start.3
  62.4 4.4 %collective-permute-start.2 = (bf16[4,128,2048]{2,1,0:T(8,128)(2,1)}, bf16[4,128,2048]{2,1,0:T(8,128)(2,1)S(1)}, u32[]{:S(2)}, u32[]{:S(2)}) collective-permute-start(bf16[4,128,2048]{2,1,0:T(8,128)(2,1)} %all-to-all-done.1.refs_0_.refs_2_.refs_8_), channel_id=1, source_target_pairs={{0,8},{8,0},{16,24},{24,16},{32,40},{40,32},{48,56},{56,48},{64,72... | collective-permute-start | bytes 6291464 | tf_op jit(solution)/shard_map/ppermute | solution.py:770
  65.3 14.4 %copy-start.8 = (f32[512,128]{1,0:T(8,128)}, f32[512,128]{1,0:T(8,128)S(1)}, u32[]{:S(2)}) copy-start(f32[512,128]{1,0:T(8,128)S(1)} %get-tuple-element.86.refs_4_.refs_5_) | copy-start | bytes 786436
  70.5 4.4 %collective-permute-start.4 = (bf16[8,128,1024]{2,1,0:T(8,128)(2,1)S(1)}, bf16[8,128,1024]{2,1,0:T(8,128)(2,1)}, u32[]{:S(2)}, u32[]{:S(2)}) collective-permute-start(bf16[8,128,1024]{2,1,0:T(8,128)(2,1)S(1)} %shard_map.264), channel_id=1, source_target_pairs={{0,8},{8,0},{16,24},{24,16},{32,40},{40,32},{48,56},{56,48},{64,72... | collective-permute-start | bytes 6291464 | tf_op jit(solution)/shard_map/ppermute | solution.py:770
  86.5 6.5 %copy-start.12 = (f32[512,256]{1,0:T(8,128)}, f32[512,256]{1,0:T(8,128)S(1)}, u32[]{:S(2)}) copy-start(f32[512,256]{1,0:T(8,128)S(1)} %get-tuple-element.89.refs_1_.refs_3_) | copy-start | bytes 1572868
  86.5 6.5 %copy-start.17 = (bf16[512,512]{1,0:T(8,128)(2,1)}, bf16[512,512]{1,0:T(8,128)(2,1)S(1)}, u32[]{:S(2)}) copy-start(bf16[512,512]{1,0:T(8,128)(2,1)S(1)} %get-tuple-element.88.refs_0_.refs_1_) | copy-start | bytes 1572868
  86.5 6.5 %copy-start.32 = (f32[512,384]{1,0:T(8,128)}, f32[512,384]{1,0:T(8,128)S(1)}, u32[]{:S(2)}) copy-start(f32[512,384]{1,0:T(8,128)S(1)} %get-tuple-element.112.refs_3_) | copy-start | bytes 2359300
  93.0 4.1 %copy-start.35 = (f32[512,256]{1,0:T(8,128)}, f32[512,256]{1,0:T(8,128)S(1)}, u32[]{:S(2)}) copy-start(f32[512,256]{1,0:T(8,128)S(1)} %get-tuple-element.110.refs_4_) | copy-start | bytes 1572868
  93.0 4.1 %copy-start.39 = (bf16[512,256]{1,0:T(8,128)(2,1)}, bf16[512,256]{1,0:T(8,128)(2,1)S(1)}, u32[]{:S(2)}) copy-start(bf16[512,256]{1,0:T(8,128)(2,1)S(1)} %get-tuple-element.115.refs_5_) | copy-start | bytes 786436
  93.0 2.7 collective-permute-start.5
  95.8 4.9 %copy-start.45 = (bf16[128,2048]{1,0:T(8,128)(2,1)S(1)}, bf16[128,2048]{1,0:T(8,128)(2,1)}, u32[]{:S(2)}) copy-start(bf16[128,2048]{1,0:T(8,128)(2,1)} %copy-done.44) | copy-start | bytes 1572868
  97.1 18.6 %all-to-all-start.2 = ((bf16[4,64,2048]{2,1,0:T(8,128)(2,1)}), bf16[4,64,2048]{2,1,0:T(8,128)(2,1)S(1)}, u32[]{:S(2)}, u32[]{:S(2)}) async-start(bf16[4,64,2048]{2,1,0:T(8,128)(2,1)} %bitcast.22), calls=%async_computation.2 | async-start | bytes 2097152 | tf_op jit(solution)/shard_map/all_to_all | solution.py:773
  100.7 147.2 %reduce-scatter.3.cloned.1.call-start = ((), (), s32[]{:S(2)}) async-start(), calls=%async_computation.11 | async-start | bytes 10027008 | tf_op jit(solution)/shard_map/reduce_scatter | solution.py:792
  134.4 5.5 %copy-start.2 = (bf16[4,64,2048]{2,1,0:T(8,128)(2,1)}, bf16[4,64,2048]{2,1,0:T(8,128)(2,1)S(1)}, u32[]{:S(2)}) copy-start(bf16[4,64,2048]{2,1,0:T(8,128)(2,1)S(1)} %all_to_all.35) | copy-start | bytes 3145732
  134.4 4.2 %collective-permute-start.6 = (bf16[4,64,2048]{2,1,0:T(8,128)(2,1)S(1)}, bf16[4,64,2048]{2,1,0:T(8,128)(2,1)S(1)}, u32[]{:S(2)}, u32[]{:S(2)}) collective-permute-start(bf16[4,64,2048]{2,1,0:T(8,128)(2,1)S(1)} %all_to_all.35), channel_id=1, source_target_pairs={{0,8},{8,0},{16,24},{24,16},{32,40},{40,32},{48,56},{56,48},{64,72... | collective-permute-start | bytes 3145736 | tf_op jit(solution)/shard_map/ppermute | solution.py:770
  170.0 3.0 collective-permute-start.7
  173.1 19.6 %copy-start.15 = (f32[64,2048]{1,0:T(8,128)S(1)}, f32[64,2048]{1,0:T(8,128)}, u32[]{:S(2)}) copy-start(f32[64,2048]{1,0:T(8,128)} %copy-done.14) | copy-start | bytes 1572868
  173.1 19.6 %copy-start.29 = (bf16[64,2048]{1,0:T(8,128)(2,1)S(1)}, bf16[64,2048]{1,0:T(8,128)(2,1)}, u32[]{:S(2)}) copy-start(bf16[64,2048]{1,0:T(8,128)(2,1)} %get-tuple-element.164.refs_2_) | copy-start | bytes 786436
  194.9 16.9 %all-to-all-start.5 = ((bf16[4,64,2048]{2,1,0:T(8,128)(2,1)}), bf16[4,64,2048]{2,1,0:T(8,128)(2,1)S(1)}, u32[]{:S(2)}, u32[]{:S(2)}) async-start(bf16[4,64,2048]{2,1,0:T(8,128)(2,1)} %copy-done.28), calls=%async_computation.5 | async-start | bytes 2097152 | tf_op jit(solution)/shard_map/all_to_all | solution.py:773
  198.4 129.1 %reduce-scatter.5.cloned.1.call-start = ((), (), s32[]{:S(2)}) async-start(), calls=%async_computation.12 | async-start | bytes 4456448 | tf_op jit(solution)/shard_map/reduce_scatter | solution.py:792
  211.8 5.0 %collective-permute-start.9 = (bf16[4,64,2048]{2,1,0:T(8,128)(2,1)S(1)}, bf16[4,64,2048]{2,1,0:T(8,128)(2,1)S(1)}, u32[]{:S(2)}, u32[]{:S(2)}) collective-permute-start(bf16[4,64,2048]{2,1,0:T(8,128)(2,1)S(1)} %all-to-all-done.5), channel_id=1, source_target_pairs={{0,8},{8,0},{16,24},{24,16},{32,40},{40,32},{48,56},{56,48},{64,72... | collective-permute-start | bytes 3145736 | tf_op jit(solution)/shard_map/ppermute | solution.py:770
  218.9 2.4 copy-start.33
  221.0 3.3 copy-start.26
  221.2 3.1 copy-start.40
  230.8 5.2 %copy-start.25 = (bf16[256,2048]{1,0:T(8,128)(2,1)S(1)}, bf16[256,2048]{1,0:T(8,128)(2,1)}, u32[]{:S(2)}) copy-start(bf16[256,2048]{1,0:T(8,128)(2,1)} %copy-done.24) | copy-start | bytes 3145732
  230.8 5.2 %collective-permute-start.8 = (bf16[256,2048]{1,0:T(8,128)(2,1)S(1)}, bf16[256,2048]{1,0:T(8,128)(2,1)S(1)}, u32[]{:S(2)}, u32[]{:S(2)}) collective-permute-start(bf16[256,2048]{1,0:T(8,128)(2,1)S(1)} %copy-done.42), channel_id=1, source_target_pairs={{0,8},{8,0},{16,24},{24,16},{32,40},{40,32},{48,56},{56,48},{64,72... | collective-permute-start | bytes 3145736 | tf_op jit(solution)/shard_map/ppermute | solution.py:770
  235.4 3.0 collective-permute-start.10
  247.8 12.5 %collective-permute-start.14 = (bf16[128,2304]{1,0:T(8,128)(2,1)}, bf16[128,2304]{1,0:T(8,128)(2,1)}, u32[]{:S(2)}, u32[]{:S(2)}) collective-permute-start(bf16[128,2304]{1,0:T(8,128)(2,1)} %reduce-scatter.3.cloned.1.call-done), channel_id=1, source_target_pairs={{8,1},{1,8},{24,17},{17,24},{40,33},{33,40},{56,49},{49,56},{72,65... | collective-permute-start | bytes 1769480 | tf_op jit(solution)/shard_map/ppermute | solution.py:821
  252.3 8.0 %copy-start.47 = (bf16[128,2304]{1,0:T(8,128)(2,1)S(1)}, bf16[128,2304]{1,0:T(8,128)(2,1)}, u32[]{:S(2)}) copy-start(bf16[128,2304]{1,0:T(8,128)(2,1)} %reduce-scatter.3.cloned.1.call-done) | copy-start | bytes 1769476
  261.5 33.3 %copy-start.6 = (bf16[128,2304]{1,0:T(8,128)(2,1)}, bf16[128,2304]{1,0:T(8,128)(2,1)S(1)}, u32[]{:S(2)}) copy-start(bf16[128,2304]{1,0:T(8,128)(2,1)S(1)} %broadcast_select_fusion.1.refs_7_.b0) | copy-start | bytes 1769476
  261.6 31.8 %copy-start.11 = (bf16[64,2048]{1,0:T(8,128)(2,1)S(1)}, bf16[64,2048]{1,0:T(8,128)(2,1)}, u32[]{:S(2)}) copy-start(bf16[64,2048]{1,0:T(8,128)(2,1)} %get-tuple-element.165.refs_1_.refs_6_) | copy-start | bytes 786436
  261.6 31.8 %copy-start.16 = (f32[64,2048]{1,0:T(8,128)S(1)}, f32[64,2048]{1,0:T(8,128)}, u32[]{:S(2)}) copy-start(f32[64,2048]{1,0:T(8,128)} %copy-done.14) | copy-start | bytes 1572868
  261.6 31.8 %copy-start.38 = (f32[64,2048]{1,0:T(8,128)S(1)}, f32[64,2048]{1,0:T(8,128)}, u32[]{:S(2)}) copy-start(f32[64,2048]{1,0:T(8,128)} %copy-done.37) | copy-start | bytes 1572868
  261.6 32.5 %collective-permute-start.15 = (bf16[128,2304]{1,0:T(8,128)(2,1)S(1)}, bf16[128,2304]{1,0:T(8,128)(2,1)S(1)}, u32[]{:S(2)}, u32[]{:S(2)}) collective-permute-start(bf16[128,2304]{1,0:T(8,128)(2,1)S(1)} %broadcast_select_fusion.1.refs_7_.b0), channel_id=1, source_target_pairs={{0,2},{2,4},{4,6},{6,0},{1,3},{3,5},{5,7},{7,1},{8,10},{10,12},{12... | collective-permute-start | bytes 1769480 | tf_op jit(solution)/shard_map/ppermute | solution.py:776
  263.0 23.5 %collective-permute-start.11 = (bf16[128,2048]{1,0:T(8,128)(2,1)S(1)}, bf16[128,2048]{1,0:T(8,128)(2,1)S(1)}, u32[]{:S(2)}, u32[]{:S(2)}) collective-permute-start(bf16[128,2048]{1,0:T(8,128)(2,1)S(1)} %get-tuple-element.156), channel_id=1, source_target_pairs={{0,2},{2,4},{4,6},{6,0},{1,3},{3,5},{5,7},{7,1},{8,10},{10,12},{12... | collective-permute-start | bytes 1572872 | tf_op jit(solution)/shard_map/ppermute | solution.py:776
  264.4 29.0 %collective-permute-start.12 = (bf16[128,2048]{1,0:T(8,128)(2,1)S(1)}, bf16[128,2048]{1,0:T(8,128)(2,1)S(1)}, u32[]{:S(2)}, u32[]{:S(2)}) collective-permute-start(bf16[128,2048]{1,0:T(8,128)(2,1)S(1)} %get-tuple-element.155), channel_id=1, source_target_pairs={{0,4},{2,6},{4,0},{6,2},{1,5},{3,7},{5,1},{7,3},{8,12},{10,14},{12... | collective-permute-start | bytes 1572872 | tf_op jit(solution)/shard_map/ppermute | solution.py:776
  265.7 27.6 %collective-permute-start.13 = (bf16[128,2048]{1,0:T(8,128)(2,1)S(1)}, bf16[128,2048]{1,0:T(8,128)(2,1)S(1)}, u32[]{:S(2)}, u32[]{:S(2)}) collective-permute-start(bf16[128,2048]{1,0:T(8,128)(2,1)S(1)} %get-tuple-element.154), channel_id=1, source_target_pairs={{0,6},{2,0},{4,2},{6,4},{1,7},{3,1},{5,3},{7,5},{8,14},{10,8},{12,... | collective-permute-start | bytes 1572872 | tf_op jit(solution)/shard_map/ppermute | solution.py:776
  294.1 2.3 copy-start.48
  294.1 2.0 collective-permute-start.16
  294.3 16.2 %collective-permute-start.18 = (bf16[128,2304]{1,0:T(8,128)(2,1)S(1)}, bf16[128,2304]{1,0:T(8,128)(2,1)}, u32[]{:S(2)}, u32[]{:S(2)}) collective-permute-start(bf16[128,2304]{1,0:T(8,128)(2,1)S(1)} %broadcast_select_fusion.1.refs_7_.b0), channel_id=1, source_target_pairs={{0,4},{2,6},{4,0},{6,2},{1,5},{3,7},{5,1},{7,3},{8,12},{10,14},{12... | collective-permute-start | bytes 1769480 | tf_op jit(solution)/shard_map/ppermute | solution.py:776
  294.8 23.6 %collective-permute-start.19 = (bf16[128,2304]{1,0:T(8,128)(2,1)S(1)}, bf16[128,2304]{1,0:T(8,128)(2,1)}, u32[]{:S(2)}, u32[]{:S(2)}) collective-permute-start(bf16[128,2304]{1,0:T(8,128)(2,1)S(1)} %broadcast_select_fusion.1.refs_7_.b0), channel_id=1, source_target_pairs={{0,6},{2,0},{4,2},{6,4},{1,7},{3,1},{5,3},{7,5},{8,14},{10,8},{12,... | collective-permute-start | bytes 1769480 | tf_op jit(solution)/shard_map/ppermute | solution.py:776
  297.5 46.8 %collective-permute-start.17 = (bf16[2,128,2048]{2,1,0:T(8,128)(2,1)}, bf16[2,128,2048]{2,1,0:T(8,128)(2,1)S(1)}, u32[]{:S(2)}, u32[]{:S(2)}) collective-permute-start(bf16[2,128,2048]{2,1,0:T(8,128)(2,1)} %pad_maximum_fusion), channel_id=1, source_target_pairs={{0,1},{9,8},{16,17},{25,24},{32,33},{41,40},{48,49},{57,56},{64,65... | collective-permute-start | bytes 3145736 | tf_op jit(solution)/shard_map/ppermute | solution.py:958
  299.9 38.7 %all-to-all-start.6 = ((bf16[128,8,128]{2,1,0:T(8,128)(2,1)}), bf16[128,8,128]{2,1,0:T(8,128)(2,1)S(1)}, u32[]{:S(2)}, u32[]{:S(2)}) async-start(bf16[128,8,128]{2,1,0:T(8,128)(2,1)} %bitcast.42), calls=%async_computation.8 | async-start | bytes 524288 | tf_op jit(solution)/shard_map/all_to_all | solution.py:929
  306.6 27.0 %copy-start.53 = (bf16[128]{0:T(256)(128)(2,1)S(1)}, bf16[128]{0:T(256)(128)(2,1)}, u32[]{:S(2)}) copy-start(bf16[128]{0:T(256)(128)(2,1)} %param.19) | copy-start | bytes 772
  327.6 11.2 %collective-permute-start.22 = (bf16[128,1024]{1,0:T(8,128)(2,1)}, bf16[128,1024]{1,0:T(8,128)(2,1)S(1)}, u32[]{:S(2)}, u32[]{:S(2)}) collective-permute-start(bf16[128,1024]{1,0:T(8,128)(2,1)} %reduce-scatter.5.cloned.1.call-done), channel_id=1, source_target_pairs={{0,2},{1,10},{2,4},{3,12},{4,6},{5,14},{6,0},{7,8},{8,3},{9,11},{1... | collective-permute-start | bytes 786440 | tf_op jit(solution)/shard_map/ppermute | solution.py:906
  331.7 8.2 %collective-permute-start.21 = (bf16[128,1024]{1,0:T(8,128)(2,1)}, bf16[128,1024]{1,0:T(8,128)(2,1)S(1)}, u32[]{:S(2)}, u32[]{:S(2)}) collective-permute-start(bf16[128,1024]{1,0:T(8,128)(2,1)} %reduce-scatter.5.cloned.1.call-done), channel_id=1, source_target_pairs={{1,8},{3,10},{5,12},{7,14},{8,1},{10,3},{12,5},{14,7},{17,24},{19,... | collective-permute-start | bytes 786440 | tf_op jit(solution)/shard_map/ppermute | solution.py:906
  334.4 11.6 %collective-permute-start.20 = (bf16[128,1024]{1,0:T(8,128)(2,1)}, bf16[128,1024]{1,0:T(8,128)(2,1)S(1)}, u32[]{:S(2)}, u32[]{:S(2)}) collective-permute-start(bf16[128,1024]{1,0:T(8,128)(2,1)} %reduce-scatter.5.cloned.1.call-done), channel_id=1, source_target_pairs={{0,6},{1,14},{2,0},{3,8},{4,2},{5,10},{6,4},{7,12},{8,7},{9,15},{1... | collective-permute-start | bytes 786440 | tf_op jit(solution)/shard_map/ppermute | solution.py:906
  337.2 10.4 %collective-permute-start.23 = (bf16[128,1024]{1,0:T(8,128)(2,1)}, bf16[128,1024]{1,0:T(8,128)(2,1)}, u32[]{:S(2)}, u32[]{:S(2)}) collective-permute-start(bf16[128,1024]{1,0:T(8,128)(2,1)} %reduce-scatter.5.cloned.1.call-done), channel_id=1, source_target_pairs={{0,4},{1,12},{2,6},{3,14},{4,0},{5,8},{6,2},{7,10},{8,5},{9,13},{1... | collective-permute-start | bytes 786440 | tf_op jit(solution)/shard_map/ppermute | solution.py:906
  338.7 7.2 %copy-start.49 = (bf16[128,1024]{1,0:T(8,128)(2,1)}, bf16[128,1024]{1,0:T(8,128)(2,1)S(1)}, u32[]{:S(2)}) copy-start(bf16[128,1024]{1,0:T(8,128)(2,1)S(1)} %collective-permute-done.22.b1) | copy-start | bytes 786436
  338.7 5.0 %collective-permute-start.24 = (f32[128]{0:T(128)S(1)}, f32[128]{0:T(128)S(1)}, u32[]{:S(2)}, u32[]{:S(2)}) collective-permute-start(f32[128]{0:T(128)S(1)} %reduce_sum.104), channel_id=1, source_target_pairs={{0,1},{1,0},{2,3},{3,2},{4,5},{5,4},{6,7},{7,6},{8,9},{9,8},{10,11... | collective-permute-start | bytes 1544 | tf_op jit(solution)/shard_map/ppermute | solution.py:962
  344.3 6.6 %copy-start.1 = (bf16[3072,128]{1,0:T(8,128)(2,1)S(1)}, bf16[3072,128]{1,0:T(8,128)(2,1)}, u32[]{:S(2)}) copy-start(bf16[3072,128]{1,0:T(8,128)(2,1)} %param.30) | copy-start | bytes 2359300
  (27 other events, 35.5 us)
Sparse Core Ops, SparseCore 0:
  10.7 54.5 all-gather.2
  68.2 75.2 all-gather.4
  161.9 85.8 reduce-scatter.2
  251.4 76.1 reduce-scatter.4
